TPU v7x, 32 devices: a whole 2x2x4 slice. The times are simulated.
32 devices in a mesh: groups: 2 (over y), tm: 4 (over z), head: 2 (over x), rep: 2 (over core).
Axes of the slice: x: 2, y: 2, z: 4, core: 2. Of those that a mesh axis runs over, the one named last changes fastest.
Arguments:
- frozen_query: bfloat16 [2048, 2560], P(('groups', 'tm', 'rep'), 'head'), parts along dimension 0, may hold values from -144 to 144
- frozen_key: bfloat16 [2048, 2560], P(('groups', 'tm'), 'head'), parts along dimension 0, may hold values from -8 to 8
- frozen_value: bfloat16 [2048, 2560], P(('groups', 'tm'), 'head'), parts along dimension 0, may hold values from -6 to 6
- token_adapter_input: bfloat16 [2048, 128], P(('groups', 'tm')), parts along dimension 0, may hold values from -6 to 6
- query_adapter_out: bfloat16 [128, 2560], P(None, 'head'), may hold values from -0.5 to 0.5
- key_adapter_out: bfloat16 [128, 2560], P(None, 'head'), may hold values from -0.5 to 0.5
- value_adapter_out: bfloat16 [128, 2560], P(None, 'head'), may hold values from -0.5 to 0.5
- out_grad: bfloat16 [2048, 2560], P(('groups', 'tm', 'rep'), 'head'), parts along dimension 0, may hold values from -6 to 6
- band_width: int32 [4, 4], replicated, may hold values from 0 to 2, as said below
Outputs:
- grad_query: float32 [256, 2560], P('groups', 'head'), parts along dimension 0
- grad_key: float32 [256, 2560], P('groups', 'head'), parts along dimension 0
- grad_value: float32 [256, 2560], P('groups', 'head'), parts along dimension 0
- low_grad: float32 [2048, 128], P(('groups', 'tm')), parts along dimension 0
There are 2 independent parts, one for each index of `groups`. A program takes and returns all parts, laid end to end along the dimension named above; an argument that names none is the same for every part. Nothing has to cross between parts.
Inputs may be any that keep to these rules, and one draw needn't show every extreme that they name: band_width[i, j] is 2 where i equals j, 1 or 2 where |i - j| is at most 1, 0 or 1 where |i - j| is at most 4, and 0 beyond.
All inputs are finite; a program needn't handle non-finite values.
Results may differ from a plain program's by a relative error of at most 0.013.
The roundings to bfloat16 on the way count: a program that leaves them out, or rounds other values in their place, can miss the bound.
Values may be sent and summed in bfloat16 or wider, within the bound.
No kernel may reach another device: no remote copies, remote signals or barrier semaphores. Data moves between devices by JAX's collectives and lax.ppermute only.
A program may use at most 64 MiB of HBM per device.

v0:
```python
import jax
import jax.numpy as jnp
from jax import lax
from jax.sharding import PartitionSpec as P

DH = 128
NEAR = 1
REACH = 4


def as_sent(x):
    return jax.tree.map(lambda a: a.astype(jnp.bfloat16) if a.dtype == jnp.float32 else a, x)


def shifted_2(block, axis, distance):
    devices = range(lax.axis_size(axis))
    route = [(i - distance, i) for i in devices if i - distance in devices]
    return lax.ppermute(block, axis, route)


def adapter_rows(frozen_rows, reduced_rows, adapter_map):
    return (
        frozen_rows.astype(jnp.float32)
        + jnp.dot(reduced_rows, adapter_map, preferred_element_type=jnp.float32)
    ).astype(jnp.bfloat16)


def contract_rows(left, right):
    return lax.dot_general(
        left, right, (((0,), (0,)), ((), ())), preferred_element_type=jnp.float32
    )


def contract_cols(left, right):
    return lax.dot_general(
        left, right, (((1,), (1,)), ((), ())), preferred_element_type=jnp.float32
    )


def exact_rows(left, right):
    return lax.dot_general(
        left.astype(jnp.float32), right, (((0,), (0,)), ((), ())), precision=lax.Precision.HIGHEST
    )


def exact_cols(left, right):
    return lax.dot_general(
        left, right.astype(jnp.float32), (((1,), (1,)), ((), ())), precision=lax.Precision.HIGHEST
    )


def on_device(
    frozen_query,
    frozen_key,
    frozen_value,
    token_adapter_input,
    query_adapter_out,
    key_adapter_out,
    value_adapter_out,
    out_grad,
    band_width,
):
    tile_rows = frozen_query.shape[0]
    frame_rows = 2 * tile_rows
    col_width = frozen_query.shape[1]
    head_count = col_width // DH
    score_scale = DH ** (-0.5)
    frame_count = band_width.shape[0]
    frame_idx = lax.axis_index("tm")
    half_idx = lax.axis_index("rep")
    reduced_block = lax.dynamic_slice_in_dim(
        token_adapter_input, half_idx * tile_rows, tile_rows, 0
    )
    query_rows = adapter_rows(frozen_query, reduced_block, query_adapter_out)
    key_row_block = adapter_rows(frozen_key, token_adapter_input, key_adapter_out)
    value_row_block = adapter_rows(frozen_value, token_adapter_input, value_adapter_out)
    frame_payload = (key_row_block, value_row_block)
    frame_ids = jnp.arange(frame_count)
    band_row = jnp.sum(jnp.where((frame_ids == frame_idx)[:, None], band_width, 0), axis=0)
    frame_tile = jnp.arange(frame_rows) // tile_rows
    key_blocks = []
    value_blocks = []
    low_blocks = []
    allowed_blocks = []
    block_sizes = []
    for offset in range(-REACH, REACH + 1):
        reach_band = jnp.sum(jnp.where(frame_ids == frame_idx + offset, band_row, 0))
        if offset == 0:
            received = frame_payload
        elif abs(offset) <= NEAR:
            received = jax.tree.map(
                lambda part, own: part.astype(own.dtype),
                shifted_2(as_sent(frame_payload), "tm", -offset),
                frame_payload,
            )
        else:
            received = jax.tree.map(
                lambda part, own: part.astype(own.dtype),
                shifted_2(as_sent(frame_payload), "tm", -offset),
                frame_payload,
            )
        key_blocks.append(received[0])
        value_blocks.append(received[1])
        low_blocks.append(None)
        allowed_blocks.append(jnp.abs(half_idx - frame_tile) < reach_band)
        block_sizes.append(received[0].shape[0])
    all_keys = jnp.concatenate(key_blocks, axis=0)
    all_values = jnp.concatenate(value_blocks, axis=0)
    allowed = jnp.concatenate(allowed_blocks, axis=0)
    query_grads = []
    key_grads = []
    value_grads = []
    for head_pos in range(head_count):
        head_cols = slice(head_pos * DH, (head_pos + 1) * DH)
        head_q = query_rows[:, head_cols]
        head_k = all_keys[:, head_cols]
        head_v = all_values[:, head_cols]
        head_do = out_grad[:, head_cols]
        scores = contract_cols(head_q, head_k) * score_scale
        scores = jnp.where(allowed[None, :], scores, -jnp.inf)
        shifted = jnp.exp(scores - jnp.max(scores, axis=1, keepdims=True))
        attn_prob = shifted / jnp.sum(shifted, axis=1, keepdims=True)
        prob_low = attn_prob.astype(jnp.bfloat16)
        attended = jnp.dot(prob_low, head_v, preferred_element_type=jnp.float32).astype(
            jnp.bfloat16
        )
        row_delta = jnp.sum(
            head_do.astype(jnp.float32) * attended.astype(jnp.float32), axis=1, keepdims=True
        )
        prob_grad = contract_cols(head_do, head_v)
        score_grad = (attn_prob * (prob_grad - row_delta)).astype(jnp.bfloat16)
        query_grads.append(
            (jnp.dot(score_grad, head_k, preferred_element_type=jnp.float32) * score_scale).astype(
                jnp.bfloat16
            )
        )
        key_grads.append((contract_rows(score_grad, head_q) * score_scale).astype(jnp.bfloat16))
        value_grads.append(contract_rows(prob_low, head_do).astype(jnp.bfloat16))
    query_grad = jnp.concatenate(query_grads, axis=1)
    key_grad = jnp.concatenate(key_grads, axis=1)
    value_grad = jnp.concatenate(value_grads, axis=1)
    tile_mask = (frame_tile == half_idx)[:, None]
    placed = jnp.where(
        tile_mask, jnp.concatenate([query_grad, query_grad]), jnp.zeros((), jnp.bfloat16)
    )
    grad_query = contract_rows(reduced_block, query_grad)
    low_part = contract_cols(placed, query_adapter_out)
    block_start = 0
    key_sum = jnp.zeros((frame_rows, col_width), jnp.float32)
    value_sum = jnp.zeros((frame_rows, col_width), jnp.float32)
    for block_pos, offset in enumerate(range(-REACH, REACH + 1)):
        block_size = block_sizes[block_pos]
        part_keys = key_grad[block_start : block_start + block_size]
        part_values = value_grad[block_start : block_start + block_size]
        block_start = block_start + block_size
        if offset == 0:
            back_keys, back_values = (part_keys, part_values)
        elif abs(offset) <= NEAR:
            back_keys, back_values = shifted_2((part_keys, part_values), "tm", offset)
        else:
            back_keys, back_values = shifted_2((part_keys, part_values), "tm", offset)
        key_sum = key_sum + back_keys.astype(jnp.float32)
        value_sum = value_sum + back_values.astype(jnp.float32)
    grad_key = exact_rows(token_adapter_input, key_sum)
    grad_value = exact_rows(token_adapter_input, value_sum)
    low_part = (
        low_part + exact_cols(key_sum, key_adapter_out) + exact_cols(value_sum, value_adapter_out)
    )
    grad_query, grad_key, grad_value = lax.psum((grad_query, grad_key, grad_value), ("tm", "rep"))
    low_grad = lax.psum(low_part, ("head", "rep"))
    return (grad_query, grad_key, grad_value, low_grad)


def solution(mesh):
    in_specs = (
        P(("groups", "tm", "rep"), "head"),
        P(("groups", "tm"), "head"),
        P(("groups", "tm"), "head"),
        P(("groups", "tm"), None),
        P(None, "head"),
        P(None, "head"),
        P(None, "head"),
        P(("groups", "tm", "rep"), "head"),
        P(),
    )
    out_specs = (
        P("groups", "head"),
        P("groups", "head"),
        P("groups", "head"),
        P(("groups", "tm"), None),
    )
    return jax.shard_map(
        on_device, mesh=mesh, in_specs=in_specs, out_specs=out_specs, check_vma=False
    )
```

profile of v0, /device:TPU:0, one launch (start us, length us, event | category | flops | bytes accessed | tf_op | source)
XLA Modules:
  0.0 467.3 jit_solution(1070601932986215366)
XLA Ops:
  7.2 1.6 fusion.71
  9.6 7.8 %collective-permute-start.8 = (bf16[256,1280]{1,0:T(8,128)(2,1)S(1)}, bf16[256,1280]{1,0:T(8,128)(2,1)}, u32[]{:S(2)}, u32[]{:S(2)}) collective-permute-start(bf16[256,1280]{1,0:T(8,128)(2,1)S(1)} %fusion.71), channel_id=1, source_target_pairs={{0,12},{1,13},{2,14},{3,15},{16,28},{17,29},{18,30},{19,31}} | collective-permute-start | bytes 1966088 | tf_op jit(solution)/shard_map/ppermute | solution.py:18
  18.4 2.2 collective-permute-start.1
  20.6 2.2 collective-permute-start.2
  23.7 1.8 broadcast_compare_fusion.6
  25.5 1.8 broadcast_compare_fusion.4
  29.9 1.6 fusion.286
  31.5 1.9 broadcast_compare_fusion
  49.8 10.0 %collective-permute-done.2 = bf16[256,1280]{1,0:T(8,128)(2,1)} collective-permute-done((bf16[256,1280]{1,0:T(8,128)(2,1)S(1)}, bf16[256,1280]{1,0:T(8,128)(2,1)}, u32[]{:S(2)}, u32[]{:S(2)}) %collective-permute-start.2) | collective-permute-done | bytes 655392 | tf_op jit(solution)/shard_map/ppermute | solution.py:18
  62.2 11.6 %collective-permute-done.3 = bf16[256,1280]{1,0:T(8,128)(2,1)S(1)} collective-permute-done((bf16[256,1280]{1,0:T(8,128)(2,1)S(1)}, bf16[256,1280]{1,0:T(8,128)(2,1)S(1)}, u32[]{:S(2)}, u32[]{:S(2)}) %collective-permute-start.3) | collective-permute-done | bytes 655392 | tf_op jit(solution)/shard_map/ppermute | solution.py:18
  76.6 14.8 %collective-permute-done.4 = bf16[256,1280]{1,0:T(8,128)(2,1)S(1)} collective-permute-done((bf16[256,1280]{1,0:T(8,128)(2,1)S(1)}, bf16[256,1280]{1,0:T(8,128)(2,1)S(1)}, u32[]{:S(2)}, u32[]{:S(2)}) %collective-permute-start.4) | collective-permute-done | bytes 655392 | tf_op jit(solution)/shard_map/ppermute | solution.py:18
  91.4 15.0 %collective-permute-start.10 = (bf16[256,1280]{1,0:T(8,128)(2,1)S(1)}, bf16[256,1280]{1,0:T(8,128)(2,1)S(1)}, u32[]{:S(2)}, u32[]{:S(2)}) collective-permute-start(bf16[256,1280]{1,0:T(8,128)(2,1)S(1)} %fusion.71), channel_id=1, source_target_pairs={{0,4},{4,8},{8,12},{1,5},{5,9},{9,13},{2,6},{6,10},{10,14},{3,7},{... | collective-permute-start | bytes 1966088 | tf_op jit(solution)/shard_map/ppermute | solution.py:18
  106.5 41.9 %collective-permute-done.5 = bf16[256,1280]{1,0:T(8,128)(2,1)S(1)} collective-permute-done((bf16[256,1280]{1,0:T(8,128)(2,1)S(1)}, bf16[256,1280]{1,0:T(8,128)(2,1)S(1)}, u32[]{:S(2)}, u32[]{:S(2)}) %collective-permute-start.5) | collective-permute-done | bytes 655392 | tf_op jit(solution)/shard_map/ppermute | solution.py:18
  156.4 11.2 %collective-permute-done.11 = bf16[256,1280]{1,0:T(8,128)(2,1)S(1)} collective-permute-done((bf16[256,1280]{1,0:T(8,128)(2,1)S(1)}, bf16[256,1280]{1,0:T(8,128)(2,1)S(1)}, u32[]{:S(2)}, u32[]{:S(2)}) %collective-permute-start.11) | collective-permute-done | bytes 655392 | tf_op jit(solution)/shard_map/ppermute | solution.py:18
  168.5 37.7 %collective-permute-done.12 = bf16[256,1280]{1,0:T(8,128)(2,1)S(1)} collective-permute-done((bf16[256,1280]{1,0:T(8,128)(2,1)S(1)}, bf16[256,1280]{1,0:T(8,128)(2,1)S(1)}, u32[]{:S(2)}, u32[]{:S(2)}) %collective-permute-start.12) | collective-permute-done | bytes 655392 | tf_op jit(solution)/shard_map/ppermute | solution.py:18
  230.2 1.6 fusion.285
  232.5 2.1 collective-permute-start.20
  234.7 2.1 collective-permute-start.19
  236.8 2.2 collective-permute-start.18
  250.7 12.8 %collective-permute-done.19 = bf16[256,1280]{0,1:T(8,128)(2,1)} collective-permute-done((bf16[256,1280]{0,1:T(8,128)(2,1)}, bf16[256,1280]{0,1:T(8,128)(2,1)}, u32[]{:S(2)}, u32[]{:S(2)}) %collective-permute-start.19) | collective-permute-done | bytes 655392 | tf_op jit(solution)/shard_map/ppermute | solution.py:18
  264.1 11.4 %collective-permute-done.18 = bf16[256,1280]{0,1:T(8,128)(2,1)} collective-permute-done((bf16[256,1280]{0,1:T(8,128)(2,1)}, bf16[256,1280]{0,1:T(8,128)(2,1)}, u32[]{:S(2)}, u32[]{:S(2)}) %collective-permute-start.18) | collective-permute-done | bytes 655392 | tf_op jit(solution)/shard_map/ppermute | solution.py:18
  277.5 18.8 %collective-permute-done.16 = bf16[256,1280]{0,1:T(8,128)(2,1)S(1)} collective-permute-done((bf16[256,1280]{0,1:T(8,128)(2,1)S(1)}, bf16[256,1280]{0,1:T(8,128)(2,1)S(1)}, u32[]{:S(2)}, u32[]{:S(2)}) %collective-permute-start.16) | collective-permute-done | bytes 655392 | tf_op jit(solution)/shard_map/ppermute | solution.py:18
  296.3 1.7 collective-permute-start.27
  305.2 7.9 %collective-permute-done.27 = bf16[256,1280]{0,1:T(8,128)(2,1)S(1)} collective-permute-done((bf16[256,1280]{0,1:T(8,128)(2,1)S(1)}, bf16[256,1280]{0,1:T(8,128)(2,1)S(1)}, u32[]{:S(2)}, u32[]{:S(2)}) %collective-permute-start.27) | collective-permute-done | bytes 655392 | tf_op jit(solution)/shard_map/ppermute | solution.py:18
  313.9 2.4 convert_add_fusion.1
  316.3 1.6 convolution_bitcast_fusion.1
  317.9 6.0 %collective-permute-done.26 = bf16[256,1280]{0,1:T(8,128)(2,1)S(1)} collective-permute-done((bf16[256,1280]{0,1:T(8,128)(2,1)S(1)}, bf16[256,1280]{0,1:T(8,128)(2,1)S(1)}, u32[]{:S(2)}, u32[]{:S(2)}) %collective-permute-start.26) | collective-permute-done | bytes 655392 | tf_op jit(solution)/shard_map/ppermute | solution.py:18
  323.9 35.3 %collective-permute-done.24 = bf16[256,1280]{0,1:T(8,128)(2,1)S(1)} collective-permute-done((bf16[256,1280]{0,1:T(8,128)(2,1)S(1)}, bf16[256,1280]{0,1:T(8,128)(2,1)S(1)}, u32[]{:S(2)}, u32[]{:S(2)}) %collective-permute-start.24) | collective-permute-done | bytes 655392 | tf_op jit(solution)/shard_map/ppermute | solution.py:18
  364.1 1.9 convolution_add_fusion.3
  366.0 58.2 %all-reduce.6.cloned.1.call-done = (f32[128,1280]{1,0:T(8,128)}, f32[128,1280]{0,1:T(8,128)}, f32[128,1280]{0,1:T(8,128)}) async-done(((f32[128,1280]{1,0:T(8,128)}, f32[128,1280]{0,1:T(8,128)}, f32[128,1280]{0,1:T(8,128)}), (f32[128,1280]{1,0:T(8,128)}, f32[128,1280]{0,1:T(8,128)}, f32[128,1280]{0,1:T(8,128)})) %all-reduce.6.cloned.1.call-update) | async-done | bytes 1966096 | tf_op jit(solution)/shard_map/psum | solution.py:169
  424.2 2.3 copy.33
  427.5 30.9 %all-reduce.4.cloned.1.call-done = f32[256,128]{1,0:T(8,128)} async-done(((f32[256,128]{1,0:T(8,128)}), f32[256,128]{1,0:T(8,128)}) %all-reduce.4.cloned.1.call-update) | async-done | bytes 131088 | tf_op jit(solution)/shard_map/psum | solution.py:170
  (230 shorter events, 89.7 us)
Async XLA Ops:
  7.2 417.0 %all-reduce.6.cloned.1.call-start = ((), (), s32[]{:S(2)}) async-start(), calls=%async_computation.1 | async-start | bytes 3932160 | tf_op jit(solution)/shard_map/psum | solution.py:169
  8.9 66.4 %collective-permute-start.7 = (bf16[256,1280]{1,0:T(8,128)(2,1)S(1)}, bf16[256,1280]{1,0:T(8,128)(2,1)S(1)}, u32[]{:S(2)}, u32[]{:S(2)}) collective-permute-start(bf16[256,1280]{1,0:T(8,128)(2,1)S(1)} %fusion.71), channel_id=1, source_target_pairs={} | collective-permute-start | bytes 1966088 | tf_op jit(solution)/shard_map/ppermute | solution.py:18
  9.6 141.6 %collective-permute-start.8 = (bf16[256,1280]{1,0:T(8,128)(2,1)S(1)}, bf16[256,1280]{1,0:T(8,128)(2,1)}, u32[]{:S(2)}, u32[]{:S(2)}) collective-permute-start(bf16[256,1280]{1,0:T(8,128)(2,1)S(1)} %fusion.71), channel_id=1, source_target_pairs={{0,12},{1,13},{2,14},{3,15},{16,28},{17,29},{18,30},{19,31}} | collective-permute-start | bytes 1966088 | tf_op jit(solution)/shard_map/ppermute | solution.py:18
  17.7 28.2 %collective-permute-start = (bf16[256,1280]{1,0:T(8,128)(2,1)S(1)}, bf16[256,1280]{1,0:T(8,128)(2,1)S(1)}, u32[]{:S(2)}, u32[]{:S(2)}) collective-permute-start(bf16[256,1280]{1,0:T(8,128)(2,1)S(1)} %fusion.70), channel_id=1, source_target_pairs={} | collective-permute-start | bytes 1966088 | tf_op jit(solution)/shard_map/ppermute | solution.py:18
  18.4 28.9 %collective-permute-start.1 = (bf16[256,1280]{1,0:T(8,128)(2,1)S(1)}, bf16[256,1280]{1,0:T(8,128)(2,1)}, u32[]{:S(2)}, u32[]{:S(2)}) collective-permute-start(bf16[256,1280]{1,0:T(8,128)(2,1)S(1)} %fusion.70), channel_id=1, source_target_pairs={{0,12},{1,13},{2,14},{3,15},{16,28},{17,29},{18,30},{19,31}} | collective-permute-start | bytes 1966088 | tf_op jit(solution)/shard_map/ppermute | solution.py:18
  20.6 39.2 %collective-permute-start.2 = (bf16[256,1280]{1,0:T(8,128)(2,1)S(1)}, bf16[256,1280]{1,0:T(8,128)(2,1)}, u32[]{:S(2)}, u32[]{:S(2)}) collective-permute-start(bf16[256,1280]{1,0:T(8,128)(2,1)S(1)} %fusion.70), channel_id=1, source_target_pairs={{0,8},{4,12},{1,9},{5,13},{2,10},{6,14},{3,11},{7,15},{16,24},{20,... | collective-permute-start | bytes 1966088 | tf_op jit(solution)/shard_map/ppermute | solution.py:18
  45.9 27.9 %collective-permute-start.3 = (bf16[256,1280]{1,0:T(8,128)(2,1)S(1)}, bf16[256,1280]{1,0:T(8,128)(2,1)S(1)}, u32[]{:S(2)}, u32[]{:S(2)}) collective-permute-start(bf16[256,1280]{1,0:T(8,128)(2,1)S(1)} %fusion.70), channel_id=1, source_target_pairs={{0,4},{4,8},{8,12},{1,5},{5,9},{9,13},{2,6},{6,10},{10,14},{3,7},{... | collective-permute-start | bytes 1966088 | tf_op jit(solution)/shard_map/ppermute | solution.py:18
  47.3 107.3 %collective-permute-start.9 = (bf16[256,1280]{1,0:T(8,128)(2,1)S(1)}, bf16[256,1280]{1,0:T(8,128)(2,1)S(1)}, u32[]{:S(2)}, u32[]{:S(2)}) collective-permute-start(bf16[256,1280]{1,0:T(8,128)(2,1)S(1)} %fusion.71), channel_id=1, source_target_pairs={{0,8},{4,12},{1,9},{5,13},{2,10},{6,14},{3,11},{7,15},{16,24},{20,... | collective-permute-start | bytes 1966088 | tf_op jit(solution)/shard_map/ppermute | solution.py:18
  59.8 31.6 %collective-permute-start.4 = (bf16[256,1280]{1,0:T(8,128)(2,1)S(1)}, bf16[256,1280]{1,0:T(8,128)(2,1)S(1)}, u32[]{:S(2)}, u32[]{:S(2)}) collective-permute-start(bf16[256,1280]{1,0:T(8,128)(2,1)S(1)} %fusion.70), channel_id=1, source_target_pairs={{4,0},{8,4},{12,8},{5,1},{9,5},{13,9},{6,2},{10,6},{14,10},{7,3},{... | collective-permute-start | bytes 1966088 | tf_op jit(solution)/shard_map/ppermute | solution.py:18
  73.8 74.5 %collective-permute-start.5 = (bf16[256,1280]{1,0:T(8,128)(2,1)S(1)}, bf16[256,1280]{1,0:T(8,128)(2,1)S(1)}, u32[]{:S(2)}, u32[]{:S(2)}) collective-permute-start(bf16[256,1280]{1,0:T(8,128)(2,1)S(1)} %fusion.70), channel_id=1, source_target_pairs={{8,0},{12,4},{9,1},{13,5},{10,2},{14,6},{11,3},{15,7},{24,16},{28,... | collective-permute-start | bytes 1966088 | tf_op jit(solution)/shard_map/ppermute | solution.py:18
  75.2 74.5 %collective-permute-start.6 = (bf16[256,1280]{1,0:T(8,128)(2,1)S(1)}, bf16[256,1280]{1,0:T(8,128)(2,1)S(1)}, u32[]{:S(2)}, u32[]{:S(2)}) collective-permute-start(bf16[256,1280]{1,0:T(8,128)(2,1)S(1)} %fusion.70), channel_id=1, source_target_pairs={{12,0},{13,1},{14,2},{15,3},{28,16},{29,17},{30,18},{31,19}} | collective-permute-start | bytes 1966088 | tf_op jit(solution)/shard_map/ppermute | solution.py:18
  91.4 64.1 %collective-permute-start.10 = (bf16[256,1280]{1,0:T(8,128)(2,1)S(1)}, bf16[256,1280]{1,0:T(8,128)(2,1)S(1)}, u32[]{:S(2)}, u32[]{:S(2)}) collective-permute-start(bf16[256,1280]{1,0:T(8,128)(2,1)S(1)} %fusion.71), channel_id=1, source_target_pairs={{0,4},{4,8},{8,12},{1,5},{5,9},{9,13},{2,6},{6,10},{10,14},{3,7},{... | collective-permute-start | bytes 1966088 | tf_op jit(solution)/shard_map/ppermute | solution.py:18
  148.4 19.2 %collective-permute-start.11 = (bf16[256,1280]{1,0:T(8,128)(2,1)S(1)}, bf16[256,1280]{1,0:T(8,128)(2,1)S(1)}, u32[]{:S(2)}, u32[]{:S(2)}) collective-permute-start(bf16[256,1280]{1,0:T(8,128)(2,1)S(1)} %fusion.71), channel_id=1, source_target_pairs={{4,0},{8,4},{12,8},{5,1},{9,5},{13,9},{6,2},{10,6},{14,10},{7,3},{... | collective-permute-start | bytes 1966088 | tf_op jit(solution)/shard_map/ppermute | solution.py:18
  149.7 56.5 %collective-permute-start.12 = (bf16[256,1280]{1,0:T(8,128)(2,1)S(1)}, bf16[256,1280]{1,0:T(8,128)(2,1)S(1)}, u32[]{:S(2)}, u32[]{:S(2)}) collective-permute-start(bf16[256,1280]{1,0:T(8,128)(2,1)S(1)} %fusion.71), channel_id=1, source_target_pairs={{8,0},{12,4},{9,1},{13,5},{10,2},{14,6},{11,3},{15,7},{24,16},{28,... | collective-permute-start | bytes 1966088 | tf_op jit(solution)/shard_map/ppermute | solution.py:18
  151.1 56.3 %collective-permute-start.13 = (bf16[256,1280]{1,0:T(8,128)(2,1)S(1)}, bf16[256,1280]{1,0:T(8,128)(2,1)S(1)}, u32[]{:S(2)}, u32[]{:S(2)}) collective-permute-start(bf16[256,1280]{1,0:T(8,128)(2,1)S(1)} %fusion.71), channel_id=1, source_target_pairs={{12,0},{13,1},{14,2},{15,3},{28,16},{29,17},{30,18},{31,19}} | collective-permute-start | bytes 1966088 | tf_op jit(solution)/shard_map/ppermute | solution.py:18
  231.9 14.3 %collective-permute-start.21 = (bf16[256,1280]{0,1:T(8,128)(2,1)S(1)}, bf16[256,1280]{0,1:T(8,128)(2,1)S(1)}, u32[]{:S(2)}, u32[]{:S(2)}) collective-permute-start(bf16[256,1280]{0,1:T(8,128)(2,1)S(1)} %get-tuple-element.29), channel_id=1, source_target_pairs={} | collective-permute-start | bytes 1966088 | tf_op jit(solution)/shard_map/ppermute | solution.py:18
  232.5 16.8 %collective-permute-start.20 = (bf16[256,1280]{0,1:T(8,128)(2,1)}, bf16[256,1280]{0,1:T(8,128)(2,1)}, u32[]{:S(2)}, u32[]{:S(2)}) collective-permute-start(bf16[256,1280]{0,1:T(8,128)(2,1)} %get-tuple-element.30), channel_id=1, source_target_pairs={{0,12},{1,13},{2,14},{3,15},{16,28},{17,29},{18,30},{19,31}} | collective-permute-start | bytes 1966088 | tf_op jit(solution)/shard_map/ppermute | solution.py:18
  234.7 28.7 %collective-permute-start.19 = (bf16[256,1280]{0,1:T(8,128)(2,1)}, bf16[256,1280]{0,1:T(8,128)(2,1)}, u32[]{:S(2)}, u32[]{:S(2)}) collective-permute-start(bf16[256,1280]{0,1:T(8,128)(2,1)} %get-tuple-element.31), channel_id=1, source_target_pairs={{0,8},{4,12},{1,9},{5,13},{2,10},{6,14},{3,11},{7,15},{16,24},{20,... | collective-permute-start | bytes 1966088 | tf_op jit(solution)/shard_map/ppermute | solution.py:18
  236.8 38.7 %collective-permute-start.18 = (bf16[256,1280]{0,1:T(8,128)(2,1)}, bf16[256,1280]{0,1:T(8,128)(2,1)}, u32[]{:S(2)}, u32[]{:S(2)}) collective-permute-start(bf16[256,1280]{0,1:T(8,128)(2,1)} %get-tuple-element.32), channel_id=1, source_target_pairs={{0,4},{4,8},{8,12},{1,5},{5,9},{9,13},{2,6},{6,10},{10,14},{3,7},{... | collective-permute-start | bytes 1966088 | tf_op jit(solution)/shard_map/ppermute | solution.py:18
  239.0 37.2 %collective-permute-start.17 = (bf16[256,1280]{0,1:T(8,128)(2,1)}, bf16[256,1280]{0,1:T(8,128)(2,1)}, u32[]{:S(2)}, u32[]{:S(2)}) collective-permute-start(bf16[256,1280]{0,1:T(8,128)(2,1)} %get-tuple-element.33), channel_id=1, source_target_pairs={{4,0},{8,4},{12,8},{5,1},{9,5},{13,9},{6,2},{10,6},{14,10},{7,3},{... | collective-permute-start | bytes 1966088 | tf_op jit(solution)/shard_map/ppermute | solution.py:18
  247.0 49.3 %collective-permute-start.16 = (bf16[256,1280]{0,1:T(8,128)(2,1)S(1)}, bf16[256,1280]{0,1:T(8,128)(2,1)S(1)}, u32[]{:S(2)}, u32[]{:S(2)}) collective-permute-start(bf16[256,1280]{0,1:T(8,128)(2,1)S(1)} %get-tuple-element.34), channel_id=1, source_target_pairs={{8,0},{12,4},{9,1},{13,5},{10,2},{14,6},{11,3},{15,7},{24,16},{28,... | collective-permute-start | bytes 1966088 | tf_op jit(solution)/shard_map/ppermute | solution.py:18
  249.4 50.6 %collective-permute-start.15 = (bf16[256,1280]{0,1:T(8,128)(2,1)S(1)}, bf16[256,1280]{0,1:T(8,128)(2,1)S(1)}, u32[]{:S(2)}, u32[]{:S(2)}) collective-permute-start(bf16[256,1280]{0,1:T(8,128)(2,1)S(1)} %get-tuple-element.35), channel_id=1, source_target_pairs={{12,0},{13,1},{14,2},{15,3},{28,16},{29,17},{30,18},{31,19}} | collective-permute-start | bytes 1966088 | tf_op jit(solution)/shard_map/ppermute | solution.py:18
  263.4 37.9 %collective-permute-start.14 = (bf16[256,1280]{0,1:T(8,128)(2,1)S(1)}, bf16[256,1280]{0,1:T(8,128)(2,1)S(1)}, u32[]{:S(2)}, u32[]{:S(2)}) collective-permute-start(bf16[256,1280]{0,1:T(8,128)(2,1)S(1)} %get-tuple-element.28), channel_id=1, source_target_pairs={} | collective-permute-start | bytes 1966088 | tf_op jit(solution)/shard_map/ppermute | solution.py:18
  275.5 27.1 %collective-permute-start.29 = (bf16[256,1280]{0,1:T(8,128)(2,1)S(1)}, bf16[256,1280]{0,1:T(8,128)(2,1)S(1)}, u32[]{:S(2)}, u32[]{:S(2)}) collective-permute-start(bf16[256,1280]{0,1:T(8,128)(2,1)S(1)} %get-tuple-element.21), channel_id=1, source_target_pairs={} | collective-permute-start | bytes 1966088 | tf_op jit(solution)/shard_map/ppermute | solution.py:18
  276.2 27.7 %collective-permute-start.28 = (bf16[256,1280]{0,1:T(8,128)(2,1)S(1)}, bf16[256,1280]{0,1:T(8,128)(2,1)S(1)}, u32[]{:S(2)}, u32[]{:S(2)}) collective-permute-start(bf16[256,1280]{0,1:T(8,128)(2,1)S(1)} %get-tuple-element.22), channel_id=1, source_target_pairs={{0,12},{1,13},{2,14},{3,15},{16,28},{17,29},{18,30},{19,31}} | collective-permute-start | bytes 1966088 | tf_op jit(solution)/shard_map/ppermute | solution.py:18
  296.3 16.9 %collective-permute-start.27 = (bf16[256,1280]{0,1:T(8,128)(2,1)S(1)}, bf16[256,1280]{0,1:T(8,128)(2,1)S(1)}, u32[]{:S(2)}, u32[]{:S(2)}) collective-permute-start(bf16[256,1280]{0,1:T(8,128)(2,1)S(1)} %get-tuple-element.23), channel_id=1, source_target_pairs={{0,8},{4,12},{1,9},{5,13},{2,10},{6,14},{3,11},{7,15},{16,24},{20,... | collective-permute-start | bytes 1966088 | tf_op jit(solution)/shard_map/ppermute | solution.py:18
  300.0 23.9 %collective-permute-start.26 = (bf16[256,1280]{0,1:T(8,128)(2,1)S(1)}, bf16[256,1280]{0,1:T(8,128)(2,1)S(1)}, u32[]{:S(2)}, u32[]{:S(2)}) collective-permute-start(bf16[256,1280]{0,1:T(8,128)(2,1)S(1)} %get-tuple-element.24), channel_id=1, source_target_pairs={{0,4},{4,8},{8,12},{1,5},{5,9},{9,13},{2,6},{6,10},{10,14},{3,7},{... | collective-permute-start | bytes 1966088 | tf_op jit(solution)/shard_map/ppermute | solution.py:18
  301.3 22.6 %collective-permute-start.25 = (bf16[256,1280]{0,1:T(8,128)(2,1)S(1)}, bf16[256,1280]{0,1:T(8,128)(2,1)S(1)}, u32[]{:S(2)}, u32[]{:S(2)}) collective-permute-start(bf16[256,1280]{0,1:T(8,128)(2,1)S(1)} %get-tuple-element.25), channel_id=1, source_target_pairs={{4,0},{8,4},{12,8},{5,1},{9,5},{13,9},{6,2},{10,6},{14,10},{7,3},{... | collective-permute-start | bytes 1966088 | tf_op jit(solution)/shard_map/ppermute | solution.py:18
  302.6 56.5 %collective-permute-start.24 = (bf16[256,1280]{0,1:T(8,128)(2,1)S(1)}, bf16[256,1280]{0,1:T(8,128)(2,1)S(1)}, u32[]{:S(2)}, u32[]{:S(2)}) collective-permute-start(bf16[256,1280]{0,1:T(8,128)(2,1)S(1)} %get-tuple-element.26), channel_id=1, source_target_pairs={{8,0},{12,4},{9,1},{13,5},{10,2},{14,6},{11,3},{15,7},{24,16},{28,... | collective-permute-start | bytes 1966088 | tf_op jit(solution)/shard_map/ppermute | solution.py:18
  303.9 55.2 %collective-permute-start.23 = (bf16[256,1280]{0,1:T(8,128)(2,1)S(1)}, bf16[256,1280]{0,1:T(8,128)(2,1)S(1)}, u32[]{:S(2)}, u32[]{:S(2)}) collective-permute-start(bf16[256,1280]{0,1:T(8,128)(2,1)S(1)} %get-tuple-element.27), channel_id=1, source_target_pairs={{12,0},{13,1},{14,2},{15,3},{28,16},{29,17},{30,18},{31,19}} | collective-permute-start | bytes 1966088 | tf_op jit(solution)/shard_map/ppermute | solution.py:18
  313.2 46.0 %collective-permute-start.22 = (bf16[256,1280]{0,1:T(8,128)(2,1)S(1)}, bf16[256,1280]{0,1:T(8,128)(2,1)S(1)}, u32[]{:S(2)}, u32[]{:S(2)}) collective-permute-start(bf16[256,1280]{0,1:T(8,128)(2,1)S(1)} %get-tuple-element.20), channel_id=1, source_target_pairs={} | collective-permute-start | bytes 1966088 | tf_op jit(solution)/shard_map/ppermute | solution.py:18
  361.5 96.9 %all-reduce.4.cloned.1.call-start = ((), (), s32[]{:S(2)}) async-start(), calls=%async_computation | async-start | bytes 262144 | tf_op jit(solution)/shard_map/psum | solution.py:170
  (31 other events, 208.3 us)
Sparse Core Ops, SparseCore 0:
  361.6 62.5 all-reduce.5
  427.2 31.1 all-reduce.3
where the time goes:
time: 473 us; the launch traced here: 467 us
  waiting for transfers between devices  309 us (65%)
  starting transfers between devices  60.5 us (13%)
  matrix products  38.1 us (8%)
  local copies, waits for them, and re-layouts  29.3 us (6%)
  between operations  15.5 us (3%)
  other arithmetic  14.6 us (3%)
    ppermute x30, waiting for transfers between devices, shifted_2(): return lax.ppermute(block, axis, route)  220 us
    ppermute x30, starting transfers between devices, shifted_2(): return lax.ppermute(block, axis, route)  60.4 us
    psum x1, waiting for transfers between devices, on_device(): lax.psum((grad_query, grad_key, grad_value), ('tm', 'rep'))  58.2 us
    psum x1, waiting for transfers between devices, on_device(): low_grad = lax.psum(low_part, ('head', 'rep'))  30.9 us
    unnamed x101, local copies, waits for them, and re-layouts  27.3 us
    dot_general x21, matrix products, contract_rows(): lax.dot_general(left, right, (((0,), (0,)), ((), ())), preferred_element_...  9.88 us
    dot_general x21, matrix products, contract_cols(): lax.dot_general(left, right, (((1,), (1,)), ((), ())), preferred_element_...  9.76 us
  transfers between devices with their start and end apart: 32, of which 15 were waited for; matrix products, arithmetic and copies ran while one was open for 11% of the time, Pallas kernels for 0%

commit v1 on v0

v1 whole, which is shorter than its diff:
```python
import functools

import jax
import jax.numpy as jnp
from jax import lax
from jax.experimental import pallas as pl
from jax.experimental.pallas import tpu as pltpu
from jax.sharding import PartitionSpec as P

DH = 128
NEAR = 1
REACH = 4
SCALE = DH ** (-0.5)
F32 = jnp.float32
BF16 = jnp.bfloat16


def dot_nn(left, right):
    return lax.dot_general(left, right, (((1,), (0,)), ((), ())), preferred_element_type=F32)


def dot_nt(left, right):
    return lax.dot_general(left, right, (((1,), (1,)), ((), ())), preferred_element_type=F32)


def dot_tn(left, right):
    return lax.dot_general(left, right, (((0,), (0,)), ((), ())), preferred_element_type=F32)


def routes(count):
    found = []
    for d in range(1, min(REACH, count - 1) + 1):
        if 2 * d >= count:
            found.append((d, (-d, d)))
        else:
            found.append((d, (-d,)))
            found.append((d, (d,)))
    return found


def pairs(count, offsets):
    return [(i + o, i) for o in offsets for i in range(count) if 0 <= i + o < count]


def swap(block, axis):
    return lax.ppermute(block, axis, [(0, 1), (1, 0)])


def attention_kernel(
    blocks, bias_ref, fq_ref, do_ref, fk_ref, fv_ref, t_ref, tr_ref, tt_ref, aq_ref, ak_ref, av_ref, *refs
):
    k_refs = refs[:blocks]
    v_refs = refs[blocks : 2 * blocks]
    gq_ref, gk_ref, gv_ref, lowq_ref, low_ref = refs[2 * blocks :]
    rows = fq_ref.shape[0]

    @pl.when(pl.program_id(0) == 0)
    def _():
        lowq_ref[...] = jnp.zeros_like(lowq_ref)
        low_ref[...] = jnp.zeros_like(low_ref)

    aq, ak, av = aq_ref[...], ak_ref[...], av_ref[...]
    query = (fq_ref[...].astype(F32) + dot_nn(tr_ref[...], aq)).astype(BF16)
    do = do_ref[...]
    own_k = (fk_ref[...].astype(F32) + dot_nn(t_ref[...], ak)).astype(BF16)
    own_v = (fv_ref[...].astype(F32) + dot_nn(t_ref[...], av)).astype(BF16)
    keys = [own_k[:rows], own_k[rows:]] + [ref[...] for ref in k_refs]
    values = [own_v[:rows], own_v[rows:]] + [ref[...] for ref in v_refs]
    count = len(keys)
    scores = [dot_nt(keys[b], query) * SCALE + bias_ref[b] for b in range(count)]
    top = functools.reduce(jnp.maximum, scores)
    top = jnp.max(top, axis=0, keepdims=True)
    shifted = [jnp.exp(s - top) for s in scores]
    total = jnp.sum(functools.reduce(jnp.add, shifted), axis=0, keepdims=True)
    inverse = 1.0 / total
    probs = [s * inverse for s in shifted]
    lows = [p.astype(BF16) for p in probs]
    attended = functools.reduce(jnp.add, [dot_tn(lows[b], values[b]) for b in range(count)])
    attended = attended.astype(BF16).astype(F32)
    delta = jnp.sum((do.astype(F32) * attended).T, axis=0, keepdims=True)
    grads = [
        (probs[b] * (dot_nt(values[b], do) - delta)).astype(BF16) for b in range(count)
    ]
    dq = functools.reduce(jnp.add, [dot_tn(grads[b], keys[b]) for b in range(count)])
    dq = (dq * SCALE).astype(BF16)
    gq_ref[...] = dot_tn(tr_ref[...], dq)
    lowq_ref[...] += dot_nt(dq, aq)
    both = jnp.concatenate([ak, av], axis=1)
    for b in range(count):
        dk = (dot_nn(grads[b], query) * SCALE).astype(BF16)
        dv = dot_nn(lows[b], do).astype(BF16)
        part = jnp.concatenate([dk, dv], axis=1)
        low_ref[b * rows : (b + 1) * rows, :] += dot_nt(part, both)
        out = dot_nn(tt_ref[:, b * rows : (b + 1) * rows], part)
        if b == 0:
            total_part = out
        else:
            total_part += out
    gk_ref[...] = total_part[:, :DH]
    gv_ref[...] = total_part[:, DH:]


def attention(bias, fq, do, fk, fv, t, tr, tt, aq, ak, av, payloads):
    rows, width = fq.shape
    heads = width // DH
    rank = t.shape[1]
    blocks = len(payloads)
    count = blocks + 2

    def col(r):
        return pl.BlockSpec((r, DH), lambda h: (0, h))

    def whole(shape):
        return pl.BlockSpec(shape, lambda h: (0, 0))

    return pl.pallas_call(
        functools.partial(attention_kernel, blocks),
        grid=(heads,),
        out_shape=[
            jax.ShapeDtypeStruct((rank, width), F32),
            jax.ShapeDtypeStruct((rank, width), F32),
            jax.ShapeDtypeStruct((rank, width), F32),
            jax.ShapeDtypeStruct((rows, rank), F32),
            jax.ShapeDtypeStruct((count * rows, rank), F32),
        ],
        in_specs=[pl.BlockSpec(memory_space=pltpu.SMEM)]
        + [col(rows), col(rows), col(2 * rows), col(2 * rows)]
        + [whole(t.shape), whole(tr.shape), whole(tt.shape)]
        + [col(rank)] * 3
        + [col(rows)] * blocks
        + [pl.BlockSpec((rows, DH), lambda h: (0, heads + h))] * blocks,
        out_specs=[col(rank)] * 3 + [whole((rows, rank)), whole((count * rows, rank))],
        compiler_params=pltpu.CompilerParams(vmem_limit_bytes=32 * 1024 * 1024),
    )(bias, fq, do, fk, fv, t, tr, tt, aq, ak, av, *payloads, *payloads)


def sum_rows(part, frame_idx, half_idx, frames):
    rows, width = part.shape
    half = width // 2
    keep = lax.dynamic_slice_in_dim(part, half_idx * half, half, 1)
    give = lax.dynamic_slice_in_dim(part, (1 - half_idx) * half, half, 1)
    mine = keep + swap(give, "rep")
    if frames & (frames - 1) or rows % frames or frames > REACH + 1:
        total = lax.psum(mine, "tm").astype(BF16)
    else:
        chunk = rows // frames
        low = mine.astype(BF16)
        acc = lax.dynamic_slice_in_dim(mine, frame_idx * chunk, chunk, 0)
        for m in range(1, frames):
            give = lax.dynamic_slice_in_dim(low, (frame_idx ^ m) * chunk, chunk, 0)
            acc = acc + lax.ppermute(give, "tm", [(i, i ^ m) for i in range(frames)]).astype(F32)
        acc = acc.astype(BF16)
        total = jnp.zeros((rows, half), BF16)
        total = lax.dynamic_update_slice_in_dim(total, acc, frame_idx * chunk, 0)
        for m in range(1, frames):
            got = lax.ppermute(acc, "tm", [(i, i ^ m) for i in range(frames)])
            total = lax.dynamic_update_slice_in_dim(total, got, (frame_idx ^ m) * chunk, 0)
    other = swap(total, "rep")
    first = jnp.where(half_idx == 0, total, other)
    second = jnp.where(half_idx == 0, other, total)
    return jnp.concatenate([first, second], axis=1).astype(F32)


def on_device(
    frozen_query,
    frozen_key,
    frozen_value,
    token_adapter_input,
    query_adapter_out,
    key_adapter_out,
    value_adapter_out,
    out_grad,
    band_width,
):
    rows, width = frozen_query.shape
    rank = token_adapter_input.shape[1]
    frames = band_width.shape[0]
    frame_idx = lax.axis_index("tm")
    half_idx = lax.axis_index("rep")
    t = token_adapter_input
    tr = lax.dynamic_slice_in_dim(t, half_idx * rows, rows, 0)

    def tile_rows_of(frozen, adapter):
        own = lax.dynamic_slice_in_dim(frozen, half_idx * rows, rows, 0)
        return (own.astype(F32) + dot_nn(tr, adapter)).astype(BF16)

    payload = jnp.concatenate(
        [tile_rows_of(frozen_key, key_adapter_out), tile_rows_of(frozen_value, value_adapter_out), tr],
        axis=1,
    )

    frame_ids = jnp.arange(frames)
    band_row = jnp.sum(jnp.where((frame_ids == frame_idx)[:, None], band_width, 0), axis=0)

    def band_at(offsets):
        seen = functools.reduce(jnp.logical_or, [frame_ids == frame_idx + o for o in offsets])
        return jnp.sum(jnp.where(seen, band_row, 0))

    own_band = band_at((0,))
    allowed = [jnp.abs(half_idx - tile) < own_band for tile in range(2)]
    payloads = []
    plan = routes(frames)
    for d, offsets in plan:
        got = lax.ppermute(payload, "tm", pairs(frames, offsets))
        band = band_at(offsets)
        payloads.append(got)
        allowed.append(band > 0)
        if d <= NEAR:
            payloads.append(swap(got, "rep"))
            allowed.append(band > 1)
    bias = jnp.where(jnp.stack(allowed), 0.0, -jnp.inf).astype(F32)
    tt = jnp.concatenate([t] + [p[:, 2 * width :] for p in payloads], axis=0).T

    gq, gk, gv, low_q, low_b = attention(
        bias, frozen_query, out_grad, frozen_key, frozen_value, t, tr, tt,
        query_adapter_out, key_adapter_out, value_adapter_out, payloads,
    )

    own = low_b[: 2 * rows]
    same = lax.dynamic_slice_in_dim(own, half_idx * rows, rows, 0) + low_q
    other = lax.dynamic_slice_in_dim(own, (1 - half_idx) * rows, rows, 0)
    start = 2 * rows
    for d, offsets in plan:
        size = 2 * rows if d <= NEAR else rows
        back = [(target, source) for source, target in pairs(frames, offsets)]
        got = lax.ppermute(low_b[start : start + size], "tm", back)
        start += size
        same = same + got[:rows]
        if d <= NEAR:
            other = other + got[rows:]
    low = jnp.where(
        half_idx == 0,
        jnp.concatenate([same, other], axis=0),
        jnp.concatenate([other, same], axis=0),
    )
    low = low + swap(low, "rep")
    low = low + swap(low, "head")

    grads = sum_rows(jnp.concatenate([gq, gk, gv], axis=0), frame_idx, half_idx, frames)
    return grads[:rank], grads[rank : 2 * rank], grads[2 * rank :], low


def solution(mesh):
    in_specs = (
        P(("groups", "tm", "rep"), "head"),
        P(("groups", "tm"), "head"),
        P(("groups", "tm"), "head"),
        P(("groups", "tm"), None),
        P(None, "head"),
        P(None, "head"),
        P(None, "head"),
        P(("groups", "tm", "rep"), "head"),
        P(),
    )
    out_specs = (
        P("groups", "head"),
        P("groups", "head"),
        P("groups", "head"),
        P(("groups", "tm"), None),
    )
    return jax.shard_map(
        on_device, mesh=mesh, in_specs=in_specs, out_specs=out_specs, check_vma=False
    )
```

time: 473 us -> 179 us (0.38)
  waiting for transfers between devices: 309 us -> 63 us
  matrix products: 38.1 us -> 2.65 us
  Pallas kernels: 0 us -> 30.4 us
  starting transfers between devices: 60.5 us -> 36.4 us
  other arithmetic: 14.6 us -> 3 us
  between operations: 15.5 us -> 6.27 us
  local copies, waits for them, and re-layouts: 29.3 us -> 36 us
    ppermute x30 -> x20, waiting for transfers between devices: 220 us -> 63 us  [the longest x4 43.2 us: on_device(): got = lax.ppermute(payload, 'tm', pairs(frames, offsets))]
    psum x2 -> x0, waiting for transfers between devices: 89 us -> none  [the longest x1 58.2 us: on_device(): lax.psum((grad_query, grad_key, grad_value), ('tm', 'rep'))]
    dot_general x69 -> x2, matrix products: 38.1 us -> 2.65 us  [dot_nn(): lax.dot_general(left, right, (((1,), (0,)), ((), ())), preferred_element_...]
    pallas_call x0 -> x1, Pallas kernels: none -> 30.4 us  [attention(): pl.pallas_call(functools.partial(attention_kernel, blocks), grid=(heads,)...]
    ppermute x30 -> x20, starting transfers between devices: 60.4 us -> 36.4 us  [the longest x4 13.3 us: on_device(): got = lax.ppermute(low_b[start:start + size], 'tm', back)]
    slice x2 -> x15, local copies, waits for them, and re-layouts: 1.96 us -> 14.6 us  [the longest x12 13.3 us: on_device(): tt = jnp.concatenate([t] + [p[:, 2 * width:] for p in payloads], axis=0).T]
    unnamed x101 -> x37, local copies, waits for them, and re-layouts: 27.3 us -> 17.8 us
    lt x4 -> x0, other arithmetic: 6.75 us -> none  [on_device(): allowed_blocks.append(jnp.abs(half_idx - frame_tile) < reach_band)]
  transfers between devices with their start and end apart: 32 -> 20, of which waited for: 15 -> 10; matrix products, arithmetic and copies ran while one was open for 11% -> 9% of each run, Pallas kernels for 0% -> 0%
where the time goes in v1:
time: 179 us; the launch traced here: 178 us
  waiting for transfers between devices  63 us (35%)
  starting transfers between devices  36.4 us (20%)
  local copies, waits for them, and re-layouts  36 us (20%)
  Pallas kernels  30.4 us (17%)
  between operations  6.27 us (4%)
  other arithmetic  3 us (2%)
  matrix products  2.65 us (1%)
    ppermute x4, waiting for transfers between devices, on_device(): got = lax.ppermute(payload, 'tm', pairs(frames, offsets))  43.2 us
    pallas_call x1, Pallas kernels, attention(): pl.pallas_call(functools.partial(attention_kernel, blocks), grid=(heads,)...  30.4 us
    unnamed x37, local copies, waits for them, and re-layouts  17.8 us
    ppermute x4, starting transfers between devices, on_device(): got = lax.ppermute(low_b[start:start + size], 'tm', back)  13.3 us
    slice x12, local copies, waits for them, and re-layouts, on_device(): tt = jnp.concatenate([t] + [p[:, 2 * width:] for p in payloads], axis=0).T  13.3 us
    ppermute x4, starting transfers between devices, on_device(): got = lax.ppermute(payload, 'tm', pairs(frames, offsets))  13.2 us
    ppermute x6, waiting for transfers between devices, swap(): return lax.ppermute(block, axis, [(0, 1), (1, 0)])  8.16 us
    ppermute x3, waiting for transfers between devices, sum_rows(): lax.ppermute(give, 'tm', [(i, i ^ m) for i in range(frames)]).astype(F32)  8.13 us
  transfers between devices with their start and end apart: 20, of which 10 were waited for; matrix products, arithmetic and copies ran while one was open for 9% of the time, Pallas kernels for 0%

profile of v1, /device:TPU:0, one launch (start us, length us, event | category | flops | bytes accessed | tf_op | source)
XLA Modules:
  0.0 177.7 jit_solution(12386552740702204350)
XLA Ops:
  5.1 5.0 %collective-permute-start = (bf16[128,2688]{1,0:T(8,128)(2,1)}, bf16[128,2688]{1,0:T(8,128)(2,1)S(1)}, u32[]{:S(2)}, u32[]{:S(2)}) collective-permute-start(bf16[128,2688]{1,0:T(8,128)(2,1)} %pad_maximum_fusion), channel_id=1, source_target_pairs={{0,4},{4,8},{8,12},{1,5},{5,9},{9,13},{2,6},{6,10},{10,14},{3,7},{... | collective-permute-start | bytes 2064392 | tf_op jit(solution)/shard_map/ppermute | solution.py:204
  11.3 3.7 %collective-permute-start.4 = (bf16[128,2688]{1,0:T(8,128)(2,1)}, bf16[128,2688]{1,0:T(8,128)(2,1)S(1)}, u32[]{:S(2)}, u32[]{:S(2)}) collective-permute-start(bf16[128,2688]{1,0:T(8,128)(2,1)} %pad_maximum_fusion), channel_id=1, source_target_pairs={{0,8},{4,12},{8,0},{12,4},{1,9},{5,13},{9,1},{13,5},{2,10},{6,14},... | collective-permute-start | bytes 2064392 | tf_op jit(solution)/shard_map/ppermute | solution.py:204
  15.0 3.3 %collective-permute-start.5 = (bf16[128,2688]{1,0:T(8,128)(2,1)}, bf16[128,2688]{1,0:T(8,128)(2,1)S(1)}, u32[]{:S(2)}, u32[]{:S(2)}) collective-permute-start(bf16[128,2688]{1,0:T(8,128)(2,1)} %pad_maximum_fusion), channel_id=1, source_target_pairs={{0,12},{12,0},{1,13},{13,1},{2,14},{14,2},{3,15},{15,3},{16,28},{2... | collective-permute-start | bytes 2064392 | tf_op jit(solution)/shard_map/ppermute | solution.py:204
  18.3 7.8 %collective-permute-done.refs_0_.refs_6_ = bf16[128,2688]{1,0:T(8,128)(2,1)S(1)} collective-permute-done((bf16[128,2688]{1,0:T(8,128)(2,1)}, bf16[128,2688]{1,0:T(8,128)(2,1)S(1)}, u32[]{:S(2)}, u32[]{:S(2)}) %collective-permute-start) | collective-permute-done | bytes 688160 | tf_op jit(solution)/shard_map/ppermute | solution.py:204
  26.1 3.4 %collective-permute-done.2.refs_2_.refs_8_ = bf16[128,2688]{1,0:T(8,128)(2,1)S(1)} collective-permute-done((bf16[128,2688]{1,0:T(8,128)(2,1)}, bf16[128,2688]{1,0:T(8,128)(2,1)S(1)}, u32[]{:S(2)}, u32[]{:S(2)}) %collective-permute-start.2) | collective-permute-done | bytes 688160 | tf_op jit(solution)/shard_map/ppermute | solution.py:204
  36.6 1.5 constant_dynamic-update-slice_fusion.6
  38.7 1.5 copy.14
  40.8 1.5 copy.16
  42.3 32.0 %collective-permute-done.4.refs_4_.refs_10_ = bf16[128,2688]{1,0:T(8,128)(2,1)S(1)} collective-permute-done((bf16[128,2688]{1,0:T(8,128)(2,1)}, bf16[128,2688]{1,0:T(8,128)(2,1)S(1)}, u32[]{:S(2)}, u32[]{:S(2)}) %collective-permute-start.4) | collective-permute-done | bytes 688160 | tf_op jit(solution)/shard_map/ppermute | solution.py:204
  74.9 1.5 copy.18
  77.0 1.5 copy.19
  78.4 1.4 constant_dynamic-update-slice_fusion.5
  80.4 1.5 copy.15
  81.9 1.4 slice.75
  83.3 1.5 copy.17
  84.8 1.4 constant_dynamic-update-slice_fusion.4
  86.1 1.4 constant_dynamic-update-slice_fusion.3
  87.5 1.4 constant_dynamic-update-slice_fusion.2
  88.9 1.4 constant_dynamic-update-slice_fusion.1
  99.6 30.4 %shard_map.120 = (f32[128,1280]{1,0:T(8,128)S(1)}, f32[128,1280]{1,0:T(8,128)S(1)}, f32[128,1280]{1,0:T(8,128)S(1)}, f32[128,128]{1,0:T(8,128)S(1)}, f32[1024,128]{1,0:T(8,128)S(1)}) custom-call(f32[8]{0:T(128)S(1)} %broadcast_select_fusion.2.bias_ref, bf16[128,1280]{1,0:T(8,128)(2,1)S(1)} %copy-done.8, bf16[128,1280]{1,0:T(8,128)(2,1)S(1)} %copy-done.9, ...), custom_call_target="tpu_custom_call" | custom-call | tf_op jit(solution)/shard_map/pallas_call | solution.py:116
  131.9 2.8 %collective-permute-done.6 = f32[384,640]{1,0:T(8,128)S(1)} collective-permute-done((f32[384,640]{1,0:T(8,128)}, f32[384,640]{1,0:T(8,128)S(1)}, u32[]{:S(2)}, u32[]{:S(2)}) %collective-permute-start.6) | collective-permute-done | bytes 983072 | tf_op jit(solution)/shard_map/ppermute | solution.py:46
  135.1 4.2 %collective-permute-start.9 = (bf16[96,640]{1,0:T(8,128)(2,1)S(1)}, bf16[96,640]{1,0:T(8,128)(2,1)S(1)}, u32[]{:S(2)}, u32[]{:S(2)}) collective-permute-start(bf16[96,640]{1,0:T(8,128)(2,1)S(1)} %get-tuple-element.34), channel_id=1, source_target_pairs={{0,12},{4,8},{8,4},{12,0},{1,13},{5,9},{9,5},{13,1},{2,14},{6,10},... | collective-permute-start | bytes 368648 | tf_op jit(solution)/shard_map/ppermute | solution.py:151
  139.3 2.0 %collective-permute-done.7 = bf16[96,640]{1,0:T(8,128)(2,1)S(1)} collective-permute-done((bf16[96,640]{1,0:T(8,128)(2,1)S(1)}, bf16[96,640]{1,0:T(8,128)(2,1)S(1)}, u32[]{:S(2)}, u32[]{:S(2)}) %collective-permute-start.7) | collective-permute-done | bytes 122912 | tf_op jit(solution)/shard_map/ppermute | solution.py:151
  141.4 6.1 %collective-permute-done.8 = bf16[96,640]{1,0:T(8,128)(2,1)S(1)} collective-permute-done((bf16[96,640]{1,0:T(8,128)(2,1)S(1)}, bf16[96,640]{1,0:T(8,128)(2,1)S(1)}, u32[]{:S(2)}, u32[]{:S(2)}) %collective-permute-start.8) | collective-permute-done | bytes 122912 | tf_op jit(solution)/shard_map/ppermute | solution.py:151
  147.6 2.5 %collective-permute-start.10 = (bf16[96,640]{1,0:T(8,128)(2,1)S(1)}, bf16[96,640]{1,0:T(8,128)(2,1)S(1)}, u32[]{:S(2)}, u32[]{:S(2)}) collective-permute-start(bf16[96,640]{1,0:T(8,128)(2,1)S(1)} %get-tuple-element.20), channel_id=1, source_target_pairs={{0,4},{4,0},{8,12},{12,8},{1,5},{5,1},{9,13},{13,9},{2,6},{6,2},{1... | collective-permute-start | bytes 368648 | tf_op jit(solution)/shard_map/ppermute | solution.py:156
  151.4 4.6 %collective-permute-start.15 = (f32[256,128]{1,0:T(8,128)S(1)}, f32[256,128]{1,0:T(8,128)S(1)}, u32[]{:S(2)}, u32[]{:S(2)}) collective-permute-start(f32[256,128]{1,0:T(8,128)S(1)} %get-tuple-element.31), channel_id=1, source_target_pairs={{0,4},{4,8},{8,12},{1,5},{5,9},{9,13},{2,6},{6,10},{10,14},{3,7},{... | collective-permute-start | bytes 393224 | tf_op jit(solution)/shard_map/ppermute | solution.py:226
  155.9 3.0 %collective-permute-start.16 = (f32[128,128]{1,0:T(8,128)S(1)}, f32[128,128]{1,0:T(8,128)S(1)}, u32[]{:S(2)}, u32[]{:S(2)}) collective-permute-start(f32[128,128]{1,0:T(8,128)S(1)} %get-tuple-element.28), channel_id=1, source_target_pairs={{8,0},{12,4},{0,8},{4,12},{9,1},{13,5},{1,9},{5,13},{10,2},{14,6},... | collective-permute-start | bytes 196616 | tf_op jit(solution)/shard_map/ppermute | solution.py:226
  160.2 4.5 %collective-permute-start.17 = (f32[128,128]{1,0:T(8,128)S(1)}, f32[128,128]{1,0:T(8,128)S(1)}, u32[]{:S(2)}, u32[]{:S(2)}) collective-permute-start(f32[128,128]{1,0:T(8,128)S(1)} %get-tuple-element.29), channel_id=1, source_target_pairs={{12,0},{0,12},{13,1},{1,13},{14,2},{2,14},{15,3},{3,15},{28,16},{1... | collective-permute-start | bytes 196616 | tf_op jit(solution)/shard_map/ppermute | solution.py:226
  164.7 1.5 collective-permute-done.12
  166.4 1.9 %collective-permute-done.16 = f32[128,128]{1,0:T(8,128)S(1)} collective-permute-done((f32[128,128]{1,0:T(8,128)S(1)}, f32[128,128]{1,0:T(8,128)S(1)}, u32[]{:S(2)}, u32[]{:S(2)}) %collective-permute-start.16) | collective-permute-done | bytes 65568 | tf_op jit(solution)/shard_map/ppermute | solution.py:226
  169.8 1.6 collective-permute-start.19
  171.4 4.0 %collective-permute-done.19 = f32[256,128]{1,0:T(8,128)S(1)} collective-permute-done((f32[256,128]{1,0:T(8,128)S(1)}, f32[256,128]{1,0:T(8,128)S(1)}, u32[]{:S(2)}, u32[]{:S(2)}) %collective-permute-start.19) | collective-permute-done | bytes 131104 | tf_op jit(solution)/shard_map/ppermute | solution.py:46
  (86 shorter events, 28.7 us)
Async XLA Ops:
  0.6 28.9 %copy-start.4 = (bf16[256,128]{1,0:T(8,128)(2,1)S(1)}, bf16[256,128]{1,0:T(8,128)(2,1)}, u32[]{:S(2)}) copy-start(bf16[256,128]{1,0:T(8,128)(2,1)} %t_ref.1) | copy-start | bytes 196612
  0.6 29.7 %copy-start.13 = (s32[4,4]{1,0:T(4,128)S(1)}, s32[4,4]{1,0:T(4,128)}, u32[]{:S(2)}) copy-start(s32[4,4]{1,0:T(4,128)} %param.17) | copy-start | bytes 196
  5.1 21.1 %collective-permute-start = (bf16[128,2688]{1,0:T(8,128)(2,1)}, bf16[128,2688]{1,0:T(8,128)(2,1)S(1)}, u32[]{:S(2)}, u32[]{:S(2)}) collective-permute-start(bf16[128,2688]{1,0:T(8,128)(2,1)} %pad_maximum_fusion), channel_id=1, source_target_pairs={{0,4},{4,8},{8,12},{1,5},{5,9},{9,13},{2,6},{6,10},{10,14},{3,7},{... | collective-permute-start | bytes 2064392 | tf_op jit(solution)/shard_map/ppermute | solution.py:204
  10.0 19.5 %collective-permute-start.2 = (bf16[128,2688]{1,0:T(8,128)(2,1)}, bf16[128,2688]{1,0:T(8,128)(2,1)S(1)}, u32[]{:S(2)}, u32[]{:S(2)}) collective-permute-start(bf16[128,2688]{1,0:T(8,128)(2,1)} %pad_maximum_fusion), channel_id=1, source_target_pairs={{4,0},{8,4},{12,8},{5,1},{9,5},{13,9},{6,2},{10,6},{14,10},{7,3},{... | collective-permute-start | bytes 2064392 | tf_op jit(solution)/shard_map/ppermute | solution.py:204
  11.3 62.9 %collective-permute-start.4 = (bf16[128,2688]{1,0:T(8,128)(2,1)}, bf16[128,2688]{1,0:T(8,128)(2,1)S(1)}, u32[]{:S(2)}, u32[]{:S(2)}) collective-permute-start(bf16[128,2688]{1,0:T(8,128)(2,1)} %pad_maximum_fusion), channel_id=1, source_target_pairs={{0,8},{4,12},{8,0},{12,4},{1,9},{5,13},{9,1},{13,5},{2,10},{6,14},... | collective-permute-start | bytes 2064392 | tf_op jit(solution)/shard_map/ppermute | solution.py:204
  15.0 61.3 %collective-permute-start.5 = (bf16[128,2688]{1,0:T(8,128)(2,1)}, bf16[128,2688]{1,0:T(8,128)(2,1)S(1)}, u32[]{:S(2)}, u32[]{:S(2)}) collective-permute-start(bf16[128,2688]{1,0:T(8,128)(2,1)} %pad_maximum_fusion), channel_id=1, source_target_pairs={{0,12},{12,0},{1,13},{13,1},{2,14},{14,2},{3,15},{15,3},{16,28},{2... | collective-permute-start | bytes 2064392 | tf_op jit(solution)/shard_map/ppermute | solution.py:204
  26.1 53.7 %collective-permute-start.1 = (bf16[128,2688]{1,0:T(8,128)(2,1)S(1)}, bf16[128,2688]{1,0:T(8,128)(2,1)S(1)}, u32[]{:S(2)}, u32[]{:S(2)}) collective-permute-start(bf16[128,2688]{1,0:T(8,128)(2,1)S(1)} %collective-permute-done.refs_0_.refs_6_), channel_id=1, source_target_pairs={{0,1},{1,0},{2,3},{3,2},{4,5},{5,4},{6,7},{7,6},{8,9},{9,8},{10,11... | collective-permute-start | bytes 2064392 | tf_op jit(solution)/shard_map/ppermute | solution.py:46
  29.5 52.4 %collective-permute-start.3 = (bf16[128,2688]{1,0:T(8,128)(2,1)S(1)}, bf16[128,2688]{1,0:T(8,128)(2,1)}, u32[]{:S(2)}, u32[]{:S(2)}) collective-permute-start(bf16[128,2688]{1,0:T(8,128)(2,1)S(1)} %collective-permute-done.2.refs_2_.refs_8_), channel_id=1, source_target_pairs={{0,1},{1,0},{2,3},{3,2},{4,5},{5,4},{6,7},{7,6},{8,9},{9,8},{10,11... | collective-permute-start | bytes 2064392 | tf_op jit(solution)/shard_map/ppermute | solution.py:46
  91.6 1.1 copy-start
  92.7 1.1 copy-start.1
  93.8 1.0 copy-start.2
  94.8 1.0 copy-start.3
  95.8 0.9 copy-start.7
  96.7 1.0 copy-start.8
  97.7 1.0 copy-start.9
  98.7 1.0 copy-start.10
  131.9 2.8 %collective-permute-start.6 = (f32[384,640]{1,0:T(8,128)}, f32[384,640]{1,0:T(8,128)S(1)}, u32[]{:S(2)}, u32[]{:S(2)}) collective-permute-start(f32[384,640]{1,0:T(8,128)} %constant_dynamic-slice_fusion.3), channel_id=1, source_target_pairs={{0,1},{1,0},{2,3},{3,2},{4,5},{5,4},{6,7},{7,6},{8,9},{9,8},{10,11... | collective-permute-start | bytes 2949128 | tf_op jit(solution)/shard_map/ppermute | solution.py:46
  131.9 7.4 %copy-start.6 = (f32[1024,128]{1,0:T(8,128)S(1)}, f32[1024,128]{1,0:T(8,128)}, u32[]{:S(2)}) copy-start(f32[1024,128]{1,0:T(8,128)} %copy-done.5) | copy-start | bytes 1572868
  134.8 33.6 %copy-start.12 = (f32[128,128]{1,0:T(8,128)S(1)}, f32[128,128]{1,0:T(8,128)}, u32[]{:S(2)}) copy-start(f32[128,128]{1,0:T(8,128)} %copy-done.11) | copy-start | bytes 196612
  134.8 6.5 %collective-permute-start.7 = (bf16[96,640]{1,0:T(8,128)(2,1)S(1)}, bf16[96,640]{1,0:T(8,128)(2,1)S(1)}, u32[]{:S(2)}, u32[]{:S(2)}) collective-permute-start(bf16[96,640]{1,0:T(8,128)(2,1)S(1)} %get-tuple-element.33), channel_id=1, source_target_pairs={{0,4},{4,0},{8,12},{12,8},{1,5},{5,1},{9,13},{13,9},{2,6},{6,2},{1... | collective-permute-start | bytes 368648 | tf_op jit(solution)/shard_map/ppermute | solution.py:151
  135.1 12.4 %collective-permute-start.8 = (bf16[96,640]{1,0:T(8,128)(2,1)S(1)}, bf16[96,640]{1,0:T(8,128)(2,1)S(1)}, u32[]{:S(2)}, u32[]{:S(2)}) collective-permute-start(bf16[96,640]{1,0:T(8,128)(2,1)S(1)} %get-tuple-element.35), channel_id=1, source_target_pairs={{0,8},{4,12},{8,0},{12,4},{1,9},{5,13},{9,1},{13,5},{2,10},{6,14},... | collective-permute-start | bytes 368648 | tf_op jit(solution)/shard_map/ppermute | solution.py:151
  135.1 12.4 %collective-permute-start.9 = (bf16[96,640]{1,0:T(8,128)(2,1)S(1)}, bf16[96,640]{1,0:T(8,128)(2,1)S(1)}, u32[]{:S(2)}, u32[]{:S(2)}) collective-permute-start(bf16[96,640]{1,0:T(8,128)(2,1)S(1)} %get-tuple-element.34), channel_id=1, source_target_pairs={{0,12},{4,8},{8,4},{12,0},{1,13},{5,9},{9,5},{13,1},{2,14},{6,10},... | collective-permute-start | bytes 368648 | tf_op jit(solution)/shard_map/ppermute | solution.py:151
  147.6 11.3 %collective-permute-start.10 = (bf16[96,640]{1,0:T(8,128)(2,1)S(1)}, bf16[96,640]{1,0:T(8,128)(2,1)S(1)}, u32[]{:S(2)}, u32[]{:S(2)}) collective-permute-start(bf16[96,640]{1,0:T(8,128)(2,1)S(1)} %get-tuple-element.20), channel_id=1, source_target_pairs={{0,4},{4,0},{8,12},{12,8},{1,5},{5,1},{9,13},{13,9},{2,6},{6,2},{1... | collective-permute-start | bytes 368648 | tf_op jit(solution)/shard_map/ppermute | solution.py:156
  150.1 10.2 %collective-permute-start.11 = (bf16[96,640]{1,0:T(8,128)(2,1)S(1)}, bf16[96,640]{1,0:T(8,128)(2,1)S(1)}, u32[]{:S(2)}, u32[]{:S(2)}) collective-permute-start(bf16[96,640]{1,0:T(8,128)(2,1)S(1)} %get-tuple-element.20), channel_id=1, source_target_pairs={{0,8},{4,12},{8,0},{12,4},{1,9},{5,13},{9,1},{13,5},{2,10},{6,14},... | collective-permute-start | bytes 368648 | tf_op jit(solution)/shard_map/ppermute | solution.py:156
  150.1 18.2 %collective-permute-start.14 = (f32[256,128]{1,0:T(8,128)S(1)}, f32[256,128]{1,0:T(8,128)S(1)}, u32[]{:S(2)}, u32[]{:S(2)}) collective-permute-start(f32[256,128]{1,0:T(8,128)S(1)} %get-tuple-element.32), channel_id=1, source_target_pairs={{4,0},{8,4},{12,8},{5,1},{9,5},{13,9},{6,2},{10,6},{14,10},{7,3},{... | collective-permute-start | bytes 393224 | tf_op jit(solution)/shard_map/ppermute | solution.py:226
  151.4 17.0 %collective-permute-start.15 = (f32[256,128]{1,0:T(8,128)S(1)}, f32[256,128]{1,0:T(8,128)S(1)}, u32[]{:S(2)}, u32[]{:S(2)}) collective-permute-start(f32[256,128]{1,0:T(8,128)S(1)} %get-tuple-element.31), channel_id=1, source_target_pairs={{0,4},{4,8},{8,12},{1,5},{5,9},{9,13},{2,6},{6,10},{10,14},{3,7},{... | collective-permute-start | bytes 393224 | tf_op jit(solution)/shard_map/ppermute | solution.py:226
  155.9 12.4 %collective-permute-start.16 = (f32[128,128]{1,0:T(8,128)S(1)}, f32[128,128]{1,0:T(8,128)S(1)}, u32[]{:S(2)}, u32[]{:S(2)}) collective-permute-start(f32[128,128]{1,0:T(8,128)S(1)} %get-tuple-element.28), channel_id=1, source_target_pairs={{8,0},{12,4},{0,8},{4,12},{9,1},{13,5},{1,9},{5,13},{10,2},{14,6},... | collective-permute-start | bytes 196616 | tf_op jit(solution)/shard_map/ppermute | solution.py:226
  158.9 7.3 %collective-permute-start.12 = (bf16[96,640]{1,0:T(8,128)(2,1)S(1)}, bf16[96,640]{1,0:T(8,128)(2,1)S(1)}, u32[]{:S(2)}, u32[]{:S(2)}) collective-permute-start(bf16[96,640]{1,0:T(8,128)(2,1)S(1)} %get-tuple-element.20), channel_id=1, source_target_pairs={{0,12},{4,8},{8,4},{12,0},{1,13},{5,9},{9,5},{13,1},{2,14},{6,10},... | collective-permute-start | bytes 368648 | tf_op jit(solution)/shard_map/ppermute | solution.py:156
  160.2 8.1 %collective-permute-start.17 = (f32[128,128]{1,0:T(8,128)S(1)}, f32[128,128]{1,0:T(8,128)S(1)}, u32[]{:S(2)}, u32[]{:S(2)}) collective-permute-start(f32[128,128]{1,0:T(8,128)S(1)} %get-tuple-element.29), channel_id=1, source_target_pairs={{12,0},{0,12},{13,1},{1,13},{14,2},{2,14},{15,3},{3,15},{28,16},{1... | collective-permute-start | bytes 196616 | tf_op jit(solution)/shard_map/ppermute | solution.py:226
  166.3 9.8 %collective-permute-start.13 = (bf16[384,640]{1,0:T(8,128)(2,1)S(1)}, bf16[384,640]{1,0:T(8,128)(2,1)S(1)}, u32[]{:S(2)}, u32[]{:S(2)}) collective-permute-start(bf16[384,640]{1,0:T(8,128)(2,1)S(1)} %constant_dynamic-update-slice_fusion.10), channel_id=1, source_target_pairs={{0,1},{1,0},{2,3},{3,2},{4,5},{5,4},{6,7},{7,6},{8,9},{9,8},{10,11... | collective-permute-start | bytes 1474568 | tf_op jit(solution)/shard_map/ppermute | solution.py:46
  168.4 1.4 collective-permute-start.18
  169.8 5.6 %collective-permute-start.19 = (f32[256,128]{1,0:T(8,128)S(1)}, f32[256,128]{1,0:T(8,128)S(1)}, u32[]{:S(2)}, u32[]{:S(2)}) collective-permute-start(f32[256,128]{1,0:T(8,128)S(1)} %add.122), channel_id=1, source_target_pairs={{0,2},{2,0},{1,3},{3,1},{4,6},{6,4},{5,7},{7,5},{8,10},{10,8},{9,1... | collective-permute-start | bytes 393224 | tf_op jit(solution)/shard_map/ppermute | solution.py:46
  (2 other events, 1.6 us)

commit v2 on v1

--- a/solution.py
+++ b/solution.py
@@ -161,7 +161,7 @@
     return jnp.concatenate([first, second], axis=1).astype(F32)
 
 
-def on_device(
+def window_plan(
     frozen_query,
     frozen_key,
     frozen_value,
@@ -240,6 +240,311 @@
     return grads[:rank], grads[rank : 2 * rank], grads[2 * rank :], low
 
 
+def head_table(heads, frames):
+    base, extra = divmod(heads, frames)
+    lead = (frames - extra) // 2
+    counts = [base + (1 if lead <= j < lead + extra else 0) for j in range(frames)]
+    return [sum(counts[:j]) for j in range(frames)], counts
+
+
+def pick(table, index):
+    ids = jnp.arange(len(table))
+    return jnp.sum(jnp.where(ids == index, jnp.array(table, jnp.int32), 0))
+
+
+def pack_kernel(slots, heads_ref, *refs):
+    full = slots[0]
+    ins, t_ref, outs = refs[: -1 - len(slots)], refs[-1 - len(slots)], refs[-len(slots) :]
+    for s in range(sum(slots)):
+        out, at = (outs[0], s) if s < full else (outs[1], s - full)
+        for a in range(4):
+            col = (4 * at + a) * DH
+            out[0, :, col : col + DH] = ins[4 * s + a][...]
+    outs[0][0, :, 4 * full * DH :] = t_ref[...]
+
+
+def pack(heads, half_idx, fq, do, fk, fv, t, slots, frames):
+    rows, rank = fq.shape[0], t.shape[1]
+    total = sum(slots)
+    scalars = jnp.concatenate([heads, half_idx[None]]).astype(jnp.int32)
+
+    def spec(s, tile):
+        def index(j, ref):
+            return (ref[frames * total] if tile else 0, ref[j * total + s])
+
+        return pl.BlockSpec((rows, DH), index)
+
+    specs, args = [], []
+    for s in range(total):
+        specs += [spec(s, False), spec(s, False), spec(s, True), spec(s, True)]
+        args += [fq, do, fk, fv]
+    specs.append(pl.BlockSpec((rows, rank), lambda j, ref: (ref[frames * total], 0)))
+    widths = [4 * n * DH for n in slots]
+    widths[0] += rank
+    return pl.pallas_call(
+        functools.partial(pack_kernel, slots),
+        grid_spec=pltpu.PrefetchScalarGridSpec(
+            num_scalar_prefetch=1,
+            grid=(frames,),
+            in_specs=specs,
+            out_specs=[pl.BlockSpec((1, rows, w), lambda j, ref: (j, 0, 0)) for w in widths],
+        ),
+        out_shape=[jax.ShapeDtypeStruct((frames, rows, w), BF16) for w in widths],
+    )(scalars, *args, t)
+
+
+def head_kernel(frames, scalar_ref, *refs):
+    grad_ref, low_ref = refs[-2:]
+    live = scalar_ref[frames * frames + pl.num_programs(0) + pl.program_id(0)] > 0
+
+    @pl.when(pl.program_id(0) == 0)
+    def _():
+        low_ref[...] = jnp.zeros_like(low_ref)
+
+    @pl.when(live)
+    def _():
+        one_head(frames, scalar_ref, *refs)
+
+    @pl.when(jnp.logical_not(live))
+    def _():
+        grad_ref[...] = jnp.zeros_like(grad_ref)
+
+
+def one_head(frames, bands, q_ref, do_ref, k_ref, v_ref, k2_ref, v2_ref, t_ref, t2_ref,
+             aq_ref, ak_ref, av_ref, grad_ref, low_ref):
+    rows = q_ref.shape[1]
+    flat = frames * rows
+
+    def load(ref):
+        return ref[...].reshape(flat, ref.shape[2])
+
+    def adapted(ref, tokens, adapter):
+        return (load(ref).astype(F32) + dot_nn(tokens, adapter)).astype(BF16)
+
+    aq, ak, av = aq_ref[...], ak_ref[...], av_ref[...]
+    t_same, t_other = load(t_ref), load(t2_ref)
+    query = adapted(q_ref, t_same, aq)
+    do = load(do_ref)
+    do_t = do.T
+    keys = jnp.concatenate([adapted(k_ref, t_same, ak), adapted(k2_ref, t_other, ak)], axis=0)
+    values = jnp.concatenate([adapted(v_ref, t_same, av), adapted(v2_ref, t_other, av)], axis=0)
+    keys_t, values_t = keys.T, values.T
+
+    def bias(i, b):
+        j, need = (b, 0) if b < frames else (b - frames, 1)
+        value = jnp.where(bands[i * frames + j] > need, 0.0, -jnp.inf).astype(F32)
+        return jnp.full((1, rows), value, F32)
+
+    span = 2 if frames % 2 == 0 else 1
+    wide = span * rows
+    dks, dvs, dqs = [None] * (2 * frames), [None] * (2 * frames), []
+    for first in range(0, frames, span):
+        mine = range(first, first + span)
+        blocks = list(range(frames)) + [
+            frames + j for j in range(frames) if any(abs(i - j) <= NEAR for i in mine)
+        ]
+        here = slice(first * rows, first * rows + wide)
+        q_p, do_p = query[here], do[here]
+
+        def gather(whole, axis):
+            parts = [
+                whole[b * rows : (b + 1) * rows] if axis == 0 else whole[:, b * rows : (b + 1) * rows]
+                for b in blocks
+            ]
+            return jnp.concatenate(parts, axis=axis)
+
+        raw = dot_nt(gather(keys, 0), q_p)
+        scores = [
+            raw[n * rows : (n + 1) * rows] * SCALE + jnp.concatenate([bias(i, b) for i in mine], axis=1)
+            for n, b in enumerate(blocks)
+        ]
+        top = jnp.max(functools.reduce(jnp.maximum, scores), axis=0, keepdims=True)
+        shifted = [jnp.exp(s - top) for s in scores]
+        inverse = 1.0 / jnp.sum(functools.reduce(jnp.add, shifted), axis=0, keepdims=True)
+        probs = [s * inverse for s in shifted]
+        low = jnp.concatenate([p.astype(BF16) for p in probs], axis=0)
+        attended = dot_nn(gather(values_t, 1), low).astype(BF16).astype(F32)
+        delta = jnp.sum(do_t[:, here].astype(F32) * attended, axis=0, keepdims=True)
+        prob_grad = dot_nt(gather(values, 0), do_p)
+        grad = jnp.concatenate(
+            [
+                (probs[n] * (prob_grad[n * rows : (n + 1) * rows] - delta)).astype(BF16)
+                for n in range(len(blocks))
+            ],
+            axis=0,
+        )
+        dqs.append((dot_nn(gather(keys_t, 1), grad) * SCALE).astype(BF16).T)
+        dk, dv = dot_nn(grad, q_p), dot_nn(low, do_p)
+        for n, b in enumerate(blocks):
+            part = slice(n * rows, (n + 1) * rows)
+            dks[b] = dk[part] if dks[b] is None else dks[b] + dk[part]
+            dvs[b] = dv[part] if dvs[b] is None else dvs[b] + dv[part]
+    dq = jnp.concatenate(dqs, axis=0)
+    grad_ref[0, :, :] = dot_tn(t_same, dq)
+    dk = (jnp.concatenate(dks, axis=0) * SCALE).astype(BF16)
+    dv = jnp.concatenate(dvs, axis=0).astype(BF16)
+    both = jnp.concatenate([dk, dv], axis=1)
+    sums = dot_tn(jnp.concatenate([t_same, t_other], axis=0), both)
+    grad_ref[1, :, :] = sums[:, :DH]
+    grad_ref[2, :, :] = sums[:, DH:]
+    lows = dot_nt(both, jnp.concatenate([ak, av], axis=1))
+    low_ref[:flat] += lows[:flat] + dot_nt(dq, aq)
+    low_ref[flat:] += lows[flat:]
+
+
+def head_group(band_width, heads, live, mine, other, tokens, tokens2, token_col, aq, ak, av):
+    frames, rows = mine.shape[:2]
+    rank = aq.shape[0]
+    slots = heads.shape[0]
+    scalars = jnp.concatenate([band_width.reshape(-1), heads, live]).astype(jnp.int32)
+
+    def spec(a):
+        return pl.BlockSpec((frames, rows, DH), lambda s, ref: (0, 0, 4 * s + a))
+
+    adapter = pl.BlockSpec((rank, DH), lambda s, ref: (0, ref[frames * frames + s]))
+    token = pl.BlockSpec((frames, rows, rank), lambda s, ref: (0, 0, token_col))
+    return pl.pallas_call(
+        functools.partial(head_kernel, frames),
+        grid_spec=pltpu.PrefetchScalarGridSpec(
+            num_scalar_prefetch=1,
+            grid=(slots,),
+            in_specs=[spec(0), spec(1), spec(2), spec(3), spec(2), spec(3), token, token] + [adapter] * 3,
+            out_specs=[
+                pl.BlockSpec((3, rank, DH), lambda s, ref: (0, 0, s)),
+                pl.BlockSpec((2 * frames * rows, rank), lambda s, ref: (0, 0)),
+            ],
+        ),
+        out_shape=[
+            jax.ShapeDtypeStruct((3, rank, slots * DH), F32),
+            jax.ShapeDtypeStruct((2 * frames * rows, rank), F32),
+        ],
+        compiler_params=pltpu.CompilerParams(vmem_limit_bytes=48 * 1024 * 1024),
+    )(scalars, mine, mine, mine, mine, other, other, tokens, tokens2, aq, ak, av)
+
+
+def place_kernel(slots, scalar_ref, mine_ref, other_ref, *refs):
+    half = scalar_ref[0]
+    count = mine_ref.shape[0]
+    outs = refs
+    total = sum(slots)
+    rank = outs[0].shape[0]
+    rows = mine_ref.shape[1]
+    for m in range(count):
+        a = mine_ref[m].astype(F32)
+        b = other_ref[m].astype(F32)
+        both = jnp.where(half == 0, jnp.concatenate([a, b], axis=0), jnp.concatenate([b, a], axis=0))
+        for s in range(total):
+            col = pl.multiple_of(scalar_ref[1 + m * total + s] * DH, DH)
+            live = scalar_ref[1 + count * total + m * total + s] > 0
+
+            @pl.when(live)
+            def _():
+                for o in range(3):
+                    outs[o][:, pl.ds(col, DH)] = both[o * rank : (o + 1) * rank, s * DH : (s + 1) * DH]
+
+
+def place(scalars, mine, other, rank, width, slots):
+    return pl.pallas_call(
+        functools.partial(place_kernel, slots),
+        in_specs=[pl.BlockSpec(memory_space=pltpu.SMEM)] + [pl.BlockSpec(memory_space=pltpu.VMEM)] * 2,
+        out_specs=[pl.BlockSpec(memory_space=pltpu.VMEM)] * 3,
+        out_shape=[jax.ShapeDtypeStruct((rank, width), F32)] * 3,
+        compiler_params=pltpu.CompilerParams(vmem_limit_bytes=32 * 1024 * 1024),
+    )(scalars, mine, other)
+
+
+def exchange_plan(
+    frozen_query,
+    frozen_key,
+    frozen_value,
+    token_adapter_input,
+    query_adapter_out,
+    key_adapter_out,
+    value_adapter_out,
+    out_grad,
+    band_width,
+):
+    rows, width = frozen_query.shape
+    rank = token_adapter_input.shape[1]
+    frames = band_width.shape[0]
+    heads = width // DH
+    frame_idx = lax.axis_index("tm")
+    half_idx = lax.axis_index("rep")
+    starts, counts = head_table(heads, frames)
+    full, most = min(counts), max(counts)
+    slots = (full, most - full) if most > full else (full,)
+    table = [[min(starts[j] + s, heads - 1) for s in range(most)] for j in range(frames)]
+    wide = [j for j in range(frames) if counts[j] == most]
+
+    def meet(block, m, targets=range(frames)):
+        return lax.ppermute(block, "tm", [(j ^ m, j) for j in targets])
+
+    flat_heads = jnp.array([h for row in table for h in row], jnp.int32)
+    packed = pack(
+        flat_heads, half_idx, frozen_query, out_grad, frozen_key, frozen_value,
+        token_adapter_input, slots, frames,
+    )
+    my_heads = jnp.stack([pick([row[s] for row in table], frame_idx) for s in range(most)])
+    my_live = (jnp.arange(most) < pick(counts, frame_idx)).astype(jnp.int32)
+    adapters = (query_adapter_out, key_adapter_out, value_adapter_out)
+    got = lax.all_to_all(packed[0], "tm", 0, 0, tiled=True)
+    got2 = swap(got, "rep")
+    token_col = 4 * full
+    grads, low = head_group(
+        band_width, my_heads[:full], my_live[:full], got, got2, got, got2, token_col, *adapters
+    )
+    grads = [grads]
+    if most > full:
+        extra = jnp.zeros_like(packed[1])
+        for m in range(frames):
+            part = lax.dynamic_slice_in_dim(packed[1], frame_idx ^ m, 1, 0)
+            part = part if m == 0 else meet(part, m, wide)
+            extra = lax.dynamic_update_slice_in_dim(extra, part, frame_idx ^ m, 0)
+        extra2 = swap(extra, "rep")
+        more, low2 = head_group(
+            band_width, my_heads[full:], my_live[full:], extra, extra2, got, got2, token_col, *adapters
+        )
+        grads.append(more)
+        low = low + low2
+
+    low = low.reshape(2, frames, rows, rank)
+    mine = lax.dynamic_slice_in_dim(low, frame_idx, 1, 1)
+    for m in range(1, frames):
+        give = lax.dynamic_slice_in_dim(low, frame_idx ^ m, 1, 1).astype(BF16)
+        mine = mine + meet(give, m).astype(F32)
+    same, other = mine[0, 0], mine[1, 0]
+    low = jnp.where(
+        half_idx == 0,
+        jnp.concatenate([same, other], axis=0),
+        jnp.concatenate([other, same], axis=0),
+    )
+    low = low + swap(low, "rep")
+    low = low + swap(low, "head")
+
+    total = jnp.concatenate(grads, axis=2).reshape(3 * rank, most * DH)
+    half = 3 * rank // 2
+    keep = lax.dynamic_slice_in_dim(total, half_idx * half, half, 0)
+    give = lax.dynamic_slice_in_dim(total, (1 - half_idx) * half, half, 0)
+    piece = (keep + swap(give, "rep")).astype(BF16)
+    pieces = jnp.stack([piece] + [meet(piece, m) for m in range(1, frames)])
+    scalars = [half_idx[None]]
+    for values in (table, [[int(s < counts[j]) for s in range(most)] for j in range(frames)]):
+        for m in range(frames):
+            scalars.append(
+                jnp.stack([pick([row[s] for row in values], frame_idx ^ m) for s in range(most)])
+            )
+    scalars = jnp.concatenate(scalars).astype(jnp.int32)
+    outs = place(scalars, pieces, swap(pieces, "rep"), rank, width, slots)
+    return outs[0], outs[1], outs[2], low
+
+
+def on_device(frozen_query, *rest):
+    frames = rest[-1].shape[0]
+    heads = frozen_query.shape[1] // DH
+    whole_reach = frames <= REACH + 1 and frames & (frames - 1) == 0 and heads >= frames
+    return (exchange_plan if whole_reach else window_plan)(frozen_query, *rest)
+
+
 def solution(mesh):
     in_specs = (
         P(("groups", "tm", "rep"), "head"),

time: 179 us -> 123 us (0.69)
  waiting for transfers between devices: 63 us -> 18.4 us
  blocking collectives: 0 us -> 35 us
  local copies, waits for them, and re-layouts: 36 us -> 20.9 us
  Pallas kernels: 30.4 us -> 15.4 us
  starting transfers between devices: 36.4 us -> 22.2 us
  other arithmetic: 3 us -> 9.64 us
  between operations: 6.27 us -> 0.9 us
  matrix products: 2.65 us -> 0 us
    ppermute x14 -> x9, waiting for transfers between devices: 54.8 us -> 16.8 us  [meet(): return lax.ppermute(block, 'tm', [(j ^ m, j) for j in targets])]
    all_to_all x0 -> x1, blocking collectives: none -> 35 us  [exchange_plan(): got = lax.all_to_all(packed[0], 'tm', 0, 0, tiled=True)]
    ppermute x14 -> x9, starting transfers between devices: 34.7 us -> 19.3 us  [meet(): return lax.ppermute(block, 'tm', [(j ^ m, j) for j in targets])]
    pallas_call x1 -> x4, Pallas kernels: 30.4 us -> 15.4 us  [the longest x2 8.72 us: head_group(): pl.pallas_call(functools.partial(head_kernel, frames), grid_spec=pltpu.Pr...]
    slice x15 -> x1, local copies, waits for them, and re-layouts: 14.6 us -> 0.58 us  [exchange_plan(): my_live[full:]]
    concatenate x2 -> x1, local copies, waits for them, and re-layouts: 1.42 us -> 15 us  [exchange_plan(): scalars = jnp.concatenate(scalars).astype(jnp.int32)]
    unnamed x37 -> x28, local copies, waits for them, and re-layouts: 17.8 us -> 4.31 us
    ppermute x6, waiting for transfers between devices: 8.16 us -> 1.59 us  [swap(): return lax.ppermute(block, axis, [(0, 1), (1, 0)])]
  transfers between devices with their start and end apart: 20 -> 15, of which waited for: 10 -> 4; matrix products, arithmetic and copies ran while one was open for 9% -> 20% of each run, Pallas kernels for 0% -> 6%
where the time goes in v2:
time: 123 us; the launch traced here: 122 us
  blocking collectives  35 us (28%)
  starting transfers between devices  22.2 us (18%)
  local copies, waits for them, and re-layouts  20.9 us (17%)
  waiting for transfers between devices  18.4 us (15%)
  Pallas kernels  15.4 us (13%)
  other arithmetic  9.64 us (8%)
    all_to_all x1, blocking collectives, exchange_plan(): got = lax.all_to_all(packed[0], 'tm', 0, 0, tiled=True)  35 us
    ppermute x9, starting transfers between devices, meet(): return lax.ppermute(block, 'tm', [(j ^ m, j) for j in targets])  19.3 us
    ppermute x9, waiting for transfers between devices, meet(): return lax.ppermute(block, 'tm', [(j ^ m, j) for j in targets])  16.8 us
    concatenate x1, local copies, waits for them, and re-layouts, exchange_plan(): scalars = jnp.concatenate(scalars).astype(jnp.int32)  15 us
    pallas_call x2, Pallas kernels, head_group(): pl.pallas_call(functools.partial(head_kernel, frames), grid_spec=pltpu.Pr...  8.72 us
    pallas_call x1, Pallas kernels, pack(): pl.pallas_call(functools.partial(pack_kernel, slots), grid_spec=pltpu.Pre...  4.42 us
    unnamed x28, local copies, waits for them, and re-layouts  4.31 us
    reduce_sum x5, other arithmetic, pick(): return jnp.sum(jnp.where(ids == index, jnp.array(table, jnp.int32), 0))  4.27 us
  transfers between devices with their start and end apart: 15, of which 4 were waited for; matrix products, arithmetic and copies ran while one was open for 20% of the time, Pallas kernels for 6%

profile of v2, /device:TPU:0, one launch (start us, length us, event | category | flops | bytes accessed | tf_op | source)
XLA Modules:
  0.0 122.4 jit_solution(14970373689361420742)
XLA Ops:
  0.6 1.2 %pad_add_fusion.1.heads_ref = s32[13]{0:T(128)} fusion(s32[1]{0:T(128)} %bitcast, s32[12]{0:T(128)} %constant.39.clone), kind=kLoop, calls=%fused_computation.20 | loop fusion | flops 13 | bytes 104 | tf_op jit(solution)/shard_map/concatenate | solution.py:269
  1.9 4.4 %shard_map.381 = (bf16[4,128,1152]{2,1,0:T(8,128)(2,1)}, bf16[4,128,512]{2,1,0:T(8,128)(2,1)}) custom-call(s32[13]{0:T(128)} %pad_add_fusion.1.heads_ref, bf16[128,1280]{1,0:T(8,128)(2,1)} %refs_8_.3, bf16[128,1280]{1,0:T(8,128)(2,1)} %refs_9_.3, bf16[256,1280]{1,0:T(8,128)(2,1)} %refs_10_.3, bf16[256,1280]{1,0:T(8,128)(2,1)} %refs_11_.1, ...), custom_call_target="tpu_custom_call" | custom-call | tf_op jit(solution)/shard_map/pallas_call | solution.py:284
  6.3 35.0 %all_to_all.5.refs_0_.refs_1_.refs_2_.refs_3_.refs_6_ = bf16[4,128,1152]{2,1,0:T(8,128)(2,1)S(1)} all-to-all(bf16[4,128,1152]{2,1,0:T(8,128)(2,1)} %get-tuple-element.13), channel_id=1, replica_groups=mesh['groups'=2,'tm'=4,'head'=2,'rep'=2] {'tm'}, dimensions={0} | all-to-all | bytes 2359296 | tf_op jit(solution)/shard_map/all_to_all | solution.py:490
  41.4 0.8 constant_dynamic-slice_fusion
  42.1 2.1 %collective-permute-start.1 = (bf16[1,128,512]{2,1,0:T(8,128)(2,1)}, bf16[1,128,512]{2,1,0:T(8,128)(2,1)S(1)}, u32[]{:S(2)}, u32[]{:S(2)}) collective-permute-start(bf16[1,128,512]{2,1,0:T(8,128)(2,1)} %get-tuple-element.43), channel_id=1, source_target_pairs={{0,4},{12,8},{1,5},{13,9},{2,6},{14,10},{3,7},{15,11},{16,20},{28,... | collective-permute-start | bytes 393224 | tf_op jit(solution)/shard_map/ppermute | solution.py:480
  44.9 4.0 %collective-permute-start.2 = (bf16[1,128,512]{2,1,0:T(8,128)(2,1)}, bf16[1,128,512]{2,1,0:T(8,128)(2,1)S(1)}, u32[]{:S(2)}, u32[]{:S(2)}) collective-permute-start(bf16[1,128,512]{2,1,0:T(8,128)(2,1)} %get-tuple-element.42), channel_id=1, source_target_pairs={{12,4},{0,8},{13,5},{1,9},{14,6},{2,10},{15,7},{3,11},{28,20},{16,... | collective-permute-start | bytes 393224 | tf_op jit(solution)/shard_map/ppermute | solution.py:480
  48.9 1.3 %select_reduce_fusion = (s32[]{:T(128)}, s32[]{:T(128)}) fusion(s32[4]{0:T(128)} %constant.43.clone, s32[]{:T(128)S(6)} %axis_index.25), kind=kLoop, calls=%fused_computation.22 | loop fusion | flops 18 | bytes 28 | tf_op jit(solution)/shard_map/reduce_sum | solution.py:252
  50.4 2.0 %collective-permute-done.2 = bf16[1,128,512]{2,1,0:T(8,128)(2,1)S(1)} collective-permute-done((bf16[1,128,512]{2,1,0:T(8,128)(2,1)}, bf16[1,128,512]{2,1,0:T(8,128)(2,1)S(1)}, u32[]{:S(2)}, u32[]{:S(2)}) %collective-permute-start.2) | collective-permute-done | bytes 131104 | tf_op jit(solution)/shard_map/ppermute | solution.py:480
  53.7 0.8 select_reduce_fusion.9
  54.5 1.3 %pad_add_fusion.2.scalar_ref = s32[18]{0:T(128)S(1)} fusion(s32[1]{0:T(128)} %slice.13, s32[1]{0:T(128)} %bitcast.3, s32[16]{0:T(128)S(1)} %reshape.18), kind=kLoop, calls=%fused_computation.21 | loop fusion | flops 36 | bytes 144 | tf_op jit(solution)/shard_map/concatenate | solution.py:399
  55.9 0.7 select_reduce_fusion.11
  56.6 1.2 pad_add_fusion.scalar_ref
  57.8 1.0 copy-done
  58.8 1.0 copy-done.2
  59.7 1.0 copy-done.3
  60.7 7.9 %shard_map.382 = (f32[3,128,256]{2,1,0:T(8,128)S(1)}, f32[1024,128]{1,0:T(8,128)S(1)}) custom-call(s32[20]{0:T(128)S(1)} %pad_add_fusion.scalar_ref, bf16[4,128,1152]{2,1,0:T(8,128)(2,1)S(1)} %all_to_all.5.refs_0_.refs_1_.refs_2_.refs_3_.refs_6_, bf16[4,128,1152]{2,1,0:T(8,128)(2,1)S(1)} %all_to_all.5.refs_0_.refs_1_.refs_2_.refs_3_.refs_6_, ...), custom_call_target="tpu_custom_call" | custom-call | tf_op jit(solution)/shard_map/pallas_call | solution.py:406
  68.7 0.8 shard_map.383
  69.5 0.8 copy-done.6
  71.6 5.7 %collective-permute-start.10 = (bf16[2,1,128,128]{3,2,1,0:T(8,128)(2,1)S(1)}, bf16[2,1,128,128]{3,2,1,0:T(8,128)(2,1)S(1)}, u32[]{:S(2)}, u32[]{:S(2)}) collective-permute-start(bf16[2,1,128,128]{3,2,1,0:T(8,128)(2,1)S(1)} %get-tuple-element.38), channel_id=1, source_target_pairs={{4,0},{0,4},{12,8},{8,12},{5,1},{1,5},{13,9},{9,13},{6,2},{2,6},{1... | collective-permute-start | bytes 196616 | tf_op jit(solution)/shard_map/ppermute | solution.py:480
  77.3 2.4 %collective-permute-start.12 = (bf16[2,1,128,128]{3,2,1,0:T(8,128)(2,1)S(1)}, bf16[2,1,128,128]{3,2,1,0:T(8,128)(2,1)S(1)}, u32[]{:S(2)}, u32[]{:S(2)}) collective-permute-start(bf16[2,1,128,128]{3,2,1,0:T(8,128)(2,1)S(1)} %get-tuple-element.39), channel_id=1, source_target_pairs={{12,0},{8,4},{4,8},{0,12},{13,1},{9,5},{5,9},{1,13},{14,2},{10,6},... | collective-permute-start | bytes 196616 | tf_op jit(solution)/shard_map/ppermute | solution.py:480
  79.7 1.6 %collective-permute-start.8 = (bf16[192,384]{1,0:T(8,128)(2,1)S(1)}, bf16[192,384]{1,0:T(8,128)(2,1)S(1)}, u32[]{:S(2)}, u32[]{:S(2)}) collective-permute-start(bf16[192,384]{1,0:T(8,128)(2,1)S(1)} %add_convert_fusion), channel_id=1, source_target_pairs={{12,0},{8,4},{4,8},{0,12},{13,1},{9,5},{5,9},{1,13},{14,2},{10,6},... | collective-permute-start | bytes 442376 | tf_op jit(solution)/shard_map/ppermute | solution.py:480
  81.3 1.9 %collective-permute-start.7 = (bf16[192,384]{1,0:T(8,128)(2,1)S(1)}, bf16[192,384]{1,0:T(8,128)(2,1)S(1)}, u32[]{:S(2)}, u32[]{:S(2)}) collective-permute-start(bf16[192,384]{1,0:T(8,128)(2,1)S(1)} %add_convert_fusion), channel_id=1, source_target_pairs={{8,0},{12,4},{0,8},{4,12},{9,1},{13,5},{1,9},{5,13},{10,2},{14,6},... | collective-permute-start | bytes 442376 | tf_op jit(solution)/shard_map/ppermute | solution.py:480
  83.3 0.9 collective-permute-start.6
  84.2 8.6 %collective-permute-done.11 = bf16[2,1,128,128]{3,2,1,0:T(8,128)(2,1)S(1)} collective-permute-done((bf16[2,1,128,128]{3,2,1,0:T(8,128)(2,1)S(1)}, bf16[2,1,128,128]{3,2,1,0:T(8,128)(2,1)S(1)}, u32[]{:S(2)}, u32[]{:S(2)}) %collective-permute-start.11) | collective-permute-done | bytes 65568 | tf_op jit(solution)/shard_map/ppermute | solution.py:480
  92.9 6.2 %collective-permute-done.7 = bf16[192,384]{1,0:T(8,128)(2,1)S(1)} collective-permute-done((bf16[192,384]{1,0:T(8,128)(2,1)S(1)}, bf16[192,384]{1,0:T(8,128)(2,1)S(1)}, u32[]{:S(2)}, u32[]{:S(2)}) %collective-permute-start.7) | collective-permute-done | bytes 147488 | tf_op jit(solution)/shard_map/ppermute | solution.py:480
  99.8 1.6 %collective-permute-done.13 = f32[256,128]{1,0:T(8,128)S(1)} collective-permute-done((f32[256,128]{1,0:T(8,128)S(1)}, f32[256,128]{1,0:T(8,128)S(1)}, u32[]{:S(2)}, u32[]{:S(2)}) %collective-permute-start.13) | collective-permute-done | bytes 131104 | tf_op jit(solution)/shard_map/ppermute | solution.py:46
  101.4 1.6 %collective-permute-start.14 = (f32[256,128]{1,0:T(8,128)S(1)}, f32[256,128]{1,0:T(8,128)S(1)}, u32[]{:S(2)}, u32[]{:S(2)}) collective-permute-start(f32[256,128]{1,0:T(8,128)S(1)} %add.58), channel_id=1, source_target_pairs={{0,2},{2,0},{1,3},{3,1},{4,6},{6,4},{5,7},{7,5},{8,10},{10,8},{9,1... | collective-permute-start | bytes 393224 | tf_op jit(solution)/shard_map/ppermute | solution.py:46
  103.0 0.7 select_reduce_fusion.4
  103.7 0.7 select_reduce_fusion.1
  104.4 15.0 %concatenate.21.scalar_ref = s32[25]{0:T(128)S(1)} concatenate(s32[1]{0:T(128)} %bitcast, s32[1]{0:T(128)} %bitcast.1, s32[1]{0:T(128)} %bitcast.2, s32[1]{0:T(128)} %bitcast.3, s32[1]{0:T(128)} %bitcast.4, s32[1]{0:T(128)} %bitcast.5, s32[1]{0:T(128)} %bitcast.6, s32[1]{0:T(128)} %bitcast.7, s32[1]{0:T(128)} %bitcast.8, s32[1]{0:T(128)} %bitcast.9, s32[1]{0:T(128)} %bitcast.10, ...), dimensions={0} | concatenate | bytes 200 | tf_op jit(solution)/shard_map/concatenate | solution.py:536
  119.4 0.7 add.59
  120.1 2.3 %shard_map.384 = (f32[128,1280]{1,0:T(8,128)}, f32[128,1280]{1,0:T(8,128)}, f32[128,1280]{1,0:T(8,128)}) custom-call(s32[25]{0:T(128)S(1)} %concatenate.21.scalar_ref, bf16[4,192,384]{2,1,0:T(8,128)(2,1)S(1)} %pad_maximum_fusion.1.mine_ref, bf16[4,192,384]{2,1,0:T(8,128)(2,1)S(1)} %collective-permute-done.9.other_ref), custom_call_target="tpu_custom_call" | custom-call | tf_op jit(solution)/shard_map/pallas_call | solution.py:447
  (59 shorter events, 4.3 us)
Async XLA Ops:
  6.3 35.1 %copy-start.8 = (bf16[4,128,512]{2,1,0:T(8,128)(2,1)S(1)}, bf16[4,128,512]{2,1,0:T(8,128)(2,1)}, u32[]{:S(2)}) copy-start(bf16[4,128,512]{2,1,0:T(8,128)(2,1)} %get-tuple-element.15) | copy-start | bytes 1572868
  41.3 9.0 %copy-start.9 = (s32[4,4]{1,0:T(4,128)S(1)}, s32[4,4]{1,0:T(4,128)}, u32[]{:S(2)}) copy-start(s32[4,4]{1,0:T(4,128)} %param.46) | copy-start | bytes 196
  41.3 16.5 %collective-permute-start = (bf16[4,128,1152]{2,1,0:T(8,128)(2,1)S(1)}, bf16[4,128,1152]{2,1,0:T(8,128)(2,1)S(1)}, u32[]{:S(2)}, u32[]{:S(2)}) collective-permute-start(bf16[4,128,1152]{2,1,0:T(8,128)(2,1)S(1)} %all_to_all.5.refs_0_.refs_1_.refs_2_.refs_3_.refs_6_), channel_id=1, source_target_pairs={{0,1},{1,0},{2,3},{3,2},{4,5},{5,4},{6,7},{7,6},{8,9},{9,8},{10,11... | collective-permute-start | bytes 3538952 | tf_op jit(solution)/shard_map/ppermute | solution.py:46
  41.3 12.4 %copy-start.10 = (s32[4]{0:T(128)S(1)}, s32[4]{0:T(128)}, u32[]{:S(2)}) copy-start(s32[4]{0:T(128)} %constant.42.clone) | copy-start | bytes 52
  41.3 12.4 %copy-start.11 = (s32[4]{0:T(128)S(1)}, s32[4]{0:T(128)}, u32[]{:S(2)}) copy-start(s32[4]{0:T(128)} %constant.41.clone) | copy-start | bytes 52
  41.3 14.6 %copy-start.13 = (s32[4]{0:T(128)S(1)}, s32[4]{0:T(128)}, u32[]{:S(2)}) copy-start(s32[4]{0:T(128)} %constant.40.clone) | copy-start | bytes 52
  42.1 8.2 %collective-permute-start.1 = (bf16[1,128,512]{2,1,0:T(8,128)(2,1)}, bf16[1,128,512]{2,1,0:T(8,128)(2,1)S(1)}, u32[]{:S(2)}, u32[]{:S(2)}) collective-permute-start(bf16[1,128,512]{2,1,0:T(8,128)(2,1)} %get-tuple-element.43), channel_id=1, source_target_pairs={{0,4},{12,8},{1,5},{13,9},{2,6},{14,10},{3,7},{15,11},{16,20},{28,... | collective-permute-start | bytes 393224 | tf_op jit(solution)/shard_map/ppermute | solution.py:480
  44.2 8.1 %collective-permute-start.3 = (bf16[1,128,512]{2,1,0:T(8,128)(2,1)S(1)}, bf16[1,128,512]{2,1,0:T(8,128)(2,1)S(1)}, u32[]{:S(2)}, u32[]{:S(2)}) collective-permute-start(bf16[1,128,512]{2,1,0:T(8,128)(2,1)S(1)} %get-tuple-element.41), channel_id=1, source_target_pairs={{8,4},{4,8},{9,5},{5,9},{10,6},{6,10},{11,7},{7,11},{24,20},{20,24... | collective-permute-start | bytes 393224 | tf_op jit(solution)/shard_map/ppermute | solution.py:480
  44.9 7.4 %collective-permute-start.2 = (bf16[1,128,512]{2,1,0:T(8,128)(2,1)}, bf16[1,128,512]{2,1,0:T(8,128)(2,1)S(1)}, u32[]{:S(2)}, u32[]{:S(2)}) collective-permute-start(bf16[1,128,512]{2,1,0:T(8,128)(2,1)} %get-tuple-element.42), channel_id=1, source_target_pairs={{12,4},{0,8},{13,5},{1,9},{14,6},{2,10},{15,7},{3,11},{28,20},{16,... | collective-permute-start | bytes 393224 | tf_op jit(solution)/shard_map/ppermute | solution.py:480
  52.4 16.3 %collective-permute-start.4 = (bf16[4,128,512]{2,1,0:T(8,128)(2,1)S(1)}, bf16[4,128,512]{2,1,0:T(8,128)(2,1)S(1)}, u32[]{:S(2)}, u32[]{:S(2)}) collective-permute-start(bf16[4,128,512]{2,1,0:T(8,128)(2,1)S(1)} %constant_dynamic-update-slice_fusion.refs_0_.refs_1_.refs_2_.refs_3_), channel_id=1, source_target_pairs={{0,1},{1,0},{2,3},{3,2},{4,5},{5,4},{6,7},{7,6},{8,9},{9,8},{10,11... | collective-permute-start | bytes 1572872 | tf_op jit(solution)/shard_map/ppermute | solution.py:46
  57.8 1.0 copy-start
  58.8 1.0 copy-start.2
  59.7 1.0 copy-start.3
  60.7 8.0 %copy-start.1 = (bf16[128,1280]{1,0:T(8,128)(2,1)S(1)}, bf16[128,1280]{1,0:T(8,128)(2,1)}, u32[]{:S(2)}) copy-start(bf16[128,1280]{1,0:T(8,128)(2,1)} %refs_8_.5) | copy-start | bytes 983044
  68.6 0.8 copy-start.4
  69.5 0.8 copy-start.6
  70.3 1.0 copy-start.5
  70.3 1.2 copy-start.7
  70.4 9.3 %collective-permute-start.5 = (f32[192,384]{1,0:T(8,128)S(1)}, f32[192,384]{1,0:T(8,128)S(1)}, u32[]{:S(2)}, u32[]{:S(2)}) collective-permute-start(f32[192,384]{1,0:T(8,128)S(1)} %constant_dynamic-slice_fusion.3), channel_id=1, source_target_pairs={{0,1},{1,0},{2,3},{3,2},{4,5},{5,4},{6,7},{7,6},{8,9},{9,8},{10,11... | collective-permute-start | bytes 884744 | tf_op jit(solution)/shard_map/ppermute | solution.py:46
  71.6 11.7 %collective-permute-start.10 = (bf16[2,1,128,128]{3,2,1,0:T(8,128)(2,1)S(1)}, bf16[2,1,128,128]{3,2,1,0:T(8,128)(2,1)S(1)}, u32[]{:S(2)}, u32[]{:S(2)}) collective-permute-start(bf16[2,1,128,128]{3,2,1,0:T(8,128)(2,1)S(1)} %get-tuple-element.38), channel_id=1, source_target_pairs={{4,0},{0,4},{12,8},{8,12},{5,1},{1,5},{13,9},{9,13},{6,2},{2,6},{1... | collective-permute-start | bytes 196616 | tf_op jit(solution)/shard_map/ppermute | solution.py:480
  77.3 6.9 %collective-permute-start.12 = (bf16[2,1,128,128]{3,2,1,0:T(8,128)(2,1)S(1)}, bf16[2,1,128,128]{3,2,1,0:T(8,128)(2,1)S(1)}, u32[]{:S(2)}, u32[]{:S(2)}) collective-permute-start(bf16[2,1,128,128]{3,2,1,0:T(8,128)(2,1)S(1)} %get-tuple-element.39), channel_id=1, source_target_pairs={{12,0},{8,4},{4,8},{0,12},{13,1},{9,5},{5,9},{1,13},{14,2},{10,6},... | collective-permute-start | bytes 196616 | tf_op jit(solution)/shard_map/ppermute | solution.py:480
  79.7 13.1 %collective-permute-start.11 = (bf16[2,1,128,128]{3,2,1,0:T(8,128)(2,1)S(1)}, bf16[2,1,128,128]{3,2,1,0:T(8,128)(2,1)S(1)}, u32[]{:S(2)}, u32[]{:S(2)}) collective-permute-start(bf16[2,1,128,128]{3,2,1,0:T(8,128)(2,1)S(1)} %get-tuple-element.40), channel_id=1, source_target_pairs={{8,0},{12,4},{0,8},{4,12},{9,1},{13,5},{1,9},{5,13},{10,2},{14,6},... | collective-permute-start | bytes 196616 | tf_op jit(solution)/shard_map/ppermute | solution.py:480
  79.7 23.9 %copy-start.12 = (s32[4]{0:T(128)S(1)}, s32[4]{0:T(128)}, u32[]{:S(2)}) copy-start(s32[4]{0:T(128)} %constant.45.clone) | copy-start | bytes 52
  79.7 13.1 %collective-permute-start.8 = (bf16[192,384]{1,0:T(8,128)(2,1)S(1)}, bf16[192,384]{1,0:T(8,128)(2,1)S(1)}, u32[]{:S(2)}, u32[]{:S(2)}) collective-permute-start(bf16[192,384]{1,0:T(8,128)(2,1)S(1)} %add_convert_fusion), channel_id=1, source_target_pairs={{12,0},{8,4},{4,8},{0,12},{13,1},{9,5},{5,9},{1,13},{14,2},{10,6},... | collective-permute-start | bytes 442376 | tf_op jit(solution)/shard_map/ppermute | solution.py:480
  81.3 17.7 %collective-permute-start.7 = (bf16[192,384]{1,0:T(8,128)(2,1)S(1)}, bf16[192,384]{1,0:T(8,128)(2,1)S(1)}, u32[]{:S(2)}, u32[]{:S(2)}) collective-permute-start(bf16[192,384]{1,0:T(8,128)(2,1)S(1)} %add_convert_fusion), channel_id=1, source_target_pairs={{8,0},{12,4},{0,8},{4,12},{9,1},{13,5},{1,9},{5,13},{10,2},{14,6},... | collective-permute-start | bytes 442376 | tf_op jit(solution)/shard_map/ppermute | solution.py:480
  83.3 15.8 %collective-permute-start.6 = (bf16[192,384]{1,0:T(8,128)(2,1)S(1)}, bf16[192,384]{1,0:T(8,128)(2,1)S(1)}, u32[]{:S(2)}, u32[]{:S(2)}) collective-permute-start(bf16[192,384]{1,0:T(8,128)(2,1)S(1)} %add_convert_fusion), channel_id=1, source_target_pairs={{4,0},{0,4},{12,8},{8,12},{5,1},{1,5},{13,9},{9,13},{6,2},{2,6},{1... | collective-permute-start | bytes 442376 | tf_op jit(solution)/shard_map/ppermute | solution.py:480
  99.1 21.0 %collective-permute-start.9 = (bf16[4,192,384]{2,1,0:T(8,128)(2,1)S(1)}, bf16[4,192,384]{2,1,0:T(8,128)(2,1)S(1)}, u32[]{:S(2)}, u32[]{:S(2)}) collective-permute-start(bf16[4,192,384]{2,1,0:T(8,128)(2,1)S(1)} %pad_maximum_fusion.1.mine_ref), channel_id=1, source_target_pairs={{0,1},{1,0},{2,3},{3,2},{4,5},{5,4},{6,7},{7,6},{8,9},{9,8},{10,11... | collective-permute-start | bytes 1769480 | tf_op jit(solution)/shard_map/ppermute | solution.py:46
  99.3 2.1 %collective-permute-start.13 = (f32[256,128]{1,0:T(8,128)S(1)}, f32[256,128]{1,0:T(8,128)S(1)}, u32[]{:S(2)}, u32[]{:S(2)}) collective-permute-start(f32[256,128]{1,0:T(8,128)S(1)} %maximum_select_fusion), channel_id=1, source_target_pairs={{0,1},{1,0},{2,3},{3,2},{4,5},{5,4},{6,7},{7,6},{8,9},{9,8},{10,11... | collective-permute-start | bytes 393224 | tf_op jit(solution)/shard_map/ppermute | solution.py:46
  101.4 18.0 %collective-permute-start.14 = (f32[256,128]{1,0:T(8,128)S(1)}, f32[256,128]{1,0:T(8,128)S(1)}, u32[]{:S(2)}, u32[]{:S(2)}) collective-permute-start(f32[256,128]{1,0:T(8,128)S(1)} %add.58), channel_id=1, source_target_pairs={{0,2},{2,0},{1,3},{3,1},{4,6},{6,4},{5,7},{7,5},{8,10},{10,8},{9,1... | collective-permute-start | bytes 393224 | tf_op jit(solution)/shard_map/ppermute | solution.py:46

commit v3 on v1

--- a/solution.py
+++ b/solution.py
@@ -161,7 +161,7 @@
     return jnp.concatenate([first, second], axis=1).astype(F32)
 
 
-def on_device(
+def window_plan(
     frozen_query,
     frozen_key,
     frozen_value,
@@ -240,6 +240,394 @@
     return grads[:rank], grads[rank : 2 * rank], grads[2 * rank :], low
 
 
+def head_table(heads, frames):
+    base, extra = divmod(heads, frames)
+    lead = (frames - extra) // 2
+    counts = [base + (1 if lead <= j < lead + extra else 0) for j in range(frames)]
+    return [sum(counts[:j]) for j in range(frames)], counts
+
+
+def lookup(table, index):
+    value = jnp.int32(table[0])
+    for j in range(1, len(table)):
+        value = jnp.where(index == j, jnp.int32(table[j]), value)
+    return value
+
+
+def column(head):
+    return pl.ds(pl.multiple_of(head * DH, DH), DH)
+
+
+def vmem(count):
+    return [pl.BlockSpec(memory_space=pltpu.VMEM)] * count
+
+
+def pack_kernel(tables, frames, with_t, fq_ref, do_ref, fk_ref, fv_ref, t_ref, *outs):
+    me, half = lax.axis_index("tm"), lax.axis_index("rep")
+    rows = fq_ref.shape[0]
+    for m in range(frames + 1):
+        out = outs[m]
+        tile = half if m < frames else 1 - half
+        own = pl.ds(pl.multiple_of(tile * rows, rows), rows)
+        for s, table in enumerate(tables):
+            cols = column(lookup(table, me ^ m if m < frames else me))
+            at = 4 * s * DH
+            if m < frames:
+                out[:, at : at + DH] = fq_ref[:, cols]
+                out[:, at + DH : at + 2 * DH] = do_ref[:, cols]
+            out[:, at + 2 * DH : at + 3 * DH] = fk_ref[own, cols]
+            out[:, at + 3 * DH : at + 4 * DH] = fv_ref[own, cols]
+        if with_t:
+            out[:, 4 * len(tables) * DH :] = t_ref[own, :]
+
+
+def pack(tables, frames, with_t, fq, do, fk, fv, t):
+    rows = fq.shape[0]
+    width = 4 * DH * len(tables) + (t.shape[1] if with_t else 0)
+    return pl.pallas_call(
+        functools.partial(pack_kernel, tables, frames, with_t),
+        in_specs=vmem(5),
+        out_specs=vmem(frames + 1),
+        out_shape=[jax.ShapeDtypeStruct((rows, width), BF16)] * (frames + 1),
+        compiler_params=pltpu.CompilerParams(vmem_limit_bytes=32 * 1024 * 1024),
+    )(fq, do, fk, fv, t)
+
+
+def one_head(frames, bands, q, do, frozen_k, frozen_v, t_same, t_other, aq, ak, av):
+    flat = t_same.shape[0]
+    rows = flat // frames
+    tokens = jnp.concatenate([t_same, t_other], axis=0)
+
+    def adapted(frozen, rows_of, adapter):
+        return (frozen.astype(F32) + dot_nn(rows_of, adapter)).astype(BF16)
+
+    query = adapted(q, t_same, aq)
+    keys, values = adapted(frozen_k, tokens, ak), adapted(frozen_v, tokens, av)
+    do_t, keys_t, values_t = do.T, keys.T, values.T
+
+    def bias(i, b):
+        j, need = (b, 0) if b < frames else (b - frames, 1)
+        value = jnp.where(bands[i, j] > need, 0.0, -jnp.inf).astype(F32)
+        return jnp.full((1, rows), value, F32)
+
+    span = 2 if frames % 2 == 0 else 1
+    wide = span * rows
+    dks, dvs, dqs = [None] * (2 * frames), [None] * (2 * frames), []
+    for first in range(0, frames, span):
+        mine = range(first, first + span)
+        blocks = list(range(frames)) + [
+            frames + j for j in range(frames) if any(abs(i - j) <= NEAR for i in mine)
+        ]
+        here = slice(first * rows, first * rows + wide)
+        q_p, do_p = query[here], do[here]
+
+        def gather(whole, axis):
+            parts = [
+                whole[b * rows : (b + 1) * rows] if axis == 0 else whole[:, b * rows : (b + 1) * rows]
+                for b in blocks
+            ]
+            return jnp.concatenate(parts, axis=axis)
+
+        raw = dot_nt(gather(keys, 0), q_p)
+        scores = [
+            raw[n * rows : (n + 1) * rows] * SCALE + jnp.concatenate([bias(i, b) for i in mine], axis=1)
+            for n, b in enumerate(blocks)
+        ]
+        top = jnp.max(functools.reduce(jnp.maximum, scores), axis=0, keepdims=True)
+        shifted = [jnp.exp(s - top) for s in scores]
+        inverse = 1.0 / jnp.sum(functools.reduce(jnp.add, shifted), axis=0, keepdims=True)
+        probs = [s * inverse for s in shifted]
+        low = jnp.concatenate([p.astype(BF16) for p in probs], axis=0)
+        attended = dot_nn(gather(values_t, 1), low).astype(BF16).astype(F32)
+        delta = jnp.sum(do_t[:, here].astype(F32) * attended, axis=0, keepdims=True)
+        prob_grad = dot_nt(gather(values, 0), do_p)
+        grad = jnp.concatenate(
+            [
+                (probs[n] * (prob_grad[n * rows : (n + 1) * rows] - delta)).astype(BF16)
+                for n in range(len(blocks))
+            ],
+            axis=0,
+        )
+        dqs.append((dot_nn(gather(keys_t, 1), grad) * SCALE).astype(BF16).T)
+        dk, dv = dot_nn(grad, q_p), dot_nn(low, do_p)
+        for n, b in enumerate(blocks):
+            part = slice(n * rows, (n + 1) * rows)
+            dks[b] = dk[part] if dks[b] is None else dks[b] + dk[part]
+            dvs[b] = dv[part] if dvs[b] is None else dvs[b] + dv[part]
+    dq = jnp.concatenate(dqs, axis=0)
+    dk = (jnp.concatenate(dks, axis=0) * SCALE).astype(BF16)
+    dv = jnp.concatenate(dvs, axis=0).astype(BF16)
+    both = jnp.concatenate([dk, dv], axis=1)
+    sums = dot_tn(tokens, both)
+    grads = jnp.concatenate([dot_tn(t_same, dq), sums[:, :DH], sums[:, DH:]], axis=0)
+    lows = dot_nt(both, jnp.concatenate([ak, av], axis=1))
+    return grads, lows[:flat] + dot_nt(dq, aq), lows[flat:]
+
+
+def group_kernel(tables, frames, counts, t_col, chained, last, *refs):
+    refs = list(refs)
+    bands = refs.pop(0)
+    mine, others = [refs.pop(0) for _ in range(frames)], [refs.pop(0) for _ in range(frames)]
+    if t_col is None:
+        t_mine, t_others = [refs.pop(0) for _ in range(frames)], [refs.pop(0) for _ in range(frames)]
+    adapters = [refs.pop(0) for _ in range(3)]
+    before = [refs.pop(0) for _ in range(2)] if chained else None
+    keep_ref, give_ref = refs.pop(0), refs.pop(0)
+    low_refs = None if last else [refs.pop(0) for _ in range(2)]
+    same, other = refs.pop(0), refs.pop(0)
+    t_same, t_other = refs.pop(0), refs.pop(0)
+    me, half = lax.axis_index("tm"), lax.axis_index("rep")
+    rows = mine[0].shape[0]
+    flat = frames * rows
+    rank = t_same.shape[1]
+    cut = 3 * rank // 2
+    slots = len(tables)
+    main = 4 * slots * DH
+    for m in range(frames):
+        at = pl.ds(pl.multiple_of((me ^ m) * rows, rows), rows)
+        same[at, :] = mine[m][:, :main]
+        other[at, :] = others[m][:, :main]
+        t_same[at, :] = t_mine[m][...] if t_col is None else mine[m][:, main:]
+        t_other[at, :] = t_others[m][...] if t_col is None else others[m][:, main:]
+
+    def body():
+        total_same = before[0][...] if chained else None
+        total_other = before[1][...] if chained else None
+        for s, table in enumerate(tables):
+            cols = column(lookup(table, me))
+            at = 4 * s * DH
+            kv = [
+                jnp.concatenate([ref[:, at + c * DH : at + (c + 1) * DH] for ref in (same, other)], axis=0)
+                for c in (2, 3)
+            ]
+            grads, low_same, low_other = one_head(
+                frames, bands, same[:, at : at + DH], same[:, at + DH : at + 2 * DH], *kv,
+                t_same[...], t_other[...], *[ref[:, cols] for ref in adapters],
+            )
+            first = half == 0
+            keep_ref[s * cut : (s + 1) * cut, :] = jnp.where(first, grads[:cut], grads[cut:])
+            give_ref[s * cut : (s + 1) * cut, :] = jnp.where(first, grads[cut:], grads[:cut])
+            total_same = low_same if total_same is None else total_same + low_same
+            total_other = low_other if total_other is None else total_other + low_other
+        if last:
+            keep_ref[slots * cut :, :] = total_same
+            give_ref[slots * cut :, :] = total_other
+        else:
+            low_refs[0][...] = total_same
+            low_refs[1][...] = total_other
+
+    if min(counts) > 0:
+        body()
+    else:
+        live = lookup(counts, me) > 0
+        pl.when(live)(body)
+
+        @pl.when(jnp.logical_not(live))
+        def _():
+            zeros = jnp.zeros((slots * cut, DH), F32)
+            keep_ref[: slots * cut, :] = zeros
+            give_ref[: slots * cut, :] = zeros
+            keep_ref[slots * cut :, :] = before[0][...]
+            give_ref[slots * cut :, :] = before[1][...]
+
+
+def head_group(tables, counts, bands, mine, others, t_mine, t_others, adapters, before, last):
+    frames, rows = len(mine), mine[0].shape[0]
+    rank = adapters[0].shape[0]
+    slots = len(tables)
+    flat = frames * rows
+    size = slots * 3 * rank // 2
+    low = jax.ShapeDtypeStruct((flat, rank), F32)
+    main = 4 * slots * DH
+    inline = t_mine is None
+    args = [bands, *mine, *others]
+    specs = [pl.BlockSpec(memory_space=pltpu.SMEM)] + vmem(2 * frames)
+    if not inline:
+        col = t_mine[0].shape[1] // rank - 1
+        args += [*t_mine, *t_others]
+        specs += [pl.BlockSpec((rows, rank), lambda n: (0, col))] * (2 * frames)
+    args += adapters
+    specs += vmem(3)
+    if before is not None:
+        args += before
+        specs += vmem(2)
+    edge = jax.ShapeDtypeStruct((size + (flat if last else 0), rank), F32)
+    shapes = [edge, edge] + ([] if last else [low, low])
+    return pl.pallas_call(
+        functools.partial(
+            group_kernel, tables, frames, counts, main if inline else None, before is not None, last
+        ),
+        grid=(1,),
+        in_specs=specs,
+        out_specs=vmem(len(shapes)),
+        out_shape=shapes,
+        scratch_shapes=[
+            pltpu.VMEM((flat, main), BF16),
+            pltpu.VMEM((flat, main), BF16),
+            pltpu.VMEM((flat, rank), BF16),
+            pltpu.VMEM((flat, rank), BF16),
+        ],
+        compiler_params=pltpu.CompilerParams(vmem_limit_bytes=48 * 1024 * 1024),
+    )(*args)
+
+
+def hand_out_kernel(frames, size, keep_ref, got_ref, own_ref, *sends):
+    me = lax.axis_index("tm")
+    rows = own_ref.shape[0]
+    grads = (keep_ref[:size, :] + got_ref[:size, :]).astype(BF16)
+    for m in range(frames):
+        at = pl.ds(pl.multiple_of(size + (me ^ m) * rows, 8), rows)
+        low = keep_ref[at, :] + got_ref[at, :]
+        if m == 0:
+            own_ref[...] = low
+        sends[m][:rows, :] = low.astype(BF16)
+        sends[m][rows:, :] = grads
+
+
+def hand_out(frames, rows, keep, got):
+    size, rank = keep.shape[0] - frames * rows, keep.shape[1]
+    send = jax.ShapeDtypeStruct((rows + size, rank), BF16)
+    return pl.pallas_call(
+        functools.partial(hand_out_kernel, frames, size),
+        in_specs=vmem(2),
+        out_specs=vmem(frames + 1),
+        out_shape=[jax.ShapeDtypeStruct((rows, rank), F32)] + [send] * frames,
+    )(keep, got)
+
+
+def collect_kernel(frames, own_ref, *refs):
+    gots, out_ref = refs[:-1], refs[-1]
+    rows = own_ref.shape[0]
+    size = gots[0].shape[0] - rows
+    low = own_ref[...]
+    for m in range(1, frames):
+        low = low + gots[m][:rows, :].astype(F32)
+    out_ref[:rows, :] = low.astype(BF16)
+    for m in range(frames):
+        out_ref[rows + m * size : rows + (m + 1) * size, :] = gots[m][rows:, :]
+
+
+def collect(own, gots):
+    frames, (rows, rank) = len(gots), own.shape
+    size = gots[0].shape[0] - rows
+    return pl.pallas_call(
+        functools.partial(collect_kernel, frames),
+        in_specs=vmem(frames + 1),
+        out_specs=pl.BlockSpec(memory_space=pltpu.VMEM),
+        out_shape=jax.ShapeDtypeStruct((rows + frames * size, rank), BF16),
+    )(own, *gots)
+
+
+def place_kernel(table, counts, full, *refs):
+    frames = len(table)
+    mine, others = refs[:frames], refs[frames : 2 * frames]
+    tail, tail2, low_head, low_diag = refs[2 * frames : 2 * frames + 4]
+    outs = refs[2 * frames + 4 :]
+    me, half = lax.axis_index("tm"), lax.axis_index("rep")
+    first = half == 0
+    rank = outs[0].shape[0]
+    cut = 3 * rank // 2
+    rows = low_head.shape[0]
+    same = tail[:rows, :].astype(F32) + low_head[...].astype(F32)
+    other = tail2[:rows, :].astype(F32) + low_diag[...].astype(F32)
+    outs[3][:rows, :] = jnp.where(first, same, other)
+    outs[3][rows:, :] = jnp.where(first, other, same)
+    for m in range(frames):
+        chip = me ^ m
+        for s in range(len(table[0])):
+            if s < full:
+                a, b = mine[m][s * cut : (s + 1) * cut, :], others[m][s * cut : (s + 1) * cut, :]
+            else:
+                at = rows + (m * (len(table[0]) - full) + s - full) * cut
+                a, b = tail[at : at + cut, :], tail2[at : at + cut, :]
+            a, b = a.astype(F32), b.astype(F32)
+
+            def write():
+                cols = column(lookup([row[s] for row in table], chip))
+                both = jnp.concatenate([jnp.where(first, a, b), jnp.where(first, b, a)], axis=0)
+                for o in range(3):
+                    outs[o][:, cols] = both[o * rank : (o + 1) * rank]
+
+            if s < full:
+                write()
+            else:
+                pl.when(lookup(counts, chip) > s)(write)
+
+
+def place(table, counts, mine, others, tail, tail2, low_head, low_diag, rank, width):
+    rows = low_head.shape[0]
+    full = min(counts)
+    return pl.pallas_call(
+        functools.partial(place_kernel, table, counts, full),
+        in_specs=vmem(2 * len(table) + 4),
+        out_specs=vmem(4),
+        out_shape=[jax.ShapeDtypeStruct((rank, width), F32)] * 3
+        + [jax.ShapeDtypeStruct((2 * rows, rank), F32)],
+        compiler_params=pltpu.CompilerParams(vmem_limit_bytes=32 * 1024 * 1024),
+    )(*mine, *others, tail, tail2, low_head, low_diag)
+
+
+def exchange_plan(
+    frozen_query,
+    frozen_key,
+    frozen_value,
+    token_adapter_input,
+    query_adapter_out,
+    key_adapter_out,
+    value_adapter_out,
+    out_grad,
+    band_width,
+):
+    rows, width = frozen_query.shape
+    rank = token_adapter_input.shape[1]
+    frames = band_width.shape[0]
+    heads = width // DH
+    starts, counts = head_table(heads, frames)
+    full, most = min(counts), max(counts)
+    table = [[min(starts[j] + s, heads - 1) for s in range(most)] for j in range(frames)]
+    columns = [[row[s] for row in table] for s in range(most)]
+    wide = [j for j in range(frames) if counts[j] == most]
+    adapters = [query_adapter_out, key_adapter_out, value_adapter_out]
+    arrays = (frozen_query, out_grad, frozen_key, frozen_value, token_adapter_input)
+
+    def meet(block, m, targets=range(frames)):
+        return lax.ppermute(block, "tm", [(j ^ m, j) for j in targets])
+
+    packed = pack(columns[:full], frames, True, *arrays)
+    mine = [packed[0]] + [meet(packed[m], m) for m in range(1, frames)]
+    packed2 = pack(columns[full:], frames, False, *arrays)
+    mine2 = [packed2[0]] + [meet(packed2[m], m, wide) for m in range(1, frames)]
+    others = [packed[frames]] + [swap(block, "rep") for block in mine[1:]]
+    others2 = [packed2[frames]] + [swap(block, "rep") for block in mine2[1:]]
+    keep, give, *low = head_group(
+        columns[:full], counts, band_width, mine, others, None, None, adapters, None, False
+    )
+    piece = (keep + swap(give, "rep")).astype(BF16)
+    pieces = [piece] + [meet(piece, m) for m in range(1, frames)]
+    pieces2 = [swap(block, "rep") for block in pieces]
+    keep, give = head_group(
+        columns[full:], [c - full for c in counts], band_width, mine2, others2, mine, others,
+        adapters, low, True,
+    )
+    own, *sends = hand_out(frames, rows, keep, swap(give, "rep"))
+    gots = [sends[0]] + [meet(sends[m], m) for m in range(1, frames)]
+    tail = collect(own, gots)
+    low = tail[:rows]
+    diag = [(0, 3), (1, 2), (2, 1), (3, 0)]
+    outs = place(
+        table, counts, pieces, pieces2, tail, swap(tail, "rep"), swap(low, "head"),
+        lax.ppermute(low, ("head", "rep"), diag), rank, width,
+    )
+    return tuple(outs)
+
+
+def on_device(frozen_query, *rest):
+    frames = rest[-1].shape[0]
+    heads = frozen_query.shape[1] // DH
+    whole_reach = frames <= REACH + 1 and frames & (frames - 1) == 0 and heads > frames and heads % frames
+    return (exchange_plan if whole_reach else window_plan)(frozen_query, *rest)
+
+
 def solution(mesh):
     in_specs = (
         P(("groups", "tm", "rep"), "head"),

time: 179 us -> 98 us (0.55)
  local copies, waits for them, and re-layouts: 36 us -> 8.77 us
  waiting for transfers between devices: 63 us -> 38.6 us
  Pallas kernels: 30.4 us -> 13.3 us
  between operations: 6.27 us -> 0.82 us
  other arithmetic: 3 us -> 0.02 us
  matrix products: 2.65 us -> 0 us
    ppermute x14 -> x13, waiting for transfers between devices: 54.8 us -> 35.8 us  [the longest x12 34 us: meet(): return lax.ppermute(block, 'tm', [(j ^ m, j) for j in targets])]
    pallas_call x1 -> x7, Pallas kernels: 30.4 us -> 13.3 us  [the longest x2 7.86 us: head_group(): pl.pallas_call(functools.partial(group_kernel, tables, frames, counts, ma...]
    slice x15 -> x1, local copies, waits for them, and re-layouts: 14.6 us -> 0.76 us  [exchange_plan(): low = tail[:rows]]
    unnamed x37 -> x30, local copies, waits for them, and re-layouts: 17.8 us -> 8.01 us
    ppermute x6 -> x14, waiting for transfers between devices: 8.16 us -> 2.77 us  [swap(): return lax.ppermute(block, axis, [(0, 1), (1, 0)])]
    dot_general x2 -> x0, matrix products: 2.65 us -> none  [dot_nn(): lax.dot_general(left, right, (((1,), (0,)), ((), ())), preferred_element_...]
    ppermute x14 -> x13, starting transfers between devices: 34.7 us -> 32.8 us  [the longest x12 31.7 us: meet(): return lax.ppermute(block, 'tm', [(j ^ m, j) for j in targets])]
    dynamic_slice x3 -> x0, local copies, waits for them, and re-layouts: 1.9 us -> none  [the longest x1 1.04 us: sum_rows(): give = lax.dynamic_slice_in_dim(part, (1 - half_idx) * half, half, 1)]
  transfers between devices with their start and end apart: 20 -> 27, of which waited for: 10 -> 8; matrix products, arithmetic and copies ran while one was open for 9% -> 1% of each run, Pallas kernels for 0% -> 11%
where the time goes in v3:
time: 98 us; the launch traced here: 97.4 us
  waiting for transfers between devices  38.6 us (39%)
  starting transfers between devices  35.9 us (37%)
  Pallas kernels  13.3 us (14%)
  local copies, waits for them, and re-layouts  8.77 us (9%)
    ppermute x12, waiting for transfers between devices, meet(): return lax.ppermute(block, 'tm', [(j ^ m, j) for j in targets])  34 us
    ppermute x12, starting transfers between devices, meet(): return lax.ppermute(block, 'tm', [(j ^ m, j) for j in targets])  31.7 us
    unnamed x30, local copies, waits for them, and re-layouts  8.01 us
    pallas_call x2, Pallas kernels, head_group(): pl.pallas_call(functools.partial(group_kernel, tables, frames, counts, ma...  7.86 us
    ppermute x14, starting transfers between devices, swap(): return lax.ppermute(block, axis, [(0, 1), (1, 0)])  3.16 us
    ppermute x14, waiting for transfers between devices, swap(): return lax.ppermute(block, axis, [(0, 1), (1, 0)])  2.77 us
  transfers between devices with their start and end apart: 27, of which 8 were waited for; matrix products, arithmetic and copies ran while one was open for 1% of the time, Pallas kernels for 11%

profile of v3, /device:TPU:0, one launch (start us, length us, event | category | flops | bytes accessed | tf_op | source)
XLA Modules:
  0.0 97.4 jit_solution(8576025031484024)
XLA Ops:
  0.6 1.1 %copy-done = bf16[256,1280]{1,0:T(8,128)(2,1)S(1)} copy-done((bf16[256,1280]{1,0:T(8,128)(2,1)S(1)}, bf16[256,1280]{1,0:T(8,128)(2,1)}, u32[]{:S(2)}) %copy-start) | copy-done | bytes 655384
  1.7 1.1 %copy-done.1 = bf16[256,1280]{1,0:T(8,128)(2,1)S(1)} copy-done((bf16[256,1280]{1,0:T(8,128)(2,1)S(1)}, bf16[256,1280]{1,0:T(8,128)(2,1)}, u32[]{:S(2)}) %copy-start.1) | copy-done | bytes 655384
  2.8 1.0 copy-done.2
  3.8 1.0 copy-done.3
  4.8 0.8 copy-done.9
  5.8 3.1 %collective-permute-start = (bf16[128,1152]{1,0:T(8,128)(2,1)S(1)}, bf16[128,1152]{1,0:T(8,128)(2,1)S(1)}, u32[]{:S(2)}, u32[]{:S(2)}) collective-permute-start(bf16[128,1152]{1,0:T(8,128)(2,1)S(1)} %get-tuple-element.26), channel_id=1, source_target_pairs={{4,0},{0,4},{12,8},{8,12},{5,1},{1,5},{13,9},{9,13},{6,2},{2,6},{1... | collective-permute-start | bytes 884744 | tf_op jit(solution)/shard_map/ppermute | solution.py:594
  8.9 2.6 %collective-permute-start.1 = (bf16[128,1152]{1,0:T(8,128)(2,1)S(1)}, bf16[128,1152]{1,0:T(8,128)(2,1)S(1)}, u32[]{:S(2)}, u32[]{:S(2)}) collective-permute-start(bf16[128,1152]{1,0:T(8,128)(2,1)S(1)} %get-tuple-element.27), channel_id=1, source_target_pairs={{8,0},{12,4},{0,8},{4,12},{9,1},{13,5},{1,9},{5,13},{10,2},{14,6},... | collective-permute-start | bytes 884744 | tf_op jit(solution)/shard_map/ppermute | solution.py:594
  11.5 10.0 %collective-permute-done.refs_2_.refs_10_ = bf16[128,1152]{1,0:T(8,128)(2,1)S(1)} collective-permute-done((bf16[128,1152]{1,0:T(8,128)(2,1)S(1)}, bf16[128,1152]{1,0:T(8,128)(2,1)S(1)}, u32[]{:S(2)}, u32[]{:S(2)}) %collective-permute-start) | collective-permute-done | bytes 294944 | tf_op jit(solution)/shard_map/ppermute | solution.py:594
  21.6 1.5 %collective-permute-start.14 = (bf16[128,512]{1,0:T(8,128)(2,1)S(1)}, bf16[128,512]{1,0:T(8,128)(2,1)S(1)}, u32[]{:S(2)}, u32[]{:S(2)}) collective-permute-start(bf16[128,512]{1,0:T(8,128)(2,1)S(1)} %get-tuple-element.33), channel_id=1, source_target_pairs={{0,4},{12,8},{1,5},{13,9},{2,6},{14,10},{3,7},{15,11},{16,20},{28,... | collective-permute-start | bytes 393224 | tf_op jit(solution)/shard_map/ppermute | solution.py:594
  23.1 9.3 %collective-permute-done.1.refs_3_.refs_11_ = bf16[128,1152]{1,0:T(8,128)(2,1)S(1)} collective-permute-done((bf16[128,1152]{1,0:T(8,128)(2,1)S(1)}, bf16[128,1152]{1,0:T(8,128)(2,1)S(1)}, u32[]{:S(2)}, u32[]{:S(2)}) %collective-permute-start.1) | collective-permute-done | bytes 294944 | tf_op jit(solution)/shard_map/ppermute | solution.py:594
  32.9 7.9 %collective-permute-start.15 = (bf16[128,512]{1,0:T(8,128)(2,1)S(1)}, bf16[128,512]{1,0:T(8,128)(2,1)S(1)}, u32[]{:S(2)}, u32[]{:S(2)}) collective-permute-start(bf16[128,512]{1,0:T(8,128)(2,1)S(1)} %get-tuple-element.34), channel_id=1, source_target_pairs={{12,4},{0,8},{13,5},{1,9},{14,6},{2,10},{15,7},{3,11},{28,20},{16,... | collective-permute-start | bytes 393224 | tf_op jit(solution)/shard_map/ppermute | solution.py:594
  41.5 2.7 %collective-permute-done.15.refs_3_ = bf16[128,512]{1,0:T(8,128)(2,1)S(1)} collective-permute-done((bf16[128,512]{1,0:T(8,128)(2,1)S(1)}, bf16[128,512]{1,0:T(8,128)(2,1)S(1)}, u32[]{:S(2)}, u32[]{:S(2)}) %collective-permute-start.15) | collective-permute-done | bytes 131104 | tf_op jit(solution)/shard_map/ppermute | solution.py:594
  44.9 7.1 %shard_map.121 = (f32[384,128]{1,0:T(8,128)S(1)}, f32[384,128]{1,0:T(8,128)S(1)}, f32[512,128]{1,0:T(8,128)S(1)}, f32[512,128]{1,0:T(8,128)S(1)}) custom-call(s32[4,4]{1,0:T(4,128)S(1)} %copy-done.10, bf16[128,1152]{1,0:T(8,128)(2,1)S(1)} %get-tuple-element.25.refs_1_.refs_9_, bf16[128,1152]{1,0:T(8,128)(2,1)S(1)} %collective-permute-done.refs_2_.refs_10_, ...), custom_call_target="tpu_custom_call" | custom-call | tf_op jit(solution)/shard_map/pallas_call | solution.py:456
  52.0 0.7 shard_map.123
  52.8 0.7 copy-done.8
  54.0 1.2 %collective-permute-done.20.got_ref = f32[704,128]{1,0:T(8,128)S(1)} collective-permute-done((f32[704,128]{1,0:T(8,128)S(1)}, f32[704,128]{1,0:T(8,128)S(1)}, u32[]{:S(2)}, u32[]{:S(2)}) %collective-permute-start.20) | collective-permute-done | bytes 360480 | tf_op jit(solution)/shard_map/ppermute | solution.py:46
  55.3 0.7 copy-done.11
  56.0 1.9 %shard_map.124 = (f32[128,128]{1,0:T(8,128)}, bf16[320,128]{1,0:T(8,128)(2,1)}, bf16[320,128]{1,0:T(8,128)(2,1)}, bf16[320,128]{1,0:T(8,128)(2,1)}, bf16[320,128]{1,0:T(8,128)(2,1)}) custom-call(f32[704,128]{1,0:T(8,128)} %copy-done.8, f32[704,128]{1,0:T(8,128)} %copy-done.11), custom_call_target="tpu_custom_call" | custom-call | tf_op jit(solution)/shard_map/pallas_call | solution.py:490
  57.8 8.2 %collective-permute-start.21 = (bf16[320,128]{1,0:T(8,128)(2,1)}, bf16[320,128]{1,0:T(8,128)(2,1)S(1)}, u32[]{:S(2)}, u32[]{:S(2)}) collective-permute-start(bf16[320,128]{1,0:T(8,128)(2,1)} %get-tuple-element.43), channel_id=1, source_target_pairs={{4,0},{0,4},{12,8},{8,12},{5,1},{1,5},{13,9},{9,13},{6,2},{2,6},{1... | collective-permute-start | bytes 245768 | tf_op jit(solution)/shard_map/ppermute | solution.py:594
  66.1 1.0 %collective-permute-start.22 = (bf16[320,128]{1,0:T(8,128)(2,1)}, bf16[320,128]{1,0:T(8,128)(2,1)S(1)}, u32[]{:S(2)}, u32[]{:S(2)}) collective-permute-start(bf16[320,128]{1,0:T(8,128)(2,1)} %get-tuple-element.44), channel_id=1, source_target_pairs={{8,0},{12,4},{0,8},{4,12},{9,1},{13,5},{1,9},{5,13},{10,2},{14,6},... | collective-permute-start | bytes 245768 | tf_op jit(solution)/shard_map/ppermute | solution.py:594
  67.1 1.5 %collective-permute-start.23 = (bf16[320,128]{1,0:T(8,128)(2,1)}, bf16[320,128]{1,0:T(8,128)(2,1)S(1)}, u32[]{:S(2)}, u32[]{:S(2)}) collective-permute-start(bf16[320,128]{1,0:T(8,128)(2,1)} %get-tuple-element.45), channel_id=1, source_target_pairs={{12,0},{8,4},{4,8},{0,12},{13,1},{9,5},{5,9},{1,13},{14,2},{10,6},... | collective-permute-start | bytes 245768 | tf_op jit(solution)/shard_map/ppermute | solution.py:594
  68.6 2.4 %collective-permute-start.9 = (bf16[384,128]{1,0:T(8,128)(2,1)S(1)}, bf16[384,128]{1,0:T(8,128)(2,1)S(1)}, u32[]{:S(2)}, u32[]{:S(2)}) collective-permute-start(bf16[384,128]{1,0:T(8,128)(2,1)S(1)} %add_convert_fusion.refs_0_), channel_id=1, source_target_pairs={{12,0},{8,4},{4,8},{0,12},{13,1},{9,5},{5,9},{1,13},{14,2},{10,6},... | collective-permute-start | bytes 294920 | tf_op jit(solution)/shard_map/ppermute | solution.py:594
  71.0 6.8 %collective-permute-done.22.refs_2_ = bf16[320,128]{1,0:T(8,128)(2,1)S(1)} collective-permute-done((bf16[320,128]{1,0:T(8,128)(2,1)}, bf16[320,128]{1,0:T(8,128)(2,1)S(1)}, u32[]{:S(2)}, u32[]{:S(2)}) %collective-permute-start.22) | collective-permute-done | bytes 81952 | tf_op jit(solution)/shard_map/ppermute | solution.py:594
  78.5 1.7 %shard_map.125.refs_8_ = bf16[896,128]{1,0:T(8,128)(2,1)} custom-call(f32[128,128]{1,0:T(8,128)} %get-tuple-element.41.own_ref, bf16[320,128]{1,0:T(8,128)(2,1)} %get-tuple-element.42.refs_0_, bf16[320,128]{1,0:T(8,128)(2,1)} %copy-done.12, bf16[320,128]{1,0:T(8,128)(2,1)} %copy-done.13, bf16[320,128]{1,0:T(8,128)(2,1)} %copy-done.14), custom_call_target="tpu_custom_call" | custom-call | tf_op jit(solution)/shard_map/pallas_call | solution.py:513
  80.2 2.9 %collective-permute-start.8 = (bf16[384,128]{1,0:T(8,128)(2,1)S(1)}, bf16[384,128]{1,0:T(8,128)(2,1)S(1)}, u32[]{:S(2)}, u32[]{:S(2)}) collective-permute-start(bf16[384,128]{1,0:T(8,128)(2,1)S(1)} %add_convert_fusion.refs_0_), channel_id=1, source_target_pairs={{8,0},{12,4},{0,8},{4,12},{9,1},{13,5},{1,9},{5,13},{10,2},{14,6},... | collective-permute-start | bytes 294920 | tf_op jit(solution)/shard_map/ppermute | solution.py:594
  83.6 5.1 %collective-permute-done.8.refs_2_ = bf16[384,128]{1,0:T(8,128)(2,1)S(1)} collective-permute-done((bf16[384,128]{1,0:T(8,128)(2,1)S(1)}, bf16[384,128]{1,0:T(8,128)(2,1)S(1)}, u32[]{:S(2)}, u32[]{:S(2)}) %collective-permute-start.8) | collective-permute-done | bytes 98336 | tf_op jit(solution)/shard_map/ppermute | solution.py:594
  89.2 0.8 slice.4
  90.0 1.1 %collective-permute-start.26 = (bf16[128,128]{1,0:T(8,128)(2,1)S(1)}, bf16[128,128]{1,0:T(8,128)(2,1)S(1)}, u32[]{:S(2)}, u32[]{:S(2)}) collective-permute-start(bf16[128,128]{1,0:T(8,128)(2,1)S(1)} %slice.4), channel_id=1, source_target_pairs={{0,3},{1,2},{2,1},{3,0},{4,7},{5,6},{6,5},{7,4},{8,11},{9,10},{10,... | collective-permute-start | bytes 98312 | tf_op jit(solution)/shard_map/ppermute | solution.py:619
  91.6 1.9 %collective-permute-done.26.refs_11_ = bf16[128,128]{1,0:T(8,128)(2,1)S(1)} collective-permute-done((bf16[128,128]{1,0:T(8,128)(2,1)S(1)}, bf16[128,128]{1,0:T(8,128)(2,1)S(1)}, u32[]{:S(2)}, u32[]{:S(2)}) %collective-permute-start.26) | collective-permute-done | bytes 32800 | tf_op jit(solution)/shard_map/ppermute | solution.py:619
  93.5 1.5 %collective-permute-done.25.refs_10_ = bf16[128,128]{1,0:T(8,128)(2,1)S(1)} collective-permute-done((bf16[128,128]{1,0:T(8,128)(2,1)S(1)}, bf16[128,128]{1,0:T(8,128)(2,1)S(1)}, u32[]{:S(2)}, u32[]{:S(2)}) %collective-permute-start.25) | collective-permute-done | bytes 32800 | tf_op jit(solution)/shard_map/ppermute | solution.py:46
  95.0 0.9 copy-done.7
  95.9 1.5 %shard_map.126 = (f32[128,1280]{1,0:T(8,128)}, f32[128,1280]{1,0:T(8,128)}, f32[128,1280]{1,0:T(8,128)}, f32[256,128]{1,0:T(8,128)}) custom-call(bf16[384,128]{1,0:T(8,128)(2,1)S(1)} %add_convert_fusion.refs_0_, bf16[384,128]{1,0:T(8,128)(2,1)S(1)} %collective-permute-done.7.refs_1_, bf16[384,128]{1,0:T(8,128)(2,1)S(1)} %collective-permute-done.8.refs_2_, ...), custom_call_target="tpu_custom_call" | custom-call | tf_op jit(solution)/shard_map/pallas_call | solution.py:560
  (61 shorter events, 4.9 us)
Async XLA Ops:
  5.8 15.6 %collective-permute-start = (bf16[128,1152]{1,0:T(8,128)(2,1)S(1)}, bf16[128,1152]{1,0:T(8,128)(2,1)S(1)}, u32[]{:S(2)}, u32[]{:S(2)}) collective-permute-start(bf16[128,1152]{1,0:T(8,128)(2,1)S(1)} %get-tuple-element.26), channel_id=1, source_target_pairs={{4,0},{0,4},{12,8},{8,12},{5,1},{1,5},{13,9},{9,13},{6,2},{2,6},{1... | collective-permute-start | bytes 884744 | tf_op jit(solution)/shard_map/ppermute | solution.py:594
  8.9 23.5 %collective-permute-start.1 = (bf16[128,1152]{1,0:T(8,128)(2,1)S(1)}, bf16[128,1152]{1,0:T(8,128)(2,1)S(1)}, u32[]{:S(2)}, u32[]{:S(2)}) collective-permute-start(bf16[128,1152]{1,0:T(8,128)(2,1)S(1)} %get-tuple-element.27), channel_id=1, source_target_pairs={{8,0},{12,4},{0,8},{4,12},{9,1},{13,5},{1,9},{5,13},{10,2},{14,6},... | collective-permute-start | bytes 884744 | tf_op jit(solution)/shard_map/ppermute | solution.py:594
  11.5 33.3 %copy-start.4 = (bf16[128,1280]{1,0:T(8,128)(2,1)S(1)}, bf16[128,1280]{1,0:T(8,128)(2,1)}, u32[]{:S(2)}) copy-start(bf16[128,1280]{1,0:T(8,128)(2,1)} %refs_17_.1) | copy-start | bytes 983044
  11.5 33.3 %copy-start.5 = (bf16[128,1280]{1,0:T(8,128)(2,1)S(1)}, bf16[128,1280]{1,0:T(8,128)(2,1)}, u32[]{:S(2)}) copy-start(bf16[128,1280]{1,0:T(8,128)(2,1)} %refs_18_.1) | copy-start | bytes 983044
  11.5 33.3 %copy-start.6 = (bf16[128,1280]{1,0:T(8,128)(2,1)S(1)}, bf16[128,1280]{1,0:T(8,128)(2,1)}, u32[]{:S(2)}) copy-start(bf16[128,1280]{1,0:T(8,128)(2,1)} %refs_19_.1) | copy-start | bytes 983044
  11.5 20.9 %collective-permute-start.2 = (bf16[128,1152]{1,0:T(8,128)(2,1)S(1)}, bf16[128,1152]{1,0:T(8,128)(2,1)S(1)}, u32[]{:S(2)}, u32[]{:S(2)}) collective-permute-start(bf16[128,1152]{1,0:T(8,128)(2,1)S(1)} %get-tuple-element.28), channel_id=1, source_target_pairs={{12,0},{8,4},{4,8},{0,12},{13,1},{9,5},{5,9},{1,13},{14,2},{10,6},... | collective-permute-start | bytes 884744 | tf_op jit(solution)/shard_map/ppermute | solution.py:594
  21.5 23.3 %collective-permute-start.3 = (bf16[128,1152]{1,0:T(8,128)(2,1)S(1)}, bf16[128,1152]{1,0:T(8,128)(2,1)S(1)}, u32[]{:S(2)}, u32[]{:S(2)}) collective-permute-start(bf16[128,1152]{1,0:T(8,128)(2,1)S(1)} %collective-permute-done.refs_2_.refs_10_), channel_id=1, source_target_pairs={{0,1},{1,0},{2,3},{3,2},{4,5},{5,4},{6,7},{7,6},{8,9},{9,8},{10,11... | collective-permute-start | bytes 884744 | tf_op jit(solution)/shard_map/ppermute | solution.py:46
  21.6 19.2 %collective-permute-start.14 = (bf16[128,512]{1,0:T(8,128)(2,1)S(1)}, bf16[128,512]{1,0:T(8,128)(2,1)S(1)}, u32[]{:S(2)}, u32[]{:S(2)}) collective-permute-start(bf16[128,512]{1,0:T(8,128)(2,1)S(1)} %get-tuple-element.33), channel_id=1, source_target_pairs={{0,4},{12,8},{1,5},{13,9},{2,6},{14,10},{3,7},{15,11},{16,20},{28,... | collective-permute-start | bytes 393224 | tf_op jit(solution)/shard_map/ppermute | solution.py:594
  32.4 12.4 %collective-permute-start.4 = (bf16[128,1152]{1,0:T(8,128)(2,1)S(1)}, bf16[128,1152]{1,0:T(8,128)(2,1)S(1)}, u32[]{:S(2)}, u32[]{:S(2)}) collective-permute-start(bf16[128,1152]{1,0:T(8,128)(2,1)S(1)} %collective-permute-done.1.refs_3_.refs_11_), channel_id=1, source_target_pairs={{0,1},{1,0},{2,3},{3,2},{4,5},{5,4},{6,7},{7,6},{8,9},{9,8},{10,11... | collective-permute-start | bytes 884744 | tf_op jit(solution)/shard_map/ppermute | solution.py:46
  32.4 12.4 %collective-permute-start.5 = (bf16[128,1152]{1,0:T(8,128)(2,1)S(1)}, bf16[128,1152]{1,0:T(8,128)(2,1)S(1)}, u32[]{:S(2)}, u32[]{:S(2)}) collective-permute-start(bf16[128,1152]{1,0:T(8,128)(2,1)S(1)} %collective-permute-done.2.refs_4_.refs_12_), channel_id=1, source_target_pairs={{0,1},{1,0},{2,3},{3,2},{4,5},{5,4},{6,7},{7,6},{8,9},{9,8},{10,11... | collective-permute-start | bytes 884744 | tf_op jit(solution)/shard_map/ppermute | solution.py:46
  32.9 11.3 %collective-permute-start.15 = (bf16[128,512]{1,0:T(8,128)(2,1)S(1)}, bf16[128,512]{1,0:T(8,128)(2,1)S(1)}, u32[]{:S(2)}, u32[]{:S(2)}) collective-permute-start(bf16[128,512]{1,0:T(8,128)(2,1)S(1)} %get-tuple-element.34), channel_id=1, source_target_pairs={{12,4},{0,8},{13,5},{1,9},{14,6},{2,10},{15,7},{3,11},{28,20},{16,... | collective-permute-start | bytes 393224 | tf_op jit(solution)/shard_map/ppermute | solution.py:594
  40.8 4.1 %copy-start.10 = (s32[4,4]{1,0:T(4,128)S(1)}, s32[4,4]{1,0:T(4,128)}, u32[]{:S(2)}) copy-start(s32[4,4]{1,0:T(4,128)} %refs_0_.3) | copy-start | bytes 196
  40.8 3.4 %collective-permute-start.16 = (bf16[128,512]{1,0:T(8,128)(2,1)S(1)}, bf16[128,512]{1,0:T(8,128)(2,1)S(1)}, u32[]{:S(2)}, u32[]{:S(2)}) collective-permute-start(bf16[128,512]{1,0:T(8,128)(2,1)S(1)} %get-tuple-element.35), channel_id=1, source_target_pairs={{8,4},{4,8},{9,5},{5,9},{10,6},{6,10},{11,7},{7,11},{24,20},{20,24... | collective-permute-start | bytes 393224 | tf_op jit(solution)/shard_map/ppermute | solution.py:594
  44.2 7.8 %collective-permute-start.17 = (bf16[128,512]{1,0:T(8,128)(2,1)S(1)}, bf16[128,512]{1,0:T(8,128)(2,1)S(1)}, u32[]{:S(2)}, u32[]{:S(2)}) collective-permute-start(bf16[128,512]{1,0:T(8,128)(2,1)S(1)} %collective-permute-done.14.refs_2_), channel_id=1, source_target_pairs={{0,1},{1,0},{2,3},{3,2},{4,5},{5,4},{6,7},{7,6},{8,9},{9,8},{10,11... | collective-permute-start | bytes 393224 | tf_op jit(solution)/shard_map/ppermute | solution.py:46
  44.2 7.8 %collective-permute-start.18 = (bf16[128,512]{1,0:T(8,128)(2,1)S(1)}, bf16[128,512]{1,0:T(8,128)(2,1)S(1)}, u32[]{:S(2)}, u32[]{:S(2)}) collective-permute-start(bf16[128,512]{1,0:T(8,128)(2,1)S(1)} %collective-permute-done.15.refs_3_), channel_id=1, source_target_pairs={{0,1},{1,0},{2,3},{3,2},{4,5},{5,4},{6,7},{7,6},{8,9},{9,8},{10,11... | collective-permute-start | bytes 393224 | tf_op jit(solution)/shard_map/ppermute | solution.py:46
  44.8 7.3 %collective-permute-start.19 = (bf16[128,512]{1,0:T(8,128)(2,1)S(1)}, bf16[128,512]{1,0:T(8,128)(2,1)S(1)}, u32[]{:S(2)}, u32[]{:S(2)}) collective-permute-start(bf16[128,512]{1,0:T(8,128)(2,1)S(1)} %collective-permute-done.16.refs_4_), channel_id=1, source_target_pairs={{0,1},{1,0},{2,3},{3,2},{4,5},{5,4},{6,7},{7,6},{8,9},{9,8},{10,11... | collective-permute-start | bytes 393224 | tf_op jit(solution)/shard_map/ppermute | solution.py:46
  53.5 1.7 %collective-permute-start.20 = (f32[704,128]{1,0:T(8,128)S(1)}, f32[704,128]{1,0:T(8,128)S(1)}, u32[]{:S(2)}, u32[]{:S(2)}) collective-permute-start(f32[704,128]{1,0:T(8,128)S(1)} %get-tuple-element.40), channel_id=1, source_target_pairs={{0,1},{1,0},{2,3},{3,2},{4,5},{5,4},{6,7},{7,6},{8,9},{9,8},{10,11... | collective-permute-start | bytes 1081352 | tf_op jit(solution)/shard_map/ppermute | solution.py:46
  53.9 14.6 %collective-permute-start.6 = (f32[384,128]{1,0:T(8,128)S(1)}, f32[384,128]{1,0:T(8,128)S(1)}, u32[]{:S(2)}, u32[]{:S(2)}) collective-permute-start(f32[384,128]{1,0:T(8,128)S(1)} %get-tuple-element.31), channel_id=1, source_target_pairs={{0,1},{1,0},{2,3},{3,2},{4,5},{5,4},{6,7},{7,6},{8,9},{9,8},{10,11... | collective-permute-start | bytes 589832 | tf_op jit(solution)/shard_map/ppermute | solution.py:46
  57.8 13.2 %collective-permute-start.21 = (bf16[320,128]{1,0:T(8,128)(2,1)}, bf16[320,128]{1,0:T(8,128)(2,1)S(1)}, u32[]{:S(2)}, u32[]{:S(2)}) collective-permute-start(bf16[320,128]{1,0:T(8,128)(2,1)} %get-tuple-element.43), channel_id=1, source_target_pairs={{4,0},{0,4},{12,8},{8,12},{5,1},{1,5},{13,9},{9,13},{6,2},{2,6},{1... | collective-permute-start | bytes 245768 | tf_op jit(solution)/shard_map/ppermute | solution.py:594
  66.1 11.8 %collective-permute-start.22 = (bf16[320,128]{1,0:T(8,128)(2,1)}, bf16[320,128]{1,0:T(8,128)(2,1)S(1)}, u32[]{:S(2)}, u32[]{:S(2)}) collective-permute-start(bf16[320,128]{1,0:T(8,128)(2,1)} %get-tuple-element.44), channel_id=1, source_target_pairs={{8,0},{12,4},{0,8},{4,12},{9,1},{13,5},{1,9},{5,13},{10,2},{14,6},... | collective-permute-start | bytes 245768 | tf_op jit(solution)/shard_map/ppermute | solution.py:594
  67.1 10.8 %collective-permute-start.23 = (bf16[320,128]{1,0:T(8,128)(2,1)}, bf16[320,128]{1,0:T(8,128)(2,1)S(1)}, u32[]{:S(2)}, u32[]{:S(2)}) collective-permute-start(bf16[320,128]{1,0:T(8,128)(2,1)} %get-tuple-element.45), channel_id=1, source_target_pairs={{12,0},{8,4},{4,8},{0,12},{13,1},{9,5},{5,9},{1,13},{14,2},{10,6},... | collective-permute-start | bytes 245768 | tf_op jit(solution)/shard_map/ppermute | solution.py:594
  68.6 14.8 %collective-permute-start.9 = (bf16[384,128]{1,0:T(8,128)(2,1)S(1)}, bf16[384,128]{1,0:T(8,128)(2,1)S(1)}, u32[]{:S(2)}, u32[]{:S(2)}) collective-permute-start(bf16[384,128]{1,0:T(8,128)(2,1)S(1)} %add_convert_fusion.refs_0_), channel_id=1, source_target_pairs={{12,0},{8,4},{4,8},{0,12},{13,1},{9,5},{5,9},{1,13},{14,2},{10,6},... | collective-permute-start | bytes 294920 | tf_op jit(solution)/shard_map/ppermute | solution.py:594
  71.0 6.9 %copy-start.12 = (bf16[320,128]{1,0:T(8,128)(2,1)}, bf16[320,128]{1,0:T(8,128)(2,1)S(1)}, u32[]{:S(2)}) copy-start(bf16[320,128]{1,0:T(8,128)(2,1)S(1)} %collective-permute-done.21.refs_1_) | copy-start | bytes 245764
  80.2 14.7 %collective-permute-start.24 = (bf16[896,128]{1,0:T(8,128)(2,1)}, bf16[896,128]{1,0:T(8,128)(2,1)S(1)}, u32[]{:S(2)}, u32[]{:S(2)}) collective-permute-start(bf16[896,128]{1,0:T(8,128)(2,1)} %shard_map.125.refs_8_), channel_id=1, source_target_pairs={{0,1},{1,0},{2,3},{3,2},{4,5},{5,4},{6,7},{7,6},{8,9},{9,8},{10,11... | collective-permute-start | bytes 688136 | tf_op jit(solution)/shard_map/ppermute | solution.py:46
  80.2 8.4 %collective-permute-start.8 = (bf16[384,128]{1,0:T(8,128)(2,1)S(1)}, bf16[384,128]{1,0:T(8,128)(2,1)S(1)}, u32[]{:S(2)}, u32[]{:S(2)}) collective-permute-start(bf16[384,128]{1,0:T(8,128)(2,1)S(1)} %add_convert_fusion.refs_0_), channel_id=1, source_target_pairs={{8,0},{12,4},{0,8},{4,12},{9,1},{13,5},{1,9},{5,13},{10,2},{14,6},... | collective-permute-start | bytes 294920 | tf_op jit(solution)/shard_map/ppermute | solution.py:594
  83.1 5.6 %collective-permute-start.7 = (bf16[384,128]{1,0:T(8,128)(2,1)S(1)}, bf16[384,128]{1,0:T(8,128)(2,1)S(1)}, u32[]{:S(2)}, u32[]{:S(2)}) collective-permute-start(bf16[384,128]{1,0:T(8,128)(2,1)S(1)} %add_convert_fusion.refs_0_), channel_id=1, source_target_pairs={{4,0},{0,4},{12,8},{8,12},{5,1},{1,5},{13,9},{9,13},{6,2},{2,6},{1... | collective-permute-start | bytes 294920 | tf_op jit(solution)/shard_map/ppermute | solution.py:594
  83.1 6.8 %collective-permute-start.10 = (bf16[384,128]{1,0:T(8,128)(2,1)S(1)}, bf16[384,128]{1,0:T(8,128)(2,1)S(1)}, u32[]{:S(2)}, u32[]{:S(2)}) collective-permute-start(bf16[384,128]{1,0:T(8,128)(2,1)S(1)} %add_convert_fusion.refs_0_), channel_id=1, source_target_pairs={{0,1},{1,0},{2,3},{3,2},{4,5},{5,4},{6,7},{7,6},{8,9},{9,8},{10,11... | collective-permute-start | bytes 294920 | tf_op jit(solution)/shard_map/ppermute | solution.py:46
  83.4 7.7 %collective-permute-start.13 = (bf16[384,128]{1,0:T(8,128)(2,1)S(1)}, bf16[384,128]{1,0:T(8,128)(2,1)S(1)}, u32[]{:S(2)}, u32[]{:S(2)}) collective-permute-start(bf16[384,128]{1,0:T(8,128)(2,1)S(1)} %collective-permute-done.9.refs_3_), channel_id=1, source_target_pairs={{0,1},{1,0},{2,3},{3,2},{4,5},{5,4},{6,7},{7,6},{8,9},{9,8},{10,11... | collective-permute-start | bytes 294920 | tf_op jit(solution)/shard_map/ppermute | solution.py:46
  88.7 2.9 %collective-permute-start.12 = (bf16[384,128]{1,0:T(8,128)(2,1)S(1)}, bf16[384,128]{1,0:T(8,128)(2,1)S(1)}, u32[]{:S(2)}, u32[]{:S(2)}) collective-permute-start(bf16[384,128]{1,0:T(8,128)(2,1)S(1)} %collective-permute-done.8.refs_2_), channel_id=1, source_target_pairs={{0,1},{1,0},{2,3},{3,2},{4,5},{5,4},{6,7},{7,6},{8,9},{9,8},{10,11... | collective-permute-start | bytes 294920 | tf_op jit(solution)/shard_map/ppermute | solution.py:46
  88.7 2.9 %collective-permute-start.11 = (bf16[384,128]{1,0:T(8,128)(2,1)S(1)}, bf16[384,128]{1,0:T(8,128)(2,1)S(1)}, u32[]{:S(2)}, u32[]{:S(2)}) collective-permute-start(bf16[384,128]{1,0:T(8,128)(2,1)S(1)} %collective-permute-done.7.refs_1_), channel_id=1, source_target_pairs={{0,1},{1,0},{2,3},{3,2},{4,5},{5,4},{6,7},{7,6},{8,9},{9,8},{10,11... | collective-permute-start | bytes 294920 | tf_op jit(solution)/shard_map/ppermute | solution.py:46
  90.0 3.5 %collective-permute-start.26 = (bf16[128,128]{1,0:T(8,128)(2,1)S(1)}, bf16[128,128]{1,0:T(8,128)(2,1)S(1)}, u32[]{:S(2)}, u32[]{:S(2)}) collective-permute-start(bf16[128,128]{1,0:T(8,128)(2,1)S(1)} %slice.4), channel_id=1, source_target_pairs={{0,3},{1,2},{2,1},{3,0},{4,7},{5,6},{6,5},{7,4},{8,11},{9,10},{10,... | collective-permute-start | bytes 98312 | tf_op jit(solution)/shard_map/ppermute | solution.py:619
  91.1 3.9 %collective-permute-start.25 = (bf16[128,128]{1,0:T(8,128)(2,1)S(1)}, bf16[128,128]{1,0:T(8,128)(2,1)S(1)}, u32[]{:S(2)}, u32[]{:S(2)}) collective-permute-start(bf16[128,128]{1,0:T(8,128)(2,1)S(1)} %slice.4), channel_id=1, source_target_pairs={{0,2},{2,0},{1,3},{3,1},{4,6},{6,4},{5,7},{7,5},{8,10},{10,8},{9,1... | collective-permute-start | bytes 98312 | tf_op jit(solution)/shard_map/ppermute | solution.py:46
  (10 other events, 8.6 us)

commit v4 on v3

--- a/solution.py
+++ b/solution.py
@@ -13,6 +13,7 @@
 SCALE = DH ** (-0.5)
 F32 = jnp.float32
 BF16 = jnp.bfloat16
+SMALL = pltpu.CompilerParams(vmem_limit_bytes=16 * 1024 * 1024)
 
 
 def dot_nn(left, right):
@@ -262,34 +263,50 @@
     return [pl.BlockSpec(memory_space=pltpu.VMEM)] * count
 
 
-def pack_kernel(tables, frames, with_t, fq_ref, do_ref, fk_ref, fv_ref, t_ref, *outs):
+def pack_kernel(table, slots, frames, both, fq_ref, do_ref, fk_ref, fv_ref, t_ref, *refs):
+    outs, sems = refs[:-1], refs[-1]
     me, half = lax.axis_index("tm"), lax.axis_index("rep")
     rows = fq_ref.shape[0]
-    for m in range(frames + 1):
-        out = outs[m]
-        tile = half if m < frames else 1 - half
-        own = pl.ds(pl.multiple_of(tile * rows, rows), rows)
-        for s, table in enumerate(tables):
-            cols = column(lookup(table, me ^ m if m < frames else me))
-            at = 4 * s * DH
-            if m < frames:
-                out[:, at : at + DH] = fq_ref[:, cols]
-                out[:, at + DH : at + 2 * DH] = do_ref[:, cols]
-            out[:, at + 2 * DH : at + 3 * DH] = fk_ref[own, cols]
-            out[:, at + 3 * DH : at + 4 * DH] = fv_ref[own, cols]
-        if with_t:
-            out[:, 4 * len(tables) * DH :] = t_ref[own, :]
-
-
-def pack(tables, frames, with_t, fq, do, fk, fv, t):
+    wide = slots * DH
+    copies = []
+
+    def copy(source, target):
+        copies.append(pltpu.make_async_copy(source, target, sems.at[len(copies)]))
+        copies[-1].start()
+
+    def tile_rows_at(tile):
+        return pl.ds(pl.multiple_of(tile * rows, rows), rows)
+
+    for m in range(len(outs)):
+        mine = m < frames
+        own = tile_rows_at(half if mine else 1 - half)
+        head = lookup(table, me ^ m if mine else me)
+        cols = pl.ds(pl.multiple_of(head * DH, DH), wide)
+        sources = [(2, fk_ref.at[own, cols]), (3, fv_ref.at[own, cols])]
+        if mine:
+            sources += [(0, fq_ref.at[:, cols]), (1, do_ref.at[:, cols])]
+        if both:
+            rest = tile_rows_at(1 - half)
+            sources += [(4, fk_ref.at[rest, cols]), (5, fv_ref.at[rest, cols])]
+        for place_in, source in sources:
+            copy(source, outs[m].at[:, pl.ds(place_in * wide, wide)])
+        if not both:
+            copy(t_ref.at[own, :], outs[m].at[:, pl.ds(4 * wide, t_ref.shape[1])])
+    for started in copies:
+        started.wait()
+
+
+def pack(table, slots, frames, both, fq, do, fk, fv, t):
     rows = fq.shape[0]
-    width = 4 * DH * len(tables) + (t.shape[1] if with_t else 0)
+    width = 6 * DH * slots if both else 4 * DH * slots + t.shape[1]
+    count = frames if both else frames + 1
+    anywhere = pl.BlockSpec(memory_space=pl.ANY)
     return pl.pallas_call(
-        functools.partial(pack_kernel, tables, frames, with_t),
-        in_specs=vmem(5),
-        out_specs=vmem(frames + 1),
-        out_shape=[jax.ShapeDtypeStruct((rows, width), BF16)] * (frames + 1),
-        compiler_params=pltpu.CompilerParams(vmem_limit_bytes=32 * 1024 * 1024),
+        functools.partial(pack_kernel, table, slots, frames, both),
+        in_specs=[anywhere] * 5,
+        out_specs=[anywhere] * count,
+        out_shape=[jax.ShapeDtypeStruct((rows, width), BF16)] * count,
+        scratch_shapes=[pltpu.SemaphoreType.DMA((6 * count,))],
     )(fq, do, fk, fv, t)
 
 
@@ -364,44 +381,50 @@
     return grads, lows[:flat] + dot_nt(dq, aq), lows[flat:]
 
 
-def group_kernel(tables, frames, counts, t_col, chained, last, *refs):
+def group_kernel(tables, frames, counts, chained, *refs):
     refs = list(refs)
-    bands = refs.pop(0)
-    mine, others = [refs.pop(0) for _ in range(frames)], [refs.pop(0) for _ in range(frames)]
-    if t_col is None:
-        t_mine, t_others = [refs.pop(0) for _ in range(frames)], [refs.pop(0) for _ in range(frames)]
-    adapters = [refs.pop(0) for _ in range(3)]
-    before = [refs.pop(0) for _ in range(2)] if chained else None
-    keep_ref, give_ref = refs.pop(0), refs.pop(0)
-    low_refs = None if last else [refs.pop(0) for _ in range(2)]
-    same, other = refs.pop(0), refs.pop(0)
-    t_same, t_other = refs.pop(0), refs.pop(0)
+
+    def take(count):
+        taken = refs[:count]
+        del refs[:count]
+        return taken
+
+    (bands,) = take(1)
+    mine = take(frames)
+    others = mine if chained else take(frames)
+    if chained:
+        t_mine, t_others = take(frames), take(frames)
+    adapters = take(3)
+    before = take(2) if chained else [None, None]
+    keep_ref, give_ref = take(2)
+    low_refs = [] if chained else take(2)
+    same, other, t_same, t_other = refs
     me, half = lax.axis_index("tm"), lax.axis_index("rep")
     rows = mine[0].shape[0]
-    flat = frames * rows
-    rank = t_same.shape[1]
-    cut = 3 * rank // 2
+    cut = 3 * t_same.shape[1] // 2
     slots = len(tables)
     main = 4 * slots * DH
-    for m in range(frames):
-        at = pl.ds(pl.multiple_of((me ^ m) * rows, rows), rows)
-        same[at, :] = mine[m][:, :main]
-        other[at, :] = others[m][:, :main]
-        t_same[at, :] = t_mine[m][...] if t_col is None else mine[m][:, main:]
-        t_other[at, :] = t_others[m][...] if t_col is None else others[m][:, main:]
+    wide = slots * DH
 
     def body():
-        total_same = before[0][...] if chained else None
-        total_other = before[1][...] if chained else None
+        for m in range(frames):
+            at = pl.ds(pl.multiple_of((me ^ m) * rows, rows), rows)
+            same[at, :] = mine[m][:, :main]
+            start = main if chained else main // 2
+            other[at, :] = others[m][:, start : start + main // 2]
+            t_same[at, :] = t_mine[m][...] if chained else mine[m][:, main:]
+            t_other[at, :] = t_others[m][...] if chained else others[m][:, main:]
+        total_same, total_other = [None if ref is None else ref[...] for ref in before]
         for s, table in enumerate(tables):
             cols = column(lookup(table, me))
-            at = 4 * s * DH
-            kv = [
-                jnp.concatenate([ref[:, at + c * DH : at + (c + 1) * DH] for ref in (same, other)], axis=0)
-                for c in (2, 3)
-            ]
+
+            def part(c):
+                return slice(c * wide + s * DH, c * wide + (s + 1) * DH)
+
             grads, low_same, low_other = one_head(
-                frames, bands, same[:, at : at + DH], same[:, at + DH : at + 2 * DH], *kv,
+                frames, bands, same[:, part(0)], same[:, part(1)],
+                jnp.concatenate([same[:, part(2)], other[:, part(0)]], axis=0),
+                jnp.concatenate([same[:, part(3)], other[:, part(1)]], axis=0),
                 t_same[...], t_other[...], *[ref[:, cols] for ref in adapters],
             )
             first = half == 0
@@ -409,7 +432,7 @@
             give_ref[s * cut : (s + 1) * cut, :] = jnp.where(first, grads[cut:], grads[:cut])
             total_same = low_same if total_same is None else total_same + low_same
             total_other = low_other if total_other is None else total_other + low_other
-        if last:
+        if chained:
             keep_ref[slots * cut :, :] = total_same
             give_ref[slots * cut :, :] = total_other
         else:
@@ -431,47 +454,48 @@
             give_ref[slots * cut :, :] = before[1][...]
 
 
-def head_group(tables, counts, bands, mine, others, t_mine, t_others, adapters, before, last):
+def head_group(tables, counts, bands, mine, others, adapters, before=None):
     frames, rows = len(mine), mine[0].shape[0]
     rank = adapters[0].shape[0]
     slots = len(tables)
     flat = frames * rows
     size = slots * 3 * rank // 2
+    main = 4 * slots * DH
+    chained = before is not None
+    args = [bands, *mine, *others, *adapters]
+    specs = [pl.BlockSpec(memory_space=pltpu.SMEM)] + vmem(frames)
+    if chained:
+        col = others[0].shape[1] // rank - 1
+        specs += [pl.BlockSpec((rows, rank), lambda n: (0, col))] * len(others) + vmem(3 + len(before))
+        args += before
+    else:
+        specs += vmem(len(others) + 3)
     low = jax.ShapeDtypeStruct((flat, rank), F32)
-    main = 4 * slots * DH
-    inline = t_mine is None
-    args = [bands, *mine, *others]
-    specs = [pl.BlockSpec(memory_space=pltpu.SMEM)] + vmem(2 * frames)
-    if not inline:
-        col = t_mine[0].shape[1] // rank - 1
-        args += [*t_mine, *t_others]
-        specs += [pl.BlockSpec((rows, rank), lambda n: (0, col))] * (2 * frames)
-    args += adapters
-    specs += vmem(3)
-    if before is not None:
-        args += before
-        specs += vmem(2)
-    edge = jax.ShapeDtypeStruct((size + (flat if last else 0), rank), F32)
-    shapes = [edge, edge] + ([] if last else [low, low])
+    edge = jax.ShapeDtypeStruct((size + (flat if chained else 0), rank), F32)
+    shapes = [edge, edge] + ([] if chained else [low, low])
     return pl.pallas_call(
-        functools.partial(
-            group_kernel, tables, frames, counts, main if inline else None, before is not None, last
-        ),
+        functools.partial(group_kernel, tables, frames, counts, chained),
         grid=(1,),
         in_specs=specs,
         out_specs=vmem(len(shapes)),
         out_shape=shapes,
         scratch_shapes=[
             pltpu.VMEM((flat, main), BF16),
-            pltpu.VMEM((flat, main), BF16),
+            pltpu.VMEM((flat, main // 2), BF16),
             pltpu.VMEM((flat, rank), BF16),
             pltpu.VMEM((flat, rank), BF16),
         ],
-        compiler_params=pltpu.CompilerParams(vmem_limit_bytes=48 * 1024 * 1024),
+        compiler_params=pltpu.CompilerParams(vmem_limit_bytes=40 * 1024 * 1024),
+        cost_estimate=pl.CostEstimate(
+            flops=4 * slots * 16 * 2 * DH * flat * 2 * flat,
+            transcendentals=slots * flat * 2 * flat,
+            bytes_accessed=8 * slots * flat * DH * 2,
+        ),
     )(*args)
 
 
-def hand_out_kernel(frames, size, keep_ref, got_ref, own_ref, *sends):
+def hand_out_kernel(frames, size, waits, keep_ref, got_ref, *refs):
+    own_ref, *sends = refs[waits:]
     me = lax.axis_index("tm")
     rows = own_ref.shape[0]
     grads = (keep_ref[:size, :] + got_ref[:size, :]).astype(BF16)
@@ -484,15 +508,16 @@
         sends[m][rows:, :] = grads
 
 
-def hand_out(frames, rows, keep, got):
+def hand_out(frames, rows, keep, got, after):
     size, rank = keep.shape[0] - frames * rows, keep.shape[1]
     send = jax.ShapeDtypeStruct((rows + size, rank), BF16)
     return pl.pallas_call(
-        functools.partial(hand_out_kernel, frames, size),
-        in_specs=vmem(2),
+        functools.partial(hand_out_kernel, frames, size, len(after)),
+        in_specs=vmem(2) + [pl.BlockSpec(memory_space=pl.ANY)] * len(after),
         out_specs=vmem(frames + 1),
         out_shape=[jax.ShapeDtypeStruct((rows, rank), F32)] + [send] * frames,
-    )(keep, got)
+        compiler_params=SMALL,
+    )(keep, got, *after)
 
 
 def collect_kernel(frames, own_ref, *refs):
@@ -515,6 +540,7 @@
         in_specs=vmem(frames + 1),
         out_specs=pl.BlockSpec(memory_space=pltpu.VMEM),
         out_shape=jax.ShapeDtypeStruct((rows + frames * size, rank), BF16),
+        compiler_params=SMALL,
     )(own, *gots)
 
 
@@ -563,7 +589,7 @@
         out_specs=vmem(4),
         out_shape=[jax.ShapeDtypeStruct((rank, width), F32)] * 3
         + [jax.ShapeDtypeStruct((2 * rows, rank), F32)],
-        compiler_params=pltpu.CompilerParams(vmem_limit_bytes=32 * 1024 * 1024),
+        compiler_params=SMALL,
     )(*mine, *others, tail, tail2, low_head, low_diag)
 
 
@@ -593,23 +619,20 @@
     def meet(block, m, targets=range(frames)):
         return lax.ppermute(block, "tm", [(j ^ m, j) for j in targets])
 
-    packed = pack(columns[:full], frames, True, *arrays)
+    packed = pack(columns[0], full, frames, False, *arrays)
     mine = [packed[0]] + [meet(packed[m], m) for m in range(1, frames)]
-    packed2 = pack(columns[full:], frames, False, *arrays)
+    packed2 = pack(columns[full], most - full, frames, True, *arrays)
     mine2 = [packed2[0]] + [meet(packed2[m], m, wide) for m in range(1, frames)]
     others = [packed[frames]] + [swap(block, "rep") for block in mine[1:]]
-    others2 = [packed2[frames]] + [swap(block, "rep") for block in mine2[1:]]
-    keep, give, *low = head_group(
-        columns[:full], counts, band_width, mine, others, None, None, adapters, None, False
-    )
+    keep, give, *low = head_group(columns[:full], counts, band_width, mine, others, adapters)
     piece = (keep + swap(give, "rep")).astype(BF16)
     pieces = [piece] + [meet(piece, m) for m in range(1, frames)]
     pieces2 = [swap(block, "rep") for block in pieces]
     keep, give = head_group(
-        columns[full:], [c - full for c in counts], band_width, mine2, others2, mine, others,
-        adapters, low, True,
-    )
-    own, *sends = hand_out(frames, rows, keep, swap(give, "rep"))
+        columns[full:], [c - full for c in counts], band_width, mine2, mine + others, adapters,
+        low,
+    )
+    own, *sends = hand_out(frames, rows, keep, swap(give, "rep"), pieces[1:])
     gots = [sends[0]] + [meet(sends[m], m) for m in range(1, frames)]
     tail = collect(own, gots)
     low = tail[:rows]

time: 98 us -> 148 us (1.51)
  Pallas kernels: 13.3 us -> 76.5 us
  local copies, waits for them, and re-layouts: 8.77 us -> 0.03 us
  starting transfers between devices: 35.9 us -> 32.3 us
    pallas_call x5, Pallas kernels: 10.1 us -> 75 us  [the longest x2 67.2 us: pack(): pl.pallas_call(functools.partial(pack_kernel, table, slots, frames, both)...]
    unnamed x30 -> x14, local copies, waits for them, and re-layouts: 8.01 us -> 0.03 us
    ppermute x12, starting transfers between devices: 31.7 us -> 28.2 us  [meet(): return lax.ppermute(block, 'tm', [(j ^ m, j) for j in targets])]
    pallas_call x1, Pallas kernels: 1.75 us -> 0.02 us  [collect(): pl.pallas_call(functools.partial(collect_kernel, frames), in_specs=vmem(f...]
    ppermute x14 -> x11, starting transfers between devices: 3.16 us -> 2.85 us  [swap(): return lax.ppermute(block, axis, [(0, 1), (1, 0)])]
  transfers between devices with their start and end apart: 27 -> 24, of which waited for: 8 -> 9; matrix products, arithmetic and copies ran while one was open for 1% -> 0% of each run, Pallas kernels for 11% -> 22%
where the time goes in v4:
time: 148 us
  Pallas kernels  76.5 us (52%)
  waiting for transfers between devices  37.7 us (25%)
  starting transfers between devices  32.3 us (22%)
    pallas_call x2, Pallas kernels, pack(): pl.pallas_call(functools.partial(pack_kernel, table, slots, frames, both)...  67.2 us
    ppermute x12, waiting for transfers between devices, meet(): return lax.ppermute(block, 'tm', [(j ^ m, j) for j in targets])  33.6 us
    ppermute x12, starting transfers between devices, meet(): return lax.ppermute(block, 'tm', [(j ^ m, j) for j in targets])  28.2 us
    pallas_call x2, Pallas kernels, head_group(): pl.pallas_call(functools.partial(group_kernel, tables, frames, counts, ch...  7.76 us
  transfers between devices with their start and end apart: 24, of which 9 were waited for; matrix products, arithmetic and copies ran while one was open for 0% of the time, Pallas kernels for 22%

profile of v4, /device:TPU:0, one launch (start us, length us, event | category | flops | bytes accessed | tf_op | source)
XLA Modules:
  0.0 147.5 jit_solution(9556570883426592636)
XLA Ops:
  0.6 42.1 %shard_map.120 = (bf16[128,1152]{1,0:T(8,128)(2,1)}, bf16[128,1152]{1,0:T(8,128)(2,1)}, bf16[128,1152]{1,0:T(8,128)(2,1)}, bf16[128,1152]{1,0:T(8,128)(2,1)}, bf16[128,1152]{1,0:T(8,128)(2,1)}) custom-call(bf16[128,1280]{1,0:T(8,128)(2,1)} %fq_ref.3, bf16[128,1280]{1,0:T(8,128)(2,1)} %do_ref.3, bf16[256,1280]{1,0:T(8,128)(2,1)} %fk_ref.3, ...), custom_call_target="tpu_custom_call" | custom-call | tf_op jit(solution)/shard_map/pallas_call | solution.py:304
  42.7 3.1 %collective-permute-start = (bf16[128,1152]{1,0:T(8,128)(2,1)}, bf16[128,1152]{1,0:T(8,128)(2,1)S(1)}, u32[]{:S(2)}, u32[]{:S(2)}) collective-permute-start(bf16[128,1152]{1,0:T(8,128)(2,1)} %get-tuple-element.25), channel_id=1, source_target_pairs={{4,0},{0,4},{12,8},{8,12},{5,1},{1,5},{13,9},{9,13},{6,2},{2,6},{1... | collective-permute-start | bytes 884744 | tf_op jit(solution)/shard_map/ppermute | solution.py:620
  45.8 2.6 %collective-permute-start.1 = (bf16[128,1152]{1,0:T(8,128)(2,1)}, bf16[128,1152]{1,0:T(8,128)(2,1)S(1)}, u32[]{:S(2)}, u32[]{:S(2)}) collective-permute-start(bf16[128,1152]{1,0:T(8,128)(2,1)} %get-tuple-element.26), channel_id=1, source_target_pairs={{8,0},{12,4},{0,8},{4,12},{9,1},{13,5},{1,9},{5,13},{10,2},{14,6},... | collective-permute-start | bytes 884744 | tf_op jit(solution)/shard_map/ppermute | solution.py:620
  48.5 10.1 %collective-permute-done.refs_2_.refs_6_ = bf16[128,1152]{1,0:T(8,128)(2,1)S(1)} collective-permute-done((bf16[128,1152]{1,0:T(8,128)(2,1)}, bf16[128,1152]{1,0:T(8,128)(2,1)S(1)}, u32[]{:S(2)}, u32[]{:S(2)}) %collective-permute-start) | collective-permute-done | bytes 294944 | tf_op jit(solution)/shard_map/ppermute | solution.py:620
  58.6 10.9 %collective-permute-done.1.refs_3_.refs_7_ = bf16[128,1152]{1,0:T(8,128)(2,1)S(1)} collective-permute-done((bf16[128,1152]{1,0:T(8,128)(2,1)}, bf16[128,1152]{1,0:T(8,128)(2,1)S(1)}, u32[]{:S(2)}, u32[]{:S(2)}) %collective-permute-start.1) | collective-permute-done | bytes 294944 | tf_op jit(solution)/shard_map/ppermute | solution.py:620
  69.5 0.5 collective-permute-start.5
  70.0 25.1 %shard_map.122 = (bf16[128,768]{1,0:T(8,128)(2,1)}, bf16[128,768]{1,0:T(8,128)(2,1)}, bf16[128,768]{1,0:T(8,128)(2,1)}, bf16[128,768]{1,0:T(8,128)(2,1)}) custom-call(bf16[128,1280]{1,0:T(8,128)(2,1)} %fq_ref.3, bf16[128,1280]{1,0:T(8,128)(2,1)} %do_ref.3, bf16[256,1280]{1,0:T(8,128)(2,1)} %fk_ref.3, bf16[256,1280]{1,0:T(8,128)(2,1)} %fv_ref.3, ...), custom_call_target="tpu_custom_call" | custom-call | tf_op jit(solution)/shard_map/pallas_call | solution.py:304
  95.2 6.9 %collective-permute-start.14 = (bf16[128,768]{1,0:T(8,128)(2,1)}, bf16[128,768]{1,0:T(8,128)(2,1)S(1)}, u32[]{:S(2)}, u32[]{:S(2)}) collective-permute-start(bf16[128,768]{1,0:T(8,128)(2,1)} %get-tuple-element.32), channel_id=1, source_target_pairs={{0,4},{12,8},{1,5},{13,9},{2,6},{14,10},{3,7},{15,11},{16,20},{28,... | collective-permute-start | bytes 589832 | tf_op jit(solution)/shard_map/ppermute | solution.py:620
  102.0 2.3 %collective-permute-start.15 = (bf16[128,768]{1,0:T(8,128)(2,1)}, bf16[128,768]{1,0:T(8,128)(2,1)S(1)}, u32[]{:S(2)}, u32[]{:S(2)}) collective-permute-start(bf16[128,768]{1,0:T(8,128)(2,1)} %get-tuple-element.33), channel_id=1, source_target_pairs={{12,4},{0,8},{13,5},{1,9},{14,6},{2,10},{15,7},{3,11},{28,20},{16,... | collective-permute-start | bytes 589832 | tf_op jit(solution)/shard_map/ppermute | solution.py:620
  104.4 0.7 collective-permute-start.16
  105.1 7.1 %shard_map.121 = (f32[384,128]{1,0:T(8,128)S(1)}, f32[384,128]{1,0:T(8,128)S(1)}, f32[512,128]{1,0:T(8,128)S(1)}, f32[512,128]{1,0:T(8,128)S(1)}) custom-call(s32[4,4]{1,0:T(4,128)S(1)} %copy-done.6, bf16[128,1152]{1,0:T(8,128)(2,1)S(1)} %copy-done.3, bf16[128,1152]{1,0:T(8,128)(2,1)S(1)} %collective-permute-done.refs_2_.refs_6_, ...), custom_call_target="tpu_custom_call" | custom-call | flops 17179869184 | bytes 2097152 | tf_op jit(solution)/shard_map/pallas_call | solution.py:476
  112.3 0.3 collective-permute-start.6
  112.6 0.6 shard_map.123
  113.2 0.4 collective-permute-start.17
  113.6 0.2 collective-permute-done.6
  113.8 1.5 %collective-permute-start.9 = (bf16[384,128]{1,0:T(8,128)(2,1)S(1)}, bf16[384,128]{1,0:T(8,128)(2,1)S(1)}, u32[]{:S(2)}, u32[]{:S(2)}) collective-permute-start(bf16[384,128]{1,0:T(8,128)(2,1)S(1)} %add_convert_fusion.refs_0_), channel_id=1, source_target_pairs={{12,0},{8,4},{4,8},{0,12},{13,1},{9,5},{5,9},{1,13},{14,2},{10,6},... | collective-permute-start | bytes 294920 | tf_op jit(solution)/shard_map/ppermute | solution.py:620
  115.3 6.5 %collective-permute-start.8 = (bf16[384,128]{1,0:T(8,128)(2,1)S(1)}, bf16[384,128]{1,0:T(8,128)(2,1)S(1)}, u32[]{:S(2)}, u32[]{:S(2)}) collective-permute-start(bf16[384,128]{1,0:T(8,128)(2,1)S(1)} %add_convert_fusion.refs_0_), channel_id=1, source_target_pairs={{8,0},{12,4},{0,8},{4,12},{9,1},{13,5},{1,9},{5,13},{10,2},{14,6},... | collective-permute-start | bytes 294920 | tf_op jit(solution)/shard_map/ppermute | solution.py:620
  121.9 0.1 collective-permute-start.7
  122.0 7.3 %collective-permute-done.8.refs_1_.refs_2_ = bf16[384,128]{1,0:T(8,128)(2,1)S(1)} collective-permute-done((bf16[384,128]{1,0:T(8,128)(2,1)S(1)}, bf16[384,128]{1,0:T(8,128)(2,1)S(1)}, u32[]{:S(2)}, u32[]{:S(2)}) %collective-permute-start.8) | collective-permute-done | bytes 98336 | tf_op jit(solution)/shard_map/ppermute | solution.py:620
  129.4 3.0 %collective-permute-start.19 = (bf16[320,128]{1,0:T(8,128)(2,1)S(1)}, bf16[320,128]{1,0:T(8,128)(2,1)S(1)}, u32[]{:S(2)}, u32[]{:S(2)}) collective-permute-start(bf16[320,128]{1,0:T(8,128)(2,1)S(1)} %get-tuple-element.42), channel_id=1, source_target_pairs={{8,0},{12,4},{0,8},{4,12},{9,1},{13,5},{1,9},{5,13},{10,2},{14,6},... | collective-permute-start | bytes 245768 | tf_op jit(solution)/shard_map/ppermute | solution.py:620
  132.4 1.4 collective-permute-start.20
  133.8 0.8 collective-permute-done.18.refs_1_
  134.6 4.5 %collective-permute-done.19.refs_2_ = bf16[320,128]{1,0:T(8,128)(2,1)S(1)} collective-permute-done((bf16[320,128]{1,0:T(8,128)(2,1)S(1)}, bf16[320,128]{1,0:T(8,128)(2,1)S(1)}, u32[]{:S(2)}, u32[]{:S(2)}) %collective-permute-start.19) | collective-permute-done | bytes 81952 | tf_op jit(solution)/shard_map/ppermute | solution.py:620
  139.2 0.5 collective-permute-start.10
  139.8 0.4 collective-permute-start.12
  140.2 0.1 collective-permute-start.11
  140.3 0.5 collective-permute-done.10.refs_4_
  140.8 1.3 collective-permute-start.23
  142.1 0.5 collective-permute-start.22
  142.6 1.5 %collective-permute-done.23.refs_11_ = bf16[128,128]{1,0:T(8,128)(2,1)S(1)} collective-permute-done((bf16[128,128]{1,0:T(8,128)(2,1)S(1)}, bf16[128,128]{1,0:T(8,128)(2,1)S(1)}, u32[]{:S(2)}, u32[]{:S(2)}) %collective-permute-start.23) | collective-permute-done | bytes 32800 | tf_op jit(solution)/shard_map/ppermute | solution.py:642
  144.1 1.9 %collective-permute-done.22.refs_10_ = bf16[128,128]{1,0:T(8,128)(2,1)S(1)} collective-permute-done((bf16[128,128]{1,0:T(8,128)(2,1)S(1)}, bf16[128,128]{1,0:T(8,128)(2,1)S(1)}, u32[]{:S(2)}, u32[]{:S(2)}) %collective-permute-start.22) | collective-permute-done | bytes 32800 | tf_op jit(solution)/shard_map/ppermute | solution.py:47
  146.0 1.5 %shard_map.126 = (f32[128,1280]{1,0:T(8,128)}, f32[128,1280]{1,0:T(8,128)}, f32[128,1280]{1,0:T(8,128)}, f32[256,128]{1,0:T(8,128)}) custom-call(bf16[384,128]{1,0:T(8,128)(2,1)S(1)} %add_convert_fusion.refs_0_, bf16[384,128]{1,0:T(8,128)(2,1)S(1)} %collective-permute-done.7.refs_0_.refs_1_, bf16[384,128]{1,0:T(8,128)(2,1)S(1)} %collective-permute-done.8.refs_1_.refs_2_, ...), custom_call_target="tpu_custom_call" | custom-call | tf_op jit(solution)/shard_map/pallas_call | solution.py:586
  (39 shorter events, 0.5 us)
Async XLA Ops:
  42.7 15.9 %collective-permute-start = (bf16[128,1152]{1,0:T(8,128)(2,1)}, bf16[128,1152]{1,0:T(8,128)(2,1)S(1)}, u32[]{:S(2)}, u32[]{:S(2)}) collective-permute-start(bf16[128,1152]{1,0:T(8,128)(2,1)} %get-tuple-element.25), channel_id=1, source_target_pairs={{4,0},{0,4},{12,8},{8,12},{5,1},{1,5},{13,9},{9,13},{6,2},{2,6},{1... | collective-permute-start | bytes 884744 | tf_op jit(solution)/shard_map/ppermute | solution.py:620
  45.8 23.7 %collective-permute-start.1 = (bf16[128,1152]{1,0:T(8,128)(2,1)}, bf16[128,1152]{1,0:T(8,128)(2,1)S(1)}, u32[]{:S(2)}, u32[]{:S(2)}) collective-permute-start(bf16[128,1152]{1,0:T(8,128)(2,1)} %get-tuple-element.26), channel_id=1, source_target_pairs={{8,0},{12,4},{0,8},{4,12},{9,1},{13,5},{1,9},{5,13},{10,2},{14,6},... | collective-permute-start | bytes 884744 | tf_op jit(solution)/shard_map/ppermute | solution.py:620
  48.4 56.7 %copy-start = (bf16[128,1280]{1,0:T(8,128)(2,1)S(1)}, bf16[128,1280]{1,0:T(8,128)(2,1)}, u32[]{:S(2)}) copy-start(bf16[128,1280]{1,0:T(8,128)(2,1)} %refs_13_.1) | copy-start | bytes 983044
  48.4 56.7 %copy-start.1 = (bf16[128,1280]{1,0:T(8,128)(2,1)S(1)}, bf16[128,1280]{1,0:T(8,128)(2,1)}, u32[]{:S(2)}) copy-start(bf16[128,1280]{1,0:T(8,128)(2,1)} %refs_14_.1) | copy-start | bytes 983044
  48.4 56.7 %copy-start.2 = (bf16[128,1280]{1,0:T(8,128)(2,1)S(1)}, bf16[128,1280]{1,0:T(8,128)(2,1)}, u32[]{:S(2)}) copy-start(bf16[128,1280]{1,0:T(8,128)(2,1)} %refs_15_.1) | copy-start | bytes 983044
  48.4 56.7 %copy-start.3 = (bf16[128,1152]{1,0:T(8,128)(2,1)S(1)}, bf16[128,1152]{1,0:T(8,128)(2,1)}, u32[]{:S(2)}) copy-start(bf16[128,1152]{1,0:T(8,128)(2,1)} %get-tuple-element.24.refs_1_.refs_5_) | copy-start | bytes 884740
  48.4 56.7 %copy-start.4 = (bf16[128,1152]{1,0:T(8,128)(2,1)S(1)}, bf16[128,1152]{1,0:T(8,128)(2,1)}, u32[]{:S(2)}) copy-start(bf16[128,1152]{1,0:T(8,128)(2,1)} %get-tuple-element.28.refs_5_.refs_9_) | copy-start | bytes 884740
  48.4 21.1 %collective-permute-start.2 = (bf16[128,1152]{1,0:T(8,128)(2,1)}, bf16[128,1152]{1,0:T(8,128)(2,1)S(1)}, u32[]{:S(2)}, u32[]{:S(2)}) collective-permute-start(bf16[128,1152]{1,0:T(8,128)(2,1)} %get-tuple-element.27), channel_id=1, source_target_pairs={{12,0},{8,4},{4,8},{0,12},{13,1},{9,5},{5,9},{1,13},{14,2},{10,6},... | collective-permute-start | bytes 884744 | tf_op jit(solution)/shard_map/ppermute | solution.py:620
  58.6 45.8 %collective-permute-start.3 = (bf16[128,1152]{1,0:T(8,128)(2,1)S(1)}, bf16[128,1152]{1,0:T(8,128)(2,1)S(1)}, u32[]{:S(2)}, u32[]{:S(2)}) collective-permute-start(bf16[128,1152]{1,0:T(8,128)(2,1)S(1)} %collective-permute-done.refs_2_.refs_6_), channel_id=1, source_target_pairs={{0,1},{1,0},{2,3},{3,2},{4,5},{5,4},{6,7},{7,6},{8,9},{9,8},{10,11... | collective-permute-start | bytes 884744 | tf_op jit(solution)/shard_map/ppermute | solution.py:47
  69.5 35.5 %collective-permute-start.4 = (bf16[128,1152]{1,0:T(8,128)(2,1)S(1)}, bf16[128,1152]{1,0:T(8,128)(2,1)S(1)}, u32[]{:S(2)}, u32[]{:S(2)}) collective-permute-start(bf16[128,1152]{1,0:T(8,128)(2,1)S(1)} %collective-permute-done.1.refs_3_.refs_7_), channel_id=1, source_target_pairs={{0,1},{1,0},{2,3},{3,2},{4,5},{5,4},{6,7},{7,6},{8,9},{9,8},{10,11... | collective-permute-start | bytes 884744 | tf_op jit(solution)/shard_map/ppermute | solution.py:47
  69.5 35.6 %collective-permute-start.5 = (bf16[128,1152]{1,0:T(8,128)(2,1)S(1)}, bf16[128,1152]{1,0:T(8,128)(2,1)S(1)}, u32[]{:S(2)}, u32[]{:S(2)}) collective-permute-start(bf16[128,1152]{1,0:T(8,128)(2,1)S(1)} %collective-permute-done.2.refs_4_.refs_8_), channel_id=1, source_target_pairs={{0,1},{1,0},{2,3},{3,2},{4,5},{5,4},{6,7},{7,6},{8,9},{9,8},{10,11... | collective-permute-start | bytes 884744 | tf_op jit(solution)/shard_map/ppermute | solution.py:47
  95.2 17.4 %collective-permute-start.14 = (bf16[128,768]{1,0:T(8,128)(2,1)}, bf16[128,768]{1,0:T(8,128)(2,1)S(1)}, u32[]{:S(2)}, u32[]{:S(2)}) collective-permute-start(bf16[128,768]{1,0:T(8,128)(2,1)} %get-tuple-element.32), channel_id=1, source_target_pairs={{0,4},{12,8},{1,5},{13,9},{2,6},{14,10},{3,7},{15,11},{16,20},{28,... | collective-permute-start | bytes 589832 | tf_op jit(solution)/shard_map/ppermute | solution.py:620
  102.0 10.5 %collective-permute-start.15 = (bf16[128,768]{1,0:T(8,128)(2,1)}, bf16[128,768]{1,0:T(8,128)(2,1)S(1)}, u32[]{:S(2)}, u32[]{:S(2)}) collective-permute-start(bf16[128,768]{1,0:T(8,128)(2,1)} %get-tuple-element.33), channel_id=1, source_target_pairs={{12,4},{0,8},{13,5},{1,9},{14,6},{2,10},{15,7},{3,11},{28,20},{16,... | collective-permute-start | bytes 589832 | tf_op jit(solution)/shard_map/ppermute | solution.py:620
  104.4 0.8 copy-start.6
  104.4 8.2 %collective-permute-start.16 = (bf16[128,768]{1,0:T(8,128)(2,1)}, bf16[128,768]{1,0:T(8,128)(2,1)S(1)}, u32[]{:S(2)}, u32[]{:S(2)}) collective-permute-start(bf16[128,768]{1,0:T(8,128)(2,1)} %get-tuple-element.34), channel_id=1, source_target_pairs={{8,4},{4,8},{9,5},{5,9},{10,6},{6,10},{11,7},{7,11},{24,20},{20,24... | collective-permute-start | bytes 589832 | tf_op jit(solution)/shard_map/ppermute | solution.py:620
  105.1 7.4 %copy-start.5 = (bf16[128,768]{1,0:T(8,128)(2,1)S(1)}, bf16[128,768]{1,0:T(8,128)(2,1)}, u32[]{:S(2)}) copy-start(bf16[128,768]{1,0:T(8,128)(2,1)} %get-tuple-element.31.refs_1_) | copy-start | bytes 589828
  112.3 1.5 %collective-permute-start.6 = (f32[384,128]{1,0:T(8,128)S(1)}, f32[384,128]{1,0:T(8,128)S(1)}, u32[]{:S(2)}, u32[]{:S(2)}) collective-permute-start(f32[384,128]{1,0:T(8,128)S(1)} %get-tuple-element.30), channel_id=1, source_target_pairs={{0,1},{1,0},{2,3},{3,2},{4,5},{5,4},{6,7},{7,6},{8,9},{9,8},{10,11... | collective-permute-start | bytes 589832 | tf_op jit(solution)/shard_map/ppermute | solution.py:47
  113.2 16.0 %collective-permute-start.17 = (f32[704,128]{1,0:T(8,128)S(1)}, f32[704,128]{1,0:T(8,128)S(1)}, u32[]{:S(2)}, u32[]{:S(2)}) collective-permute-start(f32[704,128]{1,0:T(8,128)S(1)} %get-tuple-element.38), channel_id=1, source_target_pairs={{0,1},{1,0},{2,3},{3,2},{4,5},{5,4},{6,7},{7,6},{8,9},{9,8},{10,11... | collective-permute-start | bytes 1081352 | tf_op jit(solution)/shard_map/ppermute | solution.py:47
  113.8 8.2 %collective-permute-start.9 = (bf16[384,128]{1,0:T(8,128)(2,1)S(1)}, bf16[384,128]{1,0:T(8,128)(2,1)S(1)}, u32[]{:S(2)}, u32[]{:S(2)}) collective-permute-start(bf16[384,128]{1,0:T(8,128)(2,1)S(1)} %add_convert_fusion.refs_0_), channel_id=1, source_target_pairs={{12,0},{8,4},{4,8},{0,12},{13,1},{9,5},{5,9},{1,13},{14,2},{10,6},... | collective-permute-start | bytes 294920 | tf_op jit(solution)/shard_map/ppermute | solution.py:620
  115.3 13.9 %collective-permute-start.8 = (bf16[384,128]{1,0:T(8,128)(2,1)S(1)}, bf16[384,128]{1,0:T(8,128)(2,1)S(1)}, u32[]{:S(2)}, u32[]{:S(2)}) collective-permute-start(bf16[384,128]{1,0:T(8,128)(2,1)S(1)} %add_convert_fusion.refs_0_), channel_id=1, source_target_pairs={{8,0},{12,4},{0,8},{4,12},{9,1},{13,5},{1,9},{5,13},{10,2},{14,6},... | collective-permute-start | bytes 294920 | tf_op jit(solution)/shard_map/ppermute | solution.py:620
  121.9 7.4 %collective-permute-start.7 = (bf16[384,128]{1,0:T(8,128)(2,1)S(1)}, bf16[384,128]{1,0:T(8,128)(2,1)S(1)}, u32[]{:S(2)}, u32[]{:S(2)}) collective-permute-start(bf16[384,128]{1,0:T(8,128)(2,1)S(1)} %add_convert_fusion.refs_0_), channel_id=1, source_target_pairs={{4,0},{0,4},{12,8},{8,12},{5,1},{1,5},{13,9},{9,13},{6,2},{2,6},{1... | collective-permute-start | bytes 294920 | tf_op jit(solution)/shard_map/ppermute | solution.py:620
  129.3 5.3 %collective-permute-start.18 = (bf16[320,128]{1,0:T(8,128)(2,1)S(1)}, bf16[320,128]{1,0:T(8,128)(2,1)S(1)}, u32[]{:S(2)}, u32[]{:S(2)}) collective-permute-start(bf16[320,128]{1,0:T(8,128)(2,1)S(1)} %get-tuple-element.41), channel_id=1, source_target_pairs={{4,0},{0,4},{12,8},{8,12},{5,1},{1,5},{13,9},{9,13},{6,2},{2,6},{1... | collective-permute-start | bytes 245768 | tf_op jit(solution)/shard_map/ppermute | solution.py:620
  129.4 9.7 %collective-permute-start.19 = (bf16[320,128]{1,0:T(8,128)(2,1)S(1)}, bf16[320,128]{1,0:T(8,128)(2,1)S(1)}, u32[]{:S(2)}, u32[]{:S(2)}) collective-permute-start(bf16[320,128]{1,0:T(8,128)(2,1)S(1)} %get-tuple-element.42), channel_id=1, source_target_pairs={{8,0},{12,4},{0,8},{4,12},{9,1},{13,5},{1,9},{5,13},{10,2},{14,6},... | collective-permute-start | bytes 245768 | tf_op jit(solution)/shard_map/ppermute | solution.py:620
  132.4 6.7 %collective-permute-start.20 = (bf16[320,128]{1,0:T(8,128)(2,1)S(1)}, bf16[320,128]{1,0:T(8,128)(2,1)S(1)}, u32[]{:S(2)}, u32[]{:S(2)}) collective-permute-start(bf16[320,128]{1,0:T(8,128)(2,1)S(1)} %get-tuple-element.43), channel_id=1, source_target_pairs={{12,0},{8,4},{4,8},{0,12},{13,1},{9,5},{5,9},{1,13},{14,2},{10,6},... | collective-permute-start | bytes 245768 | tf_op jit(solution)/shard_map/ppermute | solution.py:620
  139.1 6.9 %collective-permute-start.21 = (bf16[896,128]{1,0:T(8,128)(2,1)S(1)}, bf16[896,128]{1,0:T(8,128)(2,1)S(1)}, u32[]{:S(2)}, u32[]{:S(2)}) collective-permute-start(bf16[896,128]{1,0:T(8,128)(2,1)S(1)} %shard_map.125.refs_8_), channel_id=1, source_target_pairs={{0,1},{1,0},{2,3},{3,2},{4,5},{5,4},{6,7},{7,6},{8,9},{9,8},{10,11... | collective-permute-start | bytes 688136 | tf_op jit(solution)/shard_map/ppermute | solution.py:47
  139.2 1.6 %collective-permute-start.10 = (bf16[384,128]{1,0:T(8,128)(2,1)S(1)}, bf16[384,128]{1,0:T(8,128)(2,1)S(1)}, u32[]{:S(2)}, u32[]{:S(2)}) collective-permute-start(bf16[384,128]{1,0:T(8,128)(2,1)S(1)} %add_convert_fusion.refs_0_), channel_id=1, source_target_pairs={{0,1},{1,0},{2,3},{3,2},{4,5},{5,4},{6,7},{7,6},{8,9},{9,8},{10,11... | collective-permute-start | bytes 294920 | tf_op jit(solution)/shard_map/ppermute | solution.py:47
  139.7 2.4 %collective-permute-start.13 = (bf16[384,128]{1,0:T(8,128)(2,1)S(1)}, bf16[384,128]{1,0:T(8,128)(2,1)S(1)}, u32[]{:S(2)}, u32[]{:S(2)}) collective-permute-start(bf16[384,128]{1,0:T(8,128)(2,1)S(1)} %collective-permute-done.9.refs_2_.refs_3_), channel_id=1, source_target_pairs={{0,1},{1,0},{2,3},{3,2},{4,5},{5,4},{6,7},{7,6},{8,9},{9,8},{10,11... | collective-permute-start | bytes 294920 | tf_op jit(solution)/shard_map/ppermute | solution.py:47
  139.8 2.9 %collective-permute-start.12 = (bf16[384,128]{1,0:T(8,128)(2,1)S(1)}, bf16[384,128]{1,0:T(8,128)(2,1)S(1)}, u32[]{:S(2)}, u32[]{:S(2)}) collective-permute-start(bf16[384,128]{1,0:T(8,128)(2,1)S(1)} %collective-permute-done.8.refs_1_.refs_2_), channel_id=1, source_target_pairs={{0,1},{1,0},{2,3},{3,2},{4,5},{5,4},{6,7},{7,6},{8,9},{9,8},{10,11... | collective-permute-start | bytes 294920 | tf_op jit(solution)/shard_map/ppermute | solution.py:47
  140.2 2.4 %collective-permute-start.11 = (bf16[384,128]{1,0:T(8,128)(2,1)S(1)}, bf16[384,128]{1,0:T(8,128)(2,1)S(1)}, u32[]{:S(2)}, u32[]{:S(2)}) collective-permute-start(bf16[384,128]{1,0:T(8,128)(2,1)S(1)} %collective-permute-done.7.refs_0_.refs_1_), channel_id=1, source_target_pairs={{0,1},{1,0},{2,3},{3,2},{4,5},{5,4},{6,7},{7,6},{8,9},{9,8},{10,11... | collective-permute-start | bytes 294920 | tf_op jit(solution)/shard_map/ppermute | solution.py:47
  140.8 3.3 %collective-permute-start.23 = (bf16[128,128]{1,0:T(8,128)(2,1)S(1)}, bf16[128,128]{1,0:T(8,128)(2,1)S(1)}, u32[]{:S(2)}, u32[]{:S(2)}) collective-permute-start(bf16[128,128]{1,0:T(8,128)(2,1)S(1)} %slice.4), channel_id=1, source_target_pairs={{0,3},{1,2},{2,1},{3,0},{4,7},{5,6},{6,5},{7,4},{8,11},{9,10},{10,... | collective-permute-start | bytes 98312 | tf_op jit(solution)/shard_map/ppermute | solution.py:642
  142.1 3.9 %collective-permute-start.22 = (bf16[128,128]{1,0:T(8,128)(2,1)S(1)}, bf16[128,128]{1,0:T(8,128)(2,1)S(1)}, u32[]{:S(2)}, u32[]{:S(2)}) collective-permute-start(bf16[128,128]{1,0:T(8,128)(2,1)S(1)} %slice.4), channel_id=1, source_target_pairs={{0,2},{2,0},{1,3},{3,1},{4,6},{6,4},{5,7},{7,5},{8,10},{10,8},{9,1... | collective-permute-start | bytes 98312 | tf_op jit(solution)/shard_map/ppermute | solution.py:47

commit v5 on v4

--- a/solution.py
+++ b/solution.py
@@ -263,50 +263,50 @@
     return [pl.BlockSpec(memory_space=pltpu.VMEM)] * count
 
 
-def pack_kernel(table, slots, frames, both, fq_ref, do_ref, fk_ref, fv_ref, t_ref, *refs):
-    outs, sems = refs[:-1], refs[-1]
+def pack_kernel(tables, frames, full, extra, fq_ref, do_ref, fk_ref, fv_ref, t_ref, *refs):
+    count = 2 * frames + 1
+    outs, (q_in, do_in, k_in, v_in, k2_in, v2_in, sems) = refs[:count], refs[count:]
     me, half = lax.axis_index("tm"), lax.axis_index("rep")
     rows = fq_ref.shape[0]
-    wide = slots * DH
-    copies = []
-
-    def copy(source, target):
-        copies.append(pltpu.make_async_copy(source, target, sems.at[len(copies)]))
-        copies[-1].start()
-
-    def tile_rows_at(tile):
-        return pl.ds(pl.multiple_of(tile * rows, rows), rows)
-
-    for m in range(len(outs)):
-        mine = m < frames
-        own = tile_rows_at(half if mine else 1 - half)
-        head = lookup(table, me ^ m if mine else me)
-        cols = pl.ds(pl.multiple_of(head * DH, DH), wide)
-        sources = [(2, fk_ref.at[own, cols]), (3, fv_ref.at[own, cols])]
-        if mine:
-            sources += [(0, fq_ref.at[:, cols]), (1, do_ref.at[:, cols])]
-        if both:
-            rest = tile_rows_at(1 - half)
-            sources += [(4, fk_ref.at[rest, cols]), (5, fv_ref.at[rest, cols])]
-        for place_in, source in sources:
-            copy(source, outs[m].at[:, pl.ds(place_in * wide, wide)])
-        if not both:
-            copy(t_ref.at[own, :], outs[m].at[:, pl.ds(4 * wide, t_ref.shape[1])])
-    for started in copies:
-        started.wait()
-
-
-def pack(table, slots, frames, both, fq, do, fk, fv, t):
-    rows = fq.shape[0]
-    width = 6 * DH * slots if both else 4 * DH * slots + t.shape[1]
-    count = frames if both else frames + 1
+    mine = pl.ds(pl.multiple_of(half * rows, rows), rows)
+    rest = pl.ds(pl.multiple_of((1 - half) * rows, rows), rows)
+    moves = [
+        (fq_ref, q_in), (do_ref, do_in), (fk_ref.at[mine, :], k_in), (fv_ref.at[mine, :], v_in),
+        (fk_ref.at[rest, :], k2_in), (fv_ref.at[rest, :], v2_in),
+    ]
+    copies = [pltpu.make_async_copy(a, b, sems.at[n]) for n, (a, b) in enumerate(moves)]
+    for copy in copies:
+        copy.start()
+    for copy in copies:
+        copy.wait()
+
+    def fill(out, refs, chip, group, heads):
+        wide = heads * DH
+        cols = pl.ds(pl.multiple_of(lookup(tables[group], chip) * DH, DH), wide)
+        for n, ref in enumerate(refs):
+            if ref is not None:
+                out[:, n * wide : (n + 1) * wide] = ref[:, cols]
+
+    for m in range(frames):
+        fill(outs[m], (q_in, do_in, k_in, v_in), me ^ m, 0, full)
+        outs[m][:, 4 * full * DH :] = t_ref[mine, :]
+        fill(outs[frames + 1 + m], (q_in, do_in, k_in, v_in, k2_in, v2_in), me ^ m, 1, extra)
+    fill(outs[frames], (None, None, k2_in, v2_in), me, 0, full)
+    outs[frames][:, 4 * full * DH :] = t_ref[rest, :]
+
+
+def pack(tables, frames, full, extra, fq, do, fk, fv, t):
+    rows, width = fq.shape
+    first = jax.ShapeDtypeStruct((rows, 4 * DH * full + t.shape[1]), BF16)
+    second = jax.ShapeDtypeStruct((rows, 6 * DH * extra), BF16)
     anywhere = pl.BlockSpec(memory_space=pl.ANY)
     return pl.pallas_call(
-        functools.partial(pack_kernel, table, slots, frames, both),
-        in_specs=[anywhere] * 5,
-        out_specs=[anywhere] * count,
-        out_shape=[jax.ShapeDtypeStruct((rows, width), BF16)] * count,
-        scratch_shapes=[pltpu.SemaphoreType.DMA((6 * count,))],
+        functools.partial(pack_kernel, tables, frames, full, extra),
+        in_specs=[anywhere] * 4 + vmem(1),
+        out_specs=vmem(2 * frames + 1),
+        out_shape=[first] * (frames + 1) + [second] * frames,
+        scratch_shapes=[pltpu.VMEM((rows, width), BF16)] * 6 + [pltpu.SemaphoreType.DMA((6,))],
+        compiler_params=pltpu.CompilerParams(vmem_limit_bytes=56 * 1024 * 1024),
     )(fq, do, fk, fv, t)
 
 
@@ -393,10 +393,11 @@
     mine = take(frames)
     others = mine if chained else take(frames)
     if chained:
+        take(1)
         t_mine, t_others = take(frames), take(frames)
     adapters = take(3)
     before = take(2) if chained else [None, None]
-    keep_ref, give_ref = take(2)
+    keep_ref, *give_refs = take(3 if chained else 2)
     low_refs = [] if chained else take(2)
     same, other, t_same, t_other = refs
     me, half = lax.axis_index("tm"), lax.axis_index("rep")
@@ -406,6 +407,12 @@
     main = 4 * slots * DH
     wide = slots * DH
 
+    def give_out(gives):
+        whole = jnp.concatenate(gives, axis=0)
+        size = whole.shape[0] // len(give_refs)
+        for n, ref in enumerate(give_refs):
+            ref[...] = whole[n * size : (n + 1) * size].astype(ref.dtype)
+
     def body():
         for m in range(frames):
             at = pl.ds(pl.multiple_of((me ^ m) * rows, rows), rows)
@@ -414,6 +421,7 @@
             other[at, :] = others[m][:, start : start + main // 2]
             t_same[at, :] = t_mine[m][...] if chained else mine[m][:, main:]
             t_other[at, :] = t_others[m][...] if chained else others[m][:, main:]
+        gives = []
         total_same, total_other = [None if ref is None else ref[...] for ref in before]
         for s, table in enumerate(tables):
             cols = column(lookup(table, me))
@@ -429,13 +437,14 @@
             )
             first = half == 0
             keep_ref[s * cut : (s + 1) * cut, :] = jnp.where(first, grads[:cut], grads[cut:])
-            give_ref[s * cut : (s + 1) * cut, :] = jnp.where(first, grads[cut:], grads[:cut])
+            gives.append(jnp.where(first, grads[cut:], grads[:cut]))
             total_same = low_same if total_same is None else total_same + low_same
             total_other = low_other if total_other is None else total_other + low_other
         if chained:
             keep_ref[slots * cut :, :] = total_same
-            give_ref[slots * cut :, :] = total_other
-        else:
+            gives.append(total_other)
+        give_out(gives)
+        if not chained:
             low_refs[0][...] = total_same
             low_refs[1][...] = total_other
 
@@ -449,12 +458,11 @@
         def _():
             zeros = jnp.zeros((slots * cut, DH), F32)
             keep_ref[: slots * cut, :] = zeros
-            give_ref[: slots * cut, :] = zeros
             keep_ref[slots * cut :, :] = before[0][...]
-            give_ref[slots * cut :, :] = before[1][...]
-
-
-def head_group(tables, counts, bands, mine, others, adapters, before=None):
+            give_out([zeros, before[1][...]])
+
+
+def head_group(tables, counts, bands, mine, others, adapters, before=None, after=None):
     frames, rows = len(mine), mine[0].shape[0]
     rank = adapters[0].shape[0]
     slots = len(tables)
@@ -462,8 +470,10 @@
     size = slots * 3 * rank // 2
     main = 4 * slots * DH
     chained = before is not None
-    args = [bands, *mine, *others, *adapters]
+    args = [bands, *mine, *([after] if chained else []), *others, *adapters]
     specs = [pl.BlockSpec(memory_space=pltpu.SMEM)] + vmem(frames)
+    if chained:
+        specs.append(pl.BlockSpec(memory_space=pl.ANY))
     if chained:
         col = others[0].shape[1] // rank - 1
         specs += [pl.BlockSpec((rows, rank), lambda n: (0, col))] * len(others) + vmem(3 + len(before))
@@ -472,7 +482,10 @@
         specs += vmem(len(others) + 3)
     low = jax.ShapeDtypeStruct((flat, rank), F32)
     edge = jax.ShapeDtypeStruct((size + (flat if chained else 0), rank), F32)
-    shapes = [edge, edge] + ([] if chained else [low, low])
+    if chained:
+        shapes = [edge] + [jax.ShapeDtypeStruct((edge.shape[0] // 2, rank), BF16)] * 2
+    else:
+        shapes = [edge, edge, low, low]
     return pl.pallas_call(
         functools.partial(group_kernel, tables, frames, counts, chained),
         grid=(1,),
@@ -494,30 +507,43 @@
     )(*args)
 
 
-def hand_out_kernel(frames, size, waits, keep_ref, got_ref, *refs):
-    own_ref, *sends = refs[waits:]
+def gate(block, after):
+    anywhere = pl.BlockSpec(memory_space=pl.ANY)
+    return pl.pallas_call(
+        lambda *refs: None,
+        in_specs=[anywhere] * (1 + len(after)),
+        out_specs=anywhere,
+        out_shape=jax.ShapeDtypeStruct(block.shape, block.dtype),
+        input_output_aliases={0: 0},
+        compiler_params=SMALL,
+    )(block, *after)
+
+
+def hand_out_kernel(frames, size, parts, waits, keep_ref, *refs):
+    gots, (own_ref, *sends, total) = refs[:parts], refs[parts + waits :]
     me = lax.axis_index("tm")
     rows = own_ref.shape[0]
-    grads = (keep_ref[:size, :] + got_ref[:size, :]).astype(BF16)
+    total[...] = keep_ref[...] + jnp.concatenate([got[...].astype(F32) for got in gots], axis=0)
+    grads = total[:size, :].astype(BF16)
     for m in range(frames):
-        at = pl.ds(pl.multiple_of(size + (me ^ m) * rows, 8), rows)
-        low = keep_ref[at, :] + got_ref[at, :]
+        low = total[pl.ds(pl.multiple_of(size + (me ^ m) * rows, 8), rows), :]
         if m == 0:
             own_ref[...] = low
         sends[m][:rows, :] = low.astype(BF16)
         sends[m][rows:, :] = grads
 
 
-def hand_out(frames, rows, keep, got, after):
+def hand_out(frames, rows, keep, gots, after):
     size, rank = keep.shape[0] - frames * rows, keep.shape[1]
     send = jax.ShapeDtypeStruct((rows + size, rank), BF16)
     return pl.pallas_call(
-        functools.partial(hand_out_kernel, frames, size, len(after)),
-        in_specs=vmem(2) + [pl.BlockSpec(memory_space=pl.ANY)] * len(after),
+        functools.partial(hand_out_kernel, frames, size, len(gots), len(after)),
+        in_specs=vmem(1 + len(gots)) + [pl.BlockSpec(memory_space=pl.ANY)] * len(after),
         out_specs=vmem(frames + 1),
         out_shape=[jax.ShapeDtypeStruct((rows, rank), F32)] + [send] * frames,
+        scratch_shapes=[pltpu.VMEM(keep.shape, F32)],
         compiler_params=SMALL,
-    )(keep, got, *after)
+    )(keep, *gots, *after)
 
 
 def collect_kernel(frames, own_ref, *refs):
@@ -619,20 +645,22 @@
     def meet(block, m, targets=range(frames)):
         return lax.ppermute(block, "tm", [(j ^ m, j) for j in targets])
 
-    packed = pack(columns[0], full, frames, False, *arrays)
+    extra = most - full
+    tables = (columns[0], [min(h, heads - extra) for h in columns[full]])
+    packed = pack(tables, frames, full, extra, *arrays)
     mine = [packed[0]] + [meet(packed[m], m) for m in range(1, frames)]
-    packed2 = pack(columns[full], most - full, frames, True, *arrays)
+    packed2 = packed[frames + 1 :]
     mine2 = [packed2[0]] + [meet(packed2[m], m, wide) for m in range(1, frames)]
     others = [packed[frames]] + [swap(block, "rep") for block in mine[1:]]
     keep, give, *low = head_group(columns[:full], counts, band_width, mine, others, adapters)
-    piece = (keep + swap(give, "rep")).astype(BF16)
+    piece = (keep + swap(gate(give, mine2[1:]), "rep")).astype(BF16)
     pieces = [piece] + [meet(piece, m) for m in range(1, frames)]
     pieces2 = [swap(block, "rep") for block in pieces]
-    keep, give = head_group(
+    keep, *gives = head_group(
         columns[full:], [c - full for c in counts], band_width, mine2, mine + others, adapters,
-        low,
+        low, piece,
     )
-    own, *sends = hand_out(frames, rows, keep, swap(give, "rep"), pieces[1:])
+    own, *sends = hand_out(frames, rows, keep, [swap(g, "rep") for g in gives], pieces[1:])
     gots = [sends[0]] + [meet(sends[m], m) for m in range(1, frames)]
     tail = collect(own, gots)
     low = tail[:rows]

time: 148 us -> 83.7 us (0.57)
  Pallas kernels: 76.5 us -> 13.4 us
  starting transfers between devices: 32.3 us -> 28.8 us
  local copies, waits for them, and re-layouts: 0.03 us -> 1.94 us
    pallas_call x3, Pallas kernels: 67.3 us -> 4.09 us  [the longest x1 4.02 us: pack(): pl.pallas_call(functools.partial(pack_kernel, tables, frames, full, extra...]
    ppermute x12, starting transfers between devices: 28.2 us -> 24.4 us  [meet(): return lax.ppermute(block, 'tm', [(j ^ m, j) for j in targets])]
    ppermute x11 -> x12, waiting for transfers between devices: 2.6 us -> 4.55 us  [swap(): return lax.ppermute(block, axis, [(0, 1), (1, 0)])]
    unnamed x14, local copies, waits for them, and re-layouts: 0.03 us -> 1.94 us
    ppermute x11 -> x12, starting transfers between devices: 2.85 us -> 3.06 us  [swap(): return lax.ppermute(block, axis, [(0, 1), (1, 0)])]
  transfers between devices with their start and end apart: 24 -> 25, of which waited for: 9 -> 12; matrix products, arithmetic and copies ran while one was open for 0% -> 0% of each run, Pallas kernels for 22% -> 9%
where the time goes in v5:
time: 83.7 us; the launch traced here: 83.4 us
  waiting for transfers between devices  38.5 us (46%)
  starting transfers between devices  28.8 us (34%)
  Pallas kernels  13.4 us (16%)
  local copies, waits for them, and re-layouts  1.94 us (2%)
  between operations  0.86 us (1%)
    ppermute x12, waiting for transfers between devices, meet(): return lax.ppermute(block, 'tm', [(j ^ m, j) for j in targets])  32.4 us
    ppermute x12, starting transfers between devices, meet(): return lax.ppermute(block, 'tm', [(j ^ m, j) for j in targets])  24.4 us
    pallas_call x2, Pallas kernels, head_group(): pl.pallas_call(functools.partial(group_kernel, tables, frames, counts, ch...  7.74 us
    ppermute x12, waiting for transfers between devices, swap(): return lax.ppermute(block, axis, [(0, 1), (1, 0)])  4.55 us
    pallas_call x1, Pallas kernels, pack(): pl.pallas_call(functools.partial(pack_kernel, tables, frames, full, extra...  4.02 us
    ppermute x12, starting transfers between devices, swap(): return lax.ppermute(block, axis, [(0, 1), (1, 0)])  3.06 us
    unnamed x14, local copies, waits for them, and re-layouts  1.94 us
  transfers between devices with their start and end apart: 25, of which 12 were waited for; matrix products, arithmetic and copies ran while one was open for 0% of the time, Pallas kernels for 9%

profile of v5, /device:TPU:0, one launch (start us, length us, event | category | flops | bytes accessed | tf_op | source)
XLA Modules:
  0.0 83.4 jit_solution(15947233140272846429)
XLA Ops:
  0.7 4.0 %shard_map.120 = (bf16[128,1152]{1,0:T(8,128)(2,1)}, bf16[128,1152]{1,0:T(8,128)(2,1)}, bf16[128,1152]{1,0:T(8,128)(2,1)}, bf16[128,1152]{1,0:T(8,128)(2,1)}, bf...) custom-call(bf16[128,1280]{1,0:T(8,128)(2,1)} %fq_ref.1, ...), custom_call_target="tpu_custom_call" | custom-call | tf_op jit(solution)/shard_map/pallas_call | solution.py:303
  4.7 3.1 %collective-permute-start = (bf16[128,1152]{1,0:T(8,128)(2,1)}, bf16[128,1152]{1,0:T(8,128)(2,1)S(1)}, u32[]{:S(2)}, u32[]{:S(2)}) collective-permute-start(bf16[128,1152]{1,0:T(8,128)(2,1)} %get-tuple-element.26), channel_id=1, source_target_pairs={{4,0},{0,4},{12,8},{8,12},{5,1},{1,5},{13,9},{9,13},{6,2},{2,6},{1... | collective-permute-start | bytes 884744 | tf_op jit(solution)/shard_map/ppermute | solution.py:646
  7.8 2.6 %collective-permute-start.1 = (bf16[128,1152]{1,0:T(8,128)(2,1)}, bf16[128,1152]{1,0:T(8,128)(2,1)S(1)}, u32[]{:S(2)}, u32[]{:S(2)}) collective-permute-start(bf16[128,1152]{1,0:T(8,128)(2,1)} %get-tuple-element.27), channel_id=1, source_target_pairs={{8,0},{12,4},{0,8},{4,12},{9,1},{13,5},{1,9},{5,13},{10,2},{14,6},... | collective-permute-start | bytes 884744 | tf_op jit(solution)/shard_map/ppermute | solution.py:646
  10.4 10.2 %collective-permute-done.refs_2_.refs_7_ = bf16[128,1152]{1,0:T(8,128)(2,1)S(1)} collective-permute-done((bf16[128,1152]{1,0:T(8,128)(2,1)}, bf16[128,1152]{1,0:T(8,128)(2,1)S(1)}, u32[]{:S(2)}, u32[]{:S(2)}) %collective-permute-start) | collective-permute-done | bytes 294944 | tf_op jit(solution)/shard_map/ppermute | solution.py:646
  20.6 10.9 %collective-permute-done.1.refs_3_.refs_8_ = bf16[128,1152]{1,0:T(8,128)(2,1)S(1)} collective-permute-done((bf16[128,1152]{1,0:T(8,128)(2,1)}, bf16[128,1152]{1,0:T(8,128)(2,1)S(1)}, u32[]{:S(2)}, u32[]{:S(2)}) %collective-permute-start.1) | collective-permute-done | bytes 294944 | tf_op jit(solution)/shard_map/ppermute | solution.py:646
  31.5 0.5 collective-permute-start.5
  32.0 6.9 %collective-permute-start.6 = (bf16[128,768]{1,0:T(8,128)(2,1)}, bf16[128,768]{1,0:T(8,128)(2,1)S(1)}, u32[]{:S(2)}, u32[]{:S(2)}) collective-permute-start(bf16[128,768]{1,0:T(8,128)(2,1)} %get-tuple-element.32), channel_id=1, source_target_pairs={{0,4},{12,8},{1,5},{13,9},{2,6},{14,10},{3,7},{15,11},{16,20},{28,... | collective-permute-start | bytes 589832 | tf_op jit(solution)/shard_map/ppermute | solution.py:646
  38.8 2.3 %collective-permute-start.7 = (bf16[128,768]{1,0:T(8,128)(2,1)}, bf16[128,768]{1,0:T(8,128)(2,1)S(1)}, u32[]{:S(2)}, u32[]{:S(2)}) collective-permute-start(bf16[128,768]{1,0:T(8,128)(2,1)} %get-tuple-element.33), channel_id=1, source_target_pairs={{12,4},{0,8},{13,5},{1,9},{14,6},{2,10},{15,7},{3,11},{28,20},{16,... | collective-permute-start | bytes 589832 | tf_op jit(solution)/shard_map/ppermute | solution.py:646
  41.2 0.7 collective-permute-start.8
  41.9 1.0 %copy-done.3 = bf16[128,1152]{1,0:T(8,128)(2,1)S(1)} copy-done((bf16[128,1152]{1,0:T(8,128)(2,1)S(1)}, bf16[128,1152]{1,0:T(8,128)(2,1)}, u32[]{:S(2)}) %copy-start.3) | copy-done | bytes 294936
  42.9 1.0 %copy-done.4 = bf16[128,1152]{1,0:T(8,128)(2,1)S(1)} copy-done((bf16[128,1152]{1,0:T(8,128)(2,1)S(1)}, bf16[128,1152]{1,0:T(8,128)(2,1)}, u32[]{:S(2)}) %copy-start.4) | copy-done | bytes 294936
  43.8 7.1 %shard_map.121 = (f32[384,128]{1,0:T(8,128)S(1)}, f32[384,128]{1,0:T(8,128)S(1)}, f32[512,128]{1,0:T(8,128)S(1)}, f32[512,128]{1,0:T(8,128)S(1)}) custom-call(s32[4,4]{1,0:T(4,128)S(1)} %copy-done.6, bf16[128,1152]{1,0:T(8,128)(2,1)S(1)} %copy-done.3, bf16[128,1152]{1,0:T(8,128)(2,1)S(1)} %collective-permute-done.refs_2_.refs_7_, ...), custom_call_target="tpu_custom_call" | custom-call | flops 17179869184 | bytes 2097152 | tf_op jit(solution)/shard_map/pallas_call | solution.py:489
  51.3 1.2 %collective-permute-done.9 = f32[384,128]{1,0:T(8,128)S(1)} collective-permute-done((f32[384,128]{1,0:T(8,128)S(1)}, f32[384,128]{1,0:T(8,128)S(1)}, u32[]{:S(2)}, u32[]{:S(2)}) %collective-permute-start.9) | collective-permute-done | bytes 196640 | tf_op jit(solution)/shard_map/ppermute | solution.py:47
  52.5 1.5 %collective-permute-start.12 = (bf16[384,128]{1,0:T(8,128)(2,1)S(1)}, bf16[384,128]{1,0:T(8,128)(2,1)S(1)}, u32[]{:S(2)}, u32[]{:S(2)}) collective-permute-start(bf16[384,128]{1,0:T(8,128)(2,1)S(1)} %add_convert_fusion.refs_5_.refs_0_), channel_id=1, source_target_pairs={{12,0},{8,4},{4,8},{0,12},{13,1},{9,5},{5,9},{1,13},{14,2},{10,6},... | collective-permute-start | bytes 294920 | tf_op jit(solution)/shard_map/ppermute | solution.py:646
  54.1 2.1 %collective-permute-start.11 = (bf16[384,128]{1,0:T(8,128)(2,1)S(1)}, bf16[384,128]{1,0:T(8,128)(2,1)S(1)}, u32[]{:S(2)}, u32[]{:S(2)}) collective-permute-start(bf16[384,128]{1,0:T(8,128)(2,1)S(1)} %add_convert_fusion.refs_5_.refs_0_), channel_id=1, source_target_pairs={{8,0},{12,4},{0,8},{4,12},{9,1},{13,5},{1,9},{5,13},{10,2},{14,6},... | collective-permute-start | bytes 294920 | tf_op jit(solution)/shard_map/ppermute | solution.py:646
  56.2 0.8 collective-permute-start.10
  57.0 0.6 shard_map.123
  57.7 0.5 collective-permute-start.18
  58.2 0.8 collective-permute-done.17.refs_0_
  59.1 0.6 collective-permute-done.12.refs_4_.refs_3_
  59.7 5.6 %collective-permute-done.11.refs_3_.refs_2_ = bf16[384,128]{1,0:T(8,128)(2,1)S(1)} collective-permute-done((bf16[384,128]{1,0:T(8,128)(2,1)S(1)}, bf16[384,128]{1,0:T(8,128)(2,1)S(1)}, u32[]{:S(2)}, u32[]{:S(2)}) %collective-permute-start.11) | collective-permute-done | bytes 98336 | tf_op jit(solution)/shard_map/ppermute | solution.py:646
  65.5 2.4 %collective-permute-start.20 = (bf16[320,128]{1,0:T(8,128)(2,1)S(1)}, bf16[320,128]{1,0:T(8,128)(2,1)S(1)}, u32[]{:S(2)}, u32[]{:S(2)}) collective-permute-start(bf16[320,128]{1,0:T(8,128)(2,1)S(1)} %get-tuple-element.44), channel_id=1, source_target_pairs={{8,0},{12,4},{0,8},{4,12},{9,1},{13,5},{1,9},{5,13},{10,2},{14,6},... | collective-permute-start | bytes 245768 | tf_op jit(solution)/shard_map/ppermute | solution.py:646
  67.8 2.0 %collective-permute-start.21 = (bf16[320,128]{1,0:T(8,128)(2,1)S(1)}, bf16[320,128]{1,0:T(8,128)(2,1)S(1)}, u32[]{:S(2)}, u32[]{:S(2)}) collective-permute-start(bf16[320,128]{1,0:T(8,128)(2,1)S(1)} %get-tuple-element.45), channel_id=1, source_target_pairs={{12,0},{8,4},{4,8},{0,12},{13,1},{9,5},{5,9},{1,13},{14,2},{10,6},... | collective-permute-start | bytes 245768 | tf_op jit(solution)/shard_map/ppermute | solution.py:646
  69.8 0.7 collective-permute-done.19.refs_1_
  70.5 4.4 %collective-permute-done.20.refs_2_ = bf16[320,128]{1,0:T(8,128)(2,1)S(1)} collective-permute-done((bf16[320,128]{1,0:T(8,128)(2,1)S(1)}, bf16[320,128]{1,0:T(8,128)(2,1)S(1)}, u32[]{:S(2)}, u32[]{:S(2)}) %collective-permute-start.20) | collective-permute-done | bytes 81952 | tf_op jit(solution)/shard_map/ppermute | solution.py:646
  75.1 0.5 collective-permute-start.13
  76.2 0.5 collective-permute-done.13.refs_4_
  76.7 1.3 %collective-permute-start.24 = (bf16[128,128]{1,0:T(8,128)(2,1)S(1)}, bf16[128,128]{1,0:T(8,128)(2,1)S(1)}, u32[]{:S(2)}, u32[]{:S(2)}) collective-permute-start(bf16[128,128]{1,0:T(8,128)(2,1)S(1)} %slice.4), channel_id=1, source_target_pairs={{0,3},{1,2},{2,1},{3,0},{4,7},{5,6},{6,5},{7,4},{8,11},{9,10},{10,... | collective-permute-start | bytes 98312 | tf_op jit(solution)/shard_map/ppermute | solution.py:670
  78.0 0.5 collective-permute-start.23
  78.5 1.5 %collective-permute-done.24.refs_11_ = bf16[128,128]{1,0:T(8,128)(2,1)S(1)} collective-permute-done((bf16[128,128]{1,0:T(8,128)(2,1)S(1)}, bf16[128,128]{1,0:T(8,128)(2,1)S(1)}, u32[]{:S(2)}, u32[]{:S(2)}) %collective-permute-start.24) | collective-permute-done | bytes 32800 | tf_op jit(solution)/shard_map/ppermute | solution.py:670
  80.0 1.9 %collective-permute-done.23.refs_10_ = bf16[128,128]{1,0:T(8,128)(2,1)S(1)} collective-permute-done((bf16[128,128]{1,0:T(8,128)(2,1)S(1)}, bf16[128,128]{1,0:T(8,128)(2,1)S(1)}, u32[]{:S(2)}, u32[]{:S(2)}) %collective-permute-start.23) | collective-permute-done | bytes 32800 | tf_op jit(solution)/shard_map/ppermute | solution.py:47
  81.9 1.5 %shard_map.126 = (f32[128,1280]{1,0:T(8,128)}, f32[128,1280]{1,0:T(8,128)}, f32[128,1280]{1,0:T(8,128)}, f32[256,128]{1,0:T(8,128)}) custom-call(bf16[384,128]{1,0:T(8,128)(2,1)S(1)} %add_convert_fusion.refs_5_.refs_0_, bf16[384,128]{1,0:T(8,128)(2,1)S(1)} %collective-permute-done.10.refs_2_.refs_1_, ...), custom_call_target="tpu_custom_call" | custom-call | tf_op jit(solution)/shard_map/pallas_call | solution.py:612
  (41 shorter events, 1.4 us)
Async XLA Ops:
  0.6 41.2 %copy-start.2 = (bf16[128,1280]{1,0:T(8,128)(2,1)S(1)}, bf16[128,1280]{1,0:T(8,128)(2,1)}, u32[]{:S(2)}) copy-start(bf16[128,1280]{1,0:T(8,128)(2,1)} %refs_16_.1) | copy-start | bytes 983044
  0.6 41.2 %copy-start.1 = (bf16[128,1280]{1,0:T(8,128)(2,1)S(1)}, bf16[128,1280]{1,0:T(8,128)(2,1)}, u32[]{:S(2)}) copy-start(bf16[128,1280]{1,0:T(8,128)(2,1)} %refs_15_.1) | copy-start | bytes 983044
  0.7 41.2 %copy-start = (bf16[128,1280]{1,0:T(8,128)(2,1)S(1)}, bf16[128,1280]{1,0:T(8,128)(2,1)}, u32[]{:S(2)}) copy-start(bf16[128,1280]{1,0:T(8,128)(2,1)} %refs_14_.1) | copy-start | bytes 983044
  4.7 15.9 %collective-permute-start = (bf16[128,1152]{1,0:T(8,128)(2,1)}, bf16[128,1152]{1,0:T(8,128)(2,1)S(1)}, u32[]{:S(2)}, u32[]{:S(2)}) collective-permute-start(bf16[128,1152]{1,0:T(8,128)(2,1)} %get-tuple-element.26), channel_id=1, source_target_pairs={{4,0},{0,4},{12,8},{8,12},{5,1},{1,5},{13,9},{9,13},{6,2},{2,6},{1... | collective-permute-start | bytes 884744 | tf_op jit(solution)/shard_map/ppermute | solution.py:646
  7.8 23.7 %collective-permute-start.1 = (bf16[128,1152]{1,0:T(8,128)(2,1)}, bf16[128,1152]{1,0:T(8,128)(2,1)S(1)}, u32[]{:S(2)}, u32[]{:S(2)}) collective-permute-start(bf16[128,1152]{1,0:T(8,128)(2,1)} %get-tuple-element.27), channel_id=1, source_target_pairs={{8,0},{12,4},{0,8},{4,12},{9,1},{13,5},{1,9},{5,13},{10,2},{14,6},... | collective-permute-start | bytes 884744 | tf_op jit(solution)/shard_map/ppermute | solution.py:646
  10.4 21.1 %collective-permute-start.2 = (bf16[128,1152]{1,0:T(8,128)(2,1)}, bf16[128,1152]{1,0:T(8,128)(2,1)S(1)}, u32[]{:S(2)}, u32[]{:S(2)}) collective-permute-start(bf16[128,1152]{1,0:T(8,128)(2,1)} %get-tuple-element.28), channel_id=1, source_target_pairs={{12,0},{8,4},{4,8},{0,12},{13,1},{9,5},{5,9},{1,13},{14,2},{10,6},... | collective-permute-start | bytes 884744 | tf_op jit(solution)/shard_map/ppermute | solution.py:646
  20.5 20.6 %collective-permute-start.3 = (bf16[128,1152]{1,0:T(8,128)(2,1)S(1)}, bf16[128,1152]{1,0:T(8,128)(2,1)S(1)}, u32[]{:S(2)}, u32[]{:S(2)}) collective-permute-start(bf16[128,1152]{1,0:T(8,128)(2,1)S(1)} %collective-permute-done.refs_2_.refs_7_), channel_id=1, source_target_pairs={{0,1},{1,0},{2,3},{3,2},{4,5},{5,4},{6,7},{7,6},{8,9},{9,8},{10,11... | collective-permute-start | bytes 884744 | tf_op jit(solution)/shard_map/ppermute | solution.py:47
  31.5 10.4 %collective-permute-start.4 = (bf16[128,1152]{1,0:T(8,128)(2,1)S(1)}, bf16[128,1152]{1,0:T(8,128)(2,1)S(1)}, u32[]{:S(2)}, u32[]{:S(2)}) collective-permute-start(bf16[128,1152]{1,0:T(8,128)(2,1)S(1)} %collective-permute-done.1.refs_3_.refs_8_), channel_id=1, source_target_pairs={{0,1},{1,0},{2,3},{3,2},{4,5},{5,4},{6,7},{7,6},{8,9},{9,8},{10,11... | collective-permute-start | bytes 884744 | tf_op jit(solution)/shard_map/ppermute | solution.py:47
  31.5 10.4 %collective-permute-start.5 = (bf16[128,1152]{1,0:T(8,128)(2,1)S(1)}, bf16[128,1152]{1,0:T(8,128)(2,1)S(1)}, u32[]{:S(2)}, u32[]{:S(2)}) collective-permute-start(bf16[128,1152]{1,0:T(8,128)(2,1)S(1)} %collective-permute-done.2.refs_4_.refs_9_), channel_id=1, source_target_pairs={{0,1},{1,0},{2,3},{3,2},{4,5},{5,4},{6,7},{7,6},{8,9},{9,8},{10,11... | collective-permute-start | bytes 884744 | tf_op jit(solution)/shard_map/ppermute | solution.py:47
  32.0 19.0 %collective-permute-start.6 = (bf16[128,768]{1,0:T(8,128)(2,1)}, bf16[128,768]{1,0:T(8,128)(2,1)S(1)}, u32[]{:S(2)}, u32[]{:S(2)}) collective-permute-start(bf16[128,768]{1,0:T(8,128)(2,1)} %get-tuple-element.32), channel_id=1, source_target_pairs={{0,4},{12,8},{1,5},{13,9},{2,6},{14,10},{3,7},{15,11},{16,20},{28,... | collective-permute-start | bytes 589832 | tf_op jit(solution)/shard_map/ppermute | solution.py:646
  38.8 12.1 %collective-permute-start.7 = (bf16[128,768]{1,0:T(8,128)(2,1)}, bf16[128,768]{1,0:T(8,128)(2,1)S(1)}, u32[]{:S(2)}, u32[]{:S(2)}) collective-permute-start(bf16[128,768]{1,0:T(8,128)(2,1)} %get-tuple-element.33), channel_id=1, source_target_pairs={{12,4},{0,8},{13,5},{1,9},{14,6},{2,10},{15,7},{3,11},{28,20},{16,... | collective-permute-start | bytes 589832 | tf_op jit(solution)/shard_map/ppermute | solution.py:646
  41.2 0.7 copy-start.6
  41.2 9.8 %collective-permute-start.8 = (bf16[128,768]{1,0:T(8,128)(2,1)}, bf16[128,768]{1,0:T(8,128)(2,1)S(1)}, u32[]{:S(2)}, u32[]{:S(2)}) collective-permute-start(bf16[128,768]{1,0:T(8,128)(2,1)} %get-tuple-element.34), channel_id=1, source_target_pairs={{8,4},{4,8},{9,5},{5,9},{10,6},{6,10},{11,7},{7,11},{24,20},{20,24... | collective-permute-start | bytes 589832 | tf_op jit(solution)/shard_map/ppermute | solution.py:646
  41.9 1.0 %copy-start.3 = (bf16[128,1152]{1,0:T(8,128)(2,1)S(1)}, bf16[128,1152]{1,0:T(8,128)(2,1)}, u32[]{:S(2)}) copy-start(bf16[128,1152]{1,0:T(8,128)(2,1)} %get-tuple-element.25.refs_1_.refs_6_) | copy-start | bytes 884740
  42.9 1.0 %copy-start.4 = (bf16[128,1152]{1,0:T(8,128)(2,1)S(1)}, bf16[128,1152]{1,0:T(8,128)(2,1)}, u32[]{:S(2)}) copy-start(bf16[128,1152]{1,0:T(8,128)(2,1)} %get-tuple-element.29.refs_5_.refs_10_) | copy-start | bytes 884740
  51.0 1.5 %collective-permute-start.9 = (f32[384,128]{1,0:T(8,128)S(1)}, f32[384,128]{1,0:T(8,128)S(1)}, u32[]{:S(2)}, u32[]{:S(2)}) collective-permute-start(f32[384,128]{1,0:T(8,128)S(1)} %shard_map.122), channel_id=1, source_target_pairs={{0,1},{1,0},{2,3},{3,2},{4,5},{5,4},{6,7},{7,6},{8,9},{9,8},{10,11... | collective-permute-start | bytes 589832 | tf_op jit(solution)/shard_map/ppermute | solution.py:47
  52.5 4.5 %copy-start.5 = (bf16[128,768]{1,0:T(8,128)(2,1)S(1)}, bf16[128,768]{1,0:T(8,128)(2,1)}, u32[]{:S(2)}) copy-start(bf16[128,768]{1,0:T(8,128)(2,1)} %get-tuple-element.35.refs_1_) | copy-start | bytes 589828
  52.5 7.2 %collective-permute-start.12 = (bf16[384,128]{1,0:T(8,128)(2,1)S(1)}, bf16[384,128]{1,0:T(8,128)(2,1)S(1)}, u32[]{:S(2)}, u32[]{:S(2)}) collective-permute-start(bf16[384,128]{1,0:T(8,128)(2,1)S(1)} %add_convert_fusion.refs_5_.refs_0_), channel_id=1, source_target_pairs={{12,0},{8,4},{4,8},{0,12},{13,1},{9,5},{5,9},{1,13},{14,2},{10,6},... | collective-permute-start | bytes 294920 | tf_op jit(solution)/shard_map/ppermute | solution.py:646
  54.1 11.2 %collective-permute-start.11 = (bf16[384,128]{1,0:T(8,128)(2,1)S(1)}, bf16[384,128]{1,0:T(8,128)(2,1)S(1)}, u32[]{:S(2)}, u32[]{:S(2)}) collective-permute-start(bf16[384,128]{1,0:T(8,128)(2,1)S(1)} %add_convert_fusion.refs_5_.refs_0_), channel_id=1, source_target_pairs={{8,0},{12,4},{0,8},{4,12},{9,1},{13,5},{1,9},{5,13},{10,2},{14,6},... | collective-permute-start | bytes 294920 | tf_op jit(solution)/shard_map/ppermute | solution.py:646
  56.2 9.1 %collective-permute-start.10 = (bf16[384,128]{1,0:T(8,128)(2,1)S(1)}, bf16[384,128]{1,0:T(8,128)(2,1)S(1)}, u32[]{:S(2)}, u32[]{:S(2)}) collective-permute-start(bf16[384,128]{1,0:T(8,128)(2,1)S(1)} %add_convert_fusion.refs_5_.refs_0_), channel_id=1, source_target_pairs={{4,0},{0,4},{12,8},{8,12},{5,1},{1,5},{13,9},{9,13},{6,2},{2,6},{1... | collective-permute-start | bytes 294920 | tf_op jit(solution)/shard_map/ppermute | solution.py:646
  57.6 1.4 %collective-permute-start.17 = (bf16[352,128]{1,0:T(8,128)(2,1)S(1)}, bf16[352,128]{1,0:T(8,128)(2,1)S(1)}, u32[]{:S(2)}, u32[]{:S(2)}) collective-permute-start(bf16[352,128]{1,0:T(8,128)(2,1)S(1)} %get-tuple-element.39), channel_id=1, source_target_pairs={{0,1},{1,0},{2,3},{3,2},{4,5},{5,4},{6,7},{7,6},{8,9},{9,8},{10,11... | collective-permute-start | bytes 270344 | tf_op jit(solution)/shard_map/ppermute | solution.py:47
  57.7 1.4 %collective-permute-start.18 = (bf16[352,128]{1,0:T(8,128)(2,1)S(1)}, bf16[352,128]{1,0:T(8,128)(2,1)S(1)}, u32[]{:S(2)}, u32[]{:S(2)}) collective-permute-start(bf16[352,128]{1,0:T(8,128)(2,1)S(1)} %get-tuple-element.40), channel_id=1, source_target_pairs={{0,1},{1,0},{2,3},{3,2},{4,5},{5,4},{6,7},{7,6},{8,9},{9,8},{10,11... | collective-permute-start | bytes 270344 | tf_op jit(solution)/shard_map/ppermute | solution.py:47
  65.4 5.1 %collective-permute-start.19 = (bf16[320,128]{1,0:T(8,128)(2,1)S(1)}, bf16[320,128]{1,0:T(8,128)(2,1)S(1)}, u32[]{:S(2)}, u32[]{:S(2)}) collective-permute-start(bf16[320,128]{1,0:T(8,128)(2,1)S(1)} %get-tuple-element.43), channel_id=1, source_target_pairs={{4,0},{0,4},{12,8},{8,12},{5,1},{1,5},{13,9},{9,13},{6,2},{2,6},{1... | collective-permute-start | bytes 245768 | tf_op jit(solution)/shard_map/ppermute | solution.py:646
  65.5 9.5 %collective-permute-start.20 = (bf16[320,128]{1,0:T(8,128)(2,1)S(1)}, bf16[320,128]{1,0:T(8,128)(2,1)S(1)}, u32[]{:S(2)}, u32[]{:S(2)}) collective-permute-start(bf16[320,128]{1,0:T(8,128)(2,1)S(1)} %get-tuple-element.44), channel_id=1, source_target_pairs={{8,0},{12,4},{0,8},{4,12},{9,1},{13,5},{1,9},{5,13},{10,2},{14,6},... | collective-permute-start | bytes 245768 | tf_op jit(solution)/shard_map/ppermute | solution.py:646
  67.8 7.1 %collective-permute-start.21 = (bf16[320,128]{1,0:T(8,128)(2,1)S(1)}, bf16[320,128]{1,0:T(8,128)(2,1)S(1)}, u32[]{:S(2)}, u32[]{:S(2)}) collective-permute-start(bf16[320,128]{1,0:T(8,128)(2,1)S(1)} %get-tuple-element.45), channel_id=1, source_target_pairs={{12,0},{8,4},{4,8},{0,12},{13,1},{9,5},{5,9},{1,13},{14,2},{10,6},... | collective-permute-start | bytes 245768 | tf_op jit(solution)/shard_map/ppermute | solution.py:646
  75.0 6.9 %collective-permute-start.22 = (bf16[896,128]{1,0:T(8,128)(2,1)S(1)}, bf16[896,128]{1,0:T(8,128)(2,1)S(1)}, u32[]{:S(2)}, u32[]{:S(2)}) collective-permute-start(bf16[896,128]{1,0:T(8,128)(2,1)S(1)} %shard_map.125.refs_8_), channel_id=1, source_target_pairs={{0,1},{1,0},{2,3},{3,2},{4,5},{5,4},{6,7},{7,6},{8,9},{9,8},{10,11... | collective-permute-start | bytes 688136 | tf_op jit(solution)/shard_map/ppermute | solution.py:47
  75.1 1.6 %collective-permute-start.13 = (bf16[384,128]{1,0:T(8,128)(2,1)S(1)}, bf16[384,128]{1,0:T(8,128)(2,1)S(1)}, u32[]{:S(2)}, u32[]{:S(2)}) collective-permute-start(bf16[384,128]{1,0:T(8,128)(2,1)S(1)} %add_convert_fusion.refs_5_.refs_0_), channel_id=1, source_target_pairs={{0,1},{1,0},{2,3},{3,2},{4,5},{5,4},{6,7},{7,6},{8,9},{9,8},{10,11... | collective-permute-start | bytes 294920 | tf_op jit(solution)/shard_map/ppermute | solution.py:47
  75.6 2.4 %collective-permute-start.16 = (bf16[384,128]{1,0:T(8,128)(2,1)S(1)}, bf16[384,128]{1,0:T(8,128)(2,1)S(1)}, u32[]{:S(2)}, u32[]{:S(2)}) collective-permute-start(bf16[384,128]{1,0:T(8,128)(2,1)S(1)} %collective-permute-done.12.refs_4_.refs_3_), channel_id=1, source_target_pairs={{0,1},{1,0},{2,3},{3,2},{4,5},{5,4},{6,7},{7,6},{8,9},{9,8},{10,11... | collective-permute-start | bytes 294920 | tf_op jit(solution)/shard_map/ppermute | solution.py:47
  75.6 2.9 %collective-permute-start.15 = (bf16[384,128]{1,0:T(8,128)(2,1)S(1)}, bf16[384,128]{1,0:T(8,128)(2,1)S(1)}, u32[]{:S(2)}, u32[]{:S(2)}) collective-permute-start(bf16[384,128]{1,0:T(8,128)(2,1)S(1)} %collective-permute-done.11.refs_3_.refs_2_), channel_id=1, source_target_pairs={{0,1},{1,0},{2,3},{3,2},{4,5},{5,4},{6,7},{7,6},{8,9},{9,8},{10,11... | collective-permute-start | bytes 294920 | tf_op jit(solution)/shard_map/ppermute | solution.py:47
  76.1 2.4 %collective-permute-start.14 = (bf16[384,128]{1,0:T(8,128)(2,1)S(1)}, bf16[384,128]{1,0:T(8,128)(2,1)S(1)}, u32[]{:S(2)}, u32[]{:S(2)}) collective-permute-start(bf16[384,128]{1,0:T(8,128)(2,1)S(1)} %collective-permute-done.10.refs_2_.refs_1_), channel_id=1, source_target_pairs={{0,1},{1,0},{2,3},{3,2},{4,5},{5,4},{6,7},{7,6},{8,9},{9,8},{10,11... | collective-permute-start | bytes 294920 | tf_op jit(solution)/shard_map/ppermute | solution.py:47
  76.7 3.3 %collective-permute-start.24 = (bf16[128,128]{1,0:T(8,128)(2,1)S(1)}, bf16[128,128]{1,0:T(8,128)(2,1)S(1)}, u32[]{:S(2)}, u32[]{:S(2)}) collective-permute-start(bf16[128,128]{1,0:T(8,128)(2,1)S(1)} %slice.4), channel_id=1, source_target_pairs={{0,3},{1,2},{2,1},{3,0},{4,7},{5,6},{6,5},{7,4},{8,11},{9,10},{10,... | collective-permute-start | bytes 98312 | tf_op jit(solution)/shard_map/ppermute | solution.py:670
  78.0 3.9 %collective-permute-start.23 = (bf16[128,128]{1,0:T(8,128)(2,1)S(1)}, bf16[128,128]{1,0:T(8,128)(2,1)S(1)}, u32[]{:S(2)}, u32[]{:S(2)}) collective-permute-start(bf16[128,128]{1,0:T(8,128)(2,1)S(1)} %slice.4), channel_id=1, source_target_pairs={{0,2},{2,0},{1,3},{3,1},{4,6},{6,4},{5,7},{7,5},{8,10},{10,8},{9,1... | collective-permute-start | bytes 98312 | tf_op jit(solution)/shard_map/ppermute | solution.py:47

commit v6 on v5

--- a/solution.py
+++ b/solution.py
@@ -263,9 +263,8 @@
     return [pl.BlockSpec(memory_space=pltpu.VMEM)] * count
 
 
-def pack_kernel(tables, frames, full, extra, fq_ref, do_ref, fk_ref, fv_ref, t_ref, *refs):
-    count = 2 * frames + 1
-    outs, (q_in, do_in, k_in, v_in, k2_in, v2_in, sems) = refs[:count], refs[count:]
+def pack_kernel(frames, outputs, fq_ref, do_ref, fk_ref, fv_ref, t_ref, *refs):
+    outs, (q_in, do_in, k_in, v_in, k2_in, v2_in, sems) = refs[:-7], refs[-7:]
     me, half = lax.axis_index("tm"), lax.axis_index("rep")
     rows = fq_ref.shape[0]
     mine = pl.ds(pl.multiple_of(half * rows, rows), rows)
@@ -279,41 +278,59 @@
         copy.start()
     for copy in copies:
         copy.wait()
-
-    def fill(out, refs, chip, group, heads):
-        wide = heads * DH
-        cols = pl.ds(pl.multiple_of(lookup(tables[group], chip) * DH, DH), wide)
-        for n, ref in enumerate(refs):
-            if ref is not None:
-                out[:, n * wide : (n + 1) * wide] = ref[:, cols]
-
-    for m in range(frames):
-        fill(outs[m], (q_in, do_in, k_in, v_in), me ^ m, 0, full)
-        outs[m][:, 4 * full * DH :] = t_ref[mine, :]
-        fill(outs[frames + 1 + m], (q_in, do_in, k_in, v_in, k2_in, v2_in), me ^ m, 1, extra)
-    fill(outs[frames], (None, None, k2_in, v2_in), me, 0, full)
-    outs[frames][:, 4 * full * DH :] = t_ref[rest, :]
-
-
-def pack(tables, frames, full, extra, fq, do, fk, fv, t):
+    for out, parts in zip(outs, outputs):
+        at = 0
+        for table, m, what in parts:
+            if what in ("t", "other t"):
+                blocks = [t_ref[mine if what == "t" else rest, :]]
+            else:
+                cols = column(lookup(table, me ^ m))
+                sources = (q_in, do_in, k_in, v_in) if what == "mine" else (k2_in, v2_in)
+                blocks = [ref[:, cols] for ref in sources]
+            for block in blocks:
+                out[:, at : at + block.shape[1]] = block
+                at += block.shape[1]
+
+
+def pack(frames, outputs, limit, fq, do, fk, fv, t):
     rows, width = fq.shape
-    first = jax.ShapeDtypeStruct((rows, 4 * DH * full + t.shape[1]), BF16)
-    second = jax.ShapeDtypeStruct((rows, 6 * DH * extra), BF16)
+    size = {"mine": 4 * DH, "other": 2 * DH, "t": t.shape[1], "other t": t.shape[1]}
     anywhere = pl.BlockSpec(memory_space=pl.ANY)
     return pl.pallas_call(
-        functools.partial(pack_kernel, tables, frames, full, extra),
+        functools.partial(pack_kernel, frames, outputs),
         in_specs=[anywhere] * 4 + vmem(1),
-        out_specs=vmem(2 * frames + 1),
-        out_shape=[first] * (frames + 1) + [second] * frames,
+        out_specs=vmem(len(outputs)),
+        out_shape=[
+            jax.ShapeDtypeStruct((rows, sum(size[what] for _, _, what in parts)), BF16)
+            for parts in outputs
+        ],
         scratch_shapes=[pltpu.VMEM((rows, width), BF16)] * 6 + [pltpu.SemaphoreType.DMA((6,))],
-        compiler_params=pltpu.CompilerParams(vmem_limit_bytes=56 * 1024 * 1024),
+        compiler_params=pltpu.CompilerParams(vmem_limit_bytes=limit * 1024 * 1024),
     )(fq, do, fk, fv, t)
 
 
-def one_head(frames, bands, q, do, frozen_k, frozen_v, t_same, t_other, aq, ak, av):
-    flat = t_same.shape[0]
+def pick_kernel(spans, *refs):
+    out, at = refs[-1], 0
+    for n, (start, size) in enumerate(spans):
+        out[:, at : at + size] = refs[n][:, start : start + size]
+        at += size
+
+
+def pick(parts, size, after=()):
+    arrays = [array for array, _ in parts]
+    return pl.pallas_call(
+        functools.partial(pick_kernel, [(start, size) for _, start in parts]),
+        in_specs=vmem(len(arrays)) + [pl.BlockSpec(memory_space=pl.ANY)] * len(after),
+        out_specs=pl.BlockSpec(memory_space=pltpu.VMEM),
+        out_shape=jax.ShapeDtypeStruct((arrays[0].shape[0], size * len(parts)), arrays[0].dtype),
+        compiler_params=SMALL,
+    )(*arrays, *after)
+
+
+def one_head(frames, bands, q, do, frozen_k, frozen_v, tokens, aq, ak, av):
+    flat = q.shape[0]
     rows = flat // frames
-    tokens = jnp.concatenate([t_same, t_other], axis=0)
+    t_same = tokens[:flat]
 
     def adapted(frozen, rows_of, adapter):
         return (frozen.astype(F32) + dot_nn(rows_of, adapter)).astype(BF16)
@@ -381,7 +398,7 @@
     return grads, lows[:flat] + dot_nt(dq, aq), lows[flat:]
 
 
-def group_kernel(tables, frames, counts, chained, *refs):
+def group_kernel(heads, frames, chained, waits, sides, count, *refs):
     refs = list(refs)
 
     def take(count):
@@ -390,137 +407,117 @@
         return taken
 
     (bands,) = take(1)
-    mine = take(frames)
-    others = mine if chained else take(frames)
-    if chained:
-        take(1)
-        t_mine, t_others = take(frames), take(frames)
-    adapters = take(3)
-    before = take(2) if chained else [None, None]
+    arrays, adapters = take(count), take(3)
+    before = take(2) if chained else None
+    take(waits)
     keep_ref, *give_refs = take(3 if chained else 2)
     low_refs = [] if chained else take(2)
-    same, other, t_same, t_other = refs
+    q, do, k, v, tokens = refs
     me, half = lax.axis_index("tm"), lax.axis_index("rep")
-    rows = mine[0].shape[0]
-    cut = 3 * t_same.shape[1] // 2
-    slots = len(tables)
-    main = 4 * slots * DH
-    wide = slots * DH
-
-    def give_out(gives):
-        whole = jnp.concatenate(gives, axis=0)
-        size = whole.shape[0] // len(give_refs)
+    rows = arrays[0].shape[0]
+    flat = frames * rows
+    cut = 3 * tokens.shape[1] // 2
+    first = half == 0
+    same_at = [pl.ds(pl.multiple_of((me ^ m) * rows, rows), rows) for m in range(frames)]
+    other_at = [pl.ds(pl.multiple_of(flat + (me ^ m) * rows, rows), rows) for m in range(frames)]
+
+    def put(targets, places, rows_at):
+        for m, (n, start) in enumerate(places):
+            for c, target in enumerate(targets):
+                target[rows_at[m], :] = arrays[n][:, start + c * DH : start + (c + 1) * DH]
+
+    put([tokens], sides[0][0], same_at)
+    put([tokens], sides[0][1], other_at)
+
+    def run(n, table):
+        put([q, do, k, v], sides[1 + n][0], same_at)
+        put([k, v], sides[1 + n][1], other_at)
+        cols = column(lookup(table, me))
+        grads, low_same, low_other = one_head(
+            frames, bands, q[...], do[...], k[...], v[...], tokens[...], *[a[:, cols] for a in adapters]
+        )
+        keep = jnp.where(first, grads[:cut], grads[cut:])
+        give = jnp.where(first, grads[cut:], grads[:cut])
+        return keep, give, low_same, low_other
+
+    if chained:
+        keep, give, low_same, low_other = run(0, heads[0][0])
+        keep_ref[:cut, :] = keep
+        keep_ref[cut:, :] = before[0][...] + low_same
+        give = jnp.concatenate([give, before[1][...] + low_other], axis=0)
+        size = give.shape[0] // 2
         for n, ref in enumerate(give_refs):
-            ref[...] = whole[n * size : (n + 1) * size].astype(ref.dtype)
-
-    def body():
-        for m in range(frames):
-            at = pl.ds(pl.multiple_of((me ^ m) * rows, rows), rows)
-            same[at, :] = mine[m][:, :main]
-            start = main if chained else main // 2
-            other[at, :] = others[m][:, start : start + main // 2]
-            t_same[at, :] = t_mine[m][...] if chained else mine[m][:, main:]
-            t_other[at, :] = t_others[m][...] if chained else others[m][:, main:]
-        gives = []
-        total_same, total_other = [None if ref is None else ref[...] for ref in before]
-        for s, table in enumerate(tables):
-            cols = column(lookup(table, me))
-
-            def part(c):
-                return slice(c * wide + s * DH, c * wide + (s + 1) * DH)
-
-            grads, low_same, low_other = one_head(
-                frames, bands, same[:, part(0)], same[:, part(1)],
-                jnp.concatenate([same[:, part(2)], other[:, part(0)]], axis=0),
-                jnp.concatenate([same[:, part(3)], other[:, part(1)]], axis=0),
-                t_same[...], t_other[...], *[ref[:, cols] for ref in adapters],
-            )
-            first = half == 0
-            keep_ref[s * cut : (s + 1) * cut, :] = jnp.where(first, grads[:cut], grads[cut:])
-            gives.append(jnp.where(first, grads[cut:], grads[:cut]))
-            total_same = low_same if total_same is None else total_same + low_same
-            total_other = low_other if total_other is None else total_other + low_other
-        if chained:
-            keep_ref[slots * cut :, :] = total_same
-            gives.append(total_other)
-        give_out(gives)
-        if not chained:
-            low_refs[0][...] = total_same
-            low_refs[1][...] = total_other
-
-    if min(counts) > 0:
-        body()
+            ref[...] = give[n * size : (n + 1) * size].astype(ref.dtype)
+        return
+    for n, (table, counts) in enumerate(heads):
+        here = slice(n * cut, (n + 1) * cut)
+
+        def body():
+            keep, give, low_same, low_other = run(n, table)
+            keep_ref[here, :] = keep
+            give_refs[0][here, :] = give.astype(BF16)
+            if n == 0:
+                low_refs[0][...] = low_same
+                low_refs[1][...] = low_other
+            else:
+                low_refs[0][...] += low_same
+                low_refs[1][...] += low_other
+
+        if min(counts) > 0:
+            body()
+        else:
+            live = lookup(counts, me) > 0
+            pl.when(live)(body)
+
+            @pl.when(jnp.logical_not(live))
+            def _():
+                keep_ref[here, :] = jnp.zeros((cut, DH), F32)
+                give_refs[0][here, :] = jnp.zeros((cut, DH), BF16)
+
+
+def head_group(heads, bands, sides, adapters, before=(), after=()):
+    frames = len(sides[0][0])
+    arrays, places = [], []
+    for side in sides:
+        found = []
+        for pairs_of in side:
+            found.append([])
+            for array, start in pairs_of:
+                known = [n for n, a in enumerate(arrays) if a is array]
+                if not known:
+                    arrays.append(array)
+                found[-1].append((known[0] if known else len(arrays) - 1, start))
+        places.append(found)
+    rows, rank = arrays[0].shape[0], adapters[0].shape[0]
+    flat = frames * rows
+    size = len(heads) * 3 * rank // 2
+    chained = len(before) > 0
+    args = [bands, *arrays, *adapters, *before, *after]
+    specs = [pl.BlockSpec(memory_space=pltpu.SMEM)] + vmem(len(arrays) + 3 + len(before))
+    specs += [pl.BlockSpec(memory_space=pl.ANY)] * len(after)
+    low = jax.ShapeDtypeStruct((flat, rank), F32)
+    if chained:
+        half = jax.ShapeDtypeStruct(((size + flat) // 2, rank), BF16)
+        shapes = [jax.ShapeDtypeStruct((size + flat, rank), F32), half, half]
     else:
-        live = lookup(counts, me) > 0
-        pl.when(live)(body)
-
-        @pl.when(jnp.logical_not(live))
-        def _():
-            zeros = jnp.zeros((slots * cut, DH), F32)
-            keep_ref[: slots * cut, :] = zeros
-            keep_ref[slots * cut :, :] = before[0][...]
-            give_out([zeros, before[1][...]])
-
-
-def head_group(tables, counts, bands, mine, others, adapters, before=None, after=None):
-    frames, rows = len(mine), mine[0].shape[0]
-    rank = adapters[0].shape[0]
-    slots = len(tables)
-    flat = frames * rows
-    size = slots * 3 * rank // 2
-    main = 4 * slots * DH
-    chained = before is not None
-    args = [bands, *mine, *([after] if chained else []), *others, *adapters]
-    specs = [pl.BlockSpec(memory_space=pltpu.SMEM)] + vmem(frames)
-    if chained:
-        specs.append(pl.BlockSpec(memory_space=pl.ANY))
-    if chained:
-        col = others[0].shape[1] // rank - 1
-        specs += [pl.BlockSpec((rows, rank), lambda n: (0, col))] * len(others) + vmem(3 + len(before))
-        args += before
-    else:
-        specs += vmem(len(others) + 3)
-    low = jax.ShapeDtypeStruct((flat, rank), F32)
-    edge = jax.ShapeDtypeStruct((size + (flat if chained else 0), rank), F32)
-    if chained:
-        shapes = [edge] + [jax.ShapeDtypeStruct((edge.shape[0] // 2, rank), BF16)] * 2
-    else:
-        shapes = [edge, edge, low, low]
+        edge = jax.ShapeDtypeStruct((size, rank), F32)
+        shapes = [edge, jax.ShapeDtypeStruct((size, rank), BF16), low, low]
     return pl.pallas_call(
-        functools.partial(group_kernel, tables, frames, counts, chained),
-        grid=(1,),
+        functools.partial(
+            group_kernel, heads, frames, chained, len(after), places, len(arrays)
+        ),
         in_specs=specs,
         out_specs=vmem(len(shapes)),
         out_shape=shapes,
-        scratch_shapes=[
-            pltpu.VMEM((flat, main), BF16),
-            pltpu.VMEM((flat, main // 2), BF16),
-            pltpu.VMEM((flat, rank), BF16),
-            pltpu.VMEM((flat, rank), BF16),
-        ],
+        scratch_shapes=[pltpu.VMEM((flat, DH), BF16)] * 2
+        + [pltpu.VMEM((2 * flat, DH), BF16)] * 2
+        + [pltpu.VMEM((2 * flat, rank), BF16)],
         compiler_params=pltpu.CompilerParams(vmem_limit_bytes=40 * 1024 * 1024),
-        cost_estimate=pl.CostEstimate(
-            flops=4 * slots * 16 * 2 * DH * flat * 2 * flat,
-            transcendentals=slots * flat * 2 * flat,
-            bytes_accessed=8 * slots * flat * DH * 2,
-        ),
     )(*args)
 
 
-def gate(block, after):
-    anywhere = pl.BlockSpec(memory_space=pl.ANY)
-    return pl.pallas_call(
-        lambda *refs: None,
-        in_specs=[anywhere] * (1 + len(after)),
-        out_specs=anywhere,
-        out_shape=jax.ShapeDtypeStruct(block.shape, block.dtype),
-        input_output_aliases={0: 0},
-        compiler_params=SMALL,
-    )(block, *after)
-
-
-def hand_out_kernel(frames, size, parts, waits, keep_ref, *refs):
-    gots, (own_ref, *sends, total) = refs[:parts], refs[parts + waits :]
+def hand_out_kernel(frames, size, parts, keep_ref, *refs):
+    gots, pieces, (stack, own_ref, *sends, total) = refs[:parts], refs[parts : parts + frames], refs[parts + frames :]
     me = lax.axis_index("tm")
     rows = own_ref.shape[0]
     total[...] = keep_ref[...] + jnp.concatenate([got[...].astype(F32) for got in gots], axis=0)
@@ -531,50 +528,59 @@
             own_ref[...] = low
         sends[m][:rows, :] = low.astype(BF16)
         sends[m][rows:, :] = grads
-
-
-def hand_out(frames, rows, keep, gots, after):
+        high = pieces[m].shape[0]
+        stack[m * high : (m + 1) * high, :] = pieces[m][...]
+
+
+def hand_out(rows, keep, gots, pieces):
+    frames = len(pieces)
     size, rank = keep.shape[0] - frames * rows, keep.shape[1]
     send = jax.ShapeDtypeStruct((rows + size, rank), BF16)
     return pl.pallas_call(
-        functools.partial(hand_out_kernel, frames, size, len(gots), len(after)),
-        in_specs=vmem(1 + len(gots)) + [pl.BlockSpec(memory_space=pl.ANY)] * len(after),
-        out_specs=vmem(frames + 1),
-        out_shape=[jax.ShapeDtypeStruct((rows, rank), F32)] + [send] * frames,
+        functools.partial(hand_out_kernel, frames, size, len(gots)),
+        in_specs=vmem(1 + len(gots) + frames),
+        out_specs=vmem(frames + 2),
+        out_shape=[
+            jax.ShapeDtypeStruct((frames * pieces[0].shape[0], rank), BF16),
+            jax.ShapeDtypeStruct((rows, rank), F32),
+        ]
+        + [send] * frames,
         scratch_shapes=[pltpu.VMEM(keep.shape, F32)],
         compiler_params=SMALL,
-    )(keep, *gots, *after)
+    )(keep, *gots, *pieces)
 
 
 def collect_kernel(frames, own_ref, *refs):
-    gots, out_ref = refs[:-1], refs[-1]
+    gots, (out_ref, low_ref) = refs[:frames], refs[-2:]
     rows = own_ref.shape[0]
     size = gots[0].shape[0] - rows
     low = own_ref[...]
     for m in range(1, frames):
         low = low + gots[m][:rows, :].astype(F32)
     out_ref[:rows, :] = low.astype(BF16)
+    low_ref[...] = low.astype(BF16)
     for m in range(frames):
         out_ref[rows + m * size : rows + (m + 1) * size, :] = gots[m][rows:, :]
 
 
-def collect(own, gots):
+def collect(own, gots, after):
     frames, (rows, rank) = len(gots), own.shape
     size = gots[0].shape[0] - rows
     return pl.pallas_call(
         functools.partial(collect_kernel, frames),
-        in_specs=vmem(frames + 1),
-        out_specs=pl.BlockSpec(memory_space=pltpu.VMEM),
-        out_shape=jax.ShapeDtypeStruct((rows + frames * size, rank), BF16),
+        in_specs=vmem(frames + 1) + [pl.BlockSpec(memory_space=pl.ANY)] * len(after),
+        out_specs=vmem(2),
+        out_shape=[
+            jax.ShapeDtypeStruct((rows + frames * size, rank), BF16),
+            jax.ShapeDtypeStruct((rows, rank), BF16),
+        ],
         compiler_params=SMALL,
-    )(own, *gots)
-
-
-def place_kernel(table, counts, full, *refs):
-    frames = len(table)
-    mine, others = refs[:frames], refs[frames : 2 * frames]
-    tail, tail2, low_head, low_diag = refs[2 * frames : 2 * frames + 4]
-    outs = refs[2 * frames + 4 :]
+    )(own, *gots, *after)
+
+
+def place_kernel(early, late, *refs):
+    frames = len(late[0])
+    stack, stack2, tail, tail2, low_head, low_diag, *outs = refs
     me, half = lax.axis_index("tm"), lax.axis_index("rep")
     first = half == 0
     rank = outs[0].shape[0]
@@ -586,37 +592,35 @@
     outs[3][rows:, :] = jnp.where(first, other, same)
     for m in range(frames):
         chip = me ^ m
-        for s in range(len(table[0])):
-            if s < full:
-                a, b = mine[m][s * cut : (s + 1) * cut, :], others[m][s * cut : (s + 1) * cut, :]
-            else:
-                at = rows + (m * (len(table[0]) - full) + s - full) * cut
-                a, b = tail[at : at + cut, :], tail2[at : at + cut, :]
-            a, b = a.astype(F32), b.astype(F32)
-
-            def write():
-                cols = column(lookup([row[s] for row in table], chip))
+
+        def write(head, a_ref, b_ref, at):
+            def body():
+                a, b = a_ref[at : at + cut, :].astype(F32), b_ref[at : at + cut, :].astype(F32)
+                cols = column(lookup(head[0], chip))
                 both = jnp.concatenate([jnp.where(first, a, b), jnp.where(first, b, a)], axis=0)
                 for o in range(3):
                     outs[o][:, cols] = both[o * rank : (o + 1) * rank]
 
-            if s < full:
-                write()
+            if min(head[1]) > 0:
+                body()
             else:
-                pl.when(lookup(counts, chip) > s)(write)
-
-
-def place(table, counts, mine, others, tail, tail2, low_head, low_diag, rank, width):
+                pl.when(lookup(head[1], chip) > 0)(body)
+
+        for n, head in enumerate(early):
+            write(head, stack, stack2, (m * len(early) + n) * cut)
+        write(late, tail, tail2, rows + m * cut)
+
+
+def place(early, late, stack, stack2, tail, tail2, low_head, low_diag, rank, width):
     rows = low_head.shape[0]
-    full = min(counts)
     return pl.pallas_call(
-        functools.partial(place_kernel, table, counts, full),
-        in_specs=vmem(2 * len(table) + 4),
+        functools.partial(place_kernel, early, late),
+        in_specs=vmem(6),
         out_specs=vmem(4),
         out_shape=[jax.ShapeDtypeStruct((rank, width), F32)] * 3
         + [jax.ShapeDtypeStruct((2 * rows, rank), F32)],
         compiler_params=SMALL,
-    )(*mine, *others, tail, tail2, low_head, low_diag)
+    )(stack, stack2, tail, tail2, low_head, low_diag)
 
 
 def exchange_plan(
@@ -635,9 +639,11 @@
     frames = band_width.shape[0]
     heads = width // DH
     starts, counts = head_table(heads, frames)
-    full, most = min(counts), max(counts)
-    table = [[min(starts[j] + s, heads - 1) for s in range(most)] for j in range(frames)]
-    columns = [[row[s] for row in table] for s in range(most)]
+    most = max(counts)
+    columns = [[min(starts[j] + s, heads - 1) for j in range(frames)] for s in range(most)]
+    numbers = [[int(s < counts[j]) for j in range(frames)] for s in range(most)]
+    slots = list(zip(columns, numbers))
+    lead, late, rest = slots[0], slots[1], slots[2]
     wide = [j for j in range(frames) if counts[j] == most]
     adapters = [query_adapter_out, key_adapter_out, value_adapter_out]
     arrays = (frozen_query, out_grad, frozen_key, frozen_value, token_adapter_input)
@@ -645,29 +651,57 @@
     def meet(block, m, targets=range(frames)):
         return lax.ppermute(block, "tm", [(j ^ m, j) for j in targets])
 
-    extra = most - full
-    tables = (columns[0], [min(h, heads - extra) for h in columns[full]])
-    packed = pack(tables, frames, full, extra, *arrays)
-    mine = [packed[0]] + [meet(packed[m], m) for m in range(1, frames)]
-    packed2 = packed[frames + 1 :]
-    mine2 = [packed2[0]] + [meet(packed2[m], m, wide) for m in range(1, frames)]
-    others = [packed[frames]] + [swap(block, "rep") for block in mine[1:]]
-    keep, give, *low = head_group(columns[:full], counts, band_width, mine, others, adapters)
-    piece = (keep + swap(gate(give, mine2[1:]), "rep")).astype(BF16)
+    def mine(slot, m):
+        return (slot[0], m, "mine")
+
+    sent, kept, sent_late = [], [], []
+    for m in range(1, frames):
+        first = [mine(lead, m), (None, m, "t")]
+        if m == 1:
+            sent.append(first + [mine(rest, m), mine(late, m)])
+        else:
+            sent += [first, [mine(rest, m)]]
+            sent_late.append([mine(late, m)])
+    for slot in (lead, rest, late):
+        kept += [[mine(slot, 0)], [(slot[0], 0, "other")]]
+    kept += [[(None, 0, "t")], [(None, 0, "other t")]]
+    packed = pack(frames, sent, 56, *arrays)
+    packed_late = pack(frames, sent_late + kept, 16, *arrays)
+    kept = packed_late[len(sent_late) :]
+    block = meet(packed[0], 1)
+    lead_got, rest_got, late_got = [(block, 0)], [(block, 4 * DH + rank)], [(block, 8 * DH + rank)]
+    for m in range(2, frames):
+        lead_got.append((meet(packed[2 * m - 3], m), 0))
+        rest_got.append((meet(packed[2 * m - 2], m, wide), 0))
+        late_got.append((meet(packed_late[m - 2], m), 0))
+
+    def sides(n, got, wide_t, after=()):
+        size = 2 * DH + (rank if wide_t else 0)
+        cross = swap(pick([(a, start + 2 * DH) for a, start in got], size, after), "rep")
+        rows_here = [(kept[2 * n], 0)] + got
+        rows_there = [(kept[2 * n + 1], 0)] + [(cross, m * size) for m in range(frames - 1)]
+        return rows_here, rows_there, cross
+
+    *lead_side, cross = sides(0, lead_got, True, kept[:1])
+    t_side = (
+        [(kept[6], 0)] + [(a, start + 4 * DH) for a, start in lead_got],
+        [(kept[7], 0)] + [(cross, m * (2 * DH + rank) + 2 * DH) for m in range(frames - 1)],
+    )
+    *rest_side, _ = sides(1, rest_got, False)
+    early = [lead, rest]
+    keep, give, *low = head_group(early, band_width, [t_side, lead_side, rest_side], adapters)
+    *late_side, _ = sides(2, late_got, False, [give])
+    piece = (keep + swap(give, "rep").astype(F32)).astype(BF16)
     pieces = [piece] + [meet(piece, m) for m in range(1, frames)]
-    pieces2 = [swap(block, "rep") for block in pieces]
-    keep, *gives = head_group(
-        columns[full:], [c - full for c in counts], band_width, mine2, mine + others, adapters,
-        low, piece,
-    )
-    own, *sends = hand_out(frames, rows, keep, [swap(g, "rep") for g in gives], pieces[1:])
+    keep, *gives = head_group([late], band_width, [t_side, late_side], adapters, low, [piece])
+    stack, own, *sends = hand_out(rows, keep, [swap(g, "rep") for g in gives], pieces)
+    stack2 = swap(stack, "rep")
     gots = [sends[0]] + [meet(sends[m], m) for m in range(1, frames)]
-    tail = collect(own, gots)
-    low = tail[:rows]
+    tail, low = collect(own, gots, [stack2])
     diag = [(0, 3), (1, 2), (2, 1), (3, 0)]
+    low_head, low_diag = swap(low, "head"), lax.ppermute(low, ("head", "rep"), diag)
     outs = place(
-        table, counts, pieces, pieces2, tail, swap(tail, "rep"), swap(low, "head"),
-        lax.ppermute(low, ("head", "rep"), diag), rank, width,
+        early, late, stack, stack2, tail, swap(tail, "rep"), low_head, low_diag, rank, width
     )
     return tuple(outs)
 
@@ -675,7 +709,7 @@
 def on_device(frozen_query, *rest):
     frames = rest[-1].shape[0]
     heads = frozen_query.shape[1] // DH
-    whole_reach = frames <= REACH + 1 and frames & (frames - 1) == 0 and heads > frames and heads % frames
+    whole_reach = frames <= REACH + 1 and frames & (frames - 1) == 0 and 2 * frames < heads < 3 * frames
     return (exchange_plan if whole_reach else window_plan)(frozen_query, *rest)
 
 

time: 83.7 us -> 72.9 us (0.87)
  waiting for transfers between devices: 38.5 us -> 29.5 us
  local copies, waits for them, and re-layouts: 1.94 us -> 0.69 us
  starting transfers between devices: 28.8 us -> 27.7 us
    ppermute x12 -> x13, waiting for transfers between devices: 32.4 us -> 26.1 us  [meet(): return lax.ppermute(block, 'tm', [(j ^ m, j) for j in targets])]
    ppermute x12 -> x9, waiting for transfers between devices: 4.55 us -> 2.14 us  [swap(): return lax.ppermute(block, axis, [(0, 1), (1, 0)])]
    unnamed x14 -> x18, local copies, waits for them, and re-layouts: 1.94 us -> 0.69 us
    ppermute x12 -> x9, starting transfers between devices: 3.06 us -> 2.07 us  [swap(): return lax.ppermute(block, axis, [(0, 1), (1, 0)])]
    pallas_call x5 -> x8, Pallas kernels: 13.3 us -> 13.8 us  [the longest x2 7.78 us: head_group(): pl.pallas_call(functools.partial(group_kernel, heads, frames, chained, le...]
    ppermute x12 -> x13, starting transfers between devices: 24.4 us -> 24 us  [meet(): return lax.ppermute(block, 'tm', [(j ^ m, j) for j in targets])]
  transfers between devices with their start and end apart: 25 -> 23, of which waited for: 12 -> 8; matrix products, arithmetic and copies ran while one was open for 0% -> 0% of each run, Pallas kernels for 9% -> 12%
where the time goes in v6:
time: 72.9 us; the launch traced here: 72.7 us
  waiting for transfers between devices  29.5 us (40%)
  starting transfers between devices  27.7 us (38%)
  Pallas kernels  13.9 us (19%)
  between operations  0.93 us (1%)
    ppermute x13, waiting for transfers between devices, meet(): return lax.ppermute(block, 'tm', [(j ^ m, j) for j in targets])  26.1 us
    ppermute x13, starting transfers between devices, meet(): return lax.ppermute(block, 'tm', [(j ^ m, j) for j in targets])  24 us
    pallas_call x2, Pallas kernels, head_group(): pl.pallas_call(functools.partial(group_kernel, heads, frames, chained, le...  7.78 us
    pallas_call x2, Pallas kernels, pack(): pl.pallas_call(functools.partial(pack_kernel, frames, outputs), in_specs=...  4.44 us
    ppermute x9, waiting for transfers between devices, swap(): return lax.ppermute(block, axis, [(0, 1), (1, 0)])  2.14 us
    ppermute x9, starting transfers between devices, swap(): return lax.ppermute(block, axis, [(0, 1), (1, 0)])  2.07 us
    ppermute x1, starting transfers between devices, exchange_plan(): lax.ppermute(low, ('head', 'rep'), diag)  1.61 us
    pallas_call x1, Pallas kernels, place(): pl.pallas_call(functools.partial(place_kernel, early, late), in_specs=vme...  1.49 us
  transfers between devices with their start and end apart: 23, of which 8 were waited for; matrix products, arithmetic and copies ran while one was open for 0% of the time, Pallas kernels for 12%

profile of v6, /device:TPU:0, one launch (start us, length us, event | category | flops | bytes accessed | tf_op | source)
XLA Modules:
  0.0 72.7 jit_solution(15144291869024489356)
XLA Ops:
  0.7 3.6 %shard_map.121 = (bf16[128,1664]{1,0:T(8,128)(2,1)}, bf16[128,640]{1,0:T(8,128)(2,1)}, bf16[128,512]{1,0:T(8,128)(2,1)}, bf16[128,640]{1,0:T(8,128)(2,1)}, bf16[128,512]{1,0:T(8,128)(2,1)}) custom-call(bf16[128,1280]{1,0:T(8,128)(2,1)} %fq_ref.3, bf16[128,1280]{1,0:T(8,128)(2,1)} %do_ref.3, bf16[256,1280]{1,0:T(8,128)(2,1)} %fk_ref.3, ...), custom_call_target="tpu_custom_call" | custom-call | tf_op jit(solution)/shard_map/pallas_call | solution.py:299
  4.3 3.1 %collective-permute-start = (bf16[128,1664]{1,0:T(8,128)(2,1)}, bf16[128,1664]{1,0:T(8,128)(2,1)S(1)}, u32[]{:S(2)}, u32[]{:S(2)}) collective-permute-start(bf16[128,1664]{1,0:T(8,128)(2,1)} %get-tuple-element.35), channel_id=1, source_target_pairs={{4,0},{0,4},{12,8},{8,12},{5,1},{1,5},{13,9},{9,13},{6,2},{2,6},{1... | collective-permute-start | bytes 1277960 | tf_op jit(solution)/shard_map/ppermute | solution.py:652
  7.4 2.6 %collective-permute-start.1 = (bf16[128,640]{1,0:T(8,128)(2,1)}, bf16[128,640]{1,0:T(8,128)(2,1)S(1)}, u32[]{:S(2)}, u32[]{:S(2)}) collective-permute-start(bf16[128,640]{1,0:T(8,128)(2,1)} %get-tuple-element.36), channel_id=1, source_target_pairs={{8,0},{12,4},{0,8},{4,12},{9,1},{13,5},{1,9},{5,13},{10,2},{14,6},... | collective-permute-start | bytes 491528 | tf_op jit(solution)/shard_map/ppermute | solution.py:652
  10.0 3.8 %collective-permute-start.6 = (bf16[128,512]{1,0:T(8,128)(2,1)}, bf16[128,512]{1,0:T(8,128)(2,1)S(1)}, u32[]{:S(2)}, u32[]{:S(2)}) collective-permute-start(bf16[128,512]{1,0:T(8,128)(2,1)} %get-tuple-element.46), channel_id=1, source_target_pairs={{12,4},{0,8},{13,5},{1,9},{14,6},{2,10},{15,7},{3,11},{28,20},{16,... | collective-permute-start | bytes 393224 | tf_op jit(solution)/shard_map/ppermute | solution.py:652
  13.8 0.7 collective-permute-start.7
  14.5 0.9 %shard_map.120 = (bf16[128,512]{1,0:T(8,128)(2,1)S(1)}, bf16[128,512]{1,0:T(8,128)(2,1)S(1)}, bf16[128,512]{1,0:T(8,128)(2,1)S(1)}, bf16[128,256]{1,0:T(8,128)(2...) custom-call(bf16[128,1280]{1,0:T(8,128)(2,1)S(1)} %copy-done.2, ...), custom_call_target="tpu_custom_call" | custom-call | tf_op jit(solution)/shard_map/pallas_call | solution.py:299
  15.4 6.1 %collective-permute-done.1.refs_1_.refs_3_ = bf16[128,640]{1,0:T(8,128)(2,1)S(1)} collective-permute-done((bf16[128,640]{1,0:T(8,128)(2,1)}, bf16[128,640]{1,0:T(8,128)(2,1)S(1)}, u32[]{:S(2)}, u32[]{:S(2)}) %collective-permute-start.1) | collective-permute-done | bytes 163872 | tf_op jit(solution)/shard_map/ppermute | solution.py:652
  21.5 6.4 %collective-permute-done.2.refs_2_.refs_4_ = bf16[128,640]{1,0:T(8,128)(2,1)S(1)} collective-permute-done((bf16[128,640]{1,0:T(8,128)(2,1)}, bf16[128,640]{1,0:T(8,128)(2,1)S(1)}, u32[]{:S(2)}, u32[]{:S(2)}) %collective-permute-start.2) | collective-permute-done | bytes 163872 | tf_op jit(solution)/shard_map/ppermute | solution.py:652
  28.0 0.5 collective-permute-start.8
  28.6 3.5 %collective-permute-start.4 = (bf16[128,512]{1,0:T(8,128)(2,1)S(1)}, bf16[128,512]{1,0:T(8,128)(2,1)S(1)}, u32[]{:S(2)}, u32[]{:S(2)}) collective-permute-start(bf16[128,512]{1,0:T(8,128)(2,1)S(1)} %get-tuple-element.41), channel_id=1, source_target_pairs={{8,0},{12,4},{0,8},{4,12},{9,1},{13,5},{1,9},{5,13},{10,2},{14,6},... | collective-permute-start | bytes 393224 | tf_op jit(solution)/shard_map/ppermute | solution.py:652
  32.1 1.4 %collective-permute-start.5 = (bf16[128,512]{1,0:T(8,128)(2,1)S(1)}, bf16[128,512]{1,0:T(8,128)(2,1)S(1)}, u32[]{:S(2)}, u32[]{:S(2)}) collective-permute-start(bf16[128,512]{1,0:T(8,128)(2,1)S(1)} %get-tuple-element.42), channel_id=1, source_target_pairs={{12,0},{8,4},{4,8},{0,12},{13,1},{9,5},{5,9},{1,13},{14,2},{10,6},... | collective-permute-start | bytes 393224 | tf_op jit(solution)/shard_map/ppermute | solution.py:652
  33.5 0.6 copy-done.8
  34.1 3.9 %shard_map.124 = (f32[384,128]{1,0:T(8,128)S(1)}, bf16[384,128]{1,0:T(8,128)(2,1)S(1)}, f32[512,128]{1,0:T(8,128)S(1)}, f32[512,128]{1,0:T(8,128)S(1)}) custom-call(s32[4,4]{1,0:T(4,128)S(1)} %copy-done.8, bf16[128,128]{1,0:T(8,128)(2,1)S(1)} %get-tuple-element.34.refs_1_, bf16[128,1664]{1,0:T(8,128)(2,1)S(1)} %collective-permute-done.refs_0_.refs_2_, ...), custom_call_target="tpu_custom_call" | custom-call | tf_op jit(solution)/shard_map/pallas_call | solution.py:505
  38.1 3.9 %collective-permute-done.4.refs_1_.refs_8_ = bf16[128,512]{1,0:T(8,128)(2,1)S(1)} collective-permute-done((bf16[128,512]{1,0:T(8,128)(2,1)S(1)}, bf16[128,512]{1,0:T(8,128)(2,1)S(1)}, u32[]{:S(2)}, u32[]{:S(2)}) %collective-permute-start.4) | collective-permute-done | bytes 131104 | tf_op jit(solution)/shard_map/ppermute | solution.py:652
  42.1 0.1 collective-permute-start.9
  42.2 1.4 %collective-permute-start.15 = (bf16[384,128]{1,0:T(8,128)(2,1)S(1)}, bf16[384,128]{1,0:T(8,128)(2,1)S(1)}, u32[]{:S(2)}, u32[]{:S(2)}) collective-permute-start(bf16[384,128]{1,0:T(8,128)(2,1)S(1)} %add_convert_fusion.refs_17_.refs_2_), channel_id=1, source_target_pairs={{12,0},{8,4},{4,8},{0,12},{13,1},{9,5},{5,9},{1,13},{14,2},{10,6},... | collective-permute-start | bytes 294920 | tf_op jit(solution)/shard_map/ppermute | solution.py:652
  43.6 3.2 %collective-permute-start.14 = (bf16[384,128]{1,0:T(8,128)(2,1)S(1)}, bf16[384,128]{1,0:T(8,128)(2,1)S(1)}, u32[]{:S(2)}, u32[]{:S(2)}) collective-permute-start(bf16[384,128]{1,0:T(8,128)(2,1)S(1)} %add_convert_fusion.refs_17_.refs_2_), channel_id=1, source_target_pairs={{8,0},{12,4},{0,8},{4,12},{9,1},{13,5},{1,9},{5,13},{10,2},{14,6},... | collective-permute-start | bytes 294920 | tf_op jit(solution)/shard_map/ppermute | solution.py:652
  46.8 3.9 %shard_map.126 = (f32[704,128]{1,0:T(8,128)S(1)}, bf16[352,128]{1,0:T(8,128)(2,1)S(1)}, bf16[352,128]{1,0:T(8,128)(2,1)S(1)}) custom-call(s32[4,4]{1,0:T(4,128)S(1)} %copy-done.8, bf16[128,128]{1,0:T(8,128)(2,1)S(1)} %get-tuple-element.34.refs_1_, bf16[128,1664]{1,0:T(8,128)(2,1)S(1)} %collective-permute-done.refs_0_.refs_2_, ...), custom_call_target="tpu_custom_call" | custom-call | tf_op jit(solution)/shard_map/pallas_call | solution.py:505
  50.7 0.1 collective-permute-start.11
  50.8 0.5 collective-permute-start.12
  51.3 4.3 %collective-permute-done.14.refs_4_ = bf16[384,128]{1,0:T(8,128)(2,1)S(1)} collective-permute-done((bf16[384,128]{1,0:T(8,128)(2,1)S(1)}, bf16[384,128]{1,0:T(8,128)(2,1)S(1)}, u32[]{:S(2)}, u32[]{:S(2)}) %collective-permute-start.14) | collective-permute-done | bytes 98336 | tf_op jit(solution)/shard_map/ppermute | solution.py:652
  55.6 0.1 shard_map.127
  55.7 0.1 collective-permute-start.16
  55.8 1.9 %collective-permute-start.18 = (bf16[320,128]{1,0:T(8,128)(2,1)S(1)}, bf16[320,128]{1,0:T(8,128)(2,1)S(1)}, u32[]{:S(2)}, u32[]{:S(2)}) collective-permute-start(bf16[320,128]{1,0:T(8,128)(2,1)S(1)} %get-tuple-element.60), channel_id=1, source_target_pairs={{8,0},{12,4},{0,8},{4,12},{9,1},{13,5},{1,9},{5,13},{10,2},{14,6},... | collective-permute-start | bytes 245768 | tf_op jit(solution)/shard_map/ppermute | solution.py:652
  57.7 2.5 %collective-permute-start.19 = (bf16[320,128]{1,0:T(8,128)(2,1)S(1)}, bf16[320,128]{1,0:T(8,128)(2,1)S(1)}, u32[]{:S(2)}, u32[]{:S(2)}) collective-permute-start(bf16[320,128]{1,0:T(8,128)(2,1)S(1)} %get-tuple-element.61), channel_id=1, source_target_pairs={{12,0},{8,4},{4,8},{0,12},{13,1},{9,5},{5,9},{1,13},{14,2},{10,6},... | collective-permute-start | bytes 245768 | tf_op jit(solution)/shard_map/ppermute | solution.py:652
  60.2 1.6 %collective-permute-done.17.refs_1_ = bf16[320,128]{1,0:T(8,128)(2,1)S(1)} collective-permute-done((bf16[320,128]{1,0:T(8,128)(2,1)S(1)}, bf16[320,128]{1,0:T(8,128)(2,1)S(1)}, u32[]{:S(2)}, u32[]{:S(2)}) %collective-permute-start.17) | collective-permute-done | bytes 81952 | tf_op jit(solution)/shard_map/ppermute | solution.py:652
  61.8 3.8 %collective-permute-done.18.refs_2_ = bf16[320,128]{1,0:T(8,128)(2,1)S(1)} collective-permute-done((bf16[320,128]{1,0:T(8,128)(2,1)S(1)}, bf16[320,128]{1,0:T(8,128)(2,1)S(1)}, u32[]{:S(2)}, u32[]{:S(2)}) %collective-permute-start.18) | collective-permute-done | bytes 81952 | tf_op jit(solution)/shard_map/ppermute | solution.py:652
  65.7 1.6 %collective-permute-start.22 = (bf16[128,128]{1,0:T(8,128)(2,1)S(1)}, bf16[128,128]{1,0:T(8,128)(2,1)S(1)}, u32[]{:S(2)}, u32[]{:S(2)}) collective-permute-start(bf16[128,128]{1,0:T(8,128)(2,1)S(1)} %get-tuple-element.63), channel_id=1, source_target_pairs={{0,3},{1,2},{2,1},{3,0},{4,7},{5,6},{6,5},{7,4},{8,11},{9,10},{10,... | collective-permute-start | bytes 98312 | tf_op jit(solution)/shard_map/ppermute | solution.py:702
  67.3 0.5 collective-permute-start.21
  67.9 1.3 %collective-permute-done.22.refs_5_ = bf16[128,128]{1,0:T(8,128)(2,1)S(1)} collective-permute-done((bf16[128,128]{1,0:T(8,128)(2,1)S(1)}, bf16[128,128]{1,0:T(8,128)(2,1)S(1)}, u32[]{:S(2)}, u32[]{:S(2)}) %collective-permute-start.22) | collective-permute-done | bytes 32800 | tf_op jit(solution)/shard_map/ppermute | solution.py:702
  69.1 2.1 %collective-permute-done.21.refs_4_ = bf16[128,128]{1,0:T(8,128)(2,1)S(1)} collective-permute-done((bf16[128,128]{1,0:T(8,128)(2,1)S(1)}, bf16[128,128]{1,0:T(8,128)(2,1)S(1)}, u32[]{:S(2)}, u32[]{:S(2)}) %collective-permute-start.21) | collective-permute-done | bytes 32800 | tf_op jit(solution)/shard_map/ppermute | solution.py:47
  71.2 1.5 %shard_map.129 = (f32[128,1280]{1,0:T(8,128)}, f32[128,1280]{1,0:T(8,128)}, f32[128,1280]{1,0:T(8,128)}, f32[256,128]{1,0:T(8,128)}) custom-call(bf16[1536,128]{1,0:T(8,128)(2,1)S(1)} %get-tuple-element.56.refs_0_, bf16[1536,128]{1,0:T(8,128)(2,1)S(1)} %collective-permute-done.16.refs_4_.refs_1_, bf16[896,128]{1,0:T(8,128)(2,1)S(1)} %get-tuple-element.62.refs_2_, ...), custom_call_target="tpu_custom_call" | custom-call | tf_op jit(solution)/shard_map/pallas_call | solution.py:616
  (43 shorter events, 0.4 us)
Async XLA Ops:
  0.6 13.8 %copy-start.3 = (bf16[128,1280]{1,0:T(8,128)(2,1)S(1)}, bf16[128,1280]{1,0:T(8,128)(2,1)}, u32[]{:S(2)}) copy-start(bf16[128,1280]{1,0:T(8,128)(2,1)} %do_ref.3) | copy-start | bytes 983044
  0.6 13.8 %copy-start.7 = (bf16[256,128]{1,0:T(8,128)(2,1)S(1)}, bf16[256,128]{1,0:T(8,128)(2,1)}, u32[]{:S(2)}) copy-start(bf16[256,128]{1,0:T(8,128)(2,1)} %t_ref.3) | copy-start | bytes 196612
  0.7 13.8 %copy-start.1 = (bf16[256,1280]{1,0:T(8,128)(2,1)S(1)}, bf16[256,1280]{1,0:T(8,128)(2,1)}, u32[]{:S(2)}) copy-start(bf16[256,1280]{1,0:T(8,128)(2,1)} %fv_ref.3) | copy-start | bytes 1966084
  0.7 13.8 %copy-start = (bf16[256,1280]{1,0:T(8,128)(2,1)S(1)}, bf16[256,1280]{1,0:T(8,128)(2,1)}, u32[]{:S(2)}) copy-start(bf16[256,1280]{1,0:T(8,128)(2,1)} %fk_ref.3) | copy-start | bytes 1966084
  0.7 13.8 %copy-start.2 = (bf16[128,1280]{1,0:T(8,128)(2,1)S(1)}, bf16[128,1280]{1,0:T(8,128)(2,1)}, u32[]{:S(2)}) copy-start(bf16[128,1280]{1,0:T(8,128)(2,1)} %fq_ref.3) | copy-start | bytes 983044
  4.3 23.6 %collective-permute-start = (bf16[128,1664]{1,0:T(8,128)(2,1)}, bf16[128,1664]{1,0:T(8,128)(2,1)S(1)}, u32[]{:S(2)}, u32[]{:S(2)}) collective-permute-start(bf16[128,1664]{1,0:T(8,128)(2,1)} %get-tuple-element.35), channel_id=1, source_target_pairs={{4,0},{0,4},{12,8},{8,12},{5,1},{1,5},{13,9},{9,13},{6,2},{2,6},{1... | collective-permute-start | bytes 1277960 | tf_op jit(solution)/shard_map/ppermute | solution.py:652
  7.4 14.1 %collective-permute-start.1 = (bf16[128,640]{1,0:T(8,128)(2,1)}, bf16[128,640]{1,0:T(8,128)(2,1)S(1)}, u32[]{:S(2)}, u32[]{:S(2)}) collective-permute-start(bf16[128,640]{1,0:T(8,128)(2,1)} %get-tuple-element.36), channel_id=1, source_target_pairs={{8,0},{12,4},{0,8},{4,12},{9,1},{13,5},{1,9},{5,13},{10,2},{14,6},... | collective-permute-start | bytes 491528 | tf_op jit(solution)/shard_map/ppermute | solution.py:652
  10.0 17.9 %collective-permute-start.2 = (bf16[128,640]{1,0:T(8,128)(2,1)}, bf16[128,640]{1,0:T(8,128)(2,1)S(1)}, u32[]{:S(2)}, u32[]{:S(2)}) collective-permute-start(bf16[128,640]{1,0:T(8,128)(2,1)} %get-tuple-element.37), channel_id=1, source_target_pairs={{12,0},{8,4},{4,8},{0,12},{13,1},{9,5},{5,9},{1,13},{14,2},{10,6},... | collective-permute-start | bytes 491528 | tf_op jit(solution)/shard_map/ppermute | solution.py:652
  10.0 18.0 %collective-permute-start.6 = (bf16[128,512]{1,0:T(8,128)(2,1)}, bf16[128,512]{1,0:T(8,128)(2,1)S(1)}, u32[]{:S(2)}, u32[]{:S(2)}) collective-permute-start(bf16[128,512]{1,0:T(8,128)(2,1)} %get-tuple-element.46), channel_id=1, source_target_pairs={{12,4},{0,8},{13,5},{1,9},{14,6},{2,10},{15,7},{3,11},{28,20},{16,... | collective-permute-start | bytes 393224 | tf_op jit(solution)/shard_map/ppermute | solution.py:652
  13.8 14.2 %collective-permute-start.7 = (bf16[128,512]{1,0:T(8,128)(2,1)}, bf16[128,512]{1,0:T(8,128)(2,1)S(1)}, u32[]{:S(2)}, u32[]{:S(2)}) collective-permute-start(bf16[128,512]{1,0:T(8,128)(2,1)} %get-tuple-element.47), channel_id=1, source_target_pairs={{8,4},{4,8},{9,5},{5,9},{10,6},{6,10},{11,7},{7,11},{24,20},{20,24... | collective-permute-start | bytes 393224 | tf_op jit(solution)/shard_map/ppermute | solution.py:652
  27.9 5.6 %copy-start.6 = (bf16[128,1280]{1,0:T(8,128)(2,1)S(1)}, bf16[128,1280]{1,0:T(8,128)(2,1)}, u32[]{:S(2)}) copy-start(bf16[128,1280]{1,0:T(8,128)(2,1)} %refs_14_.3) | copy-start | bytes 983044
  27.9 5.6 %copy-start.4 = (bf16[128,1280]{1,0:T(8,128)(2,1)S(1)}, bf16[128,1280]{1,0:T(8,128)(2,1)}, u32[]{:S(2)}) copy-start(bf16[128,1280]{1,0:T(8,128)(2,1)} %refs_12_.1) | copy-start | bytes 983044
  27.9 5.6 %copy-start.5 = (bf16[128,1280]{1,0:T(8,128)(2,1)S(1)}, bf16[128,1280]{1,0:T(8,128)(2,1)}, u32[]{:S(2)}) copy-start(bf16[128,1280]{1,0:T(8,128)(2,1)} %refs_13_.1) | copy-start | bytes 983044
  27.9 5.5 %collective-permute-start.3 = (bf16[128,1152]{1,0:T(8,128)(2,1)S(1)}, bf16[128,1152]{1,0:T(8,128)(2,1)S(1)}, u32[]{:S(2)}, u32[]{:S(2)}) collective-permute-start(bf16[128,1152]{1,0:T(8,128)(2,1)S(1)} %shard_map.122), channel_id=1, source_target_pairs={{0,1},{1,0},{2,3},{3,2},{4,5},{5,4},{6,7},{7,6},{8,9},{9,8},{10,11... | collective-permute-start | bytes 884744 | tf_op jit(solution)/shard_map/ppermute | solution.py:47
  28.0 5.4 %collective-permute-start.8 = (bf16[128,768]{1,0:T(8,128)(2,1)S(1)}, bf16[128,768]{1,0:T(8,128)(2,1)S(1)}, u32[]{:S(2)}, u32[]{:S(2)}) collective-permute-start(bf16[128,768]{1,0:T(8,128)(2,1)S(1)} %shard_map.123), channel_id=1, source_target_pairs={{0,1},{1,0},{2,3},{3,2},{4,5},{5,4},{6,7},{7,6},{8,9},{9,8},{10,11... | collective-permute-start | bytes 589832 | tf_op jit(solution)/shard_map/ppermute | solution.py:47
  28.6 13.5 %collective-permute-start.4 = (bf16[128,512]{1,0:T(8,128)(2,1)S(1)}, bf16[128,512]{1,0:T(8,128)(2,1)S(1)}, u32[]{:S(2)}, u32[]{:S(2)}) collective-permute-start(bf16[128,512]{1,0:T(8,128)(2,1)S(1)} %get-tuple-element.41), channel_id=1, source_target_pairs={{8,0},{12,4},{0,8},{4,12},{9,1},{13,5},{1,9},{5,13},{10,2},{14,6},... | collective-permute-start | bytes 393224 | tf_op jit(solution)/shard_map/ppermute | solution.py:652
  32.1 10.0 %collective-permute-start.5 = (bf16[128,512]{1,0:T(8,128)(2,1)S(1)}, bf16[128,512]{1,0:T(8,128)(2,1)S(1)}, u32[]{:S(2)}, u32[]{:S(2)}) collective-permute-start(bf16[128,512]{1,0:T(8,128)(2,1)S(1)} %get-tuple-element.42), channel_id=1, source_target_pairs={{12,0},{8,4},{4,8},{0,12},{13,1},{9,5},{5,9},{1,13},{14,2},{10,6},... | collective-permute-start | bytes 393224 | tf_op jit(solution)/shard_map/ppermute | solution.py:652
  33.4 0.7 copy-start.8
  38.0 4.1 %collective-permute-start.10 = (bf16[384,128]{1,0:T(8,128)(2,1)S(1)}, bf16[384,128]{1,0:T(8,128)(2,1)S(1)}, u32[]{:S(2)}, u32[]{:S(2)}) collective-permute-start(bf16[384,128]{1,0:T(8,128)(2,1)S(1)} %get-tuple-element.49.refs_3_), channel_id=1, source_target_pairs={{0,1},{1,0},{2,3},{3,2},{4,5},{5,4},{6,7},{7,6},{8,9},{9,8},{10,11... | collective-permute-start | bytes 294920 | tf_op jit(solution)/shard_map/ppermute | solution.py:47
  42.1 4.8 %collective-permute-start.9 = (bf16[128,768]{1,0:T(8,128)(2,1)S(1)}, bf16[128,768]{1,0:T(8,128)(2,1)S(1)}, u32[]{:S(2)}, u32[]{:S(2)}) collective-permute-start(bf16[128,768]{1,0:T(8,128)(2,1)S(1)} %shard_map.125), channel_id=1, source_target_pairs={{0,1},{1,0},{2,3},{3,2},{4,5},{5,4},{6,7},{7,6},{8,9},{9,8},{10,11... | collective-permute-start | bytes 589832 | tf_op jit(solution)/shard_map/ppermute | solution.py:47
  42.2 9.1 %collective-permute-start.15 = (bf16[384,128]{1,0:T(8,128)(2,1)S(1)}, bf16[384,128]{1,0:T(8,128)(2,1)S(1)}, u32[]{:S(2)}, u32[]{:S(2)}) collective-permute-start(bf16[384,128]{1,0:T(8,128)(2,1)S(1)} %add_convert_fusion.refs_17_.refs_2_), channel_id=1, source_target_pairs={{12,0},{8,4},{4,8},{0,12},{13,1},{9,5},{5,9},{1,13},{14,2},{10,6},... | collective-permute-start | bytes 294920 | tf_op jit(solution)/shard_map/ppermute | solution.py:652
  43.6 11.9 %collective-permute-start.14 = (bf16[384,128]{1,0:T(8,128)(2,1)S(1)}, bf16[384,128]{1,0:T(8,128)(2,1)S(1)}, u32[]{:S(2)}, u32[]{:S(2)}) collective-permute-start(bf16[384,128]{1,0:T(8,128)(2,1)S(1)} %add_convert_fusion.refs_17_.refs_2_), channel_id=1, source_target_pairs={{8,0},{12,4},{0,8},{4,12},{9,1},{13,5},{1,9},{5,13},{10,2},{14,6},... | collective-permute-start | bytes 294920 | tf_op jit(solution)/shard_map/ppermute | solution.py:652
  46.8 8.7 %collective-permute-start.13 = (bf16[384,128]{1,0:T(8,128)(2,1)S(1)}, bf16[384,128]{1,0:T(8,128)(2,1)S(1)}, u32[]{:S(2)}, u32[]{:S(2)}) collective-permute-start(bf16[384,128]{1,0:T(8,128)(2,1)S(1)} %add_convert_fusion.refs_17_.refs_2_), channel_id=1, source_target_pairs={{4,0},{0,4},{12,8},{8,12},{5,1},{1,5},{13,9},{9,13},{6,2},{2,6},{1... | collective-permute-start | bytes 294920 | tf_op jit(solution)/shard_map/ppermute | solution.py:652
  50.7 4.8 %collective-permute-start.11 = (bf16[352,128]{1,0:T(8,128)(2,1)S(1)}, bf16[352,128]{1,0:T(8,128)(2,1)S(1)}, u32[]{:S(2)}, u32[]{:S(2)}) collective-permute-start(bf16[352,128]{1,0:T(8,128)(2,1)S(1)} %get-tuple-element.54), channel_id=1, source_target_pairs={{0,1},{1,0},{2,3},{3,2},{4,5},{5,4},{6,7},{7,6},{8,9},{9,8},{10,11... | collective-permute-start | bytes 270344 | tf_op jit(solution)/shard_map/ppermute | solution.py:47
  50.8 4.8 %collective-permute-start.12 = (bf16[352,128]{1,0:T(8,128)(2,1)S(1)}, bf16[352,128]{1,0:T(8,128)(2,1)S(1)}, u32[]{:S(2)}, u32[]{:S(2)}) collective-permute-start(bf16[352,128]{1,0:T(8,128)(2,1)S(1)} %get-tuple-element.55), channel_id=1, source_target_pairs={{0,1},{1,0},{2,3},{3,2},{4,5},{5,4},{6,7},{7,6},{8,9},{9,8},{10,11... | collective-permute-start | bytes 270344 | tf_op jit(solution)/shard_map/ppermute | solution.py:47
  55.7 9.9 %collective-permute-start.16 = (bf16[1536,128]{1,0:T(8,128)(2,1)S(1)}, bf16[1536,128]{1,0:T(8,128)(2,1)S(1)}, u32[]{:S(2)}, u32[]{:S(2)}) collective-permute-start(bf16[1536,128]{1,0:T(8,128)(2,1)S(1)} %get-tuple-element.56.refs_0_), channel_id=1, source_target_pairs={{0,1},{1,0},{2,3},{3,2},{4,5},{5,4},{6,7},{7,6},{8,9},{9,8},{10,11... | collective-permute-start | bytes 1179656 | tf_op jit(solution)/shard_map/ppermute | solution.py:47
  55.8 6.0 %collective-permute-start.17 = (bf16[320,128]{1,0:T(8,128)(2,1)S(1)}, bf16[320,128]{1,0:T(8,128)(2,1)S(1)}, u32[]{:S(2)}, u32[]{:S(2)}) collective-permute-start(bf16[320,128]{1,0:T(8,128)(2,1)S(1)} %get-tuple-element.59), channel_id=1, source_target_pairs={{4,0},{0,4},{12,8},{8,12},{5,1},{1,5},{13,9},{9,13},{6,2},{2,6},{1... | collective-permute-start | bytes 245768 | tf_op jit(solution)/shard_map/ppermute | solution.py:652
  55.8 9.8 %collective-permute-start.18 = (bf16[320,128]{1,0:T(8,128)(2,1)S(1)}, bf16[320,128]{1,0:T(8,128)(2,1)S(1)}, u32[]{:S(2)}, u32[]{:S(2)}) collective-permute-start(bf16[320,128]{1,0:T(8,128)(2,1)S(1)} %get-tuple-element.60), channel_id=1, source_target_pairs={{8,0},{12,4},{0,8},{4,12},{9,1},{13,5},{1,9},{5,13},{10,2},{14,6},... | collective-permute-start | bytes 245768 | tf_op jit(solution)/shard_map/ppermute | solution.py:652
  57.7 7.9 %collective-permute-start.19 = (bf16[320,128]{1,0:T(8,128)(2,1)S(1)}, bf16[320,128]{1,0:T(8,128)(2,1)S(1)}, u32[]{:S(2)}, u32[]{:S(2)}) collective-permute-start(bf16[320,128]{1,0:T(8,128)(2,1)S(1)} %get-tuple-element.61), channel_id=1, source_target_pairs={{12,0},{8,4},{4,8},{0,12},{13,1},{9,5},{5,9},{1,13},{14,2},{10,6},... | collective-permute-start | bytes 245768 | tf_op jit(solution)/shard_map/ppermute | solution.py:652
  65.6 5.6 %collective-permute-start.20 = (bf16[896,128]{1,0:T(8,128)(2,1)S(1)}, bf16[896,128]{1,0:T(8,128)(2,1)S(1)}, u32[]{:S(2)}, u32[]{:S(2)}) collective-permute-start(bf16[896,128]{1,0:T(8,128)(2,1)S(1)} %get-tuple-element.62.refs_2_), channel_id=1, source_target_pairs={{0,1},{1,0},{2,3},{3,2},{4,5},{5,4},{6,7},{7,6},{8,9},{9,8},{10,11... | collective-permute-start | bytes 688136 | tf_op jit(solution)/shard_map/ppermute | solution.py:47
  65.7 3.4 %collective-permute-start.22 = (bf16[128,128]{1,0:T(8,128)(2,1)S(1)}, bf16[128,128]{1,0:T(8,128)(2,1)S(1)}, u32[]{:S(2)}, u32[]{:S(2)}) collective-permute-start(bf16[128,128]{1,0:T(8,128)(2,1)S(1)} %get-tuple-element.63), channel_id=1, source_target_pairs={{0,3},{1,2},{2,1},{3,0},{4,7},{5,6},{6,5},{7,4},{8,11},{9,10},{10,... | collective-permute-start | bytes 98312 | tf_op jit(solution)/shard_map/ppermute | solution.py:702
  67.3 3.9 %collective-permute-start.21 = (bf16[128,128]{1,0:T(8,128)(2,1)S(1)}, bf16[128,128]{1,0:T(8,128)(2,1)S(1)}, u32[]{:S(2)}, u32[]{:S(2)}) collective-permute-start(bf16[128,128]{1,0:T(8,128)(2,1)S(1)} %get-tuple-element.63), channel_id=1, source_target_pairs={{0,2},{2,0},{1,3},{3,1},{4,6},{6,4},{5,7},{7,5},{8,10},{10,8},{9,1... | collective-permute-start | bytes 98312 | tf_op jit(solution)/shard_map/ppermute | solution.py:47

commit v7 on v6

--- a/solution.py
+++ b/solution.py
@@ -264,14 +264,14 @@
 
 
 def pack_kernel(frames, outputs, fq_ref, do_ref, fk_ref, fv_ref, t_ref, *refs):
-    outs, (q_in, do_in, k_in, v_in, k2_in, v2_in, sems) = refs[:-7], refs[-7:]
+    outs, (q_in, do_in, k_in, v_in, k2_in, v2_in, t_in, sems) = refs[:-8], refs[-8:]
     me, half = lax.axis_index("tm"), lax.axis_index("rep")
     rows = fq_ref.shape[0]
     mine = pl.ds(pl.multiple_of(half * rows, rows), rows)
     rest = pl.ds(pl.multiple_of((1 - half) * rows, rows), rows)
     moves = [
         (fq_ref, q_in), (do_ref, do_in), (fk_ref.at[mine, :], k_in), (fv_ref.at[mine, :], v_in),
-        (fk_ref.at[rest, :], k2_in), (fv_ref.at[rest, :], v2_in),
+        (fk_ref.at[rest, :], k2_in), (fv_ref.at[rest, :], v2_in), (t_ref, t_in),
     ]
     copies = [pltpu.make_async_copy(a, b, sems.at[n]) for n, (a, b) in enumerate(moves)]
     for copy in copies:
@@ -282,7 +282,7 @@
         at = 0
         for table, m, what in parts:
             if what in ("t", "other t"):
-                blocks = [t_ref[mine if what == "t" else rest, :]]
+                blocks = [t_in[mine if what == "t" else rest, :]]
             else:
                 cols = column(lookup(table, me ^ m))
                 sources = (q_in, do_in, k_in, v_in) if what == "mine" else (k2_in, v2_in)
@@ -295,34 +295,37 @@
 def pack(frames, outputs, limit, fq, do, fk, fv, t):
     rows, width = fq.shape
     size = {"mine": 4 * DH, "other": 2 * DH, "t": t.shape[1], "other t": t.shape[1]}
-    anywhere = pl.BlockSpec(memory_space=pl.ANY)
     return pl.pallas_call(
         functools.partial(pack_kernel, frames, outputs),
-        in_specs=[anywhere] * 4 + vmem(1),
+        in_specs=[pl.BlockSpec(memory_space=pltpu.HBM)] * 5,
         out_specs=vmem(len(outputs)),
         out_shape=[
             jax.ShapeDtypeStruct((rows, sum(size[what] for _, _, what in parts)), BF16)
             for parts in outputs
         ],
-        scratch_shapes=[pltpu.VMEM((rows, width), BF16)] * 6 + [pltpu.SemaphoreType.DMA((6,))],
+        scratch_shapes=[pltpu.VMEM((rows, width), BF16)] * 6
+        + [pltpu.VMEM(t.shape, BF16), pltpu.SemaphoreType.DMA((7,))],
         compiler_params=pltpu.CompilerParams(vmem_limit_bytes=limit * 1024 * 1024),
     )(fq, do, fk, fv, t)
 
 
-def pick_kernel(spans, *refs):
-    out, at = refs[-1], 0
+def pick_kernel(spans, apart, *refs):
+    at = 0
     for n, (start, size) in enumerate(spans):
-        out[:, at : at + size] = refs[n][:, start : start + size]
+        out = refs[n - len(spans)] if apart else refs[-1].at[:, pl.ds(at, size)]
+        out[...] = refs[n][:, start : start + size]
         at += size
 
 
-def pick(parts, size, after=()):
+def pick(parts, size, apart, after=()):
     arrays = [array for array, _ in parts]
+    rows, dtype = arrays[0].shape[0], arrays[0].dtype
+    shapes = [(rows, size)] * len(arrays) if apart else [(rows, size * len(arrays))]
     return pl.pallas_call(
-        functools.partial(pick_kernel, [(start, size) for _, start in parts]),
+        functools.partial(pick_kernel, [(start, size) for _, start in parts], apart),
         in_specs=vmem(len(arrays)) + [pl.BlockSpec(memory_space=pl.ANY)] * len(after),
-        out_specs=pl.BlockSpec(memory_space=pltpu.VMEM),
-        out_shape=jax.ShapeDtypeStruct((arrays[0].shape[0], size * len(parts)), arrays[0].dtype),
+        out_specs=vmem(len(shapes)),
+        out_shape=[jax.ShapeDtypeStruct(shape, dtype) for shape in shapes],
         compiler_params=SMALL,
     )(*arrays, *after)
 
@@ -517,7 +520,7 @@
 
 
 def hand_out_kernel(frames, size, parts, keep_ref, *refs):
-    gots, pieces, (stack, own_ref, *sends, total) = refs[:parts], refs[parts : parts + frames], refs[parts + frames :]
+    gots, (own_ref, *sends, total) = refs[:parts], refs[parts:]
     me = lax.axis_index("tm")
     rows = own_ref.shape[0]
     total[...] = keep_ref[...] + jnp.concatenate([got[...].astype(F32) for got in gots], axis=0)
@@ -528,26 +531,19 @@
             own_ref[...] = low
         sends[m][:rows, :] = low.astype(BF16)
         sends[m][rows:, :] = grads
-        high = pieces[m].shape[0]
-        stack[m * high : (m + 1) * high, :] = pieces[m][...]
-
-
-def hand_out(rows, keep, gots, pieces):
-    frames = len(pieces)
+
+
+def hand_out(frames, rows, keep, gots):
     size, rank = keep.shape[0] - frames * rows, keep.shape[1]
     send = jax.ShapeDtypeStruct((rows + size, rank), BF16)
     return pl.pallas_call(
         functools.partial(hand_out_kernel, frames, size, len(gots)),
-        in_specs=vmem(1 + len(gots) + frames),
-        out_specs=vmem(frames + 2),
-        out_shape=[
-            jax.ShapeDtypeStruct((frames * pieces[0].shape[0], rank), BF16),
-            jax.ShapeDtypeStruct((rows, rank), F32),
-        ]
-        + [send] * frames,
+        in_specs=vmem(1 + len(gots)),
+        out_specs=vmem(frames + 1),
+        out_shape=[jax.ShapeDtypeStruct((rows, rank), F32)] + [send] * frames,
         scratch_shapes=[pltpu.VMEM(keep.shape, F32)],
         compiler_params=SMALL,
-    )(keep, *gots, *pieces)
+    )(keep, *gots)
 
 
 def collect_kernel(frames, own_ref, *refs):
@@ -563,24 +559,24 @@
         out_ref[rows + m * size : rows + (m + 1) * size, :] = gots[m][rows:, :]
 
 
-def collect(own, gots, after):
+def collect(own, gots):
     frames, (rows, rank) = len(gots), own.shape
     size = gots[0].shape[0] - rows
     return pl.pallas_call(
         functools.partial(collect_kernel, frames),
-        in_specs=vmem(frames + 1) + [pl.BlockSpec(memory_space=pl.ANY)] * len(after),
+        in_specs=vmem(frames + 1),
         out_specs=vmem(2),
         out_shape=[
             jax.ShapeDtypeStruct((rows + frames * size, rank), BF16),
             jax.ShapeDtypeStruct((rows, rank), BF16),
         ],
         compiler_params=SMALL,
-    )(own, *gots, *after)
+    )(own, *gots)
 
 
 def place_kernel(early, late, *refs):
     frames = len(late[0])
-    stack, stack2, tail, tail2, low_head, low_diag, *outs = refs
+    all_ref, tail, tail2, low_head, low_diag, *outs = refs
     me, half = lax.axis_index("tm"), lax.axis_index("rep")
     first = half == 0
     rank = outs[0].shape[0]
@@ -590,37 +586,33 @@
     other = tail2[:rows, :].astype(F32) + low_diag[...].astype(F32)
     outs[3][:rows, :] = jnp.where(first, same, other)
     outs[3][rows:, :] = jnp.where(first, other, same)
+    def write(cols, a, b):
+        both = jnp.concatenate([a.astype(F32), b.astype(F32)], axis=0)
+        for o in range(3):
+            outs[o][:, cols] = both[o * rank : (o + 1) * rank]
+
+    for chip in range(frames):
+        for n, (table, numbers) in enumerate(early):
+            here = slice(n * cut, (n + 1) * cut)
+            if numbers[chip]:
+                cols = slice(table[chip] * DH, (table[chip] + 1) * DH)
+                write(cols, all_ref[2 * chip, here, :], all_ref[2 * chip + 1, here, :])
     for m in range(frames):
-        chip = me ^ m
-
-        def write(head, a_ref, b_ref, at):
-            def body():
-                a, b = a_ref[at : at + cut, :].astype(F32), b_ref[at : at + cut, :].astype(F32)
-                cols = column(lookup(head[0], chip))
-                both = jnp.concatenate([jnp.where(first, a, b), jnp.where(first, b, a)], axis=0)
-                for o in range(3):
-                    outs[o][:, cols] = both[o * rank : (o + 1) * rank]
-
-            if min(head[1]) > 0:
-                body()
-            else:
-                pl.when(lookup(head[1], chip) > 0)(body)
-
-        for n, head in enumerate(early):
-            write(head, stack, stack2, (m * len(early) + n) * cut)
-        write(late, tail, tail2, rows + m * cut)
-
-
-def place(early, late, stack, stack2, tail, tail2, low_head, low_diag, rank, width):
+        here = slice(rows + m * cut, rows + (m + 1) * cut)
+        a, b = tail[here, :], tail2[here, :]
+        write(column(lookup(late[0], me ^ m)), jnp.where(first, a, b), jnp.where(first, b, a))
+
+
+def place(early, late, everything, tail, tail2, low_head, low_diag, rank, width):
     rows = low_head.shape[0]
     return pl.pallas_call(
         functools.partial(place_kernel, early, late),
-        in_specs=vmem(6),
+        in_specs=vmem(5),
         out_specs=vmem(4),
         out_shape=[jax.ShapeDtypeStruct((rank, width), F32)] * 3
         + [jax.ShapeDtypeStruct((2 * rows, rank), F32)],
         compiler_params=SMALL,
-    )(stack, stack2, tail, tail2, low_head, low_diag)
+    )(everything, tail, tail2, low_head, low_diag)
 
 
 def exchange_plan(
@@ -675,33 +667,36 @@
         rest_got.append((meet(packed[2 * m - 2], m, wide), 0))
         late_got.append((meet(packed_late[m - 2], m), 0))
 
-    def sides(n, got, wide_t, after=()):
-        size = 2 * DH + (rank if wide_t else 0)
-        cross = swap(pick([(a, start + 2 * DH) for a, start in got], size, after), "rep")
+    def sides(n, got, wide_t, apart, after=()):
+        skip = 0 if n == 2 else 2 * DH
+        size = 4 * DH - skip + (rank if wide_t else 0)
+        picked = pick([(a, start + skip) for a, start in got], size, apart, after)
+        cross = [swap(block, "rep") for block in picked]
+        cross = [(cross[m], 2 * DH - skip) if apart else (cross[0], m * size + 2 * DH - skip) for m in range(frames - 1)]
         rows_here = [(kept[2 * n], 0)] + got
-        rows_there = [(kept[2 * n + 1], 0)] + [(cross, m * size) for m in range(frames - 1)]
+        rows_there = [(kept[2 * n + 1], 0)] + cross
         return rows_here, rows_there, cross
 
-    *lead_side, cross = sides(0, lead_got, True, kept[:1])
+    *lead_side, cross = sides(0, lead_got, True, False, kept[:1])
     t_side = (
         [(kept[6], 0)] + [(a, start + 4 * DH) for a, start in lead_got],
-        [(kept[7], 0)] + [(cross, m * (2 * DH + rank) + 2 * DH) for m in range(frames - 1)],
+        [(kept[7], 0)] + [(block, start + 2 * DH) for block, start in cross],
     )
-    *rest_side, _ = sides(1, rest_got, False)
+    *rest_side, _ = sides(1, rest_got, False, False)
     early = [lead, rest]
     keep, give, *low = head_group(early, band_width, [t_side, lead_side, rest_side], adapters)
-    *late_side, _ = sides(2, late_got, False, [give])
-    piece = (keep + swap(give, "rep").astype(F32)).astype(BF16)
-    pieces = [piece] + [meet(piece, m) for m in range(1, frames)]
-    keep, *gives = head_group([late], band_width, [t_side, late_side], adapters, low, [piece])
-    stack, own, *sends = hand_out(rows, keep, [swap(g, "rep") for g in gives], pieces)
-    stack2 = swap(stack, "rep")
+    got = swap(give, "rep")
+    *late_side, _ = sides(2, late_got, False, False, [got])
+    piece = (keep + got.astype(F32)).astype(BF16)
+    everything = lax.all_gather(piece, ("tm", "rep"))
+    keep, *gives = head_group([late], band_width, [t_side, late_side], adapters, low)
+    own, *sends = hand_out(frames, rows, keep, [swap(g, "rep") for g in gives])
     gots = [sends[0]] + [meet(sends[m], m) for m in range(1, frames)]
-    tail, low = collect(own, gots, [stack2])
+    tail, low = collect(own, gots)
     diag = [(0, 3), (1, 2), (2, 1), (3, 0)]
     low_head, low_diag = swap(low, "head"), lax.ppermute(low, ("head", "rep"), diag)
     outs = place(
-        early, late, stack, stack2, tail, swap(tail, "rep"), low_head, low_diag, rank, width
+        early, late, everything, tail, swap(tail, "rep"), low_head, low_diag, rank, width
     )
     return tuple(outs)
 

time: 72.9 us -> 79.9 us (1.096)
  blocking collectives: 0 us -> 15.4 us
  starting transfers between devices: 27.7 us -> 23.9 us
  waiting for transfers between devices: 29.5 us -> 25.7 us
  Pallas kernels: 13.9 us -> 13.1 us
    all_gather x0 -> x1, blocking collectives: none -> 15.4 us  [exchange_plan(): everything = lax.all_gather(piece, ('tm', 'rep'))]
    ppermute x13 -> x10, starting transfers between devices: 24 us -> 20.6 us  [meet(): return lax.ppermute(block, 'tm', [(j ^ m, j) for j in targets])]
    ppermute x13 -> x10, waiting for transfers between devices: 26.1 us -> 23.1 us  [meet(): return lax.ppermute(block, 'tm', [(j ^ m, j) for j in targets])]
    ppermute x1, waiting for transfers between devices: 1.26 us -> 0.01 us  [exchange_plan(): lax.ppermute(low, ('head', 'rep'), diag)]
    ppermute x1, starting transfers between devices: 1.61 us -> 0.41 us  [exchange_plan(): lax.ppermute(low, ('head', 'rep'), diag)]
    ppermute x9 -> x8, starting transfers between devices: 2.07 us -> 2.84 us  [swap(): return lax.ppermute(block, axis, [(0, 1), (1, 0)])]
    ppermute x9 -> x8, waiting for transfers between devices: 2.14 us -> 2.66 us  [swap(): return lax.ppermute(block, axis, [(0, 1), (1, 0)])]
  transfers between devices with their start and end apart: 23 -> 19, of which waited for: 8 -> 8; matrix products, arithmetic and copies ran while one was open for 0% -> 0% of each run, Pallas kernels for 12% -> 6%
where the time goes in v7:
time: 79.9 us; the launch traced here: 79.7 us
  waiting for transfers between devices  25.7 us (32%)
  starting transfers between devices  23.9 us (30%)
  blocking collectives  15.4 us (19%)
  Pallas kernels  13.1 us (16%)
  between operations  0.89 us (1%)
    ppermute x10, waiting for transfers between devices, meet(): return lax.ppermute(block, 'tm', [(j ^ m, j) for j in targets])  23.1 us
    ppermute x10, starting transfers between devices, meet(): return lax.ppermute(block, 'tm', [(j ^ m, j) for j in targets])  20.6 us
    all_gather x1, blocking collectives, exchange_plan(): everything = lax.all_gather(piece, ('tm', 'rep'))  15.4 us
    pallas_call x2, Pallas kernels, head_group(): pl.pallas_call(functools.partial(group_kernel, heads, frames, chained, le...  7.78 us
    pallas_call x2, Pallas kernels, pack(): pl.pallas_call(functools.partial(pack_kernel, frames, outputs), in_specs=...  3.71 us
    ppermute x8, starting transfers between devices, swap(): return lax.ppermute(block, axis, [(0, 1), (1, 0)])  2.84 us
    ppermute x8, waiting for transfers between devices, swap(): return lax.ppermute(block, axis, [(0, 1), (1, 0)])  2.66 us
  transfers between devices with their start and end apart: 19, of which 8 were waited for; matrix products, arithmetic and copies ran while one was open for 0% of the time, Pallas kernels for 6%

profile of v7, /device:TPU:0, one launch (start us, length us, event | category | flops | bytes accessed | tf_op | source)
XLA Modules:
  0.0 79.7 jit_solution(15483151319560049104)
XLA Ops:
  0.7 2.8 %shard_map.121 = (bf16[128,1664]{1,0:T(8,128)(2,1)}, bf16[128,640]{1,0:T(8,128)(2,1)}, bf16[128,512]{1,0:T(8,128)(2,1)}, bf16[128,640]{1,0:T(8,128)(2,1)}, bf16[128,512]{1,0:T(8,128)(2,1)}) custom-call(bf16[128,1280]{1,0:T(8,128)(2,1)} %fq_ref.3, bf16[128,1280]{1,0:T(8,128)(2,1)} %do_ref.3, bf16[256,1280]{1,0:T(8,128)(2,1)} %fk_ref.3, ...), custom_call_target="tpu_custom_call" | custom-call | tf_op jit(solution)/shard_map/pallas_call | solution.py:298
  3.5 3.1 %collective-permute-start = (bf16[128,1664]{1,0:T(8,128)(2,1)}, bf16[128,1664]{1,0:T(8,128)(2,1)S(1)}, u32[]{:S(2)}, u32[]{:S(2)}) collective-permute-start(bf16[128,1664]{1,0:T(8,128)(2,1)} %get-tuple-element.34), channel_id=1, source_target_pairs={{4,0},{0,4},{12,8},{8,12},{5,1},{1,5},{13,9},{9,13},{6,2},{2,6},{1... | collective-permute-start | bytes 1277960 | tf_op jit(solution)/shard_map/ppermute | solution.py:644
  6.5 2.6 %collective-permute-start.1 = (bf16[128,640]{1,0:T(8,128)(2,1)}, bf16[128,640]{1,0:T(8,128)(2,1)S(1)}, u32[]{:S(2)}, u32[]{:S(2)}) collective-permute-start(bf16[128,640]{1,0:T(8,128)(2,1)} %get-tuple-element.35), channel_id=1, source_target_pairs={{8,0},{12,4},{0,8},{4,12},{9,1},{13,5},{1,9},{5,13},{10,2},{14,6},... | collective-permute-start | bytes 491528 | tf_op jit(solution)/shard_map/ppermute | solution.py:644
  9.1 3.8 %collective-permute-start.4 = (bf16[128,512]{1,0:T(8,128)(2,1)}, bf16[128,512]{1,0:T(8,128)(2,1)S(1)}, u32[]{:S(2)}, u32[]{:S(2)}) collective-permute-start(bf16[128,512]{1,0:T(8,128)(2,1)} %get-tuple-element.41), channel_id=1, source_target_pairs={{12,4},{0,8},{13,5},{1,9},{14,6},{2,10},{15,7},{3,11},{28,20},{16,... | collective-permute-start | bytes 393224 | tf_op jit(solution)/shard_map/ppermute | solution.py:644
  13.0 0.7 collective-permute-start.5
  13.7 0.9 %shard_map.120 = (bf16[128,512]{1,0:T(8,128)(2,1)S(1)}, bf16[128,512]{1,0:T(8,128)(2,1)S(1)}, bf16[128,512]{1,0:T(8,128)(2,1)S(1)}, bf16[128,256]{1,0:T(8,128)(2...) custom-call(bf16[128,1280]{1,0:T(8,128)(2,1)S(1)} %copy-done.2, ...), custom_call_target="tpu_custom_call" | custom-call | tf_op jit(solution)/shard_map/pallas_call | solution.py:298
  14.6 6.0 %collective-permute-done.1.refs_1_.refs_3_ = bf16[128,640]{1,0:T(8,128)(2,1)S(1)} collective-permute-done((bf16[128,640]{1,0:T(8,128)(2,1)}, bf16[128,640]{1,0:T(8,128)(2,1)S(1)}, u32[]{:S(2)}, u32[]{:S(2)}) %collective-permute-start.1) | collective-permute-done | bytes 163872 | tf_op jit(solution)/shard_map/ppermute | solution.py:644
  20.6 6.4 %collective-permute-done.2.refs_2_.refs_4_ = bf16[128,640]{1,0:T(8,128)(2,1)S(1)} collective-permute-done((bf16[128,640]{1,0:T(8,128)(2,1)}, bf16[128,640]{1,0:T(8,128)(2,1)S(1)}, u32[]{:S(2)}, u32[]{:S(2)}) %collective-permute-start.2) | collective-permute-done | bytes 163872 | tf_op jit(solution)/shard_map/ppermute | solution.py:644
  27.1 0.1 collective-permute-start.3
  27.2 0.5 collective-permute-start.6
  27.8 3.5 %collective-permute-start.8 = (bf16[128,512]{1,0:T(8,128)(2,1)S(1)}, bf16[128,512]{1,0:T(8,128)(2,1)S(1)}, u32[]{:S(2)}, u32[]{:S(2)}) collective-permute-start(bf16[128,512]{1,0:T(8,128)(2,1)S(1)} %get-tuple-element.47), channel_id=1, source_target_pairs={{8,0},{12,4},{0,8},{4,12},{9,1},{13,5},{1,9},{5,13},{10,2},{14,6},... | collective-permute-start | bytes 393224 | tf_op jit(solution)/shard_map/ppermute | solution.py:644
  31.2 1.4 %collective-permute-start.9 = (bf16[128,512]{1,0:T(8,128)(2,1)S(1)}, bf16[128,512]{1,0:T(8,128)(2,1)S(1)}, u32[]{:S(2)}, u32[]{:S(2)}) collective-permute-start(bf16[128,512]{1,0:T(8,128)(2,1)S(1)} %get-tuple-element.48), channel_id=1, source_target_pairs={{12,0},{8,4},{4,8},{0,12},{13,1},{9,5},{5,9},{1,13},{14,2},{10,6},... | collective-permute-start | bytes 393224 | tf_op jit(solution)/shard_map/ppermute | solution.py:644
  32.6 0.6 copy-done.8
  33.3 3.9 %shard_map.124 = (f32[384,128]{1,0:T(8,128)S(1)}, bf16[384,128]{1,0:T(8,128)(2,1)S(1)}, f32[512,128]{1,0:T(8,128)S(1)}, f32[512,128]{1,0:T(8,128)S(1)}) custom-call(s32[4,4]{1,0:T(4,128)S(1)} %copy-done.8, bf16[128,128]{1,0:T(8,128)(2,1)S(1)} %get-tuple-element.33.refs_1_, bf16[128,1664]{1,0:T(8,128)(2,1)S(1)} %collective-permute-done.refs_0_.refs_2_, ...), custom_call_target="tpu_custom_call" | custom-call | tf_op jit(solution)/shard_map/pallas_call | solution.py:508
  37.2 0.1 collective-permute-start.7
  37.3 3.9 %collective-permute-done.8.refs_1_.refs_8_ = bf16[128,512]{1,0:T(8,128)(2,1)S(1)} collective-permute-done((bf16[128,512]{1,0:T(8,128)(2,1)S(1)}, bf16[128,512]{1,0:T(8,128)(2,1)S(1)}, u32[]{:S(2)}, u32[]{:S(2)}) %collective-permute-start.8) | collective-permute-done | bytes 131104 | tf_op jit(solution)/shard_map/ppermute | solution.py:644
  41.3 0.1 collective-permute-start.10
  41.3 1.7 %collective-permute-done.10.refs_11_ = bf16[128,1536]{1,0:T(8,128)(2,1)S(1)} collective-permute-done((bf16[128,1536]{1,0:T(8,128)(2,1)S(1)}, bf16[128,1536]{1,0:T(8,128)(2,1)S(1)}, u32[]{:S(2)}, u32[]{:S(2)}) %collective-permute-start.10) | collective-permute-done | bytes 393248 | tf_op jit(solution)/shard_map/ppermute | solution.py:47
  43.0 3.9 %shard_map.126 = (f32[704,128]{1,0:T(8,128)S(1)}, bf16[352,128]{1,0:T(8,128)(2,1)S(1)}, bf16[352,128]{1,0:T(8,128)(2,1)S(1)}) custom-call(s32[4,4]{1,0:T(4,128)S(1)} %copy-done.8, bf16[128,128]{1,0:T(8,128)(2,1)S(1)} %get-tuple-element.33.refs_1_, bf16[128,1664]{1,0:T(8,128)(2,1)S(1)} %collective-permute-done.refs_0_.refs_2_, ...), custom_call_target="tpu_custom_call" | custom-call | tf_op jit(solution)/shard_map/pallas_call | solution.py:508
  46.9 0.2 collective-permute-start.11
  47.1 0.4 collective-permute-start.12
  47.5 0.8 collective-permute-done.11.refs_0_
  48.3 0.2 collective-permute-done.12.refs_1_
  48.5 3.2 %collective-permute-start.13 = (bf16[320,128]{1,0:T(8,128)(2,1)S(1)}, bf16[320,128]{1,0:T(8,128)(2,1)S(1)}, u32[]{:S(2)}, u32[]{:S(2)}) collective-permute-start(bf16[320,128]{1,0:T(8,128)(2,1)S(1)} %get-tuple-element.57), channel_id=1, source_target_pairs={{4,0},{0,4},{12,8},{8,12},{5,1},{1,5},{13,9},{9,13},{6,2},{2,6},{1... | collective-permute-start | bytes 245768 | tf_op jit(solution)/shard_map/ppermute | solution.py:644
  51.7 2.4 %collective-permute-start.15 = (bf16[320,128]{1,0:T(8,128)(2,1)S(1)}, bf16[320,128]{1,0:T(8,128)(2,1)S(1)}, u32[]{:S(2)}, u32[]{:S(2)}) collective-permute-start(bf16[320,128]{1,0:T(8,128)(2,1)S(1)} %get-tuple-element.59), channel_id=1, source_target_pairs={{12,0},{8,4},{4,8},{0,12},{13,1},{9,5},{5,9},{1,13},{14,2},{10,6},... | collective-permute-start | bytes 245768 | tf_op jit(solution)/shard_map/ppermute | solution.py:644
  54.2 0.5 collective-permute-done.13.refs_1_
  54.7 6.3 %collective-permute-done.14.refs_2_ = bf16[320,128]{1,0:T(8,128)(2,1)S(1)} collective-permute-done((bf16[320,128]{1,0:T(8,128)(2,1)S(1)}, bf16[320,128]{1,0:T(8,128)(2,1)S(1)}, u32[]{:S(2)}, u32[]{:S(2)}) %collective-permute-start.14) | collective-permute-done | bytes 81952 | tf_op jit(solution)/shard_map/ppermute | solution.py:644
  60.9 0.4 collective-permute-start.18
  61.3 1.2 %collective-permute-start.17 = (bf16[128,128]{1,0:T(8,128)(2,1)S(1)}, bf16[128,128]{1,0:T(8,128)(2,1)S(1)}, u32[]{:S(2)}, u32[]{:S(2)}) collective-permute-start(bf16[128,128]{1,0:T(8,128)(2,1)S(1)} %get-tuple-element.61), channel_id=1, source_target_pairs={{0,2},{2,0},{1,3},{3,1},{4,6},{6,4},{5,7},{7,5},{8,10},{10,8},{9,1... | collective-permute-start | bytes 98312 | tf_op jit(solution)/shard_map/ppermute | solution.py:47
  62.6 0.3 collective-permute-start.16
  62.9 15.4 %all-gather = bf16[3072,128]{1,0:T(8,128)(2,1)S(1)} all-gather(bf16[384,128]{1,0:T(8,128)(2,1)S(1)} %add_convert_fusion), channel_id=2, replica_groups=mesh['groups'=2,'tm'=4,'head'=2,'rep'=2] {'tm','rep'}, dimensions={0}, use_global_device_ids=true | all-gather | bytes 884736 | tf_op jit(solution)/shard_map/all_gather | solution.py:691
  78.3 1.4 %shard_map.129 = (f32[128,1280]{1,0:T(8,128)}, f32[128,1280]{1,0:T(8,128)}, f32[128,1280]{1,0:T(8,128)}, f32[256,128]{1,0:T(8,128)}) custom-call(bf16[8,384,128]{2,1,0:T(8,128)(2,1)S(1)} %bitcast.1, bf16[896,128]{1,0:T(8,128)(2,1)S(1)} %get-tuple-element.60.refs_1_, bf16[896,128]{1,0:T(8,128)(2,1)S(1)} %collective-permute-done.16.refs_2_, ...), custom_call_target="tpu_custom_call" | custom-call | tf_op jit(solution)/shard_map/pallas_call | solution.py:608
  (36 shorter events, 0.3 us)
Async XLA Ops:
  0.6 13.0 %copy-start.3 = (bf16[128,1280]{1,0:T(8,128)(2,1)S(1)}, bf16[128,1280]{1,0:T(8,128)(2,1)}, u32[]{:S(2)}) copy-start(bf16[128,1280]{1,0:T(8,128)(2,1)} %do_ref.3) | copy-start | bytes 983044
  0.6 13.0 %copy-start.7 = (bf16[256,128]{1,0:T(8,128)(2,1)S(1)}, bf16[256,128]{1,0:T(8,128)(2,1)}, u32[]{:S(2)}) copy-start(bf16[256,128]{1,0:T(8,128)(2,1)} %t_ref.3) | copy-start | bytes 196612
  0.7 13.0 %copy-start.1 = (bf16[256,1280]{1,0:T(8,128)(2,1)S(1)}, bf16[256,1280]{1,0:T(8,128)(2,1)}, u32[]{:S(2)}) copy-start(bf16[256,1280]{1,0:T(8,128)(2,1)} %fv_ref.3) | copy-start | bytes 1966084
  0.7 13.0 %copy-start = (bf16[256,1280]{1,0:T(8,128)(2,1)S(1)}, bf16[256,1280]{1,0:T(8,128)(2,1)}, u32[]{:S(2)}) copy-start(bf16[256,1280]{1,0:T(8,128)(2,1)} %fk_ref.3) | copy-start | bytes 1966084
  0.7 13.0 %copy-start.2 = (bf16[128,1280]{1,0:T(8,128)(2,1)S(1)}, bf16[128,1280]{1,0:T(8,128)(2,1)}, u32[]{:S(2)}) copy-start(bf16[128,1280]{1,0:T(8,128)(2,1)} %fq_ref.3) | copy-start | bytes 983044
  3.5 23.6 %collective-permute-start = (bf16[128,1664]{1,0:T(8,128)(2,1)}, bf16[128,1664]{1,0:T(8,128)(2,1)S(1)}, u32[]{:S(2)}, u32[]{:S(2)}) collective-permute-start(bf16[128,1664]{1,0:T(8,128)(2,1)} %get-tuple-element.34), channel_id=1, source_target_pairs={{4,0},{0,4},{12,8},{8,12},{5,1},{1,5},{13,9},{9,13},{6,2},{2,6},{1... | collective-permute-start | bytes 1277960 | tf_op jit(solution)/shard_map/ppermute | solution.py:644
  6.5 14.1 %collective-permute-start.1 = (bf16[128,640]{1,0:T(8,128)(2,1)}, bf16[128,640]{1,0:T(8,128)(2,1)S(1)}, u32[]{:S(2)}, u32[]{:S(2)}) collective-permute-start(bf16[128,640]{1,0:T(8,128)(2,1)} %get-tuple-element.35), channel_id=1, source_target_pairs={{8,0},{12,4},{0,8},{4,12},{9,1},{13,5},{1,9},{5,13},{10,2},{14,6},... | collective-permute-start | bytes 491528 | tf_op jit(solution)/shard_map/ppermute | solution.py:644
  9.1 17.9 %collective-permute-start.2 = (bf16[128,640]{1,0:T(8,128)(2,1)}, bf16[128,640]{1,0:T(8,128)(2,1)S(1)}, u32[]{:S(2)}, u32[]{:S(2)}) collective-permute-start(bf16[128,640]{1,0:T(8,128)(2,1)} %get-tuple-element.36), channel_id=1, source_target_pairs={{12,0},{8,4},{4,8},{0,12},{13,1},{9,5},{5,9},{1,13},{14,2},{10,6},... | collective-permute-start | bytes 491528 | tf_op jit(solution)/shard_map/ppermute | solution.py:644
  9.1 18.0 %collective-permute-start.4 = (bf16[128,512]{1,0:T(8,128)(2,1)}, bf16[128,512]{1,0:T(8,128)(2,1)S(1)}, u32[]{:S(2)}, u32[]{:S(2)}) collective-permute-start(bf16[128,512]{1,0:T(8,128)(2,1)} %get-tuple-element.41), channel_id=1, source_target_pairs={{12,4},{0,8},{13,5},{1,9},{14,6},{2,10},{15,7},{3,11},{28,20},{16,... | collective-permute-start | bytes 393224 | tf_op jit(solution)/shard_map/ppermute | solution.py:644
  13.0 14.2 %collective-permute-start.5 = (bf16[128,512]{1,0:T(8,128)(2,1)}, bf16[128,512]{1,0:T(8,128)(2,1)S(1)}, u32[]{:S(2)}, u32[]{:S(2)}) collective-permute-start(bf16[128,512]{1,0:T(8,128)(2,1)} %get-tuple-element.42), channel_id=1, source_target_pairs={{8,4},{4,8},{9,5},{5,9},{10,6},{6,10},{11,7},{7,11},{24,20},{20,24... | collective-permute-start | bytes 393224 | tf_op jit(solution)/shard_map/ppermute | solution.py:644
  27.0 5.6 %copy-start.6 = (bf16[128,1280]{1,0:T(8,128)(2,1)S(1)}, bf16[128,1280]{1,0:T(8,128)(2,1)}, u32[]{:S(2)}) copy-start(bf16[128,1280]{1,0:T(8,128)(2,1)} %refs_14_.3) | copy-start | bytes 983044
  27.1 5.6 %copy-start.4 = (bf16[128,1280]{1,0:T(8,128)(2,1)S(1)}, bf16[128,1280]{1,0:T(8,128)(2,1)}, u32[]{:S(2)}) copy-start(bf16[128,1280]{1,0:T(8,128)(2,1)} %refs_12_.1) | copy-start | bytes 983044
  27.1 5.6 %copy-start.5 = (bf16[128,1280]{1,0:T(8,128)(2,1)S(1)}, bf16[128,1280]{1,0:T(8,128)(2,1)}, u32[]{:S(2)}) copy-start(bf16[128,1280]{1,0:T(8,128)(2,1)} %refs_13_.1) | copy-start | bytes 983044
  27.1 5.5 %collective-permute-start.3 = (bf16[128,1152]{1,0:T(8,128)(2,1)S(1)}, bf16[128,1152]{1,0:T(8,128)(2,1)S(1)}, u32[]{:S(2)}, u32[]{:S(2)}) collective-permute-start(bf16[128,1152]{1,0:T(8,128)(2,1)S(1)} %shard_map.122), channel_id=1, source_target_pairs={{0,1},{1,0},{2,3},{3,2},{4,5},{5,4},{6,7},{7,6},{8,9},{9,8},{10,11... | collective-permute-start | bytes 884744 | tf_op jit(solution)/shard_map/ppermute | solution.py:47
  27.2 5.4 %collective-permute-start.6 = (bf16[128,768]{1,0:T(8,128)(2,1)S(1)}, bf16[128,768]{1,0:T(8,128)(2,1)S(1)}, u32[]{:S(2)}, u32[]{:S(2)}) collective-permute-start(bf16[128,768]{1,0:T(8,128)(2,1)S(1)} %shard_map.123), channel_id=1, source_target_pairs={{0,1},{1,0},{2,3},{3,2},{4,5},{5,4},{6,7},{7,6},{8,9},{9,8},{10,11... | collective-permute-start | bytes 589832 | tf_op jit(solution)/shard_map/ppermute | solution.py:47
  27.8 13.5 %collective-permute-start.8 = (bf16[128,512]{1,0:T(8,128)(2,1)S(1)}, bf16[128,512]{1,0:T(8,128)(2,1)S(1)}, u32[]{:S(2)}, u32[]{:S(2)}) collective-permute-start(bf16[128,512]{1,0:T(8,128)(2,1)S(1)} %get-tuple-element.47), channel_id=1, source_target_pairs={{8,0},{12,4},{0,8},{4,12},{9,1},{13,5},{1,9},{5,13},{10,2},{14,6},... | collective-permute-start | bytes 393224 | tf_op jit(solution)/shard_map/ppermute | solution.py:644
  31.2 10.0 %collective-permute-start.9 = (bf16[128,512]{1,0:T(8,128)(2,1)S(1)}, bf16[128,512]{1,0:T(8,128)(2,1)S(1)}, u32[]{:S(2)}, u32[]{:S(2)}) collective-permute-start(bf16[128,512]{1,0:T(8,128)(2,1)S(1)} %get-tuple-element.48), channel_id=1, source_target_pairs={{12,0},{8,4},{4,8},{0,12},{13,1},{9,5},{5,9},{1,13},{14,2},{10,6},... | collective-permute-start | bytes 393224 | tf_op jit(solution)/shard_map/ppermute | solution.py:644
  32.6 0.7 copy-start.8
  37.2 4.0 %collective-permute-start.7 = (bf16[384,128]{1,0:T(8,128)(2,1)S(1)}, bf16[384,128]{1,0:T(8,128)(2,1)S(1)}, u32[]{:S(2)}, u32[]{:S(2)}) collective-permute-start(bf16[384,128]{1,0:T(8,128)(2,1)S(1)} %get-tuple-element.45), channel_id=1, source_target_pairs={{0,1},{1,0},{2,3},{3,2},{4,5},{5,4},{6,7},{7,6},{8,9},{9,8},{10,11... | collective-permute-start | bytes 294920 | tf_op jit(solution)/shard_map/ppermute | solution.py:47
  41.3 1.8 %collective-permute-start.10 = (bf16[128,1536]{1,0:T(8,128)(2,1)S(1)}, bf16[128,1536]{1,0:T(8,128)(2,1)S(1)}, u32[]{:S(2)}, u32[]{:S(2)}) collective-permute-start(bf16[128,1536]{1,0:T(8,128)(2,1)S(1)} %shard_map.125), channel_id=1, source_target_pairs={{0,1},{1,0},{2,3},{3,2},{4,5},{5,4},{6,7},{7,6},{8,9},{9,8},{10,11... | collective-permute-start | bytes 1179656 | tf_op jit(solution)/shard_map/ppermute | solution.py:47
  46.9 1.4 %collective-permute-start.11 = (bf16[352,128]{1,0:T(8,128)(2,1)S(1)}, bf16[352,128]{1,0:T(8,128)(2,1)S(1)}, u32[]{:S(2)}, u32[]{:S(2)}) collective-permute-start(bf16[352,128]{1,0:T(8,128)(2,1)S(1)} %get-tuple-element.53), channel_id=1, source_target_pairs={{0,1},{1,0},{2,3},{3,2},{4,5},{5,4},{6,7},{7,6},{8,9},{9,8},{10,11... | collective-permute-start | bytes 270344 | tf_op jit(solution)/shard_map/ppermute | solution.py:47
  47.1 1.3 %collective-permute-start.12 = (bf16[352,128]{1,0:T(8,128)(2,1)S(1)}, bf16[352,128]{1,0:T(8,128)(2,1)S(1)}, u32[]{:S(2)}, u32[]{:S(2)}) collective-permute-start(bf16[352,128]{1,0:T(8,128)(2,1)S(1)} %get-tuple-element.54), channel_id=1, source_target_pairs={{0,1},{1,0},{2,3},{3,2},{4,5},{5,4},{6,7},{7,6},{8,9},{9,8},{10,11... | collective-permute-start | bytes 270344 | tf_op jit(solution)/shard_map/ppermute | solution.py:47
  48.5 6.1 %collective-permute-start.13 = (bf16[320,128]{1,0:T(8,128)(2,1)S(1)}, bf16[320,128]{1,0:T(8,128)(2,1)S(1)}, u32[]{:S(2)}, u32[]{:S(2)}) collective-permute-start(bf16[320,128]{1,0:T(8,128)(2,1)S(1)} %get-tuple-element.57), channel_id=1, source_target_pairs={{4,0},{0,4},{12,8},{8,12},{5,1},{1,5},{13,9},{9,13},{6,2},{2,6},{1... | collective-permute-start | bytes 245768 | tf_op jit(solution)/shard_map/ppermute | solution.py:644
  51.7 9.2 %collective-permute-start.14 = (bf16[320,128]{1,0:T(8,128)(2,1)S(1)}, bf16[320,128]{1,0:T(8,128)(2,1)S(1)}, u32[]{:S(2)}, u32[]{:S(2)}) collective-permute-start(bf16[320,128]{1,0:T(8,128)(2,1)S(1)} %get-tuple-element.58), channel_id=1, source_target_pairs={{8,0},{12,4},{0,8},{4,12},{9,1},{13,5},{1,9},{5,13},{10,2},{14,6},... | collective-permute-start | bytes 245768 | tf_op jit(solution)/shard_map/ppermute | solution.py:644
  51.7 9.2 %collective-permute-start.15 = (bf16[320,128]{1,0:T(8,128)(2,1)S(1)}, bf16[320,128]{1,0:T(8,128)(2,1)S(1)}, u32[]{:S(2)}, u32[]{:S(2)}) collective-permute-start(bf16[320,128]{1,0:T(8,128)(2,1)S(1)} %get-tuple-element.59), channel_id=1, source_target_pairs={{12,0},{8,4},{4,8},{0,12},{13,1},{9,5},{5,9},{1,13},{14,2},{10,6},... | collective-permute-start | bytes 245768 | tf_op jit(solution)/shard_map/ppermute | solution.py:644
  60.9 17.4 %collective-permute-start.18 = (bf16[128,128]{1,0:T(8,128)(2,1)S(1)}, bf16[128,128]{1,0:T(8,128)(2,1)S(1)}, u32[]{:S(2)}, u32[]{:S(2)}) collective-permute-start(bf16[128,128]{1,0:T(8,128)(2,1)S(1)} %get-tuple-element.61), channel_id=1, source_target_pairs={{0,3},{1,2},{2,1},{3,0},{4,7},{5,6},{6,5},{7,4},{8,11},{9,10},{10,... | collective-permute-start | bytes 98312 | tf_op jit(solution)/shard_map/ppermute | solution.py:697
  61.3 17.0 %collective-permute-start.17 = (bf16[128,128]{1,0:T(8,128)(2,1)S(1)}, bf16[128,128]{1,0:T(8,128)(2,1)S(1)}, u32[]{:S(2)}, u32[]{:S(2)}) collective-permute-start(bf16[128,128]{1,0:T(8,128)(2,1)S(1)} %get-tuple-element.61), channel_id=1, source_target_pairs={{0,2},{2,0},{1,3},{3,1},{4,6},{6,4},{5,7},{7,5},{8,10},{10,8},{9,1... | collective-permute-start | bytes 98312 | tf_op jit(solution)/shard_map/ppermute | solution.py:47
  62.6 15.7 %collective-permute-start.16 = (bf16[896,128]{1,0:T(8,128)(2,1)S(1)}, bf16[896,128]{1,0:T(8,128)(2,1)S(1)}, u32[]{:S(2)}, u32[]{:S(2)}) collective-permute-start(bf16[896,128]{1,0:T(8,128)(2,1)S(1)} %get-tuple-element.60.refs_1_), channel_id=1, source_target_pairs={{0,1},{1,0},{2,3},{3,2},{4,5},{5,4},{6,7},{7,6},{8,9},{9,8},{10,11... | collective-permute-start | bytes 688136 | tf_op jit(solution)/shard_map/ppermute | solution.py:47

commit v8 on v7

--- a/solution.py
+++ b/solution.py
@@ -13,6 +13,7 @@
 SCALE = DH ** (-0.5)
 F32 = jnp.float32
 BF16 = jnp.bfloat16
+GIVES = 4
 SMALL = pltpu.CompilerParams(vmem_limit_bytes=16 * 1024 * 1024)
 
 
@@ -265,14 +266,16 @@
 
 def pack_kernel(frames, outputs, fq_ref, do_ref, fk_ref, fv_ref, t_ref, *refs):
     outs, (q_in, do_in, k_in, v_in, k2_in, v2_in, t_in, sems) = refs[:-8], refs[-8:]
+    wanted = {what for parts in outputs for _, _, what in parts}
     me, half = lax.axis_index("tm"), lax.axis_index("rep")
     rows = fq_ref.shape[0]
     mine = pl.ds(pl.multiple_of(half * rows, rows), rows)
     rest = pl.ds(pl.multiple_of((1 - half) * rows, rows), rows)
     moves = [
-        (fq_ref, q_in), (do_ref, do_in), (fk_ref.at[mine, :], k_in), (fv_ref.at[mine, :], v_in),
-        (fk_ref.at[rest, :], k2_in), (fv_ref.at[rest, :], v2_in), (t_ref, t_in),
+        (fq_ref, q_in), (do_ref, do_in), (fk_ref.at[mine, :], k_in), (fv_ref.at[mine, :], v_in), (t_ref, t_in)
     ]
+    if "other" in wanted:
+        moves += [(fk_ref.at[rest, :], k2_in), (fv_ref.at[rest, :], v2_in)]
     copies = [pltpu.make_async_copy(a, b, sems.at[n]) for n, (a, b) in enumerate(moves)]
     for copy in copies:
         copy.start()
@@ -413,7 +416,7 @@
     arrays, adapters = take(count), take(3)
     before = take(2) if chained else None
     take(waits)
-    keep_ref, *give_refs = take(3 if chained else 2)
+    keep_ref, *give_refs = take(1 + GIVES if chained else 2)
     low_refs = [] if chained else take(2)
     q, do, k, v, tokens = refs
     me, half = lax.axis_index("tm"), lax.axis_index("rep")
@@ -448,7 +451,7 @@
         keep_ref[:cut, :] = keep
         keep_ref[cut:, :] = before[0][...] + low_same
         give = jnp.concatenate([give, before[1][...] + low_other], axis=0)
-        size = give.shape[0] // 2
+        size = give.shape[0] // GIVES
         for n, ref in enumerate(give_refs):
             ref[...] = give[n * size : (n + 1) * size].astype(ref.dtype)
         return
@@ -500,8 +503,8 @@
     specs += [pl.BlockSpec(memory_space=pl.ANY)] * len(after)
     low = jax.ShapeDtypeStruct((flat, rank), F32)
     if chained:
-        half = jax.ShapeDtypeStruct(((size + flat) // 2, rank), BF16)
-        shapes = [jax.ShapeDtypeStruct((size + flat, rank), F32), half, half]
+        part = jax.ShapeDtypeStruct(((size + flat) // GIVES, rank), BF16)
+        shapes = [jax.ShapeDtypeStruct((size + flat, rank), F32)] + [part] * GIVES
     else:
         edge = jax.ShapeDtypeStruct((size, rank), F32)
         shapes = [edge, jax.ShapeDtypeStruct((size, rank), BF16), low, low]
@@ -520,7 +523,7 @@
 
 
 def hand_out_kernel(frames, size, parts, keep_ref, *refs):
-    gots, (own_ref, *sends, total) = refs[:parts], refs[parts:]
+    gots, (piece, facing), (own_ref, *sends, total) = refs[:parts], refs[parts : parts + 2], refs[-frames - 2 :]
     me = lax.axis_index("tm")
     rows = own_ref.shape[0]
     total[...] = keep_ref[...] + jnp.concatenate([got[...].astype(F32) for got in gots], axis=0)
@@ -530,24 +533,26 @@
         if m == 0:
             own_ref[...] = low
         sends[m][:rows, :] = low.astype(BF16)
-        sends[m][rows:, :] = grads
-
-
-def hand_out(frames, rows, keep, gots):
+        sends[m][rows : rows + size, :] = grads
+    sends[1][rows + size : rows + 3 * size, :] = piece[...]
+    sends[1][rows + 3 * size :, :] = facing[size:, :]
+
+
+def hand_out(frames, rows, keep, gots, piece, facing, after):
     size, rank = keep.shape[0] - frames * rows, keep.shape[1]
-    send = jax.ShapeDtypeStruct((rows + size, rank), BF16)
+    sends = [jax.ShapeDtypeStruct((rows + size * (4 if m == 1 else 1), rank), BF16) for m in range(frames)]
     return pl.pallas_call(
         functools.partial(hand_out_kernel, frames, size, len(gots)),
-        in_specs=vmem(1 + len(gots)),
+        in_specs=vmem(3 + len(gots)) + [pl.BlockSpec(memory_space=pl.ANY)] * len(after),
         out_specs=vmem(frames + 1),
-        out_shape=[jax.ShapeDtypeStruct((rows, rank), F32)] + [send] * frames,
+        out_shape=[jax.ShapeDtypeStruct((rows, rank), F32)] + sends,
         scratch_shapes=[pltpu.VMEM(keep.shape, F32)],
         compiler_params=SMALL,
-    )(keep, *gots)
-
-
-def collect_kernel(frames, own_ref, *refs):
-    gots, (out_ref, low_ref) = refs[:frames], refs[-2:]
+    )(keep, *gots, piece, facing, *after)
+
+
+def collect_kernel(frames, wide, own_ref, *refs):
+    gots, (piece, far, facing), (out_ref, low_ref) = refs[:frames], refs[frames : frames + 3], refs[-2:]
     rows = own_ref.shape[0]
     size = gots[0].shape[0] - rows
     low = own_ref[...]
@@ -555,28 +560,32 @@
         low = low + gots[m][:rows, :].astype(F32)
     out_ref[:rows, :] = low.astype(BF16)
     low_ref[...] = low.astype(BF16)
-    for m in range(frames):
-        out_ref[rows + m * size : rows + (m + 1) * size, :] = gots[m][rows:, :]
-
-
-def collect(own, gots):
+    near = rows + size
+    middle = lookup(wide, lax.axis_index("tm")) > 0
+    blocks = [got[rows:near, :] for got in gots]
+    blocks += [piece[:size, :], gots[1][near : near + size, :], far[...], facing[:size, :]]
+    blocks.append(jnp.where(middle, piece[size:, :], gots[1][near + size : near + 2 * size, :]))
+    blocks.append(jnp.where(middle, facing[size:, :], gots[1][near + 2 * size :, :]))
+    for n, block in enumerate(blocks):
+        out_ref[rows + n * size : rows + (n + 1) * size, :] = block
+
+
+def collect(wide, own, gots, piece, far, facing):
     frames, (rows, rank) = len(gots), own.shape
     size = gots[0].shape[0] - rows
     return pl.pallas_call(
-        functools.partial(collect_kernel, frames),
-        in_specs=vmem(frames + 1),
+        functools.partial(collect_kernel, frames, wide),
+        in_specs=vmem(frames + 4),
         out_specs=vmem(2),
         out_shape=[
-            jax.ShapeDtypeStruct((rows + frames * size, rank), BF16),
+            jax.ShapeDtypeStruct((rows + (2 * frames + 2) * size, rank), BF16),
             jax.ShapeDtypeStruct((rows, rank), BF16),
         ],
         compiler_params=SMALL,
-    )(own, *gots)
-
-
-def place_kernel(early, late, *refs):
-    frames = len(late[0])
-    all_ref, tail, tail2, low_head, low_diag, *outs = refs
+    )(own, *gots, piece, far, facing)
+
+
+def place_kernel(frames, lead, late, rest, tail, tail2, low_head, low_diag, *outs):
     me, half = lax.axis_index("tm"), lax.axis_index("rep")
     first = half == 0
     rank = outs[0].shape[0]
@@ -586,33 +595,27 @@
     other = tail2[:rows, :].astype(F32) + low_diag[...].astype(F32)
     outs[3][:rows, :] = jnp.where(first, same, other)
     outs[3][rows:, :] = jnp.where(first, other, same)
-    def write(cols, a, b):
-        both = jnp.concatenate([a.astype(F32), b.astype(F32)], axis=0)
+    side = me // 2
+    places = [lookup(late, me ^ m) for m in range(frames)] + [lookup(lead, me ^ m) for m in range(frames)]
+    places += [lookup(rest, 1 + side), lookup(rest, 2 - side)]
+    for n, head in enumerate(places):
+        here = slice(rows + n * cut, rows + (n + 1) * cut)
+        a, b = tail[here, :].astype(F32), tail2[here, :].astype(F32)
+        both = jnp.concatenate([jnp.where(first, a, b), jnp.where(first, b, a)], axis=0)
         for o in range(3):
-            outs[o][:, cols] = both[o * rank : (o + 1) * rank]
-
-    for chip in range(frames):
-        for n, (table, numbers) in enumerate(early):
-            here = slice(n * cut, (n + 1) * cut)
-            if numbers[chip]:
-                cols = slice(table[chip] * DH, (table[chip] + 1) * DH)
-                write(cols, all_ref[2 * chip, here, :], all_ref[2 * chip + 1, here, :])
-    for m in range(frames):
-        here = slice(rows + m * cut, rows + (m + 1) * cut)
-        a, b = tail[here, :], tail2[here, :]
-        write(column(lookup(late[0], me ^ m)), jnp.where(first, a, b), jnp.where(first, b, a))
-
-
-def place(early, late, everything, tail, tail2, low_head, low_diag, rank, width):
+            outs[o][:, column(head)] = both[o * rank : (o + 1) * rank]
+
+
+def place(frames, lead, late, rest, tail, tail2, low_head, low_diag, rank, width):
     rows = low_head.shape[0]
     return pl.pallas_call(
-        functools.partial(place_kernel, early, late),
-        in_specs=vmem(5),
+        functools.partial(place_kernel, frames, lead, late, rest),
+        in_specs=vmem(4),
         out_specs=vmem(4),
         out_shape=[jax.ShapeDtypeStruct((rank, width), F32)] * 3
         + [jax.ShapeDtypeStruct((2 * rows, rank), F32)],
         compiler_params=SMALL,
-    )(everything, tail, tail2, low_head, low_diag)
+    )(tail, tail2, low_head, low_diag)
 
 
 def exchange_plan(
@@ -640,8 +643,13 @@
     adapters = [query_adapter_out, key_adapter_out, value_adapter_out]
     arrays = (frozen_query, out_grad, frozen_key, frozen_value, token_adapter_input)
 
-    def meet(block, m, targets=range(frames)):
-        return lax.ppermute(block, "tm", [(j ^ m, j) for j in targets])
+    def meet(name, block, m, targets=range(frames)):
+        with jax.named_scope(f"{name}_over_tm"):
+            return lax.ppermute(block, "tm", [(j ^ m, j) for j in targets])
+
+    def swap_in_chip(name, block):
+        with jax.named_scope(f"{name}_in_chip"):
+            return swap(block, "rep")
 
     def mine(slot, m):
         return (slot[0], m, "mine")
@@ -660,43 +668,47 @@
     packed = pack(frames, sent, 56, *arrays)
     packed_late = pack(frames, sent_late + kept, 16, *arrays)
     kept = packed_late[len(sent_late) :]
-    block = meet(packed[0], 1)
+    block = meet("nearest", packed[0], 1)
     lead_got, rest_got, late_got = [(block, 0)], [(block, 4 * DH + rank)], [(block, 8 * DH + rank)]
     for m in range(2, frames):
-        lead_got.append((meet(packed[2 * m - 3], m), 0))
-        rest_got.append((meet(packed[2 * m - 2], m, wide), 0))
-        late_got.append((meet(packed_late[m - 2], m), 0))
-
-    def sides(n, got, wide_t, apart, after=()):
-        skip = 0 if n == 2 else 2 * DH
+        lead_got.append((meet("lead", packed[2 * m - 3], m), 0))
+        rest_got.append((meet("rest", packed[2 * m - 2], m, wide), 0))
+        late_got.append((meet("late", packed_late[m - 2], m), 0))
+
+    def sides(name, n, got, wide_t, apart, skip, after=()):
         size = 4 * DH - skip + (rank if wide_t else 0)
         picked = pick([(a, start + skip) for a, start in got], size, apart, after)
-        cross = [swap(block, "rep") for block in picked]
-        cross = [(cross[m], 2 * DH - skip) if apart else (cross[0], m * size + 2 * DH - skip) for m in range(frames - 1)]
+        cross = [swap_in_chip(name, block) for block in picked]
+        where = 2 * DH - skip
+        cross = [(cross[m], where) if apart else (cross[0], m * size + where) for m in range(frames - 1)]
         rows_here = [(kept[2 * n], 0)] + got
         rows_there = [(kept[2 * n + 1], 0)] + cross
         return rows_here, rows_there, cross
 
-    *lead_side, cross = sides(0, lead_got, True, False, kept[:1])
+    *lead_side, cross = sides("lead", 0, lead_got, True, False, 2 * DH, kept[:1])
     t_side = (
         [(kept[6], 0)] + [(a, start + 4 * DH) for a, start in lead_got],
         [(kept[7], 0)] + [(block, start + 2 * DH) for block, start in cross],
     )
-    *rest_side, _ = sides(1, rest_got, False, False)
+    *rest_side, _ = sides("rest", 1, rest_got, False, False, 2 * DH)
     early = [lead, rest]
     keep, give, *low = head_group(early, band_width, [t_side, lead_side, rest_side], adapters)
-    got = swap(give, "rep")
-    *late_side, _ = sides(2, late_got, False, False, [got])
+    got = swap_in_chip("early_gradients", give)
     piece = (keep + got.astype(F32)).astype(BF16)
-    everything = lax.all_gather(piece, ("tm", "rep"))
-    keep, *gives = head_group([late], band_width, [t_side, late_side], adapters, low)
-    own, *sends = hand_out(frames, rows, keep, [swap(g, "rep") for g in gives])
-    gots = [sends[0]] + [meet(sends[m], m) for m in range(1, frames)]
-    tail, low = collect(own, gots)
+    *late_side, _ = sides("late", 2, late_got, False, False, 0, [got])
+    cut = 3 * rank // 2
+    far = meet("early_gradients", piece[:cut], 2)
+    facing = meet("early_gradients", piece, 3)
+    keep, *gives = head_group([late], band_width, [t_side, late_side], adapters, low, [piece])
+    gives = [swap_in_chip("late_sums", g) for g in gives]
+    own, *sends = hand_out(frames, rows, keep, gives, piece, facing, [far])
+    gots = [sends[0]] + [meet("late_sums", sends[m], m) for m in range(1, frames)]
+    tail, low = collect(rest[1], own, gots, piece, far, facing)
     diag = [(0, 3), (1, 2), (2, 1), (3, 0)]
-    low_head, low_diag = swap(low, "head"), lax.ppermute(low, ("head", "rep"), diag)
+    with jax.named_scope("low_over_head"):
+        low_head, low_diag = swap(low, "head"), lax.ppermute(low, ("head", "rep"), diag)
     outs = place(
-        early, late, everything, tail, swap(tail, "rep"), low_head, low_diag, rank, width
+        frames, lead[0], late[0], rest[0], tail, swap_in_chip("tail", tail), low_head, low_diag, rank, width
     )
     return tuple(outs)
 
@@ -704,7 +716,7 @@
 def on_device(frozen_query, *rest):
     frames = rest[-1].shape[0]
     heads = frozen_query.shape[1] // DH
-    whole_reach = frames <= REACH + 1 and frames & (frames - 1) == 0 and 2 * frames < heads < 3 * frames
+    whole_reach = frames == 4 and heads == 2 * frames + 2
     return (exchange_plan if whole_reach else window_plan)(frozen_query, *rest)
 
 

time: 79.9 us -> 71.7 us (0.90)
  blocking collectives: 15.4 us -> 0 us
  starting transfers between devices: 23.9 us -> 27.5 us
  waiting for transfers between devices: 25.7 us -> 29.2 us
    all_gather x1 -> x0, blocking collectives: 15.4 us -> none  [exchange_plan(): everything = lax.all_gather(piece, ('tm', 'rep'))]
    ppermute x10 -> x12, starting transfers between devices: 20.6 us -> 24.1 us  [meet(): return lax.ppermute(block, 'tm', [(j ^ m, j) for j in targets])]
    ppermute x10 -> x12, waiting for transfers between devices: 23.1 us -> 25 us  [meet(): return lax.ppermute(block, 'tm', [(j ^ m, j) for j in targets])]
    ppermute x1, waiting for transfers between devices: 0.01 us -> 0.92 us  [exchange_plan(): lax.ppermute(low, ('head', 'rep'), diag)]
    ppermute x8 -> x10, waiting for transfers between devices: 2.66 us -> 3.27 us  [swap(): return lax.ppermute(block, axis, [(0, 1), (1, 0)])]
    ppermute x8 -> x10, starting transfers between devices: 2.84 us -> 3.1 us  [swap(): return lax.ppermute(block, axis, [(0, 1), (1, 0)])]
  transfers between devices with their start and end apart: 19 -> 23, of which waited for: 8 -> 10; matrix products, arithmetic and copies ran while one was open for 0% -> 0% of each run, Pallas kernels for 6% -> 13%
where the time goes in v8:
time: 71.7 us; the launch traced here: 71.5 us
  waiting for transfers between devices  29.2 us (41%)
  starting transfers between devices  27.5 us (38%)
  Pallas kernels  13.2 us (18%)
  between operations  0.92 us (1%)
    ppermute x12, waiting for transfers between devices, meet(): return lax.ppermute(block, 'tm', [(j ^ m, j) for j in targets])  25 us
    ppermute x12, starting transfers between devices, meet(): return lax.ppermute(block, 'tm', [(j ^ m, j) for j in targets])  24.1 us
    pallas_call x2, Pallas kernels, head_group(): pl.pallas_call(functools.partial(group_kernel, heads, frames, chained, le...  7.97 us
    pallas_call x2, Pallas kernels, pack(): pl.pallas_call(functools.partial(pack_kernel, frames, outputs), in_specs=...  3.51 us
    ppermute x10, waiting for transfers between devices, swap(): return lax.ppermute(block, axis, [(0, 1), (1, 0)])  3.27 us
    ppermute x10, starting transfers between devices, swap(): return lax.ppermute(block, axis, [(0, 1), (1, 0)])  3.1 us
    pallas_call x1, Pallas kernels, place(): pl.pallas_call(functools.partial(place_kernel, frames, lead, late, rest),...  1.47 us
  transfers between devices with their start and end apart: 23, of which 10 were waited for; matrix products, arithmetic and copies ran while one was open for 0% of the time, Pallas kernels for 13%

profile of v8, /device:TPU:0, one launch (start us, length us, event | category | flops | bytes accessed | tf_op | source)
XLA Modules:
  0.0 71.5 jit_solution(15998808962740301058)
XLA Ops:
  0.7 2.6 %shard_map.121 = (bf16[128,1664]{1,0:T(8,128)(2,1)}, bf16[128,640]{1,0:T(8,128)(2,1)}, bf16[128,512]{1,0:T(8,128)(2,1)}, bf16[128,640]{1,0:T(8,128)(2,1)}, bf16[128,512]{1,0:T(8,128)(2,1)}) custom-call(bf16[128,1280]{1,0:T(8,128)(2,1)} %fq_ref.3, bf16[128,1280]{1,0:T(8,128)(2,1)} %do_ref.3, bf16[256,1280]{1,0:T(8,128)(2,1)} %fk_ref.3, ...), custom_call_target="tpu_custom_call" | custom-call | tf_op jit(solution)/shard_map/pallas_call | solution.py:301
  3.3 3.1 %collective-permute-start = (bf16[128,1664]{1,0:T(8,128)(2,1)}, bf16[128,1664]{1,0:T(8,128)(2,1)S(1)}, u32[]{:S(2)}, u32[]{:S(2)}) collective-permute-start(bf16[128,1664]{1,0:T(8,128)(2,1)} %get-tuple-element.36), channel_id=1, source_target_pairs={{4,0},{0,4},{12,8},{8,12},{5,1},{1,5},{13,9},{9,13},{6,2},{2,6},{1... | collective-permute-start | bytes 1277960 | tf_op jit(solution)/shard_map/nearest_over_tm/ppermute | solution.py:648
  6.3 2.6 %collective-permute-start.1 = (bf16[128,640]{1,0:T(8,128)(2,1)}, bf16[128,640]{1,0:T(8,128)(2,1)S(1)}, u32[]{:S(2)}, u32[]{:S(2)}) collective-permute-start(bf16[128,640]{1,0:T(8,128)(2,1)} %get-tuple-element.37), channel_id=1, source_target_pairs={{8,0},{12,4},{0,8},{4,12},{9,1},{13,5},{1,9},{5,13},{10,2},{14,6},... | collective-permute-start | bytes 491528 | tf_op jit(solution)/shard_map/lead_over_tm/ppermute | solution.py:648
  8.9 3.8 %collective-permute-start.6 = (bf16[128,512]{1,0:T(8,128)(2,1)}, bf16[128,512]{1,0:T(8,128)(2,1)S(1)}, u32[]{:S(2)}, u32[]{:S(2)}) collective-permute-start(bf16[128,512]{1,0:T(8,128)(2,1)} %get-tuple-element.47), channel_id=1, source_target_pairs={{12,4},{0,8},{13,5},{1,9},{14,6},{2,10},{15,7},{3,11},{28,20},{16,... | collective-permute-start | bytes 393224 | tf_op jit(solution)/shard_map/rest_over_tm/ppermute | solution.py:648
  12.8 0.7 collective-permute-start.7
  13.5 0.9 %shard_map.120 = (bf16[128,512]{1,0:T(8,128)(2,1)S(1)}, bf16[128,512]{1,0:T(8,128)(2,1)S(1)}, bf16[128,512]{1,0:T(8,128)(2,1)S(1)}, bf16[128,256]{1,0:T(8,128)(2...) custom-call(bf16[128,1280]{1,0:T(8,128)(2,1)S(1)} %copy-done.2, ...), custom_call_target="tpu_custom_call" | custom-call | tf_op jit(solution)/shard_map/pallas_call | solution.py:301
  14.4 6.0 %collective-permute-done.1.refs_1_.refs_3_ = bf16[128,640]{1,0:T(8,128)(2,1)S(1)} collective-permute-done((bf16[128,640]{1,0:T(8,128)(2,1)}, bf16[128,640]{1,0:T(8,128)(2,1)S(1)}, u32[]{:S(2)}, u32[]{:S(2)}) %collective-permute-start.1) | collective-permute-done | bytes 163872 | tf_op jit(solution)/shard_map/lead_over_tm/ppermute | solution.py:648
  20.4 6.4 %collective-permute-done.2.refs_2_.refs_4_ = bf16[128,640]{1,0:T(8,128)(2,1)S(1)} collective-permute-done((bf16[128,640]{1,0:T(8,128)(2,1)}, bf16[128,640]{1,0:T(8,128)(2,1)S(1)}, u32[]{:S(2)}, u32[]{:S(2)}) %collective-permute-start.2) | collective-permute-done | bytes 163872 | tf_op jit(solution)/shard_map/lead_over_tm/ppermute | solution.py:648
  27.0 0.5 collective-permute-start.8
  27.6 3.5 %collective-permute-start.4 = (bf16[128,512]{1,0:T(8,128)(2,1)S(1)}, bf16[128,512]{1,0:T(8,128)(2,1)S(1)}, u32[]{:S(2)}, u32[]{:S(2)}) collective-permute-start(bf16[128,512]{1,0:T(8,128)(2,1)S(1)} %get-tuple-element.42), channel_id=1, source_target_pairs={{8,0},{12,4},{0,8},{4,12},{9,1},{13,5},{1,9},{5,13},{10,2},{14,6},... | collective-permute-start | bytes 393224 | tf_op jit(solution)/shard_map/late_over_tm/ppermute | solution.py:648
  31.0 1.4 %collective-permute-start.5 = (bf16[128,512]{1,0:T(8,128)(2,1)S(1)}, bf16[128,512]{1,0:T(8,128)(2,1)S(1)}, u32[]{:S(2)}, u32[]{:S(2)}) collective-permute-start(bf16[128,512]{1,0:T(8,128)(2,1)S(1)} %get-tuple-element.43), channel_id=1, source_target_pairs={{12,0},{8,4},{4,8},{0,12},{13,1},{9,5},{5,9},{1,13},{14,2},{10,6},... | collective-permute-start | bytes 393224 | tf_op jit(solution)/shard_map/late_over_tm/ppermute | solution.py:648
  32.4 0.6 copy-done.8
  33.1 4.1 %shard_map.124 = (f32[384,128]{1,0:T(8,128)S(1)}, bf16[384,128]{1,0:T(8,128)(2,1)S(1)}, f32[512,128]{1,0:T(8,128)S(1)}, f32[512,128]{1,0:T(8,128)S(1)}) custom-call(s32[4,4]{1,0:T(4,128)S(1)} %copy-done.8, bf16[128,128]{1,0:T(8,128)(2,1)S(1)} %get-tuple-element.35.refs_1_, bf16[128,1664]{1,0:T(8,128)(2,1)S(1)} %collective-permute-done.refs_0_.refs_2_, ...), custom_call_target="tpu_custom_call" | custom-call | tf_op jit(solution)/shard_map/pallas_call | solution.py:511
  37.3 3.8 %collective-permute-done.4.refs_1_.refs_8_ = bf16[128,512]{1,0:T(8,128)(2,1)S(1)} collective-permute-done((bf16[128,512]{1,0:T(8,128)(2,1)S(1)}, bf16[128,512]{1,0:T(8,128)(2,1)S(1)}, u32[]{:S(2)}, u32[]{:S(2)}) %collective-permute-start.4) | collective-permute-done | bytes 131104 | tf_op jit(solution)/shard_map/late_over_tm/ppermute | solution.py:648
  41.2 1.4 %collective-permute-start.15 = (bf16[384,128]{1,0:T(8,128)(2,1)S(1)}, bf16[384,128]{1,0:T(8,128)(2,1)S(1)}, u32[]{:S(2)}, u32[]{:S(2)}) collective-permute-start(bf16[384,128]{1,0:T(8,128)(2,1)S(1)} %add_convert_fusion.refs_17_.refs_4_), channel_id=1, source_target_pairs={{12,0},{8,4},{4,8},{0,12},{13,1},{9,5},{5,9},{1,13},{14,2},{10,6},... | collective-permute-start | bytes 294920 | tf_op jit(solution)/shard_map/early_gradients_over_tm/ppermute | solution.py:648
  42.6 3.2 %collective-permute-start.16 = (bf16[192,128]{1,0:T(8,128)(2,1)S(1)}, bf16[192,128]{1,0:T(8,128)(2,1)S(1)}, u32[]{:S(2)}, u32[]{:S(2)}) collective-permute-start(bf16[192,128]{1,0:T(8,128)(2,1)S(1)} %slice.4), channel_id=1, source_target_pairs={{8,0},{12,4},{0,8},{4,12},{9,1},{13,5},{1,9},{5,13},{10,2},{14,6},... | collective-permute-start | bytes 147464 | tf_op jit(solution)/shard_map/early_gradients_over_tm/ppermute | solution.py:648
  45.8 3.9 %shard_map.126 = (f32[704,128]{1,0:T(8,128)S(1)}, bf16[176,128]{1,0:T(8,128)(2,1)S(1)}, bf16[176,128]{1,0:T(8,128)(2,1)S(1)}, bf16[176,128]{1,0:T(8,128)(2,1)S(1)}, bf16[176,128]{1,0:T(8,128)(2,1)S(1)}) custom-call(s32[4,4]{1,0:T(4,128)S(1)} %copy-done.8, bf16[128,128]{1,0:T(8,128)(2,1)S(1)} %get-tuple-element.35.refs_1_, ...), custom_call_target="tpu_custom_call" | custom-call | tf_op jit(solution)/shard_map/pallas_call | solution.py:511
  49.8 0.5 collective-permute-start.12
  50.3 0.1 collective-permute-start.13
  50.4 2.1 %collective-permute-done.16.refs_6_.refs_5_ = bf16[192,128]{1,0:T(8,128)(2,1)S(1)} collective-permute-done((bf16[192,128]{1,0:T(8,128)(2,1)S(1)}, bf16[192,128]{1,0:T(8,128)(2,1)S(1)}, u32[]{:S(2)}, u32[]{:S(2)}) %collective-permute-start.16) | collective-permute-done | bytes 49184 | tf_op jit(solution)/shard_map/early_gradients_over_tm/ppermute | solution.py:648
  52.5 1.1 %collective-permute-done.14.refs_3_ = bf16[176,128]{1,0:T(8,128)(2,1)S(1)} collective-permute-done((bf16[176,128]{1,0:T(8,128)(2,1)S(1)}, bf16[176,128]{1,0:T(8,128)(2,1)S(1)}, u32[]{:S(2)}, u32[]{:S(2)}) %collective-permute-start.14) | collective-permute-done | bytes 45088 | tf_op jit(solution)/shard_map/late_sums_in_chip/ppermute | solution.py:48
  53.7 0.1 shard_map.127
  53.8 1.9 %collective-permute-start.18 = (bf16[320,128]{1,0:T(8,128)(2,1)S(1)}, bf16[320,128]{1,0:T(8,128)(2,1)S(1)}, u32[]{:S(2)}, u32[]{:S(2)}) collective-permute-start(bf16[320,128]{1,0:T(8,128)(2,1)S(1)} %get-tuple-element.62), channel_id=1, source_target_pairs={{8,0},{12,4},{0,8},{4,12},{9,1},{13,5},{1,9},{5,13},{10,2},{14,6},... | collective-permute-start | bytes 245768 | tf_op jit(solution)/shard_map/late_sums_over_tm/ppermute | solution.py:648
  55.7 2.5 %collective-permute-start.19 = (bf16[320,128]{1,0:T(8,128)(2,1)S(1)}, bf16[320,128]{1,0:T(8,128)(2,1)S(1)}, u32[]{:S(2)}, u32[]{:S(2)}) collective-permute-start(bf16[320,128]{1,0:T(8,128)(2,1)S(1)} %get-tuple-element.63), channel_id=1, source_target_pairs={{12,0},{8,4},{4,8},{0,12},{13,1},{9,5},{5,9},{1,13},{14,2},{10,6},... | collective-permute-start | bytes 245768 | tf_op jit(solution)/shard_map/late_sums_over_tm/ppermute | solution.py:648
  58.2 3.3 %collective-permute-done.18.refs_2_ = bf16[320,128]{1,0:T(8,128)(2,1)S(1)} collective-permute-done((bf16[320,128]{1,0:T(8,128)(2,1)S(1)}, bf16[320,128]{1,0:T(8,128)(2,1)S(1)}, u32[]{:S(2)}, u32[]{:S(2)}) %collective-permute-start.18) | collective-permute-done | bytes 81952 | tf_op jit(solution)/shard_map/late_sums_over_tm/ppermute | solution.py:648
  61.5 3.2 %collective-permute-done.19.refs_3_ = bf16[320,128]{1,0:T(8,128)(2,1)S(1)} collective-permute-done((bf16[320,128]{1,0:T(8,128)(2,1)S(1)}, bf16[320,128]{1,0:T(8,128)(2,1)S(1)}, u32[]{:S(2)}, u32[]{:S(2)}) %collective-permute-start.19) | collective-permute-done | bytes 81952 | tf_op jit(solution)/shard_map/late_sums_over_tm/ppermute | solution.py:648
  64.7 0.3 collective-permute-done.17.refs_1_
  65.1 1.6 %collective-permute-start.21 = (bf16[128,128]{1,0:T(8,128)(2,1)S(1)}, bf16[128,128]{1,0:T(8,128)(2,1)S(1)}, u32[]{:S(2)}, u32[]{:S(2)}) collective-permute-start(bf16[128,128]{1,0:T(8,128)(2,1)S(1)} %get-tuple-element.65), channel_id=1, source_target_pairs={{0,2},{2,0},{1,3},{3,1},{4,6},{6,4},{5,7},{7,5},{8,10},{10,8},{9,1... | collective-permute-start | bytes 98312 | tf_op jit(solution)/shard_map/low_over_head/ppermute | solution.py:48
  66.7 0.3 collective-permute-start.22
  67.0 2.1 %collective-permute-done.21.low_head = bf16[128,128]{1,0:T(8,128)(2,1)S(1)} collective-permute-done((bf16[128,128]{1,0:T(8,128)(2,1)S(1)}, bf16[128,128]{1,0:T(8,128)(2,1)S(1)}, u32[]{:S(2)}, u32[]{:S(2)}) %collective-permute-start.21) | collective-permute-done | bytes 32800 | tf_op jit(solution)/shard_map/low_over_head/ppermute | solution.py:48
  69.1 0.9 %collective-permute-done.22.low_diag = bf16[128,128]{1,0:T(8,128)(2,1)S(1)} collective-permute-done((bf16[128,128]{1,0:T(8,128)(2,1)S(1)}, bf16[128,128]{1,0:T(8,128)(2,1)S(1)}, u32[]{:S(2)}, u32[]{:S(2)}) %collective-permute-start.22) | collective-permute-done | bytes 32800 | tf_op jit(solution)/shard_map/low_over_head/ppermute | solution.py:709
  70.0 1.5 %shard_map.129 = (f32[128,1280]{1,0:T(8,128)}, f32[128,1280]{1,0:T(8,128)}, f32[128,1280]{1,0:T(8,128)}, f32[256,128]{1,0:T(8,128)}) custom-call(bf16[2048,128]{1,0:T(8,128)(2,1)S(1)} %get-tuple-element.64.tail, bf16[2048,128]{1,0:T(8,128)(2,1)S(1)} %collective-permute-done.20.tail2, bf16[128,128]{1,0:T(8,128)(2,1)S(1)} %collective-permute-done.21.low_head, ...), custom_call_target="tpu_custom_call" | custom-call | tf_op jit(solution)/shard_map/pallas_call | solution.py:611
  (44 shorter events, 0.7 us)
Async XLA Ops:
  0.6 12.8 %copy-start.2 = (bf16[128,1280]{1,0:T(8,128)(2,1)S(1)}, bf16[128,1280]{1,0:T(8,128)(2,1)}, u32[]{:S(2)}) copy-start(bf16[128,1280]{1,0:T(8,128)(2,1)} %fq_ref.3) | copy-start | bytes 983044
  0.6 12.8 %copy-start.3 = (bf16[128,1280]{1,0:T(8,128)(2,1)S(1)}, bf16[128,1280]{1,0:T(8,128)(2,1)}, u32[]{:S(2)}) copy-start(bf16[128,1280]{1,0:T(8,128)(2,1)} %do_ref.3) | copy-start | bytes 983044
  0.7 12.8 %copy-start = (bf16[256,1280]{1,0:T(8,128)(2,1)S(1)}, bf16[256,1280]{1,0:T(8,128)(2,1)}, u32[]{:S(2)}) copy-start(bf16[256,1280]{1,0:T(8,128)(2,1)} %fk_ref.3) | copy-start | bytes 1966084
  0.7 12.8 %copy-start.1 = (bf16[256,1280]{1,0:T(8,128)(2,1)S(1)}, bf16[256,1280]{1,0:T(8,128)(2,1)}, u32[]{:S(2)}) copy-start(bf16[256,1280]{1,0:T(8,128)(2,1)} %fv_ref.3) | copy-start | bytes 1966084
  0.7 12.8 %copy-start.7 = (bf16[256,128]{1,0:T(8,128)(2,1)S(1)}, bf16[256,128]{1,0:T(8,128)(2,1)}, u32[]{:S(2)}) copy-start(bf16[256,128]{1,0:T(8,128)(2,1)} %t_ref.3) | copy-start | bytes 196612
  3.3 23.6 %collective-permute-start = (bf16[128,1664]{1,0:T(8,128)(2,1)}, bf16[128,1664]{1,0:T(8,128)(2,1)S(1)}, u32[]{:S(2)}, u32[]{:S(2)}) collective-permute-start(bf16[128,1664]{1,0:T(8,128)(2,1)} %get-tuple-element.36), channel_id=1, source_target_pairs={{4,0},{0,4},{12,8},{8,12},{5,1},{1,5},{13,9},{9,13},{6,2},{2,6},{1... | collective-permute-start | bytes 1277960 | tf_op jit(solution)/shard_map/nearest_over_tm/ppermute | solution.py:648
  6.3 14.1 %collective-permute-start.1 = (bf16[128,640]{1,0:T(8,128)(2,1)}, bf16[128,640]{1,0:T(8,128)(2,1)S(1)}, u32[]{:S(2)}, u32[]{:S(2)}) collective-permute-start(bf16[128,640]{1,0:T(8,128)(2,1)} %get-tuple-element.37), channel_id=1, source_target_pairs={{8,0},{12,4},{0,8},{4,12},{9,1},{13,5},{1,9},{5,13},{10,2},{14,6},... | collective-permute-start | bytes 491528 | tf_op jit(solution)/shard_map/lead_over_tm/ppermute | solution.py:648
  8.9 17.9 %collective-permute-start.2 = (bf16[128,640]{1,0:T(8,128)(2,1)}, bf16[128,640]{1,0:T(8,128)(2,1)S(1)}, u32[]{:S(2)}, u32[]{:S(2)}) collective-permute-start(bf16[128,640]{1,0:T(8,128)(2,1)} %get-tuple-element.38), channel_id=1, source_target_pairs={{12,0},{8,4},{4,8},{0,12},{13,1},{9,5},{5,9},{1,13},{14,2},{10,6},... | collective-permute-start | bytes 491528 | tf_op jit(solution)/shard_map/lead_over_tm/ppermute | solution.py:648
  8.9 18.0 %collective-permute-start.6 = (bf16[128,512]{1,0:T(8,128)(2,1)}, bf16[128,512]{1,0:T(8,128)(2,1)S(1)}, u32[]{:S(2)}, u32[]{:S(2)}) collective-permute-start(bf16[128,512]{1,0:T(8,128)(2,1)} %get-tuple-element.47), channel_id=1, source_target_pairs={{12,4},{0,8},{13,5},{1,9},{14,6},{2,10},{15,7},{3,11},{28,20},{16,... | collective-permute-start | bytes 393224 | tf_op jit(solution)/shard_map/rest_over_tm/ppermute | solution.py:648
  12.8 14.2 %collective-permute-start.7 = (bf16[128,512]{1,0:T(8,128)(2,1)}, bf16[128,512]{1,0:T(8,128)(2,1)S(1)}, u32[]{:S(2)}, u32[]{:S(2)}) collective-permute-start(bf16[128,512]{1,0:T(8,128)(2,1)} %get-tuple-element.48), channel_id=1, source_target_pairs={{8,4},{4,8},{9,5},{5,9},{10,6},{6,10},{11,7},{7,11},{24,20},{20,24... | collective-permute-start | bytes 393224 | tf_op jit(solution)/shard_map/rest_over_tm/ppermute | solution.py:648
  26.8 5.6 %copy-start.6 = (bf16[128,1280]{1,0:T(8,128)(2,1)S(1)}, bf16[128,1280]{1,0:T(8,128)(2,1)}, u32[]{:S(2)}) copy-start(bf16[128,1280]{1,0:T(8,128)(2,1)} %refs_14_.3) | copy-start | bytes 983044
  26.9 5.6 %copy-start.4 = (bf16[128,1280]{1,0:T(8,128)(2,1)S(1)}, bf16[128,1280]{1,0:T(8,128)(2,1)}, u32[]{:S(2)}) copy-start(bf16[128,1280]{1,0:T(8,128)(2,1)} %refs_12_.1) | copy-start | bytes 983044
  26.9 5.6 %copy-start.5 = (bf16[128,1280]{1,0:T(8,128)(2,1)S(1)}, bf16[128,1280]{1,0:T(8,128)(2,1)}, u32[]{:S(2)}) copy-start(bf16[128,1280]{1,0:T(8,128)(2,1)} %refs_13_.1) | copy-start | bytes 983044
  26.9 5.5 %collective-permute-start.3 = (bf16[128,1152]{1,0:T(8,128)(2,1)S(1)}, bf16[128,1152]{1,0:T(8,128)(2,1)S(1)}, u32[]{:S(2)}, u32[]{:S(2)}) collective-permute-start(bf16[128,1152]{1,0:T(8,128)(2,1)S(1)} %shard_map.122), channel_id=1, source_target_pairs={{0,1},{1,0},{2,3},{3,2},{4,5},{5,4},{6,7},{7,6},{8,9},{9,8},{10,11... | collective-permute-start | bytes 884744 | tf_op jit(solution)/shard_map/lead_in_chip/ppermute | solution.py:48
  27.0 5.4 %collective-permute-start.8 = (bf16[128,768]{1,0:T(8,128)(2,1)S(1)}, bf16[128,768]{1,0:T(8,128)(2,1)S(1)}, u32[]{:S(2)}, u32[]{:S(2)}) collective-permute-start(bf16[128,768]{1,0:T(8,128)(2,1)S(1)} %shard_map.123), channel_id=1, source_target_pairs={{0,1},{1,0},{2,3},{3,2},{4,5},{5,4},{6,7},{7,6},{8,9},{9,8},{10,11... | collective-permute-start | bytes 589832 | tf_op jit(solution)/shard_map/rest_in_chip/ppermute | solution.py:48
  27.6 13.5 %collective-permute-start.4 = (bf16[128,512]{1,0:T(8,128)(2,1)S(1)}, bf16[128,512]{1,0:T(8,128)(2,1)S(1)}, u32[]{:S(2)}, u32[]{:S(2)}) collective-permute-start(bf16[128,512]{1,0:T(8,128)(2,1)S(1)} %get-tuple-element.42), channel_id=1, source_target_pairs={{8,0},{12,4},{0,8},{4,12},{9,1},{13,5},{1,9},{5,13},{10,2},{14,6},... | collective-permute-start | bytes 393224 | tf_op jit(solution)/shard_map/late_over_tm/ppermute | solution.py:648
  31.0 10.0 %collective-permute-start.5 = (bf16[128,512]{1,0:T(8,128)(2,1)S(1)}, bf16[128,512]{1,0:T(8,128)(2,1)S(1)}, u32[]{:S(2)}, u32[]{:S(2)}) collective-permute-start(bf16[128,512]{1,0:T(8,128)(2,1)S(1)} %get-tuple-element.43), channel_id=1, source_target_pairs={{12,0},{8,4},{4,8},{0,12},{13,1},{9,5},{5,9},{1,13},{14,2},{10,6},... | collective-permute-start | bytes 393224 | tf_op jit(solution)/shard_map/late_over_tm/ppermute | solution.py:648
  32.4 0.7 copy-start.8
  37.2 3.8 %collective-permute-start.9 = (bf16[384,128]{1,0:T(8,128)(2,1)S(1)}, bf16[384,128]{1,0:T(8,128)(2,1)S(1)}, u32[]{:S(2)}, u32[]{:S(2)}) collective-permute-start(bf16[384,128]{1,0:T(8,128)(2,1)S(1)} %get-tuple-element.50), channel_id=1, source_target_pairs={{0,1},{1,0},{2,3},{3,2},{4,5},{5,4},{6,7},{7,6},{8,9},{9,8},{10,11... | collective-permute-start | bytes 294920 | tf_op jit(solution)/shard_map/early_gradients_in_chip/ppermute | solution.py:48
  41.0 4.8 %collective-permute-start.10 = (bf16[128,1536]{1,0:T(8,128)(2,1)S(1)}, bf16[128,1536]{1,0:T(8,128)(2,1)S(1)}, u32[]{:S(2)}, u32[]{:S(2)}) collective-permute-start(bf16[128,1536]{1,0:T(8,128)(2,1)S(1)} %shard_map.125), channel_id=1, source_target_pairs={{0,1},{1,0},{2,3},{3,2},{4,5},{5,4},{6,7},{7,6},{8,9},{9,8},{10,11... | collective-permute-start | bytes 1179656 | tf_op jit(solution)/shard_map/late_in_chip/ppermute | solution.py:48
  41.2 11.3 %collective-permute-start.15 = (bf16[384,128]{1,0:T(8,128)(2,1)S(1)}, bf16[384,128]{1,0:T(8,128)(2,1)S(1)}, u32[]{:S(2)}, u32[]{:S(2)}) collective-permute-start(bf16[384,128]{1,0:T(8,128)(2,1)S(1)} %add_convert_fusion.refs_17_.refs_4_), channel_id=1, source_target_pairs={{12,0},{8,4},{4,8},{0,12},{13,1},{9,5},{5,9},{1,13},{14,2},{10,6},... | collective-permute-start | bytes 294920 | tf_op jit(solution)/shard_map/early_gradients_over_tm/ppermute | solution.py:648
  42.6 9.8 %collective-permute-start.16 = (bf16[192,128]{1,0:T(8,128)(2,1)S(1)}, bf16[192,128]{1,0:T(8,128)(2,1)S(1)}, u32[]{:S(2)}, u32[]{:S(2)}) collective-permute-start(bf16[192,128]{1,0:T(8,128)(2,1)S(1)} %slice.4), channel_id=1, source_target_pairs={{8,0},{12,4},{0,8},{4,12},{9,1},{13,5},{1,9},{5,13},{10,2},{14,6},... | collective-permute-start | bytes 147464 | tf_op jit(solution)/shard_map/early_gradients_over_tm/ppermute | solution.py:648
  49.7 2.8 %collective-permute-start.11 = (bf16[176,128]{1,0:T(8,128)(2,1)S(1)}, bf16[176,128]{1,0:T(8,128)(2,1)S(1)}, u32[]{:S(2)}, u32[]{:S(2)}) collective-permute-start(bf16[176,128]{1,0:T(8,128)(2,1)S(1)} %get-tuple-element.55), channel_id=1, source_target_pairs={{0,1},{1,0},{2,3},{3,2},{4,5},{5,4},{6,7},{7,6},{8,9},{9,8},{10,11... | collective-permute-start | bytes 135176 | tf_op jit(solution)/shard_map/late_sums_in_chip/ppermute | solution.py:48
  49.8 2.7 %collective-permute-start.12 = (bf16[176,128]{1,0:T(8,128)(2,1)S(1)}, bf16[176,128]{1,0:T(8,128)(2,1)S(1)}, u32[]{:S(2)}, u32[]{:S(2)}) collective-permute-start(bf16[176,128]{1,0:T(8,128)(2,1)S(1)} %get-tuple-element.56), channel_id=1, source_target_pairs={{0,1},{1,0},{2,3},{3,2},{4,5},{5,4},{6,7},{7,6},{8,9},{9,8},{10,11... | collective-permute-start | bytes 135176 | tf_op jit(solution)/shard_map/late_sums_in_chip/ppermute | solution.py:48
  50.3 2.2 %collective-permute-start.13 = (bf16[176,128]{1,0:T(8,128)(2,1)S(1)}, bf16[176,128]{1,0:T(8,128)(2,1)S(1)}, u32[]{:S(2)}, u32[]{:S(2)}) collective-permute-start(bf16[176,128]{1,0:T(8,128)(2,1)S(1)} %get-tuple-element.57), channel_id=1, source_target_pairs={{0,1},{1,0},{2,3},{3,2},{4,5},{5,4},{6,7},{7,6},{8,9},{9,8},{10,11... | collective-permute-start | bytes 135176 | tf_op jit(solution)/shard_map/late_sums_in_chip/ppermute | solution.py:48
  52.4 1.2 %collective-permute-start.14 = (bf16[176,128]{1,0:T(8,128)(2,1)S(1)}, bf16[176,128]{1,0:T(8,128)(2,1)S(1)}, u32[]{:S(2)}, u32[]{:S(2)}) collective-permute-start(bf16[176,128]{1,0:T(8,128)(2,1)S(1)} %get-tuple-element.58), channel_id=1, source_target_pairs={{0,1},{1,0},{2,3},{3,2},{4,5},{5,4},{6,7},{7,6},{8,9},{9,8},{10,11... | collective-permute-start | bytes 135176 | tf_op jit(solution)/shard_map/late_sums_in_chip/ppermute | solution.py:48
  53.7 11.2 %collective-permute-start.17 = (bf16[896,128]{1,0:T(8,128)(2,1)S(1)}, bf16[896,128]{1,0:T(8,128)(2,1)S(1)}, u32[]{:S(2)}, u32[]{:S(2)}) collective-permute-start(bf16[896,128]{1,0:T(8,128)(2,1)S(1)} %get-tuple-element.61), channel_id=1, source_target_pairs={{4,0},{0,4},{12,8},{8,12},{5,1},{1,5},{13,9},{9,13},{6,2},{2,6},{1... | collective-permute-start | bytes 688136 | tf_op jit(solution)/shard_map/late_sums_over_tm/ppermute | solution.py:648
  53.8 7.7 %collective-permute-start.18 = (bf16[320,128]{1,0:T(8,128)(2,1)S(1)}, bf16[320,128]{1,0:T(8,128)(2,1)S(1)}, u32[]{:S(2)}, u32[]{:S(2)}) collective-permute-start(bf16[320,128]{1,0:T(8,128)(2,1)S(1)} %get-tuple-element.62), channel_id=1, source_target_pairs={{8,0},{12,4},{0,8},{4,12},{9,1},{13,5},{1,9},{5,13},{10,2},{14,6},... | collective-permute-start | bytes 245768 | tf_op jit(solution)/shard_map/late_sums_over_tm/ppermute | solution.py:648
  55.7 9.0 %collective-permute-start.19 = (bf16[320,128]{1,0:T(8,128)(2,1)S(1)}, bf16[320,128]{1,0:T(8,128)(2,1)S(1)}, u32[]{:S(2)}, u32[]{:S(2)}) collective-permute-start(bf16[320,128]{1,0:T(8,128)(2,1)S(1)} %get-tuple-element.63), channel_id=1, source_target_pairs={{12,0},{8,4},{4,8},{0,12},{13,1},{9,5},{5,9},{1,13},{14,2},{10,6},... | collective-permute-start | bytes 245768 | tf_op jit(solution)/shard_map/late_sums_over_tm/ppermute | solution.py:648
  65.1 5.0 %collective-permute-start.20 = (bf16[2048,128]{1,0:T(8,128)(2,1)S(1)}, bf16[2048,128]{1,0:T(8,128)(2,1)S(1)}, u32[]{:S(2)}, u32[]{:S(2)}) collective-permute-start(bf16[2048,128]{1,0:T(8,128)(2,1)S(1)} %get-tuple-element.64.tail), channel_id=1, source_target_pairs={{0,1},{1,0},{2,3},{3,2},{4,5},{5,4},{6,7},{7,6},{8,9},{9,8},{10,11... | collective-permute-start | bytes 1572872 | tf_op jit(solution)/shard_map/tail_in_chip/ppermute | solution.py:48
  65.1 4.0 %collective-permute-start.21 = (bf16[128,128]{1,0:T(8,128)(2,1)S(1)}, bf16[128,128]{1,0:T(8,128)(2,1)S(1)}, u32[]{:S(2)}, u32[]{:S(2)}) collective-permute-start(bf16[128,128]{1,0:T(8,128)(2,1)S(1)} %get-tuple-element.65), channel_id=1, source_target_pairs={{0,2},{2,0},{1,3},{3,1},{4,6},{6,4},{5,7},{7,5},{8,10},{10,8},{9,1... | collective-permute-start | bytes 98312 | tf_op jit(solution)/shard_map/low_over_head/ppermute | solution.py:48
  66.7 3.3 %collective-permute-start.22 = (bf16[128,128]{1,0:T(8,128)(2,1)S(1)}, bf16[128,128]{1,0:T(8,128)(2,1)S(1)}, u32[]{:S(2)}, u32[]{:S(2)}) collective-permute-start(bf16[128,128]{1,0:T(8,128)(2,1)S(1)} %get-tuple-element.65), channel_id=1, source_target_pairs={{0,3},{1,2},{2,1},{3,0},{4,7},{5,6},{6,5},{7,4},{8,11},{9,10},{10,... | collective-permute-start | bytes 98312 | tf_op jit(solution)/shard_map/low_over_head/ppermute | solution.py:709

commit v9 on v8

--- a/solution.py
+++ b/solution.py
@@ -13,7 +13,7 @@
 SCALE = DH ** (-0.5)
 F32 = jnp.float32
 BF16 = jnp.bfloat16
-GIVES = 4
+GIVES = 2
 SMALL = pltpu.CompilerParams(vmem_limit_bytes=16 * 1024 * 1024)
 
 
@@ -523,99 +523,113 @@
 
 
 def hand_out_kernel(frames, size, parts, keep_ref, *refs):
-    gots, (piece, facing), (own_ref, *sends, total) = refs[:parts], refs[parts : parts + 2], refs[-frames - 2 :]
+    gots, (piece, facing), (own_ref, *sends, total) = refs[:parts], refs[parts : parts + 2], refs[parts + 2 :]
+    lows, grads = sends[: frames - 1], sends[frames - 1 :]
     me = lax.axis_index("tm")
     rows = own_ref.shape[0]
     total[...] = keep_ref[...] + jnp.concatenate([got[...].astype(F32) for got in gots], axis=0)
-    grads = total[:size, :].astype(BF16)
     for m in range(frames):
         low = total[pl.ds(pl.multiple_of(size + (me ^ m) * rows, 8), rows), :]
         if m == 0:
             own_ref[...] = low
-        sends[m][:rows, :] = low.astype(BF16)
-        sends[m][rows : rows + size, :] = grads
-    sends[1][rows + size : rows + 3 * size, :] = piece[...]
-    sends[1][rows + 3 * size :, :] = facing[size:, :]
-
-
-def hand_out(frames, rows, keep, gots, piece, facing, after):
+        else:
+            lows[m - 1][...] = low.astype(BF16)
+            grads[m - 1][:size, :] = total[:size, :].astype(BF16)
+    grads[0][size : 3 * size, :] = piece[...]
+    grads[0][3 * size :, :] = facing[size:, :]
+    grads[1][size:, :] = piece[:size, :]
+
+
+def hand_out(frames, rows, keep, gots, piece, facing):
     size, rank = keep.shape[0] - frames * rows, keep.shape[1]
-    sends = [jax.ShapeDtypeStruct((rows + size * (4 if m == 1 else 1), rank), BF16) for m in range(frames)]
-    return pl.pallas_call(
+    low = jax.ShapeDtypeStruct((rows, rank), BF16)
+    outs = pl.pallas_call(
         functools.partial(hand_out_kernel, frames, size, len(gots)),
-        in_specs=vmem(3 + len(gots)) + [pl.BlockSpec(memory_space=pl.ANY)] * len(after),
-        out_specs=vmem(frames + 1),
-        out_shape=[jax.ShapeDtypeStruct((rows, rank), F32)] + sends,
+        in_specs=vmem(3 + len(gots)),
+        out_specs=vmem(2 * frames - 1),
+        out_shape=[jax.ShapeDtypeStruct((rows, rank), F32)]
+        + [low] * (frames - 1)
+        + [jax.ShapeDtypeStruct((size * n, rank), BF16) for n in (4, 2, 1)],
         scratch_shapes=[pltpu.VMEM(keep.shape, F32)],
         compiler_params=SMALL,
-    )(keep, *gots, piece, facing, *after)
-
-
-def collect_kernel(frames, wide, own_ref, *refs):
-    gots, (piece, far, facing), (out_ref, low_ref) = refs[:frames], refs[frames : frames + 3], refs[-2:]
-    rows = own_ref.shape[0]
-    size = gots[0].shape[0] - rows
+    )(keep, *gots, piece, facing)
+    return outs[0], outs[1:frames], outs[frames:]
+
+
+def sum_low_kernel(own_ref, *refs):
     low = own_ref[...]
-    for m in range(1, frames):
-        low = low + gots[m][:rows, :].astype(F32)
-    out_ref[:rows, :] = low.astype(BF16)
-    low_ref[...] = low.astype(BF16)
-    near = rows + size
+    for got in refs[:-1]:
+        low = low + got[...].astype(F32)
+    refs[-1][...] = low.astype(BF16)
+
+
+def sum_low(own, gots):
+    return pl.pallas_call(
+        sum_low_kernel,
+        in_specs=vmem(1 + len(gots)),
+        out_specs=pl.BlockSpec(memory_space=pltpu.VMEM),
+        out_shape=jax.ShapeDtypeStruct(own.shape, BF16),
+        compiler_params=SMALL,
+    )(own, *gots)
+
+
+def collect_kernel(wide, low_ref, low_head, own, near, third, last, piece, facing, out_ref):
+    rows, size = low_ref.shape[0], own.shape[0]
+    out_ref[:rows, :] = (low_ref[...].astype(F32) + low_head[...].astype(F32)).astype(BF16)
     middle = lookup(wide, lax.axis_index("tm")) > 0
-    blocks = [got[rows:near, :] for got in gots]
-    blocks += [piece[:size, :], gots[1][near : near + size, :], far[...], facing[:size, :]]
-    blocks.append(jnp.where(middle, piece[size:, :], gots[1][near + size : near + 2 * size, :]))
-    blocks.append(jnp.where(middle, facing[size:, :], gots[1][near + 2 * size :, :]))
+
+    def part(ref, n):
+        return ref[n * size : (n + 1) * size, :]
+
+    blocks = [part(ref, 0) for ref in (own, near, third, last)]
+    blocks += [part(piece, 0), part(near, 1), part(third, 1), part(facing, 0)]
+    blocks.append(jnp.where(middle, part(piece, 1), part(near, 2)))
+    blocks.append(jnp.where(middle, part(facing, 1), part(near, 3)))
     for n, block in enumerate(blocks):
         out_ref[rows + n * size : rows + (n + 1) * size, :] = block
 
 
-def collect(wide, own, gots, piece, far, facing):
-    frames, (rows, rank) = len(gots), own.shape
-    size = gots[0].shape[0] - rows
+def collect(wide, low, low_head, own, gots, piece, facing):
+    (rows, rank), size = low.shape, own.shape[0]
     return pl.pallas_call(
-        functools.partial(collect_kernel, frames, wide),
-        in_specs=vmem(frames + 4),
-        out_specs=vmem(2),
-        out_shape=[
-            jax.ShapeDtypeStruct((rows + (2 * frames + 2) * size, rank), BF16),
-            jax.ShapeDtypeStruct((rows, rank), BF16),
-        ],
+        functools.partial(collect_kernel, wide),
+        in_specs=vmem(5 + len(gots)),
+        out_specs=pl.BlockSpec(memory_space=pltpu.VMEM),
+        out_shape=jax.ShapeDtypeStruct((rows + 10 * size, rank), BF16),
         compiler_params=SMALL,
-    )(own, *gots, piece, far, facing)
-
-
-def place_kernel(frames, lead, late, rest, tail, tail2, low_head, low_diag, *outs):
+    )(low, low_head, own, *gots, piece, facing)
+
+
+def place_kernel(frames, lead, late, rest, tail, tail2, *outs):
     me, half = lax.axis_index("tm"), lax.axis_index("rep")
     first = half == 0
     rank = outs[0].shape[0]
     cut = 3 * rank // 2
-    rows = low_head.shape[0]
-    same = tail[:rows, :].astype(F32) + low_head[...].astype(F32)
-    other = tail2[:rows, :].astype(F32) + low_diag[...].astype(F32)
-    outs[3][:rows, :] = jnp.where(first, same, other)
-    outs[3][rows:, :] = jnp.where(first, other, same)
+    rows = outs[3].shape[0] // 2
+
+    def both(here):
+        a, b = tail[here, :].astype(F32), tail2[here, :].astype(F32)
+        return jnp.concatenate([jnp.where(first, a, b), jnp.where(first, b, a)], axis=0)
+
+    outs[3][...] = both(slice(0, rows))
     side = me // 2
     places = [lookup(late, me ^ m) for m in range(frames)] + [lookup(lead, me ^ m) for m in range(frames)]
     places += [lookup(rest, 1 + side), lookup(rest, 2 - side)]
     for n, head in enumerate(places):
-        here = slice(rows + n * cut, rows + (n + 1) * cut)
-        a, b = tail[here, :].astype(F32), tail2[here, :].astype(F32)
-        both = jnp.concatenate([jnp.where(first, a, b), jnp.where(first, b, a)], axis=0)
+        whole = both(slice(rows + n * cut, rows + (n + 1) * cut))
         for o in range(3):
-            outs[o][:, column(head)] = both[o * rank : (o + 1) * rank]
-
-
-def place(frames, lead, late, rest, tail, tail2, low_head, low_diag, rank, width):
-    rows = low_head.shape[0]
+            outs[o][:, column(head)] = whole[o * rank : (o + 1) * rank]
+
+
+def place(frames, lead, late, rest, tail, tail2, rows, rank, width):
     return pl.pallas_call(
         functools.partial(place_kernel, frames, lead, late, rest),
-        in_specs=vmem(4),
+        in_specs=vmem(2),
         out_specs=vmem(4),
         out_shape=[jax.ShapeDtypeStruct((rank, width), F32)] * 3
         + [jax.ShapeDtypeStruct((2 * rows, rank), F32)],
         compiler_params=SMALL,
-    )(tail, tail2, low_head, low_diag)
+    )(tail, tail2)
 
 
 def exchange_plan(
@@ -696,19 +710,17 @@
     got = swap_in_chip("early_gradients", give)
     piece = (keep + got.astype(F32)).astype(BF16)
     *late_side, _ = sides("late", 2, late_got, False, False, 0, [got])
-    cut = 3 * rank // 2
-    far = meet("early_gradients", piece[:cut], 2)
     facing = meet("early_gradients", piece, 3)
     keep, *gives = head_group([late], band_width, [t_side, late_side], adapters, low, [piece])
     gives = [swap_in_chip("late_sums", g) for g in gives]
-    own, *sends = hand_out(frames, rows, keep, gives, piece, facing, [far])
-    gots = [sends[0]] + [meet("late_sums", sends[m], m) for m in range(1, frames)]
-    tail, low = collect(rest[1], own, gots, piece, far, facing)
-    diag = [(0, 3), (1, 2), (2, 1), (3, 0)]
+    own_low, lows, grads = hand_out(frames, rows, keep, gives, piece, facing)
+    low = sum_low(own_low, [meet("low", block, m) for m, block in enumerate(lows, 1)])
+    gots = [meet("late_gradients", block, m) for m, block in enumerate(grads, 1)]
     with jax.named_scope("low_over_head"):
-        low_head, low_diag = swap(low, "head"), lax.ppermute(low, ("head", "rep"), diag)
+        low_head = swap(low, "head")
+    tail = collect(rest[1], low, low_head, grads[2], gots, piece, facing)
     outs = place(
-        frames, lead[0], late[0], rest[0], tail, swap_in_chip("tail", tail), low_head, low_diag, rank, width
+        frames, lead[0], late[0], rest[0], tail, swap_in_chip("tail", tail), rows, rank, width
     )
     return tuple(outs)
 

time: 71.7 us -> 70 us (0.976)
  waiting for transfers between devices: 29.2 us -> 26.9 us
    ppermute x12 -> x14, starting transfers between devices: 24.1 us -> 25.2 us  [meet(): return lax.ppermute(block, 'tm', [(j ^ m, j) for j in targets])]
    ppermute x10 -> x8, waiting for transfers between devices: 3.27 us -> 2.17 us  [swap(): return lax.ppermute(block, axis, [(0, 1), (1, 0)])]
    ppermute x1 -> x0, waiting for transfers between devices: 0.92 us -> none  [exchange_plan(): lax.ppermute(low, ('head', 'rep'), diag)]
    ppermute x12 -> x14, waiting for transfers between devices: 25 us -> 24.7 us  [meet(): return lax.ppermute(block, 'tm', [(j ^ m, j) for j in targets])]
    ppermute x10 -> x8, starting transfers between devices: 3.1 us -> 2.96 us  [swap(): return lax.ppermute(block, axis, [(0, 1), (1, 0)])]
  transfers between devices with their start and end apart: 23 -> 22, of which waited for: 10 -> 9; matrix products, arithmetic and copies ran while one was open for 0% -> 0% of each run, Pallas kernels for 13% -> 13%
where the time goes in v9:
time: 70 us; the launch traced here: 69.8 us
  starting transfers between devices  28.2 us (40%)
  waiting for transfers between devices  26.9 us (38%)
  Pallas kernels  13.2 us (19%)
  between operations  0.91 us (1%)
    ppermute x14, starting transfers between devices, meet(): return lax.ppermute(block, 'tm', [(j ^ m, j) for j in targets])  25.2 us
    ppermute x14, waiting for transfers between devices, meet(): return lax.ppermute(block, 'tm', [(j ^ m, j) for j in targets])  24.7 us
    pallas_call x2, Pallas kernels, head_group(): pl.pallas_call(functools.partial(group_kernel, heads, frames, chained, le...  7.97 us
    pallas_call x2, Pallas kernels, pack(): pl.pallas_call(functools.partial(pack_kernel, frames, outputs), in_specs=...  3.5 us
    ppermute x8, starting transfers between devices, swap(): return lax.ppermute(block, axis, [(0, 1), (1, 0)])  2.96 us
    ppermute x8, waiting for transfers between devices, swap(): return lax.ppermute(block, axis, [(0, 1), (1, 0)])  2.17 us
    pallas_call x1, Pallas kernels, place(): pl.pallas_call(functools.partial(place_kernel, frames, lead, late, rest),...  1.47 us
  transfers between devices with their start and end apart: 22, of which 9 were waited for; matrix products, arithmetic and copies ran while one was open for 0% of the time, Pallas kernels for 13%

profile of v9, /device:TPU:0, one launch (start us, length us, event | category | flops | bytes accessed | tf_op | source)
XLA Modules:
  0.0 69.8 jit_solution(8291525168717385315)
XLA Ops:
  0.7 2.6 %shard_map.121 = (bf16[128,1664]{1,0:T(8,128)(2,1)}, bf16[128,640]{1,0:T(8,128)(2,1)}, bf16[128,512]{1,0:T(8,128)(2,1)}, bf16[128,640]{1,0:T(8,128)(2,1)}, bf16[128,512]{1,0:T(8,128)(2,1)}) custom-call(bf16[128,1280]{1,0:T(8,128)(2,1)} %fq_ref.3, bf16[128,1280]{1,0:T(8,128)(2,1)} %do_ref.3, bf16[256,1280]{1,0:T(8,128)(2,1)} %fk_ref.3, ...), custom_call_target="tpu_custom_call" | custom-call | tf_op jit(solution)/shard_map/pallas_call | solution.py:301
  3.2 3.1 %collective-permute-start = (bf16[128,1664]{1,0:T(8,128)(2,1)}, bf16[128,1664]{1,0:T(8,128)(2,1)S(1)}, u32[]{:S(2)}, u32[]{:S(2)}) collective-permute-start(bf16[128,1664]{1,0:T(8,128)(2,1)} %get-tuple-element.34), channel_id=1, source_target_pairs={{4,0},{0,4},{12,8},{8,12},{5,1},{1,5},{13,9},{9,13},{6,2},{2,6},{1... | collective-permute-start | bytes 1277960 | tf_op jit(solution)/shard_map/nearest_over_tm/ppermute | solution.py:662
  6.3 2.6 %collective-permute-start.1 = (bf16[128,640]{1,0:T(8,128)(2,1)}, bf16[128,640]{1,0:T(8,128)(2,1)S(1)}, u32[]{:S(2)}, u32[]{:S(2)}) collective-permute-start(bf16[128,640]{1,0:T(8,128)(2,1)} %get-tuple-element.35), channel_id=1, source_target_pairs={{8,0},{12,4},{0,8},{4,12},{9,1},{13,5},{1,9},{5,13},{10,2},{14,6},... | collective-permute-start | bytes 491528 | tf_op jit(solution)/shard_map/lead_over_tm/ppermute | solution.py:662
  8.9 3.8 %collective-permute-start.6 = (bf16[128,512]{1,0:T(8,128)(2,1)}, bf16[128,512]{1,0:T(8,128)(2,1)S(1)}, u32[]{:S(2)}, u32[]{:S(2)}) collective-permute-start(bf16[128,512]{1,0:T(8,128)(2,1)} %get-tuple-element.45), channel_id=1, source_target_pairs={{12,4},{0,8},{13,5},{1,9},{14,6},{2,10},{15,7},{3,11},{28,20},{16,... | collective-permute-start | bytes 393224 | tf_op jit(solution)/shard_map/rest_over_tm/ppermute | solution.py:662
  12.7 0.7 collective-permute-start.7
  13.5 0.9 %shard_map.120 = (bf16[128,512]{1,0:T(8,128)(2,1)S(1)}, bf16[128,512]{1,0:T(8,128)(2,1)S(1)}, bf16[128,512]{1,0:T(8,128)(2,1)S(1)}, bf16[128,256]{1,0:T(8,128)(2...) custom-call(bf16[128,1280]{1,0:T(8,128)(2,1)S(1)} %copy-done.2, ...), custom_call_target="tpu_custom_call" | custom-call | tf_op jit(solution)/shard_map/pallas_call | solution.py:301
  14.4 6.0 %collective-permute-done.1.refs_1_.refs_3_ = bf16[128,640]{1,0:T(8,128)(2,1)S(1)} collective-permute-done((bf16[128,640]{1,0:T(8,128)(2,1)}, bf16[128,640]{1,0:T(8,128)(2,1)S(1)}, u32[]{:S(2)}, u32[]{:S(2)}) %collective-permute-start.1) | collective-permute-done | bytes 163872 | tf_op jit(solution)/shard_map/lead_over_tm/ppermute | solution.py:662
  20.4 6.4 %collective-permute-done.2.refs_2_.refs_4_ = bf16[128,640]{1,0:T(8,128)(2,1)S(1)} collective-permute-done((bf16[128,640]{1,0:T(8,128)(2,1)}, bf16[128,640]{1,0:T(8,128)(2,1)S(1)}, u32[]{:S(2)}, u32[]{:S(2)}) %collective-permute-start.2) | collective-permute-done | bytes 163872 | tf_op jit(solution)/shard_map/lead_over_tm/ppermute | solution.py:662
  27.0 0.5 collective-permute-start.8
  27.6 3.5 %collective-permute-start.4 = (bf16[128,512]{1,0:T(8,128)(2,1)S(1)}, bf16[128,512]{1,0:T(8,128)(2,1)S(1)}, u32[]{:S(2)}, u32[]{:S(2)}) collective-permute-start(bf16[128,512]{1,0:T(8,128)(2,1)S(1)} %get-tuple-element.40), channel_id=1, source_target_pairs={{8,0},{12,4},{0,8},{4,12},{9,1},{13,5},{1,9},{5,13},{10,2},{14,6},... | collective-permute-start | bytes 393224 | tf_op jit(solution)/shard_map/late_over_tm/ppermute | solution.py:662
  31.0 1.4 %collective-permute-start.5 = (bf16[128,512]{1,0:T(8,128)(2,1)S(1)}, bf16[128,512]{1,0:T(8,128)(2,1)S(1)}, u32[]{:S(2)}, u32[]{:S(2)}) collective-permute-start(bf16[128,512]{1,0:T(8,128)(2,1)S(1)} %get-tuple-element.41), channel_id=1, source_target_pairs={{12,0},{8,4},{4,8},{0,12},{13,1},{9,5},{5,9},{1,13},{14,2},{10,6},... | collective-permute-start | bytes 393224 | tf_op jit(solution)/shard_map/late_over_tm/ppermute | solution.py:662
  32.4 0.6 copy-done.8
  33.1 4.1 %shard_map.124 = (f32[384,128]{1,0:T(8,128)S(1)}, bf16[384,128]{1,0:T(8,128)(2,1)S(1)}, f32[512,128]{1,0:T(8,128)S(1)}, f32[512,128]{1,0:T(8,128)S(1)}) custom-call(s32[4,4]{1,0:T(4,128)S(1)} %copy-done.8, bf16[128,128]{1,0:T(8,128)(2,1)S(1)} %get-tuple-element.33.refs_1_, bf16[128,1664]{1,0:T(8,128)(2,1)S(1)} %collective-permute-done.refs_0_.refs_2_, ...), custom_call_target="tpu_custom_call" | custom-call | tf_op jit(solution)/shard_map/pallas_call | solution.py:511
  37.2 3.8 %collective-permute-done.4.refs_1_.refs_8_ = bf16[128,512]{1,0:T(8,128)(2,1)S(1)} collective-permute-done((bf16[128,512]{1,0:T(8,128)(2,1)S(1)}, bf16[128,512]{1,0:T(8,128)(2,1)S(1)}, u32[]{:S(2)}, u32[]{:S(2)}) %collective-permute-start.4) | collective-permute-done | bytes 131104 | tf_op jit(solution)/shard_map/late_over_tm/ppermute | solution.py:662
  41.2 1.4 %collective-permute-start.13 = (bf16[384,128]{1,0:T(8,128)(2,1)S(1)}, bf16[384,128]{1,0:T(8,128)(2,1)S(1)}, u32[]{:S(2)}, u32[]{:S(2)}) collective-permute-start(bf16[384,128]{1,0:T(8,128)(2,1)S(1)} %add_convert_fusion.refs_17_.refs_2_.piece), channel_id=1, source_target_pairs={{12,0},{8,4},{4,8},{0,12},{13,1},{9,5},{5,9},{1,13},{14,2},{10,6},... | collective-permute-start | bytes 294920 | tf_op jit(solution)/shard_map/early_gradients_over_tm/ppermute | solution.py:662
  42.6 0.3 collective-permute-done.10.refs_11_
  42.8 3.9 %shard_map.126 = (f32[704,128]{1,0:T(8,128)S(1)}, bf16[352,128]{1,0:T(8,128)(2,1)S(1)}, bf16[352,128]{1,0:T(8,128)(2,1)S(1)}) custom-call(s32[4,4]{1,0:T(4,128)S(1)} %copy-done.8, bf16[128,128]{1,0:T(8,128)(2,1)S(1)} %get-tuple-element.33.refs_1_, bf16[128,1664]{1,0:T(8,128)(2,1)S(1)} %collective-permute-done.refs_0_.refs_2_, ...), custom_call_target="tpu_custom_call" | custom-call | tf_op jit(solution)/shard_map/pallas_call | solution.py:511
  46.7 0.2 collective-permute-start.11
  46.9 0.4 collective-permute-start.12
  47.3 1.0 %collective-permute-done.13.refs_3_.facing = bf16[384,128]{1,0:T(8,128)(2,1)S(1)} collective-permute-done((bf16[384,128]{1,0:T(8,128)(2,1)S(1)}, bf16[384,128]{1,0:T(8,128)(2,1)S(1)}, u32[]{:S(2)}, u32[]{:S(2)}) %collective-permute-start.13) | collective-permute-done | bytes 98336 | tf_op jit(solution)/shard_map/early_gradients_over_tm/ppermute | solution.py:662
  48.3 0.1 shard_map.127
  48.4 3.1 %collective-permute-start.18 = (bf16[768,128]{1,0:T(8,128)(2,1)S(1)}, bf16[768,128]{1,0:T(8,128)(2,1)S(1)}, u32[]{:S(2)}, u32[]{:S(2)}) collective-permute-start(bf16[768,128]{1,0:T(8,128)(2,1)S(1)} %get-tuple-element.60), channel_id=1, source_target_pairs={{4,0},{0,4},{12,8},{8,12},{5,1},{1,5},{13,9},{9,13},{6,2},{2,6},{1... | collective-permute-start | bytes 589832 | tf_op jit(solution)/shard_map/late_gradients_over_tm/ppermute | solution.py:662
  51.5 1.9 %collective-permute-start.14 = (bf16[128,128]{1,0:T(8,128)(2,1)S(1)}, bf16[128,128]{1,0:T(8,128)(2,1)S(1)}, u32[]{:S(2)}, u32[]{:S(2)}) collective-permute-start(bf16[128,128]{1,0:T(8,128)(2,1)S(1)} %get-tuple-element.56), channel_id=1, source_target_pairs={{4,0},{0,4},{12,8},{8,12},{5,1},{1,5},{13,9},{9,13},{6,2},{2,6},{1... | collective-permute-start | bytes 98312 | tf_op jit(solution)/shard_map/low_over_tm/ppermute | solution.py:662
  53.4 1.1 %collective-permute-start.15 = (bf16[128,128]{1,0:T(8,128)(2,1)S(1)}, bf16[128,128]{1,0:T(8,128)(2,1)S(1)}, u32[]{:S(2)}, u32[]{:S(2)}) collective-permute-start(bf16[128,128]{1,0:T(8,128)(2,1)S(1)} %get-tuple-element.57), channel_id=1, source_target_pairs={{8,0},{12,4},{0,8},{4,12},{9,1},{13,5},{1,9},{5,13},{10,2},{14,6},... | collective-permute-start | bytes 98312 | tf_op jit(solution)/shard_map/low_over_tm/ppermute | solution.py:662
  54.5 1.4 %collective-permute-start.16 = (bf16[128,128]{1,0:T(8,128)(2,1)S(1)}, bf16[128,128]{1,0:T(8,128)(2,1)S(1)}, u32[]{:S(2)}, u32[]{:S(2)}) collective-permute-start(bf16[128,128]{1,0:T(8,128)(2,1)S(1)} %get-tuple-element.58), channel_id=1, source_target_pairs={{12,0},{8,4},{4,8},{0,12},{13,1},{9,5},{5,9},{1,13},{14,2},{10,6},... | collective-permute-start | bytes 98312 | tf_op jit(solution)/shard_map/low_over_tm/ppermute | solution.py:662
  55.9 4.5 %collective-permute-done.14.refs_0_ = bf16[128,128]{1,0:T(8,128)(2,1)S(1)} collective-permute-done((bf16[128,128]{1,0:T(8,128)(2,1)S(1)}, bf16[128,128]{1,0:T(8,128)(2,1)S(1)}, u32[]{:S(2)}, u32[]{:S(2)}) %collective-permute-start.14) | collective-permute-done | bytes 32800 | tf_op jit(solution)/shard_map/low_over_tm/ppermute | solution.py:662
  60.4 1.4 %collective-permute-start.20 = (bf16[192,128]{1,0:T(8,128)(2,1)S(1)}, bf16[192,128]{1,0:T(8,128)(2,1)S(1)}, u32[]{:S(2)}, u32[]{:S(2)}) collective-permute-start(bf16[192,128]{1,0:T(8,128)(2,1)S(1)} %get-tuple-element.59.own), channel_id=1, source_target_pairs={{12,0},{8,4},{4,8},{0,12},{13,1},{9,5},{5,9},{1,13},{14,2},{10,6},... | collective-permute-start | bytes 147464 | tf_op jit(solution)/shard_map/late_gradients_over_tm/ppermute | solution.py:662
  61.8 0.4 collective-permute-done.16.refs_2_
  62.2 1.6 %collective-permute-start.17 = (bf16[128,128]{1,0:T(8,128)(2,1)S(1)}, bf16[128,128]{1,0:T(8,128)(2,1)S(1)}, u32[]{:S(2)}, u32[]{:S(2)}) collective-permute-start(bf16[128,128]{1,0:T(8,128)(2,1)S(1)} %shard_map.128.low_ref), channel_id=1, source_target_pairs={{0,2},{2,0},{1,3},{3,1},{4,6},{6,4},{5,7},{7,5},{8,10},{10,8},{9,1... | collective-permute-start | bytes 98312 | tf_op jit(solution)/shard_map/low_over_head/ppermute | solution.py:48
  63.8 2.5 %collective-permute-done.20.last = bf16[192,128]{1,0:T(8,128)(2,1)S(1)} collective-permute-done((bf16[192,128]{1,0:T(8,128)(2,1)S(1)}, bf16[192,128]{1,0:T(8,128)(2,1)S(1)}, u32[]{:S(2)}, u32[]{:S(2)}) %collective-permute-start.20) | collective-permute-done | bytes 49184 | tf_op jit(solution)/shard_map/late_gradients_over_tm/ppermute | solution.py:662
  66.5 1.9 %collective-permute-done.21.tail2 = bf16[2048,128]{1,0:T(8,128)(2,1)S(1)} collective-permute-done((bf16[2048,128]{1,0:T(8,128)(2,1)S(1)}, bf16[2048,128]{1,0:T(8,128)(2,1)S(1)}, u32[]{:S(2)}, u32[]{:S(2)}) %collective-permute-start.21) | collective-permute-done | bytes 524320 | tf_op jit(solution)/shard_map/tail_in_chip/ppermute | solution.py:48
  68.4 1.5 %shard_map.130 = (f32[128,1280]{1,0:T(8,128)}, f32[128,1280]{1,0:T(8,128)}, f32[128,1280]{1,0:T(8,128)}, f32[256,128]{1,0:T(8,128)}) custom-call(bf16[2048,128]{1,0:T(8,128)(2,1)S(1)} %shard_map.129.tail, bf16[2048,128]{1,0:T(8,128)(2,1)S(1)} %collective-permute-done.21.tail2), custom_call_target="tpu_custom_call" | custom-call | tf_op jit(solution)/shard_map/pallas_call | solution.py:625
  (42 shorter events, 0.5 us)
Async XLA Ops:
  0.6 12.8 %copy-start.3 = (bf16[128,1280]{1,0:T(8,128)(2,1)S(1)}, bf16[128,1280]{1,0:T(8,128)(2,1)}, u32[]{:S(2)}) copy-start(bf16[128,1280]{1,0:T(8,128)(2,1)} %do_ref.3) | copy-start | bytes 983044
  0.6 12.8 %copy-start.7 = (bf16[256,128]{1,0:T(8,128)(2,1)S(1)}, bf16[256,128]{1,0:T(8,128)(2,1)}, u32[]{:S(2)}) copy-start(bf16[256,128]{1,0:T(8,128)(2,1)} %t_ref.3) | copy-start | bytes 196612
  0.7 12.8 %copy-start.1 = (bf16[256,1280]{1,0:T(8,128)(2,1)S(1)}, bf16[256,1280]{1,0:T(8,128)(2,1)}, u32[]{:S(2)}) copy-start(bf16[256,1280]{1,0:T(8,128)(2,1)} %fv_ref.3) | copy-start | bytes 1966084
  0.7 12.8 %copy-start = (bf16[256,1280]{1,0:T(8,128)(2,1)S(1)}, bf16[256,1280]{1,0:T(8,128)(2,1)}, u32[]{:S(2)}) copy-start(bf16[256,1280]{1,0:T(8,128)(2,1)} %fk_ref.3) | copy-start | bytes 1966084
  0.7 12.8 %copy-start.2 = (bf16[128,1280]{1,0:T(8,128)(2,1)S(1)}, bf16[128,1280]{1,0:T(8,128)(2,1)}, u32[]{:S(2)}) copy-start(bf16[128,1280]{1,0:T(8,128)(2,1)} %fq_ref.3) | copy-start | bytes 983044
  3.2 23.6 %collective-permute-start = (bf16[128,1664]{1,0:T(8,128)(2,1)}, bf16[128,1664]{1,0:T(8,128)(2,1)S(1)}, u32[]{:S(2)}, u32[]{:S(2)}) collective-permute-start(bf16[128,1664]{1,0:T(8,128)(2,1)} %get-tuple-element.34), channel_id=1, source_target_pairs={{4,0},{0,4},{12,8},{8,12},{5,1},{1,5},{13,9},{9,13},{6,2},{2,6},{1... | collective-permute-start | bytes 1277960 | tf_op jit(solution)/shard_map/nearest_over_tm/ppermute | solution.py:662
  6.3 14.1 %collective-permute-start.1 = (bf16[128,640]{1,0:T(8,128)(2,1)}, bf16[128,640]{1,0:T(8,128)(2,1)S(1)}, u32[]{:S(2)}, u32[]{:S(2)}) collective-permute-start(bf16[128,640]{1,0:T(8,128)(2,1)} %get-tuple-element.35), channel_id=1, source_target_pairs={{8,0},{12,4},{0,8},{4,12},{9,1},{13,5},{1,9},{5,13},{10,2},{14,6},... | collective-permute-start | bytes 491528 | tf_op jit(solution)/shard_map/lead_over_tm/ppermute | solution.py:662
  8.9 17.9 %collective-permute-start.2 = (bf16[128,640]{1,0:T(8,128)(2,1)}, bf16[128,640]{1,0:T(8,128)(2,1)S(1)}, u32[]{:S(2)}, u32[]{:S(2)}) collective-permute-start(bf16[128,640]{1,0:T(8,128)(2,1)} %get-tuple-element.36), channel_id=1, source_target_pairs={{12,0},{8,4},{4,8},{0,12},{13,1},{9,5},{5,9},{1,13},{14,2},{10,6},... | collective-permute-start | bytes 491528 | tf_op jit(solution)/shard_map/lead_over_tm/ppermute | solution.py:662
  8.9 18.0 %collective-permute-start.6 = (bf16[128,512]{1,0:T(8,128)(2,1)}, bf16[128,512]{1,0:T(8,128)(2,1)S(1)}, u32[]{:S(2)}, u32[]{:S(2)}) collective-permute-start(bf16[128,512]{1,0:T(8,128)(2,1)} %get-tuple-element.45), channel_id=1, source_target_pairs={{12,4},{0,8},{13,5},{1,9},{14,6},{2,10},{15,7},{3,11},{28,20},{16,... | collective-permute-start | bytes 393224 | tf_op jit(solution)/shard_map/rest_over_tm/ppermute | solution.py:662
  12.7 14.2 %collective-permute-start.7 = (bf16[128,512]{1,0:T(8,128)(2,1)}, bf16[128,512]{1,0:T(8,128)(2,1)S(1)}, u32[]{:S(2)}, u32[]{:S(2)}) collective-permute-start(bf16[128,512]{1,0:T(8,128)(2,1)} %get-tuple-element.46), channel_id=1, source_target_pairs={{8,4},{4,8},{9,5},{5,9},{10,6},{6,10},{11,7},{7,11},{24,20},{20,24... | collective-permute-start | bytes 393224 | tf_op jit(solution)/shard_map/rest_over_tm/ppermute | solution.py:662
  26.8 5.6 %copy-start.6 = (bf16[128,1280]{1,0:T(8,128)(2,1)S(1)}, bf16[128,1280]{1,0:T(8,128)(2,1)}, u32[]{:S(2)}) copy-start(bf16[128,1280]{1,0:T(8,128)(2,1)} %refs_14_.3) | copy-start | bytes 983044
  26.9 5.6 %copy-start.4 = (bf16[128,1280]{1,0:T(8,128)(2,1)S(1)}, bf16[128,1280]{1,0:T(8,128)(2,1)}, u32[]{:S(2)}) copy-start(bf16[128,1280]{1,0:T(8,128)(2,1)} %refs_12_.1) | copy-start | bytes 983044
  26.9 5.6 %copy-start.5 = (bf16[128,1280]{1,0:T(8,128)(2,1)S(1)}, bf16[128,1280]{1,0:T(8,128)(2,1)}, u32[]{:S(2)}) copy-start(bf16[128,1280]{1,0:T(8,128)(2,1)} %refs_13_.1) | copy-start | bytes 983044
  26.9 5.5 %collective-permute-start.3 = (bf16[128,1152]{1,0:T(8,128)(2,1)S(1)}, bf16[128,1152]{1,0:T(8,128)(2,1)S(1)}, u32[]{:S(2)}, u32[]{:S(2)}) collective-permute-start(bf16[128,1152]{1,0:T(8,128)(2,1)S(1)} %shard_map.122), channel_id=1, source_target_pairs={{0,1},{1,0},{2,3},{3,2},{4,5},{5,4},{6,7},{7,6},{8,9},{9,8},{10,11... | collective-permute-start | bytes 884744 | tf_op jit(solution)/shard_map/lead_in_chip/ppermute | solution.py:48
  27.0 5.4 %collective-permute-start.8 = (bf16[128,768]{1,0:T(8,128)(2,1)S(1)}, bf16[128,768]{1,0:T(8,128)(2,1)S(1)}, u32[]{:S(2)}, u32[]{:S(2)}) collective-permute-start(bf16[128,768]{1,0:T(8,128)(2,1)S(1)} %shard_map.123), channel_id=1, source_target_pairs={{0,1},{1,0},{2,3},{3,2},{4,5},{5,4},{6,7},{7,6},{8,9},{9,8},{10,11... | collective-permute-start | bytes 589832 | tf_op jit(solution)/shard_map/rest_in_chip/ppermute | solution.py:48
  27.6 13.5 %collective-permute-start.4 = (bf16[128,512]{1,0:T(8,128)(2,1)S(1)}, bf16[128,512]{1,0:T(8,128)(2,1)S(1)}, u32[]{:S(2)}, u32[]{:S(2)}) collective-permute-start(bf16[128,512]{1,0:T(8,128)(2,1)S(1)} %get-tuple-element.40), channel_id=1, source_target_pairs={{8,0},{12,4},{0,8},{4,12},{9,1},{13,5},{1,9},{5,13},{10,2},{14,6},... | collective-permute-start | bytes 393224 | tf_op jit(solution)/shard_map/late_over_tm/ppermute | solution.py:662
  31.0 10.0 %collective-permute-start.5 = (bf16[128,512]{1,0:T(8,128)(2,1)S(1)}, bf16[128,512]{1,0:T(8,128)(2,1)S(1)}, u32[]{:S(2)}, u32[]{:S(2)}) collective-permute-start(bf16[128,512]{1,0:T(8,128)(2,1)S(1)} %get-tuple-element.41), channel_id=1, source_target_pairs={{12,0},{8,4},{4,8},{0,12},{13,1},{9,5},{5,9},{1,13},{14,2},{10,6},... | collective-permute-start | bytes 393224 | tf_op jit(solution)/shard_map/late_over_tm/ppermute | solution.py:662
  32.4 0.7 copy-start.8
  37.2 3.8 %collective-permute-start.9 = (bf16[384,128]{1,0:T(8,128)(2,1)S(1)}, bf16[384,128]{1,0:T(8,128)(2,1)S(1)}, u32[]{:S(2)}, u32[]{:S(2)}) collective-permute-start(bf16[384,128]{1,0:T(8,128)(2,1)S(1)} %get-tuple-element.48), channel_id=1, source_target_pairs={{0,1},{1,0},{2,3},{3,2},{4,5},{5,4},{6,7},{7,6},{8,9},{9,8},{10,11... | collective-permute-start | bytes 294920 | tf_op jit(solution)/shard_map/early_gradients_in_chip/ppermute | solution.py:48
  41.0 1.8 %collective-permute-start.10 = (bf16[128,1536]{1,0:T(8,128)(2,1)S(1)}, bf16[128,1536]{1,0:T(8,128)(2,1)S(1)}, u32[]{:S(2)}, u32[]{:S(2)}) collective-permute-start(bf16[128,1536]{1,0:T(8,128)(2,1)S(1)} %shard_map.125), channel_id=1, source_target_pairs={{0,1},{1,0},{2,3},{3,2},{4,5},{5,4},{6,7},{7,6},{8,9},{9,8},{10,11... | collective-permute-start | bytes 1179656 | tf_op jit(solution)/shard_map/late_in_chip/ppermute | solution.py:48
  41.2 7.2 %collective-permute-start.13 = (bf16[384,128]{1,0:T(8,128)(2,1)S(1)}, bf16[384,128]{1,0:T(8,128)(2,1)S(1)}, u32[]{:S(2)}, u32[]{:S(2)}) collective-permute-start(bf16[384,128]{1,0:T(8,128)(2,1)S(1)} %add_convert_fusion.refs_17_.refs_2_.piece), channel_id=1, source_target_pairs={{12,0},{8,4},{4,8},{0,12},{13,1},{9,5},{5,9},{1,13},{14,2},{10,6},... | collective-permute-start | bytes 294920 | tf_op jit(solution)/shard_map/early_gradients_over_tm/ppermute | solution.py:662
  46.7 1.6 %collective-permute-start.11 = (bf16[352,128]{1,0:T(8,128)(2,1)S(1)}, bf16[352,128]{1,0:T(8,128)(2,1)S(1)}, u32[]{:S(2)}, u32[]{:S(2)}) collective-permute-start(bf16[352,128]{1,0:T(8,128)(2,1)S(1)} %get-tuple-element.53), channel_id=1, source_target_pairs={{0,1},{1,0},{2,3},{3,2},{4,5},{5,4},{6,7},{7,6},{8,9},{9,8},{10,11... | collective-permute-start | bytes 270344 | tf_op jit(solution)/shard_map/late_sums_in_chip/ppermute | solution.py:48
  46.9 1.4 %collective-permute-start.12 = (bf16[352,128]{1,0:T(8,128)(2,1)S(1)}, bf16[352,128]{1,0:T(8,128)(2,1)S(1)}, u32[]{:S(2)}, u32[]{:S(2)}) collective-permute-start(bf16[352,128]{1,0:T(8,128)(2,1)S(1)} %get-tuple-element.54), channel_id=1, source_target_pairs={{0,1},{1,0},{2,3},{3,2},{4,5},{5,4},{6,7},{7,6},{8,9},{9,8},{10,11... | collective-permute-start | bytes 270344 | tf_op jit(solution)/shard_map/late_sums_in_chip/ppermute | solution.py:48
  48.4 17.9 %collective-permute-start.18 = (bf16[768,128]{1,0:T(8,128)(2,1)S(1)}, bf16[768,128]{1,0:T(8,128)(2,1)S(1)}, u32[]{:S(2)}, u32[]{:S(2)}) collective-permute-start(bf16[768,128]{1,0:T(8,128)(2,1)S(1)} %get-tuple-element.60), channel_id=1, source_target_pairs={{4,0},{0,4},{12,8},{8,12},{5,1},{1,5},{13,9},{9,13},{6,2},{2,6},{1... | collective-permute-start | bytes 589832 | tf_op jit(solution)/shard_map/late_gradients_over_tm/ppermute | solution.py:662
  51.5 14.8 %collective-permute-start.19 = (bf16[384,128]{1,0:T(8,128)(2,1)S(1)}, bf16[384,128]{1,0:T(8,128)(2,1)S(1)}, u32[]{:S(2)}, u32[]{:S(2)}) collective-permute-start(bf16[384,128]{1,0:T(8,128)(2,1)S(1)} %get-tuple-element.61), channel_id=1, source_target_pairs={{8,0},{12,4},{0,8},{4,12},{9,1},{13,5},{1,9},{5,13},{10,2},{14,6},... | collective-permute-start | bytes 294920 | tf_op jit(solution)/shard_map/late_gradients_over_tm/ppermute | solution.py:662
  51.5 8.9 %collective-permute-start.14 = (bf16[128,128]{1,0:T(8,128)(2,1)S(1)}, bf16[128,128]{1,0:T(8,128)(2,1)S(1)}, u32[]{:S(2)}, u32[]{:S(2)}) collective-permute-start(bf16[128,128]{1,0:T(8,128)(2,1)S(1)} %get-tuple-element.56), channel_id=1, source_target_pairs={{4,0},{0,4},{12,8},{8,12},{5,1},{1,5},{13,9},{9,13},{6,2},{2,6},{1... | collective-permute-start | bytes 98312 | tf_op jit(solution)/shard_map/low_over_tm/ppermute | solution.py:662
  53.4 8.3 %collective-permute-start.15 = (bf16[128,128]{1,0:T(8,128)(2,1)S(1)}, bf16[128,128]{1,0:T(8,128)(2,1)S(1)}, u32[]{:S(2)}, u32[]{:S(2)}) collective-permute-start(bf16[128,128]{1,0:T(8,128)(2,1)S(1)} %get-tuple-element.57), channel_id=1, source_target_pairs={{8,0},{12,4},{0,8},{4,12},{9,1},{13,5},{1,9},{5,13},{10,2},{14,6},... | collective-permute-start | bytes 98312 | tf_op jit(solution)/shard_map/low_over_tm/ppermute | solution.py:662
  54.5 7.7 %collective-permute-start.16 = (bf16[128,128]{1,0:T(8,128)(2,1)S(1)}, bf16[128,128]{1,0:T(8,128)(2,1)S(1)}, u32[]{:S(2)}, u32[]{:S(2)}) collective-permute-start(bf16[128,128]{1,0:T(8,128)(2,1)S(1)} %get-tuple-element.58), channel_id=1, source_target_pairs={{12,0},{8,4},{4,8},{0,12},{13,1},{9,5},{5,9},{1,13},{14,2},{10,6},... | collective-permute-start | bytes 98312 | tf_op jit(solution)/shard_map/low_over_tm/ppermute | solution.py:662
  60.4 5.9 %collective-permute-start.20 = (bf16[192,128]{1,0:T(8,128)(2,1)S(1)}, bf16[192,128]{1,0:T(8,128)(2,1)S(1)}, u32[]{:S(2)}, u32[]{:S(2)}) collective-permute-start(bf16[192,128]{1,0:T(8,128)(2,1)S(1)} %get-tuple-element.59.own), channel_id=1, source_target_pairs={{12,0},{8,4},{4,8},{0,12},{13,1},{9,5},{5,9},{1,13},{14,2},{10,6},... | collective-permute-start | bytes 147464 | tf_op jit(solution)/shard_map/late_gradients_over_tm/ppermute | solution.py:662
  62.2 4.1 %collective-permute-start.17 = (bf16[128,128]{1,0:T(8,128)(2,1)S(1)}, bf16[128,128]{1,0:T(8,128)(2,1)S(1)}, u32[]{:S(2)}, u32[]{:S(2)}) collective-permute-start(bf16[128,128]{1,0:T(8,128)(2,1)S(1)} %shard_map.128.low_ref), channel_id=1, source_target_pairs={{0,2},{2,0},{1,3},{3,1},{4,6},{6,4},{5,7},{7,5},{8,10},{10,8},{9,1... | collective-permute-start | bytes 98312 | tf_op jit(solution)/shard_map/low_over_head/ppermute | solution.py:48
  66.4 2.0 %collective-permute-start.21 = (bf16[2048,128]{1,0:T(8,128)(2,1)S(1)}, bf16[2048,128]{1,0:T(8,128)(2,1)S(1)}, u32[]{:S(2)}, u32[]{:S(2)}) collective-permute-start(bf16[2048,128]{1,0:T(8,128)(2,1)S(1)} %shard_map.129.tail), channel_id=1, source_target_pairs={{0,1},{1,0},{2,3},{3,2},{4,5},{5,4},{6,7},{7,6},{8,9},{9,8},{10,11... | collective-permute-start | bytes 1572872 | tf_op jit(solution)/shard_map/tail_in_chip/ppermute | solution.py:48

commit v10 on v8

--- a/solution.py
+++ b/solution.py
@@ -13,7 +13,7 @@
 SCALE = DH ** (-0.5)
 F32 = jnp.float32
 BF16 = jnp.bfloat16
-GIVES = 4
+GIVES = 2
 SMALL = pltpu.CompilerParams(vmem_limit_bytes=16 * 1024 * 1024)
 
 
@@ -312,23 +312,23 @@
     )(fq, do, fk, fv, t)
 
 
-def pick_kernel(spans, apart, *refs):
-    at = 0
-    for n, (start, size) in enumerate(spans):
-        out = refs[n - len(spans)] if apart else refs[-1].at[:, pl.ds(at, size)]
-        out[...] = refs[n][:, start : start + size]
-        at += size
-
-
-def pick(parts, size, apart, after=()):
+def pick_kernel(spans, groups, *refs):
+    n = 0
+    for out, count in zip(refs[-len(groups) :], groups):
+        for at in range(count):
+            start, size = spans[n]
+            out[:, at * size : (at + 1) * size] = refs[n][:, start : start + size]
+            n += 1
+
+
+def pick(parts, size, groups, after=()):
     arrays = [array for array, _ in parts]
     rows, dtype = arrays[0].shape[0], arrays[0].dtype
-    shapes = [(rows, size)] * len(arrays) if apart else [(rows, size * len(arrays))]
     return pl.pallas_call(
-        functools.partial(pick_kernel, [(start, size) for _, start in parts], apart),
+        functools.partial(pick_kernel, [(start, size) for _, start in parts], groups),
         in_specs=vmem(len(arrays)) + [pl.BlockSpec(memory_space=pl.ANY)] * len(after),
-        out_specs=vmem(len(shapes)),
-        out_shape=[jax.ShapeDtypeStruct(shape, dtype) for shape in shapes],
+        out_specs=vmem(len(groups)),
+        out_shape=[jax.ShapeDtypeStruct((rows, size * count), dtype) for count in groups],
         compiler_params=SMALL,
     )(*arrays, *after)
 
@@ -352,48 +352,58 @@
 
     span = 2 if frames % 2 == 0 else 1
     wide = span * rows
-    dks, dvs, dqs = [None] * (2 * frames), [None] * (2 * frames), []
-    for first in range(0, frames, span):
-        mine = range(first, first + span)
-        blocks = list(range(frames)) + [
-            frames + j for j in range(frames) if any(abs(i - j) <= NEAR for i in mine)
+    groups = [range(first, first + span) for first in range(0, frames, span)]
+    seen = [
+        list(range(frames))
+        + [frames + j for j in range(frames) if any(abs(i - j) <= NEAR for i in mine)]
+        for mine in groups
+    ]
+    here = [slice(mine[0] * rows, mine[0] * rows + wide) for mine in groups]
+    pairs_of = range(len(groups))
+
+    def gather(whole, g, axis):
+        parts = [
+            whole[b * rows : (b + 1) * rows] if axis == 0 else whole[:, b * rows : (b + 1) * rows]
+            for b in seen[g]
         ]
-        here = slice(first * rows, first * rows + wide)
-        q_p, do_p = query[here], do[here]
-
-        def gather(whole, axis):
-            parts = [
-                whole[b * rows : (b + 1) * rows] if axis == 0 else whole[:, b * rows : (b + 1) * rows]
-                for b in blocks
-            ]
-            return jnp.concatenate(parts, axis=axis)
-
-        raw = dot_nt(gather(keys, 0), q_p)
+        return jnp.concatenate(parts, axis=axis)
+
+    def block(whole, n):
+        return whole[n * rows : (n + 1) * rows]
+
+    def softmax(g, raw):
         scores = [
-            raw[n * rows : (n + 1) * rows] * SCALE + jnp.concatenate([bias(i, b) for i in mine], axis=1)
-            for n, b in enumerate(blocks)
+            block(raw, n) * SCALE + jnp.concatenate([bias(i, b) for i in groups[g]], axis=1)
+            for n, b in enumerate(seen[g])
         ]
         top = jnp.max(functools.reduce(jnp.maximum, scores), axis=0, keepdims=True)
         shifted = [jnp.exp(s - top) for s in scores]
         inverse = 1.0 / jnp.sum(functools.reduce(jnp.add, shifted), axis=0, keepdims=True)
-        probs = [s * inverse for s in shifted]
-        low = jnp.concatenate([p.astype(BF16) for p in probs], axis=0)
-        attended = dot_nn(gather(values_t, 1), low).astype(BF16).astype(F32)
-        delta = jnp.sum(do_t[:, here].astype(F32) * attended, axis=0, keepdims=True)
-        prob_grad = dot_nt(gather(values, 0), do_p)
-        grad = jnp.concatenate(
-            [
-                (probs[n] * (prob_grad[n * rows : (n + 1) * rows] - delta)).astype(BF16)
-                for n in range(len(blocks))
-            ],
-            axis=0,
-        )
-        dqs.append((dot_nn(gather(keys_t, 1), grad) * SCALE).astype(BF16).T)
-        dk, dv = dot_nn(grad, q_p), dot_nn(low, do_p)
-        for n, b in enumerate(blocks):
-            part = slice(n * rows, (n + 1) * rows)
-            dks[b] = dk[part] if dks[b] is None else dks[b] + dk[part]
-            dvs[b] = dv[part] if dvs[b] is None else dvs[b] + dv[part]
+        return [s * inverse for s in shifted]
+
+    raws = [dot_nt(gather(keys, g, 0), query[here[g]]) for g in pairs_of]
+    prob_grads = [dot_nt(gather(values, g, 0), do[here[g]]) for g in pairs_of]
+    probs = [softmax(g, raws[g]) for g in pairs_of]
+    lows = [jnp.concatenate([p.astype(BF16) for p in probs[g]], axis=0) for g in pairs_of]
+    grads = []
+    for g in pairs_of:
+        attended = dot_nn(gather(values_t, g, 1), lows[g]).astype(BF16).astype(F32)
+        delta = jnp.sum(do_t[:, here[g]].astype(F32) * attended, axis=0, keepdims=True)
+        parts = [
+            (probs[g][n] * (block(prob_grads[g], n) - delta)).astype(BF16) for n in range(len(seen[g]))
+        ]
+        grads.append(jnp.concatenate(parts, axis=0))
+    dvs, dks = [None] * (2 * frames), [None] * (2 * frames)
+
+    def add(sums, g, whole):
+        for n, b in enumerate(seen[g]):
+            sums[b] = block(whole, n) if sums[b] is None else sums[b] + block(whole, n)
+
+    for g in pairs_of:
+        add(dvs, g, dot_nn(lows[g], do[here[g]]))
+    for g in pairs_of:
+        add(dks, g, dot_nn(grads[g], query[here[g]]))
+    dqs = [(dot_nn(gather(keys_t, g, 1), grads[g]) * SCALE).astype(BF16).T for g in pairs_of]
     dq = jnp.concatenate(dqs, axis=0)
     dk = (jnp.concatenate(dks, axis=0) * SCALE).astype(BF16)
     dv = jnp.concatenate(dvs, axis=0).astype(BF16)
@@ -523,66 +533,69 @@
 
 
 def hand_out_kernel(frames, size, parts, keep_ref, *refs):
-    gots, (piece, facing), (own_ref, *sends, total) = refs[:parts], refs[parts : parts + 2], refs[-frames - 2 :]
+    gots, (piece, facing), (own_ref, *sends, total) = refs[:parts], refs[parts : parts + 2], refs[parts + 2 :]
     me = lax.axis_index("tm")
     rows = own_ref.shape[0]
     total[...] = keep_ref[...] + jnp.concatenate([got[...].astype(F32) for got in gots], axis=0)
-    grads = total[:size, :].astype(BF16)
     for m in range(frames):
         low = total[pl.ds(pl.multiple_of(size + (me ^ m) * rows, 8), rows), :]
         if m == 0:
             own_ref[...] = low
-        sends[m][:rows, :] = low.astype(BF16)
-        sends[m][rows : rows + size, :] = grads
-    sends[1][rows + size : rows + 3 * size, :] = piece[...]
-    sends[1][rows + 3 * size :, :] = facing[size:, :]
-
-
-def hand_out(frames, rows, keep, gots, piece, facing, after):
+        else:
+            sends[m - 1][:rows, :] = low.astype(BF16)
+            sends[m - 1][rows : rows + size, :] = total[:size, :].astype(BF16)
+    sends[0][rows + size : rows + 3 * size, :] = piece[...]
+    sends[0][rows + 3 * size :, :] = facing[size:, :]
+    sends[1][rows + size :, :] = piece[:size, :]
+
+
+def hand_out(frames, rows, keep, gots, piece, facing):
     size, rank = keep.shape[0] - frames * rows, keep.shape[1]
-    sends = [jax.ShapeDtypeStruct((rows + size * (4 if m == 1 else 1), rank), BF16) for m in range(frames)]
-    return pl.pallas_call(
+    own, *sends = pl.pallas_call(
         functools.partial(hand_out_kernel, frames, size, len(gots)),
-        in_specs=vmem(3 + len(gots)) + [pl.BlockSpec(memory_space=pl.ANY)] * len(after),
-        out_specs=vmem(frames + 1),
-        out_shape=[jax.ShapeDtypeStruct((rows, rank), F32)] + sends,
+        in_specs=vmem(3 + len(gots)),
+        out_specs=vmem(frames),
+        out_shape=[jax.ShapeDtypeStruct((rows, rank), F32)]
+        + [jax.ShapeDtypeStruct((rows + size * n, rank), BF16) for n in (4, 2, 1)],
         scratch_shapes=[pltpu.VMEM(keep.shape, F32)],
         compiler_params=SMALL,
-    )(keep, *gots, piece, facing, *after)
-
-
-def collect_kernel(frames, wide, own_ref, *refs):
-    gots, (piece, far, facing), (out_ref, low_ref) = refs[:frames], refs[frames : frames + 3], refs[-2:]
-    rows = own_ref.shape[0]
-    size = gots[0].shape[0] - rows
-    low = own_ref[...]
-    for m in range(1, frames):
-        low = low + gots[m][:rows, :].astype(F32)
+    )(keep, *gots, piece, facing)
+    return own, sends
+
+
+def collect_kernel(wide, own_low, own, near, third, last, piece, facing, out_ref, low_ref):
+    rows = own_low.shape[0]
+    size = own.shape[0] - rows
+    low = own_low[...]
+    for got in (near, third, last):
+        low = low + got[:rows, :].astype(F32)
     out_ref[:rows, :] = low.astype(BF16)
     low_ref[...] = low.astype(BF16)
-    near = rows + size
     middle = lookup(wide, lax.axis_index("tm")) > 0
-    blocks = [got[rows:near, :] for got in gots]
-    blocks += [piece[:size, :], gots[1][near : near + size, :], far[...], facing[:size, :]]
-    blocks.append(jnp.where(middle, piece[size:, :], gots[1][near + size : near + 2 * size, :]))
-    blocks.append(jnp.where(middle, facing[size:, :], gots[1][near + 2 * size :, :]))
+
+    def part(ref, n):
+        return ref[rows + n * size : rows + (n + 1) * size, :]
+
+    blocks = [part(ref, 0) for ref in (own, near, third, last)]
+    blocks += [piece[:size, :], part(near, 1), part(third, 1), facing[:size, :]]
+    blocks.append(jnp.where(middle, piece[size:, :], part(near, 2)))
+    blocks.append(jnp.where(middle, facing[size:, :], part(near, 3)))
     for n, block in enumerate(blocks):
         out_ref[rows + n * size : rows + (n + 1) * size, :] = block
 
 
-def collect(wide, own, gots, piece, far, facing):
-    frames, (rows, rank) = len(gots), own.shape
-    size = gots[0].shape[0] - rows
+def collect(wide, own_low, own, gots, piece, facing):
+    (rows, rank), size = own_low.shape, piece.shape[0] // 2
     return pl.pallas_call(
-        functools.partial(collect_kernel, frames, wide),
-        in_specs=vmem(frames + 4),
+        functools.partial(collect_kernel, wide),
+        in_specs=vmem(4 + len(gots)),
         out_specs=vmem(2),
         out_shape=[
-            jax.ShapeDtypeStruct((rows + (2 * frames + 2) * size, rank), BF16),
+            jax.ShapeDtypeStruct((rows + 10 * size, rank), BF16),
             jax.ShapeDtypeStruct((rows, rank), BF16),
         ],
         compiler_params=SMALL,
-    )(own, *gots, piece, far, facing)
+    )(own_low, own, *gots, piece, facing)
 
 
 def place_kernel(frames, lead, late, rest, tail, tail2, low_head, low_diag, *outs):
@@ -675,35 +688,33 @@
         rest_got.append((meet("rest", packed[2 * m - 2], m, wide), 0))
         late_got.append((meet("late", packed_late[m - 2], m), 0))
 
-    def sides(name, n, got, wide_t, apart, skip, after=()):
+    def sides(name, n, got, wide_t, groups, skip, after=()):
         size = 4 * DH - skip + (rank if wide_t else 0)
-        picked = pick([(a, start + skip) for a, start in got], size, apart, after)
+        picked = pick([(a, start + skip) for a, start in got], size, groups, after)
         cross = [swap_in_chip(name, block) for block in picked]
         where = 2 * DH - skip
-        cross = [(cross[m], where) if apart else (cross[0], m * size + where) for m in range(frames - 1)]
+        cross = [(block, at * size + where) for block, count in zip(cross, groups) for at in range(count)]
         rows_here = [(kept[2 * n], 0)] + got
         rows_there = [(kept[2 * n + 1], 0)] + cross
         return rows_here, rows_there, cross
 
-    *lead_side, cross = sides("lead", 0, lead_got, True, False, 2 * DH, kept[:1])
+    *lead_side, cross = sides("lead", 0, lead_got, True, (3,), 2 * DH, kept[:1])
     t_side = (
         [(kept[6], 0)] + [(a, start + 4 * DH) for a, start in lead_got],
         [(kept[7], 0)] + [(block, start + 2 * DH) for block, start in cross],
     )
-    *rest_side, _ = sides("rest", 1, rest_got, False, False, 2 * DH)
+    *rest_side, _ = sides("rest", 1, rest_got, False, (3,), 2 * DH)
     early = [lead, rest]
     keep, give, *low = head_group(early, band_width, [t_side, lead_side, rest_side], adapters)
     got = swap_in_chip("early_gradients", give)
     piece = (keep + got.astype(F32)).astype(BF16)
-    *late_side, _ = sides("late", 2, late_got, False, False, 0, [got])
-    cut = 3 * rank // 2
-    far = meet("early_gradients", piece[:cut], 2)
+    *late_side, _ = sides("late", 2, late_got, False, (3,), 0, [got])
     facing = meet("early_gradients", piece, 3)
     keep, *gives = head_group([late], band_width, [t_side, late_side], adapters, low, [piece])
     gives = [swap_in_chip("late_sums", g) for g in gives]
-    own, *sends = hand_out(frames, rows, keep, gives, piece, facing, [far])
-    gots = [sends[0]] + [meet("late_sums", sends[m], m) for m in range(1, frames)]
-    tail, low = collect(rest[1], own, gots, piece, far, facing)
+    own_low, sends = hand_out(frames, rows, keep, gives, piece, facing)
+    gots = [meet("late_sums", block, m) for m, block in enumerate(sends, 1)]
+    tail, low = collect(rest[1], own_low, sends[2], gots, piece, facing)
     diag = [(0, 3), (1, 2), (2, 1), (3, 0)]
     with jax.named_scope("low_over_head"):
         low_head, low_diag = swap(low, "head"), lax.ppermute(low, ("head", "rep"), diag)

time: 71.7 us -> 70.2 us (0.979)
  starting transfers between devices: 27.5 us -> 25 us
  waiting for transfers between devices: 29.2 us -> 31.3 us
  Pallas kernels: 13.2 us -> 12.1 us
    ppermute x12 -> x11, waiting for transfers between devices: 25 us -> 27.7 us  [meet(): return lax.ppermute(block, 'tm', [(j ^ m, j) for j in targets])]
    ppermute x12 -> x11, starting transfers between devices: 24.1 us -> 21.5 us  [meet(): return lax.ppermute(block, 'tm', [(j ^ m, j) for j in targets])]
    ppermute x1, starting transfers between devices: 0.31 us -> 1.61 us  [exchange_plan(): lax.ppermute(low, ('head', 'rep'), diag)]
    ppermute x10 -> x8, starting transfers between devices: 3.1 us -> 1.94 us  [swap(): return lax.ppermute(block, axis, [(0, 1), (1, 0)])]
    pallas_call x2, Pallas kernels: 7.97 us -> 6.88 us  [head_group(): pl.pallas_call(functools.partial(group_kernel, heads, frames, chained, le...]
    ppermute x10 -> x8, waiting for transfers between devices: 3.27 us -> 2.39 us  [swap(): return lax.ppermute(block, axis, [(0, 1), (1, 0)])]
  transfers between devices with their start and end apart: 23 -> 20, of which waited for: 10 -> 8; matrix products, arithmetic and copies ran while one was open for 0% -> 0% of each run, Pallas kernels for 13% -> 11%
where the time goes in v10:
time: 70.2 us; the launch traced here: 70.1 us
  waiting for transfers between devices  31.3 us (45%)
  starting transfers between devices  25 us (36%)
  Pallas kernels  12.1 us (17%)
  between operations  0.9 us (1%)
    ppermute x11, waiting for transfers between devices, meet(): return lax.ppermute(block, 'tm', [(j ^ m, j) for j in targets])  27.7 us
    ppermute x11, starting transfers between devices, meet(): return lax.ppermute(block, 'tm', [(j ^ m, j) for j in targets])  21.5 us
    pallas_call x2, Pallas kernels, head_group(): pl.pallas_call(functools.partial(group_kernel, heads, frames, chained, le...  6.88 us
    pallas_call x2, Pallas kernels, pack(): pl.pallas_call(functools.partial(pack_kernel, frames, outputs), in_specs=...  3.51 us
    ppermute x8, waiting for transfers between devices, swap(): return lax.ppermute(block, axis, [(0, 1), (1, 0)])  2.39 us
    ppermute x8, starting transfers between devices, swap(): return lax.ppermute(block, axis, [(0, 1), (1, 0)])  1.94 us
    ppermute x1, starting transfers between devices, exchange_plan(): lax.ppermute(low, ('head', 'rep'), diag)  1.61 us
    pallas_call x1, Pallas kernels, place(): pl.pallas_call(functools.partial(place_kernel, frames, lead, late, rest),...  1.47 us
  transfers between devices with their start and end apart: 20, of which 8 were waited for; matrix products, arithmetic and copies ran while one was open for 0% of the time, Pallas kernels for 11%

profile of v10, /device:TPU:0, one launch (start us, length us, event | category | flops | bytes accessed | tf_op | source)
XLA Modules:
  0.0 70.1 jit_solution(4238409507896391569)
XLA Ops:
  0.7 2.6 %shard_map.121 = (bf16[128,1664]{1,0:T(8,128)(2,1)}, bf16[128,640]{1,0:T(8,128)(2,1)}, bf16[128,512]{1,0:T(8,128)(2,1)}, bf16[128,640]{1,0:T(8,128)(2,1)}, bf16[128,512]{1,0:T(8,128)(2,1)}) custom-call(bf16[128,1280]{1,0:T(8,128)(2,1)} %fq_ref.3, bf16[128,1280]{1,0:T(8,128)(2,1)} %do_ref.3, bf16[256,1280]{1,0:T(8,128)(2,1)} %fk_ref.3, ...), custom_call_target="tpu_custom_call" | custom-call | tf_op jit(solution)/shard_map/pallas_call | solution.py:301
  3.3 3.1 %collective-permute-start = (bf16[128,1664]{1,0:T(8,128)(2,1)}, bf16[128,1664]{1,0:T(8,128)(2,1)S(1)}, u32[]{:S(2)}, u32[]{:S(2)}) collective-permute-start(bf16[128,1664]{1,0:T(8,128)(2,1)} %get-tuple-element.33), channel_id=1, source_target_pairs={{4,0},{0,4},{12,8},{8,12},{5,1},{1,5},{13,9},{9,13},{6,2},{2,6},{1... | collective-permute-start | bytes 1277960 | tf_op jit(solution)/shard_map/nearest_over_tm/ppermute | solution.py:661
  6.3 2.6 %collective-permute-start.1 = (bf16[128,640]{1,0:T(8,128)(2,1)}, bf16[128,640]{1,0:T(8,128)(2,1)S(1)}, u32[]{:S(2)}, u32[]{:S(2)}) collective-permute-start(bf16[128,640]{1,0:T(8,128)(2,1)} %get-tuple-element.34), channel_id=1, source_target_pairs={{8,0},{12,4},{0,8},{4,12},{9,1},{13,5},{1,9},{5,13},{10,2},{14,6},... | collective-permute-start | bytes 491528 | tf_op jit(solution)/shard_map/lead_over_tm/ppermute | solution.py:661
  8.9 3.8 %collective-permute-start.6 = (bf16[128,512]{1,0:T(8,128)(2,1)}, bf16[128,512]{1,0:T(8,128)(2,1)S(1)}, u32[]{:S(2)}, u32[]{:S(2)}) collective-permute-start(bf16[128,512]{1,0:T(8,128)(2,1)} %get-tuple-element.44), channel_id=1, source_target_pairs={{12,4},{0,8},{13,5},{1,9},{14,6},{2,10},{15,7},{3,11},{28,20},{16,... | collective-permute-start | bytes 393224 | tf_op jit(solution)/shard_map/rest_over_tm/ppermute | solution.py:661
  12.8 0.7 collective-permute-start.7
  13.5 0.9 %shard_map.120 = (bf16[128,512]{1,0:T(8,128)(2,1)S(1)}, bf16[128,512]{1,0:T(8,128)(2,1)S(1)}, bf16[128,512]{1,0:T(8,128)(2,1)S(1)}, bf16[128,256]{1,0:T(8,128)(2...) custom-call(bf16[128,1280]{1,0:T(8,128)(2,1)S(1)} %copy-done.2, ...), custom_call_target="tpu_custom_call" | custom-call | tf_op jit(solution)/shard_map/pallas_call | solution.py:301
  14.4 6.0 %collective-permute-done.1.refs_1_.refs_3_ = bf16[128,640]{1,0:T(8,128)(2,1)S(1)} collective-permute-done((bf16[128,640]{1,0:T(8,128)(2,1)}, bf16[128,640]{1,0:T(8,128)(2,1)S(1)}, u32[]{:S(2)}, u32[]{:S(2)}) %collective-permute-start.1) | collective-permute-done | bytes 163872 | tf_op jit(solution)/shard_map/lead_over_tm/ppermute | solution.py:661
  20.4 6.4 %collective-permute-done.2.refs_2_.refs_4_ = bf16[128,640]{1,0:T(8,128)(2,1)S(1)} collective-permute-done((bf16[128,640]{1,0:T(8,128)(2,1)}, bf16[128,640]{1,0:T(8,128)(2,1)S(1)}, u32[]{:S(2)}, u32[]{:S(2)}) %collective-permute-start.2) | collective-permute-done | bytes 163872 | tf_op jit(solution)/shard_map/lead_over_tm/ppermute | solution.py:661
  26.9 0.1 collective-permute-start.3
  27.0 0.5 collective-permute-start.8
  27.6 3.5 %collective-permute-start.4 = (bf16[128,512]{1,0:T(8,128)(2,1)S(1)}, bf16[128,512]{1,0:T(8,128)(2,1)S(1)}, u32[]{:S(2)}, u32[]{:S(2)}) collective-permute-start(bf16[128,512]{1,0:T(8,128)(2,1)S(1)} %get-tuple-element.39), channel_id=1, source_target_pairs={{8,0},{12,4},{0,8},{4,12},{9,1},{13,5},{1,9},{5,13},{10,2},{14,6},... | collective-permute-start | bytes 393224 | tf_op jit(solution)/shard_map/late_over_tm/ppermute | solution.py:661
  31.0 1.4 %collective-permute-start.5 = (bf16[128,512]{1,0:T(8,128)(2,1)S(1)}, bf16[128,512]{1,0:T(8,128)(2,1)S(1)}, u32[]{:S(2)}, u32[]{:S(2)}) collective-permute-start(bf16[128,512]{1,0:T(8,128)(2,1)S(1)} %get-tuple-element.40), channel_id=1, source_target_pairs={{12,0},{8,4},{4,8},{0,12},{13,1},{9,5},{5,9},{1,13},{14,2},{10,6},... | collective-permute-start | bytes 393224 | tf_op jit(solution)/shard_map/late_over_tm/ppermute | solution.py:661
  32.4 0.6 copy-done.8
  33.1 3.4 %shard_map.124 = (f32[384,128]{1,0:T(8,128)S(1)}, bf16[384,128]{1,0:T(8,128)(2,1)S(1)}, f32[512,128]{1,0:T(8,128)S(1)}, f32[512,128]{1,0:T(8,128)S(1)}) custom-call(s32[4,4]{1,0:T(4,128)S(1)} %copy-done.8, bf16[128,128]{1,0:T(8,128)(2,1)S(1)} %get-tuple-element.32.refs_1_, bf16[128,1664]{1,0:T(8,128)(2,1)S(1)} %collective-permute-done.refs_0_.refs_2_, ...), custom_call_target="tpu_custom_call" | custom-call | tf_op jit(solution)/shard_map/pallas_call | solution.py:521
  36.5 0.1 collective-permute-start.9
  36.6 4.4 %collective-permute-done.4.refs_1_.refs_8_ = bf16[128,512]{1,0:T(8,128)(2,1)S(1)} collective-permute-done((bf16[128,512]{1,0:T(8,128)(2,1)S(1)}, bf16[128,512]{1,0:T(8,128)(2,1)S(1)}, u32[]{:S(2)}, u32[]{:S(2)}) %collective-permute-start.4) | collective-permute-done | bytes 131104 | tf_op jit(solution)/shard_map/late_over_tm/ppermute | solution.py:661
  41.0 0.1 collective-permute-start.10
  41.2 1.4 %collective-permute-start.13 = (bf16[384,128]{1,0:T(8,128)(2,1)S(1)}, bf16[384,128]{1,0:T(8,128)(2,1)S(1)}, u32[]{:S(2)}, u32[]{:S(2)}) collective-permute-start(bf16[384,128]{1,0:T(8,128)(2,1)S(1)} %add_convert_fusion.refs_17_.refs_2_.piece), channel_id=1, source_target_pairs={{12,0},{8,4},{4,8},{0,12},{13,1},{9,5},{5,9},{1,13},{14,2},{10,6},... | collective-permute-start | bytes 294920 | tf_op jit(solution)/shard_map/early_gradients_over_tm/ppermute | solution.py:661
  42.6 0.3 collective-permute-done.10.refs_11_
  42.8 3.4 %shard_map.126 = (f32[704,128]{1,0:T(8,128)S(1)}, bf16[352,128]{1,0:T(8,128)(2,1)S(1)}, bf16[352,128]{1,0:T(8,128)(2,1)S(1)}) custom-call(s32[4,4]{1,0:T(4,128)S(1)} %copy-done.8, bf16[128,128]{1,0:T(8,128)(2,1)S(1)} %get-tuple-element.32.refs_1_, bf16[128,1664]{1,0:T(8,128)(2,1)S(1)} %collective-permute-done.refs_0_.refs_2_, ...), custom_call_target="tpu_custom_call" | custom-call | tf_op jit(solution)/shard_map/pallas_call | solution.py:521
  46.3 0.2 collective-permute-start.11
  46.5 0.4 collective-permute-start.12
  46.8 1.5 %collective-permute-done.13.refs_3_.facing = bf16[384,128]{1,0:T(8,128)(2,1)S(1)} collective-permute-done((bf16[384,128]{1,0:T(8,128)(2,1)S(1)}, bf16[384,128]{1,0:T(8,128)(2,1)S(1)}, u32[]{:S(2)}, u32[]{:S(2)}) %collective-permute-start.13) | collective-permute-done | bytes 98336 | tf_op jit(solution)/shard_map/early_gradients_over_tm/ppermute | solution.py:661
  48.3 0.1 shard_map.127
  48.4 2.6 %collective-permute-start.14 = (bf16[896,128]{1,0:T(8,128)(2,1)S(1)}, bf16[896,128]{1,0:T(8,128)(2,1)S(1)}, u32[]{:S(2)}, u32[]{:S(2)}) collective-permute-start(bf16[896,128]{1,0:T(8,128)(2,1)S(1)} %get-tuple-element.56), channel_id=1, source_target_pairs={{4,0},{0,4},{12,8},{8,12},{5,1},{1,5},{13,9},{9,13},{6,2},{2,6},{1... | collective-permute-start | bytes 688136 | tf_op jit(solution)/shard_map/late_sums_over_tm/ppermute | solution.py:661
  51.1 2.4 %collective-permute-start.16 = (bf16[320,128]{1,0:T(8,128)(2,1)S(1)}, bf16[320,128]{1,0:T(8,128)(2,1)S(1)}, u32[]{:S(2)}, u32[]{:S(2)}) collective-permute-start(bf16[320,128]{1,0:T(8,128)(2,1)S(1)} %get-tuple-element.55.own), channel_id=1, source_target_pairs={{12,0},{8,4},{4,8},{0,12},{13,1},{9,5},{5,9},{1,13},{14,2},{10,6},... | collective-permute-start | bytes 245768 | tf_op jit(solution)/shard_map/late_sums_over_tm/ppermute | solution.py:661
  53.5 9.4 %collective-permute-done.16.last = bf16[320,128]{1,0:T(8,128)(2,1)S(1)} collective-permute-done((bf16[320,128]{1,0:T(8,128)(2,1)S(1)}, bf16[320,128]{1,0:T(8,128)(2,1)S(1)}, u32[]{:S(2)}, u32[]{:S(2)}) %collective-permute-start.16) | collective-permute-done | bytes 81952 | tf_op jit(solution)/shard_map/late_sums_over_tm/ppermute | solution.py:661
  63.1 1.6 %collective-permute-start.19 = (bf16[128,128]{1,0:T(8,128)(2,1)S(1)}, bf16[128,128]{1,0:T(8,128)(2,1)S(1)}, u32[]{:S(2)}, u32[]{:S(2)}) collective-permute-start(bf16[128,128]{1,0:T(8,128)(2,1)S(1)} %get-tuple-element.59), channel_id=1, source_target_pairs={{0,3},{1,2},{2,1},{3,0},{4,7},{5,6},{6,5},{7,4},{8,11},{9,10},{10,... | collective-permute-start | bytes 98312 | tf_op jit(solution)/shard_map/low_over_head/ppermute | solution.py:720
  64.7 0.5 collective-permute-start.18
  65.2 1.3 %collective-permute-done.19.low_diag = bf16[128,128]{1,0:T(8,128)(2,1)S(1)} collective-permute-done((bf16[128,128]{1,0:T(8,128)(2,1)S(1)}, bf16[128,128]{1,0:T(8,128)(2,1)S(1)}, u32[]{:S(2)}, u32[]{:S(2)}) %collective-permute-start.19) | collective-permute-done | bytes 32800 | tf_op jit(solution)/shard_map/low_over_head/ppermute | solution.py:720
  66.5 2.1 %collective-permute-done.18.low_head = bf16[128,128]{1,0:T(8,128)(2,1)S(1)} collective-permute-done((bf16[128,128]{1,0:T(8,128)(2,1)S(1)}, bf16[128,128]{1,0:T(8,128)(2,1)S(1)}, u32[]{:S(2)}, u32[]{:S(2)}) %collective-permute-start.18) | collective-permute-done | bytes 32800 | tf_op jit(solution)/shard_map/low_over_head/ppermute | solution.py:48
  68.6 1.5 %shard_map.129 = (f32[128,1280]{1,0:T(8,128)}, f32[128,1280]{1,0:T(8,128)}, f32[128,1280]{1,0:T(8,128)}, f32[256,128]{1,0:T(8,128)}) custom-call(bf16[2048,128]{1,0:T(8,128)(2,1)S(1)} %get-tuple-element.58.tail, bf16[2048,128]{1,0:T(8,128)(2,1)S(1)} %collective-permute-done.17.tail2, bf16[128,128]{1,0:T(8,128)(2,1)S(1)} %collective-permute-done.18.low_head, ...), custom_call_target="tpu_custom_call" | custom-call | tf_op jit(solution)/shard_map/pallas_call | solution.py:624
  (37 shorter events, 0.3 us)
Async XLA Ops:
  0.6 12.8 %copy-start.3 = (bf16[128,1280]{1,0:T(8,128)(2,1)S(1)}, bf16[128,1280]{1,0:T(8,128)(2,1)}, u32[]{:S(2)}) copy-start(bf16[128,1280]{1,0:T(8,128)(2,1)} %do_ref.3) | copy-start | bytes 983044
  0.6 12.8 %copy-start.7 = (bf16[256,128]{1,0:T(8,128)(2,1)S(1)}, bf16[256,128]{1,0:T(8,128)(2,1)}, u32[]{:S(2)}) copy-start(bf16[256,128]{1,0:T(8,128)(2,1)} %t_ref.3) | copy-start | bytes 196612
  0.7 12.8 %copy-start.1 = (bf16[256,1280]{1,0:T(8,128)(2,1)S(1)}, bf16[256,1280]{1,0:T(8,128)(2,1)}, u32[]{:S(2)}) copy-start(bf16[256,1280]{1,0:T(8,128)(2,1)} %fv_ref.3) | copy-start | bytes 1966084
  0.7 12.8 %copy-start = (bf16[256,1280]{1,0:T(8,128)(2,1)S(1)}, bf16[256,1280]{1,0:T(8,128)(2,1)}, u32[]{:S(2)}) copy-start(bf16[256,1280]{1,0:T(8,128)(2,1)} %fk_ref.3) | copy-start | bytes 1966084
  0.7 12.8 %copy-start.2 = (bf16[128,1280]{1,0:T(8,128)(2,1)S(1)}, bf16[128,1280]{1,0:T(8,128)(2,1)}, u32[]{:S(2)}) copy-start(bf16[128,1280]{1,0:T(8,128)(2,1)} %fq_ref.3) | copy-start | bytes 983044
  3.3 23.6 %collective-permute-start = (bf16[128,1664]{1,0:T(8,128)(2,1)}, bf16[128,1664]{1,0:T(8,128)(2,1)S(1)}, u32[]{:S(2)}, u32[]{:S(2)}) collective-permute-start(bf16[128,1664]{1,0:T(8,128)(2,1)} %get-tuple-element.33), channel_id=1, source_target_pairs={{4,0},{0,4},{12,8},{8,12},{5,1},{1,5},{13,9},{9,13},{6,2},{2,6},{1... | collective-permute-start | bytes 1277960 | tf_op jit(solution)/shard_map/nearest_over_tm/ppermute | solution.py:661
  6.3 14.1 %collective-permute-start.1 = (bf16[128,640]{1,0:T(8,128)(2,1)}, bf16[128,640]{1,0:T(8,128)(2,1)S(1)}, u32[]{:S(2)}, u32[]{:S(2)}) collective-permute-start(bf16[128,640]{1,0:T(8,128)(2,1)} %get-tuple-element.34), channel_id=1, source_target_pairs={{8,0},{12,4},{0,8},{4,12},{9,1},{13,5},{1,9},{5,13},{10,2},{14,6},... | collective-permute-start | bytes 491528 | tf_op jit(solution)/shard_map/lead_over_tm/ppermute | solution.py:661
  8.9 17.9 %collective-permute-start.2 = (bf16[128,640]{1,0:T(8,128)(2,1)}, bf16[128,640]{1,0:T(8,128)(2,1)S(1)}, u32[]{:S(2)}, u32[]{:S(2)}) collective-permute-start(bf16[128,640]{1,0:T(8,128)(2,1)} %get-tuple-element.35), channel_id=1, source_target_pairs={{12,0},{8,4},{4,8},{0,12},{13,1},{9,5},{5,9},{1,13},{14,2},{10,6},... | collective-permute-start | bytes 491528 | tf_op jit(solution)/shard_map/lead_over_tm/ppermute | solution.py:661
  8.9 18.0 %collective-permute-start.6 = (bf16[128,512]{1,0:T(8,128)(2,1)}, bf16[128,512]{1,0:T(8,128)(2,1)S(1)}, u32[]{:S(2)}, u32[]{:S(2)}) collective-permute-start(bf16[128,512]{1,0:T(8,128)(2,1)} %get-tuple-element.44), channel_id=1, source_target_pairs={{12,4},{0,8},{13,5},{1,9},{14,6},{2,10},{15,7},{3,11},{28,20},{16,... | collective-permute-start | bytes 393224 | tf_op jit(solution)/shard_map/rest_over_tm/ppermute | solution.py:661
  12.8 14.2 %collective-permute-start.7 = (bf16[128,512]{1,0:T(8,128)(2,1)}, bf16[128,512]{1,0:T(8,128)(2,1)S(1)}, u32[]{:S(2)}, u32[]{:S(2)}) collective-permute-start(bf16[128,512]{1,0:T(8,128)(2,1)} %get-tuple-element.45), channel_id=1, source_target_pairs={{8,4},{4,8},{9,5},{5,9},{10,6},{6,10},{11,7},{7,11},{24,20},{20,24... | collective-permute-start | bytes 393224 | tf_op jit(solution)/shard_map/rest_over_tm/ppermute | solution.py:661
  26.8 5.6 %copy-start.6 = (bf16[128,1280]{1,0:T(8,128)(2,1)S(1)}, bf16[128,1280]{1,0:T(8,128)(2,1)}, u32[]{:S(2)}) copy-start(bf16[128,1280]{1,0:T(8,128)(2,1)} %refs_14_.3) | copy-start | bytes 983044
  26.9 5.6 %copy-start.4 = (bf16[128,1280]{1,0:T(8,128)(2,1)S(1)}, bf16[128,1280]{1,0:T(8,128)(2,1)}, u32[]{:S(2)}) copy-start(bf16[128,1280]{1,0:T(8,128)(2,1)} %refs_12_.1) | copy-start | bytes 983044
  26.9 5.6 %copy-start.5 = (bf16[128,1280]{1,0:T(8,128)(2,1)S(1)}, bf16[128,1280]{1,0:T(8,128)(2,1)}, u32[]{:S(2)}) copy-start(bf16[128,1280]{1,0:T(8,128)(2,1)} %refs_13_.1) | copy-start | bytes 983044
  26.9 5.5 %collective-permute-start.3 = (bf16[128,1152]{1,0:T(8,128)(2,1)S(1)}, bf16[128,1152]{1,0:T(8,128)(2,1)S(1)}, u32[]{:S(2)}, u32[]{:S(2)}) collective-permute-start(bf16[128,1152]{1,0:T(8,128)(2,1)S(1)} %shard_map.122), channel_id=1, source_target_pairs={{0,1},{1,0},{2,3},{3,2},{4,5},{5,4},{6,7},{7,6},{8,9},{9,8},{10,11... | collective-permute-start | bytes 884744 | tf_op jit(solution)/shard_map/lead_in_chip/ppermute | solution.py:48
  27.0 5.4 %collective-permute-start.8 = (bf16[128,768]{1,0:T(8,128)(2,1)S(1)}, bf16[128,768]{1,0:T(8,128)(2,1)S(1)}, u32[]{:S(2)}, u32[]{:S(2)}) collective-permute-start(bf16[128,768]{1,0:T(8,128)(2,1)S(1)} %shard_map.123), channel_id=1, source_target_pairs={{0,1},{1,0},{2,3},{3,2},{4,5},{5,4},{6,7},{7,6},{8,9},{9,8},{10,11... | collective-permute-start | bytes 589832 | tf_op jit(solution)/shard_map/rest_in_chip/ppermute | solution.py:48
  27.6 13.5 %collective-permute-start.4 = (bf16[128,512]{1,0:T(8,128)(2,1)S(1)}, bf16[128,512]{1,0:T(8,128)(2,1)S(1)}, u32[]{:S(2)}, u32[]{:S(2)}) collective-permute-start(bf16[128,512]{1,0:T(8,128)(2,1)S(1)} %get-tuple-element.39), channel_id=1, source_target_pairs={{8,0},{12,4},{0,8},{4,12},{9,1},{13,5},{1,9},{5,13},{10,2},{14,6},... | collective-permute-start | bytes 393224 | tf_op jit(solution)/shard_map/late_over_tm/ppermute | solution.py:661
  31.0 10.0 %collective-permute-start.5 = (bf16[128,512]{1,0:T(8,128)(2,1)S(1)}, bf16[128,512]{1,0:T(8,128)(2,1)S(1)}, u32[]{:S(2)}, u32[]{:S(2)}) collective-permute-start(bf16[128,512]{1,0:T(8,128)(2,1)S(1)} %get-tuple-element.40), channel_id=1, source_target_pairs={{12,0},{8,4},{4,8},{0,12},{13,1},{9,5},{5,9},{1,13},{14,2},{10,6},... | collective-permute-start | bytes 393224 | tf_op jit(solution)/shard_map/late_over_tm/ppermute | solution.py:661
  32.4 0.7 copy-start.8
  36.5 4.5 %collective-permute-start.9 = (bf16[384,128]{1,0:T(8,128)(2,1)S(1)}, bf16[384,128]{1,0:T(8,128)(2,1)S(1)}, u32[]{:S(2)}, u32[]{:S(2)}) collective-permute-start(bf16[384,128]{1,0:T(8,128)(2,1)S(1)} %get-tuple-element.47), channel_id=1, source_target_pairs={{0,1},{1,0},{2,3},{3,2},{4,5},{5,4},{6,7},{7,6},{8,9},{9,8},{10,11... | collective-permute-start | bytes 294920 | tf_op jit(solution)/shard_map/early_gradients_in_chip/ppermute | solution.py:48
  41.0 1.8 %collective-permute-start.10 = (bf16[128,1536]{1,0:T(8,128)(2,1)S(1)}, bf16[128,1536]{1,0:T(8,128)(2,1)S(1)}, u32[]{:S(2)}, u32[]{:S(2)}) collective-permute-start(bf16[128,1536]{1,0:T(8,128)(2,1)S(1)} %shard_map.125), channel_id=1, source_target_pairs={{0,1},{1,0},{2,3},{3,2},{4,5},{5,4},{6,7},{7,6},{8,9},{9,8},{10,11... | collective-permute-start | bytes 1179656 | tf_op jit(solution)/shard_map/late_in_chip/ppermute | solution.py:48
  41.2 7.2 %collective-permute-start.13 = (bf16[384,128]{1,0:T(8,128)(2,1)S(1)}, bf16[384,128]{1,0:T(8,128)(2,1)S(1)}, u32[]{:S(2)}, u32[]{:S(2)}) collective-permute-start(bf16[384,128]{1,0:T(8,128)(2,1)S(1)} %add_convert_fusion.refs_17_.refs_2_.piece), channel_id=1, source_target_pairs={{12,0},{8,4},{4,8},{0,12},{13,1},{9,5},{5,9},{1,13},{14,2},{10,6},... | collective-permute-start | bytes 294920 | tf_op jit(solution)/shard_map/early_gradients_over_tm/ppermute | solution.py:661
  46.3 2.1 %collective-permute-start.11 = (bf16[352,128]{1,0:T(8,128)(2,1)S(1)}, bf16[352,128]{1,0:T(8,128)(2,1)S(1)}, u32[]{:S(2)}, u32[]{:S(2)}) collective-permute-start(bf16[352,128]{1,0:T(8,128)(2,1)S(1)} %get-tuple-element.52), channel_id=1, source_target_pairs={{0,1},{1,0},{2,3},{3,2},{4,5},{5,4},{6,7},{7,6},{8,9},{9,8},{10,11... | collective-permute-start | bytes 270344 | tf_op jit(solution)/shard_map/late_sums_in_chip/ppermute | solution.py:48
  46.5 1.9 %collective-permute-start.12 = (bf16[352,128]{1,0:T(8,128)(2,1)S(1)}, bf16[352,128]{1,0:T(8,128)(2,1)S(1)}, u32[]{:S(2)}, u32[]{:S(2)}) collective-permute-start(bf16[352,128]{1,0:T(8,128)(2,1)S(1)} %get-tuple-element.53), channel_id=1, source_target_pairs={{0,1},{1,0},{2,3},{3,2},{4,5},{5,4},{6,7},{7,6},{8,9},{9,8},{10,11... | collective-permute-start | bytes 270344 | tf_op jit(solution)/shard_map/late_sums_in_chip/ppermute | solution.py:48
  48.4 14.5 %collective-permute-start.14 = (bf16[896,128]{1,0:T(8,128)(2,1)S(1)}, bf16[896,128]{1,0:T(8,128)(2,1)S(1)}, u32[]{:S(2)}, u32[]{:S(2)}) collective-permute-start(bf16[896,128]{1,0:T(8,128)(2,1)S(1)} %get-tuple-element.56), channel_id=1, source_target_pairs={{4,0},{0,4},{12,8},{8,12},{5,1},{1,5},{13,9},{9,13},{6,2},{2,6},{1... | collective-permute-start | bytes 688136 | tf_op jit(solution)/shard_map/late_sums_over_tm/ppermute | solution.py:661
  51.1 11.9 %collective-permute-start.15 = (bf16[512,128]{1,0:T(8,128)(2,1)S(1)}, bf16[512,128]{1,0:T(8,128)(2,1)S(1)}, u32[]{:S(2)}, u32[]{:S(2)}) collective-permute-start(bf16[512,128]{1,0:T(8,128)(2,1)S(1)} %get-tuple-element.57), channel_id=1, source_target_pairs={{8,0},{12,4},{0,8},{4,12},{9,1},{13,5},{1,9},{5,13},{10,2},{14,6},... | collective-permute-start | bytes 393224 | tf_op jit(solution)/shard_map/late_sums_over_tm/ppermute | solution.py:661
  51.1 11.8 %collective-permute-start.16 = (bf16[320,128]{1,0:T(8,128)(2,1)S(1)}, bf16[320,128]{1,0:T(8,128)(2,1)S(1)}, u32[]{:S(2)}, u32[]{:S(2)}) collective-permute-start(bf16[320,128]{1,0:T(8,128)(2,1)S(1)} %get-tuple-element.55.own), channel_id=1, source_target_pairs={{12,0},{8,4},{4,8},{0,12},{13,1},{9,5},{5,9},{1,13},{14,2},{10,6},... | collective-permute-start | bytes 245768 | tf_op jit(solution)/shard_map/late_sums_over_tm/ppermute | solution.py:661
  63.0 5.6 %collective-permute-start.17 = (bf16[2048,128]{1,0:T(8,128)(2,1)S(1)}, bf16[2048,128]{1,0:T(8,128)(2,1)S(1)}, u32[]{:S(2)}, u32[]{:S(2)}) collective-permute-start(bf16[2048,128]{1,0:T(8,128)(2,1)S(1)} %get-tuple-element.58.tail), channel_id=1, source_target_pairs={{0,1},{1,0},{2,3},{3,2},{4,5},{5,4},{6,7},{7,6},{8,9},{9,8},{10,11... | collective-permute-start | bytes 1572872 | tf_op jit(solution)/shard_map/tail_in_chip/ppermute | solution.py:48
  63.1 3.4 %collective-permute-start.19 = (bf16[128,128]{1,0:T(8,128)(2,1)S(1)}, bf16[128,128]{1,0:T(8,128)(2,1)S(1)}, u32[]{:S(2)}, u32[]{:S(2)}) collective-permute-start(bf16[128,128]{1,0:T(8,128)(2,1)S(1)} %get-tuple-element.59), channel_id=1, source_target_pairs={{0,3},{1,2},{2,1},{3,0},{4,7},{5,6},{6,5},{7,4},{8,11},{9,10},{10,... | collective-permute-start | bytes 98312 | tf_op jit(solution)/shard_map/low_over_head/ppermute | solution.py:720
  64.7 3.9 %collective-permute-start.18 = (bf16[128,128]{1,0:T(8,128)(2,1)S(1)}, bf16[128,128]{1,0:T(8,128)(2,1)S(1)}, u32[]{:S(2)}, u32[]{:S(2)}) collective-permute-start(bf16[128,128]{1,0:T(8,128)(2,1)S(1)} %get-tuple-element.59), channel_id=1, source_target_pairs={{0,2},{2,0},{1,3},{3,1},{4,6},{6,4},{5,7},{7,5},{8,10},{10,8},{9,1... | collective-permute-start | bytes 98312 | tf_op jit(solution)/shard_map/low_over_head/ppermute | solution.py:48

commit v11 on v10

--- a/solution.py
+++ b/solution.py
@@ -532,8 +532,24 @@
     )(*args)
 
 
+def stack_kernel(first, second, out):
+    at = first.shape[0]
+    out[:at, :] = first[...]
+    out[at:, :] = second[: out.shape[0] - at, :]
+
+
+def stack(first, second, rows):
+    return pl.pallas_call(
+        stack_kernel,
+        in_specs=vmem(2),
+        out_specs=pl.BlockSpec(memory_space=pltpu.VMEM),
+        out_shape=jax.ShapeDtypeStruct((rows, first.shape[1]), first.dtype),
+        compiler_params=SMALL,
+    )(first, second)
+
+
 def hand_out_kernel(frames, size, parts, keep_ref, *refs):
-    gots, (piece, facing), (own_ref, *sends, total) = refs[:parts], refs[parts : parts + 2], refs[parts + 2 :]
+    gots, (own_ref, *sends, total) = refs[:parts], refs[-frames - 1 :]
     me = lax.axis_index("tm")
     rows = own_ref.shape[0]
     total[...] = keep_ref[...] + jnp.concatenate([got[...].astype(F32) for got in gots], axis=0)
@@ -543,59 +559,52 @@
             own_ref[...] = low
         else:
             sends[m - 1][:rows, :] = low.astype(BF16)
-            sends[m - 1][rows : rows + size, :] = total[:size, :].astype(BF16)
-    sends[0][rows + size : rows + 3 * size, :] = piece[...]
-    sends[0][rows + 3 * size :, :] = facing[size:, :]
-    sends[1][rows + size :, :] = piece[:size, :]
-
-
-def hand_out(frames, rows, keep, gots, piece, facing):
+            sends[m - 1][rows:, :] = total[:size, :].astype(BF16)
+
+
+def hand_out(frames, rows, keep, gots, after):
     size, rank = keep.shape[0] - frames * rows, keep.shape[1]
     own, *sends = pl.pallas_call(
         functools.partial(hand_out_kernel, frames, size, len(gots)),
-        in_specs=vmem(3 + len(gots)),
+        in_specs=vmem(1 + len(gots)) + [pl.BlockSpec(memory_space=pl.ANY)] * len(after),
         out_specs=vmem(frames),
         out_shape=[jax.ShapeDtypeStruct((rows, rank), F32)]
-        + [jax.ShapeDtypeStruct((rows + size * n, rank), BF16) for n in (4, 2, 1)],
+        + [jax.ShapeDtypeStruct((rows + size, rank), BF16)] * (frames - 1),
         scratch_shapes=[pltpu.VMEM(keep.shape, F32)],
         compiler_params=SMALL,
-    )(keep, *gots, piece, facing)
+    )(keep, *gots, *after)
     return own, sends
 
 
-def collect_kernel(wide, own_low, own, near, third, last, piece, facing, out_ref, low_ref):
-    rows = own_low.shape[0]
-    size = own.shape[0] - rows
+def collect_kernel(wide, own_low, own, near, third, last, piece, pair, facing, passed, *outs):
+    out_ref, low_ref = outs
+    rows, size = own_low.shape[0], piece.shape[0] // 2
     low = own_low[...]
     for got in (near, third, last):
         low = low + got[:rows, :].astype(F32)
     out_ref[:rows, :] = low.astype(BF16)
     low_ref[...] = low.astype(BF16)
     middle = lookup(wide, lax.axis_index("tm")) > 0
-
-    def part(ref, n):
-        return ref[rows + n * size : rows + (n + 1) * size, :]
-
-    blocks = [part(ref, 0) for ref in (own, near, third, last)]
-    blocks += [piece[:size, :], part(near, 1), part(third, 1), facing[:size, :]]
-    blocks.append(jnp.where(middle, piece[size:, :], part(near, 2)))
-    blocks.append(jnp.where(middle, facing[size:, :], part(near, 3)))
+    far = [jnp.where(middle, facing[part, :], passed[part, :]) for part in (slice(n * size, (n + 1) * size) for n in range(3))]
+    blocks = [ref[rows:, :] for ref in (own, near, third, last)]
+    blocks += [piece[:size, :], pair[:size, :], far[0], far[2]]
+    blocks += [jnp.where(middle, piece[size:, :], pair[size:, :]), far[1]]
     for n, block in enumerate(blocks):
         out_ref[rows + n * size : rows + (n + 1) * size, :] = block
 
 
-def collect(wide, own_low, own, gots, piece, facing):
-    (rows, rank), size = own_low.shape, piece.shape[0] // 2
+def collect(wide, own_low, own, gots, *pieces):
+    (rows, rank), size = own_low.shape, pieces[0].shape[0] // 2
     return pl.pallas_call(
         functools.partial(collect_kernel, wide),
-        in_specs=vmem(4 + len(gots)),
+        in_specs=vmem(2 + len(gots) + len(pieces)),
         out_specs=vmem(2),
         out_shape=[
             jax.ShapeDtypeStruct((rows + 10 * size, rank), BF16),
             jax.ShapeDtypeStruct((rows, rank), BF16),
         ],
         compiler_params=SMALL,
-    )(own_low, own, *gots, piece, facing)
+    )(own_low, own, *gots, *pieces)
 
 
 def place_kernel(frames, lead, late, rest, tail, tail2, low_head, low_diag, *outs):
@@ -609,8 +618,10 @@
     outs[3][:rows, :] = jnp.where(first, same, other)
     outs[3][rows:, :] = jnp.where(first, other, same)
     side = me // 2
-    places = [lookup(late, me ^ m) for m in range(frames)] + [lookup(lead, me ^ m) for m in range(frames)]
-    places += [lookup(rest, 1 + side), lookup(rest, 2 - side)]
+    facing = 2 - side
+    places = [lookup(late, me ^ m) for m in range(frames)]
+    places += [lookup(lead, chip) for chip in (me, me ^ 1, facing, facing ^ 1)]
+    places += [lookup(rest, 1 + side), lookup(rest, facing)]
     for n, head in enumerate(places):
         here = slice(rows + n * cut, rows + (n + 1) * cut)
         a, b = tail[here, :].astype(F32), tail2[here, :].astype(F32)
@@ -706,15 +717,26 @@
     *rest_side, _ = sides("rest", 1, rest_got, False, (3,), 2 * DH)
     early = [lead, rest]
     keep, give, *low = head_group(early, band_width, [t_side, lead_side, rest_side], adapters)
+    cut = 3 * rank // 2
+
+    def hand_on(name, block, targets):
+        with jax.named_scope(f"{name}_over_tm"):
+            return lax.ppermute(block, "tm", targets)
+
+    inner, outer = [(1, 2), (2, 1)], [(1, 0), (2, 3)]
     got = swap_in_chip("early_gradients", give)
     piece = (keep + got.astype(F32)).astype(BF16)
+    pair = meet("early_gradients", piece, 1)
     *late_side, _ = sides("late", 2, late_got, False, (3,), 0, [got])
-    facing = meet("early_gradients", piece, 3)
-    keep, *gives = head_group([late], band_width, [t_side, late_side], adapters, low, [piece])
+    facing = hand_on("early_pairs", stack(piece, pair, 3 * cut), inner)
+    passed = hand_on("early_passed", facing, outer)
+    keep, *gives = head_group([late], band_width, [t_side, late_side], adapters, low, [])
     gives = [swap_in_chip("late_sums", g) for g in gives]
-    own_low, sends = hand_out(frames, rows, keep, gives, piece, facing)
+    own_low, sends = hand_out(frames, rows, keep, gives, [])
     gots = [meet("late_sums", block, m) for m, block in enumerate(sends, 1)]
-    tail, low = collect(rest[1], own_low, sends[2], gots, piece, facing)
+    tail, low = collect(
+        rest[1], own_low, sends[0], gots, piece, pair, facing, passed
+    )
     diag = [(0, 3), (1, 2), (2, 1), (3, 0)]
     with jax.named_scope("low_over_head"):
         low_head, low_diag = swap(low, "head"), lax.ppermute(low, ("head", "rep"), diag)

time: 70.2 us -> 73.7 us (1.050)
  starting transfers between devices: 25 us -> 30.3 us
  waiting for transfers between devices: 31.3 us -> 29.5 us
    ppermute x11, waiting for transfers between devices: 27.7 us -> 24.1 us  [meet(): return lax.ppermute(block, 'tm', [(j ^ m, j) for j in targets])]
    ppermute x11, starting transfers between devices: 21.5 us -> 25.1 us  [meet(): return lax.ppermute(block, 'tm', [(j ^ m, j) for j in targets])]
    ppermute x0 -> x2, waiting for transfers between devices: none -> 2.35 us  [hand_on(): return lax.ppermute(block, 'tm', targets)]
    ppermute x0 -> x2, starting transfers between devices: none -> 1.95 us  [hand_on(): return lax.ppermute(block, 'tm', targets)]
    ppermute x1, starting transfers between devices: 1.61 us -> 0.31 us  [exchange_plan(): lax.ppermute(low, ('head', 'rep'), diag)]
    ppermute x8, starting transfers between devices: 1.94 us -> 2.95 us  [swap(): return lax.ppermute(block, axis, [(0, 1), (1, 0)])]
  transfers between devices with their start and end apart: 20 -> 22, of which waited for: 8 -> 9; matrix products, arithmetic and copies ran while one was open for 0% -> 0% of each run, Pallas kernels for 11% -> 11%
where the time goes in v11:
time: 73.7 us; the launch traced here: 73.5 us
  starting transfers between devices  30.3 us (41%)
  waiting for transfers between devices  29.5 us (40%)
  Pallas kernels  12.1 us (16%)
  between operations  0.95 us (1%)
    ppermute x11, starting transfers between devices, meet(): return lax.ppermute(block, 'tm', [(j ^ m, j) for j in targets])  25.1 us
    ppermute x11, waiting for transfers between devices, meet(): return lax.ppermute(block, 'tm', [(j ^ m, j) for j in targets])  24.1 us
    pallas_call x2, Pallas kernels, head_group(): pl.pallas_call(functools.partial(group_kernel, heads, frames, chained, le...  6.89 us
    pallas_call x2, Pallas kernels, pack(): pl.pallas_call(functools.partial(pack_kernel, frames, outputs), in_specs=...  3.51 us
    ppermute x8, starting transfers between devices, swap(): return lax.ppermute(block, axis, [(0, 1), (1, 0)])  2.95 us
    ppermute x2, waiting for transfers between devices, hand_on(): return lax.ppermute(block, 'tm', targets)  2.35 us
    ppermute x8, waiting for transfers between devices, swap(): return lax.ppermute(block, axis, [(0, 1), (1, 0)])  2.14 us
    ppermute x2, starting transfers between devices, hand_on(): return lax.ppermute(block, 'tm', targets)  1.95 us
  transfers between devices with their start and end apart: 22, of which 9 were waited for; matrix products, arithmetic and copies ran while one was open for 0% of the time, Pallas kernels for 11%

profile of v11, /device:TPU:0, one launch (start us, length us, event | category | flops | bytes accessed | tf_op | source)
XLA Modules:
  0.0 73.5 jit_solution(12222031289388252435)
XLA Ops:
  0.7 2.6 %shard_map.121 = (bf16[128,1664]{1,0:T(8,128)(2,1)}, bf16[128,640]{1,0:T(8,128)(2,1)}, bf16[128,512]{1,0:T(8,128)(2,1)}, bf16[128,640]{1,0:T(8,128)(2,1)}, bf16[128,512]{1,0:T(8,128)(2,1)}) custom-call(bf16[128,1280]{1,0:T(8,128)(2,1)} %fq_ref.3, bf16[128,1280]{1,0:T(8,128)(2,1)} %do_ref.3, bf16[256,1280]{1,0:T(8,128)(2,1)} %fk_ref.3, ...), custom_call_target="tpu_custom_call" | custom-call | tf_op jit(solution)/shard_map/pallas_call | solution.py:301
  3.3 3.1 %collective-permute-start = (bf16[128,1664]{1,0:T(8,128)(2,1)}, bf16[128,1664]{1,0:T(8,128)(2,1)S(1)}, u32[]{:S(2)}, u32[]{:S(2)}) collective-permute-start(bf16[128,1664]{1,0:T(8,128)(2,1)} %get-tuple-element.33), channel_id=1, source_target_pairs={{4,0},{0,4},{12,8},{8,12},{5,1},{1,5},{13,9},{9,13},{6,2},{2,6},{1... | collective-permute-start | bytes 1277960 | tf_op jit(solution)/shard_map/nearest_over_tm/ppermute | solution.py:672
  6.3 2.6 %collective-permute-start.1 = (bf16[128,640]{1,0:T(8,128)(2,1)}, bf16[128,640]{1,0:T(8,128)(2,1)S(1)}, u32[]{:S(2)}, u32[]{:S(2)}) collective-permute-start(bf16[128,640]{1,0:T(8,128)(2,1)} %get-tuple-element.34), channel_id=1, source_target_pairs={{8,0},{12,4},{0,8},{4,12},{9,1},{13,5},{1,9},{5,13},{10,2},{14,6},... | collective-permute-start | bytes 491528 | tf_op jit(solution)/shard_map/lead_over_tm/ppermute | solution.py:672
  8.9 3.8 %collective-permute-start.6 = (bf16[128,512]{1,0:T(8,128)(2,1)}, bf16[128,512]{1,0:T(8,128)(2,1)S(1)}, u32[]{:S(2)}, u32[]{:S(2)}) collective-permute-start(bf16[128,512]{1,0:T(8,128)(2,1)} %get-tuple-element.44), channel_id=1, source_target_pairs={{12,4},{0,8},{13,5},{1,9},{14,6},{2,10},{15,7},{3,11},{28,20},{16,... | collective-permute-start | bytes 393224 | tf_op jit(solution)/shard_map/rest_over_tm/ppermute | solution.py:672
  12.8 0.7 collective-permute-start.7
  13.5 0.9 %shard_map.120 = (bf16[128,512]{1,0:T(8,128)(2,1)S(1)}, bf16[128,512]{1,0:T(8,128)(2,1)S(1)}, bf16[128,512]{1,0:T(8,128)(2,1)S(1)}, bf16[128,256]{1,0:T(8,128)(2...) custom-call(bf16[128,1280]{1,0:T(8,128)(2,1)S(1)} %copy-done.2, ...), custom_call_target="tpu_custom_call" | custom-call | tf_op jit(solution)/shard_map/pallas_call | solution.py:301
  14.4 6.0 %collective-permute-done.1.refs_1_.refs_3_ = bf16[128,640]{1,0:T(8,128)(2,1)S(1)} collective-permute-done((bf16[128,640]{1,0:T(8,128)(2,1)}, bf16[128,640]{1,0:T(8,128)(2,1)S(1)}, u32[]{:S(2)}, u32[]{:S(2)}) %collective-permute-start.1) | collective-permute-done | bytes 163872 | tf_op jit(solution)/shard_map/lead_over_tm/ppermute | solution.py:672
  20.4 6.4 %collective-permute-done.2.refs_2_.refs_4_ = bf16[128,640]{1,0:T(8,128)(2,1)S(1)} collective-permute-done((bf16[128,640]{1,0:T(8,128)(2,1)}, bf16[128,640]{1,0:T(8,128)(2,1)S(1)}, u32[]{:S(2)}, u32[]{:S(2)}) %collective-permute-start.2) | collective-permute-done | bytes 163872 | tf_op jit(solution)/shard_map/lead_over_tm/ppermute | solution.py:672
  27.0 0.5 collective-permute-start.8
  27.6 3.5 %collective-permute-start.4 = (bf16[128,512]{1,0:T(8,128)(2,1)S(1)}, bf16[128,512]{1,0:T(8,128)(2,1)S(1)}, u32[]{:S(2)}, u32[]{:S(2)}) collective-permute-start(bf16[128,512]{1,0:T(8,128)(2,1)S(1)} %get-tuple-element.39), channel_id=1, source_target_pairs={{8,0},{12,4},{0,8},{4,12},{9,1},{13,5},{1,9},{5,13},{10,2},{14,6},... | collective-permute-start | bytes 393224 | tf_op jit(solution)/shard_map/late_over_tm/ppermute | solution.py:672
  31.0 1.4 %collective-permute-start.5 = (bf16[128,512]{1,0:T(8,128)(2,1)S(1)}, bf16[128,512]{1,0:T(8,128)(2,1)S(1)}, u32[]{:S(2)}, u32[]{:S(2)}) collective-permute-start(bf16[128,512]{1,0:T(8,128)(2,1)S(1)} %get-tuple-element.40), channel_id=1, source_target_pairs={{12,0},{8,4},{4,8},{0,12},{13,1},{9,5},{5,9},{1,13},{14,2},{10,6},... | collective-permute-start | bytes 393224 | tf_op jit(solution)/shard_map/late_over_tm/ppermute | solution.py:672
  32.4 0.6 copy-done.8
  33.1 3.4 %shard_map.124 = (f32[384,128]{1,0:T(8,128)S(1)}, bf16[384,128]{1,0:T(8,128)(2,1)S(1)}, f32[512,128]{1,0:T(8,128)S(1)}, f32[512,128]{1,0:T(8,128)S(1)}) custom-call(s32[4,4]{1,0:T(4,128)S(1)} %copy-done.8, bf16[128,128]{1,0:T(8,128)(2,1)S(1)} %get-tuple-element.32.refs_1_, bf16[128,1664]{1,0:T(8,128)(2,1)S(1)} %collective-permute-done.refs_0_.refs_2_, ...), custom_call_target="tpu_custom_call" | custom-call | tf_op jit(solution)/shard_map/pallas_call | solution.py:521
  36.6 4.4 %collective-permute-done.4.refs_1_.refs_8_ = bf16[128,512]{1,0:T(8,128)(2,1)S(1)} collective-permute-done((bf16[128,512]{1,0:T(8,128)(2,1)S(1)}, bf16[128,512]{1,0:T(8,128)(2,1)S(1)}, u32[]{:S(2)}, u32[]{:S(2)}) %collective-permute-start.4) | collective-permute-done | bytes 131104 | tf_op jit(solution)/shard_map/late_over_tm/ppermute | solution.py:672
  41.2 3.2 %collective-permute-start.16 = (bf16[384,128]{1,0:T(8,128)(2,1)S(1)}, bf16[384,128]{1,0:T(8,128)(2,1)S(1)}, u32[]{:S(2)}, u32[]{:S(2)}) collective-permute-start(bf16[384,128]{1,0:T(8,128)(2,1)S(1)} %add_convert_fusion.first.piece), channel_id=1, source_target_pairs={{4,0},{0,4},{12,8},{8,12},{5,1},{1,5},{13,9},{9,13},{6,2},{2,6},{1... | collective-permute-start | bytes 294920 | tf_op jit(solution)/shard_map/early_gradients_over_tm/ppermute | solution.py:672
  44.3 3.5 %collective-permute-done.16.second.pair = bf16[384,128]{1,0:T(8,128)(2,1)S(1)} collective-permute-done((bf16[384,128]{1,0:T(8,128)(2,1)S(1)}, bf16[384,128]{1,0:T(8,128)(2,1)S(1)}, u32[]{:S(2)}, u32[]{:S(2)}) %collective-permute-start.16) | collective-permute-done | bytes 98336 | tf_op jit(solution)/shard_map/early_gradients_over_tm/ppermute | solution.py:672
  47.8 0.7 collective-permute-start.17
  48.5 3.4 %shard_map.126 = (f32[704,128]{1,0:T(8,128)S(1)}, bf16[352,128]{1,0:T(8,128)(2,1)S(1)}, bf16[352,128]{1,0:T(8,128)(2,1)S(1)}) custom-call(s32[4,4]{1,0:T(4,128)S(1)} %copy-done.8, bf16[128,128]{1,0:T(8,128)(2,1)S(1)} %get-tuple-element.32.refs_1_, bf16[128,1664]{1,0:T(8,128)(2,1)S(1)} %collective-permute-done.refs_0_.refs_2_, ...), custom_call_target="tpu_custom_call" | custom-call | tf_op jit(solution)/shard_map/pallas_call | solution.py:521
  52.0 0.5 collective-permute-start.12
  52.5 1.3 %collective-permute-start.18 = (bf16[576,128]{1,0:T(8,128)(2,1)S(1)}, bf16[576,128]{1,0:T(8,128)(2,1)S(1)}, u32[]{:S(2)}, u32[]{:S(2)}) collective-permute-start(bf16[576,128]{1,0:T(8,128)(2,1)S(1)} %collective-permute-done.17.facing), channel_id=1, source_target_pairs={{4,0},{8,12},{5,1},{9,13},{6,2},{10,14},{7,3},{11,15},{20,16},{24,... | collective-permute-start | bytes 442376 | tf_op jit(solution)/shard_map/early_passed_over_tm/ppermute | solution.py:724
  53.9 4.5 %collective-permute-start.13 = (bf16[320,128]{1,0:T(8,128)(2,1)S(1)}, bf16[320,128]{1,0:T(8,128)(2,1)S(1)}, u32[]{:S(2)}, u32[]{:S(2)}) collective-permute-start(bf16[320,128]{1,0:T(8,128)(2,1)S(1)} %get-tuple-element.54.own), channel_id=1, source_target_pairs={{4,0},{0,4},{12,8},{8,12},{5,1},{1,5},{13,9},{9,13},{6,2},{2,6},{1... | collective-permute-start | bytes 245768 | tf_op jit(solution)/shard_map/late_sums_over_tm/ppermute | solution.py:672
  58.4 0.1 collective-permute-start.14
  58.5 2.3 %collective-permute-start.15 = (bf16[320,128]{1,0:T(8,128)(2,1)S(1)}, bf16[320,128]{1,0:T(8,128)(2,1)S(1)}, u32[]{:S(2)}, u32[]{:S(2)}) collective-permute-start(bf16[320,128]{1,0:T(8,128)(2,1)S(1)} %get-tuple-element.56), channel_id=1, source_target_pairs={{12,0},{8,4},{4,8},{0,12},{13,1},{9,5},{5,9},{1,13},{14,2},{10,6},... | collective-permute-start | bytes 245768 | tf_op jit(solution)/shard_map/late_sums_over_tm/ppermute | solution.py:672
  60.8 2.4 %collective-permute-done.18.passed = bf16[576,128]{1,0:T(8,128)(2,1)S(1)} collective-permute-done((bf16[576,128]{1,0:T(8,128)(2,1)S(1)}, bf16[576,128]{1,0:T(8,128)(2,1)S(1)}, u32[]{:S(2)}, u32[]{:S(2)}) %collective-permute-start.18) | collective-permute-done | bytes 147488 | tf_op jit(solution)/shard_map/early_passed_over_tm/ppermute | solution.py:724
  63.2 1.7 %collective-permute-done.13.near = bf16[320,128]{1,0:T(8,128)(2,1)S(1)} collective-permute-done((bf16[320,128]{1,0:T(8,128)(2,1)S(1)}, bf16[320,128]{1,0:T(8,128)(2,1)S(1)}, u32[]{:S(2)}, u32[]{:S(2)}) %collective-permute-start.13) | collective-permute-done | bytes 81952 | tf_op jit(solution)/shard_map/late_sums_over_tm/ppermute | solution.py:672
  64.9 2.1 %collective-permute-done.14.third = bf16[320,128]{1,0:T(8,128)(2,1)S(1)} collective-permute-done((bf16[320,128]{1,0:T(8,128)(2,1)S(1)}, bf16[320,128]{1,0:T(8,128)(2,1)S(1)}, u32[]{:S(2)}, u32[]{:S(2)}) %collective-permute-start.14) | collective-permute-done | bytes 81952 | tf_op jit(solution)/shard_map/late_sums_over_tm/ppermute | solution.py:672
  67.0 0.1 shard_map.129
  67.1 1.6 %collective-permute-start.20 = (bf16[128,128]{1,0:T(8,128)(2,1)S(1)}, bf16[128,128]{1,0:T(8,128)(2,1)S(1)}, u32[]{:S(2)}, u32[]{:S(2)}) collective-permute-start(bf16[128,128]{1,0:T(8,128)(2,1)S(1)} %get-tuple-element.59), channel_id=1, source_target_pairs={{0,2},{2,0},{1,3},{3,1},{4,6},{6,4},{5,7},{7,5},{8,10},{10,8},{9,1... | collective-permute-start | bytes 98312 | tf_op jit(solution)/shard_map/low_over_head/ppermute | solution.py:48
  68.7 0.3 collective-permute-start.21
  69.0 2.1 %collective-permute-done.20.low_head = bf16[128,128]{1,0:T(8,128)(2,1)S(1)} collective-permute-done((bf16[128,128]{1,0:T(8,128)(2,1)S(1)}, bf16[128,128]{1,0:T(8,128)(2,1)S(1)}, u32[]{:S(2)}, u32[]{:S(2)}) %collective-permute-start.20) | collective-permute-done | bytes 32800 | tf_op jit(solution)/shard_map/low_over_head/ppermute | solution.py:48
  71.1 0.9 %collective-permute-done.21.low_diag = bf16[128,128]{1,0:T(8,128)(2,1)S(1)} collective-permute-done((bf16[128,128]{1,0:T(8,128)(2,1)S(1)}, bf16[128,128]{1,0:T(8,128)(2,1)S(1)}, u32[]{:S(2)}, u32[]{:S(2)}) %collective-permute-start.21) | collective-permute-done | bytes 32800 | tf_op jit(solution)/shard_map/low_over_head/ppermute | solution.py:742
  72.0 1.5 %shard_map.130 = (f32[128,1280]{1,0:T(8,128)}, f32[128,1280]{1,0:T(8,128)}, f32[128,1280]{1,0:T(8,128)}, f32[256,128]{1,0:T(8,128)}) custom-call(bf16[2048,128]{1,0:T(8,128)(2,1)S(1)} %get-tuple-element.58.tail, bf16[2048,128]{1,0:T(8,128)(2,1)S(1)} %collective-permute-done.19.tail2, bf16[128,128]{1,0:T(8,128)(2,1)S(1)} %collective-permute-done.20.low_head, ...), custom_call_target="tpu_custom_call" | custom-call | tf_op jit(solution)/shard_map/pallas_call | solution.py:635
  (42 shorter events, 0.6 us)
Async XLA Ops:
  0.6 12.8 %copy-start.2 = (bf16[128,1280]{1,0:T(8,128)(2,1)S(1)}, bf16[128,1280]{1,0:T(8,128)(2,1)}, u32[]{:S(2)}) copy-start(bf16[128,1280]{1,0:T(8,128)(2,1)} %fq_ref.3) | copy-start | bytes 983044
  0.6 12.8 %copy-start.3 = (bf16[128,1280]{1,0:T(8,128)(2,1)S(1)}, bf16[128,1280]{1,0:T(8,128)(2,1)}, u32[]{:S(2)}) copy-start(bf16[128,1280]{1,0:T(8,128)(2,1)} %do_ref.3) | copy-start | bytes 983044
  0.7 12.8 %copy-start = (bf16[256,1280]{1,0:T(8,128)(2,1)S(1)}, bf16[256,1280]{1,0:T(8,128)(2,1)}, u32[]{:S(2)}) copy-start(bf16[256,1280]{1,0:T(8,128)(2,1)} %fk_ref.3) | copy-start | bytes 1966084
  0.7 12.8 %copy-start.1 = (bf16[256,1280]{1,0:T(8,128)(2,1)S(1)}, bf16[256,1280]{1,0:T(8,128)(2,1)}, u32[]{:S(2)}) copy-start(bf16[256,1280]{1,0:T(8,128)(2,1)} %fv_ref.3) | copy-start | bytes 1966084
  0.7 12.8 %copy-start.7 = (bf16[256,128]{1,0:T(8,128)(2,1)S(1)}, bf16[256,128]{1,0:T(8,128)(2,1)}, u32[]{:S(2)}) copy-start(bf16[256,128]{1,0:T(8,128)(2,1)} %t_ref.3) | copy-start | bytes 196612
  3.3 23.6 %collective-permute-start = (bf16[128,1664]{1,0:T(8,128)(2,1)}, bf16[128,1664]{1,0:T(8,128)(2,1)S(1)}, u32[]{:S(2)}, u32[]{:S(2)}) collective-permute-start(bf16[128,1664]{1,0:T(8,128)(2,1)} %get-tuple-element.33), channel_id=1, source_target_pairs={{4,0},{0,4},{12,8},{8,12},{5,1},{1,5},{13,9},{9,13},{6,2},{2,6},{1... | collective-permute-start | bytes 1277960 | tf_op jit(solution)/shard_map/nearest_over_tm/ppermute | solution.py:672
  6.3 14.1 %collective-permute-start.1 = (bf16[128,640]{1,0:T(8,128)(2,1)}, bf16[128,640]{1,0:T(8,128)(2,1)S(1)}, u32[]{:S(2)}, u32[]{:S(2)}) collective-permute-start(bf16[128,640]{1,0:T(8,128)(2,1)} %get-tuple-element.34), channel_id=1, source_target_pairs={{8,0},{12,4},{0,8},{4,12},{9,1},{13,5},{1,9},{5,13},{10,2},{14,6},... | collective-permute-start | bytes 491528 | tf_op jit(solution)/shard_map/lead_over_tm/ppermute | solution.py:672
  8.9 17.9 %collective-permute-start.2 = (bf16[128,640]{1,0:T(8,128)(2,1)}, bf16[128,640]{1,0:T(8,128)(2,1)S(1)}, u32[]{:S(2)}, u32[]{:S(2)}) collective-permute-start(bf16[128,640]{1,0:T(8,128)(2,1)} %get-tuple-element.35), channel_id=1, source_target_pairs={{12,0},{8,4},{4,8},{0,12},{13,1},{9,5},{5,9},{1,13},{14,2},{10,6},... | collective-permute-start | bytes 491528 | tf_op jit(solution)/shard_map/lead_over_tm/ppermute | solution.py:672
  8.9 18.0 %collective-permute-start.6 = (bf16[128,512]{1,0:T(8,128)(2,1)}, bf16[128,512]{1,0:T(8,128)(2,1)S(1)}, u32[]{:S(2)}, u32[]{:S(2)}) collective-permute-start(bf16[128,512]{1,0:T(8,128)(2,1)} %get-tuple-element.44), channel_id=1, source_target_pairs={{12,4},{0,8},{13,5},{1,9},{14,6},{2,10},{15,7},{3,11},{28,20},{16,... | collective-permute-start | bytes 393224 | tf_op jit(solution)/shard_map/rest_over_tm/ppermute | solution.py:672
  12.8 14.2 %collective-permute-start.7 = (bf16[128,512]{1,0:T(8,128)(2,1)}, bf16[128,512]{1,0:T(8,128)(2,1)S(1)}, u32[]{:S(2)}, u32[]{:S(2)}) collective-permute-start(bf16[128,512]{1,0:T(8,128)(2,1)} %get-tuple-element.45), channel_id=1, source_target_pairs={{8,4},{4,8},{9,5},{5,9},{10,6},{6,10},{11,7},{7,11},{24,20},{20,24... | collective-permute-start | bytes 393224 | tf_op jit(solution)/shard_map/rest_over_tm/ppermute | solution.py:672
  26.8 5.6 %copy-start.6 = (bf16[128,1280]{1,0:T(8,128)(2,1)S(1)}, bf16[128,1280]{1,0:T(8,128)(2,1)}, u32[]{:S(2)}) copy-start(bf16[128,1280]{1,0:T(8,128)(2,1)} %refs_14_.3) | copy-start | bytes 983044
  26.9 5.6 %copy-start.4 = (bf16[128,1280]{1,0:T(8,128)(2,1)S(1)}, bf16[128,1280]{1,0:T(8,128)(2,1)}, u32[]{:S(2)}) copy-start(bf16[128,1280]{1,0:T(8,128)(2,1)} %refs_12_.1) | copy-start | bytes 983044
  26.9 5.6 %copy-start.5 = (bf16[128,1280]{1,0:T(8,128)(2,1)S(1)}, bf16[128,1280]{1,0:T(8,128)(2,1)}, u32[]{:S(2)}) copy-start(bf16[128,1280]{1,0:T(8,128)(2,1)} %refs_13_.1) | copy-start | bytes 983044
  26.9 5.5 %collective-permute-start.3 = (bf16[128,1152]{1,0:T(8,128)(2,1)S(1)}, bf16[128,1152]{1,0:T(8,128)(2,1)S(1)}, u32[]{:S(2)}, u32[]{:S(2)}) collective-permute-start(bf16[128,1152]{1,0:T(8,128)(2,1)S(1)} %shard_map.122), channel_id=1, source_target_pairs={{0,1},{1,0},{2,3},{3,2},{4,5},{5,4},{6,7},{7,6},{8,9},{9,8},{10,11... | collective-permute-start | bytes 884744 | tf_op jit(solution)/shard_map/lead_in_chip/ppermute | solution.py:48
  27.0 5.4 %collective-permute-start.8 = (bf16[128,768]{1,0:T(8,128)(2,1)S(1)}, bf16[128,768]{1,0:T(8,128)(2,1)S(1)}, u32[]{:S(2)}, u32[]{:S(2)}) collective-permute-start(bf16[128,768]{1,0:T(8,128)(2,1)S(1)} %shard_map.123), channel_id=1, source_target_pairs={{0,1},{1,0},{2,3},{3,2},{4,5},{5,4},{6,7},{7,6},{8,9},{9,8},{10,11... | collective-permute-start | bytes 589832 | tf_op jit(solution)/shard_map/rest_in_chip/ppermute | solution.py:48
  27.6 13.5 %collective-permute-start.4 = (bf16[128,512]{1,0:T(8,128)(2,1)S(1)}, bf16[128,512]{1,0:T(8,128)(2,1)S(1)}, u32[]{:S(2)}, u32[]{:S(2)}) collective-permute-start(bf16[128,512]{1,0:T(8,128)(2,1)S(1)} %get-tuple-element.39), channel_id=1, source_target_pairs={{8,0},{12,4},{0,8},{4,12},{9,1},{13,5},{1,9},{5,13},{10,2},{14,6},... | collective-permute-start | bytes 393224 | tf_op jit(solution)/shard_map/late_over_tm/ppermute | solution.py:672
  31.0 10.0 %collective-permute-start.5 = (bf16[128,512]{1,0:T(8,128)(2,1)S(1)}, bf16[128,512]{1,0:T(8,128)(2,1)S(1)}, u32[]{:S(2)}, u32[]{:S(2)}) collective-permute-start(bf16[128,512]{1,0:T(8,128)(2,1)S(1)} %get-tuple-element.40), channel_id=1, source_target_pairs={{12,0},{8,4},{4,8},{0,12},{13,1},{9,5},{5,9},{1,13},{14,2},{10,6},... | collective-permute-start | bytes 393224 | tf_op jit(solution)/shard_map/late_over_tm/ppermute | solution.py:672
  32.4 0.7 copy-start.8
  36.5 4.5 %collective-permute-start.9 = (bf16[384,128]{1,0:T(8,128)(2,1)S(1)}, bf16[384,128]{1,0:T(8,128)(2,1)S(1)}, u32[]{:S(2)}, u32[]{:S(2)}) collective-permute-start(bf16[384,128]{1,0:T(8,128)(2,1)S(1)} %get-tuple-element.47), channel_id=1, source_target_pairs={{0,1},{1,0},{2,3},{3,2},{4,5},{5,4},{6,7},{7,6},{8,9},{9,8},{10,11... | collective-permute-start | bytes 294920 | tf_op jit(solution)/shard_map/early_gradients_in_chip/ppermute | solution.py:48
  41.1 7.4 %collective-permute-start.10 = (bf16[128,1536]{1,0:T(8,128)(2,1)S(1)}, bf16[128,1536]{1,0:T(8,128)(2,1)S(1)}, u32[]{:S(2)}, u32[]{:S(2)}) collective-permute-start(bf16[128,1536]{1,0:T(8,128)(2,1)S(1)} %shard_map.125), channel_id=1, source_target_pairs={{0,1},{1,0},{2,3},{3,2},{4,5},{5,4},{6,7},{7,6},{8,9},{9,8},{10,11... | collective-permute-start | bytes 1179656 | tf_op jit(solution)/shard_map/late_in_chip/ppermute | solution.py:48
  41.2 6.6 %collective-permute-start.16 = (bf16[384,128]{1,0:T(8,128)(2,1)S(1)}, bf16[384,128]{1,0:T(8,128)(2,1)S(1)}, u32[]{:S(2)}, u32[]{:S(2)}) collective-permute-start(bf16[384,128]{1,0:T(8,128)(2,1)S(1)} %add_convert_fusion.first.piece), channel_id=1, source_target_pairs={{4,0},{0,4},{12,8},{8,12},{5,1},{1,5},{13,9},{9,13},{6,2},{2,6},{1... | collective-permute-start | bytes 294920 | tf_op jit(solution)/shard_map/early_gradients_over_tm/ppermute | solution.py:672
  47.8 4.7 %collective-permute-start.17 = (bf16[576,128]{1,0:T(8,128)(2,1)S(1)}, bf16[576,128]{1,0:T(8,128)(2,1)S(1)}, u32[]{:S(2)}, u32[]{:S(2)}) collective-permute-start(bf16[576,128]{1,0:T(8,128)(2,1)S(1)} %shard_map.128), channel_id=1, source_target_pairs={{4,8},{8,4},{5,9},{9,5},{6,10},{10,6},{7,11},{11,7},{20,24},{24,20... | collective-permute-start | bytes 442376 | tf_op jit(solution)/shard_map/early_pairs_over_tm/ppermute | solution.py:724
  51.9 1.9 %collective-permute-start.11 = (bf16[352,128]{1,0:T(8,128)(2,1)S(1)}, bf16[352,128]{1,0:T(8,128)(2,1)S(1)}, u32[]{:S(2)}, u32[]{:S(2)}) collective-permute-start(bf16[352,128]{1,0:T(8,128)(2,1)S(1)} %get-tuple-element.51), channel_id=1, source_target_pairs={{0,1},{1,0},{2,3},{3,2},{4,5},{5,4},{6,7},{7,6},{8,9},{9,8},{10,11... | collective-permute-start | bytes 270344 | tf_op jit(solution)/shard_map/late_sums_in_chip/ppermute | solution.py:48
  52.0 1.8 %collective-permute-start.12 = (bf16[352,128]{1,0:T(8,128)(2,1)S(1)}, bf16[352,128]{1,0:T(8,128)(2,1)S(1)}, u32[]{:S(2)}, u32[]{:S(2)}) collective-permute-start(bf16[352,128]{1,0:T(8,128)(2,1)S(1)} %get-tuple-element.52), channel_id=1, source_target_pairs={{0,1},{1,0},{2,3},{3,2},{4,5},{5,4},{6,7},{7,6},{8,9},{9,8},{10,11... | collective-permute-start | bytes 270344 | tf_op jit(solution)/shard_map/late_sums_in_chip/ppermute | solution.py:48
  52.5 10.6 %collective-permute-start.18 = (bf16[576,128]{1,0:T(8,128)(2,1)S(1)}, bf16[576,128]{1,0:T(8,128)(2,1)S(1)}, u32[]{:S(2)}, u32[]{:S(2)}) collective-permute-start(bf16[576,128]{1,0:T(8,128)(2,1)S(1)} %collective-permute-done.17.facing), channel_id=1, source_target_pairs={{4,0},{8,12},{5,1},{9,13},{6,2},{10,14},{7,3},{11,15},{20,16},{24,... | collective-permute-start | bytes 442376 | tf_op jit(solution)/shard_map/early_passed_over_tm/ppermute | solution.py:724
  53.9 11.0 %collective-permute-start.13 = (bf16[320,128]{1,0:T(8,128)(2,1)S(1)}, bf16[320,128]{1,0:T(8,128)(2,1)S(1)}, u32[]{:S(2)}, u32[]{:S(2)}) collective-permute-start(bf16[320,128]{1,0:T(8,128)(2,1)S(1)} %get-tuple-element.54.own), channel_id=1, source_target_pairs={{4,0},{0,4},{12,8},{8,12},{5,1},{1,5},{13,9},{9,13},{6,2},{2,6},{1... | collective-permute-start | bytes 245768 | tf_op jit(solution)/shard_map/late_sums_over_tm/ppermute | solution.py:672
  58.4 8.6 %collective-permute-start.14 = (bf16[320,128]{1,0:T(8,128)(2,1)S(1)}, bf16[320,128]{1,0:T(8,128)(2,1)S(1)}, u32[]{:S(2)}, u32[]{:S(2)}) collective-permute-start(bf16[320,128]{1,0:T(8,128)(2,1)S(1)} %get-tuple-element.55), channel_id=1, source_target_pairs={{8,0},{12,4},{0,8},{4,12},{9,1},{13,5},{1,9},{5,13},{10,2},{14,6},... | collective-permute-start | bytes 245768 | tf_op jit(solution)/shard_map/late_sums_over_tm/ppermute | solution.py:672
  58.5 8.5 %collective-permute-start.15 = (bf16[320,128]{1,0:T(8,128)(2,1)S(1)}, bf16[320,128]{1,0:T(8,128)(2,1)S(1)}, u32[]{:S(2)}, u32[]{:S(2)}) collective-permute-start(bf16[320,128]{1,0:T(8,128)(2,1)S(1)} %get-tuple-element.56), channel_id=1, source_target_pairs={{12,0},{8,4},{4,8},{0,12},{13,1},{9,5},{5,9},{1,13},{14,2},{10,6},... | collective-permute-start | bytes 245768 | tf_op jit(solution)/shard_map/late_sums_over_tm/ppermute | solution.py:672
  67.1 5.0 %collective-permute-start.19 = (bf16[2048,128]{1,0:T(8,128)(2,1)S(1)}, bf16[2048,128]{1,0:T(8,128)(2,1)S(1)}, u32[]{:S(2)}, u32[]{:S(2)}) collective-permute-start(bf16[2048,128]{1,0:T(8,128)(2,1)S(1)} %get-tuple-element.58.tail), channel_id=1, source_target_pairs={{0,1},{1,0},{2,3},{3,2},{4,5},{5,4},{6,7},{7,6},{8,9},{9,8},{10,11... | collective-permute-start | bytes 1572872 | tf_op jit(solution)/shard_map/tail_in_chip/ppermute | solution.py:48
  67.1 4.0 %collective-permute-start.20 = (bf16[128,128]{1,0:T(8,128)(2,1)S(1)}, bf16[128,128]{1,0:T(8,128)(2,1)S(1)}, u32[]{:S(2)}, u32[]{:S(2)}) collective-permute-start(bf16[128,128]{1,0:T(8,128)(2,1)S(1)} %get-tuple-element.59), channel_id=1, source_target_pairs={{0,2},{2,0},{1,3},{3,1},{4,6},{6,4},{5,7},{7,5},{8,10},{10,8},{9,1... | collective-permute-start | bytes 98312 | tf_op jit(solution)/shard_map/low_over_head/ppermute | solution.py:48
  68.7 3.3 %collective-permute-start.21 = (bf16[128,128]{1,0:T(8,128)(2,1)S(1)}, bf16[128,128]{1,0:T(8,128)(2,1)S(1)}, u32[]{:S(2)}, u32[]{:S(2)}) collective-permute-start(bf16[128,128]{1,0:T(8,128)(2,1)S(1)} %get-tuple-element.59), channel_id=1, source_target_pairs={{0,3},{1,2},{2,1},{3,0},{4,7},{5,6},{6,5},{7,4},{8,11},{9,10},{10,... | collective-permute-start | bytes 98312 | tf_op jit(solution)/shard_map/low_over_head/ppermute | solution.py:742

commit v12 on v10

--- a/solution.py
+++ b/solution.py
@@ -533,102 +533,110 @@
 
 
 def hand_out_kernel(frames, size, parts, keep_ref, *refs):
-    gots, (piece, facing), (own_ref, *sends, total) = refs[:parts], refs[parts : parts + 2], refs[parts + 2 :]
+    gots, (piece, facing) = refs[:parts], refs[parts : parts + 2]
+    own_low, own_late, near, last, low_third, third, total = refs[-7:]
     me = lax.axis_index("tm")
-    rows = own_ref.shape[0]
+    rows = own_low.shape[0]
     total[...] = keep_ref[...] + jnp.concatenate([got[...].astype(F32) for got in gots], axis=0)
-    for m in range(frames):
-        low = total[pl.ds(pl.multiple_of(size + (me ^ m) * rows, 8), rows), :]
-        if m == 0:
-            own_ref[...] = low
-        else:
-            sends[m - 1][:rows, :] = low.astype(BF16)
-            sends[m - 1][rows : rows + size, :] = total[:size, :].astype(BF16)
-    sends[0][rows + size : rows + 3 * size, :] = piece[...]
-    sends[0][rows + 3 * size :, :] = facing[size:, :]
-    sends[1][rows + size :, :] = piece[:size, :]
-
-
-def hand_out(frames, rows, keep, gots, piece, facing):
+
+    def low(m):
+        return total[pl.ds(pl.multiple_of(size + (me ^ m) * rows, 8), rows), :]
+
+    late = total[:size, :].astype(BF16)
+    own_low[...] = low(0)
+    own_late[...] = late
+    near[:rows, :] = low(1).astype(BF16)
+    near[rows : rows + size, :] = late
+    near[rows + size :, :] = facing[size:, :]
+    low_third[...] = low(2).astype(BF16)
+    last[:rows, :] = low(3).astype(BF16)
+    last[rows:, :] = late
+    third[:size, :] = late
+    third[size:, :] = piece[:size, :]
+
+
+def hand_out(frames, rows, keep, gots, piece, facing, after):
     size, rank = keep.shape[0] - frames * rows, keep.shape[1]
-    own, *sends = pl.pallas_call(
+    sizes = (size, rows + 2 * size, rows + size, rows, 2 * size)
+    return pl.pallas_call(
         functools.partial(hand_out_kernel, frames, size, len(gots)),
-        in_specs=vmem(3 + len(gots)),
-        out_specs=vmem(frames),
+        in_specs=vmem(3 + len(gots)) + [pl.BlockSpec(memory_space=pl.ANY)] * len(after),
+        out_specs=vmem(1 + len(sizes)),
         out_shape=[jax.ShapeDtypeStruct((rows, rank), F32)]
-        + [jax.ShapeDtypeStruct((rows + size * n, rank), BF16) for n in (4, 2, 1)],
+        + [jax.ShapeDtypeStruct((n, rank), BF16) for n in sizes],
         scratch_shapes=[pltpu.VMEM(keep.shape, F32)],
         compiler_params=SMALL,
-    )(keep, *gots, piece, facing)
-    return own, sends
-
-
-def collect_kernel(wide, own_low, own, near, third, last, piece, facing, out_ref, low_ref):
-    rows = own_low.shape[0]
-    size = own.shape[0] - rows
-    low = own_low[...]
-    for got in (near, third, last):
-        low = low + got[:rows, :].astype(F32)
-    out_ref[:rows, :] = low.astype(BF16)
-    low_ref[...] = low.astype(BF16)
+    )(keep, *gots, piece, facing, *after)
+
+
+def sum_low_kernel(own, near, third, last, out):
+    rows = own.shape[0]
+    out[...] = own[...] + near[:rows, :].astype(F32) + third[...].astype(F32) + last[:rows, :].astype(F32)
+
+
+def sum_low(own, near, third, last):
+    return pl.pallas_call(
+        sum_low_kernel,
+        in_specs=vmem(4),
+        out_specs=pl.BlockSpec(memory_space=pltpu.VMEM),
+        out_shape=jax.ShapeDtypeStruct(own.shape, F32),
+        compiler_params=SMALL,
+    )(own, near, third, last)
+
+
+def collect_kernel(wide, low_ref, low_head, own, near, third, last, piece, pair, facing, out_ref):
+    rows, size = low_ref.shape[0], own.shape[0]
+    out_ref[:rows, :] = (low_ref[...] + low_head[...]).astype(BF16)
     middle = lookup(wide, lax.axis_index("tm")) > 0
-
-    def part(ref, n):
-        return ref[rows + n * size : rows + (n + 1) * size, :]
-
-    blocks = [part(ref, 0) for ref in (own, near, third, last)]
-    blocks += [piece[:size, :], part(near, 1), part(third, 1), facing[:size, :]]
-    blocks.append(jnp.where(middle, piece[size:, :], part(near, 2)))
-    blocks.append(jnp.where(middle, facing[size:, :], part(near, 3)))
+    blocks = [own[...], near[rows : rows + size, :], third[:size, :], last[rows:, :]]
+    blocks += [piece[:size, :], pair[:size, :], third[size:, :], facing[:size, :]]
+    blocks.append(jnp.where(middle, piece[size:, :], pair[size:, :]))
+    blocks.append(jnp.where(middle, facing[size:, :], near[rows + size :, :]))
     for n, block in enumerate(blocks):
         out_ref[rows + n * size : rows + (n + 1) * size, :] = block
 
 
-def collect(wide, own_low, own, gots, piece, facing):
-    (rows, rank), size = own_low.shape, piece.shape[0] // 2
+def collect(wide, low, low_head, *pieces):
+    (rows, rank), size = low.shape, pieces[0].shape[0]
     return pl.pallas_call(
         functools.partial(collect_kernel, wide),
-        in_specs=vmem(4 + len(gots)),
-        out_specs=vmem(2),
-        out_shape=[
-            jax.ShapeDtypeStruct((rows + 10 * size, rank), BF16),
-            jax.ShapeDtypeStruct((rows, rank), BF16),
-        ],
+        in_specs=vmem(2 + len(pieces)),
+        out_specs=pl.BlockSpec(memory_space=pltpu.VMEM),
+        out_shape=jax.ShapeDtypeStruct((rows + 10 * size, rank), BF16),
         compiler_params=SMALL,
-    )(own_low, own, *gots, piece, facing)
-
-
-def place_kernel(frames, lead, late, rest, tail, tail2, low_head, low_diag, *outs):
+    )(low, low_head, *pieces)
+
+
+def place_kernel(frames, lead, late, rest, tail, tail2, *outs):
     me, half = lax.axis_index("tm"), lax.axis_index("rep")
     first = half == 0
     rank = outs[0].shape[0]
     cut = 3 * rank // 2
-    rows = low_head.shape[0]
-    same = tail[:rows, :].astype(F32) + low_head[...].astype(F32)
-    other = tail2[:rows, :].astype(F32) + low_diag[...].astype(F32)
-    outs[3][:rows, :] = jnp.where(first, same, other)
-    outs[3][rows:, :] = jnp.where(first, other, same)
+    rows = outs[3].shape[0] // 2
+
+    def both(here):
+        a, b = tail[here, :].astype(F32), tail2[here, :].astype(F32)
+        return jnp.concatenate([jnp.where(first, a, b), jnp.where(first, b, a)], axis=0)
+
+    outs[3][...] = both(slice(0, rows))
     side = me // 2
     places = [lookup(late, me ^ m) for m in range(frames)] + [lookup(lead, me ^ m) for m in range(frames)]
     places += [lookup(rest, 1 + side), lookup(rest, 2 - side)]
     for n, head in enumerate(places):
-        here = slice(rows + n * cut, rows + (n + 1) * cut)
-        a, b = tail[here, :].astype(F32), tail2[here, :].astype(F32)
-        both = jnp.concatenate([jnp.where(first, a, b), jnp.where(first, b, a)], axis=0)
+        whole = both(slice(rows + n * cut, rows + (n + 1) * cut))
         for o in range(3):
-            outs[o][:, column(head)] = both[o * rank : (o + 1) * rank]
-
-
-def place(frames, lead, late, rest, tail, tail2, low_head, low_diag, rank, width):
-    rows = low_head.shape[0]
+            outs[o][:, column(head)] = whole[o * rank : (o + 1) * rank]
+
+
+def place(frames, lead, late, rest, tail, tail2, rows, rank, width):
     return pl.pallas_call(
         functools.partial(place_kernel, frames, lead, late, rest),
-        in_specs=vmem(4),
+        in_specs=vmem(2),
         out_specs=vmem(4),
         out_shape=[jax.ShapeDtypeStruct((rank, width), F32)] * 3
         + [jax.ShapeDtypeStruct((2 * rows, rank), F32)],
         compiler_params=SMALL,
-    )(tail, tail2, low_head, low_diag)
+    )(tail, tail2)
 
 
 def exchange_plan(
@@ -709,17 +717,21 @@
     got = swap_in_chip("early_gradients", give)
     piece = (keep + got.astype(F32)).astype(BF16)
     *late_side, _ = sides("late", 2, late_got, False, (3,), 0, [got])
+    pair = meet("early_gradients", piece, 1)
     facing = meet("early_gradients", piece, 3)
-    keep, *gives = head_group([late], band_width, [t_side, late_side], adapters, low, [piece])
+    keep, *gives = head_group([late], band_width, [t_side, late_side], adapters, low, [])
     gives = [swap_in_chip("late_sums", g) for g in gives]
-    own_low, sends = hand_out(frames, rows, keep, gives, piece, facing)
-    gots = [meet("late_sums", block, m) for m, block in enumerate(sends, 1)]
-    tail, low = collect(rest[1], own_low, sends[2], gots, piece, facing)
-    diag = [(0, 3), (1, 2), (2, 1), (3, 0)]
+    own_low, own, near, last, low_third, third = hand_out(
+        frames, rows, keep, gives, piece, facing, [pair]
+    )
+    near, last = meet("late_sums", near, 1), meet("late_sums", last, 3)
+    low = sum_low(own_low, near, meet("low", low_third, 2), last)
+    third = meet("late_gradients", third, 2)
     with jax.named_scope("low_over_head"):
-        low_head, low_diag = swap(low, "head"), lax.ppermute(low, ("head", "rep"), diag)
+        low_head = swap(low, "head")
+    tail = collect(rest[1], low, low_head, own, near, third, last, piece, pair, facing)
     outs = place(
-        frames, lead[0], late[0], rest[0], tail, swap_in_chip("tail", tail), low_head, low_diag, rank, width
+        frames, lead[0], late[0], rest[0], tail, swap_in_chip("tail", tail), rows, rank, width
     )
     return tuple(outs)
 

time: 70.2 us -> 71 us (1.011)
  starting transfers between devices: 25 us -> 27.8 us
  waiting for transfers between devices: 31.3 us -> 29.3 us
    ppermute x11 -> x13, starting transfers between devices: 21.5 us -> 24.9 us  [meet(): return lax.ppermute(block, 'tm', [(j ^ m, j) for j in targets])]
    ppermute x11 -> x13, waiting for transfers between devices: 27.7 us -> 24.7 us  [meet(): return lax.ppermute(block, 'tm', [(j ^ m, j) for j in targets])]
    ppermute x8, waiting for transfers between devices: 2.39 us -> 4.67 us  [swap(): return lax.ppermute(block, axis, [(0, 1), (1, 0)])]
    ppermute x1 -> x0, starting transfers between devices: 1.61 us -> none  [exchange_plan(): lax.ppermute(low, ('head', 'rep'), diag)]
    ppermute x1 -> x0, waiting for transfers between devices: 1.26 us -> none  [exchange_plan(): lax.ppermute(low, ('head', 'rep'), diag)]
    ppermute x8, starting transfers between devices: 1.94 us -> 2.95 us  [swap(): return lax.ppermute(block, axis, [(0, 1), (1, 0)])]
  transfers between devices with their start and end apart: 20 -> 21, of which waited for: 8 -> 7; matrix products, arithmetic and copies ran while one was open for 0% -> 0% of each run, Pallas kernels for 11% -> 11%
where the time goes in v12:
time: 71 us; the launch traced here: 70.9 us
  waiting for transfers between devices  29.3 us (41%)
  starting transfers between devices  27.8 us (39%)
  Pallas kernels  12.1 us (17%)
  between operations  0.92 us (1%)
    ppermute x13, starting transfers between devices, meet(): return lax.ppermute(block, 'tm', [(j ^ m, j) for j in targets])  24.9 us
    ppermute x13, waiting for transfers between devices, meet(): return lax.ppermute(block, 'tm', [(j ^ m, j) for j in targets])  24.7 us
    pallas_call x2, Pallas kernels, head_group(): pl.pallas_call(functools.partial(group_kernel, heads, frames, chained, le...  6.87 us
    ppermute x8, waiting for transfers between devices, swap(): return lax.ppermute(block, axis, [(0, 1), (1, 0)])  4.67 us
    pallas_call x2, Pallas kernels, pack(): pl.pallas_call(functools.partial(pack_kernel, frames, outputs), in_specs=...  3.51 us
    ppermute x8, starting transfers between devices, swap(): return lax.ppermute(block, axis, [(0, 1), (1, 0)])  2.95 us
    pallas_call x1, Pallas kernels, place(): pl.pallas_call(functools.partial(place_kernel, frames, lead, late, rest),...  1.47 us
  transfers between devices with their start and end apart: 21, of which 7 were waited for; matrix products, arithmetic and copies ran while one was open for 0% of the time, Pallas kernels for 11%

profile of v12, /device:TPU:0, one launch (start us, length us, event | category | flops | bytes accessed | tf_op | source)
XLA Modules:
  0.0 70.9 jit_solution(11962733611832378437)
XLA Ops:
  0.7 2.6 %shard_map.121 = (bf16[128,1664]{1,0:T(8,128)(2,1)}, bf16[128,640]{1,0:T(8,128)(2,1)}, bf16[128,512]{1,0:T(8,128)(2,1)}, bf16[128,640]{1,0:T(8,128)(2,1)}, bf16[128,512]{1,0:T(8,128)(2,1)}) custom-call(bf16[128,1280]{1,0:T(8,128)(2,1)} %fq_ref.3, bf16[128,1280]{1,0:T(8,128)(2,1)} %do_ref.3, bf16[256,1280]{1,0:T(8,128)(2,1)} %fk_ref.3, ...), custom_call_target="tpu_custom_call" | custom-call | tf_op jit(solution)/shard_map/pallas_call | solution.py:301
  3.3 3.1 %collective-permute-start = (bf16[128,1664]{1,0:T(8,128)(2,1)}, bf16[128,1664]{1,0:T(8,128)(2,1)S(1)}, u32[]{:S(2)}, u32[]{:S(2)}) collective-permute-start(bf16[128,1664]{1,0:T(8,128)(2,1)} %get-tuple-element.33), channel_id=1, source_target_pairs={{4,0},{0,4},{12,8},{8,12},{5,1},{1,5},{13,9},{9,13},{6,2},{2,6},{1... | collective-permute-start | bytes 1277960 | tf_op jit(solution)/shard_map/nearest_over_tm/ppermute | solution.py:669
  6.3 2.6 %collective-permute-start.1 = (bf16[128,640]{1,0:T(8,128)(2,1)}, bf16[128,640]{1,0:T(8,128)(2,1)S(1)}, u32[]{:S(2)}, u32[]{:S(2)}) collective-permute-start(bf16[128,640]{1,0:T(8,128)(2,1)} %get-tuple-element.34), channel_id=1, source_target_pairs={{8,0},{12,4},{0,8},{4,12},{9,1},{13,5},{1,9},{5,13},{10,2},{14,6},... | collective-permute-start | bytes 491528 | tf_op jit(solution)/shard_map/lead_over_tm/ppermute | solution.py:669
  8.9 3.8 %collective-permute-start.6 = (bf16[128,512]{1,0:T(8,128)(2,1)}, bf16[128,512]{1,0:T(8,128)(2,1)S(1)}, u32[]{:S(2)}, u32[]{:S(2)}) collective-permute-start(bf16[128,512]{1,0:T(8,128)(2,1)} %get-tuple-element.44), channel_id=1, source_target_pairs={{12,4},{0,8},{13,5},{1,9},{14,6},{2,10},{15,7},{3,11},{28,20},{16,... | collective-permute-start | bytes 393224 | tf_op jit(solution)/shard_map/rest_over_tm/ppermute | solution.py:669
  12.8 0.7 collective-permute-start.7
  13.5 0.9 %shard_map.120 = (bf16[128,512]{1,0:T(8,128)(2,1)S(1)}, bf16[128,512]{1,0:T(8,128)(2,1)S(1)}, bf16[128,512]{1,0:T(8,128)(2,1)S(1)}, bf16[128,256]{1,0:T(8,128)(2...) custom-call(bf16[128,1280]{1,0:T(8,128)(2,1)S(1)} %copy-done.2, ...), custom_call_target="tpu_custom_call" | custom-call | tf_op jit(solution)/shard_map/pallas_call | solution.py:301
  14.4 6.0 %collective-permute-done.1.refs_1_.refs_3_ = bf16[128,640]{1,0:T(8,128)(2,1)S(1)} collective-permute-done((bf16[128,640]{1,0:T(8,128)(2,1)}, bf16[128,640]{1,0:T(8,128)(2,1)S(1)}, u32[]{:S(2)}, u32[]{:S(2)}) %collective-permute-start.1) | collective-permute-done | bytes 163872 | tf_op jit(solution)/shard_map/lead_over_tm/ppermute | solution.py:669
  20.4 6.4 %collective-permute-done.2.refs_2_.refs_4_ = bf16[128,640]{1,0:T(8,128)(2,1)S(1)} collective-permute-done((bf16[128,640]{1,0:T(8,128)(2,1)}, bf16[128,640]{1,0:T(8,128)(2,1)S(1)}, u32[]{:S(2)}, u32[]{:S(2)}) %collective-permute-start.2) | collective-permute-done | bytes 163872 | tf_op jit(solution)/shard_map/lead_over_tm/ppermute | solution.py:669
  26.9 0.1 collective-permute-start.3
  27.0 0.5 collective-permute-start.8
  27.6 3.5 %collective-permute-start.4 = (bf16[128,512]{1,0:T(8,128)(2,1)S(1)}, bf16[128,512]{1,0:T(8,128)(2,1)S(1)}, u32[]{:S(2)}, u32[]{:S(2)}) collective-permute-start(bf16[128,512]{1,0:T(8,128)(2,1)S(1)} %get-tuple-element.39), channel_id=1, source_target_pairs={{8,0},{12,4},{0,8},{4,12},{9,1},{13,5},{1,9},{5,13},{10,2},{14,6},... | collective-permute-start | bytes 393224 | tf_op jit(solution)/shard_map/late_over_tm/ppermute | solution.py:669
  31.0 1.4 %collective-permute-start.5 = (bf16[128,512]{1,0:T(8,128)(2,1)S(1)}, bf16[128,512]{1,0:T(8,128)(2,1)S(1)}, u32[]{:S(2)}, u32[]{:S(2)}) collective-permute-start(bf16[128,512]{1,0:T(8,128)(2,1)S(1)} %get-tuple-element.40), channel_id=1, source_target_pairs={{12,0},{8,4},{4,8},{0,12},{13,1},{9,5},{5,9},{1,13},{14,2},{10,6},... | collective-permute-start | bytes 393224 | tf_op jit(solution)/shard_map/late_over_tm/ppermute | solution.py:669
  32.4 0.6 copy-done.8
  33.1 3.4 %shard_map.124 = (f32[384,128]{1,0:T(8,128)S(1)}, bf16[384,128]{1,0:T(8,128)(2,1)S(1)}, f32[512,128]{1,0:T(8,128)S(1)}, f32[512,128]{1,0:T(8,128)S(1)}) custom-call(s32[4,4]{1,0:T(4,128)S(1)} %copy-done.8, bf16[128,128]{1,0:T(8,128)(2,1)S(1)} %get-tuple-element.32.refs_1_, bf16[128,1664]{1,0:T(8,128)(2,1)S(1)} %collective-permute-done.refs_0_.refs_2_, ...), custom_call_target="tpu_custom_call" | custom-call | tf_op jit(solution)/shard_map/pallas_call | solution.py:521
  36.5 0.1 collective-permute-start.9
  36.6 4.4 %collective-permute-done.4.refs_1_.refs_8_ = bf16[128,512]{1,0:T(8,128)(2,1)S(1)} collective-permute-done((bf16[128,512]{1,0:T(8,128)(2,1)S(1)}, bf16[128,512]{1,0:T(8,128)(2,1)S(1)}, u32[]{:S(2)}, u32[]{:S(2)}) %collective-permute-start.4) | collective-permute-done | bytes 131104 | tf_op jit(solution)/shard_map/late_over_tm/ppermute | solution.py:669
  41.0 0.1 collective-permute-start.10
  41.2 3.2 %collective-permute-start.14 = (bf16[384,128]{1,0:T(8,128)(2,1)S(1)}, bf16[384,128]{1,0:T(8,128)(2,1)S(1)}, u32[]{:S(2)}, u32[]{:S(2)}) collective-permute-start(bf16[384,128]{1,0:T(8,128)(2,1)S(1)} %add_convert_fusion.refs_2_.piece), channel_id=1, source_target_pairs={{4,0},{0,4},{12,8},{8,12},{5,1},{1,5},{13,9},{9,13},{6,2},{2,6},{1... | collective-permute-start | bytes 294920 | tf_op jit(solution)/shard_map/early_gradients_over_tm/ppermute | solution.py:669
  44.3 1.4 %collective-permute-start.13 = (bf16[384,128]{1,0:T(8,128)(2,1)S(1)}, bf16[384,128]{1,0:T(8,128)(2,1)S(1)}, u32[]{:S(2)}, u32[]{:S(2)}) collective-permute-start(bf16[384,128]{1,0:T(8,128)(2,1)S(1)} %add_convert_fusion.refs_2_.piece), channel_id=1, source_target_pairs={{12,0},{8,4},{4,8},{0,12},{13,1},{9,5},{5,9},{1,13},{14,2},{10,6},... | collective-permute-start | bytes 294920 | tf_op jit(solution)/shard_map/early_gradients_over_tm/ppermute | solution.py:669
  45.7 3.4 %shard_map.126 = (f32[704,128]{1,0:T(8,128)S(1)}, bf16[352,128]{1,0:T(8,128)(2,1)S(1)}, bf16[352,128]{1,0:T(8,128)(2,1)S(1)}) custom-call(s32[4,4]{1,0:T(4,128)S(1)} %copy-done.8, bf16[128,128]{1,0:T(8,128)(2,1)S(1)} %get-tuple-element.32.refs_1_, bf16[128,1664]{1,0:T(8,128)(2,1)S(1)} %collective-permute-done.refs_0_.refs_2_, ...), custom_call_target="tpu_custom_call" | custom-call | tf_op jit(solution)/shard_map/pallas_call | solution.py:521
  49.1 0.1 collective-permute-start.11
  49.2 0.5 collective-permute-start.12
  49.7 1.5 %collective-permute-done.13.refs_3_.facing = bf16[384,128]{1,0:T(8,128)(2,1)S(1)} collective-permute-done((bf16[384,128]{1,0:T(8,128)(2,1)S(1)}, bf16[384,128]{1,0:T(8,128)(2,1)S(1)}, u32[]{:S(2)}, u32[]{:S(2)}) %collective-permute-start.13) | collective-permute-done | bytes 98336 | tf_op jit(solution)/shard_map/early_gradients_over_tm/ppermute | solution.py:669
  51.2 0.1 shard_map.127
  51.3 2.3 %collective-permute-start.17 = (bf16[320,128]{1,0:T(8,128)(2,1)S(1)}, bf16[320,128]{1,0:T(8,128)(2,1)S(1)}, u32[]{:S(2)}, u32[]{:S(2)}) collective-permute-start(bf16[320,128]{1,0:T(8,128)(2,1)S(1)} %get-tuple-element.57), channel_id=1, source_target_pairs={{12,0},{8,4},{4,8},{0,12},{13,1},{9,5},{5,9},{1,13},{14,2},{10,6},... | collective-permute-start | bytes 245768 | tf_op jit(solution)/shard_map/late_sums_over_tm/ppermute | solution.py:669
  53.7 1.1 %collective-permute-start.16 = (bf16[128,128]{1,0:T(8,128)(2,1)S(1)}, bf16[128,128]{1,0:T(8,128)(2,1)S(1)}, u32[]{:S(2)}, u32[]{:S(2)}) collective-permute-start(bf16[128,128]{1,0:T(8,128)(2,1)S(1)} %get-tuple-element.56), channel_id=1, source_target_pairs={{8,0},{12,4},{0,8},{4,12},{9,1},{13,5},{1,9},{5,13},{10,2},{14,6},... | collective-permute-start | bytes 98312 | tf_op jit(solution)/shard_map/low_over_tm/ppermute | solution.py:669
  54.8 1.8 %collective-permute-start.19 = (bf16[384,128]{1,0:T(8,128)(2,1)S(1)}, bf16[384,128]{1,0:T(8,128)(2,1)S(1)}, u32[]{:S(2)}, u32[]{:S(2)}) collective-permute-start(bf16[384,128]{1,0:T(8,128)(2,1)S(1)} %get-tuple-element.59), channel_id=1, source_target_pairs={{8,0},{12,4},{0,8},{4,12},{9,1},{13,5},{1,9},{5,13},{10,2},{14,6},... | collective-permute-start | bytes 294920 | tf_op jit(solution)/shard_map/late_gradients_over_tm/ppermute | solution.py:669
  56.6 6.4 %collective-permute-done.16.third = bf16[128,128]{1,0:T(8,128)(2,1)S(1)} collective-permute-done((bf16[128,128]{1,0:T(8,128)(2,1)S(1)}, bf16[128,128]{1,0:T(8,128)(2,1)S(1)}, u32[]{:S(2)}, u32[]{:S(2)}) %collective-permute-start.16) | collective-permute-done | bytes 32800 | tf_op jit(solution)/shard_map/low_over_tm/ppermute | solution.py:669
  63.0 1.6 %collective-permute-start.18 = (f32[128,128]{1,0:T(8,128)S(1)}, f32[128,128]{1,0:T(8,128)S(1)}, u32[]{:S(2)}, u32[]{:S(2)}) collective-permute-start(f32[128,128]{1,0:T(8,128)S(1)} %shard_map.128.low_ref), channel_id=1, source_target_pairs={{0,2},{2,0},{1,3},{3,1},{4,6},{6,4},{5,7},{7,5},{8,10},{10,8},{9,1... | collective-permute-start | bytes 196616 | tf_op jit(solution)/shard_map/low_over_head/ppermute | solution.py:48
  64.6 2.8 %collective-permute-done.18.low_head = f32[128,128]{1,0:T(8,128)S(1)} collective-permute-done((f32[128,128]{1,0:T(8,128)S(1)}, f32[128,128]{1,0:T(8,128)S(1)}, u32[]{:S(2)}, u32[]{:S(2)}) %collective-permute-start.18) | collective-permute-done | bytes 65568 | tf_op jit(solution)/shard_map/low_over_head/ppermute | solution.py:48
  67.5 1.9 %collective-permute-done.20.tail2 = bf16[2048,128]{1,0:T(8,128)(2,1)S(1)} collective-permute-done((bf16[2048,128]{1,0:T(8,128)(2,1)S(1)}, bf16[2048,128]{1,0:T(8,128)(2,1)S(1)}, u32[]{:S(2)}, u32[]{:S(2)}) %collective-permute-start.20) | collective-permute-done | bytes 524320 | tf_op jit(solution)/shard_map/tail_in_chip/ppermute | solution.py:48
  69.4 1.5 %shard_map.130 = (f32[128,1280]{1,0:T(8,128)}, f32[128,1280]{1,0:T(8,128)}, f32[128,1280]{1,0:T(8,128)}, f32[256,128]{1,0:T(8,128)}) custom-call(bf16[2048,128]{1,0:T(8,128)(2,1)S(1)} %shard_map.129.tail, bf16[2048,128]{1,0:T(8,128)(2,1)S(1)} %collective-permute-done.20.tail2), custom_call_target="tpu_custom_call" | custom-call | tf_op jit(solution)/shard_map/pallas_call | solution.py:632
  (40 shorter events, 0.4 us)
Async XLA Ops:
  0.6 12.8 %copy-start.3 = (bf16[128,1280]{1,0:T(8,128)(2,1)S(1)}, bf16[128,1280]{1,0:T(8,128)(2,1)}, u32[]{:S(2)}) copy-start(bf16[128,1280]{1,0:T(8,128)(2,1)} %do_ref.3) | copy-start | bytes 983044
  0.6 12.8 %copy-start.7 = (bf16[256,128]{1,0:T(8,128)(2,1)S(1)}, bf16[256,128]{1,0:T(8,128)(2,1)}, u32[]{:S(2)}) copy-start(bf16[256,128]{1,0:T(8,128)(2,1)} %t_ref.3) | copy-start | bytes 196612
  0.7 12.8 %copy-start.1 = (bf16[256,1280]{1,0:T(8,128)(2,1)S(1)}, bf16[256,1280]{1,0:T(8,128)(2,1)}, u32[]{:S(2)}) copy-start(bf16[256,1280]{1,0:T(8,128)(2,1)} %fv_ref.3) | copy-start | bytes 1966084
  0.7 12.8 %copy-start = (bf16[256,1280]{1,0:T(8,128)(2,1)S(1)}, bf16[256,1280]{1,0:T(8,128)(2,1)}, u32[]{:S(2)}) copy-start(bf16[256,1280]{1,0:T(8,128)(2,1)} %fk_ref.3) | copy-start | bytes 1966084
  0.7 12.8 %copy-start.2 = (bf16[128,1280]{1,0:T(8,128)(2,1)S(1)}, bf16[128,1280]{1,0:T(8,128)(2,1)}, u32[]{:S(2)}) copy-start(bf16[128,1280]{1,0:T(8,128)(2,1)} %fq_ref.3) | copy-start | bytes 983044
  3.3 23.6 %collective-permute-start = (bf16[128,1664]{1,0:T(8,128)(2,1)}, bf16[128,1664]{1,0:T(8,128)(2,1)S(1)}, u32[]{:S(2)}, u32[]{:S(2)}) collective-permute-start(bf16[128,1664]{1,0:T(8,128)(2,1)} %get-tuple-element.33), channel_id=1, source_target_pairs={{4,0},{0,4},{12,8},{8,12},{5,1},{1,5},{13,9},{9,13},{6,2},{2,6},{1... | collective-permute-start | bytes 1277960 | tf_op jit(solution)/shard_map/nearest_over_tm/ppermute | solution.py:669
  6.3 14.1 %collective-permute-start.1 = (bf16[128,640]{1,0:T(8,128)(2,1)}, bf16[128,640]{1,0:T(8,128)(2,1)S(1)}, u32[]{:S(2)}, u32[]{:S(2)}) collective-permute-start(bf16[128,640]{1,0:T(8,128)(2,1)} %get-tuple-element.34), channel_id=1, source_target_pairs={{8,0},{12,4},{0,8},{4,12},{9,1},{13,5},{1,9},{5,13},{10,2},{14,6},... | collective-permute-start | bytes 491528 | tf_op jit(solution)/shard_map/lead_over_tm/ppermute | solution.py:669
  8.9 17.9 %collective-permute-start.2 = (bf16[128,640]{1,0:T(8,128)(2,1)}, bf16[128,640]{1,0:T(8,128)(2,1)S(1)}, u32[]{:S(2)}, u32[]{:S(2)}) collective-permute-start(bf16[128,640]{1,0:T(8,128)(2,1)} %get-tuple-element.35), channel_id=1, source_target_pairs={{12,0},{8,4},{4,8},{0,12},{13,1},{9,5},{5,9},{1,13},{14,2},{10,6},... | collective-permute-start | bytes 491528 | tf_op jit(solution)/shard_map/lead_over_tm/ppermute | solution.py:669
  8.9 18.0 %collective-permute-start.6 = (bf16[128,512]{1,0:T(8,128)(2,1)}, bf16[128,512]{1,0:T(8,128)(2,1)S(1)}, u32[]{:S(2)}, u32[]{:S(2)}) collective-permute-start(bf16[128,512]{1,0:T(8,128)(2,1)} %get-tuple-element.44), channel_id=1, source_target_pairs={{12,4},{0,8},{13,5},{1,9},{14,6},{2,10},{15,7},{3,11},{28,20},{16,... | collective-permute-start | bytes 393224 | tf_op jit(solution)/shard_map/rest_over_tm/ppermute | solution.py:669
  12.8 14.2 %collective-permute-start.7 = (bf16[128,512]{1,0:T(8,128)(2,1)}, bf16[128,512]{1,0:T(8,128)(2,1)S(1)}, u32[]{:S(2)}, u32[]{:S(2)}) collective-permute-start(bf16[128,512]{1,0:T(8,128)(2,1)} %get-tuple-element.45), channel_id=1, source_target_pairs={{8,4},{4,8},{9,5},{5,9},{10,6},{6,10},{11,7},{7,11},{24,20},{20,24... | collective-permute-start | bytes 393224 | tf_op jit(solution)/shard_map/rest_over_tm/ppermute | solution.py:669
  26.8 5.6 %copy-start.6 = (bf16[128,1280]{1,0:T(8,128)(2,1)S(1)}, bf16[128,1280]{1,0:T(8,128)(2,1)}, u32[]{:S(2)}) copy-start(bf16[128,1280]{1,0:T(8,128)(2,1)} %refs_14_.3) | copy-start | bytes 983044
  26.9 5.6 %copy-start.4 = (bf16[128,1280]{1,0:T(8,128)(2,1)S(1)}, bf16[128,1280]{1,0:T(8,128)(2,1)}, u32[]{:S(2)}) copy-start(bf16[128,1280]{1,0:T(8,128)(2,1)} %refs_12_.1) | copy-start | bytes 983044
  26.9 5.6 %copy-start.5 = (bf16[128,1280]{1,0:T(8,128)(2,1)S(1)}, bf16[128,1280]{1,0:T(8,128)(2,1)}, u32[]{:S(2)}) copy-start(bf16[128,1280]{1,0:T(8,128)(2,1)} %refs_13_.1) | copy-start | bytes 983044
  26.9 5.5 %collective-permute-start.3 = (bf16[128,1152]{1,0:T(8,128)(2,1)S(1)}, bf16[128,1152]{1,0:T(8,128)(2,1)S(1)}, u32[]{:S(2)}, u32[]{:S(2)}) collective-permute-start(bf16[128,1152]{1,0:T(8,128)(2,1)S(1)} %shard_map.122), channel_id=1, source_target_pairs={{0,1},{1,0},{2,3},{3,2},{4,5},{5,4},{6,7},{7,6},{8,9},{9,8},{10,11... | collective-permute-start | bytes 884744 | tf_op jit(solution)/shard_map/lead_in_chip/ppermute | solution.py:48
  27.0 5.4 %collective-permute-start.8 = (bf16[128,768]{1,0:T(8,128)(2,1)S(1)}, bf16[128,768]{1,0:T(8,128)(2,1)S(1)}, u32[]{:S(2)}, u32[]{:S(2)}) collective-permute-start(bf16[128,768]{1,0:T(8,128)(2,1)S(1)} %shard_map.123), channel_id=1, source_target_pairs={{0,1},{1,0},{2,3},{3,2},{4,5},{5,4},{6,7},{7,6},{8,9},{9,8},{10,11... | collective-permute-start | bytes 589832 | tf_op jit(solution)/shard_map/rest_in_chip/ppermute | solution.py:48
  27.6 13.5 %collective-permute-start.4 = (bf16[128,512]{1,0:T(8,128)(2,1)S(1)}, bf16[128,512]{1,0:T(8,128)(2,1)S(1)}, u32[]{:S(2)}, u32[]{:S(2)}) collective-permute-start(bf16[128,512]{1,0:T(8,128)(2,1)S(1)} %get-tuple-element.39), channel_id=1, source_target_pairs={{8,0},{12,4},{0,8},{4,12},{9,1},{13,5},{1,9},{5,13},{10,2},{14,6},... | collective-permute-start | bytes 393224 | tf_op jit(solution)/shard_map/late_over_tm/ppermute | solution.py:669
  31.0 10.0 %collective-permute-start.5 = (bf16[128,512]{1,0:T(8,128)(2,1)S(1)}, bf16[128,512]{1,0:T(8,128)(2,1)S(1)}, u32[]{:S(2)}, u32[]{:S(2)}) collective-permute-start(bf16[128,512]{1,0:T(8,128)(2,1)S(1)} %get-tuple-element.40), channel_id=1, source_target_pairs={{12,0},{8,4},{4,8},{0,12},{13,1},{9,5},{5,9},{1,13},{14,2},{10,6},... | collective-permute-start | bytes 393224 | tf_op jit(solution)/shard_map/late_over_tm/ppermute | solution.py:669
  32.4 0.7 copy-start.8
  36.5 4.5 %collective-permute-start.9 = (bf16[384,128]{1,0:T(8,128)(2,1)S(1)}, bf16[384,128]{1,0:T(8,128)(2,1)S(1)}, u32[]{:S(2)}, u32[]{:S(2)}) collective-permute-start(bf16[384,128]{1,0:T(8,128)(2,1)S(1)} %get-tuple-element.47), channel_id=1, source_target_pairs={{0,1},{1,0},{2,3},{3,2},{4,5},{5,4},{6,7},{7,6},{8,9},{9,8},{10,11... | collective-permute-start | bytes 294920 | tf_op jit(solution)/shard_map/early_gradients_in_chip/ppermute | solution.py:48
  41.0 4.6 %collective-permute-start.10 = (bf16[128,1536]{1,0:T(8,128)(2,1)S(1)}, bf16[128,1536]{1,0:T(8,128)(2,1)S(1)}, u32[]{:S(2)}, u32[]{:S(2)}) collective-permute-start(bf16[128,1536]{1,0:T(8,128)(2,1)S(1)} %shard_map.125), channel_id=1, source_target_pairs={{0,1},{1,0},{2,3},{3,2},{4,5},{5,4},{6,7},{7,6},{8,9},{9,8},{10,11... | collective-permute-start | bytes 1179656 | tf_op jit(solution)/shard_map/late_in_chip/ppermute | solution.py:48
  41.2 8.5 %collective-permute-start.14 = (bf16[384,128]{1,0:T(8,128)(2,1)S(1)}, bf16[384,128]{1,0:T(8,128)(2,1)S(1)}, u32[]{:S(2)}, u32[]{:S(2)}) collective-permute-start(bf16[384,128]{1,0:T(8,128)(2,1)S(1)} %add_convert_fusion.refs_2_.piece), channel_id=1, source_target_pairs={{4,0},{0,4},{12,8},{8,12},{5,1},{1,5},{13,9},{9,13},{6,2},{2,6},{1... | collective-permute-start | bytes 294920 | tf_op jit(solution)/shard_map/early_gradients_over_tm/ppermute | solution.py:669
  44.3 6.8 %collective-permute-start.13 = (bf16[384,128]{1,0:T(8,128)(2,1)S(1)}, bf16[384,128]{1,0:T(8,128)(2,1)S(1)}, u32[]{:S(2)}, u32[]{:S(2)}) collective-permute-start(bf16[384,128]{1,0:T(8,128)(2,1)S(1)} %add_convert_fusion.refs_2_.piece), channel_id=1, source_target_pairs={{12,0},{8,4},{4,8},{0,12},{13,1},{9,5},{5,9},{1,13},{14,2},{10,6},... | collective-permute-start | bytes 294920 | tf_op jit(solution)/shard_map/early_gradients_over_tm/ppermute | solution.py:669
  49.1 2.0 %collective-permute-start.11 = (bf16[352,128]{1,0:T(8,128)(2,1)S(1)}, bf16[352,128]{1,0:T(8,128)(2,1)S(1)}, u32[]{:S(2)}, u32[]{:S(2)}) collective-permute-start(bf16[352,128]{1,0:T(8,128)(2,1)S(1)} %get-tuple-element.51), channel_id=1, source_target_pairs={{0,1},{1,0},{2,3},{3,2},{4,5},{5,4},{6,7},{7,6},{8,9},{9,8},{10,11... | collective-permute-start | bytes 270344 | tf_op jit(solution)/shard_map/late_sums_in_chip/ppermute | solution.py:48
  49.2 2.0 %collective-permute-start.12 = (bf16[352,128]{1,0:T(8,128)(2,1)S(1)}, bf16[352,128]{1,0:T(8,128)(2,1)S(1)}, u32[]{:S(2)}, u32[]{:S(2)}) collective-permute-start(bf16[352,128]{1,0:T(8,128)(2,1)S(1)} %get-tuple-element.52), channel_id=1, source_target_pairs={{0,1},{1,0},{2,3},{3,2},{4,5},{5,4},{6,7},{7,6},{8,9},{9,8},{10,11... | collective-permute-start | bytes 270344 | tf_op jit(solution)/shard_map/late_sums_in_chip/ppermute | solution.py:48
  51.2 11.7 %collective-permute-start.15 = (bf16[512,128]{1,0:T(8,128)(2,1)S(1)}, bf16[512,128]{1,0:T(8,128)(2,1)S(1)}, u32[]{:S(2)}, u32[]{:S(2)}) collective-permute-start(bf16[512,128]{1,0:T(8,128)(2,1)S(1)} %get-tuple-element.55), channel_id=1, source_target_pairs={{4,0},{0,4},{12,8},{8,12},{5,1},{1,5},{13,9},{9,13},{6,2},{2,6},{1... | collective-permute-start | bytes 393224 | tf_op jit(solution)/shard_map/late_sums_over_tm/ppermute | solution.py:669
  51.3 11.7 %collective-permute-start.17 = (bf16[320,128]{1,0:T(8,128)(2,1)S(1)}, bf16[320,128]{1,0:T(8,128)(2,1)S(1)}, u32[]{:S(2)}, u32[]{:S(2)}) collective-permute-start(bf16[320,128]{1,0:T(8,128)(2,1)S(1)} %get-tuple-element.57), channel_id=1, source_target_pairs={{12,0},{8,4},{4,8},{0,12},{13,1},{9,5},{5,9},{1,13},{14,2},{10,6},... | collective-permute-start | bytes 245768 | tf_op jit(solution)/shard_map/late_sums_over_tm/ppermute | solution.py:669
  53.7 9.3 %collective-permute-start.16 = (bf16[128,128]{1,0:T(8,128)(2,1)S(1)}, bf16[128,128]{1,0:T(8,128)(2,1)S(1)}, u32[]{:S(2)}, u32[]{:S(2)}) collective-permute-start(bf16[128,128]{1,0:T(8,128)(2,1)S(1)} %get-tuple-element.56), channel_id=1, source_target_pairs={{8,0},{12,4},{0,8},{4,12},{9,1},{13,5},{1,9},{5,13},{10,2},{14,6},... | collective-permute-start | bytes 98312 | tf_op jit(solution)/shard_map/low_over_tm/ppermute | solution.py:669
  54.8 9.8 %collective-permute-start.19 = (bf16[384,128]{1,0:T(8,128)(2,1)S(1)}, bf16[384,128]{1,0:T(8,128)(2,1)S(1)}, u32[]{:S(2)}, u32[]{:S(2)}) collective-permute-start(bf16[384,128]{1,0:T(8,128)(2,1)S(1)} %get-tuple-element.59), channel_id=1, source_target_pairs={{8,0},{12,4},{0,8},{4,12},{9,1},{13,5},{1,9},{5,13},{10,2},{14,6},... | collective-permute-start | bytes 294920 | tf_op jit(solution)/shard_map/late_gradients_over_tm/ppermute | solution.py:669
  63.0 4.3 %collective-permute-start.18 = (f32[128,128]{1,0:T(8,128)S(1)}, f32[128,128]{1,0:T(8,128)S(1)}, u32[]{:S(2)}, u32[]{:S(2)}) collective-permute-start(f32[128,128]{1,0:T(8,128)S(1)} %shard_map.128.low_ref), channel_id=1, source_target_pairs={{0,2},{2,0},{1,3},{3,1},{4,6},{6,4},{5,7},{7,5},{8,10},{10,8},{9,1... | collective-permute-start | bytes 196616 | tf_op jit(solution)/shard_map/low_over_head/ppermute | solution.py:48
  67.4 2.0 %collective-permute-start.20 = (bf16[2048,128]{1,0:T(8,128)(2,1)S(1)}, bf16[2048,128]{1,0:T(8,128)(2,1)S(1)}, u32[]{:S(2)}, u32[]{:S(2)}) collective-permute-start(bf16[2048,128]{1,0:T(8,128)(2,1)S(1)} %shard_map.129.tail), channel_id=1, source_target_pairs={{0,1},{1,0},{2,3},{3,2},{4,5},{5,4},{6,7},{7,6},{8,9},{9,8},{10,11... | collective-permute-start | bytes 1572872 | tf_op jit(solution)/shard_map/tail_in_chip/ppermute | solution.py:48

commit v13 on v10

--- a/solution.py
+++ b/solution.py
@@ -533,7 +533,7 @@
 
 
 def hand_out_kernel(frames, size, parts, keep_ref, *refs):
-    gots, (piece, facing), (own_ref, *sends, total) = refs[:parts], refs[parts : parts + 2], refs[parts + 2 :]
+    gots, facing, (own_ref, *sends, total) = refs[:parts], refs[parts], refs[-frames - 1 :]
     me = lax.axis_index("tm")
     rows = own_ref.shape[0]
     total[...] = keep_ref[...] + jnp.concatenate([got[...].astype(F32) for got in gots], axis=0)
@@ -544,26 +544,24 @@
         else:
             sends[m - 1][:rows, :] = low.astype(BF16)
             sends[m - 1][rows : rows + size, :] = total[:size, :].astype(BF16)
-    sends[0][rows + size : rows + 3 * size, :] = piece[...]
-    sends[0][rows + 3 * size :, :] = facing[size:, :]
-    sends[1][rows + size :, :] = piece[:size, :]
-
-
-def hand_out(frames, rows, keep, gots, piece, facing):
+    sends[0][rows + size :, :] = facing[...]
+
+
+def hand_out(frames, rows, keep, gots, facing, after):
     size, rank = keep.shape[0] - frames * rows, keep.shape[1]
     own, *sends = pl.pallas_call(
         functools.partial(hand_out_kernel, frames, size, len(gots)),
-        in_specs=vmem(3 + len(gots)),
+        in_specs=vmem(2 + len(gots)) + [pl.BlockSpec(memory_space=pl.ANY)] * len(after),
         out_specs=vmem(frames),
         out_shape=[jax.ShapeDtypeStruct((rows, rank), F32)]
-        + [jax.ShapeDtypeStruct((rows + size * n, rank), BF16) for n in (4, 2, 1)],
+        + [jax.ShapeDtypeStruct((rows + size * n, rank), BF16) for n in (3, 1, 1)],
         scratch_shapes=[pltpu.VMEM(keep.shape, F32)],
         compiler_params=SMALL,
-    )(keep, *gots, piece, facing)
+    )(keep, *gots, facing, *after)
     return own, sends
 
 
-def collect_kernel(wide, own_low, own, near, third, last, piece, facing, out_ref, low_ref):
+def collect_kernel(wide, own_low, own, near, third, last, piece, pair, far, facing, out_ref, low_ref):
     rows = own_low.shape[0]
     size = own.shape[0] - rows
     low = own_low[...]
@@ -577,25 +575,26 @@
         return ref[rows + n * size : rows + (n + 1) * size, :]
 
     blocks = [part(ref, 0) for ref in (own, near, third, last)]
-    blocks += [piece[:size, :], part(near, 1), part(third, 1), facing[:size, :]]
-    blocks.append(jnp.where(middle, piece[size:, :], part(near, 2)))
-    blocks.append(jnp.where(middle, facing[size:, :], part(near, 3)))
+    blocks += [piece[:size, :], pair[:size, :]]
+    blocks += [jnp.where(middle, far[...], part(near, 1)), facing[:size, :]]
+    blocks.append(jnp.where(middle, piece[size:, :], pair[size:, :]))
+    blocks.append(jnp.where(middle, facing[size:, :], part(near, 2)))
     for n, block in enumerate(blocks):
         out_ref[rows + n * size : rows + (n + 1) * size, :] = block
 
 
-def collect(wide, own_low, own, gots, piece, facing):
-    (rows, rank), size = own_low.shape, piece.shape[0] // 2
+def collect(wide, own_low, own, gots, *pieces):
+    (rows, rank), size = own_low.shape, pieces[0].shape[0] // 2
     return pl.pallas_call(
         functools.partial(collect_kernel, wide),
-        in_specs=vmem(4 + len(gots)),
+        in_specs=vmem(2 + len(gots) + len(pieces)),
         out_specs=vmem(2),
         out_shape=[
             jax.ShapeDtypeStruct((rows + 10 * size, rank), BF16),
             jax.ShapeDtypeStruct((rows, rank), BF16),
         ],
         compiler_params=SMALL,
-    )(own_low, own, *gots, piece, facing)
+    )(own_low, own, *gots, *pieces)
 
 
 def place_kernel(frames, lead, late, rest, tail, tail2, low_head, low_diag, *outs):
@@ -709,12 +708,16 @@
     got = swap_in_chip("early_gradients", give)
     piece = (keep + got.astype(F32)).astype(BF16)
     *late_side, _ = sides("late", 2, late_got, False, (3,), 0, [got])
+    cut = 3 * rank // 2
+    pair = meet("early_gradients", piece, 1)
     facing = meet("early_gradients", piece, 3)
+    with jax.named_scope("early_lead_over_tm"):
+        far = lax.ppermute(piece[:cut], "tm", [(0, 2), (3, 1)])
     keep, *gives = head_group([late], band_width, [t_side, late_side], adapters, low, [piece])
     gives = [swap_in_chip("late_sums", g) for g in gives]
-    own_low, sends = hand_out(frames, rows, keep, gives, piece, facing)
+    own_low, sends = hand_out(frames, rows, keep, gives, facing, [pair])
     gots = [meet("late_sums", block, m) for m, block in enumerate(sends, 1)]
-    tail, low = collect(rest[1], own_low, sends[2], gots, piece, facing)
+    tail, low = collect(rest[1], own_low, sends[2], gots, piece, pair, far, facing)
     diag = [(0, 3), (1, 2), (2, 1), (3, 0)]
     with jax.named_scope("low_over_head"):
         low_head, low_diag = swap(low, "head"), lax.ppermute(low, ("head", "rep"), diag)

time: 70.2 us -> 68.2 us (0.972)
  waiting for transfers between devices: 31.3 us -> 26.1 us
  starting transfers between devices: 25 us -> 28.1 us
    ppermute x11 -> x12, waiting for transfers between devices: 27.7 us -> 19.5 us  [meet(): return lax.ppermute(block, 'tm', [(j ^ m, j) for j in targets])]
    ppermute x0 -> x1, waiting for transfers between devices: none -> 3.54 us  [exchange_plan(): far = lax.ppermute(piece[:cut], 'tm', [(0, 2), (3, 1)])]
    ppermute x0 -> x1, starting transfers between devices: none -> 1.82 us  [exchange_plan(): far = lax.ppermute(piece[:cut], 'tm', [(0, 2), (3, 1)])]
    ppermute x11 -> x12, starting transfers between devices: 21.5 us -> 23.1 us  [meet(): return lax.ppermute(block, 'tm', [(j ^ m, j) for j in targets])]
    ppermute x1, starting transfers between devices: 1.61 us -> 0.31 us  [exchange_plan(): lax.ppermute(low, ('head', 'rep'), diag)]
    ppermute x8, starting transfers between devices: 1.94 us -> 2.95 us  [swap(): return lax.ppermute(block, axis, [(0, 1), (1, 0)])]
  transfers between devices with their start and end apart: 20 -> 22, of which waited for: 8 -> 8; matrix products, arithmetic and copies ran while one was open for 0% -> 0% of each run, Pallas kernels for 11% -> 12%
where the time goes in v13:
time: 68.2 us; the launch traced here: 68 us
  starting transfers between devices  28.1 us (41%)
  waiting for transfers between devices  26.1 us (38%)
  Pallas kernels  12.1 us (18%)
  between operations  0.91 us (1%)
  local copies, waits for them, and re-layouts  0.69 us (1%)
    ppermute x12, starting transfers between devices, meet(): return lax.ppermute(block, 'tm', [(j ^ m, j) for j in targets])  23.1 us
    ppermute x12, waiting for transfers between devices, meet(): return lax.ppermute(block, 'tm', [(j ^ m, j) for j in targets])  19.5 us
    pallas_call x2, Pallas kernels, head_group(): pl.pallas_call(functools.partial(group_kernel, heads, frames, chained, le...  6.88 us
    ppermute x1, waiting for transfers between devices, exchange_plan(): far = lax.ppermute(piece[:cut], 'tm', [(0, 2), (3, 1)])  3.54 us
    pallas_call x2, Pallas kernels, pack(): pl.pallas_call(functools.partial(pack_kernel, frames, outputs), in_specs=...  3.51 us
    ppermute x8, starting transfers between devices, swap(): return lax.ppermute(block, axis, [(0, 1), (1, 0)])  2.95 us
    ppermute x8, waiting for transfers between devices, swap(): return lax.ppermute(block, axis, [(0, 1), (1, 0)])  2.14 us
    ppermute x1, starting transfers between devices, exchange_plan(): far = lax.ppermute(piece[:cut], 'tm', [(0, 2), (3, 1)])  1.82 us
  transfers between devices with their start and end apart: 22, of which 8 were waited for; matrix products, arithmetic and copies ran while one was open for 0% of the time, Pallas kernels for 12%

profile of v13, /device:TPU:0, one launch (start us, length us, event | category | flops | bytes accessed | tf_op | source)
XLA Modules:
  0.0 68.0 jit_solution(7613407943474921803)
XLA Ops:
  0.7 2.6 %shard_map.121 = (bf16[128,1664]{1,0:T(8,128)(2,1)}, bf16[128,640]{1,0:T(8,128)(2,1)}, bf16[128,512]{1,0:T(8,128)(2,1)}, bf16[128,640]{1,0:T(8,128)(2,1)}, bf16[128,512]{1,0:T(8,128)(2,1)}) custom-call(bf16[128,1280]{1,0:T(8,128)(2,1)} %fq_ref.3, bf16[128,1280]{1,0:T(8,128)(2,1)} %do_ref.3, bf16[256,1280]{1,0:T(8,128)(2,1)} %fk_ref.3, ...), custom_call_target="tpu_custom_call" | custom-call | tf_op jit(solution)/shard_map/pallas_call | solution.py:301
  3.3 3.1 %collective-permute-start = (bf16[128,1664]{1,0:T(8,128)(2,1)}, bf16[128,1664]{1,0:T(8,128)(2,1)S(1)}, u32[]{:S(2)}, u32[]{:S(2)}) collective-permute-start(bf16[128,1664]{1,0:T(8,128)(2,1)} %get-tuple-element.33), channel_id=1, source_target_pairs={{4,0},{0,4},{12,8},{8,12},{5,1},{1,5},{13,9},{9,13},{6,2},{2,6},{1... | collective-permute-start | bytes 1277960 | tf_op jit(solution)/shard_map/nearest_over_tm/ppermute | solution.py:660
  6.3 2.6 %collective-permute-start.1 = (bf16[128,640]{1,0:T(8,128)(2,1)}, bf16[128,640]{1,0:T(8,128)(2,1)S(1)}, u32[]{:S(2)}, u32[]{:S(2)}) collective-permute-start(bf16[128,640]{1,0:T(8,128)(2,1)} %get-tuple-element.34), channel_id=1, source_target_pairs={{8,0},{12,4},{0,8},{4,12},{9,1},{13,5},{1,9},{5,13},{10,2},{14,6},... | collective-permute-start | bytes 491528 | tf_op jit(solution)/shard_map/lead_over_tm/ppermute | solution.py:660
  8.9 3.8 %collective-permute-start.6 = (bf16[128,512]{1,0:T(8,128)(2,1)}, bf16[128,512]{1,0:T(8,128)(2,1)S(1)}, u32[]{:S(2)}, u32[]{:S(2)}) collective-permute-start(bf16[128,512]{1,0:T(8,128)(2,1)} %get-tuple-element.44), channel_id=1, source_target_pairs={{12,4},{0,8},{13,5},{1,9},{14,6},{2,10},{15,7},{3,11},{28,20},{16,... | collective-permute-start | bytes 393224 | tf_op jit(solution)/shard_map/rest_over_tm/ppermute | solution.py:660
  12.8 0.7 collective-permute-start.7
  13.5 0.9 %shard_map.120 = (bf16[128,512]{1,0:T(8,128)(2,1)S(1)}, bf16[128,512]{1,0:T(8,128)(2,1)S(1)}, bf16[128,512]{1,0:T(8,128)(2,1)S(1)}, bf16[128,256]{1,0:T(8,128)(2...) custom-call(bf16[128,1280]{1,0:T(8,128)(2,1)S(1)} %copy-done.2, ...), custom_call_target="tpu_custom_call" | custom-call | tf_op jit(solution)/shard_map/pallas_call | solution.py:301
  14.4 6.0 %collective-permute-done.1.refs_1_.refs_3_ = bf16[128,640]{1,0:T(8,128)(2,1)S(1)} collective-permute-done((bf16[128,640]{1,0:T(8,128)(2,1)}, bf16[128,640]{1,0:T(8,128)(2,1)S(1)}, u32[]{:S(2)}, u32[]{:S(2)}) %collective-permute-start.1) | collective-permute-done | bytes 163872 | tf_op jit(solution)/shard_map/lead_over_tm/ppermute | solution.py:660
  20.4 6.4 %collective-permute-done.2.refs_2_.refs_4_ = bf16[128,640]{1,0:T(8,128)(2,1)S(1)} collective-permute-done((bf16[128,640]{1,0:T(8,128)(2,1)}, bf16[128,640]{1,0:T(8,128)(2,1)S(1)}, u32[]{:S(2)}, u32[]{:S(2)}) %collective-permute-start.2) | collective-permute-done | bytes 163872 | tf_op jit(solution)/shard_map/lead_over_tm/ppermute | solution.py:660
  26.9 0.1 collective-permute-start.3
  27.0 0.5 collective-permute-start.8
  27.6 3.5 %collective-permute-start.4 = (bf16[128,512]{1,0:T(8,128)(2,1)S(1)}, bf16[128,512]{1,0:T(8,128)(2,1)S(1)}, u32[]{:S(2)}, u32[]{:S(2)}) collective-permute-start(bf16[128,512]{1,0:T(8,128)(2,1)S(1)} %get-tuple-element.39), channel_id=1, source_target_pairs={{8,0},{12,4},{0,8},{4,12},{9,1},{13,5},{1,9},{5,13},{10,2},{14,6},... | collective-permute-start | bytes 393224 | tf_op jit(solution)/shard_map/late_over_tm/ppermute | solution.py:660
  31.0 1.4 %collective-permute-start.5 = (bf16[128,512]{1,0:T(8,128)(2,1)S(1)}, bf16[128,512]{1,0:T(8,128)(2,1)S(1)}, u32[]{:S(2)}, u32[]{:S(2)}) collective-permute-start(bf16[128,512]{1,0:T(8,128)(2,1)S(1)} %get-tuple-element.40), channel_id=1, source_target_pairs={{12,0},{8,4},{4,8},{0,12},{13,1},{9,5},{5,9},{1,13},{14,2},{10,6},... | collective-permute-start | bytes 393224 | tf_op jit(solution)/shard_map/late_over_tm/ppermute | solution.py:660
  32.4 0.6 copy-done.8
  33.1 3.4 %shard_map.124 = (f32[384,128]{1,0:T(8,128)S(1)}, bf16[384,128]{1,0:T(8,128)(2,1)S(1)}, f32[512,128]{1,0:T(8,128)S(1)}, f32[512,128]{1,0:T(8,128)S(1)}) custom-call(s32[4,4]{1,0:T(4,128)S(1)} %copy-done.8, bf16[128,128]{1,0:T(8,128)(2,1)S(1)} %get-tuple-element.32.refs_1_, bf16[128,1664]{1,0:T(8,128)(2,1)S(1)} %collective-permute-done.refs_0_.refs_2_, ...), custom_call_target="tpu_custom_call" | custom-call | tf_op jit(solution)/shard_map/pallas_call | solution.py:521
  36.6 4.4 %collective-permute-done.4.refs_1_.refs_8_ = bf16[128,512]{1,0:T(8,128)(2,1)S(1)} collective-permute-done((bf16[128,512]{1,0:T(8,128)(2,1)S(1)}, bf16[128,512]{1,0:T(8,128)(2,1)S(1)}, u32[]{:S(2)}, u32[]{:S(2)}) %collective-permute-start.4) | collective-permute-done | bytes 131104 | tf_op jit(solution)/shard_map/late_over_tm/ppermute | solution.py:660
  41.1 0.1 collective-permute-start.10
  41.2 1.4 %collective-permute-start.13 = (bf16[384,128]{1,0:T(8,128)(2,1)S(1)}, bf16[384,128]{1,0:T(8,128)(2,1)S(1)}, u32[]{:S(2)}, u32[]{:S(2)}) collective-permute-start(bf16[384,128]{1,0:T(8,128)(2,1)S(1)} %add_convert_fusion.refs_17_.piece), channel_id=1, source_target_pairs={{12,0},{8,4},{4,8},{0,12},{13,1},{9,5},{5,9},{1,13},{14,2},{10,6},... | collective-permute-start | bytes 294920 | tf_op jit(solution)/shard_map/early_gradients_over_tm/ppermute | solution.py:660
  42.6 2.2 %collective-permute-start.14 = (bf16[384,128]{1,0:T(8,128)(2,1)S(1)}, bf16[384,128]{1,0:T(8,128)(2,1)S(1)}, u32[]{:S(2)}, u32[]{:S(2)}) collective-permute-start(bf16[384,128]{1,0:T(8,128)(2,1)S(1)} %add_convert_fusion.refs_17_.piece), channel_id=1, source_target_pairs={{4,0},{0,4},{12,8},{8,12},{5,1},{1,5},{13,9},{9,13},{6,2},{2,6},{1... | collective-permute-start | bytes 294920 | tf_op jit(solution)/shard_map/early_gradients_over_tm/ppermute | solution.py:660
  44.8 3.4 %shard_map.126 = (f32[704,128]{1,0:T(8,128)S(1)}, bf16[352,128]{1,0:T(8,128)(2,1)S(1)}, bf16[352,128]{1,0:T(8,128)(2,1)S(1)}) custom-call(s32[4,4]{1,0:T(4,128)S(1)} %copy-done.8, bf16[128,128]{1,0:T(8,128)(2,1)S(1)} %get-tuple-element.32.refs_1_, bf16[128,1664]{1,0:T(8,128)(2,1)S(1)} %collective-permute-done.refs_0_.refs_2_, ...), custom_call_target="tpu_custom_call" | custom-call | tf_op jit(solution)/shard_map/pallas_call | solution.py:521
  48.3 0.5 collective-permute-start.12
  48.8 1.3 %collective-permute-done.14.refs_3_.pair = bf16[384,128]{1,0:T(8,128)(2,1)S(1)} collective-permute-done((bf16[384,128]{1,0:T(8,128)(2,1)S(1)}, bf16[384,128]{1,0:T(8,128)(2,1)S(1)}, u32[]{:S(2)}, u32[]{:S(2)}) %collective-permute-start.14) | collective-permute-done | bytes 98336 | tf_op jit(solution)/shard_map/early_gradients_over_tm/ppermute | solution.py:660
  50.2 0.9 %collective-permute-start.15 = (bf16[704,128]{1,0:T(8,128)(2,1)S(1)}, bf16[704,128]{1,0:T(8,128)(2,1)S(1)}, u32[]{:S(2)}, u32[]{:S(2)}) collective-permute-start(bf16[704,128]{1,0:T(8,128)(2,1)S(1)} %get-tuple-element.56), channel_id=1, source_target_pairs={{4,0},{0,4},{12,8},{8,12},{5,1},{1,5},{13,9},{9,13},{6,2},{2,6},{1... | collective-permute-start | bytes 540680 | tf_op jit(solution)/shard_map/late_sums_over_tm/ppermute | solution.py:660
  51.1 1.9 %collective-permute-start.16 = (bf16[320,128]{1,0:T(8,128)(2,1)S(1)}, bf16[320,128]{1,0:T(8,128)(2,1)S(1)}, u32[]{:S(2)}, u32[]{:S(2)}) collective-permute-start(bf16[320,128]{1,0:T(8,128)(2,1)S(1)} %get-tuple-element.57), channel_id=1, source_target_pairs={{8,0},{12,4},{0,8},{4,12},{9,1},{13,5},{1,9},{5,13},{10,2},{14,6},... | collective-permute-start | bytes 245768 | tf_op jit(solution)/shard_map/late_sums_over_tm/ppermute | solution.py:660
  52.9 1.7 %collective-permute-start.17 = (bf16[320,128]{1,0:T(8,128)(2,1)S(1)}, bf16[320,128]{1,0:T(8,128)(2,1)S(1)}, u32[]{:S(2)}, u32[]{:S(2)}) collective-permute-start(bf16[320,128]{1,0:T(8,128)(2,1)S(1)} %get-tuple-element.55.own), channel_id=1, source_target_pairs={{12,0},{8,4},{4,8},{0,12},{13,1},{9,5},{5,9},{1,13},{14,2},{10,6},... | collective-permute-start | bytes 245768 | tf_op jit(solution)/shard_map/late_sums_over_tm/ppermute | solution.py:660
  54.6 1.8 %collective-permute-start.18 = (bf16[192,128]{1,0:T(8,128)(2,1)S(1)}, bf16[192,128]{1,0:T(8,128)(2,1)S(1)}, u32[]{:S(2)}, u32[]{:S(2)}) collective-permute-start(bf16[192,128]{1,0:T(8,128)(2,1)S(1)} %slice.4), channel_id=1, source_target_pairs={{0,8},{12,4},{1,9},{13,5},{2,10},{14,6},{3,11},{15,7},{16,24},{28,... | collective-permute-start | bytes 147464 | tf_op jit(solution)/shard_map/early_lead_over_tm/ppermute | solution.py:715
  56.4 3.5 %collective-permute-done.18.far = bf16[192,128]{1,0:T(8,128)(2,1)S(1)} collective-permute-done((bf16[192,128]{1,0:T(8,128)(2,1)S(1)}, bf16[192,128]{1,0:T(8,128)(2,1)S(1)}, u32[]{:S(2)}, u32[]{:S(2)}) %collective-permute-start.18) | collective-permute-done | bytes 49184 | tf_op jit(solution)/shard_map/early_lead_over_tm/ppermute | solution.py:715
  60.0 1.5 %collective-permute-done.17.last = bf16[320,128]{1,0:T(8,128)(2,1)S(1)} collective-permute-done((bf16[320,128]{1,0:T(8,128)(2,1)S(1)}, bf16[320,128]{1,0:T(8,128)(2,1)S(1)}, u32[]{:S(2)}, u32[]{:S(2)}) %collective-permute-start.17) | collective-permute-done | bytes 81952 | tf_op jit(solution)/shard_map/late_sums_over_tm/ppermute | solution.py:660
  61.6 1.6 %collective-permute-start.20 = (bf16[128,128]{1,0:T(8,128)(2,1)S(1)}, bf16[128,128]{1,0:T(8,128)(2,1)S(1)}, u32[]{:S(2)}, u32[]{:S(2)}) collective-permute-start(bf16[128,128]{1,0:T(8,128)(2,1)S(1)} %get-tuple-element.59), channel_id=1, source_target_pairs={{0,2},{2,0},{1,3},{3,1},{4,6},{6,4},{5,7},{7,5},{8,10},{10,8},{9,1... | collective-permute-start | bytes 98312 | tf_op jit(solution)/shard_map/low_over_head/ppermute | solution.py:48
  63.1 0.3 collective-permute-start.21
  63.5 2.1 %collective-permute-done.20.low_head = bf16[128,128]{1,0:T(8,128)(2,1)S(1)} collective-permute-done((bf16[128,128]{1,0:T(8,128)(2,1)S(1)}, bf16[128,128]{1,0:T(8,128)(2,1)S(1)}, u32[]{:S(2)}, u32[]{:S(2)}) %collective-permute-start.20) | collective-permute-done | bytes 32800 | tf_op jit(solution)/shard_map/low_over_head/ppermute | solution.py:48
  65.6 0.9 %collective-permute-done.21.low_diag = bf16[128,128]{1,0:T(8,128)(2,1)S(1)} collective-permute-done((bf16[128,128]{1,0:T(8,128)(2,1)S(1)}, bf16[128,128]{1,0:T(8,128)(2,1)S(1)}, u32[]{:S(2)}, u32[]{:S(2)}) %collective-permute-start.21) | collective-permute-done | bytes 32800 | tf_op jit(solution)/shard_map/low_over_head/ppermute | solution.py:723
  66.5 1.5 %shard_map.129 = (f32[128,1280]{1,0:T(8,128)}, f32[128,1280]{1,0:T(8,128)}, f32[128,1280]{1,0:T(8,128)}, f32[256,128]{1,0:T(8,128)}) custom-call(bf16[2048,128]{1,0:T(8,128)(2,1)S(1)} %get-tuple-element.58.tail, bf16[2048,128]{1,0:T(8,128)(2,1)S(1)} %collective-permute-done.19.tail2, bf16[128,128]{1,0:T(8,128)(2,1)S(1)} %collective-permute-done.20.low_head, ...), custom_call_target="tpu_custom_call" | custom-call | tf_op jit(solution)/shard_map/pallas_call | solution.py:623
  (42 shorter events, 0.5 us)
Async XLA Ops:
  0.6 12.8 %copy-start.2 = (bf16[128,1280]{1,0:T(8,128)(2,1)S(1)}, bf16[128,1280]{1,0:T(8,128)(2,1)}, u32[]{:S(2)}) copy-start(bf16[128,1280]{1,0:T(8,128)(2,1)} %fq_ref.3) | copy-start | bytes 983044
  0.6 12.8 %copy-start.3 = (bf16[128,1280]{1,0:T(8,128)(2,1)S(1)}, bf16[128,1280]{1,0:T(8,128)(2,1)}, u32[]{:S(2)}) copy-start(bf16[128,1280]{1,0:T(8,128)(2,1)} %do_ref.3) | copy-start | bytes 983044
  0.7 12.8 %copy-start = (bf16[256,1280]{1,0:T(8,128)(2,1)S(1)}, bf16[256,1280]{1,0:T(8,128)(2,1)}, u32[]{:S(2)}) copy-start(bf16[256,1280]{1,0:T(8,128)(2,1)} %fk_ref.3) | copy-start | bytes 1966084
  0.7 12.8 %copy-start.1 = (bf16[256,1280]{1,0:T(8,128)(2,1)S(1)}, bf16[256,1280]{1,0:T(8,128)(2,1)}, u32[]{:S(2)}) copy-start(bf16[256,1280]{1,0:T(8,128)(2,1)} %fv_ref.3) | copy-start | bytes 1966084
  0.7 12.8 %copy-start.7 = (bf16[256,128]{1,0:T(8,128)(2,1)S(1)}, bf16[256,128]{1,0:T(8,128)(2,1)}, u32[]{:S(2)}) copy-start(bf16[256,128]{1,0:T(8,128)(2,1)} %t_ref.3) | copy-start | bytes 196612
  3.3 23.6 %collective-permute-start = (bf16[128,1664]{1,0:T(8,128)(2,1)}, bf16[128,1664]{1,0:T(8,128)(2,1)S(1)}, u32[]{:S(2)}, u32[]{:S(2)}) collective-permute-start(bf16[128,1664]{1,0:T(8,128)(2,1)} %get-tuple-element.33), channel_id=1, source_target_pairs={{4,0},{0,4},{12,8},{8,12},{5,1},{1,5},{13,9},{9,13},{6,2},{2,6},{1... | collective-permute-start | bytes 1277960 | tf_op jit(solution)/shard_map/nearest_over_tm/ppermute | solution.py:660
  6.3 14.1 %collective-permute-start.1 = (bf16[128,640]{1,0:T(8,128)(2,1)}, bf16[128,640]{1,0:T(8,128)(2,1)S(1)}, u32[]{:S(2)}, u32[]{:S(2)}) collective-permute-start(bf16[128,640]{1,0:T(8,128)(2,1)} %get-tuple-element.34), channel_id=1, source_target_pairs={{8,0},{12,4},{0,8},{4,12},{9,1},{13,5},{1,9},{5,13},{10,2},{14,6},... | collective-permute-start | bytes 491528 | tf_op jit(solution)/shard_map/lead_over_tm/ppermute | solution.py:660
  8.9 17.9 %collective-permute-start.2 = (bf16[128,640]{1,0:T(8,128)(2,1)}, bf16[128,640]{1,0:T(8,128)(2,1)S(1)}, u32[]{:S(2)}, u32[]{:S(2)}) collective-permute-start(bf16[128,640]{1,0:T(8,128)(2,1)} %get-tuple-element.35), channel_id=1, source_target_pairs={{12,0},{8,4},{4,8},{0,12},{13,1},{9,5},{5,9},{1,13},{14,2},{10,6},... | collective-permute-start | bytes 491528 | tf_op jit(solution)/shard_map/lead_over_tm/ppermute | solution.py:660
  8.9 18.0 %collective-permute-start.6 = (bf16[128,512]{1,0:T(8,128)(2,1)}, bf16[128,512]{1,0:T(8,128)(2,1)S(1)}, u32[]{:S(2)}, u32[]{:S(2)}) collective-permute-start(bf16[128,512]{1,0:T(8,128)(2,1)} %get-tuple-element.44), channel_id=1, source_target_pairs={{12,4},{0,8},{13,5},{1,9},{14,6},{2,10},{15,7},{3,11},{28,20},{16,... | collective-permute-start | bytes 393224 | tf_op jit(solution)/shard_map/rest_over_tm/ppermute | solution.py:660
  12.8 14.2 %collective-permute-start.7 = (bf16[128,512]{1,0:T(8,128)(2,1)}, bf16[128,512]{1,0:T(8,128)(2,1)S(1)}, u32[]{:S(2)}, u32[]{:S(2)}) collective-permute-start(bf16[128,512]{1,0:T(8,128)(2,1)} %get-tuple-element.45), channel_id=1, source_target_pairs={{8,4},{4,8},{9,5},{5,9},{10,6},{6,10},{11,7},{7,11},{24,20},{20,24... | collective-permute-start | bytes 393224 | tf_op jit(solution)/shard_map/rest_over_tm/ppermute | solution.py:660
  26.8 5.6 %copy-start.6 = (bf16[128,1280]{1,0:T(8,128)(2,1)S(1)}, bf16[128,1280]{1,0:T(8,128)(2,1)}, u32[]{:S(2)}) copy-start(bf16[128,1280]{1,0:T(8,128)(2,1)} %refs_14_.3) | copy-start | bytes 983044
  26.9 5.6 %copy-start.4 = (bf16[128,1280]{1,0:T(8,128)(2,1)S(1)}, bf16[128,1280]{1,0:T(8,128)(2,1)}, u32[]{:S(2)}) copy-start(bf16[128,1280]{1,0:T(8,128)(2,1)} %refs_12_.1) | copy-start | bytes 983044
  26.9 5.6 %copy-start.5 = (bf16[128,1280]{1,0:T(8,128)(2,1)S(1)}, bf16[128,1280]{1,0:T(8,128)(2,1)}, u32[]{:S(2)}) copy-start(bf16[128,1280]{1,0:T(8,128)(2,1)} %refs_13_.1) | copy-start | bytes 983044
  26.9 5.5 %collective-permute-start.3 = (bf16[128,1152]{1,0:T(8,128)(2,1)S(1)}, bf16[128,1152]{1,0:T(8,128)(2,1)S(1)}, u32[]{:S(2)}, u32[]{:S(2)}) collective-permute-start(bf16[128,1152]{1,0:T(8,128)(2,1)S(1)} %shard_map.122), channel_id=1, source_target_pairs={{0,1},{1,0},{2,3},{3,2},{4,5},{5,4},{6,7},{7,6},{8,9},{9,8},{10,11... | collective-permute-start | bytes 884744 | tf_op jit(solution)/shard_map/lead_in_chip/ppermute | solution.py:48
  27.0 5.4 %collective-permute-start.8 = (bf16[128,768]{1,0:T(8,128)(2,1)S(1)}, bf16[128,768]{1,0:T(8,128)(2,1)S(1)}, u32[]{:S(2)}, u32[]{:S(2)}) collective-permute-start(bf16[128,768]{1,0:T(8,128)(2,1)S(1)} %shard_map.123), channel_id=1, source_target_pairs={{0,1},{1,0},{2,3},{3,2},{4,5},{5,4},{6,7},{7,6},{8,9},{9,8},{10,11... | collective-permute-start | bytes 589832 | tf_op jit(solution)/shard_map/rest_in_chip/ppermute | solution.py:48
  27.6 13.5 %collective-permute-start.4 = (bf16[128,512]{1,0:T(8,128)(2,1)S(1)}, bf16[128,512]{1,0:T(8,128)(2,1)S(1)}, u32[]{:S(2)}, u32[]{:S(2)}) collective-permute-start(bf16[128,512]{1,0:T(8,128)(2,1)S(1)} %get-tuple-element.39), channel_id=1, source_target_pairs={{8,0},{12,4},{0,8},{4,12},{9,1},{13,5},{1,9},{5,13},{10,2},{14,6},... | collective-permute-start | bytes 393224 | tf_op jit(solution)/shard_map/late_over_tm/ppermute | solution.py:660
  31.0 10.0 %collective-permute-start.5 = (bf16[128,512]{1,0:T(8,128)(2,1)S(1)}, bf16[128,512]{1,0:T(8,128)(2,1)S(1)}, u32[]{:S(2)}, u32[]{:S(2)}) collective-permute-start(bf16[128,512]{1,0:T(8,128)(2,1)S(1)} %get-tuple-element.40), channel_id=1, source_target_pairs={{12,0},{8,4},{4,8},{0,12},{13,1},{9,5},{5,9},{1,13},{14,2},{10,6},... | collective-permute-start | bytes 393224 | tf_op jit(solution)/shard_map/late_over_tm/ppermute | solution.py:660
  32.4 0.7 %copy-start.8 = (s32[4,4]{1,0:T(4,128)S(1)}, s32[4,4]{1,0:T(4,128)}, u32[]{:S(2)}) copy-start(s32[4,4]{1,0:T(4,128)} %refs_0_.3) | copy-start | bytes 196
  36.5 4.5 %collective-permute-start.9 = (bf16[384,128]{1,0:T(8,128)(2,1)S(1)}, bf16[384,128]{1,0:T(8,128)(2,1)S(1)}, u32[]{:S(2)}, u32[]{:S(2)}) collective-permute-start(bf16[384,128]{1,0:T(8,128)(2,1)S(1)} %get-tuple-element.47), channel_id=1, source_target_pairs={{0,1},{1,0},{2,3},{3,2},{4,5},{5,4},{6,7},{7,6},{8,9},{9,8},{10,11... | collective-permute-start | bytes 294920 | tf_op jit(solution)/shard_map/early_gradients_in_chip/ppermute | solution.py:48
  41.1 3.7 %collective-permute-start.10 = (bf16[128,1536]{1,0:T(8,128)(2,1)S(1)}, bf16[128,1536]{1,0:T(8,128)(2,1)S(1)}, u32[]{:S(2)}, u32[]{:S(2)}) collective-permute-start(bf16[128,1536]{1,0:T(8,128)(2,1)S(1)} %shard_map.125), channel_id=1, source_target_pairs={{0,1},{1,0},{2,3},{3,2},{4,5},{5,4},{6,7},{7,6},{8,9},{9,8},{10,11... | collective-permute-start | bytes 1179656 | tf_op jit(solution)/shard_map/late_in_chip/ppermute | solution.py:48
  41.2 7.6 %collective-permute-start.13 = (bf16[384,128]{1,0:T(8,128)(2,1)S(1)}, bf16[384,128]{1,0:T(8,128)(2,1)S(1)}, u32[]{:S(2)}, u32[]{:S(2)}) collective-permute-start(bf16[384,128]{1,0:T(8,128)(2,1)S(1)} %add_convert_fusion.refs_17_.piece), channel_id=1, source_target_pairs={{12,0},{8,4},{4,8},{0,12},{13,1},{9,5},{5,9},{1,13},{14,2},{10,6},... | collective-permute-start | bytes 294920 | tf_op jit(solution)/shard_map/early_gradients_over_tm/ppermute | solution.py:660
  42.6 7.5 %collective-permute-start.14 = (bf16[384,128]{1,0:T(8,128)(2,1)S(1)}, bf16[384,128]{1,0:T(8,128)(2,1)S(1)}, u32[]{:S(2)}, u32[]{:S(2)}) collective-permute-start(bf16[384,128]{1,0:T(8,128)(2,1)S(1)} %add_convert_fusion.refs_17_.piece), channel_id=1, source_target_pairs={{4,0},{0,4},{12,8},{8,12},{5,1},{1,5},{13,9},{9,13},{6,2},{2,6},{1... | collective-permute-start | bytes 294920 | tf_op jit(solution)/shard_map/early_gradients_over_tm/ppermute | solution.py:660
  48.2 1.8 %collective-permute-start.11 = (bf16[352,128]{1,0:T(8,128)(2,1)S(1)}, bf16[352,128]{1,0:T(8,128)(2,1)S(1)}, u32[]{:S(2)}, u32[]{:S(2)}) collective-permute-start(bf16[352,128]{1,0:T(8,128)(2,1)S(1)} %get-tuple-element.52), channel_id=1, source_target_pairs={{0,1},{1,0},{2,3},{3,2},{4,5},{5,4},{6,7},{7,6},{8,9},{9,8},{10,11... | collective-permute-start | bytes 270344 | tf_op jit(solution)/shard_map/late_sums_in_chip/ppermute | solution.py:48
  48.3 1.8 %collective-permute-start.12 = (bf16[352,128]{1,0:T(8,128)(2,1)S(1)}, bf16[352,128]{1,0:T(8,128)(2,1)S(1)}, u32[]{:S(2)}, u32[]{:S(2)}) collective-permute-start(bf16[352,128]{1,0:T(8,128)(2,1)S(1)} %get-tuple-element.53), channel_id=1, source_target_pairs={{0,1},{1,0},{2,3},{3,2},{4,5},{5,4},{6,7},{7,6},{8,9},{9,8},{10,11... | collective-permute-start | bytes 270344 | tf_op jit(solution)/shard_map/late_sums_in_chip/ppermute | solution.py:48
  50.2 11.3 %collective-permute-start.15 = (bf16[704,128]{1,0:T(8,128)(2,1)S(1)}, bf16[704,128]{1,0:T(8,128)(2,1)S(1)}, u32[]{:S(2)}, u32[]{:S(2)}) collective-permute-start(bf16[704,128]{1,0:T(8,128)(2,1)S(1)} %get-tuple-element.56), channel_id=1, source_target_pairs={{4,0},{0,4},{12,8},{8,12},{5,1},{1,5},{13,9},{9,13},{6,2},{2,6},{1... | collective-permute-start | bytes 540680 | tf_op jit(solution)/shard_map/late_sums_over_tm/ppermute | solution.py:660
  51.1 8.9 %collective-permute-start.16 = (bf16[320,128]{1,0:T(8,128)(2,1)S(1)}, bf16[320,128]{1,0:T(8,128)(2,1)S(1)}, u32[]{:S(2)}, u32[]{:S(2)}) collective-permute-start(bf16[320,128]{1,0:T(8,128)(2,1)S(1)} %get-tuple-element.57), channel_id=1, source_target_pairs={{8,0},{12,4},{0,8},{4,12},{9,1},{13,5},{1,9},{5,13},{10,2},{14,6},... | collective-permute-start | bytes 245768 | tf_op jit(solution)/shard_map/late_sums_over_tm/ppermute | solution.py:660
  52.9 8.5 %collective-permute-start.17 = (bf16[320,128]{1,0:T(8,128)(2,1)S(1)}, bf16[320,128]{1,0:T(8,128)(2,1)S(1)}, u32[]{:S(2)}, u32[]{:S(2)}) collective-permute-start(bf16[320,128]{1,0:T(8,128)(2,1)S(1)} %get-tuple-element.55.own), channel_id=1, source_target_pairs={{12,0},{8,4},{4,8},{0,12},{13,1},{9,5},{5,9},{1,13},{14,2},{10,6},... | collective-permute-start | bytes 245768 | tf_op jit(solution)/shard_map/late_sums_over_tm/ppermute | solution.py:660
  54.6 5.4 %collective-permute-start.18 = (bf16[192,128]{1,0:T(8,128)(2,1)S(1)}, bf16[192,128]{1,0:T(8,128)(2,1)S(1)}, u32[]{:S(2)}, u32[]{:S(2)}) collective-permute-start(bf16[192,128]{1,0:T(8,128)(2,1)S(1)} %slice.4), channel_id=1, source_target_pairs={{0,8},{12,4},{1,9},{13,5},{2,10},{14,6},{3,11},{15,7},{16,24},{28,... | collective-permute-start | bytes 147464 | tf_op jit(solution)/shard_map/early_lead_over_tm/ppermute | solution.py:715
  61.5 5.0 %collective-permute-start.19 = (bf16[2048,128]{1,0:T(8,128)(2,1)S(1)}, bf16[2048,128]{1,0:T(8,128)(2,1)S(1)}, u32[]{:S(2)}, u32[]{:S(2)}) collective-permute-start(bf16[2048,128]{1,0:T(8,128)(2,1)S(1)} %get-tuple-element.58.tail), channel_id=1, source_target_pairs={{0,1},{1,0},{2,3},{3,2},{4,5},{5,4},{6,7},{7,6},{8,9},{9,8},{10,11... | collective-permute-start | bytes 1572872 | tf_op jit(solution)/shard_map/tail_in_chip/ppermute | solution.py:48
  61.6 4.0 %collective-permute-start.20 = (bf16[128,128]{1,0:T(8,128)(2,1)S(1)}, bf16[128,128]{1,0:T(8,128)(2,1)S(1)}, u32[]{:S(2)}, u32[]{:S(2)}) collective-permute-start(bf16[128,128]{1,0:T(8,128)(2,1)S(1)} %get-tuple-element.59), channel_id=1, source_target_pairs={{0,2},{2,0},{1,3},{3,1},{4,6},{6,4},{5,7},{7,5},{8,10},{10,8},{9,1... | collective-permute-start | bytes 98312 | tf_op jit(solution)/shard_map/low_over_head/ppermute | solution.py:48
  63.1 3.3 %collective-permute-start.21 = (bf16[128,128]{1,0:T(8,128)(2,1)S(1)}, bf16[128,128]{1,0:T(8,128)(2,1)S(1)}, u32[]{:S(2)}, u32[]{:S(2)}) collective-permute-start(bf16[128,128]{1,0:T(8,128)(2,1)S(1)} %get-tuple-element.59), channel_id=1, source_target_pairs={{0,3},{1,2},{2,1},{3,0},{4,7},{5,6},{6,5},{7,4},{8,11},{9,10},{10,... | collective-permute-start | bytes 98312 | tf_op jit(solution)/shard_map/low_over_head/ppermute | solution.py:723

commit v14 on v13

--- a/solution.py
+++ b/solution.py
@@ -1,4 +1,5 @@
 import functools
+import math
 
 import jax
 import jax.numpy as jnp
@@ -11,6 +12,7 @@
 NEAR = 1
 REACH = 4
 SCALE = DH ** (-0.5)
+SCALE_2 = SCALE * math.log2(math.e)
 F32 = jnp.float32
 BF16 = jnp.bfloat16
 GIVES = 2
@@ -373,11 +375,11 @@
 
     def softmax(g, raw):
         scores = [
-            block(raw, n) * SCALE + jnp.concatenate([bias(i, b) for i in groups[g]], axis=1)
+            block(raw, n) * SCALE_2 + jnp.concatenate([bias(i, b) for i in groups[g]], axis=1)
             for n, b in enumerate(seen[g])
         ]
         top = jnp.max(functools.reduce(jnp.maximum, scores), axis=0, keepdims=True)
-        shifted = [jnp.exp(s - top) for s in scores]
+        shifted = [jnp.exp2(s - top) for s in scores]
         inverse = 1.0 / jnp.sum(functools.reduce(jnp.add, shifted), axis=0, keepdims=True)
         return [s * inverse for s in shifted]
 
@@ -597,35 +599,49 @@
     )(own_low, own, *gots, *pieces)
 
 
-def place_kernel(frames, lead, late, rest, tail, tail2, low_head, low_diag, *outs):
+def place_kernel(frames, lead, late, rest, tail, tail2, low_head, low_diag, *refs):
+    outs, filled, sems = refs[:4], refs[4:8], refs[8]
     me, half = lax.axis_index("tm"), lax.axis_index("rep")
     first = half == 0
-    rank = outs[0].shape[0]
+    rank = filled[0].shape[0]
     cut = 3 * rank // 2
     rows = low_head.shape[0]
-    same = tail[:rows, :].astype(F32) + low_head[...].astype(F32)
-    other = tail2[:rows, :].astype(F32) + low_diag[...].astype(F32)
-    outs[3][:rows, :] = jnp.where(first, same, other)
-    outs[3][rows:, :] = jnp.where(first, other, same)
     side = me // 2
     places = [lookup(late, me ^ m) for m in range(frames)] + [lookup(lead, me ^ m) for m in range(frames)]
     places += [lookup(rest, 1 + side), lookup(rest, 2 - side)]
-    for n, head in enumerate(places):
-        here = slice(rows + n * cut, rows + (n + 1) * cut)
-        a, b = tail[here, :].astype(F32), tail2[here, :].astype(F32)
-        both = jnp.concatenate([jnp.where(first, a, b), jnp.where(first, b, a)], axis=0)
-        for o in range(3):
-            outs[o][:, column(head)] = both[o * rank : (o + 1) * rank]
+    copies = [pltpu.make_async_copy(filled[o], outs[o], sems.at[o]) for o in range(4)]
+
+    def rows_of(ref, n, start, stop):
+        return ref[rows + n * cut + start : rows + n * cut + stop, :].astype(F32)
+
+    for o in range(3):
+        for n, head in enumerate(places):
+            parts = []
+            for owner, low_end, high_end in ((0, 0, cut), (1, cut, 2 * cut)):
+                start, stop = max(o * rank, low_end), min((o + 1) * rank, high_end)
+                if start < stop:
+                    mine, its = (rows_of(ref, n, start - low_end, stop - low_end) for ref in (tail, tail2))
+                    parts.append(jnp.where(first, mine, its) if owner == 0 else jnp.where(first, its, mine))
+            filled[o][:, column(head)] = parts[0] if len(parts) == 1 else jnp.concatenate(parts, axis=0)
+        copies[o].start()
+    same = tail[:rows, :].astype(F32) + low_head[...].astype(F32)
+    other = tail2[:rows, :].astype(F32) + low_diag[...].astype(F32)
+    filled[3][:rows, :] = jnp.where(first, same, other)
+    filled[3][rows:, :] = jnp.where(first, other, same)
+    copies[3].start()
+    for copy in copies:
+        copy.wait()
 
 
 def place(frames, lead, late, rest, tail, tail2, low_head, low_diag, rank, width):
     rows = low_head.shape[0]
+    shapes = [(rank, width)] * 3 + [(2 * rows, rank)]
     return pl.pallas_call(
         functools.partial(place_kernel, frames, lead, late, rest),
         in_specs=vmem(4),
-        out_specs=vmem(4),
-        out_shape=[jax.ShapeDtypeStruct((rank, width), F32)] * 3
-        + [jax.ShapeDtypeStruct((2 * rows, rank), F32)],
+        out_specs=[pl.BlockSpec(memory_space=pl.ANY)] * 4,
+        out_shape=[jax.ShapeDtypeStruct(shape, F32) for shape in shapes],
+        scratch_shapes=[pltpu.VMEM(shape, F32) for shape in shapes] + [pltpu.SemaphoreType.DMA((4,))],
         compiler_params=SMALL,
     )(tail, tail2, low_head, low_diag)
 

time: 68.2 us -> 68.2 us (level)
  transfers between devices with their start and end apart: 22 -> 22, of which waited for: 8 -> 8; matrix products, arithmetic and copies ran while one was open for 0% -> 0% of each run, Pallas kernels for 12% -> 11%
where the time goes in v14:
time: 68.2 us; the launch traced here: 68 us
  starting transfers between devices  28.2 us (41%)
  waiting for transfers between devices  26.3 us (39%)
  Pallas kernels  11.9 us (17%)
  between operations  0.91 us (1%)
  local copies, waits for them, and re-layouts  0.69 us (1%)
    ppermute x12, starting transfers between devices, meet(): return lax.ppermute(block, 'tm', [(j ^ m, j) for j in targets])  23.1 us
    ppermute x12, waiting for transfers between devices, meet(): return lax.ppermute(block, 'tm', [(j ^ m, j) for j in targets])  19.8 us
    pallas_call x2, Pallas kernels, head_group(): pl.pallas_call(functools.partial(group_kernel, heads, frames, chained, le...  6.7 us
    pallas_call x2, Pallas kernels, pack(): pl.pallas_call(functools.partial(pack_kernel, frames, outputs), in_specs=...  3.51 us
    ppermute x1, waiting for transfers between devices, exchange_plan(): far = lax.ppermute(piece[:cut], 'tm', [(0, 2), (3, 1)])  3.45 us
    ppermute x8, starting transfers between devices, swap(): return lax.ppermute(block, axis, [(0, 1), (1, 0)])  2.95 us
    ppermute x8, waiting for transfers between devices, swap(): return lax.ppermute(block, axis, [(0, 1), (1, 0)])  2.14 us
    ppermute x1, starting transfers between devices, exchange_plan(): far = lax.ppermute(piece[:cut], 'tm', [(0, 2), (3, 1)])  1.82 us
  transfers between devices with their start and end apart: 22, of which 8 were waited for; matrix products, arithmetic and copies ran while one was open for 0% of the time, Pallas kernels for 11%

profile of v14, /device:TPU:0, one launch (start us, length us, event | category | flops | bytes accessed | tf_op | source)
XLA Modules:
  0.0 68.0 jit_solution(10778867798940271393)
XLA Ops:
  0.7 2.6 %shard_map.121 = (bf16[128,1664]{1,0:T(8,128)(2,1)}, bf16[128,640]{1,0:T(8,128)(2,1)}, bf16[128,512]{1,0:T(8,128)(2,1)}, bf16[128,640]{1,0:T(8,128)(2,1)}, bf16[128,512]{1,0:T(8,128)(2,1)}) custom-call(bf16[128,1280]{1,0:T(8,128)(2,1)} %fq_ref.3, bf16[128,1280]{1,0:T(8,128)(2,1)} %do_ref.3, bf16[256,1280]{1,0:T(8,128)(2,1)} %fk_ref.3, ...), custom_call_target="tpu_custom_call" | custom-call | tf_op jit(solution)/shard_map/pallas_call | solution.py:303
  3.3 3.1 %collective-permute-start = (bf16[128,1664]{1,0:T(8,128)(2,1)}, bf16[128,1664]{1,0:T(8,128)(2,1)S(1)}, u32[]{:S(2)}, u32[]{:S(2)}) collective-permute-start(bf16[128,1664]{1,0:T(8,128)(2,1)} %get-tuple-element.33), channel_id=1, source_target_pairs={{4,0},{0,4},{12,8},{8,12},{5,1},{1,5},{13,9},{9,13},{6,2},{2,6},{1... | collective-permute-start | bytes 1277960 | tf_op jit(solution)/shard_map/nearest_over_tm/ppermute | solution.py:676
  6.3 2.6 %collective-permute-start.1 = (bf16[128,640]{1,0:T(8,128)(2,1)}, bf16[128,640]{1,0:T(8,128)(2,1)S(1)}, u32[]{:S(2)}, u32[]{:S(2)}) collective-permute-start(bf16[128,640]{1,0:T(8,128)(2,1)} %get-tuple-element.34), channel_id=1, source_target_pairs={{8,0},{12,4},{0,8},{4,12},{9,1},{13,5},{1,9},{5,13},{10,2},{14,6},... | collective-permute-start | bytes 491528 | tf_op jit(solution)/shard_map/lead_over_tm/ppermute | solution.py:676
  8.9 3.8 %collective-permute-start.6 = (bf16[128,512]{1,0:T(8,128)(2,1)}, bf16[128,512]{1,0:T(8,128)(2,1)S(1)}, u32[]{:S(2)}, u32[]{:S(2)}) collective-permute-start(bf16[128,512]{1,0:T(8,128)(2,1)} %get-tuple-element.44), channel_id=1, source_target_pairs={{12,4},{0,8},{13,5},{1,9},{14,6},{2,10},{15,7},{3,11},{28,20},{16,... | collective-permute-start | bytes 393224 | tf_op jit(solution)/shard_map/rest_over_tm/ppermute | solution.py:676
  12.8 0.7 collective-permute-start.7
  13.5 0.9 %shard_map.120 = (bf16[128,512]{1,0:T(8,128)(2,1)S(1)}, bf16[128,512]{1,0:T(8,128)(2,1)S(1)}, bf16[128,512]{1,0:T(8,128)(2,1)S(1)}, bf16[128,256]{1,0:T(8,128)(2...) custom-call(bf16[128,1280]{1,0:T(8,128)(2,1)S(1)} %copy-done.2, ...), custom_call_target="tpu_custom_call" | custom-call | tf_op jit(solution)/shard_map/pallas_call | solution.py:303
  14.4 6.0 %collective-permute-done.1.refs_1_.refs_3_ = bf16[128,640]{1,0:T(8,128)(2,1)S(1)} collective-permute-done((bf16[128,640]{1,0:T(8,128)(2,1)}, bf16[128,640]{1,0:T(8,128)(2,1)S(1)}, u32[]{:S(2)}, u32[]{:S(2)}) %collective-permute-start.1) | collective-permute-done | bytes 163872 | tf_op jit(solution)/shard_map/lead_over_tm/ppermute | solution.py:676
  20.4 6.4 %collective-permute-done.2.refs_2_.refs_4_ = bf16[128,640]{1,0:T(8,128)(2,1)S(1)} collective-permute-done((bf16[128,640]{1,0:T(8,128)(2,1)}, bf16[128,640]{1,0:T(8,128)(2,1)S(1)}, u32[]{:S(2)}, u32[]{:S(2)}) %collective-permute-start.2) | collective-permute-done | bytes 163872 | tf_op jit(solution)/shard_map/lead_over_tm/ppermute | solution.py:676
  26.9 0.1 collective-permute-start.3
  27.0 0.5 collective-permute-start.8
  27.6 3.5 %collective-permute-start.4 = (bf16[128,512]{1,0:T(8,128)(2,1)S(1)}, bf16[128,512]{1,0:T(8,128)(2,1)S(1)}, u32[]{:S(2)}, u32[]{:S(2)}) collective-permute-start(bf16[128,512]{1,0:T(8,128)(2,1)S(1)} %get-tuple-element.39), channel_id=1, source_target_pairs={{8,0},{12,4},{0,8},{4,12},{9,1},{13,5},{1,9},{5,13},{10,2},{14,6},... | collective-permute-start | bytes 393224 | tf_op jit(solution)/shard_map/late_over_tm/ppermute | solution.py:676
  31.0 1.4 %collective-permute-start.5 = (bf16[128,512]{1,0:T(8,128)(2,1)S(1)}, bf16[128,512]{1,0:T(8,128)(2,1)S(1)}, u32[]{:S(2)}, u32[]{:S(2)}) collective-permute-start(bf16[128,512]{1,0:T(8,128)(2,1)S(1)} %get-tuple-element.40), channel_id=1, source_target_pairs={{12,0},{8,4},{4,8},{0,12},{13,1},{9,5},{5,9},{1,13},{14,2},{10,6},... | collective-permute-start | bytes 393224 | tf_op jit(solution)/shard_map/late_over_tm/ppermute | solution.py:676
  32.4 0.6 copy-done.8
  33.1 3.4 %shard_map.124 = (f32[384,128]{1,0:T(8,128)S(1)}, bf16[384,128]{1,0:T(8,128)(2,1)S(1)}, f32[512,128]{1,0:T(8,128)S(1)}, f32[512,128]{1,0:T(8,128)S(1)}) custom-call(s32[4,4]{1,0:T(4,128)S(1)} %copy-done.8, bf16[128,128]{1,0:T(8,128)(2,1)S(1)} %get-tuple-element.32.refs_1_, bf16[128,1664]{1,0:T(8,128)(2,1)S(1)} %collective-permute-done.refs_0_.refs_2_, ...), custom_call_target="tpu_custom_call" | custom-call | tf_op jit(solution)/shard_map/pallas_call | solution.py:523
  36.5 0.1 collective-permute-start.9
  36.5 4.5 %collective-permute-done.4.refs_1_.refs_8_ = bf16[128,512]{1,0:T(8,128)(2,1)S(1)} collective-permute-done((bf16[128,512]{1,0:T(8,128)(2,1)S(1)}, bf16[128,512]{1,0:T(8,128)(2,1)S(1)}, u32[]{:S(2)}, u32[]{:S(2)}) %collective-permute-start.4) | collective-permute-done | bytes 131104 | tf_op jit(solution)/shard_map/late_over_tm/ppermute | solution.py:676
  41.2 1.4 %collective-permute-start.13 = (bf16[384,128]{1,0:T(8,128)(2,1)S(1)}, bf16[384,128]{1,0:T(8,128)(2,1)S(1)}, u32[]{:S(2)}, u32[]{:S(2)}) collective-permute-start(bf16[384,128]{1,0:T(8,128)(2,1)S(1)} %add_convert_fusion.refs_17_.piece), channel_id=1, source_target_pairs={{12,0},{8,4},{4,8},{0,12},{13,1},{9,5},{5,9},{1,13},{14,2},{10,6},... | collective-permute-start | bytes 294920 | tf_op jit(solution)/shard_map/early_gradients_over_tm/ppermute | solution.py:676
  42.6 2.2 %collective-permute-start.14 = (bf16[384,128]{1,0:T(8,128)(2,1)S(1)}, bf16[384,128]{1,0:T(8,128)(2,1)S(1)}, u32[]{:S(2)}, u32[]{:S(2)}) collective-permute-start(bf16[384,128]{1,0:T(8,128)(2,1)S(1)} %add_convert_fusion.refs_17_.piece), channel_id=1, source_target_pairs={{4,0},{0,4},{12,8},{8,12},{5,1},{1,5},{13,9},{9,13},{6,2},{2,6},{1... | collective-permute-start | bytes 294920 | tf_op jit(solution)/shard_map/early_gradients_over_tm/ppermute | solution.py:676
  44.8 3.3 %shard_map.126 = (f32[704,128]{1,0:T(8,128)S(1)}, bf16[352,128]{1,0:T(8,128)(2,1)S(1)}, bf16[352,128]{1,0:T(8,128)(2,1)S(1)}) custom-call(s32[4,4]{1,0:T(4,128)S(1)} %copy-done.8, bf16[128,128]{1,0:T(8,128)(2,1)S(1)} %get-tuple-element.32.refs_1_, bf16[128,1664]{1,0:T(8,128)(2,1)S(1)} %collective-permute-done.refs_0_.refs_2_, ...), custom_call_target="tpu_custom_call" | custom-call | tf_op jit(solution)/shard_map/pallas_call | solution.py:523
  48.2 0.5 collective-permute-start.12
  48.7 1.3 %collective-permute-done.14.refs_3_.pair = bf16[384,128]{1,0:T(8,128)(2,1)S(1)} collective-permute-done((bf16[384,128]{1,0:T(8,128)(2,1)S(1)}, bf16[384,128]{1,0:T(8,128)(2,1)S(1)}, u32[]{:S(2)}, u32[]{:S(2)}) %collective-permute-start.14) | collective-permute-done | bytes 98336 | tf_op jit(solution)/shard_map/early_gradients_over_tm/ppermute | solution.py:676
  50.2 0.9 %collective-permute-start.15 = (bf16[704,128]{1,0:T(8,128)(2,1)S(1)}, bf16[704,128]{1,0:T(8,128)(2,1)S(1)}, u32[]{:S(2)}, u32[]{:S(2)}) collective-permute-start(bf16[704,128]{1,0:T(8,128)(2,1)S(1)} %get-tuple-element.56), channel_id=1, source_target_pairs={{4,0},{0,4},{12,8},{8,12},{5,1},{1,5},{13,9},{9,13},{6,2},{2,6},{1... | collective-permute-start | bytes 540680 | tf_op jit(solution)/shard_map/late_sums_over_tm/ppermute | solution.py:676
  51.1 1.8 %collective-permute-start.16 = (bf16[320,128]{1,0:T(8,128)(2,1)S(1)}, bf16[320,128]{1,0:T(8,128)(2,1)S(1)}, u32[]{:S(2)}, u32[]{:S(2)}) collective-permute-start(bf16[320,128]{1,0:T(8,128)(2,1)S(1)} %get-tuple-element.57), channel_id=1, source_target_pairs={{8,0},{12,4},{0,8},{4,12},{9,1},{13,5},{1,9},{5,13},{10,2},{14,6},... | collective-permute-start | bytes 245768 | tf_op jit(solution)/shard_map/late_sums_over_tm/ppermute | solution.py:676
  52.8 1.8 %collective-permute-start.17 = (bf16[320,128]{1,0:T(8,128)(2,1)S(1)}, bf16[320,128]{1,0:T(8,128)(2,1)S(1)}, u32[]{:S(2)}, u32[]{:S(2)}) collective-permute-start(bf16[320,128]{1,0:T(8,128)(2,1)S(1)} %get-tuple-element.55.own), channel_id=1, source_target_pairs={{12,0},{8,4},{4,8},{0,12},{13,1},{9,5},{5,9},{1,13},{14,2},{10,6},... | collective-permute-start | bytes 245768 | tf_op jit(solution)/shard_map/late_sums_over_tm/ppermute | solution.py:676
  54.6 1.8 %collective-permute-start.18 = (bf16[192,128]{1,0:T(8,128)(2,1)S(1)}, bf16[192,128]{1,0:T(8,128)(2,1)S(1)}, u32[]{:S(2)}, u32[]{:S(2)}) collective-permute-start(bf16[192,128]{1,0:T(8,128)(2,1)S(1)} %slice.4), channel_id=1, source_target_pairs={{0,8},{12,4},{1,9},{13,5},{2,10},{14,6},{3,11},{15,7},{16,24},{28,... | collective-permute-start | bytes 147464 | tf_op jit(solution)/shard_map/early_lead_over_tm/ppermute | solution.py:731
  56.4 3.4 %collective-permute-done.18.far = bf16[192,128]{1,0:T(8,128)(2,1)S(1)} collective-permute-done((bf16[192,128]{1,0:T(8,128)(2,1)S(1)}, bf16[192,128]{1,0:T(8,128)(2,1)S(1)}, u32[]{:S(2)}, u32[]{:S(2)}) %collective-permute-start.18) | collective-permute-done | bytes 49184 | tf_op jit(solution)/shard_map/early_lead_over_tm/ppermute | solution.py:731
  59.9 1.6 %collective-permute-done.17.last = bf16[320,128]{1,0:T(8,128)(2,1)S(1)} collective-permute-done((bf16[320,128]{1,0:T(8,128)(2,1)S(1)}, bf16[320,128]{1,0:T(8,128)(2,1)S(1)}, u32[]{:S(2)}, u32[]{:S(2)}) %collective-permute-start.17) | collective-permute-done | bytes 81952 | tf_op jit(solution)/shard_map/late_sums_over_tm/ppermute | solution.py:676
  61.6 1.6 %collective-permute-start.20 = (bf16[128,128]{1,0:T(8,128)(2,1)S(1)}, bf16[128,128]{1,0:T(8,128)(2,1)S(1)}, u32[]{:S(2)}, u32[]{:S(2)}) collective-permute-start(bf16[128,128]{1,0:T(8,128)(2,1)S(1)} %get-tuple-element.59), channel_id=1, source_target_pairs={{0,2},{2,0},{1,3},{3,1},{4,6},{6,4},{5,7},{7,5},{8,10},{10,8},{9,1... | collective-permute-start | bytes 98312 | tf_op jit(solution)/shard_map/low_over_head/ppermute | solution.py:50
  63.2 0.3 collective-permute-start.21
  63.5 2.1 %collective-permute-done.20.low_head = bf16[128,128]{1,0:T(8,128)(2,1)S(1)} collective-permute-done((bf16[128,128]{1,0:T(8,128)(2,1)S(1)}, bf16[128,128]{1,0:T(8,128)(2,1)S(1)}, u32[]{:S(2)}, u32[]{:S(2)}) %collective-permute-start.20) | collective-permute-done | bytes 32800 | tf_op jit(solution)/shard_map/low_over_head/ppermute | solution.py:50
  65.6 0.9 %collective-permute-done.21.low_diag = bf16[128,128]{1,0:T(8,128)(2,1)S(1)} collective-permute-done((bf16[128,128]{1,0:T(8,128)(2,1)S(1)}, bf16[128,128]{1,0:T(8,128)(2,1)S(1)}, u32[]{:S(2)}, u32[]{:S(2)}) %collective-permute-start.21) | collective-permute-done | bytes 32800 | tf_op jit(solution)/shard_map/low_over_head/ppermute | solution.py:739
  66.5 1.5 %shard_map.129 = (f32[128,1280]{1,0:T(8,128)}, f32[128,1280]{1,0:T(8,128)}, f32[128,1280]{1,0:T(8,128)}, f32[256,128]{1,0:T(8,128)}) custom-call(bf16[2048,128]{1,0:T(8,128)(2,1)S(1)} %get-tuple-element.58.tail, bf16[2048,128]{1,0:T(8,128)(2,1)S(1)} %collective-permute-done.19.tail2, bf16[128,128]{1,0:T(8,128)(2,1)S(1)} %collective-permute-done.20.low_head, ...), custom_call_target="tpu_custom_call" | custom-call | tf_op jit(solution)/shard_map/pallas_call | solution.py:639
  (42 shorter events, 0.5 us)
Async XLA Ops:
  0.6 12.8 %copy-start.2 = (bf16[128,1280]{1,0:T(8,128)(2,1)S(1)}, bf16[128,1280]{1,0:T(8,128)(2,1)}, u32[]{:S(2)}) copy-start(bf16[128,1280]{1,0:T(8,128)(2,1)} %fq_ref.3) | copy-start | bytes 983044
  0.6 12.8 %copy-start.3 = (bf16[128,1280]{1,0:T(8,128)(2,1)S(1)}, bf16[128,1280]{1,0:T(8,128)(2,1)}, u32[]{:S(2)}) copy-start(bf16[128,1280]{1,0:T(8,128)(2,1)} %do_ref.3) | copy-start | bytes 983044
  0.7 12.8 %copy-start = (bf16[256,1280]{1,0:T(8,128)(2,1)S(1)}, bf16[256,1280]{1,0:T(8,128)(2,1)}, u32[]{:S(2)}) copy-start(bf16[256,1280]{1,0:T(8,128)(2,1)} %fk_ref.3) | copy-start | bytes 1966084
  0.7 12.8 %copy-start.1 = (bf16[256,1280]{1,0:T(8,128)(2,1)S(1)}, bf16[256,1280]{1,0:T(8,128)(2,1)}, u32[]{:S(2)}) copy-start(bf16[256,1280]{1,0:T(8,128)(2,1)} %fv_ref.3) | copy-start | bytes 1966084
  0.7 12.8 %copy-start.7 = (bf16[256,128]{1,0:T(8,128)(2,1)S(1)}, bf16[256,128]{1,0:T(8,128)(2,1)}, u32[]{:S(2)}) copy-start(bf16[256,128]{1,0:T(8,128)(2,1)} %t_ref.3) | copy-start | bytes 196612
  3.3 23.6 %collective-permute-start = (bf16[128,1664]{1,0:T(8,128)(2,1)}, bf16[128,1664]{1,0:T(8,128)(2,1)S(1)}, u32[]{:S(2)}, u32[]{:S(2)}) collective-permute-start(bf16[128,1664]{1,0:T(8,128)(2,1)} %get-tuple-element.33), channel_id=1, source_target_pairs={{4,0},{0,4},{12,8},{8,12},{5,1},{1,5},{13,9},{9,13},{6,2},{2,6},{1... | collective-permute-start | bytes 1277960 | tf_op jit(solution)/shard_map/nearest_over_tm/ppermute | solution.py:676
  6.3 14.1 %collective-permute-start.1 = (bf16[128,640]{1,0:T(8,128)(2,1)}, bf16[128,640]{1,0:T(8,128)(2,1)S(1)}, u32[]{:S(2)}, u32[]{:S(2)}) collective-permute-start(bf16[128,640]{1,0:T(8,128)(2,1)} %get-tuple-element.34), channel_id=1, source_target_pairs={{8,0},{12,4},{0,8},{4,12},{9,1},{13,5},{1,9},{5,13},{10,2},{14,6},... | collective-permute-start | bytes 491528 | tf_op jit(solution)/shard_map/lead_over_tm/ppermute | solution.py:676
  8.9 17.9 %collective-permute-start.2 = (bf16[128,640]{1,0:T(8,128)(2,1)}, bf16[128,640]{1,0:T(8,128)(2,1)S(1)}, u32[]{:S(2)}, u32[]{:S(2)}) collective-permute-start(bf16[128,640]{1,0:T(8,128)(2,1)} %get-tuple-element.35), channel_id=1, source_target_pairs={{12,0},{8,4},{4,8},{0,12},{13,1},{9,5},{5,9},{1,13},{14,2},{10,6},... | collective-permute-start | bytes 491528 | tf_op jit(solution)/shard_map/lead_over_tm/ppermute | solution.py:676
  8.9 18.0 %collective-permute-start.6 = (bf16[128,512]{1,0:T(8,128)(2,1)}, bf16[128,512]{1,0:T(8,128)(2,1)S(1)}, u32[]{:S(2)}, u32[]{:S(2)}) collective-permute-start(bf16[128,512]{1,0:T(8,128)(2,1)} %get-tuple-element.44), channel_id=1, source_target_pairs={{12,4},{0,8},{13,5},{1,9},{14,6},{2,10},{15,7},{3,11},{28,20},{16,... | collective-permute-start | bytes 393224 | tf_op jit(solution)/shard_map/rest_over_tm/ppermute | solution.py:676
  12.8 14.2 %collective-permute-start.7 = (bf16[128,512]{1,0:T(8,128)(2,1)}, bf16[128,512]{1,0:T(8,128)(2,1)S(1)}, u32[]{:S(2)}, u32[]{:S(2)}) collective-permute-start(bf16[128,512]{1,0:T(8,128)(2,1)} %get-tuple-element.45), channel_id=1, source_target_pairs={{8,4},{4,8},{9,5},{5,9},{10,6},{6,10},{11,7},{7,11},{24,20},{20,24... | collective-permute-start | bytes 393224 | tf_op jit(solution)/shard_map/rest_over_tm/ppermute | solution.py:676
  26.8 5.6 %copy-start.6 = (bf16[128,1280]{1,0:T(8,128)(2,1)S(1)}, bf16[128,1280]{1,0:T(8,128)(2,1)}, u32[]{:S(2)}) copy-start(bf16[128,1280]{1,0:T(8,128)(2,1)} %refs_14_.3) | copy-start | bytes 983044
  26.9 5.6 %copy-start.4 = (bf16[128,1280]{1,0:T(8,128)(2,1)S(1)}, bf16[128,1280]{1,0:T(8,128)(2,1)}, u32[]{:S(2)}) copy-start(bf16[128,1280]{1,0:T(8,128)(2,1)} %refs_12_.1) | copy-start | bytes 983044
  26.9 5.6 %copy-start.5 = (bf16[128,1280]{1,0:T(8,128)(2,1)S(1)}, bf16[128,1280]{1,0:T(8,128)(2,1)}, u32[]{:S(2)}) copy-start(bf16[128,1280]{1,0:T(8,128)(2,1)} %refs_13_.1) | copy-start | bytes 983044
  26.9 5.5 %collective-permute-start.3 = (bf16[128,1152]{1,0:T(8,128)(2,1)S(1)}, bf16[128,1152]{1,0:T(8,128)(2,1)S(1)}, u32[]{:S(2)}, u32[]{:S(2)}) collective-permute-start(bf16[128,1152]{1,0:T(8,128)(2,1)S(1)} %shard_map.122), channel_id=1, source_target_pairs={{0,1},{1,0},{2,3},{3,2},{4,5},{5,4},{6,7},{7,6},{8,9},{9,8},{10,11... | collective-permute-start | bytes 884744 | tf_op jit(solution)/shard_map/lead_in_chip/ppermute | solution.py:50
  27.0 5.4 %collective-permute-start.8 = (bf16[128,768]{1,0:T(8,128)(2,1)S(1)}, bf16[128,768]{1,0:T(8,128)(2,1)S(1)}, u32[]{:S(2)}, u32[]{:S(2)}) collective-permute-start(bf16[128,768]{1,0:T(8,128)(2,1)S(1)} %shard_map.123), channel_id=1, source_target_pairs={{0,1},{1,0},{2,3},{3,2},{4,5},{5,4},{6,7},{7,6},{8,9},{9,8},{10,11... | collective-permute-start | bytes 589832 | tf_op jit(solution)/shard_map/rest_in_chip/ppermute | solution.py:50
  27.6 13.5 %collective-permute-start.4 = (bf16[128,512]{1,0:T(8,128)(2,1)S(1)}, bf16[128,512]{1,0:T(8,128)(2,1)S(1)}, u32[]{:S(2)}, u32[]{:S(2)}) collective-permute-start(bf16[128,512]{1,0:T(8,128)(2,1)S(1)} %get-tuple-element.39), channel_id=1, source_target_pairs={{8,0},{12,4},{0,8},{4,12},{9,1},{13,5},{1,9},{5,13},{10,2},{14,6},... | collective-permute-start | bytes 393224 | tf_op jit(solution)/shard_map/late_over_tm/ppermute | solution.py:676
  31.0 10.0 %collective-permute-start.5 = (bf16[128,512]{1,0:T(8,128)(2,1)S(1)}, bf16[128,512]{1,0:T(8,128)(2,1)S(1)}, u32[]{:S(2)}, u32[]{:S(2)}) collective-permute-start(bf16[128,512]{1,0:T(8,128)(2,1)S(1)} %get-tuple-element.40), channel_id=1, source_target_pairs={{12,0},{8,4},{4,8},{0,12},{13,1},{9,5},{5,9},{1,13},{14,2},{10,6},... | collective-permute-start | bytes 393224 | tf_op jit(solution)/shard_map/late_over_tm/ppermute | solution.py:676
  32.4 0.7 %copy-start.8 = (s32[4,4]{1,0:T(4,128)S(1)}, s32[4,4]{1,0:T(4,128)}, u32[]{:S(2)}) copy-start(s32[4,4]{1,0:T(4,128)} %refs_0_.3) | copy-start | bytes 196
  36.5 4.6 %collective-permute-start.9 = (bf16[384,128]{1,0:T(8,128)(2,1)S(1)}, bf16[384,128]{1,0:T(8,128)(2,1)S(1)}, u32[]{:S(2)}, u32[]{:S(2)}) collective-permute-start(bf16[384,128]{1,0:T(8,128)(2,1)S(1)} %get-tuple-element.47), channel_id=1, source_target_pairs={{0,1},{1,0},{2,3},{3,2},{4,5},{5,4},{6,7},{7,6},{8,9},{9,8},{10,11... | collective-permute-start | bytes 294920 | tf_op jit(solution)/shard_map/early_gradients_in_chip/ppermute | solution.py:50
  41.1 3.7 %collective-permute-start.10 = (bf16[128,1536]{1,0:T(8,128)(2,1)S(1)}, bf16[128,1536]{1,0:T(8,128)(2,1)S(1)}, u32[]{:S(2)}, u32[]{:S(2)}) collective-permute-start(bf16[128,1536]{1,0:T(8,128)(2,1)S(1)} %shard_map.125), channel_id=1, source_target_pairs={{0,1},{1,0},{2,3},{3,2},{4,5},{5,4},{6,7},{7,6},{8,9},{9,8},{10,11... | collective-permute-start | bytes 1179656 | tf_op jit(solution)/shard_map/late_in_chip/ppermute | solution.py:50
  41.2 7.6 %collective-permute-start.13 = (bf16[384,128]{1,0:T(8,128)(2,1)S(1)}, bf16[384,128]{1,0:T(8,128)(2,1)S(1)}, u32[]{:S(2)}, u32[]{:S(2)}) collective-permute-start(bf16[384,128]{1,0:T(8,128)(2,1)S(1)} %add_convert_fusion.refs_17_.piece), channel_id=1, source_target_pairs={{12,0},{8,4},{4,8},{0,12},{13,1},{9,5},{5,9},{1,13},{14,2},{10,6},... | collective-permute-start | bytes 294920 | tf_op jit(solution)/shard_map/early_gradients_over_tm/ppermute | solution.py:676
  42.6 7.5 %collective-permute-start.14 = (bf16[384,128]{1,0:T(8,128)(2,1)S(1)}, bf16[384,128]{1,0:T(8,128)(2,1)S(1)}, u32[]{:S(2)}, u32[]{:S(2)}) collective-permute-start(bf16[384,128]{1,0:T(8,128)(2,1)S(1)} %add_convert_fusion.refs_17_.piece), channel_id=1, source_target_pairs={{4,0},{0,4},{12,8},{8,12},{5,1},{1,5},{13,9},{9,13},{6,2},{2,6},{1... | collective-permute-start | bytes 294920 | tf_op jit(solution)/shard_map/early_gradients_over_tm/ppermute | solution.py:676
  48.1 1.9 %collective-permute-start.11 = (bf16[352,128]{1,0:T(8,128)(2,1)S(1)}, bf16[352,128]{1,0:T(8,128)(2,1)S(1)}, u32[]{:S(2)}, u32[]{:S(2)}) collective-permute-start(bf16[352,128]{1,0:T(8,128)(2,1)S(1)} %get-tuple-element.52), channel_id=1, source_target_pairs={{0,1},{1,0},{2,3},{3,2},{4,5},{5,4},{6,7},{7,6},{8,9},{9,8},{10,11... | collective-permute-start | bytes 270344 | tf_op jit(solution)/shard_map/late_sums_in_chip/ppermute | solution.py:50
  48.2 1.9 %collective-permute-start.12 = (bf16[352,128]{1,0:T(8,128)(2,1)S(1)}, bf16[352,128]{1,0:T(8,128)(2,1)S(1)}, u32[]{:S(2)}, u32[]{:S(2)}) collective-permute-start(bf16[352,128]{1,0:T(8,128)(2,1)S(1)} %get-tuple-element.53), channel_id=1, source_target_pairs={{0,1},{1,0},{2,3},{3,2},{4,5},{5,4},{6,7},{7,6},{8,9},{9,8},{10,11... | collective-permute-start | bytes 270344 | tf_op jit(solution)/shard_map/late_sums_in_chip/ppermute | solution.py:50
  50.2 11.3 %collective-permute-start.15 = (bf16[704,128]{1,0:T(8,128)(2,1)S(1)}, bf16[704,128]{1,0:T(8,128)(2,1)S(1)}, u32[]{:S(2)}, u32[]{:S(2)}) collective-permute-start(bf16[704,128]{1,0:T(8,128)(2,1)S(1)} %get-tuple-element.56), channel_id=1, source_target_pairs={{4,0},{0,4},{12,8},{8,12},{5,1},{1,5},{13,9},{9,13},{6,2},{2,6},{1... | collective-permute-start | bytes 540680 | tf_op jit(solution)/shard_map/late_sums_over_tm/ppermute | solution.py:676
  51.1 8.8 %collective-permute-start.16 = (bf16[320,128]{1,0:T(8,128)(2,1)S(1)}, bf16[320,128]{1,0:T(8,128)(2,1)S(1)}, u32[]{:S(2)}, u32[]{:S(2)}) collective-permute-start(bf16[320,128]{1,0:T(8,128)(2,1)S(1)} %get-tuple-element.57), channel_id=1, source_target_pairs={{8,0},{12,4},{0,8},{4,12},{9,1},{13,5},{1,9},{5,13},{10,2},{14,6},... | collective-permute-start | bytes 245768 | tf_op jit(solution)/shard_map/late_sums_over_tm/ppermute | solution.py:676
  52.8 8.6 %collective-permute-start.17 = (bf16[320,128]{1,0:T(8,128)(2,1)S(1)}, bf16[320,128]{1,0:T(8,128)(2,1)S(1)}, u32[]{:S(2)}, u32[]{:S(2)}) collective-permute-start(bf16[320,128]{1,0:T(8,128)(2,1)S(1)} %get-tuple-element.55.own), channel_id=1, source_target_pairs={{12,0},{8,4},{4,8},{0,12},{13,1},{9,5},{5,9},{1,13},{14,2},{10,6},... | collective-permute-start | bytes 245768 | tf_op jit(solution)/shard_map/late_sums_over_tm/ppermute | solution.py:676
  54.6 5.3 %collective-permute-start.18 = (bf16[192,128]{1,0:T(8,128)(2,1)S(1)}, bf16[192,128]{1,0:T(8,128)(2,1)S(1)}, u32[]{:S(2)}, u32[]{:S(2)}) collective-permute-start(bf16[192,128]{1,0:T(8,128)(2,1)S(1)} %slice.4), channel_id=1, source_target_pairs={{0,8},{12,4},{1,9},{13,5},{2,10},{14,6},{3,11},{15,7},{16,24},{28,... | collective-permute-start | bytes 147464 | tf_op jit(solution)/shard_map/early_lead_over_tm/ppermute | solution.py:731
  61.5 5.0 %collective-permute-start.19 = (bf16[2048,128]{1,0:T(8,128)(2,1)S(1)}, bf16[2048,128]{1,0:T(8,128)(2,1)S(1)}, u32[]{:S(2)}, u32[]{:S(2)}) collective-permute-start(bf16[2048,128]{1,0:T(8,128)(2,1)S(1)} %get-tuple-element.58.tail), channel_id=1, source_target_pairs={{0,1},{1,0},{2,3},{3,2},{4,5},{5,4},{6,7},{7,6},{8,9},{9,8},{10,11... | collective-permute-start | bytes 1572872 | tf_op jit(solution)/shard_map/tail_in_chip/ppermute | solution.py:50
  61.6 4.0 %collective-permute-start.20 = (bf16[128,128]{1,0:T(8,128)(2,1)S(1)}, bf16[128,128]{1,0:T(8,128)(2,1)S(1)}, u32[]{:S(2)}, u32[]{:S(2)}) collective-permute-start(bf16[128,128]{1,0:T(8,128)(2,1)S(1)} %get-tuple-element.59), channel_id=1, source_target_pairs={{0,2},{2,0},{1,3},{3,1},{4,6},{6,4},{5,7},{7,5},{8,10},{10,8},{9,1... | collective-permute-start | bytes 98312 | tf_op jit(solution)/shard_map/low_over_head/ppermute | solution.py:50
  63.2 3.3 %collective-permute-start.21 = (bf16[128,128]{1,0:T(8,128)(2,1)S(1)}, bf16[128,128]{1,0:T(8,128)(2,1)S(1)}, u32[]{:S(2)}, u32[]{:S(2)}) collective-permute-start(bf16[128,128]{1,0:T(8,128)(2,1)S(1)} %get-tuple-element.59), channel_id=1, source_target_pairs={{0,3},{1,2},{2,1},{3,0},{4,7},{5,6},{6,5},{7,4},{8,11},{9,10},{10,... | collective-permute-start | bytes 98312 | tf_op jit(solution)/shard_map/low_over_head/ppermute | solution.py:739

commit v15 on v14

--- a/solution.py
+++ b/solution.py
@@ -16,6 +16,7 @@
 F32 = jnp.float32
 BF16 = jnp.bfloat16
 GIVES = 2
+CHUNK = 32
 SMALL = pltpu.CompilerParams(vmem_limit_bytes=16 * 1024 * 1024)
 
 
@@ -266,8 +267,18 @@
     return [pl.BlockSpec(memory_space=pltpu.VMEM)] * count
 
 
+def chunked(source, target, sems, at, chunk):
+    rows = target.shape[0]
+    return [
+        pltpu.make_async_copy(
+            source.at[pl.ds(r * chunk, chunk), :], target.at[pl.ds(r * chunk, chunk), :], sems.at[at + r]
+        )
+        for r in range(rows // chunk)
+    ]
+
+
 def pack_kernel(frames, outputs, fq_ref, do_ref, fk_ref, fv_ref, t_ref, *refs):
-    outs, (q_in, do_in, k_in, v_in, k2_in, v2_in, t_in, sems) = refs[:-8], refs[-8:]
+    outs, (q_in, do_in, k_in, v_in, k2_in, v2_in, t_in, sems), held = refs[: len(outputs)], refs[-8:], refs[len(outputs) : -8]
     wanted = {what for parts in outputs for _, _, what in parts}
     me, half = lax.axis_index("tm"), lax.axis_index("rep")
     rows = fq_ref.shape[0]
@@ -278,12 +289,16 @@
     ]
     if "other" in wanted:
         moves += [(fk_ref.at[rest, :], k2_in), (fv_ref.at[rest, :], v2_in)]
-    copies = [pltpu.make_async_copy(a, b, sems.at[n]) for n, (a, b) in enumerate(moves)]
+    copies = []
+    for source, target in moves:
+        copies += chunked(source, target, sems, len(copies), CHUNK)
     for copy in copies:
         copy.start()
     for copy in copies:
         copy.wait()
-    for out, parts in zip(outs, outputs):
+    leaving, used = [], len(copies)
+    for n, parts in enumerate(outputs):
+        out = held[n] if held else outs[n]
         at = 0
         for table, m, what in parts:
             if what in ("t", "other t"):
@@ -295,22 +310,31 @@
             for block in blocks:
                 out[:, at : at + block.shape[1]] = block
                 at += block.shape[1]
-
-
-def pack(frames, outputs, limit, fq, do, fk, fv, t):
+        if held:
+            more = chunked(out, outs[n], sems, used + len(leaving), CHUNK)
+            for copy in more:
+                copy.start()
+            leaving += more
+    for copy in leaving:
+        copy.wait()
+
+
+def pack(frames, outputs, apart, fq, do, fk, fv, t):
     rows, width = fq.shape
     size = {"mine": 4 * DH, "other": 2 * DH, "t": t.shape[1], "other t": t.shape[1]}
+    shapes = [(rows, sum(size[what] for _, _, what in parts)) for parts in outputs]
+    held = [pltpu.VMEM(shape, BF16) for shape in shapes] if apart else []
+    count = (8 + (len(shapes) if apart else 0)) * (rows // CHUNK)
+    limit = (56 if apart else 16) * 1024 * 1024
     return pl.pallas_call(
         functools.partial(pack_kernel, frames, outputs),
         in_specs=[pl.BlockSpec(memory_space=pltpu.HBM)] * 5,
-        out_specs=vmem(len(outputs)),
-        out_shape=[
-            jax.ShapeDtypeStruct((rows, sum(size[what] for _, _, what in parts)), BF16)
-            for parts in outputs
-        ],
-        scratch_shapes=[pltpu.VMEM((rows, width), BF16)] * 6
-        + [pltpu.VMEM(t.shape, BF16), pltpu.SemaphoreType.DMA((7,))],
-        compiler_params=pltpu.CompilerParams(vmem_limit_bytes=limit * 1024 * 1024),
+        out_specs=[pl.BlockSpec(memory_space=pl.ANY)] * len(shapes) if apart else vmem(len(shapes)),
+        out_shape=[jax.ShapeDtypeStruct(shape, BF16) for shape in shapes],
+        scratch_shapes=held
+        + [pltpu.VMEM((rows, width), BF16)] * 6
+        + [pltpu.VMEM(t.shape, BF16), pltpu.SemaphoreType.DMA((count,))],
+        compiler_params=pltpu.CompilerParams(vmem_limit_bytes=limit),
     )(fq, do, fk, fv, t)
 
 
@@ -609,7 +633,9 @@
     side = me // 2
     places = [lookup(late, me ^ m) for m in range(frames)] + [lookup(lead, me ^ m) for m in range(frames)]
     places += [lookup(rest, 1 + side), lookup(rest, 2 - side)]
-    copies = [pltpu.make_async_copy(filled[o], outs[o], sems.at[o]) for o in range(4)]
+    copies = []
+    for o in range(4):
+        copies.append(chunked(filled[o], outs[o], sems, sum(map(len, copies)), CHUNK))
 
     def rows_of(ref, n, start, stop):
         return ref[rows + n * cut + start : rows + n * cut + stop, :].astype(F32)
@@ -623,13 +649,15 @@
                     mine, its = (rows_of(ref, n, start - low_end, stop - low_end) for ref in (tail, tail2))
                     parts.append(jnp.where(first, mine, its) if owner == 0 else jnp.where(first, its, mine))
             filled[o][:, column(head)] = parts[0] if len(parts) == 1 else jnp.concatenate(parts, axis=0)
-        copies[o].start()
+        for copy in copies[o]:
+            copy.start()
     same = tail[:rows, :].astype(F32) + low_head[...].astype(F32)
     other = tail2[:rows, :].astype(F32) + low_diag[...].astype(F32)
     filled[3][:rows, :] = jnp.where(first, same, other)
     filled[3][rows:, :] = jnp.where(first, other, same)
-    copies[3].start()
-    for copy in copies:
+    for copy in copies[3]:
+        copy.start()
+    for copy in sum(copies, []):
         copy.wait()
 
 
@@ -641,7 +669,8 @@
         in_specs=vmem(4),
         out_specs=[pl.BlockSpec(memory_space=pl.ANY)] * 4,
         out_shape=[jax.ShapeDtypeStruct(shape, F32) for shape in shapes],
-        scratch_shapes=[pltpu.VMEM(shape, F32) for shape in shapes] + [pltpu.SemaphoreType.DMA((4,))],
+        scratch_shapes=[pltpu.VMEM(shape, F32) for shape in shapes]
+        + [pltpu.SemaphoreType.DMA((sum(r // CHUNK for r, _ in shapes),))],
         compiler_params=SMALL,
     )(tail, tail2, low_head, low_diag)
 
@@ -693,8 +722,8 @@
     for slot in (lead, rest, late):
         kept += [[mine(slot, 0)], [(slot[0], 0, "other")]]
     kept += [[(None, 0, "t")], [(None, 0, "other t")]]
-    packed = pack(frames, sent, 56, *arrays)
-    packed_late = pack(frames, sent_late + kept, 16, *arrays)
+    packed = pack(frames, sent, True, *arrays)
+    packed_late = pack(frames, sent_late + kept, False, *arrays)
     kept = packed_late[len(sent_late) :]
     block = meet("nearest", packed[0], 1)
     lead_got, rest_got, late_got = [(block, 0)], [(block, 4 * DH + rank)], [(block, 8 * DH + rank)]

time: 68.2 us -> 68.7 us (level)
  Pallas kernels: 11.9 us -> 14.6 us
  waiting for transfers between devices: 26.3 us -> 24.1 us
    pallas_call x2, Pallas kernels: 3.51 us -> 6.1 us  [pack(): pl.pallas_call(functools.partial(pack_kernel, frames, outputs), in_specs=...]
    ppermute x12, waiting for transfers between devices: 19.8 us -> 17.6 us  [meet(): return lax.ppermute(block, 'tm', [(j ^ m, j) for j in targets])]
  transfers between devices with their start and end apart: 22 -> 22, of which waited for: 8 -> 8; matrix products, arithmetic and copies ran while one was open for 0% -> 0% of each run, Pallas kernels for 11% -> 14%
where the time goes in v15:
time: 68.7 us; the launch traced here: 68.5 us
  starting transfers between devices  28.2 us (41%)
  waiting for transfers between devices  24.1 us (35%)
  Pallas kernels  14.6 us (21%)
  between operations  0.91 us (1%)
  local copies, waits for them, and re-layouts  0.69 us (1%)
    ppermute x12, starting transfers between devices, meet(): return lax.ppermute(block, 'tm', [(j ^ m, j) for j in targets])  23.1 us
    ppermute x12, waiting for transfers between devices, meet(): return lax.ppermute(block, 'tm', [(j ^ m, j) for j in targets])  17.6 us
    pallas_call x2, Pallas kernels, head_group(): pl.pallas_call(functools.partial(group_kernel, heads, frames, chained, le...  6.7 us
    pallas_call x2, Pallas kernels, pack(): pl.pallas_call(functools.partial(pack_kernel, frames, outputs), in_specs=...  6.1 us
    ppermute x1, waiting for transfers between devices, exchange_plan(): far = lax.ppermute(piece[:cut], 'tm', [(0, 2), (3, 1)])  3.45 us
    ppermute x8, starting transfers between devices, swap(): return lax.ppermute(block, axis, [(0, 1), (1, 0)])  2.95 us
    ppermute x8, waiting for transfers between devices, swap(): return lax.ppermute(block, axis, [(0, 1), (1, 0)])  2.14 us
    ppermute x1, starting transfers between devices, exchange_plan(): far = lax.ppermute(piece[:cut], 'tm', [(0, 2), (3, 1)])  1.82 us
  transfers between devices with their start and end apart: 22, of which 8 were waited for; matrix products, arithmetic and copies ran while one was open for 0% of the time, Pallas kernels for 14%

profile of v15, /device:TPU:0, one launch (start us, length us, event | category | flops | bytes accessed | tf_op | source)
XLA Modules:
  0.0 68.5 jit_solution(8435511709716286888)
XLA Ops:
  0.7 3.0 %shard_map.121 = (bf16[128,1664]{1,0:T(8,128)(2,1)}, bf16[128,640]{1,0:T(8,128)(2,1)}, bf16[128,512]{1,0:T(8,128)(2,1)}, bf16[128,640]{1,0:T(8,128)(2,1)}, bf16[128,512]{1,0:T(8,128)(2,1)}) custom-call(bf16[128,1280]{1,0:T(8,128)(2,1)} %fq_ref.3, bf16[128,1280]{1,0:T(8,128)(2,1)} %do_ref.3, bf16[256,1280]{1,0:T(8,128)(2,1)} %fk_ref.3, ...), custom_call_target="tpu_custom_call" | custom-call | tf_op jit(solution)/shard_map/pallas_call | solution.py:329
  3.7 3.1 %collective-permute-start = (bf16[128,1664]{1,0:T(8,128)(2,1)}, bf16[128,1664]{1,0:T(8,128)(2,1)S(1)}, u32[]{:S(2)}, u32[]{:S(2)}) collective-permute-start(bf16[128,1664]{1,0:T(8,128)(2,1)} %get-tuple-element.33), channel_id=1, source_target_pairs={{4,0},{0,4},{12,8},{8,12},{5,1},{1,5},{13,9},{9,13},{6,2},{2,6},{1... | collective-permute-start | bytes 1277960 | tf_op jit(solution)/shard_map/nearest_over_tm/ppermute | solution.py:705
  6.7 2.6 %collective-permute-start.1 = (bf16[128,640]{1,0:T(8,128)(2,1)}, bf16[128,640]{1,0:T(8,128)(2,1)S(1)}, u32[]{:S(2)}, u32[]{:S(2)}) collective-permute-start(bf16[128,640]{1,0:T(8,128)(2,1)} %get-tuple-element.34), channel_id=1, source_target_pairs={{8,0},{12,4},{0,8},{4,12},{9,1},{13,5},{1,9},{5,13},{10,2},{14,6},... | collective-permute-start | bytes 491528 | tf_op jit(solution)/shard_map/lead_over_tm/ppermute | solution.py:705
  9.3 3.8 %collective-permute-start.6 = (bf16[128,512]{1,0:T(8,128)(2,1)}, bf16[128,512]{1,0:T(8,128)(2,1)S(1)}, u32[]{:S(2)}, u32[]{:S(2)}) collective-permute-start(bf16[128,512]{1,0:T(8,128)(2,1)} %get-tuple-element.44), channel_id=1, source_target_pairs={{12,4},{0,8},{13,5},{1,9},{14,6},{2,10},{15,7},{3,11},{28,20},{16,... | collective-permute-start | bytes 393224 | tf_op jit(solution)/shard_map/rest_over_tm/ppermute | solution.py:705
  13.2 0.7 collective-permute-start.7
  13.9 3.1 %shard_map.120 = (bf16[128,512]{1,0:T(8,128)(2,1)S(1)}, bf16[128,512]{1,0:T(8,128)(2,1)S(1)}, bf16[128,512]{1,0:T(8,128)(2,1)S(1)}, bf16[128,256]{1,0:T(8,128)(2...) custom-call(bf16[128,1280]{1,0:T(8,128)(2,1)S(1)} %copy-done.2, ...), custom_call_target="tpu_custom_call" | custom-call | tf_op jit(solution)/shard_map/pallas_call | solution.py:329
  17.0 3.8 %collective-permute-done.1.refs_1_.refs_3_ = bf16[128,640]{1,0:T(8,128)(2,1)S(1)} collective-permute-done((bf16[128,640]{1,0:T(8,128)(2,1)}, bf16[128,640]{1,0:T(8,128)(2,1)S(1)}, u32[]{:S(2)}, u32[]{:S(2)}) %collective-permute-start.1) | collective-permute-done | bytes 163872 | tf_op jit(solution)/shard_map/lead_over_tm/ppermute | solution.py:705
  20.8 6.4 %collective-permute-done.2.refs_2_.refs_4_ = bf16[128,640]{1,0:T(8,128)(2,1)S(1)} collective-permute-done((bf16[128,640]{1,0:T(8,128)(2,1)}, bf16[128,640]{1,0:T(8,128)(2,1)S(1)}, u32[]{:S(2)}, u32[]{:S(2)}) %collective-permute-start.2) | collective-permute-done | bytes 163872 | tf_op jit(solution)/shard_map/lead_over_tm/ppermute | solution.py:705
  27.3 0.1 collective-permute-start.3
  27.4 0.5 collective-permute-start.8
  28.0 3.5 %collective-permute-start.4 = (bf16[128,512]{1,0:T(8,128)(2,1)S(1)}, bf16[128,512]{1,0:T(8,128)(2,1)S(1)}, u32[]{:S(2)}, u32[]{:S(2)}) collective-permute-start(bf16[128,512]{1,0:T(8,128)(2,1)S(1)} %get-tuple-element.39), channel_id=1, source_target_pairs={{8,0},{12,4},{0,8},{4,12},{9,1},{13,5},{1,9},{5,13},{10,2},{14,6},... | collective-permute-start | bytes 393224 | tf_op jit(solution)/shard_map/late_over_tm/ppermute | solution.py:705
  31.5 1.4 %collective-permute-start.5 = (bf16[128,512]{1,0:T(8,128)(2,1)S(1)}, bf16[128,512]{1,0:T(8,128)(2,1)S(1)}, u32[]{:S(2)}, u32[]{:S(2)}) collective-permute-start(bf16[128,512]{1,0:T(8,128)(2,1)S(1)} %get-tuple-element.40), channel_id=1, source_target_pairs={{12,0},{8,4},{4,8},{0,12},{13,1},{9,5},{5,9},{1,13},{14,2},{10,6},... | collective-permute-start | bytes 393224 | tf_op jit(solution)/shard_map/late_over_tm/ppermute | solution.py:705
  32.8 0.6 copy-done.8
  33.5 3.4 %shard_map.124 = (f32[384,128]{1,0:T(8,128)S(1)}, bf16[384,128]{1,0:T(8,128)(2,1)S(1)}, f32[512,128]{1,0:T(8,128)S(1)}, f32[512,128]{1,0:T(8,128)S(1)}) custom-call(s32[4,4]{1,0:T(4,128)S(1)} %copy-done.8, bf16[128,128]{1,0:T(8,128)(2,1)S(1)} %get-tuple-element.32.refs_1_, bf16[128,1664]{1,0:T(8,128)(2,1)S(1)} %collective-permute-done.refs_0_.refs_2_, ...), custom_call_target="tpu_custom_call" | custom-call | tf_op jit(solution)/shard_map/pallas_call | solution.py:547
  36.9 0.1 collective-permute-start.9
  36.9 4.5 %collective-permute-done.4.refs_1_.refs_8_ = bf16[128,512]{1,0:T(8,128)(2,1)S(1)} collective-permute-done((bf16[128,512]{1,0:T(8,128)(2,1)S(1)}, bf16[128,512]{1,0:T(8,128)(2,1)S(1)}, u32[]{:S(2)}, u32[]{:S(2)}) %collective-permute-start.4) | collective-permute-done | bytes 131104 | tf_op jit(solution)/shard_map/late_over_tm/ppermute | solution.py:705
  41.6 1.4 %collective-permute-start.13 = (bf16[384,128]{1,0:T(8,128)(2,1)S(1)}, bf16[384,128]{1,0:T(8,128)(2,1)S(1)}, u32[]{:S(2)}, u32[]{:S(2)}) collective-permute-start(bf16[384,128]{1,0:T(8,128)(2,1)S(1)} %add_convert_fusion.refs_17_.piece), channel_id=1, source_target_pairs={{12,0},{8,4},{4,8},{0,12},{13,1},{9,5},{5,9},{1,13},{14,2},{10,6},... | collective-permute-start | bytes 294920 | tf_op jit(solution)/shard_map/early_gradients_over_tm/ppermute | solution.py:705
  43.0 2.2 %collective-permute-start.14 = (bf16[384,128]{1,0:T(8,128)(2,1)S(1)}, bf16[384,128]{1,0:T(8,128)(2,1)S(1)}, u32[]{:S(2)}, u32[]{:S(2)}) collective-permute-start(bf16[384,128]{1,0:T(8,128)(2,1)S(1)} %add_convert_fusion.refs_17_.piece), channel_id=1, source_target_pairs={{4,0},{0,4},{12,8},{8,12},{5,1},{1,5},{13,9},{9,13},{6,2},{2,6},{1... | collective-permute-start | bytes 294920 | tf_op jit(solution)/shard_map/early_gradients_over_tm/ppermute | solution.py:705
  45.2 3.3 %shard_map.126 = (f32[704,128]{1,0:T(8,128)S(1)}, bf16[352,128]{1,0:T(8,128)(2,1)S(1)}, bf16[352,128]{1,0:T(8,128)(2,1)S(1)}) custom-call(s32[4,4]{1,0:T(4,128)S(1)} %copy-done.8, bf16[128,128]{1,0:T(8,128)(2,1)S(1)} %get-tuple-element.32.refs_1_, bf16[128,1664]{1,0:T(8,128)(2,1)S(1)} %collective-permute-done.refs_0_.refs_2_, ...), custom_call_target="tpu_custom_call" | custom-call | tf_op jit(solution)/shard_map/pallas_call | solution.py:547
  48.6 0.5 collective-permute-start.12
  49.1 1.3 %collective-permute-done.14.refs_3_.pair = bf16[384,128]{1,0:T(8,128)(2,1)S(1)} collective-permute-done((bf16[384,128]{1,0:T(8,128)(2,1)S(1)}, bf16[384,128]{1,0:T(8,128)(2,1)S(1)}, u32[]{:S(2)}, u32[]{:S(2)}) %collective-permute-start.14) | collective-permute-done | bytes 98336 | tf_op jit(solution)/shard_map/early_gradients_over_tm/ppermute | solution.py:705
  50.6 0.9 %collective-permute-start.15 = (bf16[704,128]{1,0:T(8,128)(2,1)S(1)}, bf16[704,128]{1,0:T(8,128)(2,1)S(1)}, u32[]{:S(2)}, u32[]{:S(2)}) collective-permute-start(bf16[704,128]{1,0:T(8,128)(2,1)S(1)} %get-tuple-element.56), channel_id=1, source_target_pairs={{4,0},{0,4},{12,8},{8,12},{5,1},{1,5},{13,9},{9,13},{6,2},{2,6},{1... | collective-permute-start | bytes 540680 | tf_op jit(solution)/shard_map/late_sums_over_tm/ppermute | solution.py:705
  51.5 1.8 %collective-permute-start.16 = (bf16[320,128]{1,0:T(8,128)(2,1)S(1)}, bf16[320,128]{1,0:T(8,128)(2,1)S(1)}, u32[]{:S(2)}, u32[]{:S(2)}) collective-permute-start(bf16[320,128]{1,0:T(8,128)(2,1)S(1)} %get-tuple-element.57), channel_id=1, source_target_pairs={{8,0},{12,4},{0,8},{4,12},{9,1},{13,5},{1,9},{5,13},{10,2},{14,6},... | collective-permute-start | bytes 245768 | tf_op jit(solution)/shard_map/late_sums_over_tm/ppermute | solution.py:705
  53.2 1.8 %collective-permute-start.17 = (bf16[320,128]{1,0:T(8,128)(2,1)S(1)}, bf16[320,128]{1,0:T(8,128)(2,1)S(1)}, u32[]{:S(2)}, u32[]{:S(2)}) collective-permute-start(bf16[320,128]{1,0:T(8,128)(2,1)S(1)} %get-tuple-element.55.own), channel_id=1, source_target_pairs={{12,0},{8,4},{4,8},{0,12},{13,1},{9,5},{5,9},{1,13},{14,2},{10,6},... | collective-permute-start | bytes 245768 | tf_op jit(solution)/shard_map/late_sums_over_tm/ppermute | solution.py:705
  55.0 1.8 %collective-permute-start.18 = (bf16[192,128]{1,0:T(8,128)(2,1)S(1)}, bf16[192,128]{1,0:T(8,128)(2,1)S(1)}, u32[]{:S(2)}, u32[]{:S(2)}) collective-permute-start(bf16[192,128]{1,0:T(8,128)(2,1)S(1)} %slice.4), channel_id=1, source_target_pairs={{0,8},{12,4},{1,9},{13,5},{2,10},{14,6},{3,11},{15,7},{16,24},{28,... | collective-permute-start | bytes 147464 | tf_op jit(solution)/shard_map/early_lead_over_tm/ppermute | solution.py:760
  56.8 3.4 %collective-permute-done.18.far = bf16[192,128]{1,0:T(8,128)(2,1)S(1)} collective-permute-done((bf16[192,128]{1,0:T(8,128)(2,1)S(1)}, bf16[192,128]{1,0:T(8,128)(2,1)S(1)}, u32[]{:S(2)}, u32[]{:S(2)}) %collective-permute-start.18) | collective-permute-done | bytes 49184 | tf_op jit(solution)/shard_map/early_lead_over_tm/ppermute | solution.py:760
  60.3 1.6 %collective-permute-done.17.last = bf16[320,128]{1,0:T(8,128)(2,1)S(1)} collective-permute-done((bf16[320,128]{1,0:T(8,128)(2,1)S(1)}, bf16[320,128]{1,0:T(8,128)(2,1)S(1)}, u32[]{:S(2)}, u32[]{:S(2)}) %collective-permute-start.17) | collective-permute-done | bytes 81952 | tf_op jit(solution)/shard_map/late_sums_over_tm/ppermute | solution.py:705
  62.0 1.6 %collective-permute-start.20 = (bf16[128,128]{1,0:T(8,128)(2,1)S(1)}, bf16[128,128]{1,0:T(8,128)(2,1)S(1)}, u32[]{:S(2)}, u32[]{:S(2)}) collective-permute-start(bf16[128,128]{1,0:T(8,128)(2,1)S(1)} %get-tuple-element.59), channel_id=1, source_target_pairs={{0,2},{2,0},{1,3},{3,1},{4,6},{6,4},{5,7},{7,5},{8,10},{10,8},{9,1... | collective-permute-start | bytes 98312 | tf_op jit(solution)/shard_map/low_over_head/ppermute | solution.py:51
  63.6 0.3 collective-permute-start.21
  63.9 2.1 %collective-permute-done.20.low_head = bf16[128,128]{1,0:T(8,128)(2,1)S(1)} collective-permute-done((bf16[128,128]{1,0:T(8,128)(2,1)S(1)}, bf16[128,128]{1,0:T(8,128)(2,1)S(1)}, u32[]{:S(2)}, u32[]{:S(2)}) %collective-permute-start.20) | collective-permute-done | bytes 32800 | tf_op jit(solution)/shard_map/low_over_head/ppermute | solution.py:51
  66.0 0.9 %collective-permute-done.21.low_diag = bf16[128,128]{1,0:T(8,128)(2,1)S(1)} collective-permute-done((bf16[128,128]{1,0:T(8,128)(2,1)S(1)}, bf16[128,128]{1,0:T(8,128)(2,1)S(1)}, u32[]{:S(2)}, u32[]{:S(2)}) %collective-permute-start.21) | collective-permute-done | bytes 32800 | tf_op jit(solution)/shard_map/low_over_head/ppermute | solution.py:768
  66.9 1.5 %shard_map.129 = (f32[128,1280]{1,0:T(8,128)}, f32[128,1280]{1,0:T(8,128)}, f32[128,1280]{1,0:T(8,128)}, f32[256,128]{1,0:T(8,128)}) custom-call(bf16[2048,128]{1,0:T(8,128)(2,1)S(1)} %get-tuple-element.58.tail, bf16[2048,128]{1,0:T(8,128)(2,1)S(1)} %collective-permute-done.19.tail2, bf16[128,128]{1,0:T(8,128)(2,1)S(1)} %collective-permute-done.20.low_head, ...), custom_call_target="tpu_custom_call" | custom-call | tf_op jit(solution)/shard_map/pallas_call | solution.py:667
  (42 shorter events, 0.5 us)
Async XLA Ops:
  0.6 13.2 %copy-start.2 = (bf16[128,1280]{1,0:T(8,128)(2,1)S(1)}, bf16[128,1280]{1,0:T(8,128)(2,1)}, u32[]{:S(2)}) copy-start(bf16[128,1280]{1,0:T(8,128)(2,1)} %fq_ref.3) | copy-start | bytes 983044
  0.6 13.2 %copy-start.3 = (bf16[128,1280]{1,0:T(8,128)(2,1)S(1)}, bf16[128,1280]{1,0:T(8,128)(2,1)}, u32[]{:S(2)}) copy-start(bf16[128,1280]{1,0:T(8,128)(2,1)} %do_ref.3) | copy-start | bytes 983044
  0.7 13.2 %copy-start = (bf16[256,1280]{1,0:T(8,128)(2,1)S(1)}, bf16[256,1280]{1,0:T(8,128)(2,1)}, u32[]{:S(2)}) copy-start(bf16[256,1280]{1,0:T(8,128)(2,1)} %fk_ref.3) | copy-start | bytes 1966084
  0.7 13.2 %copy-start.1 = (bf16[256,1280]{1,0:T(8,128)(2,1)S(1)}, bf16[256,1280]{1,0:T(8,128)(2,1)}, u32[]{:S(2)}) copy-start(bf16[256,1280]{1,0:T(8,128)(2,1)} %fv_ref.3) | copy-start | bytes 1966084
  0.7 13.2 %copy-start.7 = (bf16[256,128]{1,0:T(8,128)(2,1)S(1)}, bf16[256,128]{1,0:T(8,128)(2,1)}, u32[]{:S(2)}) copy-start(bf16[256,128]{1,0:T(8,128)(2,1)} %t_ref.3) | copy-start | bytes 196612
  3.7 23.6 %collective-permute-start = (bf16[128,1664]{1,0:T(8,128)(2,1)}, bf16[128,1664]{1,0:T(8,128)(2,1)S(1)}, u32[]{:S(2)}, u32[]{:S(2)}) collective-permute-start(bf16[128,1664]{1,0:T(8,128)(2,1)} %get-tuple-element.33), channel_id=1, source_target_pairs={{4,0},{0,4},{12,8},{8,12},{5,1},{1,5},{13,9},{9,13},{6,2},{2,6},{1... | collective-permute-start | bytes 1277960 | tf_op jit(solution)/shard_map/nearest_over_tm/ppermute | solution.py:705
  6.7 14.1 %collective-permute-start.1 = (bf16[128,640]{1,0:T(8,128)(2,1)}, bf16[128,640]{1,0:T(8,128)(2,1)S(1)}, u32[]{:S(2)}, u32[]{:S(2)}) collective-permute-start(bf16[128,640]{1,0:T(8,128)(2,1)} %get-tuple-element.34), channel_id=1, source_target_pairs={{8,0},{12,4},{0,8},{4,12},{9,1},{13,5},{1,9},{5,13},{10,2},{14,6},... | collective-permute-start | bytes 491528 | tf_op jit(solution)/shard_map/lead_over_tm/ppermute | solution.py:705
  9.3 17.9 %collective-permute-start.2 = (bf16[128,640]{1,0:T(8,128)(2,1)}, bf16[128,640]{1,0:T(8,128)(2,1)S(1)}, u32[]{:S(2)}, u32[]{:S(2)}) collective-permute-start(bf16[128,640]{1,0:T(8,128)(2,1)} %get-tuple-element.35), channel_id=1, source_target_pairs={{12,0},{8,4},{4,8},{0,12},{13,1},{9,5},{5,9},{1,13},{14,2},{10,6},... | collective-permute-start | bytes 491528 | tf_op jit(solution)/shard_map/lead_over_tm/ppermute | solution.py:705
  9.3 18.0 %collective-permute-start.6 = (bf16[128,512]{1,0:T(8,128)(2,1)}, bf16[128,512]{1,0:T(8,128)(2,1)S(1)}, u32[]{:S(2)}, u32[]{:S(2)}) collective-permute-start(bf16[128,512]{1,0:T(8,128)(2,1)} %get-tuple-element.44), channel_id=1, source_target_pairs={{12,4},{0,8},{13,5},{1,9},{14,6},{2,10},{15,7},{3,11},{28,20},{16,... | collective-permute-start | bytes 393224 | tf_op jit(solution)/shard_map/rest_over_tm/ppermute | solution.py:705
  13.2 14.2 %collective-permute-start.7 = (bf16[128,512]{1,0:T(8,128)(2,1)}, bf16[128,512]{1,0:T(8,128)(2,1)S(1)}, u32[]{:S(2)}, u32[]{:S(2)}) collective-permute-start(bf16[128,512]{1,0:T(8,128)(2,1)} %get-tuple-element.45), channel_id=1, source_target_pairs={{8,4},{4,8},{9,5},{5,9},{10,6},{6,10},{11,7},{7,11},{24,20},{20,24... | collective-permute-start | bytes 393224 | tf_op jit(solution)/shard_map/rest_over_tm/ppermute | solution.py:705
  27.2 5.6 %copy-start.6 = (bf16[128,1280]{1,0:T(8,128)(2,1)S(1)}, bf16[128,1280]{1,0:T(8,128)(2,1)}, u32[]{:S(2)}) copy-start(bf16[128,1280]{1,0:T(8,128)(2,1)} %refs_14_.3) | copy-start | bytes 983044
  27.3 5.6 %copy-start.4 = (bf16[128,1280]{1,0:T(8,128)(2,1)S(1)}, bf16[128,1280]{1,0:T(8,128)(2,1)}, u32[]{:S(2)}) copy-start(bf16[128,1280]{1,0:T(8,128)(2,1)} %refs_12_.1) | copy-start | bytes 983044
  27.3 5.6 %copy-start.5 = (bf16[128,1280]{1,0:T(8,128)(2,1)S(1)}, bf16[128,1280]{1,0:T(8,128)(2,1)}, u32[]{:S(2)}) copy-start(bf16[128,1280]{1,0:T(8,128)(2,1)} %refs_13_.1) | copy-start | bytes 983044
  27.3 5.5 %collective-permute-start.3 = (bf16[128,1152]{1,0:T(8,128)(2,1)S(1)}, bf16[128,1152]{1,0:T(8,128)(2,1)S(1)}, u32[]{:S(2)}, u32[]{:S(2)}) collective-permute-start(bf16[128,1152]{1,0:T(8,128)(2,1)S(1)} %shard_map.122), channel_id=1, source_target_pairs={{0,1},{1,0},{2,3},{3,2},{4,5},{5,4},{6,7},{7,6},{8,9},{9,8},{10,11... | collective-permute-start | bytes 884744 | tf_op jit(solution)/shard_map/lead_in_chip/ppermute | solution.py:51
  27.4 5.4 %collective-permute-start.8 = (bf16[128,768]{1,0:T(8,128)(2,1)S(1)}, bf16[128,768]{1,0:T(8,128)(2,1)S(1)}, u32[]{:S(2)}, u32[]{:S(2)}) collective-permute-start(bf16[128,768]{1,0:T(8,128)(2,1)S(1)} %shard_map.123), channel_id=1, source_target_pairs={{0,1},{1,0},{2,3},{3,2},{4,5},{5,4},{6,7},{7,6},{8,9},{9,8},{10,11... | collective-permute-start | bytes 589832 | tf_op jit(solution)/shard_map/rest_in_chip/ppermute | solution.py:51
  28.0 13.5 %collective-permute-start.4 = (bf16[128,512]{1,0:T(8,128)(2,1)S(1)}, bf16[128,512]{1,0:T(8,128)(2,1)S(1)}, u32[]{:S(2)}, u32[]{:S(2)}) collective-permute-start(bf16[128,512]{1,0:T(8,128)(2,1)S(1)} %get-tuple-element.39), channel_id=1, source_target_pairs={{8,0},{12,4},{0,8},{4,12},{9,1},{13,5},{1,9},{5,13},{10,2},{14,6},... | collective-permute-start | bytes 393224 | tf_op jit(solution)/shard_map/late_over_tm/ppermute | solution.py:705
  31.5 10.0 %collective-permute-start.5 = (bf16[128,512]{1,0:T(8,128)(2,1)S(1)}, bf16[128,512]{1,0:T(8,128)(2,1)S(1)}, u32[]{:S(2)}, u32[]{:S(2)}) collective-permute-start(bf16[128,512]{1,0:T(8,128)(2,1)S(1)} %get-tuple-element.40), channel_id=1, source_target_pairs={{12,0},{8,4},{4,8},{0,12},{13,1},{9,5},{5,9},{1,13},{14,2},{10,6},... | collective-permute-start | bytes 393224 | tf_op jit(solution)/shard_map/late_over_tm/ppermute | solution.py:705
  32.8 0.7 copy-start.8
  36.9 4.6 %collective-permute-start.9 = (bf16[384,128]{1,0:T(8,128)(2,1)S(1)}, bf16[384,128]{1,0:T(8,128)(2,1)S(1)}, u32[]{:S(2)}, u32[]{:S(2)}) collective-permute-start(bf16[384,128]{1,0:T(8,128)(2,1)S(1)} %get-tuple-element.47), channel_id=1, source_target_pairs={{0,1},{1,0},{2,3},{3,2},{4,5},{5,4},{6,7},{7,6},{8,9},{9,8},{10,11... | collective-permute-start | bytes 294920 | tf_op jit(solution)/shard_map/early_gradients_in_chip/ppermute | solution.py:51
  41.5 3.7 %collective-permute-start.10 = (bf16[128,1536]{1,0:T(8,128)(2,1)S(1)}, bf16[128,1536]{1,0:T(8,128)(2,1)S(1)}, u32[]{:S(2)}, u32[]{:S(2)}) collective-permute-start(bf16[128,1536]{1,0:T(8,128)(2,1)S(1)} %shard_map.125), channel_id=1, source_target_pairs={{0,1},{1,0},{2,3},{3,2},{4,5},{5,4},{6,7},{7,6},{8,9},{9,8},{10,11... | collective-permute-start | bytes 1179656 | tf_op jit(solution)/shard_map/late_in_chip/ppermute | solution.py:51
  41.6 7.6 %collective-permute-start.13 = (bf16[384,128]{1,0:T(8,128)(2,1)S(1)}, bf16[384,128]{1,0:T(8,128)(2,1)S(1)}, u32[]{:S(2)}, u32[]{:S(2)}) collective-permute-start(bf16[384,128]{1,0:T(8,128)(2,1)S(1)} %add_convert_fusion.refs_17_.piece), channel_id=1, source_target_pairs={{12,0},{8,4},{4,8},{0,12},{13,1},{9,5},{5,9},{1,13},{14,2},{10,6},... | collective-permute-start | bytes 294920 | tf_op jit(solution)/shard_map/early_gradients_over_tm/ppermute | solution.py:705
  43.0 7.5 %collective-permute-start.14 = (bf16[384,128]{1,0:T(8,128)(2,1)S(1)}, bf16[384,128]{1,0:T(8,128)(2,1)S(1)}, u32[]{:S(2)}, u32[]{:S(2)}) collective-permute-start(bf16[384,128]{1,0:T(8,128)(2,1)S(1)} %add_convert_fusion.refs_17_.piece), channel_id=1, source_target_pairs={{4,0},{0,4},{12,8},{8,12},{5,1},{1,5},{13,9},{9,13},{6,2},{2,6},{1... | collective-permute-start | bytes 294920 | tf_op jit(solution)/shard_map/early_gradients_over_tm/ppermute | solution.py:705
  48.6 1.9 %collective-permute-start.11 = (bf16[352,128]{1,0:T(8,128)(2,1)S(1)}, bf16[352,128]{1,0:T(8,128)(2,1)S(1)}, u32[]{:S(2)}, u32[]{:S(2)}) collective-permute-start(bf16[352,128]{1,0:T(8,128)(2,1)S(1)} %get-tuple-element.52), channel_id=1, source_target_pairs={{0,1},{1,0},{2,3},{3,2},{4,5},{5,4},{6,7},{7,6},{8,9},{9,8},{10,11... | collective-permute-start | bytes 270344 | tf_op jit(solution)/shard_map/late_sums_in_chip/ppermute | solution.py:51
  48.6 1.9 %collective-permute-start.12 = (bf16[352,128]{1,0:T(8,128)(2,1)S(1)}, bf16[352,128]{1,0:T(8,128)(2,1)S(1)}, u32[]{:S(2)}, u32[]{:S(2)}) collective-permute-start(bf16[352,128]{1,0:T(8,128)(2,1)S(1)} %get-tuple-element.53), channel_id=1, source_target_pairs={{0,1},{1,0},{2,3},{3,2},{4,5},{5,4},{6,7},{7,6},{8,9},{9,8},{10,11... | collective-permute-start | bytes 270344 | tf_op jit(solution)/shard_map/late_sums_in_chip/ppermute | solution.py:51
  50.6 11.3 %collective-permute-start.15 = (bf16[704,128]{1,0:T(8,128)(2,1)S(1)}, bf16[704,128]{1,0:T(8,128)(2,1)S(1)}, u32[]{:S(2)}, u32[]{:S(2)}) collective-permute-start(bf16[704,128]{1,0:T(8,128)(2,1)S(1)} %get-tuple-element.56), channel_id=1, source_target_pairs={{4,0},{0,4},{12,8},{8,12},{5,1},{1,5},{13,9},{9,13},{6,2},{2,6},{1... | collective-permute-start | bytes 540680 | tf_op jit(solution)/shard_map/late_sums_over_tm/ppermute | solution.py:705
  51.5 8.8 %collective-permute-start.16 = (bf16[320,128]{1,0:T(8,128)(2,1)S(1)}, bf16[320,128]{1,0:T(8,128)(2,1)S(1)}, u32[]{:S(2)}, u32[]{:S(2)}) collective-permute-start(bf16[320,128]{1,0:T(8,128)(2,1)S(1)} %get-tuple-element.57), channel_id=1, source_target_pairs={{8,0},{12,4},{0,8},{4,12},{9,1},{13,5},{1,9},{5,13},{10,2},{14,6},... | collective-permute-start | bytes 245768 | tf_op jit(solution)/shard_map/late_sums_over_tm/ppermute | solution.py:705
  53.2 8.6 %collective-permute-start.17 = (bf16[320,128]{1,0:T(8,128)(2,1)S(1)}, bf16[320,128]{1,0:T(8,128)(2,1)S(1)}, u32[]{:S(2)}, u32[]{:S(2)}) collective-permute-start(bf16[320,128]{1,0:T(8,128)(2,1)S(1)} %get-tuple-element.55.own), channel_id=1, source_target_pairs={{12,0},{8,4},{4,8},{0,12},{13,1},{9,5},{5,9},{1,13},{14,2},{10,6},... | collective-permute-start | bytes 245768 | tf_op jit(solution)/shard_map/late_sums_over_tm/ppermute | solution.py:705
  55.0 5.3 %collective-permute-start.18 = (bf16[192,128]{1,0:T(8,128)(2,1)S(1)}, bf16[192,128]{1,0:T(8,128)(2,1)S(1)}, u32[]{:S(2)}, u32[]{:S(2)}) collective-permute-start(bf16[192,128]{1,0:T(8,128)(2,1)S(1)} %slice.4), channel_id=1, source_target_pairs={{0,8},{12,4},{1,9},{13,5},{2,10},{14,6},{3,11},{15,7},{16,24},{28,... | collective-permute-start | bytes 147464 | tf_op jit(solution)/shard_map/early_lead_over_tm/ppermute | solution.py:760
  61.9 5.0 %collective-permute-start.19 = (bf16[2048,128]{1,0:T(8,128)(2,1)S(1)}, bf16[2048,128]{1,0:T(8,128)(2,1)S(1)}, u32[]{:S(2)}, u32[]{:S(2)}) collective-permute-start(bf16[2048,128]{1,0:T(8,128)(2,1)S(1)} %get-tuple-element.58.tail), channel_id=1, source_target_pairs={{0,1},{1,0},{2,3},{3,2},{4,5},{5,4},{6,7},{7,6},{8,9},{9,8},{10,11... | collective-permute-start | bytes 1572872 | tf_op jit(solution)/shard_map/tail_in_chip/ppermute | solution.py:51
  62.0 4.0 %collective-permute-start.20 = (bf16[128,128]{1,0:T(8,128)(2,1)S(1)}, bf16[128,128]{1,0:T(8,128)(2,1)S(1)}, u32[]{:S(2)}, u32[]{:S(2)}) collective-permute-start(bf16[128,128]{1,0:T(8,128)(2,1)S(1)} %get-tuple-element.59), channel_id=1, source_target_pairs={{0,2},{2,0},{1,3},{3,1},{4,6},{6,4},{5,7},{7,5},{8,10},{10,8},{9,1... | collective-permute-start | bytes 98312 | tf_op jit(solution)/shard_map/low_over_head/ppermute | solution.py:51
  63.6 3.3 %collective-permute-start.21 = (bf16[128,128]{1,0:T(8,128)(2,1)S(1)}, bf16[128,128]{1,0:T(8,128)(2,1)S(1)}, u32[]{:S(2)}, u32[]{:S(2)}) collective-permute-start(bf16[128,128]{1,0:T(8,128)(2,1)S(1)} %get-tuple-element.59), channel_id=1, source_target_pairs={{0,3},{1,2},{2,1},{3,0},{4,7},{5,6},{6,5},{7,4},{8,11},{9,10},{10,... | collective-permute-start | bytes 98312 | tf_op jit(solution)/shard_map/low_over_head/ppermute | solution.py:768

commit v16 on v14

--- a/solution.py
+++ b/solution.py
@@ -15,7 +15,7 @@
 SCALE_2 = SCALE * math.log2(math.e)
 F32 = jnp.float32
 BF16 = jnp.bfloat16
-GIVES = 2
+GIVES = 4
 SMALL = pltpu.CompilerParams(vmem_limit_bytes=16 * 1024 * 1024)
 
 
@@ -535,7 +535,7 @@
 
 
 def hand_out_kernel(frames, size, parts, keep_ref, *refs):
-    gots, facing, (own_ref, *sends, total) = refs[:parts], refs[parts], refs[-frames - 1 :]
+    gots, (own_ref, *sends, total) = refs[:parts], refs[-frames - 1 :]
     me = lax.axis_index("tm")
     rows = own_ref.shape[0]
     total[...] = keep_ref[...] + jnp.concatenate([got[...].astype(F32) for got in gots], axis=0)
@@ -545,25 +545,43 @@
             own_ref[...] = low
         else:
             sends[m - 1][:rows, :] = low.astype(BF16)
-            sends[m - 1][rows : rows + size, :] = total[:size, :].astype(BF16)
-    sends[0][rows + size :, :] = facing[...]
-
-
-def hand_out(frames, rows, keep, gots, facing, after):
+            sends[m - 1][rows:, :] = total[:size, :].astype(BF16)
+
+
+def hand_out(frames, rows, keep, gots, after):
     size, rank = keep.shape[0] - frames * rows, keep.shape[1]
     own, *sends = pl.pallas_call(
         functools.partial(hand_out_kernel, frames, size, len(gots)),
-        in_specs=vmem(2 + len(gots)) + [pl.BlockSpec(memory_space=pl.ANY)] * len(after),
+        in_specs=vmem(1 + len(gots)) + [pl.BlockSpec(memory_space=pl.ANY)] * len(after),
         out_specs=vmem(frames),
         out_shape=[jax.ShapeDtypeStruct((rows, rank), F32)]
-        + [jax.ShapeDtypeStruct((rows + size * n, rank), BF16) for n in (3, 1, 1)],
+        + [jax.ShapeDtypeStruct((rows + size, rank), BF16)] * (frames - 1),
         scratch_shapes=[pltpu.VMEM(keep.shape, F32)],
         compiler_params=SMALL,
-    )(keep, *gots, facing, *after)
+    )(keep, *gots, *after)
     return own, sends
 
 
-def collect_kernel(wide, own_low, own, near, third, last, piece, pair, far, facing, out_ref, low_ref):
+def relay_kernel(wide, piece, facing, lead_ref, rest_ref):
+    size = lead_ref.shape[0]
+    middle = lookup(wide, lax.axis_index("tm")) > 0
+    lead_ref[...] = jnp.where(middle, facing[:size, :], piece[:size, :])
+    rest_ref[...] = facing[size:, :]
+
+
+def relay(wide, piece, facing):
+    half = jax.ShapeDtypeStruct((piece.shape[0] // 2, piece.shape[1]), piece.dtype)
+    return pl.pallas_call(
+        functools.partial(relay_kernel, wide),
+        in_specs=vmem(2),
+        out_specs=vmem(2),
+        out_shape=[half, half],
+        compiler_params=SMALL,
+    )(piece, facing)
+
+
+def collect_kernel(wide, own_low, own, near, third, last, piece, pair, facing, lead_far, rest_far, *outs):
+    out_ref, low_ref = outs
     rows = own_low.shape[0]
     size = own.shape[0] - rows
     low = own_low[...]
@@ -572,15 +590,10 @@
     out_ref[:rows, :] = low.astype(BF16)
     low_ref[...] = low.astype(BF16)
     middle = lookup(wide, lax.axis_index("tm")) > 0
-
-    def part(ref, n):
-        return ref[rows + n * size : rows + (n + 1) * size, :]
-
-    blocks = [part(ref, 0) for ref in (own, near, third, last)]
-    blocks += [piece[:size, :], pair[:size, :]]
-    blocks += [jnp.where(middle, far[...], part(near, 1)), facing[:size, :]]
+    blocks = [ref[rows:, :] for ref in (own, near, third, last)]
+    blocks += [piece[:size, :], pair[:size, :], lead_far[...], facing[:size, :]]
     blocks.append(jnp.where(middle, piece[size:, :], pair[size:, :]))
-    blocks.append(jnp.where(middle, facing[size:, :], part(near, 2)))
+    blocks.append(jnp.where(middle, facing[size:, :], rest_far[...]))
     for n, block in enumerate(blocks):
         out_ref[rows + n * size : rows + (n + 1) * size, :] = block
 
@@ -724,16 +737,18 @@
     got = swap_in_chip("early_gradients", give)
     piece = (keep + got.astype(F32)).astype(BF16)
     *late_side, _ = sides("late", 2, late_got, False, (3,), 0, [got])
-    cut = 3 * rank // 2
     pair = meet("early_gradients", piece, 1)
     facing = meet("early_gradients", piece, 3)
-    with jax.named_scope("early_lead_over_tm"):
-        far = lax.ppermute(piece[:cut], "tm", [(0, 2), (3, 1)])
     keep, *gives = head_group([late], band_width, [t_side, late_side], adapters, low, [piece])
     gives = [swap_in_chip("late_sums", g) for g in gives]
-    own_low, sends = hand_out(frames, rows, keep, gives, facing, [pair])
+    own_low, sends = hand_out(frames, rows, keep, gives, [pair])
     gots = [meet("late_sums", block, m) for m, block in enumerate(sends, 1)]
-    tail, low = collect(rest[1], own_low, sends[2], gots, piece, pair, far, facing)
+    lead_far, rest_far = relay(rest[1], piece, facing)
+    with jax.named_scope("relayed_over_tm"):
+        outward = [(1, 0), (2, 3)]
+        lead_far = lax.ppermute(lead_far, "tm", [(0, 2), (3, 1), *outward])
+        rest_far = lax.ppermute(rest_far, "tm", outward)
+    tail, low = collect(rest[1], own_low, sends[2], gots, piece, pair, facing, lead_far, rest_far)
     diag = [(0, 3), (1, 2), (2, 1), (3, 0)]
     with jax.named_scope("low_over_head"):
         low_head, low_diag = swap(low, "head"), lax.ppermute(low, ("head", "rep"), diag)

time: 68.2 us -> 69 us (1.012)
  starting transfers between devices: 28.2 us -> 29.3 us
    ppermute x12, waiting for transfers between devices: 19.8 us -> 16.9 us  [meet(): return lax.ppermute(block, 'tm', [(j ^ m, j) for j in targets])]
    ppermute x1 -> x2, waiting for transfers between devices: 3.45 us -> 5.09 us  [the longest x1 3.81 us: exchange_plan(): lead_far = lax.ppermute(lead_far, 'tm', [(0, 2), (3, 1), *outward])]
    ppermute x12, starting transfers between devices: 23.1 us -> 24 us  [meet(): return lax.ppermute(block, 'tm', [(j ^ m, j) for j in targets])]
    ppermute x8 -> x10, waiting for transfers between devices: 2.14 us -> 3 us  [swap(): return lax.ppermute(block, axis, [(0, 1), (1, 0)])]
    ppermute x8 -> x10, starting transfers between devices: 2.95 us -> 3.46 us  [swap(): return lax.ppermute(block, axis, [(0, 1), (1, 0)])]
    ppermute x1 -> x2, starting transfers between devices: 1.82 us -> 1.52 us  [the longest x1 1.28 us: exchange_plan(): rest_far = lax.ppermute(rest_far, 'tm', outward)]
  transfers between devices with their start and end apart: 22 -> 25, of which waited for: 8 -> 11; matrix products, arithmetic and copies ran while one was open for 0% -> 0% of each run, Pallas kernels for 11% -> 11%
where the time goes in v16:
time: 69 us; the launch traced here: 68.8 us
  starting transfers between devices  29.3 us (42%)
  waiting for transfers between devices  25.9 us (38%)
  Pallas kernels  11.9 us (17%)
  between operations  0.92 us (1%)
    ppermute x12, starting transfers between devices, meet(): return lax.ppermute(block, 'tm', [(j ^ m, j) for j in targets])  24 us
    ppermute x12, waiting for transfers between devices, meet(): return lax.ppermute(block, 'tm', [(j ^ m, j) for j in targets])  16.9 us
    pallas_call x2, Pallas kernels, head_group(): pl.pallas_call(functools.partial(group_kernel, heads, frames, chained, le...  6.71 us
    ppermute x1, waiting for transfers between devices, exchange_plan(): lead_far = lax.ppermute(lead_far, 'tm', [(0, 2), (3, 1), *outward])  3.81 us
    pallas_call x2, Pallas kernels, pack(): pl.pallas_call(functools.partial(pack_kernel, frames, outputs), in_specs=...  3.51 us
    ppermute x10, starting transfers between devices, swap(): return lax.ppermute(block, axis, [(0, 1), (1, 0)])  3.46 us
    ppermute x10, waiting for transfers between devices, swap(): return lax.ppermute(block, axis, [(0, 1), (1, 0)])  3 us
    pallas_call x1, Pallas kernels, place(): pl.pallas_call(functools.partial(place_kernel, frames, lead, late, rest),...  1.5 us
  transfers between devices with their start and end apart: 25, of which 11 were waited for; matrix products, arithmetic and copies ran while one was open for 0% of the time, Pallas kernels for 11%

profile of v16, /device:TPU:0, one launch (start us, length us, event | category | flops | bytes accessed | tf_op | source)
XLA Modules:
  0.0 68.8 jit_solution(8052475472073524992)
XLA Ops:
  0.7 2.6 %shard_map.121 = (bf16[128,1664]{1,0:T(8,128)(2,1)}, bf16[128,640]{1,0:T(8,128)(2,1)}, bf16[128,512]{1,0:T(8,128)(2,1)}, bf16[128,640]{1,0:T(8,128)(2,1)}, bf16[128,512]{1,0:T(8,128)(2,1)}) custom-call(bf16[128,1280]{1,0:T(8,128)(2,1)} %fq_ref.3, bf16[128,1280]{1,0:T(8,128)(2,1)} %do_ref.3, bf16[256,1280]{1,0:T(8,128)(2,1)} %fk_ref.3, ...), custom_call_target="tpu_custom_call" | custom-call | tf_op jit(solution)/shard_map/pallas_call | solution.py:303
  3.3 3.1 %collective-permute-start = (bf16[128,1664]{1,0:T(8,128)(2,1)}, bf16[128,1664]{1,0:T(8,128)(2,1)S(1)}, u32[]{:S(2)}, u32[]{:S(2)}) collective-permute-start(bf16[128,1664]{1,0:T(8,128)(2,1)} %get-tuple-element.37), channel_id=1, source_target_pairs={{4,0},{0,4},{12,8},{8,12},{5,1},{1,5},{13,9},{9,13},{6,2},{2,6},{1... | collective-permute-start | bytes 1277960 | tf_op jit(solution)/shard_map/nearest_over_tm/ppermute | solution.py:689
  6.3 2.6 %collective-permute-start.1 = (bf16[128,640]{1,0:T(8,128)(2,1)}, bf16[128,640]{1,0:T(8,128)(2,1)S(1)}, u32[]{:S(2)}, u32[]{:S(2)}) collective-permute-start(bf16[128,640]{1,0:T(8,128)(2,1)} %get-tuple-element.38), channel_id=1, source_target_pairs={{8,0},{12,4},{0,8},{4,12},{9,1},{13,5},{1,9},{5,13},{10,2},{14,6},... | collective-permute-start | bytes 491528 | tf_op jit(solution)/shard_map/lead_over_tm/ppermute | solution.py:689
  8.9 3.8 %collective-permute-start.6 = (bf16[128,512]{1,0:T(8,128)(2,1)}, bf16[128,512]{1,0:T(8,128)(2,1)S(1)}, u32[]{:S(2)}, u32[]{:S(2)}) collective-permute-start(bf16[128,512]{1,0:T(8,128)(2,1)} %get-tuple-element.48), channel_id=1, source_target_pairs={{12,4},{0,8},{13,5},{1,9},{14,6},{2,10},{15,7},{3,11},{28,20},{16,... | collective-permute-start | bytes 393224 | tf_op jit(solution)/shard_map/rest_over_tm/ppermute | solution.py:689
  12.8 0.7 collective-permute-start.7
  13.5 0.9 %shard_map.120 = (bf16[128,512]{1,0:T(8,128)(2,1)S(1)}, bf16[128,512]{1,0:T(8,128)(2,1)S(1)}, bf16[128,512]{1,0:T(8,128)(2,1)S(1)}, bf16[128,256]{1,0:T(8,128)(2...) custom-call(bf16[128,1280]{1,0:T(8,128)(2,1)S(1)} %copy-done.2, ...), custom_call_target="tpu_custom_call" | custom-call | tf_op jit(solution)/shard_map/pallas_call | solution.py:303
  14.4 6.0 %collective-permute-done.1.refs_1_.refs_3_ = bf16[128,640]{1,0:T(8,128)(2,1)S(1)} collective-permute-done((bf16[128,640]{1,0:T(8,128)(2,1)}, bf16[128,640]{1,0:T(8,128)(2,1)S(1)}, u32[]{:S(2)}, u32[]{:S(2)}) %collective-permute-start.1) | collective-permute-done | bytes 163872 | tf_op jit(solution)/shard_map/lead_over_tm/ppermute | solution.py:689
  20.4 6.4 %collective-permute-done.2.refs_2_.refs_4_ = bf16[128,640]{1,0:T(8,128)(2,1)S(1)} collective-permute-done((bf16[128,640]{1,0:T(8,128)(2,1)}, bf16[128,640]{1,0:T(8,128)(2,1)S(1)}, u32[]{:S(2)}, u32[]{:S(2)}) %collective-permute-start.2) | collective-permute-done | bytes 163872 | tf_op jit(solution)/shard_map/lead_over_tm/ppermute | solution.py:689
  27.0 0.5 collective-permute-start.8
  27.6 3.5 %collective-permute-start.4 = (bf16[128,512]{1,0:T(8,128)(2,1)S(1)}, bf16[128,512]{1,0:T(8,128)(2,1)S(1)}, u32[]{:S(2)}, u32[]{:S(2)}) collective-permute-start(bf16[128,512]{1,0:T(8,128)(2,1)S(1)} %get-tuple-element.43), channel_id=1, source_target_pairs={{8,0},{12,4},{0,8},{4,12},{9,1},{13,5},{1,9},{5,13},{10,2},{14,6},... | collective-permute-start | bytes 393224 | tf_op jit(solution)/shard_map/late_over_tm/ppermute | solution.py:689
  31.1 1.4 %collective-permute-start.5 = (bf16[128,512]{1,0:T(8,128)(2,1)S(1)}, bf16[128,512]{1,0:T(8,128)(2,1)S(1)}, u32[]{:S(2)}, u32[]{:S(2)}) collective-permute-start(bf16[128,512]{1,0:T(8,128)(2,1)S(1)} %get-tuple-element.44), channel_id=1, source_target_pairs={{12,0},{8,4},{4,8},{0,12},{13,1},{9,5},{5,9},{1,13},{14,2},{10,6},... | collective-permute-start | bytes 393224 | tf_op jit(solution)/shard_map/late_over_tm/ppermute | solution.py:689
  32.4 0.6 copy-done.8
  33.1 3.4 %shard_map.124 = (f32[384,128]{1,0:T(8,128)S(1)}, bf16[384,128]{1,0:T(8,128)(2,1)S(1)}, f32[512,128]{1,0:T(8,128)S(1)}, f32[512,128]{1,0:T(8,128)S(1)}) custom-call(s32[4,4]{1,0:T(4,128)S(1)} %copy-done.8, bf16[128,128]{1,0:T(8,128)(2,1)S(1)} %get-tuple-element.36.refs_1_, bf16[128,1664]{1,0:T(8,128)(2,1)S(1)} %collective-permute-done.refs_0_.refs_2_, ...), custom_call_target="tpu_custom_call" | custom-call | tf_op jit(solution)/shard_map/pallas_call | solution.py:523
  36.5 4.5 %collective-permute-done.4.refs_1_.refs_8_ = bf16[128,512]{1,0:T(8,128)(2,1)S(1)} collective-permute-done((bf16[128,512]{1,0:T(8,128)(2,1)S(1)}, bf16[128,512]{1,0:T(8,128)(2,1)S(1)}, u32[]{:S(2)}, u32[]{:S(2)}) %collective-permute-start.4) | collective-permute-done | bytes 131104 | tf_op jit(solution)/shard_map/late_over_tm/ppermute | solution.py:689
  41.2 3.2 %collective-permute-start.15 = (bf16[384,128]{1,0:T(8,128)(2,1)S(1)}, bf16[384,128]{1,0:T(8,128)(2,1)S(1)}, u32[]{:S(2)}, u32[]{:S(2)}) collective-permute-start(bf16[384,128]{1,0:T(8,128)(2,1)S(1)} %add_convert_fusion.refs_17_.piece), channel_id=1, source_target_pairs={{4,0},{0,4},{12,8},{8,12},{5,1},{1,5},{13,9},{9,13},{6,2},{2,6},{1... | collective-permute-start | bytes 294920 | tf_op jit(solution)/shard_map/early_gradients_over_tm/ppermute | solution.py:689
  44.3 1.4 %collective-permute-start.19 = (bf16[384,128]{1,0:T(8,128)(2,1)S(1)}, bf16[384,128]{1,0:T(8,128)(2,1)S(1)}, u32[]{:S(2)}, u32[]{:S(2)}) collective-permute-start(bf16[384,128]{1,0:T(8,128)(2,1)S(1)} %add_convert_fusion.refs_17_.piece), channel_id=1, source_target_pairs={{12,0},{8,4},{4,8},{0,12},{13,1},{9,5},{5,9},{1,13},{14,2},{10,6},... | collective-permute-start | bytes 294920 | tf_op jit(solution)/shard_map/early_gradients_over_tm/ppermute | solution.py:689
  45.7 3.3 %shard_map.126 = (f32[704,128]{1,0:T(8,128)S(1)}, bf16[176,128]{1,0:T(8,128)(2,1)S(1)}, bf16[176,128]{1,0:T(8,128)(2,1)S(1)}, bf16[176,128]{1,0:T(8,128)(2,1)S(1)}, bf16[176,128]{1,0:T(8,128)(2,1)S(1)}) custom-call(s32[4,4]{1,0:T(4,128)S(1)} %copy-done.8, bf16[128,128]{1,0:T(8,128)(2,1)S(1)} %get-tuple-element.36.refs_1_, ...), custom_call_target="tpu_custom_call" | custom-call | tf_op jit(solution)/shard_map/pallas_call | solution.py:523
  49.1 0.5 collective-permute-start.12
  49.7 0.4 collective-permute-start.14
  50.5 0.3 collective-permute-done.13.refs_2_
  51.1 0.3 collective-permute-start.16
  51.4 2.8 %collective-permute-start.17 = (bf16[320,128]{1,0:T(8,128)(2,1)S(1)}, bf16[320,128]{1,0:T(8,128)(2,1)S(1)}, u32[]{:S(2)}, u32[]{:S(2)}) collective-permute-start(bf16[320,128]{1,0:T(8,128)(2,1)S(1)} %get-tuple-element.63), channel_id=1, source_target_pairs={{8,0},{12,4},{0,8},{4,12},{9,1},{13,5},{1,9},{5,13},{10,2},{14,6},... | collective-permute-start | bytes 245768 | tf_op jit(solution)/shard_map/late_sums_over_tm/ppermute | solution.py:689
  54.2 1.4 %collective-permute-start.18 = (bf16[320,128]{1,0:T(8,128)(2,1)S(1)}, bf16[320,128]{1,0:T(8,128)(2,1)S(1)}, u32[]{:S(2)}, u32[]{:S(2)}) collective-permute-start(bf16[320,128]{1,0:T(8,128)(2,1)S(1)} %get-tuple-element.61.own), channel_id=1, source_target_pairs={{12,0},{8,4},{4,8},{0,12},{13,1},{9,5},{5,9},{1,13},{14,2},{10,6},... | collective-permute-start | bytes 245768 | tf_op jit(solution)/shard_map/late_sums_over_tm/ppermute | solution.py:689
  55.6 0.2 collective-permute-start.20
  55.8 1.3 %collective-permute-start.21 = (bf16[192,128]{1,0:T(8,128)(2,1)S(1)}, bf16[192,128]{1,0:T(8,128)(2,1)S(1)}, u32[]{:S(2)}, u32[]{:S(2)}) collective-permute-start(bf16[192,128]{1,0:T(8,128)(2,1)S(1)} %get-tuple-element.65), channel_id=1, source_target_pairs={{4,0},{8,12},{5,1},{9,13},{6,2},{10,14},{7,3},{11,15},{20,16},{24,... | collective-permute-start | bytes 147464 | tf_op jit(solution)/shard_map/relayed_over_tm/ppermute | solution.py:750
  57.1 3.8 %collective-permute-done.20.lead_far = bf16[192,128]{1,0:T(8,128)(2,1)S(1)} collective-permute-done((bf16[192,128]{1,0:T(8,128)(2,1)S(1)}, bf16[192,128]{1,0:T(8,128)(2,1)S(1)}, u32[]{:S(2)}, u32[]{:S(2)}) %collective-permute-start.20) | collective-permute-done | bytes 49184 | tf_op jit(solution)/shard_map/relayed_over_tm/ppermute | solution.py:749
  60.9 1.3 %collective-permute-done.21.rest_far = bf16[192,128]{1,0:T(8,128)(2,1)S(1)} collective-permute-done((bf16[192,128]{1,0:T(8,128)(2,1)S(1)}, bf16[192,128]{1,0:T(8,128)(2,1)S(1)}, u32[]{:S(2)}, u32[]{:S(2)}) %collective-permute-start.21) | collective-permute-done | bytes 49184 | tf_op jit(solution)/shard_map/relayed_over_tm/ppermute | solution.py:750
  62.4 1.6 %collective-permute-start.23 = (bf16[128,128]{1,0:T(8,128)(2,1)S(1)}, bf16[128,128]{1,0:T(8,128)(2,1)S(1)}, u32[]{:S(2)}, u32[]{:S(2)}) collective-permute-start(bf16[128,128]{1,0:T(8,128)(2,1)S(1)} %get-tuple-element.67), channel_id=1, source_target_pairs={{0,2},{2,0},{1,3},{3,1},{4,6},{6,4},{5,7},{7,5},{8,10},{10,8},{9,1... | collective-permute-start | bytes 98312 | tf_op jit(solution)/shard_map/low_over_head/ppermute | solution.py:50
  63.9 0.3 collective-permute-start.24
  64.2 2.1 %collective-permute-done.23.low_head = bf16[128,128]{1,0:T(8,128)(2,1)S(1)} collective-permute-done((bf16[128,128]{1,0:T(8,128)(2,1)S(1)}, bf16[128,128]{1,0:T(8,128)(2,1)S(1)}, u32[]{:S(2)}, u32[]{:S(2)}) %collective-permute-start.23) | collective-permute-done | bytes 32800 | tf_op jit(solution)/shard_map/low_over_head/ppermute | solution.py:50
  66.3 0.9 %collective-permute-done.24.low_diag = bf16[128,128]{1,0:T(8,128)(2,1)S(1)} collective-permute-done((bf16[128,128]{1,0:T(8,128)(2,1)S(1)}, bf16[128,128]{1,0:T(8,128)(2,1)S(1)}, u32[]{:S(2)}, u32[]{:S(2)}) %collective-permute-start.24) | collective-permute-done | bytes 32800 | tf_op jit(solution)/shard_map/low_over_head/ppermute | solution.py:754
  67.3 1.5 %shard_map.130 = (f32[128,1280]{1,0:T(8,128)}, f32[128,1280]{1,0:T(8,128)}, f32[128,1280]{1,0:T(8,128)}, f32[256,128]{1,0:T(8,128)}) custom-call(bf16[2048,128]{1,0:T(8,128)(2,1)S(1)} %get-tuple-element.66.tail, bf16[2048,128]{1,0:T(8,128)(2,1)S(1)} %collective-permute-done.22.tail2, bf16[128,128]{1,0:T(8,128)(2,1)S(1)} %collective-permute-done.23.low_head, ...), custom_call_target="tpu_custom_call" | custom-call | tf_op jit(solution)/shard_map/pallas_call | solution.py:652
  (48 shorter events, 1.3 us)
Async XLA Ops:
  0.6 12.8 %copy-start.2 = (bf16[128,1280]{1,0:T(8,128)(2,1)S(1)}, bf16[128,1280]{1,0:T(8,128)(2,1)}, u32[]{:S(2)}) copy-start(bf16[128,1280]{1,0:T(8,128)(2,1)} %fq_ref.3) | copy-start | bytes 983044
  0.6 12.8 %copy-start.3 = (bf16[128,1280]{1,0:T(8,128)(2,1)S(1)}, bf16[128,1280]{1,0:T(8,128)(2,1)}, u32[]{:S(2)}) copy-start(bf16[128,1280]{1,0:T(8,128)(2,1)} %do_ref.3) | copy-start | bytes 983044
  0.7 12.8 %copy-start = (bf16[256,1280]{1,0:T(8,128)(2,1)S(1)}, bf16[256,1280]{1,0:T(8,128)(2,1)}, u32[]{:S(2)}) copy-start(bf16[256,1280]{1,0:T(8,128)(2,1)} %fk_ref.3) | copy-start | bytes 1966084
  0.7 12.8 %copy-start.1 = (bf16[256,1280]{1,0:T(8,128)(2,1)S(1)}, bf16[256,1280]{1,0:T(8,128)(2,1)}, u32[]{:S(2)}) copy-start(bf16[256,1280]{1,0:T(8,128)(2,1)} %fv_ref.3) | copy-start | bytes 1966084
  0.7 12.8 %copy-start.7 = (bf16[256,128]{1,0:T(8,128)(2,1)S(1)}, bf16[256,128]{1,0:T(8,128)(2,1)}, u32[]{:S(2)}) copy-start(bf16[256,128]{1,0:T(8,128)(2,1)} %t_ref.3) | copy-start | bytes 196612
  3.3 23.6 %collective-permute-start = (bf16[128,1664]{1,0:T(8,128)(2,1)}, bf16[128,1664]{1,0:T(8,128)(2,1)S(1)}, u32[]{:S(2)}, u32[]{:S(2)}) collective-permute-start(bf16[128,1664]{1,0:T(8,128)(2,1)} %get-tuple-element.37), channel_id=1, source_target_pairs={{4,0},{0,4},{12,8},{8,12},{5,1},{1,5},{13,9},{9,13},{6,2},{2,6},{1... | collective-permute-start | bytes 1277960 | tf_op jit(solution)/shard_map/nearest_over_tm/ppermute | solution.py:689
  6.3 14.1 %collective-permute-start.1 = (bf16[128,640]{1,0:T(8,128)(2,1)}, bf16[128,640]{1,0:T(8,128)(2,1)S(1)}, u32[]{:S(2)}, u32[]{:S(2)}) collective-permute-start(bf16[128,640]{1,0:T(8,128)(2,1)} %get-tuple-element.38), channel_id=1, source_target_pairs={{8,0},{12,4},{0,8},{4,12},{9,1},{13,5},{1,9},{5,13},{10,2},{14,6},... | collective-permute-start | bytes 491528 | tf_op jit(solution)/shard_map/lead_over_tm/ppermute | solution.py:689
  8.9 17.9 %collective-permute-start.2 = (bf16[128,640]{1,0:T(8,128)(2,1)}, bf16[128,640]{1,0:T(8,128)(2,1)S(1)}, u32[]{:S(2)}, u32[]{:S(2)}) collective-permute-start(bf16[128,640]{1,0:T(8,128)(2,1)} %get-tuple-element.39), channel_id=1, source_target_pairs={{12,0},{8,4},{4,8},{0,12},{13,1},{9,5},{5,9},{1,13},{14,2},{10,6},... | collective-permute-start | bytes 491528 | tf_op jit(solution)/shard_map/lead_over_tm/ppermute | solution.py:689
  8.9 18.0 %collective-permute-start.6 = (bf16[128,512]{1,0:T(8,128)(2,1)}, bf16[128,512]{1,0:T(8,128)(2,1)S(1)}, u32[]{:S(2)}, u32[]{:S(2)}) collective-permute-start(bf16[128,512]{1,0:T(8,128)(2,1)} %get-tuple-element.48), channel_id=1, source_target_pairs={{12,4},{0,8},{13,5},{1,9},{14,6},{2,10},{15,7},{3,11},{28,20},{16,... | collective-permute-start | bytes 393224 | tf_op jit(solution)/shard_map/rest_over_tm/ppermute | solution.py:689
  12.8 14.2 %collective-permute-start.7 = (bf16[128,512]{1,0:T(8,128)(2,1)}, bf16[128,512]{1,0:T(8,128)(2,1)S(1)}, u32[]{:S(2)}, u32[]{:S(2)}) collective-permute-start(bf16[128,512]{1,0:T(8,128)(2,1)} %get-tuple-element.49), channel_id=1, source_target_pairs={{8,4},{4,8},{9,5},{5,9},{10,6},{6,10},{11,7},{7,11},{24,20},{20,24... | collective-permute-start | bytes 393224 | tf_op jit(solution)/shard_map/rest_over_tm/ppermute | solution.py:689
  26.8 5.6 %copy-start.6 = (bf16[128,1280]{1,0:T(8,128)(2,1)S(1)}, bf16[128,1280]{1,0:T(8,128)(2,1)}, u32[]{:S(2)}) copy-start(bf16[128,1280]{1,0:T(8,128)(2,1)} %refs_14_.3) | copy-start | bytes 983044
  26.9 5.6 %copy-start.4 = (bf16[128,1280]{1,0:T(8,128)(2,1)S(1)}, bf16[128,1280]{1,0:T(8,128)(2,1)}, u32[]{:S(2)}) copy-start(bf16[128,1280]{1,0:T(8,128)(2,1)} %refs_12_.1) | copy-start | bytes 983044
  26.9 5.5 %collective-permute-start.3 = (bf16[128,1152]{1,0:T(8,128)(2,1)S(1)}, bf16[128,1152]{1,0:T(8,128)(2,1)S(1)}, u32[]{:S(2)}, u32[]{:S(2)}) collective-permute-start(bf16[128,1152]{1,0:T(8,128)(2,1)S(1)} %shard_map.122), channel_id=1, source_target_pairs={{0,1},{1,0},{2,3},{3,2},{4,5},{5,4},{6,7},{7,6},{8,9},{9,8},{10,11... | collective-permute-start | bytes 884744 | tf_op jit(solution)/shard_map/lead_in_chip/ppermute | solution.py:50
  27.0 5.4 %collective-permute-start.8 = (bf16[128,768]{1,0:T(8,128)(2,1)S(1)}, bf16[128,768]{1,0:T(8,128)(2,1)S(1)}, u32[]{:S(2)}, u32[]{:S(2)}) collective-permute-start(bf16[128,768]{1,0:T(8,128)(2,1)S(1)} %shard_map.123), channel_id=1, source_target_pairs={{0,1},{1,0},{2,3},{3,2},{4,5},{5,4},{6,7},{7,6},{8,9},{9,8},{10,11... | collective-permute-start | bytes 589832 | tf_op jit(solution)/shard_map/rest_in_chip/ppermute | solution.py:50
  27.6 13.5 %collective-permute-start.4 = (bf16[128,512]{1,0:T(8,128)(2,1)S(1)}, bf16[128,512]{1,0:T(8,128)(2,1)S(1)}, u32[]{:S(2)}, u32[]{:S(2)}) collective-permute-start(bf16[128,512]{1,0:T(8,128)(2,1)S(1)} %get-tuple-element.43), channel_id=1, source_target_pairs={{8,0},{12,4},{0,8},{4,12},{9,1},{13,5},{1,9},{5,13},{10,2},{14,6},... | collective-permute-start | bytes 393224 | tf_op jit(solution)/shard_map/late_over_tm/ppermute | solution.py:689
  31.1 10.0 %collective-permute-start.5 = (bf16[128,512]{1,0:T(8,128)(2,1)S(1)}, bf16[128,512]{1,0:T(8,128)(2,1)S(1)}, u32[]{:S(2)}, u32[]{:S(2)}) collective-permute-start(bf16[128,512]{1,0:T(8,128)(2,1)S(1)} %get-tuple-element.44), channel_id=1, source_target_pairs={{12,0},{8,4},{4,8},{0,12},{13,1},{9,5},{5,9},{1,13},{14,2},{10,6},... | collective-permute-start | bytes 393224 | tf_op jit(solution)/shard_map/late_over_tm/ppermute | solution.py:689
  36.5 4.6 %collective-permute-start.9 = (bf16[384,128]{1,0:T(8,128)(2,1)S(1)}, bf16[384,128]{1,0:T(8,128)(2,1)S(1)}, u32[]{:S(2)}, u32[]{:S(2)}) collective-permute-start(bf16[384,128]{1,0:T(8,128)(2,1)S(1)} %get-tuple-element.51), channel_id=1, source_target_pairs={{0,1},{1,0},{2,3},{3,2},{4,5},{5,4},{6,7},{7,6},{8,9},{9,8},{10,11... | collective-permute-start | bytes 294920 | tf_op jit(solution)/shard_map/early_gradients_in_chip/ppermute | solution.py:50
  41.1 4.6 %collective-permute-start.10 = (bf16[128,1536]{1,0:T(8,128)(2,1)S(1)}, bf16[128,1536]{1,0:T(8,128)(2,1)S(1)}, u32[]{:S(2)}, u32[]{:S(2)}) collective-permute-start(bf16[128,1536]{1,0:T(8,128)(2,1)S(1)} %shard_map.125), channel_id=1, source_target_pairs={{0,1},{1,0},{2,3},{3,2},{4,5},{5,4},{6,7},{7,6},{8,9},{9,8},{10,11... | collective-permute-start | bytes 1179656 | tf_op jit(solution)/shard_map/late_in_chip/ppermute | solution.py:50
  41.2 8.5 %collective-permute-start.15 = (bf16[384,128]{1,0:T(8,128)(2,1)S(1)}, bf16[384,128]{1,0:T(8,128)(2,1)S(1)}, u32[]{:S(2)}, u32[]{:S(2)}) collective-permute-start(bf16[384,128]{1,0:T(8,128)(2,1)S(1)} %add_convert_fusion.refs_17_.piece), channel_id=1, source_target_pairs={{4,0},{0,4},{12,8},{8,12},{5,1},{1,5},{13,9},{9,13},{6,2},{2,6},{1... | collective-permute-start | bytes 294920 | tf_op jit(solution)/shard_map/early_gradients_over_tm/ppermute | solution.py:689
  44.3 11.2 %collective-permute-start.19 = (bf16[384,128]{1,0:T(8,128)(2,1)S(1)}, bf16[384,128]{1,0:T(8,128)(2,1)S(1)}, u32[]{:S(2)}, u32[]{:S(2)}) collective-permute-start(bf16[384,128]{1,0:T(8,128)(2,1)S(1)} %add_convert_fusion.refs_17_.piece), channel_id=1, source_target_pairs={{12,0},{8,4},{4,8},{0,12},{13,1},{9,5},{5,9},{1,13},{14,2},{10,6},... | collective-permute-start | bytes 294920 | tf_op jit(solution)/shard_map/early_gradients_over_tm/ppermute | solution.py:689
  49.1 1.3 %collective-permute-start.11 = (bf16[176,128]{1,0:T(8,128)(2,1)S(1)}, bf16[176,128]{1,0:T(8,128)(2,1)S(1)}, u32[]{:S(2)}, u32[]{:S(2)}) collective-permute-start(bf16[176,128]{1,0:T(8,128)(2,1)S(1)} %get-tuple-element.56), channel_id=1, source_target_pairs={{0,1},{1,0},{2,3},{3,2},{4,5},{5,4},{6,7},{7,6},{8,9},{9,8},{10,11... | collective-permute-start | bytes 135176 | tf_op jit(solution)/shard_map/late_sums_in_chip/ppermute | solution.py:50
  49.1 1.4 %collective-permute-start.12 = (bf16[176,128]{1,0:T(8,128)(2,1)S(1)}, bf16[176,128]{1,0:T(8,128)(2,1)S(1)}, u32[]{:S(2)}, u32[]{:S(2)}) collective-permute-start(bf16[176,128]{1,0:T(8,128)(2,1)S(1)} %get-tuple-element.57), channel_id=1, source_target_pairs={{0,1},{1,0},{2,3},{3,2},{4,5},{5,4},{6,7},{7,6},{8,9},{9,8},{10,11... | collective-permute-start | bytes 135176 | tf_op jit(solution)/shard_map/late_sums_in_chip/ppermute | solution.py:50
  49.6 1.2 %collective-permute-start.13 = (bf16[176,128]{1,0:T(8,128)(2,1)S(1)}, bf16[176,128]{1,0:T(8,128)(2,1)S(1)}, u32[]{:S(2)}, u32[]{:S(2)}) collective-permute-start(bf16[176,128]{1,0:T(8,128)(2,1)S(1)} %get-tuple-element.58), channel_id=1, source_target_pairs={{0,1},{1,0},{2,3},{3,2},{4,5},{5,4},{6,7},{7,6},{8,9},{9,8},{10,11... | collective-permute-start | bytes 135176 | tf_op jit(solution)/shard_map/late_sums_in_chip/ppermute | solution.py:50
  49.7 1.3 %collective-permute-start.14 = (bf16[176,128]{1,0:T(8,128)(2,1)S(1)}, bf16[176,128]{1,0:T(8,128)(2,1)S(1)}, u32[]{:S(2)}, u32[]{:S(2)}) collective-permute-start(bf16[176,128]{1,0:T(8,128)(2,1)S(1)} %get-tuple-element.59), channel_id=1, source_target_pairs={{0,1},{1,0},{2,3},{3,2},{4,5},{5,4},{6,7},{7,6},{8,9},{9,8},{10,11... | collective-permute-start | bytes 135176 | tf_op jit(solution)/shard_map/late_sums_in_chip/ppermute | solution.py:50
  51.1 11.1 %collective-permute-start.16 = (bf16[320,128]{1,0:T(8,128)(2,1)S(1)}, bf16[320,128]{1,0:T(8,128)(2,1)S(1)}, u32[]{:S(2)}, u32[]{:S(2)}) collective-permute-start(bf16[320,128]{1,0:T(8,128)(2,1)S(1)} %get-tuple-element.62), channel_id=1, source_target_pairs={{4,0},{0,4},{12,8},{8,12},{5,1},{1,5},{13,9},{9,13},{6,2},{2,6},{1... | collective-permute-start | bytes 245768 | tf_op jit(solution)/shard_map/late_sums_over_tm/ppermute | solution.py:689
  51.4 10.8 %collective-permute-start.17 = (bf16[320,128]{1,0:T(8,128)(2,1)S(1)}, bf16[320,128]{1,0:T(8,128)(2,1)S(1)}, u32[]{:S(2)}, u32[]{:S(2)}) collective-permute-start(bf16[320,128]{1,0:T(8,128)(2,1)S(1)} %get-tuple-element.63), channel_id=1, source_target_pairs={{8,0},{12,4},{0,8},{4,12},{9,1},{13,5},{1,9},{5,13},{10,2},{14,6},... | collective-permute-start | bytes 245768 | tf_op jit(solution)/shard_map/late_sums_over_tm/ppermute | solution.py:689
  54.2 8.0 %collective-permute-start.18 = (bf16[320,128]{1,0:T(8,128)(2,1)S(1)}, bf16[320,128]{1,0:T(8,128)(2,1)S(1)}, u32[]{:S(2)}, u32[]{:S(2)}) collective-permute-start(bf16[320,128]{1,0:T(8,128)(2,1)S(1)} %get-tuple-element.61.own), channel_id=1, source_target_pairs={{12,0},{8,4},{4,8},{0,12},{13,1},{9,5},{5,9},{1,13},{14,2},{10,6},... | collective-permute-start | bytes 245768 | tf_op jit(solution)/shard_map/late_sums_over_tm/ppermute | solution.py:689
  55.6 5.3 %collective-permute-start.20 = (bf16[192,128]{1,0:T(8,128)(2,1)S(1)}, bf16[192,128]{1,0:T(8,128)(2,1)S(1)}, u32[]{:S(2)}, u32[]{:S(2)}) collective-permute-start(bf16[192,128]{1,0:T(8,128)(2,1)S(1)} %get-tuple-element.64), channel_id=1, source_target_pairs={{0,8},{12,4},{4,0},{8,12},{1,9},{13,5},{5,1},{9,13},{2,10},{14,6},... | collective-permute-start | bytes 147464 | tf_op jit(solution)/shard_map/relayed_over_tm/ppermute | solution.py:749
  55.8 6.4 %collective-permute-start.21 = (bf16[192,128]{1,0:T(8,128)(2,1)S(1)}, bf16[192,128]{1,0:T(8,128)(2,1)S(1)}, u32[]{:S(2)}, u32[]{:S(2)}) collective-permute-start(bf16[192,128]{1,0:T(8,128)(2,1)S(1)} %get-tuple-element.65), channel_id=1, source_target_pairs={{4,0},{8,12},{5,1},{9,13},{6,2},{10,14},{7,3},{11,15},{20,16},{24,... | collective-permute-start | bytes 147464 | tf_op jit(solution)/shard_map/relayed_over_tm/ppermute | solution.py:750
  62.3 5.0 %collective-permute-start.22 = (bf16[2048,128]{1,0:T(8,128)(2,1)S(1)}, bf16[2048,128]{1,0:T(8,128)(2,1)S(1)}, u32[]{:S(2)}, u32[]{:S(2)}) collective-permute-start(bf16[2048,128]{1,0:T(8,128)(2,1)S(1)} %get-tuple-element.66.tail), channel_id=1, source_target_pairs={{0,1},{1,0},{2,3},{3,2},{4,5},{5,4},{6,7},{7,6},{8,9},{9,8},{10,11... | collective-permute-start | bytes 1572872 | tf_op jit(solution)/shard_map/tail_in_chip/ppermute | solution.py:50
  62.4 4.0 %collective-permute-start.23 = (bf16[128,128]{1,0:T(8,128)(2,1)S(1)}, bf16[128,128]{1,0:T(8,128)(2,1)S(1)}, u32[]{:S(2)}, u32[]{:S(2)}) collective-permute-start(bf16[128,128]{1,0:T(8,128)(2,1)S(1)} %get-tuple-element.67), channel_id=1, source_target_pairs={{0,2},{2,0},{1,3},{3,1},{4,6},{6,4},{5,7},{7,5},{8,10},{10,8},{9,1... | collective-permute-start | bytes 98312 | tf_op jit(solution)/shard_map/low_over_head/ppermute | solution.py:50
  63.9 3.3 %collective-permute-start.24 = (bf16[128,128]{1,0:T(8,128)(2,1)S(1)}, bf16[128,128]{1,0:T(8,128)(2,1)S(1)}, u32[]{:S(2)}, u32[]{:S(2)}) collective-permute-start(bf16[128,128]{1,0:T(8,128)(2,1)S(1)} %get-tuple-element.67), channel_id=1, source_target_pairs={{0,3},{1,2},{2,1},{3,0},{4,7},{5,6},{6,5},{7,4},{8,11},{9,10},{10,... | collective-permute-start | bytes 98312 | tf_op jit(solution)/shard_map/low_over_head/ppermute | solution.py:754
  (2 other events, 6.2 us)

commit v17 on v12

--- a/solution.py
+++ b/solution.py
@@ -1,4 +1,5 @@
 import functools
+import math
 
 import jax
 import jax.numpy as jnp
@@ -11,6 +12,7 @@
 NEAR = 1
 REACH = 4
 SCALE = DH ** (-0.5)
+SCALE_2 = SCALE * math.log2(math.e)
 F32 = jnp.float32
 BF16 = jnp.bfloat16
 GIVES = 2
@@ -373,11 +375,11 @@
 
     def softmax(g, raw):
         scores = [
-            block(raw, n) * SCALE + jnp.concatenate([bias(i, b) for i in groups[g]], axis=1)
+            block(raw, n) * SCALE_2 + jnp.concatenate([bias(i, b) for i in groups[g]], axis=1)
             for n, b in enumerate(seen[g])
         ]
         top = jnp.max(functools.reduce(jnp.maximum, scores), axis=0, keepdims=True)
-        shifted = [jnp.exp(s - top) for s in scores]
+        shifted = [jnp.exp2(s - top) for s in scores]
         inverse = 1.0 / jnp.sum(functools.reduce(jnp.add, shifted), axis=0, keepdims=True)
         return [s * inverse for s in shifted]
 
@@ -533,8 +535,8 @@
 
 
 def hand_out_kernel(frames, size, parts, keep_ref, *refs):
-    gots, (piece, facing) = refs[:parts], refs[parts : parts + 2]
-    own_low, own_late, near, last, low_third, third, total = refs[-7:]
+    gots, facing = refs[:parts], refs[parts]
+    own_low, own_late, near, low_third, low_last, total = refs[-6:]
     me = lax.axis_index("tm")
     rows = own_low.shape[0]
     total[...] = keep_ref[...] + jnp.concatenate([got[...].astype(F32) for got in gots], axis=0)
@@ -547,31 +549,44 @@
     own_late[...] = late
     near[:rows, :] = low(1).astype(BF16)
     near[rows : rows + size, :] = late
-    near[rows + size :, :] = facing[size:, :]
+    near[rows + size :, :] = facing[...]
     low_third[...] = low(2).astype(BF16)
-    last[:rows, :] = low(3).astype(BF16)
-    last[rows:, :] = late
-    third[:size, :] = late
-    third[size:, :] = piece[:size, :]
-
-
-def hand_out(frames, rows, keep, gots, piece, facing, after):
+    low_last[...] = low(3).astype(BF16)
+
+
+def hand_out(frames, rows, keep, gots, facing, after):
     size, rank = keep.shape[0] - frames * rows, keep.shape[1]
-    sizes = (size, rows + 2 * size, rows + size, rows, 2 * size)
     return pl.pallas_call(
         functools.partial(hand_out_kernel, frames, size, len(gots)),
-        in_specs=vmem(3 + len(gots)) + [pl.BlockSpec(memory_space=pl.ANY)] * len(after),
-        out_specs=vmem(1 + len(sizes)),
+        in_specs=vmem(2 + len(gots)) + [pl.BlockSpec(memory_space=pl.ANY)] * len(after),
+        out_specs=vmem(5),
         out_shape=[jax.ShapeDtypeStruct((rows, rank), F32)]
-        + [jax.ShapeDtypeStruct((n, rank), BF16) for n in sizes],
+        + [jax.ShapeDtypeStruct((n, rank), BF16) for n in (size, rows + 3 * size, rows, rows)],
         scratch_shapes=[pltpu.VMEM(keep.shape, F32)],
         compiler_params=SMALL,
-    )(keep, *gots, piece, facing, *after)
+    )(keep, *gots, facing, *after)
+
+
+def hold_kernel(late, piece, *refs):
+    late_out, lead_out = refs[-2:]
+    late_out[...] = late[...]
+    lead_out[...] = piece[: lead_out.shape[0], :]
+
+
+def hold(late, piece, after):
+    return pl.pallas_call(
+        hold_kernel,
+        in_specs=vmem(2) + [pl.BlockSpec(memory_space=pl.ANY)] * len(after),
+        out_specs=vmem(2),
+        out_shape=[jax.ShapeDtypeStruct(late.shape, late.dtype)] * 2,
+        compiler_params=SMALL,
+    )(late, piece, *after)
 
 
 def sum_low_kernel(own, near, third, last, out):
     rows = own.shape[0]
-    out[...] = own[...] + near[:rows, :].astype(F32) + third[...].astype(F32) + last[:rows, :].astype(F32)
+    low = own[...] + near[:rows, :].astype(F32) + third[...].astype(F32) + last[...].astype(F32)
+    out[...] = low.astype(BF16)
 
 
 def sum_low(own, near, third, last):
@@ -579,19 +594,23 @@
         sum_low_kernel,
         in_specs=vmem(4),
         out_specs=pl.BlockSpec(memory_space=pltpu.VMEM),
-        out_shape=jax.ShapeDtypeStruct(own.shape, F32),
+        out_shape=jax.ShapeDtypeStruct(own.shape, BF16),
         compiler_params=SMALL,
     )(own, near, third, last)
 
 
-def collect_kernel(wide, low_ref, low_head, own, near, third, last, piece, pair, facing, out_ref):
-    rows, size = low_ref.shape[0], own.shape[0]
-    out_ref[:rows, :] = (low_ref[...] + low_head[...]).astype(BF16)
+def collect_kernel(wide, low, low_head, own, near, third, last, piece, pair, far, facing, out_ref):
+    rows, size = low.shape[0], own.shape[0]
+    out_ref[:rows, :] = (low[...].astype(F32) + low_head[...].astype(F32)).astype(BF16)
     middle = lookup(wide, lax.axis_index("tm")) > 0
-    blocks = [own[...], near[rows : rows + size, :], third[:size, :], last[rows:, :]]
-    blocks += [piece[:size, :], pair[:size, :], third[size:, :], facing[:size, :]]
+
+    def part(n):
+        return near[rows + n * size : rows + (n + 1) * size, :]
+
+    blocks = [own[...], part(0), third[...], last[...], piece[:size, :], pair[:size, :]]
+    blocks += [jnp.where(middle, far[...], part(1)), facing[:size, :]]
     blocks.append(jnp.where(middle, piece[size:, :], pair[size:, :]))
-    blocks.append(jnp.where(middle, facing[size:, :], near[rows + size :, :]))
+    blocks.append(jnp.where(middle, facing[size:, :], part(2)))
     for n, block in enumerate(blocks):
         out_ref[rows + n * size : rows + (n + 1) * size, :] = block
 
@@ -719,17 +738,19 @@
     *late_side, _ = sides("late", 2, late_got, False, (3,), 0, [got])
     pair = meet("early_gradients", piece, 1)
     facing = meet("early_gradients", piece, 3)
-    keep, *gives = head_group([late], band_width, [t_side, late_side], adapters, low, [])
+    keep, *gives = head_group([late], band_width, [t_side, late_side], adapters, low, [piece])
     gives = [swap_in_chip("late_sums", g) for g in gives]
-    own_low, own, near, last, low_third, third = hand_out(
-        frames, rows, keep, gives, piece, facing, [pair]
-    )
-    near, last = meet("late_sums", near, 1), meet("late_sums", last, 3)
-    low = sum_low(own_low, near, meet("low", low_third, 2), last)
-    third = meet("late_gradients", third, 2)
+    own_low, own, near, low_third, low_last = hand_out(frames, rows, keep, gives, facing, [pair])
+    near = meet("late_sums", near, 1)
+    low_third, low_last = meet("low", low_third, 2), meet("low", low_last, 3)
+    held, lead_held = hold(own, piece, [low_third, low_last])
+    third, last = meet("late_gradients", held, 2), meet("late_gradients", held, 3)
+    with jax.named_scope("early_lead_over_tm"):
+        far = lax.ppermute(lead_held, "tm", [(0, 2), (3, 1)])
+    low = sum_low(own_low, near, low_third, low_last)
     with jax.named_scope("low_over_head"):
         low_head = swap(low, "head")
-    tail = collect(rest[1], low, low_head, own, near, third, last, piece, pair, facing)
+    tail = collect(rest[1], low, low_head, own, near, third, last, piece, pair, far, facing)
     outs = place(
         frames, lead[0], late[0], rest[0], tail, swap_in_chip("tail", tail), rows, rank, width
     )

time: 71 us -> 72.7 us (1.024)
  starting transfers between devices: 27.8 us -> 32.2 us
  waiting for transfers between devices: 29.3 us -> 26.7 us
    ppermute x0 -> x1, starting transfers between devices: none -> 3.56 us  [exchange_plan(): far = lax.ppermute(lead_held, 'tm', [(0, 2), (3, 1)])]
    ppermute x13 -> x14, waiting for transfers between devices: 24.7 us -> 22.4 us  [meet(): return lax.ppermute(block, 'tm', [(j ^ m, j) for j in targets])]
    ppermute x13 -> x14, starting transfers between devices: 24.9 us -> 25.7 us  [meet(): return lax.ppermute(block, 'tm', [(j ^ m, j) for j in targets])]
  transfers between devices with their start and end apart: 21 -> 23, of which waited for: 7 -> 9; matrix products, arithmetic and copies ran while one was open for 0% -> 0% of each run, Pallas kernels for 11% -> 11%
where the time goes in v17:
time: 72.7 us; the launch traced here: 72.5 us
  starting transfers between devices  32.2 us (44%)
  waiting for transfers between devices  26.7 us (37%)
  Pallas kernels  11.9 us (16%)
  between operations  0.93 us (1%)
    ppermute x14, starting transfers between devices, meet(): return lax.ppermute(block, 'tm', [(j ^ m, j) for j in targets])  25.7 us
    ppermute x14, waiting for transfers between devices, meet(): return lax.ppermute(block, 'tm', [(j ^ m, j) for j in targets])  22.4 us
    pallas_call x2, Pallas kernels, head_group(): pl.pallas_call(functools.partial(group_kernel, heads, frames, chained, le...  6.7 us
    ppermute x8, waiting for transfers between devices, swap(): return lax.ppermute(block, axis, [(0, 1), (1, 0)])  4.2 us
    ppermute x1, starting transfers between devices, exchange_plan(): far = lax.ppermute(lead_held, 'tm', [(0, 2), (3, 1)])  3.56 us
    pallas_call x2, Pallas kernels, pack(): pl.pallas_call(functools.partial(pack_kernel, frames, outputs), in_specs=...  3.51 us
    ppermute x8, starting transfers between devices, swap(): return lax.ppermute(block, axis, [(0, 1), (1, 0)])  2.95 us
    pallas_call x1, Pallas kernels, place(): pl.pallas_call(functools.partial(place_kernel, frames, lead, late, rest),...  1.47 us
  transfers between devices with their start and end apart: 23, of which 9 were waited for; matrix products, arithmetic and copies ran while one was open for 0% of the time, Pallas kernels for 11%

profile of v17, /device:TPU:0, one launch (start us, length us, event | category | flops | bytes accessed | tf_op | source)
XLA Modules:
  0.0 72.5 jit_solution(8166597902850464610)
XLA Ops:
  0.7 2.6 %shard_map.121 = (bf16[128,1664]{1,0:T(8,128)(2,1)}, bf16[128,640]{1,0:T(8,128)(2,1)}, bf16[128,512]{1,0:T(8,128)(2,1)}, bf16[128,640]{1,0:T(8,128)(2,1)}, bf16[128,512]{1,0:T(8,128)(2,1)}) custom-call(bf16[128,1280]{1,0:T(8,128)(2,1)} %fq_ref.3, bf16[128,1280]{1,0:T(8,128)(2,1)} %do_ref.3, bf16[256,1280]{1,0:T(8,128)(2,1)} %fk_ref.3, ...), custom_call_target="tpu_custom_call" | custom-call | tf_op jit(solution)/shard_map/pallas_call | solution.py:303
  3.3 3.1 %collective-permute-start = (bf16[128,1664]{1,0:T(8,128)(2,1)}, bf16[128,1664]{1,0:T(8,128)(2,1)S(1)}, u32[]{:S(2)}, u32[]{:S(2)}) collective-permute-start(bf16[128,1664]{1,0:T(8,128)(2,1)} %get-tuple-element.34), channel_id=1, source_target_pairs={{4,0},{0,4},{12,8},{8,12},{5,1},{1,5},{13,9},{9,13},{6,2},{2,6},{1... | collective-permute-start | bytes 1277960 | tf_op jit(solution)/shard_map/nearest_over_tm/ppermute | solution.py:688
  6.3 2.6 %collective-permute-start.1 = (bf16[128,640]{1,0:T(8,128)(2,1)}, bf16[128,640]{1,0:T(8,128)(2,1)S(1)}, u32[]{:S(2)}, u32[]{:S(2)}) collective-permute-start(bf16[128,640]{1,0:T(8,128)(2,1)} %get-tuple-element.35), channel_id=1, source_target_pairs={{8,0},{12,4},{0,8},{4,12},{9,1},{13,5},{1,9},{5,13},{10,2},{14,6},... | collective-permute-start | bytes 491528 | tf_op jit(solution)/shard_map/lead_over_tm/ppermute | solution.py:688
  8.9 3.8 %collective-permute-start.6 = (bf16[128,512]{1,0:T(8,128)(2,1)}, bf16[128,512]{1,0:T(8,128)(2,1)S(1)}, u32[]{:S(2)}, u32[]{:S(2)}) collective-permute-start(bf16[128,512]{1,0:T(8,128)(2,1)} %get-tuple-element.45), channel_id=1, source_target_pairs={{12,4},{0,8},{13,5},{1,9},{14,6},{2,10},{15,7},{3,11},{28,20},{16,... | collective-permute-start | bytes 393224 | tf_op jit(solution)/shard_map/rest_over_tm/ppermute | solution.py:688
  12.8 0.7 collective-permute-start.7
  13.5 0.9 %shard_map.120 = (bf16[128,512]{1,0:T(8,128)(2,1)S(1)}, bf16[128,512]{1,0:T(8,128)(2,1)S(1)}, bf16[128,512]{1,0:T(8,128)(2,1)S(1)}, bf16[128,256]{1,0:T(8,128)(2...) custom-call(bf16[128,1280]{1,0:T(8,128)(2,1)S(1)} %copy-done.2, ...), custom_call_target="tpu_custom_call" | custom-call | tf_op jit(solution)/shard_map/pallas_call | solution.py:303
  14.4 6.0 %collective-permute-done.1.refs_1_.refs_3_ = bf16[128,640]{1,0:T(8,128)(2,1)S(1)} collective-permute-done((bf16[128,640]{1,0:T(8,128)(2,1)}, bf16[128,640]{1,0:T(8,128)(2,1)S(1)}, u32[]{:S(2)}, u32[]{:S(2)}) %collective-permute-start.1) | collective-permute-done | bytes 163872 | tf_op jit(solution)/shard_map/lead_over_tm/ppermute | solution.py:688
  20.4 6.4 %collective-permute-done.2.refs_2_.refs_4_ = bf16[128,640]{1,0:T(8,128)(2,1)S(1)} collective-permute-done((bf16[128,640]{1,0:T(8,128)(2,1)}, bf16[128,640]{1,0:T(8,128)(2,1)S(1)}, u32[]{:S(2)}, u32[]{:S(2)}) %collective-permute-start.2) | collective-permute-done | bytes 163872 | tf_op jit(solution)/shard_map/lead_over_tm/ppermute | solution.py:688
  27.0 0.5 collective-permute-start.8
  27.6 3.5 %collective-permute-start.4 = (bf16[128,512]{1,0:T(8,128)(2,1)S(1)}, bf16[128,512]{1,0:T(8,128)(2,1)S(1)}, u32[]{:S(2)}, u32[]{:S(2)}) collective-permute-start(bf16[128,512]{1,0:T(8,128)(2,1)S(1)} %get-tuple-element.40), channel_id=1, source_target_pairs={{8,0},{12,4},{0,8},{4,12},{9,1},{13,5},{1,9},{5,13},{10,2},{14,6},... | collective-permute-start | bytes 393224 | tf_op jit(solution)/shard_map/late_over_tm/ppermute | solution.py:688
  31.0 1.4 %collective-permute-start.5 = (bf16[128,512]{1,0:T(8,128)(2,1)S(1)}, bf16[128,512]{1,0:T(8,128)(2,1)S(1)}, u32[]{:S(2)}, u32[]{:S(2)}) collective-permute-start(bf16[128,512]{1,0:T(8,128)(2,1)S(1)} %get-tuple-element.41), channel_id=1, source_target_pairs={{12,0},{8,4},{4,8},{0,12},{13,1},{9,5},{5,9},{1,13},{14,2},{10,6},... | collective-permute-start | bytes 393224 | tf_op jit(solution)/shard_map/late_over_tm/ppermute | solution.py:688
  32.4 0.6 copy-done.8
  33.1 3.4 %shard_map.124 = (f32[384,128]{1,0:T(8,128)S(1)}, bf16[384,128]{1,0:T(8,128)(2,1)S(1)}, f32[512,128]{1,0:T(8,128)S(1)}, f32[512,128]{1,0:T(8,128)S(1)}) custom-call(s32[4,4]{1,0:T(4,128)S(1)} %copy-done.8, bf16[128,128]{1,0:T(8,128)(2,1)S(1)} %get-tuple-element.33.refs_1_, bf16[128,1664]{1,0:T(8,128)(2,1)S(1)} %collective-permute-done.refs_0_.refs_2_, ...), custom_call_target="tpu_custom_call" | custom-call | tf_op jit(solution)/shard_map/pallas_call | solution.py:523
  36.5 4.5 %collective-permute-done.4.refs_1_.refs_8_ = bf16[128,512]{1,0:T(8,128)(2,1)S(1)} collective-permute-done((bf16[128,512]{1,0:T(8,128)(2,1)S(1)}, bf16[128,512]{1,0:T(8,128)(2,1)S(1)}, u32[]{:S(2)}, u32[]{:S(2)}) %collective-permute-start.4) | collective-permute-done | bytes 131104 | tf_op jit(solution)/shard_map/late_over_tm/ppermute | solution.py:688
  41.2 1.4 %collective-permute-start.13 = (bf16[384,128]{1,0:T(8,128)(2,1)S(1)}, bf16[384,128]{1,0:T(8,128)(2,1)S(1)}, u32[]{:S(2)}, u32[]{:S(2)}) collective-permute-start(bf16[384,128]{1,0:T(8,128)(2,1)S(1)} %add_convert_fusion.refs_17_.piece), channel_id=1, source_target_pairs={{12,0},{8,4},{4,8},{0,12},{13,1},{9,5},{5,9},{1,13},{14,2},{10,6},... | collective-permute-start | bytes 294920 | tf_op jit(solution)/shard_map/early_gradients_over_tm/ppermute | solution.py:688
  42.6 2.2 %collective-permute-start.14 = (bf16[384,128]{1,0:T(8,128)(2,1)S(1)}, bf16[384,128]{1,0:T(8,128)(2,1)S(1)}, u32[]{:S(2)}, u32[]{:S(2)}) collective-permute-start(bf16[384,128]{1,0:T(8,128)(2,1)S(1)} %add_convert_fusion.refs_17_.piece), channel_id=1, source_target_pairs={{4,0},{0,4},{12,8},{8,12},{5,1},{1,5},{13,9},{9,13},{6,2},{2,6},{1... | collective-permute-start | bytes 294920 | tf_op jit(solution)/shard_map/early_gradients_over_tm/ppermute | solution.py:688
  44.8 3.3 %shard_map.126 = (f32[704,128]{1,0:T(8,128)S(1)}, bf16[352,128]{1,0:T(8,128)(2,1)S(1)}, bf16[352,128]{1,0:T(8,128)(2,1)S(1)}) custom-call(s32[4,4]{1,0:T(4,128)S(1)} %copy-done.8, bf16[128,128]{1,0:T(8,128)(2,1)S(1)} %get-tuple-element.33.refs_1_, bf16[128,1664]{1,0:T(8,128)(2,1)S(1)} %collective-permute-done.refs_0_.refs_2_, ...), custom_call_target="tpu_custom_call" | custom-call | tf_op jit(solution)/shard_map/pallas_call | solution.py:523
  48.2 0.5 collective-permute-start.12
  48.7 1.4 %collective-permute-done.14.refs_3_.pair = bf16[384,128]{1,0:T(8,128)(2,1)S(1)} collective-permute-done((bf16[384,128]{1,0:T(8,128)(2,1)S(1)}, bf16[384,128]{1,0:T(8,128)(2,1)S(1)}, u32[]{:S(2)}, u32[]{:S(2)}) %collective-permute-start.14) | collective-permute-done | bytes 98336 | tf_op jit(solution)/shard_map/early_gradients_over_tm/ppermute | solution.py:688
  50.2 0.9 %collective-permute-start.15 = (bf16[704,128]{1,0:T(8,128)(2,1)S(1)}, bf16[704,128]{1,0:T(8,128)(2,1)S(1)}, u32[]{:S(2)}, u32[]{:S(2)}) collective-permute-start(bf16[704,128]{1,0:T(8,128)(2,1)S(1)} %get-tuple-element.56), channel_id=1, source_target_pairs={{4,0},{0,4},{12,8},{8,12},{5,1},{1,5},{13,9},{9,13},{6,2},{2,6},{1... | collective-permute-start | bytes 540680 | tf_op jit(solution)/shard_map/late_sums_over_tm/ppermute | solution.py:688
  51.0 1.8 %collective-permute-start.16 = (bf16[128,128]{1,0:T(8,128)(2,1)S(1)}, bf16[128,128]{1,0:T(8,128)(2,1)S(1)}, u32[]{:S(2)}, u32[]{:S(2)}) collective-permute-start(bf16[128,128]{1,0:T(8,128)(2,1)S(1)} %get-tuple-element.57), channel_id=1, source_target_pairs={{8,0},{12,4},{0,8},{4,12},{9,1},{13,5},{1,9},{5,13},{10,2},{14,6},... | collective-permute-start | bytes 98312 | tf_op jit(solution)/shard_map/low_over_tm/ppermute | solution.py:688
  52.8 1.8 %collective-permute-start.17 = (bf16[128,128]{1,0:T(8,128)(2,1)S(1)}, bf16[128,128]{1,0:T(8,128)(2,1)S(1)}, u32[]{:S(2)}, u32[]{:S(2)}) collective-permute-start(bf16[128,128]{1,0:T(8,128)(2,1)S(1)} %get-tuple-element.58), channel_id=1, source_target_pairs={{12,0},{8,4},{4,8},{0,12},{13,1},{9,5},{5,9},{1,13},{14,2},{10,6},... | collective-permute-start | bytes 98312 | tf_op jit(solution)/shard_map/low_over_tm/ppermute | solution.py:688
  54.6 1.7 %collective-permute-done.16.third.refs_0_ = bf16[128,128]{1,0:T(8,128)(2,1)S(1)} collective-permute-done((bf16[128,128]{1,0:T(8,128)(2,1)S(1)}, bf16[128,128]{1,0:T(8,128)(2,1)S(1)}, u32[]{:S(2)}, u32[]{:S(2)}) %collective-permute-start.16) | collective-permute-done | bytes 32800 | tf_op jit(solution)/shard_map/low_over_tm/ppermute | solution.py:688
  56.3 2.4 %collective-permute-done.17.last.refs_1_ = bf16[128,128]{1,0:T(8,128)(2,1)S(1)} collective-permute-done((bf16[128,128]{1,0:T(8,128)(2,1)S(1)}, bf16[128,128]{1,0:T(8,128)(2,1)S(1)}, u32[]{:S(2)}, u32[]{:S(2)}) %collective-permute-start.17) | collective-permute-done | bytes 32800 | tf_op jit(solution)/shard_map/low_over_tm/ppermute | solution.py:688
  58.7 1.0 %collective-permute-start.19 = (bf16[192,128]{1,0:T(8,128)(2,1)S(1)}, bf16[192,128]{1,0:T(8,128)(2,1)S(1)}, u32[]{:S(2)}, u32[]{:S(2)}) collective-permute-start(bf16[192,128]{1,0:T(8,128)(2,1)S(1)} %get-tuple-element.60), channel_id=1, source_target_pairs={{8,0},{12,4},{0,8},{4,12},{9,1},{13,5},{1,9},{5,13},{10,2},{14,6},... | collective-permute-start | bytes 147464 | tf_op jit(solution)/shard_map/late_gradients_over_tm/ppermute | solution.py:688
  59.8 1.6 %collective-permute-start.20 = (bf16[192,128]{1,0:T(8,128)(2,1)S(1)}, bf16[192,128]{1,0:T(8,128)(2,1)S(1)}, u32[]{:S(2)}, u32[]{:S(2)}) collective-permute-start(bf16[192,128]{1,0:T(8,128)(2,1)S(1)} %get-tuple-element.60), channel_id=1, source_target_pairs={{12,0},{8,4},{4,8},{0,12},{13,1},{9,5},{5,9},{1,13},{14,2},{10,6},... | collective-permute-start | bytes 147464 | tf_op jit(solution)/shard_map/late_gradients_over_tm/ppermute | solution.py:688
  61.4 3.6 %collective-permute-start.21 = (bf16[192,128]{1,0:T(8,128)(2,1)S(1)}, bf16[192,128]{1,0:T(8,128)(2,1)S(1)}, u32[]{:S(2)}, u32[]{:S(2)}) collective-permute-start(bf16[192,128]{1,0:T(8,128)(2,1)S(1)} %get-tuple-element.61), channel_id=1, source_target_pairs={{0,8},{12,4},{1,9},{13,5},{2,10},{14,6},{3,11},{15,7},{16,24},{28,... | collective-permute-start | bytes 147464 | tf_op jit(solution)/shard_map/early_lead_over_tm/ppermute | solution.py:749
  65.0 1.6 %collective-permute-start.18 = (bf16[128,128]{1,0:T(8,128)(2,1)S(1)}, bf16[128,128]{1,0:T(8,128)(2,1)S(1)}, u32[]{:S(2)}, u32[]{:S(2)}) collective-permute-start(bf16[128,128]{1,0:T(8,128)(2,1)S(1)} %shard_map.128.low), channel_id=1, source_target_pairs={{0,2},{2,0},{1,3},{3,1},{4,6},{6,4},{5,7},{7,5},{8,10},{10,8},{9,1... | collective-permute-start | bytes 98312 | tf_op jit(solution)/shard_map/low_over_head/ppermute | solution.py:50
  66.6 0.1 collective-permute-done.21.far
  66.7 2.3 %collective-permute-done.18.low_head = bf16[128,128]{1,0:T(8,128)(2,1)S(1)} collective-permute-done((bf16[128,128]{1,0:T(8,128)(2,1)S(1)}, bf16[128,128]{1,0:T(8,128)(2,1)S(1)}, u32[]{:S(2)}, u32[]{:S(2)}) %collective-permute-start.18) | collective-permute-done | bytes 32800 | tf_op jit(solution)/shard_map/low_over_head/ppermute | solution.py:50
  69.1 1.9 %collective-permute-done.22.tail2 = bf16[2048,128]{1,0:T(8,128)(2,1)S(1)} collective-permute-done((bf16[2048,128]{1,0:T(8,128)(2,1)S(1)}, bf16[2048,128]{1,0:T(8,128)(2,1)S(1)}, u32[]{:S(2)}, u32[]{:S(2)}) %collective-permute-start.22) | collective-permute-done | bytes 524320 | tf_op jit(solution)/shard_map/tail_in_chip/ppermute | solution.py:50
  71.0 1.5 %shard_map.131 = (f32[128,1280]{1,0:T(8,128)}, f32[128,1280]{1,0:T(8,128)}, f32[128,1280]{1,0:T(8,128)}, f32[256,128]{1,0:T(8,128)}) custom-call(bf16[2048,128]{1,0:T(8,128)(2,1)S(1)} %shard_map.130.tail, bf16[2048,128]{1,0:T(8,128)(2,1)S(1)} %collective-permute-done.22.tail2), custom_call_target="tpu_custom_call" | custom-call | tf_op jit(solution)/shard_map/pallas_call | solution.py:651
  (45 shorter events, 0.7 us)
Async XLA Ops:
  0.6 12.8 %copy-start.2 = (bf16[128,1280]{1,0:T(8,128)(2,1)S(1)}, bf16[128,1280]{1,0:T(8,128)(2,1)}, u32[]{:S(2)}) copy-start(bf16[128,1280]{1,0:T(8,128)(2,1)} %fq_ref.3) | copy-start | bytes 983044
  0.6 12.8 %copy-start.3 = (bf16[128,1280]{1,0:T(8,128)(2,1)S(1)}, bf16[128,1280]{1,0:T(8,128)(2,1)}, u32[]{:S(2)}) copy-start(bf16[128,1280]{1,0:T(8,128)(2,1)} %do_ref.3) | copy-start | bytes 983044
  0.7 12.8 %copy-start = (bf16[256,1280]{1,0:T(8,128)(2,1)S(1)}, bf16[256,1280]{1,0:T(8,128)(2,1)}, u32[]{:S(2)}) copy-start(bf16[256,1280]{1,0:T(8,128)(2,1)} %fk_ref.3) | copy-start | bytes 1966084
  0.7 12.8 %copy-start.1 = (bf16[256,1280]{1,0:T(8,128)(2,1)S(1)}, bf16[256,1280]{1,0:T(8,128)(2,1)}, u32[]{:S(2)}) copy-start(bf16[256,1280]{1,0:T(8,128)(2,1)} %fv_ref.3) | copy-start | bytes 1966084
  0.7 12.8 %copy-start.7 = (bf16[256,128]{1,0:T(8,128)(2,1)S(1)}, bf16[256,128]{1,0:T(8,128)(2,1)}, u32[]{:S(2)}) copy-start(bf16[256,128]{1,0:T(8,128)(2,1)} %t_ref.3) | copy-start | bytes 196612
  3.3 23.6 %collective-permute-start = (bf16[128,1664]{1,0:T(8,128)(2,1)}, bf16[128,1664]{1,0:T(8,128)(2,1)S(1)}, u32[]{:S(2)}, u32[]{:S(2)}) collective-permute-start(bf16[128,1664]{1,0:T(8,128)(2,1)} %get-tuple-element.34), channel_id=1, source_target_pairs={{4,0},{0,4},{12,8},{8,12},{5,1},{1,5},{13,9},{9,13},{6,2},{2,6},{1... | collective-permute-start | bytes 1277960 | tf_op jit(solution)/shard_map/nearest_over_tm/ppermute | solution.py:688
  6.3 14.1 %collective-permute-start.1 = (bf16[128,640]{1,0:T(8,128)(2,1)}, bf16[128,640]{1,0:T(8,128)(2,1)S(1)}, u32[]{:S(2)}, u32[]{:S(2)}) collective-permute-start(bf16[128,640]{1,0:T(8,128)(2,1)} %get-tuple-element.35), channel_id=1, source_target_pairs={{8,0},{12,4},{0,8},{4,12},{9,1},{13,5},{1,9},{5,13},{10,2},{14,6},... | collective-permute-start | bytes 491528 | tf_op jit(solution)/shard_map/lead_over_tm/ppermute | solution.py:688
  8.9 17.9 %collective-permute-start.2 = (bf16[128,640]{1,0:T(8,128)(2,1)}, bf16[128,640]{1,0:T(8,128)(2,1)S(1)}, u32[]{:S(2)}, u32[]{:S(2)}) collective-permute-start(bf16[128,640]{1,0:T(8,128)(2,1)} %get-tuple-element.36), channel_id=1, source_target_pairs={{12,0},{8,4},{4,8},{0,12},{13,1},{9,5},{5,9},{1,13},{14,2},{10,6},... | collective-permute-start | bytes 491528 | tf_op jit(solution)/shard_map/lead_over_tm/ppermute | solution.py:688
  8.9 18.0 %collective-permute-start.6 = (bf16[128,512]{1,0:T(8,128)(2,1)}, bf16[128,512]{1,0:T(8,128)(2,1)S(1)}, u32[]{:S(2)}, u32[]{:S(2)}) collective-permute-start(bf16[128,512]{1,0:T(8,128)(2,1)} %get-tuple-element.45), channel_id=1, source_target_pairs={{12,4},{0,8},{13,5},{1,9},{14,6},{2,10},{15,7},{3,11},{28,20},{16,... | collective-permute-start | bytes 393224 | tf_op jit(solution)/shard_map/rest_over_tm/ppermute | solution.py:688
  12.8 14.2 %collective-permute-start.7 = (bf16[128,512]{1,0:T(8,128)(2,1)}, bf16[128,512]{1,0:T(8,128)(2,1)S(1)}, u32[]{:S(2)}, u32[]{:S(2)}) collective-permute-start(bf16[128,512]{1,0:T(8,128)(2,1)} %get-tuple-element.46), channel_id=1, source_target_pairs={{8,4},{4,8},{9,5},{5,9},{10,6},{6,10},{11,7},{7,11},{24,20},{20,24... | collective-permute-start | bytes 393224 | tf_op jit(solution)/shard_map/rest_over_tm/ppermute | solution.py:688
  26.8 5.6 %copy-start.6 = (bf16[128,1280]{1,0:T(8,128)(2,1)S(1)}, bf16[128,1280]{1,0:T(8,128)(2,1)}, u32[]{:S(2)}) copy-start(bf16[128,1280]{1,0:T(8,128)(2,1)} %refs_14_.3) | copy-start | bytes 983044
  26.9 5.6 %copy-start.4 = (bf16[128,1280]{1,0:T(8,128)(2,1)S(1)}, bf16[128,1280]{1,0:T(8,128)(2,1)}, u32[]{:S(2)}) copy-start(bf16[128,1280]{1,0:T(8,128)(2,1)} %refs_12_.1) | copy-start | bytes 983044
  26.9 5.6 %copy-start.5 = (bf16[128,1280]{1,0:T(8,128)(2,1)S(1)}, bf16[128,1280]{1,0:T(8,128)(2,1)}, u32[]{:S(2)}) copy-start(bf16[128,1280]{1,0:T(8,128)(2,1)} %refs_13_.1) | copy-start | bytes 983044
  26.9 5.5 %collective-permute-start.3 = (bf16[128,1152]{1,0:T(8,128)(2,1)S(1)}, bf16[128,1152]{1,0:T(8,128)(2,1)S(1)}, u32[]{:S(2)}, u32[]{:S(2)}) collective-permute-start(bf16[128,1152]{1,0:T(8,128)(2,1)S(1)} %shard_map.122), channel_id=1, source_target_pairs={{0,1},{1,0},{2,3},{3,2},{4,5},{5,4},{6,7},{7,6},{8,9},{9,8},{10,11... | collective-permute-start | bytes 884744 | tf_op jit(solution)/shard_map/lead_in_chip/ppermute | solution.py:50
  27.0 5.4 %collective-permute-start.8 = (bf16[128,768]{1,0:T(8,128)(2,1)S(1)}, bf16[128,768]{1,0:T(8,128)(2,1)S(1)}, u32[]{:S(2)}, u32[]{:S(2)}) collective-permute-start(bf16[128,768]{1,0:T(8,128)(2,1)S(1)} %shard_map.123), channel_id=1, source_target_pairs={{0,1},{1,0},{2,3},{3,2},{4,5},{5,4},{6,7},{7,6},{8,9},{9,8},{10,11... | collective-permute-start | bytes 589832 | tf_op jit(solution)/shard_map/rest_in_chip/ppermute | solution.py:50
  27.6 13.5 %collective-permute-start.4 = (bf16[128,512]{1,0:T(8,128)(2,1)S(1)}, bf16[128,512]{1,0:T(8,128)(2,1)S(1)}, u32[]{:S(2)}, u32[]{:S(2)}) collective-permute-start(bf16[128,512]{1,0:T(8,128)(2,1)S(1)} %get-tuple-element.40), channel_id=1, source_target_pairs={{8,0},{12,4},{0,8},{4,12},{9,1},{13,5},{1,9},{5,13},{10,2},{14,6},... | collective-permute-start | bytes 393224 | tf_op jit(solution)/shard_map/late_over_tm/ppermute | solution.py:688
  31.0 10.0 %collective-permute-start.5 = (bf16[128,512]{1,0:T(8,128)(2,1)S(1)}, bf16[128,512]{1,0:T(8,128)(2,1)S(1)}, u32[]{:S(2)}, u32[]{:S(2)}) collective-permute-start(bf16[128,512]{1,0:T(8,128)(2,1)S(1)} %get-tuple-element.41), channel_id=1, source_target_pairs={{12,0},{8,4},{4,8},{0,12},{13,1},{9,5},{5,9},{1,13},{14,2},{10,6},... | collective-permute-start | bytes 393224 | tf_op jit(solution)/shard_map/late_over_tm/ppermute | solution.py:688
  32.4 0.7 copy-start.8
  36.5 4.6 %collective-permute-start.9 = (bf16[384,128]{1,0:T(8,128)(2,1)S(1)}, bf16[384,128]{1,0:T(8,128)(2,1)S(1)}, u32[]{:S(2)}, u32[]{:S(2)}) collective-permute-start(bf16[384,128]{1,0:T(8,128)(2,1)S(1)} %get-tuple-element.48), channel_id=1, source_target_pairs={{0,1},{1,0},{2,3},{3,2},{4,5},{5,4},{6,7},{7,6},{8,9},{9,8},{10,11... | collective-permute-start | bytes 294920 | tf_op jit(solution)/shard_map/early_gradients_in_chip/ppermute | solution.py:50
  41.0 3.7 %collective-permute-start.10 = (bf16[128,1536]{1,0:T(8,128)(2,1)S(1)}, bf16[128,1536]{1,0:T(8,128)(2,1)S(1)}, u32[]{:S(2)}, u32[]{:S(2)}) collective-permute-start(bf16[128,1536]{1,0:T(8,128)(2,1)S(1)} %shard_map.125), channel_id=1, source_target_pairs={{0,1},{1,0},{2,3},{3,2},{4,5},{5,4},{6,7},{7,6},{8,9},{9,8},{10,11... | collective-permute-start | bytes 1179656 | tf_op jit(solution)/shard_map/late_in_chip/ppermute | solution.py:50
  41.2 7.6 %collective-permute-start.13 = (bf16[384,128]{1,0:T(8,128)(2,1)S(1)}, bf16[384,128]{1,0:T(8,128)(2,1)S(1)}, u32[]{:S(2)}, u32[]{:S(2)}) collective-permute-start(bf16[384,128]{1,0:T(8,128)(2,1)S(1)} %add_convert_fusion.refs_17_.piece), channel_id=1, source_target_pairs={{12,0},{8,4},{4,8},{0,12},{13,1},{9,5},{5,9},{1,13},{14,2},{10,6},... | collective-permute-start | bytes 294920 | tf_op jit(solution)/shard_map/early_gradients_over_tm/ppermute | solution.py:688
  42.6 7.5 %collective-permute-start.14 = (bf16[384,128]{1,0:T(8,128)(2,1)S(1)}, bf16[384,128]{1,0:T(8,128)(2,1)S(1)}, u32[]{:S(2)}, u32[]{:S(2)}) collective-permute-start(bf16[384,128]{1,0:T(8,128)(2,1)S(1)} %add_convert_fusion.refs_17_.piece), channel_id=1, source_target_pairs={{4,0},{0,4},{12,8},{8,12},{5,1},{1,5},{13,9},{9,13},{6,2},{2,6},{1... | collective-permute-start | bytes 294920 | tf_op jit(solution)/shard_map/early_gradients_over_tm/ppermute | solution.py:688
  48.1 1.9 %collective-permute-start.11 = (bf16[352,128]{1,0:T(8,128)(2,1)S(1)}, bf16[352,128]{1,0:T(8,128)(2,1)S(1)}, u32[]{:S(2)}, u32[]{:S(2)}) collective-permute-start(bf16[352,128]{1,0:T(8,128)(2,1)S(1)} %get-tuple-element.53), channel_id=1, source_target_pairs={{0,1},{1,0},{2,3},{3,2},{4,5},{5,4},{6,7},{7,6},{8,9},{9,8},{10,11... | collective-permute-start | bytes 270344 | tf_op jit(solution)/shard_map/late_sums_in_chip/ppermute | solution.py:50
  48.2 1.9 %collective-permute-start.12 = (bf16[352,128]{1,0:T(8,128)(2,1)S(1)}, bf16[352,128]{1,0:T(8,128)(2,1)S(1)}, u32[]{:S(2)}, u32[]{:S(2)}) collective-permute-start(bf16[352,128]{1,0:T(8,128)(2,1)S(1)} %get-tuple-element.54), channel_id=1, source_target_pairs={{0,1},{1,0},{2,3},{3,2},{4,5},{5,4},{6,7},{7,6},{8,9},{9,8},{10,11... | collective-permute-start | bytes 270344 | tf_op jit(solution)/shard_map/late_sums_in_chip/ppermute | solution.py:50
  50.2 14.8 %collective-permute-start.15 = (bf16[704,128]{1,0:T(8,128)(2,1)S(1)}, bf16[704,128]{1,0:T(8,128)(2,1)S(1)}, u32[]{:S(2)}, u32[]{:S(2)}) collective-permute-start(bf16[704,128]{1,0:T(8,128)(2,1)S(1)} %get-tuple-element.56), channel_id=1, source_target_pairs={{4,0},{0,4},{12,8},{8,12},{5,1},{1,5},{13,9},{9,13},{6,2},{2,6},{1... | collective-permute-start | bytes 540680 | tf_op jit(solution)/shard_map/late_sums_over_tm/ppermute | solution.py:688
  51.0 5.3 %collective-permute-start.16 = (bf16[128,128]{1,0:T(8,128)(2,1)S(1)}, bf16[128,128]{1,0:T(8,128)(2,1)S(1)}, u32[]{:S(2)}, u32[]{:S(2)}) collective-permute-start(bf16[128,128]{1,0:T(8,128)(2,1)S(1)} %get-tuple-element.57), channel_id=1, source_target_pairs={{8,0},{12,4},{0,8},{4,12},{9,1},{13,5},{1,9},{5,13},{10,2},{14,6},... | collective-permute-start | bytes 98312 | tf_op jit(solution)/shard_map/low_over_tm/ppermute | solution.py:688
  52.8 5.9 %collective-permute-start.17 = (bf16[128,128]{1,0:T(8,128)(2,1)S(1)}, bf16[128,128]{1,0:T(8,128)(2,1)S(1)}, u32[]{:S(2)}, u32[]{:S(2)}) collective-permute-start(bf16[128,128]{1,0:T(8,128)(2,1)S(1)} %get-tuple-element.58), channel_id=1, source_target_pairs={{12,0},{8,4},{4,8},{0,12},{13,1},{9,5},{5,9},{1,13},{14,2},{10,6},... | collective-permute-start | bytes 98312 | tf_op jit(solution)/shard_map/low_over_tm/ppermute | solution.py:688
  58.7 7.8 %collective-permute-start.19 = (bf16[192,128]{1,0:T(8,128)(2,1)S(1)}, bf16[192,128]{1,0:T(8,128)(2,1)S(1)}, u32[]{:S(2)}, u32[]{:S(2)}) collective-permute-start(bf16[192,128]{1,0:T(8,128)(2,1)S(1)} %get-tuple-element.60), channel_id=1, source_target_pairs={{8,0},{12,4},{0,8},{4,12},{9,1},{13,5},{1,9},{5,13},{10,2},{14,6},... | collective-permute-start | bytes 147464 | tf_op jit(solution)/shard_map/late_gradients_over_tm/ppermute | solution.py:688
  59.8 6.8 %collective-permute-start.20 = (bf16[192,128]{1,0:T(8,128)(2,1)S(1)}, bf16[192,128]{1,0:T(8,128)(2,1)S(1)}, u32[]{:S(2)}, u32[]{:S(2)}) collective-permute-start(bf16[192,128]{1,0:T(8,128)(2,1)S(1)} %get-tuple-element.60), channel_id=1, source_target_pairs={{12,0},{8,4},{4,8},{0,12},{13,1},{9,5},{5,9},{1,13},{14,2},{10,6},... | collective-permute-start | bytes 147464 | tf_op jit(solution)/shard_map/late_gradients_over_tm/ppermute | solution.py:688
  61.4 5.3 %collective-permute-start.21 = (bf16[192,128]{1,0:T(8,128)(2,1)S(1)}, bf16[192,128]{1,0:T(8,128)(2,1)S(1)}, u32[]{:S(2)}, u32[]{:S(2)}) collective-permute-start(bf16[192,128]{1,0:T(8,128)(2,1)S(1)} %get-tuple-element.61), channel_id=1, source_target_pairs={{0,8},{12,4},{1,9},{13,5},{2,10},{14,6},{3,11},{15,7},{16,24},{28,... | collective-permute-start | bytes 147464 | tf_op jit(solution)/shard_map/early_lead_over_tm/ppermute | solution.py:749
  65.0 4.0 %collective-permute-start.18 = (bf16[128,128]{1,0:T(8,128)(2,1)S(1)}, bf16[128,128]{1,0:T(8,128)(2,1)S(1)}, u32[]{:S(2)}, u32[]{:S(2)}) collective-permute-start(bf16[128,128]{1,0:T(8,128)(2,1)S(1)} %shard_map.128.low), channel_id=1, source_target_pairs={{0,2},{2,0},{1,3},{3,1},{4,6},{6,4},{5,7},{7,5},{8,10},{10,8},{9,1... | collective-permute-start | bytes 98312 | tf_op jit(solution)/shard_map/low_over_head/ppermute | solution.py:50
  69.0 2.0 %collective-permute-start.22 = (bf16[2048,128]{1,0:T(8,128)(2,1)S(1)}, bf16[2048,128]{1,0:T(8,128)(2,1)S(1)}, u32[]{:S(2)}, u32[]{:S(2)}) collective-permute-start(bf16[2048,128]{1,0:T(8,128)(2,1)S(1)} %shard_map.130.tail), channel_id=1, source_target_pairs={{0,1},{1,0},{2,3},{3,2},{4,5},{5,4},{6,7},{7,6},{8,9},{9,8},{10,11... | collective-permute-start | bytes 1572872 | tf_op jit(solution)/shard_map/tail_in_chip/ppermute | solution.py:50

commit v18 on v14

--- a/solution.py
+++ b/solution.py
@@ -723,7 +723,7 @@
     keep, give, *low = head_group(early, band_width, [t_side, lead_side, rest_side], adapters)
     got = swap_in_chip("early_gradients", give)
     piece = (keep + got.astype(F32)).astype(BF16)
-    *late_side, _ = sides("late", 2, late_got, False, (3,), 0, [got])
+    *late_side, _ = sides("late", 2, late_got, False, (3,), 2 * DH, [got])
     cut = 3 * rank // 2
     pair = meet("early_gradients", piece, 1)
     facing = meet("early_gradients", piece, 3)

time: 68.2 us -> 69.7 us (1.022)
  starting transfers between devices: 28.2 us -> 29.4 us
    ppermute x1, starting transfers between devices: 0.31 us -> 1.61 us  [exchange_plan(): lax.ppermute(low, ('head', 'rep'), diag)]
    ppermute x1, waiting for transfers between devices: 3.45 us -> 2.32 us  [exchange_plan(): far = lax.ppermute(piece[:cut], 'tm', [(0, 2), (3, 1)])]
    ppermute x12, waiting for transfers between devices: 19.8 us -> 20.9 us  [meet(): return lax.ppermute(block, 'tm', [(j ^ m, j) for j in targets])]
    ppermute x8, starting transfers between devices: 2.95 us -> 1.93 us  [swap(): return lax.ppermute(block, axis, [(0, 1), (1, 0)])]
    ppermute x12, starting transfers between devices: 23.1 us -> 24 us  [meet(): return lax.ppermute(block, 'tm', [(j ^ m, j) for j in targets])]
where the time goes in v18:
time: 69.7 us; the launch traced here: 69.5 us
  starting transfers between devices  29.4 us (42%)
  waiting for transfers between devices  26.6 us (38%)
  Pallas kernels  11.9 us (17%)
  between operations  0.92 us (1%)
    ppermute x12, starting transfers between devices, meet(): return lax.ppermute(block, 'tm', [(j ^ m, j) for j in targets])  24 us
    ppermute x12, waiting for transfers between devices, meet(): return lax.ppermute(block, 'tm', [(j ^ m, j) for j in targets])  20.9 us
    pallas_call x2, Pallas kernels, head_group(): pl.pallas_call(functools.partial(group_kernel, heads, frames, chained, le...  6.7 us
    pallas_call x2, Pallas kernels, pack(): pl.pallas_call(functools.partial(pack_kernel, frames, outputs), in_specs=...  3.51 us
    ppermute x1, waiting for transfers between devices, exchange_plan(): far = lax.ppermute(piece[:cut], 'tm', [(0, 2), (3, 1)])  2.32 us
    ppermute x8, waiting for transfers between devices, swap(): return lax.ppermute(block, axis, [(0, 1), (1, 0)])  2.13 us
    ppermute x8, starting transfers between devices, swap(): return lax.ppermute(block, axis, [(0, 1), (1, 0)])  1.93 us
    ppermute x1, starting transfers between devices, exchange_plan(): far = lax.ppermute(piece[:cut], 'tm', [(0, 2), (3, 1)])  1.89 us
  transfers between devices with their start and end apart: 22, of which 8 were waited for; matrix products, arithmetic and copies ran while one was open for 0% of the time, Pallas kernels for 11%

profile of v18, /device:TPU:0, one launch (start us, length us, event | category | flops | bytes accessed | tf_op | source)
XLA Modules:
  0.0 69.5 jit_solution(4769027793925423647)
XLA Ops:
  0.7 2.6 %shard_map.121 = (bf16[128,1664]{1,0:T(8,128)(2,1)}, bf16[128,640]{1,0:T(8,128)(2,1)}, bf16[128,512]{1,0:T(8,128)(2,1)}, bf16[128,640]{1,0:T(8,128)(2,1)}, bf16[128,512]{1,0:T(8,128)(2,1)}) custom-call(bf16[128,1280]{1,0:T(8,128)(2,1)} %fq_ref.3, bf16[128,1280]{1,0:T(8,128)(2,1)} %do_ref.3, bf16[256,1280]{1,0:T(8,128)(2,1)} %fk_ref.3, ...), custom_call_target="tpu_custom_call" | custom-call | tf_op jit(solution)/shard_map/pallas_call | solution.py:303
  3.3 3.1 %collective-permute-start = (bf16[128,1664]{1,0:T(8,128)(2,1)}, bf16[128,1664]{1,0:T(8,128)(2,1)S(1)}, u32[]{:S(2)}, u32[]{:S(2)}) collective-permute-start(bf16[128,1664]{1,0:T(8,128)(2,1)} %get-tuple-element.33), channel_id=1, source_target_pairs={{4,0},{0,4},{12,8},{8,12},{5,1},{1,5},{13,9},{9,13},{6,2},{2,6},{1... | collective-permute-start | bytes 1277960 | tf_op jit(solution)/shard_map/nearest_over_tm/ppermute | solution.py:676
  6.3 2.6 %collective-permute-start.1 = (bf16[128,640]{1,0:T(8,128)(2,1)}, bf16[128,640]{1,0:T(8,128)(2,1)S(1)}, u32[]{:S(2)}, u32[]{:S(2)}) collective-permute-start(bf16[128,640]{1,0:T(8,128)(2,1)} %get-tuple-element.34), channel_id=1, source_target_pairs={{8,0},{12,4},{0,8},{4,12},{9,1},{13,5},{1,9},{5,13},{10,2},{14,6},... | collective-permute-start | bytes 491528 | tf_op jit(solution)/shard_map/lead_over_tm/ppermute | solution.py:676
  8.9 3.8 %collective-permute-start.6 = (bf16[128,512]{1,0:T(8,128)(2,1)}, bf16[128,512]{1,0:T(8,128)(2,1)S(1)}, u32[]{:S(2)}, u32[]{:S(2)}) collective-permute-start(bf16[128,512]{1,0:T(8,128)(2,1)} %get-tuple-element.44), channel_id=1, source_target_pairs={{12,4},{0,8},{13,5},{1,9},{14,6},{2,10},{15,7},{3,11},{28,20},{16,... | collective-permute-start | bytes 393224 | tf_op jit(solution)/shard_map/rest_over_tm/ppermute | solution.py:676
  12.8 0.7 collective-permute-start.7
  13.5 0.9 %shard_map.120 = (bf16[128,512]{1,0:T(8,128)(2,1)S(1)}, bf16[128,512]{1,0:T(8,128)(2,1)S(1)}, bf16[128,512]{1,0:T(8,128)(2,1)S(1)}, bf16[128,256]{1,0:T(8,128)(2...) custom-call(bf16[128,1280]{1,0:T(8,128)(2,1)S(1)} %copy-done.2, ...), custom_call_target="tpu_custom_call" | custom-call | tf_op jit(solution)/shard_map/pallas_call | solution.py:303
  14.4 6.0 %collective-permute-done.1.refs_1_.refs_3_ = bf16[128,640]{1,0:T(8,128)(2,1)S(1)} collective-permute-done((bf16[128,640]{1,0:T(8,128)(2,1)}, bf16[128,640]{1,0:T(8,128)(2,1)S(1)}, u32[]{:S(2)}, u32[]{:S(2)}) %collective-permute-start.1) | collective-permute-done | bytes 163872 | tf_op jit(solution)/shard_map/lead_over_tm/ppermute | solution.py:676
  20.4 6.4 %collective-permute-done.2.refs_2_.refs_4_ = bf16[128,640]{1,0:T(8,128)(2,1)S(1)} collective-permute-done((bf16[128,640]{1,0:T(8,128)(2,1)}, bf16[128,640]{1,0:T(8,128)(2,1)S(1)}, u32[]{:S(2)}, u32[]{:S(2)}) %collective-permute-start.2) | collective-permute-done | bytes 163872 | tf_op jit(solution)/shard_map/lead_over_tm/ppermute | solution.py:676
  26.9 0.1 collective-permute-start.3
  27.0 0.5 collective-permute-start.8
  27.6 3.5 %collective-permute-start.4 = (bf16[128,512]{1,0:T(8,128)(2,1)S(1)}, bf16[128,512]{1,0:T(8,128)(2,1)S(1)}, u32[]{:S(2)}, u32[]{:S(2)}) collective-permute-start(bf16[128,512]{1,0:T(8,128)(2,1)S(1)} %get-tuple-element.39), channel_id=1, source_target_pairs={{8,0},{12,4},{0,8},{4,12},{9,1},{13,5},{1,9},{5,13},{10,2},{14,6},... | collective-permute-start | bytes 393224 | tf_op jit(solution)/shard_map/late_over_tm/ppermute | solution.py:676
  31.0 1.4 %collective-permute-start.5 = (bf16[128,512]{1,0:T(8,128)(2,1)S(1)}, bf16[128,512]{1,0:T(8,128)(2,1)S(1)}, u32[]{:S(2)}, u32[]{:S(2)}) collective-permute-start(bf16[128,512]{1,0:T(8,128)(2,1)S(1)} %get-tuple-element.40), channel_id=1, source_target_pairs={{12,0},{8,4},{4,8},{0,12},{13,1},{9,5},{5,9},{1,13},{14,2},{10,6},... | collective-permute-start | bytes 393224 | tf_op jit(solution)/shard_map/late_over_tm/ppermute | solution.py:676
  32.4 0.6 copy-done.8
  33.1 3.4 %shard_map.124 = (f32[384,128]{1,0:T(8,128)S(1)}, bf16[384,128]{1,0:T(8,128)(2,1)S(1)}, f32[512,128]{1,0:T(8,128)S(1)}, f32[512,128]{1,0:T(8,128)S(1)}) custom-call(s32[4,4]{1,0:T(4,128)S(1)} %copy-done.8, bf16[128,128]{1,0:T(8,128)(2,1)S(1)} %get-tuple-element.32.refs_1_, bf16[128,1664]{1,0:T(8,128)(2,1)S(1)} %collective-permute-done.refs_0_.refs_2_, ...), custom_call_target="tpu_custom_call" | custom-call | tf_op jit(solution)/shard_map/pallas_call | solution.py:523
  36.5 4.5 %collective-permute-done.4.refs_1_.refs_8_ = bf16[128,512]{1,0:T(8,128)(2,1)S(1)} collective-permute-done((bf16[128,512]{1,0:T(8,128)(2,1)S(1)}, bf16[128,512]{1,0:T(8,128)(2,1)S(1)}, u32[]{:S(2)}, u32[]{:S(2)}) %collective-permute-start.4) | collective-permute-done | bytes 131104 | tf_op jit(solution)/shard_map/late_over_tm/ppermute | solution.py:676
  41.2 3.2 %collective-permute-start.14 = (bf16[384,128]{1,0:T(8,128)(2,1)S(1)}, bf16[384,128]{1,0:T(8,128)(2,1)S(1)}, u32[]{:S(2)}, u32[]{:S(2)}) collective-permute-start(bf16[384,128]{1,0:T(8,128)(2,1)S(1)} %add_convert_fusion.refs_17_.piece), channel_id=1, source_target_pairs={{4,0},{0,4},{12,8},{8,12},{5,1},{1,5},{13,9},{9,13},{6,2},{2,6},{1... | collective-permute-start | bytes 294920 | tf_op jit(solution)/shard_map/early_gradients_over_tm/ppermute | solution.py:676
  44.3 1.4 %collective-permute-start.13 = (bf16[384,128]{1,0:T(8,128)(2,1)S(1)}, bf16[384,128]{1,0:T(8,128)(2,1)S(1)}, u32[]{:S(2)}, u32[]{:S(2)}) collective-permute-start(bf16[384,128]{1,0:T(8,128)(2,1)S(1)} %add_convert_fusion.refs_17_.piece), channel_id=1, source_target_pairs={{12,0},{8,4},{4,8},{0,12},{13,1},{9,5},{5,9},{1,13},{14,2},{10,6},... | collective-permute-start | bytes 294920 | tf_op jit(solution)/shard_map/early_gradients_over_tm/ppermute | solution.py:676
  45.7 3.3 %shard_map.126 = (f32[704,128]{1,0:T(8,128)S(1)}, bf16[352,128]{1,0:T(8,128)(2,1)S(1)}, bf16[352,128]{1,0:T(8,128)(2,1)S(1)}) custom-call(s32[4,4]{1,0:T(4,128)S(1)} %copy-done.8, bf16[128,128]{1,0:T(8,128)(2,1)S(1)} %get-tuple-element.32.refs_1_, bf16[128,1664]{1,0:T(8,128)(2,1)S(1)} %collective-permute-done.refs_0_.refs_2_, ...), custom_call_target="tpu_custom_call" | custom-call | tf_op jit(solution)/shard_map/pallas_call | solution.py:523
  49.0 0.1 collective-permute-start.11
  49.1 0.5 collective-permute-start.12
  49.6 1.5 %collective-permute-done.13.refs_2_.facing = bf16[384,128]{1,0:T(8,128)(2,1)S(1)} collective-permute-done((bf16[384,128]{1,0:T(8,128)(2,1)S(1)}, bf16[384,128]{1,0:T(8,128)(2,1)S(1)}, u32[]{:S(2)}, u32[]{:S(2)}) %collective-permute-start.13) | collective-permute-done | bytes 98336 | tf_op jit(solution)/shard_map/early_gradients_over_tm/ppermute | solution.py:676
  51.2 0.1 collective-permute-start.15
  51.3 2.8 %collective-permute-start.16 = (bf16[320,128]{1,0:T(8,128)(2,1)S(1)}, bf16[320,128]{1,0:T(8,128)(2,1)S(1)}, u32[]{:S(2)}, u32[]{:S(2)}) collective-permute-start(bf16[320,128]{1,0:T(8,128)(2,1)S(1)} %get-tuple-element.57), channel_id=1, source_target_pairs={{8,0},{12,4},{0,8},{4,12},{9,1},{13,5},{1,9},{5,13},{10,2},{14,6},... | collective-permute-start | bytes 245768 | tf_op jit(solution)/shard_map/late_sums_over_tm/ppermute | solution.py:676
  54.1 1.5 %collective-permute-start.17 = (bf16[320,128]{1,0:T(8,128)(2,1)S(1)}, bf16[320,128]{1,0:T(8,128)(2,1)S(1)}, u32[]{:S(2)}, u32[]{:S(2)}) collective-permute-start(bf16[320,128]{1,0:T(8,128)(2,1)S(1)} %get-tuple-element.55.own), channel_id=1, source_target_pairs={{12,0},{8,4},{4,8},{0,12},{13,1},{9,5},{5,9},{1,13},{14,2},{10,6},... | collective-permute-start | bytes 245768 | tf_op jit(solution)/shard_map/late_sums_over_tm/ppermute | solution.py:676
  55.7 1.9 %collective-permute-start.18 = (bf16[192,128]{1,0:T(8,128)(2,1)S(1)}, bf16[192,128]{1,0:T(8,128)(2,1)S(1)}, u32[]{:S(2)}, u32[]{:S(2)}) collective-permute-start(bf16[192,128]{1,0:T(8,128)(2,1)S(1)} %slice.4), channel_id=1, source_target_pairs={{0,8},{12,4},{1,9},{13,5},{2,10},{14,6},{3,11},{15,7},{16,24},{28,... | collective-permute-start | bytes 147464 | tf_op jit(solution)/shard_map/early_lead_over_tm/ppermute | solution.py:731
  57.6 2.3 %collective-permute-done.18.far = bf16[192,128]{1,0:T(8,128)(2,1)S(1)} collective-permute-done((bf16[192,128]{1,0:T(8,128)(2,1)S(1)}, bf16[192,128]{1,0:T(8,128)(2,1)S(1)}, u32[]{:S(2)}, u32[]{:S(2)}) %collective-permute-start.18) | collective-permute-done | bytes 49184 | tf_op jit(solution)/shard_map/early_lead_over_tm/ppermute | solution.py:731
  59.9 2.5 %collective-permute-done.17.last = bf16[320,128]{1,0:T(8,128)(2,1)S(1)} collective-permute-done((bf16[320,128]{1,0:T(8,128)(2,1)S(1)}, bf16[320,128]{1,0:T(8,128)(2,1)S(1)}, u32[]{:S(2)}, u32[]{:S(2)}) %collective-permute-start.17) | collective-permute-done | bytes 81952 | tf_op jit(solution)/shard_map/late_sums_over_tm/ppermute | solution.py:676
  62.5 1.6 %collective-permute-start.21 = (bf16[128,128]{1,0:T(8,128)(2,1)S(1)}, bf16[128,128]{1,0:T(8,128)(2,1)S(1)}, u32[]{:S(2)}, u32[]{:S(2)}) collective-permute-start(bf16[128,128]{1,0:T(8,128)(2,1)S(1)} %get-tuple-element.59), channel_id=1, source_target_pairs={{0,3},{1,2},{2,1},{3,0},{4,7},{5,6},{6,5},{7,4},{8,11},{9,10},{10,... | collective-permute-start | bytes 98312 | tf_op jit(solution)/shard_map/low_over_head/ppermute | solution.py:739
  64.1 0.5 collective-permute-start.20
  64.7 1.3 %collective-permute-done.21.low_diag = bf16[128,128]{1,0:T(8,128)(2,1)S(1)} collective-permute-done((bf16[128,128]{1,0:T(8,128)(2,1)S(1)}, bf16[128,128]{1,0:T(8,128)(2,1)S(1)}, u32[]{:S(2)}, u32[]{:S(2)}) %collective-permute-start.21) | collective-permute-done | bytes 32800 | tf_op jit(solution)/shard_map/low_over_head/ppermute | solution.py:739
  65.9 2.1 %collective-permute-done.20.low_head = bf16[128,128]{1,0:T(8,128)(2,1)S(1)} collective-permute-done((bf16[128,128]{1,0:T(8,128)(2,1)S(1)}, bf16[128,128]{1,0:T(8,128)(2,1)S(1)}, u32[]{:S(2)}, u32[]{:S(2)}) %collective-permute-start.20) | collective-permute-done | bytes 32800 | tf_op jit(solution)/shard_map/low_over_head/ppermute | solution.py:50
  68.0 1.5 %shard_map.129 = (f32[128,1280]{1,0:T(8,128)}, f32[128,1280]{1,0:T(8,128)}, f32[128,1280]{1,0:T(8,128)}, f32[256,128]{1,0:T(8,128)}) custom-call(bf16[2048,128]{1,0:T(8,128)(2,1)S(1)} %get-tuple-element.58.tail, bf16[2048,128]{1,0:T(8,128)(2,1)S(1)} %collective-permute-done.19.tail2, bf16[128,128]{1,0:T(8,128)(2,1)S(1)} %collective-permute-done.20.low_head, ...), custom_call_target="tpu_custom_call" | custom-call | tf_op jit(solution)/shard_map/pallas_call | solution.py:639
  (42 shorter events, 0.5 us)
Async XLA Ops:
  0.6 12.8 %copy-start.3 = (bf16[128,1280]{1,0:T(8,128)(2,1)S(1)}, bf16[128,1280]{1,0:T(8,128)(2,1)}, u32[]{:S(2)}) copy-start(bf16[128,1280]{1,0:T(8,128)(2,1)} %do_ref.3) | copy-start | bytes 983044
  0.6 12.8 %copy-start.7 = (bf16[256,128]{1,0:T(8,128)(2,1)S(1)}, bf16[256,128]{1,0:T(8,128)(2,1)}, u32[]{:S(2)}) copy-start(bf16[256,128]{1,0:T(8,128)(2,1)} %t_ref.3) | copy-start | bytes 196612
  0.7 12.8 %copy-start.1 = (bf16[256,1280]{1,0:T(8,128)(2,1)S(1)}, bf16[256,1280]{1,0:T(8,128)(2,1)}, u32[]{:S(2)}) copy-start(bf16[256,1280]{1,0:T(8,128)(2,1)} %fv_ref.3) | copy-start | bytes 1966084
  0.7 12.8 %copy-start = (bf16[256,1280]{1,0:T(8,128)(2,1)S(1)}, bf16[256,1280]{1,0:T(8,128)(2,1)}, u32[]{:S(2)}) copy-start(bf16[256,1280]{1,0:T(8,128)(2,1)} %fk_ref.3) | copy-start | bytes 1966084
  0.7 12.8 %copy-start.2 = (bf16[128,1280]{1,0:T(8,128)(2,1)S(1)}, bf16[128,1280]{1,0:T(8,128)(2,1)}, u32[]{:S(2)}) copy-start(bf16[128,1280]{1,0:T(8,128)(2,1)} %fq_ref.3) | copy-start | bytes 983044
  3.3 23.6 %collective-permute-start = (bf16[128,1664]{1,0:T(8,128)(2,1)}, bf16[128,1664]{1,0:T(8,128)(2,1)S(1)}, u32[]{:S(2)}, u32[]{:S(2)}) collective-permute-start(bf16[128,1664]{1,0:T(8,128)(2,1)} %get-tuple-element.33), channel_id=1, source_target_pairs={{4,0},{0,4},{12,8},{8,12},{5,1},{1,5},{13,9},{9,13},{6,2},{2,6},{1... | collective-permute-start | bytes 1277960 | tf_op jit(solution)/shard_map/nearest_over_tm/ppermute | solution.py:676
  6.3 14.1 %collective-permute-start.1 = (bf16[128,640]{1,0:T(8,128)(2,1)}, bf16[128,640]{1,0:T(8,128)(2,1)S(1)}, u32[]{:S(2)}, u32[]{:S(2)}) collective-permute-start(bf16[128,640]{1,0:T(8,128)(2,1)} %get-tuple-element.34), channel_id=1, source_target_pairs={{8,0},{12,4},{0,8},{4,12},{9,1},{13,5},{1,9},{5,13},{10,2},{14,6},... | collective-permute-start | bytes 491528 | tf_op jit(solution)/shard_map/lead_over_tm/ppermute | solution.py:676
  8.9 17.9 %collective-permute-start.2 = (bf16[128,640]{1,0:T(8,128)(2,1)}, bf16[128,640]{1,0:T(8,128)(2,1)S(1)}, u32[]{:S(2)}, u32[]{:S(2)}) collective-permute-start(bf16[128,640]{1,0:T(8,128)(2,1)} %get-tuple-element.35), channel_id=1, source_target_pairs={{12,0},{8,4},{4,8},{0,12},{13,1},{9,5},{5,9},{1,13},{14,2},{10,6},... | collective-permute-start | bytes 491528 | tf_op jit(solution)/shard_map/lead_over_tm/ppermute | solution.py:676
  8.9 18.0 %collective-permute-start.6 = (bf16[128,512]{1,0:T(8,128)(2,1)}, bf16[128,512]{1,0:T(8,128)(2,1)S(1)}, u32[]{:S(2)}, u32[]{:S(2)}) collective-permute-start(bf16[128,512]{1,0:T(8,128)(2,1)} %get-tuple-element.44), channel_id=1, source_target_pairs={{12,4},{0,8},{13,5},{1,9},{14,6},{2,10},{15,7},{3,11},{28,20},{16,... | collective-permute-start | bytes 393224 | tf_op jit(solution)/shard_map/rest_over_tm/ppermute | solution.py:676
  12.8 14.2 %collective-permute-start.7 = (bf16[128,512]{1,0:T(8,128)(2,1)}, bf16[128,512]{1,0:T(8,128)(2,1)S(1)}, u32[]{:S(2)}, u32[]{:S(2)}) collective-permute-start(bf16[128,512]{1,0:T(8,128)(2,1)} %get-tuple-element.45), channel_id=1, source_target_pairs={{8,4},{4,8},{9,5},{5,9},{10,6},{6,10},{11,7},{7,11},{24,20},{20,24... | collective-permute-start | bytes 393224 | tf_op jit(solution)/shard_map/rest_over_tm/ppermute | solution.py:676
  26.8 5.6 %copy-start.6 = (bf16[128,1280]{1,0:T(8,128)(2,1)S(1)}, bf16[128,1280]{1,0:T(8,128)(2,1)}, u32[]{:S(2)}) copy-start(bf16[128,1280]{1,0:T(8,128)(2,1)} %refs_14_.3) | copy-start | bytes 983044
  26.9 5.6 %copy-start.4 = (bf16[128,1280]{1,0:T(8,128)(2,1)S(1)}, bf16[128,1280]{1,0:T(8,128)(2,1)}, u32[]{:S(2)}) copy-start(bf16[128,1280]{1,0:T(8,128)(2,1)} %refs_12_.1) | copy-start | bytes 983044
  26.9 5.6 %copy-start.5 = (bf16[128,1280]{1,0:T(8,128)(2,1)S(1)}, bf16[128,1280]{1,0:T(8,128)(2,1)}, u32[]{:S(2)}) copy-start(bf16[128,1280]{1,0:T(8,128)(2,1)} %refs_13_.1) | copy-start | bytes 983044
  26.9 5.5 %collective-permute-start.3 = (bf16[128,1152]{1,0:T(8,128)(2,1)S(1)}, bf16[128,1152]{1,0:T(8,128)(2,1)S(1)}, u32[]{:S(2)}, u32[]{:S(2)}) collective-permute-start(bf16[128,1152]{1,0:T(8,128)(2,1)S(1)} %shard_map.122), channel_id=1, source_target_pairs={{0,1},{1,0},{2,3},{3,2},{4,5},{5,4},{6,7},{7,6},{8,9},{9,8},{10,11... | collective-permute-start | bytes 884744 | tf_op jit(solution)/shard_map/lead_in_chip/ppermute | solution.py:50
  27.0 5.4 %collective-permute-start.8 = (bf16[128,768]{1,0:T(8,128)(2,1)S(1)}, bf16[128,768]{1,0:T(8,128)(2,1)S(1)}, u32[]{:S(2)}, u32[]{:S(2)}) collective-permute-start(bf16[128,768]{1,0:T(8,128)(2,1)S(1)} %shard_map.123), channel_id=1, source_target_pairs={{0,1},{1,0},{2,3},{3,2},{4,5},{5,4},{6,7},{7,6},{8,9},{9,8},{10,11... | collective-permute-start | bytes 589832 | tf_op jit(solution)/shard_map/rest_in_chip/ppermute | solution.py:50
  27.6 13.5 %collective-permute-start.4 = (bf16[128,512]{1,0:T(8,128)(2,1)S(1)}, bf16[128,512]{1,0:T(8,128)(2,1)S(1)}, u32[]{:S(2)}, u32[]{:S(2)}) collective-permute-start(bf16[128,512]{1,0:T(8,128)(2,1)S(1)} %get-tuple-element.39), channel_id=1, source_target_pairs={{8,0},{12,4},{0,8},{4,12},{9,1},{13,5},{1,9},{5,13},{10,2},{14,6},... | collective-permute-start | bytes 393224 | tf_op jit(solution)/shard_map/late_over_tm/ppermute | solution.py:676
  31.0 10.0 %collective-permute-start.5 = (bf16[128,512]{1,0:T(8,128)(2,1)S(1)}, bf16[128,512]{1,0:T(8,128)(2,1)S(1)}, u32[]{:S(2)}, u32[]{:S(2)}) collective-permute-start(bf16[128,512]{1,0:T(8,128)(2,1)S(1)} %get-tuple-element.40), channel_id=1, source_target_pairs={{12,0},{8,4},{4,8},{0,12},{13,1},{9,5},{5,9},{1,13},{14,2},{10,6},... | collective-permute-start | bytes 393224 | tf_op jit(solution)/shard_map/late_over_tm/ppermute | solution.py:676
  32.4 0.7 copy-start.8
  36.5 4.6 %collective-permute-start.9 = (bf16[384,128]{1,0:T(8,128)(2,1)S(1)}, bf16[384,128]{1,0:T(8,128)(2,1)S(1)}, u32[]{:S(2)}, u32[]{:S(2)}) collective-permute-start(bf16[384,128]{1,0:T(8,128)(2,1)S(1)} %get-tuple-element.47), channel_id=1, source_target_pairs={{0,1},{1,0},{2,3},{3,2},{4,5},{5,4},{6,7},{7,6},{8,9},{9,8},{10,11... | collective-permute-start | bytes 294920 | tf_op jit(solution)/shard_map/early_gradients_in_chip/ppermute | solution.py:50
  41.0 4.6 %collective-permute-start.10 = (bf16[128,768]{1,0:T(8,128)(2,1)S(1)}, bf16[128,768]{1,0:T(8,128)(2,1)S(1)}, u32[]{:S(2)}, u32[]{:S(2)}) collective-permute-start(bf16[128,768]{1,0:T(8,128)(2,1)S(1)} %shard_map.125), channel_id=1, source_target_pairs={{0,1},{1,0},{2,3},{3,2},{4,5},{5,4},{6,7},{7,6},{8,9},{9,8},{10,11... | collective-permute-start | bytes 589832 | tf_op jit(solution)/shard_map/late_in_chip/ppermute | solution.py:50
  41.2 8.5 %collective-permute-start.14 = (bf16[384,128]{1,0:T(8,128)(2,1)S(1)}, bf16[384,128]{1,0:T(8,128)(2,1)S(1)}, u32[]{:S(2)}, u32[]{:S(2)}) collective-permute-start(bf16[384,128]{1,0:T(8,128)(2,1)S(1)} %add_convert_fusion.refs_17_.piece), channel_id=1, source_target_pairs={{4,0},{0,4},{12,8},{8,12},{5,1},{1,5},{13,9},{9,13},{6,2},{2,6},{1... | collective-permute-start | bytes 294920 | tf_op jit(solution)/shard_map/early_gradients_over_tm/ppermute | solution.py:676
  44.3 6.8 %collective-permute-start.13 = (bf16[384,128]{1,0:T(8,128)(2,1)S(1)}, bf16[384,128]{1,0:T(8,128)(2,1)S(1)}, u32[]{:S(2)}, u32[]{:S(2)}) collective-permute-start(bf16[384,128]{1,0:T(8,128)(2,1)S(1)} %add_convert_fusion.refs_17_.piece), channel_id=1, source_target_pairs={{12,0},{8,4},{4,8},{0,12},{13,1},{9,5},{5,9},{1,13},{14,2},{10,6},... | collective-permute-start | bytes 294920 | tf_op jit(solution)/shard_map/early_gradients_over_tm/ppermute | solution.py:676
  49.0 2.1 %collective-permute-start.11 = (bf16[352,128]{1,0:T(8,128)(2,1)S(1)}, bf16[352,128]{1,0:T(8,128)(2,1)S(1)}, u32[]{:S(2)}, u32[]{:S(2)}) collective-permute-start(bf16[352,128]{1,0:T(8,128)(2,1)S(1)} %get-tuple-element.52), channel_id=1, source_target_pairs={{0,1},{1,0},{2,3},{3,2},{4,5},{5,4},{6,7},{7,6},{8,9},{9,8},{10,11... | collective-permute-start | bytes 270344 | tf_op jit(solution)/shard_map/late_sums_in_chip/ppermute | solution.py:50
  49.1 2.0 %collective-permute-start.12 = (bf16[352,128]{1,0:T(8,128)(2,1)S(1)}, bf16[352,128]{1,0:T(8,128)(2,1)S(1)}, u32[]{:S(2)}, u32[]{:S(2)}) collective-permute-start(bf16[352,128]{1,0:T(8,128)(2,1)S(1)} %get-tuple-element.53), channel_id=1, source_target_pairs={{0,1},{1,0},{2,3},{3,2},{4,5},{5,4},{6,7},{7,6},{8,9},{9,8},{10,11... | collective-permute-start | bytes 270344 | tf_op jit(solution)/shard_map/late_sums_in_chip/ppermute | solution.py:50
  51.2 11.1 %collective-permute-start.15 = (bf16[704,128]{1,0:T(8,128)(2,1)S(1)}, bf16[704,128]{1,0:T(8,128)(2,1)S(1)}, u32[]{:S(2)}, u32[]{:S(2)}) collective-permute-start(bf16[704,128]{1,0:T(8,128)(2,1)S(1)} %get-tuple-element.56), channel_id=1, source_target_pairs={{4,0},{0,4},{12,8},{8,12},{5,1},{1,5},{13,9},{9,13},{6,2},{2,6},{1... | collective-permute-start | bytes 540680 | tf_op jit(solution)/shard_map/late_sums_over_tm/ppermute | solution.py:676
  51.3 8.6 %collective-permute-start.16 = (bf16[320,128]{1,0:T(8,128)(2,1)S(1)}, bf16[320,128]{1,0:T(8,128)(2,1)S(1)}, u32[]{:S(2)}, u32[]{:S(2)}) collective-permute-start(bf16[320,128]{1,0:T(8,128)(2,1)S(1)} %get-tuple-element.57), channel_id=1, source_target_pairs={{8,0},{12,4},{0,8},{4,12},{9,1},{13,5},{1,9},{5,13},{10,2},{14,6},... | collective-permute-start | bytes 245768 | tf_op jit(solution)/shard_map/late_sums_over_tm/ppermute | solution.py:676
  54.1 8.2 %collective-permute-start.17 = (bf16[320,128]{1,0:T(8,128)(2,1)S(1)}, bf16[320,128]{1,0:T(8,128)(2,1)S(1)}, u32[]{:S(2)}, u32[]{:S(2)}) collective-permute-start(bf16[320,128]{1,0:T(8,128)(2,1)S(1)} %get-tuple-element.55.own), channel_id=1, source_target_pairs={{12,0},{8,4},{4,8},{0,12},{13,1},{9,5},{5,9},{1,13},{14,2},{10,6},... | collective-permute-start | bytes 245768 | tf_op jit(solution)/shard_map/late_sums_over_tm/ppermute | solution.py:676
  55.7 4.2 %collective-permute-start.18 = (bf16[192,128]{1,0:T(8,128)(2,1)S(1)}, bf16[192,128]{1,0:T(8,128)(2,1)S(1)}, u32[]{:S(2)}, u32[]{:S(2)}) collective-permute-start(bf16[192,128]{1,0:T(8,128)(2,1)S(1)} %slice.4), channel_id=1, source_target_pairs={{0,8},{12,4},{1,9},{13,5},{2,10},{14,6},{3,11},{15,7},{16,24},{28,... | collective-permute-start | bytes 147464 | tf_op jit(solution)/shard_map/early_lead_over_tm/ppermute | solution.py:731
  62.4 5.6 %collective-permute-start.19 = (bf16[2048,128]{1,0:T(8,128)(2,1)S(1)}, bf16[2048,128]{1,0:T(8,128)(2,1)S(1)}, u32[]{:S(2)}, u32[]{:S(2)}) collective-permute-start(bf16[2048,128]{1,0:T(8,128)(2,1)S(1)} %get-tuple-element.58.tail), channel_id=1, source_target_pairs={{0,1},{1,0},{2,3},{3,2},{4,5},{5,4},{6,7},{7,6},{8,9},{9,8},{10,11... | collective-permute-start | bytes 1572872 | tf_op jit(solution)/shard_map/tail_in_chip/ppermute | solution.py:50
  62.5 3.4 %collective-permute-start.21 = (bf16[128,128]{1,0:T(8,128)(2,1)S(1)}, bf16[128,128]{1,0:T(8,128)(2,1)S(1)}, u32[]{:S(2)}, u32[]{:S(2)}) collective-permute-start(bf16[128,128]{1,0:T(8,128)(2,1)S(1)} %get-tuple-element.59), channel_id=1, source_target_pairs={{0,3},{1,2},{2,1},{3,0},{4,7},{5,6},{6,5},{7,4},{8,11},{9,10},{10,... | collective-permute-start | bytes 98312 | tf_op jit(solution)/shard_map/low_over_head/ppermute | solution.py:739
  64.1 3.9 %collective-permute-start.20 = (bf16[128,128]{1,0:T(8,128)(2,1)S(1)}, bf16[128,128]{1,0:T(8,128)(2,1)S(1)}, u32[]{:S(2)}, u32[]{:S(2)}) collective-permute-start(bf16[128,128]{1,0:T(8,128)(2,1)S(1)} %get-tuple-element.59), channel_id=1, source_target_pairs={{0,2},{2,0},{1,3},{3,1},{4,6},{6,4},{5,7},{7,5},{8,10},{10,8},{9,1... | collective-permute-start | bytes 98312 | tf_op jit(solution)/shard_map/low_over_head/ppermute | solution.py:50

commit v19 on v18

--- a/solution.py
+++ b/solution.py
@@ -535,7 +535,7 @@
 
 
 def hand_out_kernel(frames, size, parts, keep_ref, *refs):
-    gots, facing, (own_ref, *sends, total) = refs[:parts], refs[parts], refs[-frames - 1 :]
+    gots, facing, (own_ref, *sends, total) = refs[:parts], refs[-frames - 2], refs[-frames - 1 :]
     me = lax.axis_index("tm")
     rows = own_ref.shape[0]
     total[...] = keep_ref[...] + jnp.concatenate([got[...].astype(F32) for got in gots], axis=0)
@@ -553,13 +553,13 @@
     size, rank = keep.shape[0] - frames * rows, keep.shape[1]
     own, *sends = pl.pallas_call(
         functools.partial(hand_out_kernel, frames, size, len(gots)),
-        in_specs=vmem(2 + len(gots)) + [pl.BlockSpec(memory_space=pl.ANY)] * len(after),
+        in_specs=vmem(1 + len(gots)) + [pl.BlockSpec(memory_space=pl.ANY)] * len(after) + vmem(1),
         out_specs=vmem(frames),
         out_shape=[jax.ShapeDtypeStruct((rows, rank), F32)]
         + [jax.ShapeDtypeStruct((rows + size * n, rank), BF16) for n in (3, 1, 1)],
         scratch_shapes=[pltpu.VMEM(keep.shape, F32)],
         compiler_params=SMALL,
-    )(keep, *gots, facing, *after)
+    )(keep, *gots, *after, facing)
     return own, sends
 
 
@@ -725,8 +725,8 @@
     piece = (keep + got.astype(F32)).astype(BF16)
     *late_side, _ = sides("late", 2, late_got, False, (3,), 2 * DH, [got])
     cut = 3 * rank // 2
-    pair = meet("early_gradients", piece, 1)
-    facing = meet("early_gradients", piece, 3)
+    pair = meet("early_pair", piece, 1)
+    facing = meet("early_facing", piece, 3)
     with jax.named_scope("early_lead_over_tm"):
         far = lax.ppermute(piece[:cut], "tm", [(0, 2), (3, 1)])
     keep, *gives = head_group([late], band_width, [t_side, late_side], adapters, low, [piece])

time: 69.7 us -> 68.8 us (0.987)
  starting transfers between devices: 29.4 us -> 28.4 us
    ppermute x1, waiting for transfers between devices: 2.32 us -> 3.25 us  [exchange_plan(): far = lax.ppermute(piece[:cut], 'tm', [(0, 2), (3, 1)])]
    ppermute x12, starting transfers between devices: 24 us -> 23.1 us  [meet(): return lax.ppermute(block, 'tm', [(j ^ m, j) for j in targets])]
    ppermute x12, waiting for transfers between devices: 20.9 us -> 20 us  [meet(): return lax.ppermute(block, 'tm', [(j ^ m, j) for j in targets])]
where the time goes in v19:
time: 68.8 us; the launch traced here: 68.6 us
  starting transfers between devices  28.4 us (41%)
  waiting for transfers between devices  26.7 us (39%)
  Pallas kernels  11.9 us (17%)
  between operations  0.91 us (1%)
  local copies, waits for them, and re-layouts  0.69 us (1%)
    ppermute x12, starting transfers between devices, meet(): return lax.ppermute(block, 'tm', [(j ^ m, j) for j in targets])  23.1 us
    ppermute x12, waiting for transfers between devices, meet(): return lax.ppermute(block, 'tm', [(j ^ m, j) for j in targets])  20 us
    pallas_call x2, Pallas kernels, head_group(): pl.pallas_call(functools.partial(group_kernel, heads, frames, chained, le...  6.7 us
    pallas_call x2, Pallas kernels, pack(): pl.pallas_call(functools.partial(pack_kernel, frames, outputs), in_specs=...  3.51 us
    ppermute x1, waiting for transfers between devices, exchange_plan(): far = lax.ppermute(piece[:cut], 'tm', [(0, 2), (3, 1)])  3.25 us
    ppermute x8, waiting for transfers between devices, swap(): return lax.ppermute(block, axis, [(0, 1), (1, 0)])  2.13 us
    ppermute x8, starting transfers between devices, swap(): return lax.ppermute(block, axis, [(0, 1), (1, 0)])  1.93 us
    ppermute x1, starting transfers between devices, exchange_plan(): far = lax.ppermute(piece[:cut], 'tm', [(0, 2), (3, 1)])  1.82 us
  transfers between devices with their start and end apart: 22, of which 8 were waited for; matrix products, arithmetic and copies ran while one was open for 0% of the time, Pallas kernels for 11%

profile of v19, /device:TPU:0, one launch (start us, length us, event | category | flops | bytes accessed | tf_op | source)
XLA Modules:
  0.0 68.6 jit_solution(10144754448840827001)
XLA Ops:
  0.7 2.6 %shard_map.121 = (bf16[128,1664]{1,0:T(8,128)(2,1)}, bf16[128,640]{1,0:T(8,128)(2,1)}, bf16[128,512]{1,0:T(8,128)(2,1)}, bf16[128,640]{1,0:T(8,128)(2,1)}, bf16[128,512]{1,0:T(8,128)(2,1)}) custom-call(bf16[128,1280]{1,0:T(8,128)(2,1)} %fq_ref.3, bf16[128,1280]{1,0:T(8,128)(2,1)} %do_ref.3, bf16[256,1280]{1,0:T(8,128)(2,1)} %fk_ref.3, ...), custom_call_target="tpu_custom_call" | custom-call | tf_op jit(solution)/shard_map/pallas_call | solution.py:303
  3.3 3.1 %collective-permute-start = (bf16[128,1664]{1,0:T(8,128)(2,1)}, bf16[128,1664]{1,0:T(8,128)(2,1)S(1)}, u32[]{:S(2)}, u32[]{:S(2)}) collective-permute-start(bf16[128,1664]{1,0:T(8,128)(2,1)} %get-tuple-element.33), channel_id=1, source_target_pairs={{4,0},{0,4},{12,8},{8,12},{5,1},{1,5},{13,9},{9,13},{6,2},{2,6},{1... | collective-permute-start | bytes 1277960 | tf_op jit(solution)/shard_map/nearest_over_tm/ppermute | solution.py:676
  6.3 2.6 %collective-permute-start.1 = (bf16[128,640]{1,0:T(8,128)(2,1)}, bf16[128,640]{1,0:T(8,128)(2,1)S(1)}, u32[]{:S(2)}, u32[]{:S(2)}) collective-permute-start(bf16[128,640]{1,0:T(8,128)(2,1)} %get-tuple-element.34), channel_id=1, source_target_pairs={{8,0},{12,4},{0,8},{4,12},{9,1},{13,5},{1,9},{5,13},{10,2},{14,6},... | collective-permute-start | bytes 491528 | tf_op jit(solution)/shard_map/lead_over_tm/ppermute | solution.py:676
  8.9 3.8 %collective-permute-start.6 = (bf16[128,512]{1,0:T(8,128)(2,1)}, bf16[128,512]{1,0:T(8,128)(2,1)S(1)}, u32[]{:S(2)}, u32[]{:S(2)}) collective-permute-start(bf16[128,512]{1,0:T(8,128)(2,1)} %get-tuple-element.44), channel_id=1, source_target_pairs={{12,4},{0,8},{13,5},{1,9},{14,6},{2,10},{15,7},{3,11},{28,20},{16,... | collective-permute-start | bytes 393224 | tf_op jit(solution)/shard_map/rest_over_tm/ppermute | solution.py:676
  12.8 0.7 collective-permute-start.7
  13.5 0.9 %shard_map.120 = (bf16[128,512]{1,0:T(8,128)(2,1)S(1)}, bf16[128,512]{1,0:T(8,128)(2,1)S(1)}, bf16[128,512]{1,0:T(8,128)(2,1)S(1)}, bf16[128,256]{1,0:T(8,128)(2...) custom-call(bf16[128,1280]{1,0:T(8,128)(2,1)S(1)} %copy-done.2, ...), custom_call_target="tpu_custom_call" | custom-call | tf_op jit(solution)/shard_map/pallas_call | solution.py:303
  14.4 6.0 %collective-permute-done.1.refs_1_.refs_3_ = bf16[128,640]{1,0:T(8,128)(2,1)S(1)} collective-permute-done((bf16[128,640]{1,0:T(8,128)(2,1)}, bf16[128,640]{1,0:T(8,128)(2,1)S(1)}, u32[]{:S(2)}, u32[]{:S(2)}) %collective-permute-start.1) | collective-permute-done | bytes 163872 | tf_op jit(solution)/shard_map/lead_over_tm/ppermute | solution.py:676
  20.4 6.4 %collective-permute-done.2.refs_2_.refs_4_ = bf16[128,640]{1,0:T(8,128)(2,1)S(1)} collective-permute-done((bf16[128,640]{1,0:T(8,128)(2,1)}, bf16[128,640]{1,0:T(8,128)(2,1)S(1)}, u32[]{:S(2)}, u32[]{:S(2)}) %collective-permute-start.2) | collective-permute-done | bytes 163872 | tf_op jit(solution)/shard_map/lead_over_tm/ppermute | solution.py:676
  26.9 0.1 collective-permute-start.3
  27.0 0.5 collective-permute-start.8
  27.6 3.5 %collective-permute-start.4 = (bf16[128,512]{1,0:T(8,128)(2,1)S(1)}, bf16[128,512]{1,0:T(8,128)(2,1)S(1)}, u32[]{:S(2)}, u32[]{:S(2)}) collective-permute-start(bf16[128,512]{1,0:T(8,128)(2,1)S(1)} %get-tuple-element.39), channel_id=1, source_target_pairs={{8,0},{12,4},{0,8},{4,12},{9,1},{13,5},{1,9},{5,13},{10,2},{14,6},... | collective-permute-start | bytes 393224 | tf_op jit(solution)/shard_map/late_over_tm/ppermute | solution.py:676
  31.0 1.4 %collective-permute-start.5 = (bf16[128,512]{1,0:T(8,128)(2,1)S(1)}, bf16[128,512]{1,0:T(8,128)(2,1)S(1)}, u32[]{:S(2)}, u32[]{:S(2)}) collective-permute-start(bf16[128,512]{1,0:T(8,128)(2,1)S(1)} %get-tuple-element.40), channel_id=1, source_target_pairs={{12,0},{8,4},{4,8},{0,12},{13,1},{9,5},{5,9},{1,13},{14,2},{10,6},... | collective-permute-start | bytes 393224 | tf_op jit(solution)/shard_map/late_over_tm/ppermute | solution.py:676
  32.4 0.6 copy-done.8
  33.1 3.4 %shard_map.124 = (f32[384,128]{1,0:T(8,128)S(1)}, bf16[384,128]{1,0:T(8,128)(2,1)S(1)}, f32[512,128]{1,0:T(8,128)S(1)}, f32[512,128]{1,0:T(8,128)S(1)}) custom-call(s32[4,4]{1,0:T(4,128)S(1)} %copy-done.8, bf16[128,128]{1,0:T(8,128)(2,1)S(1)} %get-tuple-element.32.refs_1_, bf16[128,1664]{1,0:T(8,128)(2,1)S(1)} %collective-permute-done.refs_0_.refs_2_, ...), custom_call_target="tpu_custom_call" | custom-call | tf_op jit(solution)/shard_map/pallas_call | solution.py:523
  36.5 0.1 collective-permute-start.9
  36.5 4.5 %collective-permute-done.4.refs_1_.refs_8_ = bf16[128,512]{1,0:T(8,128)(2,1)S(1)} collective-permute-done((bf16[128,512]{1,0:T(8,128)(2,1)S(1)}, bf16[128,512]{1,0:T(8,128)(2,1)S(1)}, u32[]{:S(2)}, u32[]{:S(2)}) %collective-permute-start.4) | collective-permute-done | bytes 131104 | tf_op jit(solution)/shard_map/late_over_tm/ppermute | solution.py:676
  41.2 1.4 %collective-permute-start.14 = (bf16[384,128]{1,0:T(8,128)(2,1)S(1)}, bf16[384,128]{1,0:T(8,128)(2,1)S(1)}, u32[]{:S(2)}, u32[]{:S(2)}) collective-permute-start(bf16[384,128]{1,0:T(8,128)(2,1)S(1)} %add_convert_fusion.refs_17_.piece), channel_id=1, source_target_pairs={{12,0},{8,4},{4,8},{0,12},{13,1},{9,5},{5,9},{1,13},{14,2},{10,6},... | collective-permute-start | bytes 294920 | tf_op jit(solution)/shard_map/early_facing_over_tm/ppermute | solution.py:676
  42.6 2.2 %collective-permute-start.13 = (bf16[384,128]{1,0:T(8,128)(2,1)S(1)}, bf16[384,128]{1,0:T(8,128)(2,1)S(1)}, u32[]{:S(2)}, u32[]{:S(2)}) collective-permute-start(bf16[384,128]{1,0:T(8,128)(2,1)S(1)} %add_convert_fusion.refs_17_.piece), channel_id=1, source_target_pairs={{4,0},{0,4},{12,8},{8,12},{5,1},{1,5},{13,9},{9,13},{6,2},{2,6},{1... | collective-permute-start | bytes 294920 | tf_op jit(solution)/shard_map/early_pair_over_tm/ppermute | solution.py:676
  44.8 3.3 %shard_map.126 = (f32[704,128]{1,0:T(8,128)S(1)}, bf16[352,128]{1,0:T(8,128)(2,1)S(1)}, bf16[352,128]{1,0:T(8,128)(2,1)S(1)}) custom-call(s32[4,4]{1,0:T(4,128)S(1)} %copy-done.8, bf16[128,128]{1,0:T(8,128)(2,1)S(1)} %get-tuple-element.32.refs_1_, bf16[128,1664]{1,0:T(8,128)(2,1)S(1)} %collective-permute-done.refs_0_.refs_2_, ...), custom_call_target="tpu_custom_call" | custom-call | tf_op jit(solution)/shard_map/pallas_call | solution.py:523
  48.2 0.5 collective-permute-start.12
  48.7 1.4 %collective-permute-done.13.refs_2_.pair = bf16[384,128]{1,0:T(8,128)(2,1)S(1)} collective-permute-done((bf16[384,128]{1,0:T(8,128)(2,1)S(1)}, bf16[384,128]{1,0:T(8,128)(2,1)S(1)}, u32[]{:S(2)}, u32[]{:S(2)}) %collective-permute-start.13) | collective-permute-done | bytes 98336 | tf_op jit(solution)/shard_map/early_pair_over_tm/ppermute | solution.py:676
  50.1 0.9 %collective-permute-start.15 = (bf16[704,128]{1,0:T(8,128)(2,1)S(1)}, bf16[704,128]{1,0:T(8,128)(2,1)S(1)}, u32[]{:S(2)}, u32[]{:S(2)}) collective-permute-start(bf16[704,128]{1,0:T(8,128)(2,1)S(1)} %get-tuple-element.56), channel_id=1, source_target_pairs={{4,0},{0,4},{12,8},{8,12},{5,1},{1,5},{13,9},{9,13},{6,2},{2,6},{1... | collective-permute-start | bytes 540680 | tf_op jit(solution)/shard_map/late_sums_over_tm/ppermute | solution.py:676
  51.0 1.8 %collective-permute-start.16 = (bf16[320,128]{1,0:T(8,128)(2,1)S(1)}, bf16[320,128]{1,0:T(8,128)(2,1)S(1)}, u32[]{:S(2)}, u32[]{:S(2)}) collective-permute-start(bf16[320,128]{1,0:T(8,128)(2,1)S(1)} %get-tuple-element.57), channel_id=1, source_target_pairs={{8,0},{12,4},{0,8},{4,12},{9,1},{13,5},{1,9},{5,13},{10,2},{14,6},... | collective-permute-start | bytes 245768 | tf_op jit(solution)/shard_map/late_sums_over_tm/ppermute | solution.py:676
  52.8 1.8 %collective-permute-start.17 = (bf16[320,128]{1,0:T(8,128)(2,1)S(1)}, bf16[320,128]{1,0:T(8,128)(2,1)S(1)}, u32[]{:S(2)}, u32[]{:S(2)}) collective-permute-start(bf16[320,128]{1,0:T(8,128)(2,1)S(1)} %get-tuple-element.55.own), channel_id=1, source_target_pairs={{12,0},{8,4},{4,8},{0,12},{13,1},{9,5},{5,9},{1,13},{14,2},{10,6},... | collective-permute-start | bytes 245768 | tf_op jit(solution)/shard_map/late_sums_over_tm/ppermute | solution.py:676
  54.6 1.8 %collective-permute-start.18 = (bf16[192,128]{1,0:T(8,128)(2,1)S(1)}, bf16[192,128]{1,0:T(8,128)(2,1)S(1)}, u32[]{:S(2)}, u32[]{:S(2)}) collective-permute-start(bf16[192,128]{1,0:T(8,128)(2,1)S(1)} %slice.4), channel_id=1, source_target_pairs={{0,8},{12,4},{1,9},{13,5},{2,10},{14,6},{3,11},{15,7},{16,24},{28,... | collective-permute-start | bytes 147464 | tf_op jit(solution)/shard_map/early_lead_over_tm/ppermute | solution.py:731
  56.4 3.2 %collective-permute-done.18.far = bf16[192,128]{1,0:T(8,128)(2,1)S(1)} collective-permute-done((bf16[192,128]{1,0:T(8,128)(2,1)S(1)}, bf16[192,128]{1,0:T(8,128)(2,1)S(1)}, u32[]{:S(2)}, u32[]{:S(2)}) %collective-permute-start.18) | collective-permute-done | bytes 49184 | tf_op jit(solution)/shard_map/early_lead_over_tm/ppermute | solution.py:731
  59.7 1.8 %collective-permute-done.17.last = bf16[320,128]{1,0:T(8,128)(2,1)S(1)} collective-permute-done((bf16[320,128]{1,0:T(8,128)(2,1)S(1)}, bf16[320,128]{1,0:T(8,128)(2,1)S(1)}, u32[]{:S(2)}, u32[]{:S(2)}) %collective-permute-start.17) | collective-permute-done | bytes 81952 | tf_op jit(solution)/shard_map/late_sums_over_tm/ppermute | solution.py:676
  61.6 1.6 %collective-permute-start.21 = (bf16[128,128]{1,0:T(8,128)(2,1)S(1)}, bf16[128,128]{1,0:T(8,128)(2,1)S(1)}, u32[]{:S(2)}, u32[]{:S(2)}) collective-permute-start(bf16[128,128]{1,0:T(8,128)(2,1)S(1)} %get-tuple-element.59), channel_id=1, source_target_pairs={{0,3},{1,2},{2,1},{3,0},{4,7},{5,6},{6,5},{7,4},{8,11},{9,10},{10,... | collective-permute-start | bytes 98312 | tf_op jit(solution)/shard_map/low_over_head/ppermute | solution.py:739
  63.2 0.5 collective-permute-start.20
  63.7 1.3 %collective-permute-done.21.low_diag = bf16[128,128]{1,0:T(8,128)(2,1)S(1)} collective-permute-done((bf16[128,128]{1,0:T(8,128)(2,1)S(1)}, bf16[128,128]{1,0:T(8,128)(2,1)S(1)}, u32[]{:S(2)}, u32[]{:S(2)}) %collective-permute-start.21) | collective-permute-done | bytes 32800 | tf_op jit(solution)/shard_map/low_over_head/ppermute | solution.py:739
  65.0 2.1 %collective-permute-done.20.low_head = bf16[128,128]{1,0:T(8,128)(2,1)S(1)} collective-permute-done((bf16[128,128]{1,0:T(8,128)(2,1)S(1)}, bf16[128,128]{1,0:T(8,128)(2,1)S(1)}, u32[]{:S(2)}, u32[]{:S(2)}) %collective-permute-start.20) | collective-permute-done | bytes 32800 | tf_op jit(solution)/shard_map/low_over_head/ppermute | solution.py:50
  67.1 1.5 %shard_map.129 = (f32[128,1280]{1,0:T(8,128)}, f32[128,1280]{1,0:T(8,128)}, f32[128,1280]{1,0:T(8,128)}, f32[256,128]{1,0:T(8,128)}) custom-call(bf16[2048,128]{1,0:T(8,128)(2,1)S(1)} %get-tuple-element.58.tail, bf16[2048,128]{1,0:T(8,128)(2,1)S(1)} %collective-permute-done.19.tail2, bf16[128,128]{1,0:T(8,128)(2,1)S(1)} %collective-permute-done.20.low_head, ...), custom_call_target="tpu_custom_call" | custom-call | tf_op jit(solution)/shard_map/pallas_call | solution.py:639
  (42 shorter events, 0.5 us)
Async XLA Ops:
  0.6 12.8 %copy-start.3 = (bf16[128,1280]{1,0:T(8,128)(2,1)S(1)}, bf16[128,1280]{1,0:T(8,128)(2,1)}, u32[]{:S(2)}) copy-start(bf16[128,1280]{1,0:T(8,128)(2,1)} %do_ref.3) | copy-start | bytes 983044
  0.6 12.8 %copy-start.7 = (bf16[256,128]{1,0:T(8,128)(2,1)S(1)}, bf16[256,128]{1,0:T(8,128)(2,1)}, u32[]{:S(2)}) copy-start(bf16[256,128]{1,0:T(8,128)(2,1)} %t_ref.3) | copy-start | bytes 196612
  0.7 12.8 %copy-start.1 = (bf16[256,1280]{1,0:T(8,128)(2,1)S(1)}, bf16[256,1280]{1,0:T(8,128)(2,1)}, u32[]{:S(2)}) copy-start(bf16[256,1280]{1,0:T(8,128)(2,1)} %fv_ref.3) | copy-start | bytes 1966084
  0.7 12.8 %copy-start = (bf16[256,1280]{1,0:T(8,128)(2,1)S(1)}, bf16[256,1280]{1,0:T(8,128)(2,1)}, u32[]{:S(2)}) copy-start(bf16[256,1280]{1,0:T(8,128)(2,1)} %fk_ref.3) | copy-start | bytes 1966084
  0.7 12.8 %copy-start.2 = (bf16[128,1280]{1,0:T(8,128)(2,1)S(1)}, bf16[128,1280]{1,0:T(8,128)(2,1)}, u32[]{:S(2)}) copy-start(bf16[128,1280]{1,0:T(8,128)(2,1)} %fq_ref.3) | copy-start | bytes 983044
  3.3 23.6 %collective-permute-start = (bf16[128,1664]{1,0:T(8,128)(2,1)}, bf16[128,1664]{1,0:T(8,128)(2,1)S(1)}, u32[]{:S(2)}, u32[]{:S(2)}) collective-permute-start(bf16[128,1664]{1,0:T(8,128)(2,1)} %get-tuple-element.33), channel_id=1, source_target_pairs={{4,0},{0,4},{12,8},{8,12},{5,1},{1,5},{13,9},{9,13},{6,2},{2,6},{1... | collective-permute-start | bytes 1277960 | tf_op jit(solution)/shard_map/nearest_over_tm/ppermute | solution.py:676
  6.3 14.1 %collective-permute-start.1 = (bf16[128,640]{1,0:T(8,128)(2,1)}, bf16[128,640]{1,0:T(8,128)(2,1)S(1)}, u32[]{:S(2)}, u32[]{:S(2)}) collective-permute-start(bf16[128,640]{1,0:T(8,128)(2,1)} %get-tuple-element.34), channel_id=1, source_target_pairs={{8,0},{12,4},{0,8},{4,12},{9,1},{13,5},{1,9},{5,13},{10,2},{14,6},... | collective-permute-start | bytes 491528 | tf_op jit(solution)/shard_map/lead_over_tm/ppermute | solution.py:676
  8.9 17.9 %collective-permute-start.2 = (bf16[128,640]{1,0:T(8,128)(2,1)}, bf16[128,640]{1,0:T(8,128)(2,1)S(1)}, u32[]{:S(2)}, u32[]{:S(2)}) collective-permute-start(bf16[128,640]{1,0:T(8,128)(2,1)} %get-tuple-element.35), channel_id=1, source_target_pairs={{12,0},{8,4},{4,8},{0,12},{13,1},{9,5},{5,9},{1,13},{14,2},{10,6},... | collective-permute-start | bytes 491528 | tf_op jit(solution)/shard_map/lead_over_tm/ppermute | solution.py:676
  8.9 18.0 %collective-permute-start.6 = (bf16[128,512]{1,0:T(8,128)(2,1)}, bf16[128,512]{1,0:T(8,128)(2,1)S(1)}, u32[]{:S(2)}, u32[]{:S(2)}) collective-permute-start(bf16[128,512]{1,0:T(8,128)(2,1)} %get-tuple-element.44), channel_id=1, source_target_pairs={{12,4},{0,8},{13,5},{1,9},{14,6},{2,10},{15,7},{3,11},{28,20},{16,... | collective-permute-start | bytes 393224 | tf_op jit(solution)/shard_map/rest_over_tm/ppermute | solution.py:676
  12.8 14.2 %collective-permute-start.7 = (bf16[128,512]{1,0:T(8,128)(2,1)}, bf16[128,512]{1,0:T(8,128)(2,1)S(1)}, u32[]{:S(2)}, u32[]{:S(2)}) collective-permute-start(bf16[128,512]{1,0:T(8,128)(2,1)} %get-tuple-element.45), channel_id=1, source_target_pairs={{8,4},{4,8},{9,5},{5,9},{10,6},{6,10},{11,7},{7,11},{24,20},{20,24... | collective-permute-start | bytes 393224 | tf_op jit(solution)/shard_map/rest_over_tm/ppermute | solution.py:676
  26.8 5.6 %copy-start.6 = (bf16[128,1280]{1,0:T(8,128)(2,1)S(1)}, bf16[128,1280]{1,0:T(8,128)(2,1)}, u32[]{:S(2)}) copy-start(bf16[128,1280]{1,0:T(8,128)(2,1)} %refs_14_.3) | copy-start | bytes 983044
  26.9 5.6 %copy-start.4 = (bf16[128,1280]{1,0:T(8,128)(2,1)S(1)}, bf16[128,1280]{1,0:T(8,128)(2,1)}, u32[]{:S(2)}) copy-start(bf16[128,1280]{1,0:T(8,128)(2,1)} %refs_12_.1) | copy-start | bytes 983044
  26.9 5.6 %copy-start.5 = (bf16[128,1280]{1,0:T(8,128)(2,1)S(1)}, bf16[128,1280]{1,0:T(8,128)(2,1)}, u32[]{:S(2)}) copy-start(bf16[128,1280]{1,0:T(8,128)(2,1)} %refs_13_.1) | copy-start | bytes 983044
  26.9 5.5 %collective-permute-start.3 = (bf16[128,1152]{1,0:T(8,128)(2,1)S(1)}, bf16[128,1152]{1,0:T(8,128)(2,1)S(1)}, u32[]{:S(2)}, u32[]{:S(2)}) collective-permute-start(bf16[128,1152]{1,0:T(8,128)(2,1)S(1)} %shard_map.122), channel_id=1, source_target_pairs={{0,1},{1,0},{2,3},{3,2},{4,5},{5,4},{6,7},{7,6},{8,9},{9,8},{10,11... | collective-permute-start | bytes 884744 | tf_op jit(solution)/shard_map/lead_in_chip/ppermute | solution.py:50
  27.0 5.4 %collective-permute-start.8 = (bf16[128,768]{1,0:T(8,128)(2,1)S(1)}, bf16[128,768]{1,0:T(8,128)(2,1)S(1)}, u32[]{:S(2)}, u32[]{:S(2)}) collective-permute-start(bf16[128,768]{1,0:T(8,128)(2,1)S(1)} %shard_map.123), channel_id=1, source_target_pairs={{0,1},{1,0},{2,3},{3,2},{4,5},{5,4},{6,7},{7,6},{8,9},{9,8},{10,11... | collective-permute-start | bytes 589832 | tf_op jit(solution)/shard_map/rest_in_chip/ppermute | solution.py:50
  27.6 13.5 %collective-permute-start.4 = (bf16[128,512]{1,0:T(8,128)(2,1)S(1)}, bf16[128,512]{1,0:T(8,128)(2,1)S(1)}, u32[]{:S(2)}, u32[]{:S(2)}) collective-permute-start(bf16[128,512]{1,0:T(8,128)(2,1)S(1)} %get-tuple-element.39), channel_id=1, source_target_pairs={{8,0},{12,4},{0,8},{4,12},{9,1},{13,5},{1,9},{5,13},{10,2},{14,6},... | collective-permute-start | bytes 393224 | tf_op jit(solution)/shard_map/late_over_tm/ppermute | solution.py:676
  31.0 10.0 %collective-permute-start.5 = (bf16[128,512]{1,0:T(8,128)(2,1)S(1)}, bf16[128,512]{1,0:T(8,128)(2,1)S(1)}, u32[]{:S(2)}, u32[]{:S(2)}) collective-permute-start(bf16[128,512]{1,0:T(8,128)(2,1)S(1)} %get-tuple-element.40), channel_id=1, source_target_pairs={{12,0},{8,4},{4,8},{0,12},{13,1},{9,5},{5,9},{1,13},{14,2},{10,6},... | collective-permute-start | bytes 393224 | tf_op jit(solution)/shard_map/late_over_tm/ppermute | solution.py:676
  32.4 0.7 copy-start.8
  36.5 4.6 %collective-permute-start.9 = (bf16[384,128]{1,0:T(8,128)(2,1)S(1)}, bf16[384,128]{1,0:T(8,128)(2,1)S(1)}, u32[]{:S(2)}, u32[]{:S(2)}) collective-permute-start(bf16[384,128]{1,0:T(8,128)(2,1)S(1)} %get-tuple-element.47), channel_id=1, source_target_pairs={{0,1},{1,0},{2,3},{3,2},{4,5},{5,4},{6,7},{7,6},{8,9},{9,8},{10,11... | collective-permute-start | bytes 294920 | tf_op jit(solution)/shard_map/early_gradients_in_chip/ppermute | solution.py:50
  41.0 3.7 %collective-permute-start.10 = (bf16[128,768]{1,0:T(8,128)(2,1)S(1)}, bf16[128,768]{1,0:T(8,128)(2,1)S(1)}, u32[]{:S(2)}, u32[]{:S(2)}) collective-permute-start(bf16[128,768]{1,0:T(8,128)(2,1)S(1)} %shard_map.125), channel_id=1, source_target_pairs={{0,1},{1,0},{2,3},{3,2},{4,5},{5,4},{6,7},{7,6},{8,9},{9,8},{10,11... | collective-permute-start | bytes 589832 | tf_op jit(solution)/shard_map/late_in_chip/ppermute | solution.py:50
  41.2 7.6 %collective-permute-start.14 = (bf16[384,128]{1,0:T(8,128)(2,1)S(1)}, bf16[384,128]{1,0:T(8,128)(2,1)S(1)}, u32[]{:S(2)}, u32[]{:S(2)}) collective-permute-start(bf16[384,128]{1,0:T(8,128)(2,1)S(1)} %add_convert_fusion.refs_17_.piece), channel_id=1, source_target_pairs={{12,0},{8,4},{4,8},{0,12},{13,1},{9,5},{5,9},{1,13},{14,2},{10,6},... | collective-permute-start | bytes 294920 | tf_op jit(solution)/shard_map/early_facing_over_tm/ppermute | solution.py:676
  42.6 7.5 %collective-permute-start.13 = (bf16[384,128]{1,0:T(8,128)(2,1)S(1)}, bf16[384,128]{1,0:T(8,128)(2,1)S(1)}, u32[]{:S(2)}, u32[]{:S(2)}) collective-permute-start(bf16[384,128]{1,0:T(8,128)(2,1)S(1)} %add_convert_fusion.refs_17_.piece), channel_id=1, source_target_pairs={{4,0},{0,4},{12,8},{8,12},{5,1},{1,5},{13,9},{9,13},{6,2},{2,6},{1... | collective-permute-start | bytes 294920 | tf_op jit(solution)/shard_map/early_pair_over_tm/ppermute | solution.py:676
  48.1 1.9 %collective-permute-start.11 = (bf16[352,128]{1,0:T(8,128)(2,1)S(1)}, bf16[352,128]{1,0:T(8,128)(2,1)S(1)}, u32[]{:S(2)}, u32[]{:S(2)}) collective-permute-start(bf16[352,128]{1,0:T(8,128)(2,1)S(1)} %get-tuple-element.52), channel_id=1, source_target_pairs={{0,1},{1,0},{2,3},{3,2},{4,5},{5,4},{6,7},{7,6},{8,9},{9,8},{10,11... | collective-permute-start | bytes 270344 | tf_op jit(solution)/shard_map/late_sums_in_chip/ppermute | solution.py:50
  48.2 1.9 %collective-permute-start.12 = (bf16[352,128]{1,0:T(8,128)(2,1)S(1)}, bf16[352,128]{1,0:T(8,128)(2,1)S(1)}, u32[]{:S(2)}, u32[]{:S(2)}) collective-permute-start(bf16[352,128]{1,0:T(8,128)(2,1)S(1)} %get-tuple-element.53), channel_id=1, source_target_pairs={{0,1},{1,0},{2,3},{3,2},{4,5},{5,4},{6,7},{7,6},{8,9},{9,8},{10,11... | collective-permute-start | bytes 270344 | tf_op jit(solution)/shard_map/late_sums_in_chip/ppermute | solution.py:50
  50.1 11.3 %collective-permute-start.15 = (bf16[704,128]{1,0:T(8,128)(2,1)S(1)}, bf16[704,128]{1,0:T(8,128)(2,1)S(1)}, u32[]{:S(2)}, u32[]{:S(2)}) collective-permute-start(bf16[704,128]{1,0:T(8,128)(2,1)S(1)} %get-tuple-element.56), channel_id=1, source_target_pairs={{4,0},{0,4},{12,8},{8,12},{5,1},{1,5},{13,9},{9,13},{6,2},{2,6},{1... | collective-permute-start | bytes 540680 | tf_op jit(solution)/shard_map/late_sums_over_tm/ppermute | solution.py:676
  51.0 8.6 %collective-permute-start.16 = (bf16[320,128]{1,0:T(8,128)(2,1)S(1)}, bf16[320,128]{1,0:T(8,128)(2,1)S(1)}, u32[]{:S(2)}, u32[]{:S(2)}) collective-permute-start(bf16[320,128]{1,0:T(8,128)(2,1)S(1)} %get-tuple-element.57), channel_id=1, source_target_pairs={{8,0},{12,4},{0,8},{4,12},{9,1},{13,5},{1,9},{5,13},{10,2},{14,6},... | collective-permute-start | bytes 245768 | tf_op jit(solution)/shard_map/late_sums_over_tm/ppermute | solution.py:676
  52.8 8.6 %collective-permute-start.17 = (bf16[320,128]{1,0:T(8,128)(2,1)S(1)}, bf16[320,128]{1,0:T(8,128)(2,1)S(1)}, u32[]{:S(2)}, u32[]{:S(2)}) collective-permute-start(bf16[320,128]{1,0:T(8,128)(2,1)S(1)} %get-tuple-element.55.own), channel_id=1, source_target_pairs={{12,0},{8,4},{4,8},{0,12},{13,1},{9,5},{5,9},{1,13},{14,2},{10,6},... | collective-permute-start | bytes 245768 | tf_op jit(solution)/shard_map/late_sums_over_tm/ppermute | solution.py:676
  54.6 5.1 %collective-permute-start.18 = (bf16[192,128]{1,0:T(8,128)(2,1)S(1)}, bf16[192,128]{1,0:T(8,128)(2,1)S(1)}, u32[]{:S(2)}, u32[]{:S(2)}) collective-permute-start(bf16[192,128]{1,0:T(8,128)(2,1)S(1)} %slice.4), channel_id=1, source_target_pairs={{0,8},{12,4},{1,9},{13,5},{2,10},{14,6},{3,11},{15,7},{16,24},{28,... | collective-permute-start | bytes 147464 | tf_op jit(solution)/shard_map/early_lead_over_tm/ppermute | solution.py:731
  61.5 5.6 %collective-permute-start.19 = (bf16[2048,128]{1,0:T(8,128)(2,1)S(1)}, bf16[2048,128]{1,0:T(8,128)(2,1)S(1)}, u32[]{:S(2)}, u32[]{:S(2)}) collective-permute-start(bf16[2048,128]{1,0:T(8,128)(2,1)S(1)} %get-tuple-element.58.tail), channel_id=1, source_target_pairs={{0,1},{1,0},{2,3},{3,2},{4,5},{5,4},{6,7},{7,6},{8,9},{9,8},{10,11... | collective-permute-start | bytes 1572872 | tf_op jit(solution)/shard_map/tail_in_chip/ppermute | solution.py:50
  61.6 3.4 %collective-permute-start.21 = (bf16[128,128]{1,0:T(8,128)(2,1)S(1)}, bf16[128,128]{1,0:T(8,128)(2,1)S(1)}, u32[]{:S(2)}, u32[]{:S(2)}) collective-permute-start(bf16[128,128]{1,0:T(8,128)(2,1)S(1)} %get-tuple-element.59), channel_id=1, source_target_pairs={{0,3},{1,2},{2,1},{3,0},{4,7},{5,6},{6,5},{7,4},{8,11},{9,10},{10,... | collective-permute-start | bytes 98312 | tf_op jit(solution)/shard_map/low_over_head/ppermute | solution.py:739
  63.2 3.9 %collective-permute-start.20 = (bf16[128,128]{1,0:T(8,128)(2,1)S(1)}, bf16[128,128]{1,0:T(8,128)(2,1)S(1)}, u32[]{:S(2)}, u32[]{:S(2)}) collective-permute-start(bf16[128,128]{1,0:T(8,128)(2,1)S(1)} %get-tuple-element.59), channel_id=1, source_target_pairs={{0,2},{2,0},{1,3},{3,1},{4,6},{6,4},{5,7},{7,5},{8,10},{10,8},{9,1... | collective-permute-start | bytes 98312 | tf_op jit(solution)/shard_map/low_over_head/ppermute | solution.py:50

commit v20 on v19

--- a/solution.py
+++ b/solution.py
@@ -599,7 +599,7 @@
     )(own_low, own, *gots, *pieces)
 
 
-def place_kernel(frames, lead, late, rest, tail, tail2, low_head, low_diag, *refs):
+def place_kernel(frames, lead, late, rest, tail, tail2, low_diag, low_head, *refs):
     outs, filled, sems = refs[:4], refs[4:8], refs[8]
     me, half = lax.axis_index("tm"), lax.axis_index("rep")
     first = half == 0
@@ -643,7 +643,7 @@
         out_shape=[jax.ShapeDtypeStruct(shape, F32) for shape in shapes],
         scratch_shapes=[pltpu.VMEM(shape, F32) for shape in shapes] + [pltpu.SemaphoreType.DMA((4,))],
         compiler_params=SMALL,
-    )(tail, tail2, low_head, low_diag)
+    )(tail, tail2, low_diag, low_head)
 
 
 def exchange_plan(

time: 68.8 us -> 68.2 us (level)
    ppermute x1, starting transfers between devices: 1.61 us -> 0.31 us  [exchange_plan(): lax.ppermute(low, ('head', 'rep'), diag)]
    ppermute x8, starting transfers between devices: 1.93 us -> 2.95 us  [swap(): return lax.ppermute(block, axis, [(0, 1), (1, 0)])]
where the time goes in v20:
time: 68.2 us; the launch traced here: 68 us
  starting transfers between devices  28.1 us (41%)
  waiting for transfers between devices  26.3 us (39%)
  Pallas kernels  11.9 us (17%)
  between operations  0.91 us (1%)
  local copies, waits for them, and re-layouts  0.69 us (1%)
    ppermute x12, starting transfers between devices, meet(): return lax.ppermute(block, 'tm', [(j ^ m, j) for j in targets])  23.1 us
    ppermute x12, waiting for transfers between devices, meet(): return lax.ppermute(block, 'tm', [(j ^ m, j) for j in targets])  20 us
    pallas_call x2, Pallas kernels, head_group(): pl.pallas_call(functools.partial(group_kernel, heads, frames, chained, le...  6.7 us
    pallas_call x2, Pallas kernels, pack(): pl.pallas_call(functools.partial(pack_kernel, frames, outputs), in_specs=...  3.51 us
    ppermute x1, waiting for transfers between devices, exchange_plan(): far = lax.ppermute(piece[:cut], 'tm', [(0, 2), (3, 1)])  3.25 us
    ppermute x8, starting transfers between devices, swap(): return lax.ppermute(block, axis, [(0, 1), (1, 0)])  2.95 us
    ppermute x8, waiting for transfers between devices, swap(): return lax.ppermute(block, axis, [(0, 1), (1, 0)])  2.14 us
    ppermute x1, starting transfers between devices, exchange_plan(): far = lax.ppermute(piece[:cut], 'tm', [(0, 2), (3, 1)])  1.82 us
  transfers between devices with their start and end apart: 22, of which 8 were waited for; matrix products, arithmetic and copies ran while one was open for 0% of the time, Pallas kernels for 11%

profile of v20, /device:TPU:0, one launch (start us, length us, event | category | flops | bytes accessed | tf_op | source)
XLA Modules:
  0.0 68.0 jit_solution(15110504431769611587)
XLA Ops:
  0.7 2.6 %shard_map.121 = (bf16[128,1664]{1,0:T(8,128)(2,1)}, bf16[128,640]{1,0:T(8,128)(2,1)}, bf16[128,512]{1,0:T(8,128)(2,1)}, bf16[128,640]{1,0:T(8,128)(2,1)}, bf16[128,512]{1,0:T(8,128)(2,1)}) custom-call(bf16[128,1280]{1,0:T(8,128)(2,1)} %fq_ref.3, bf16[128,1280]{1,0:T(8,128)(2,1)} %do_ref.3, bf16[256,1280]{1,0:T(8,128)(2,1)} %fk_ref.3, ...), custom_call_target="tpu_custom_call" | custom-call | tf_op jit(solution)/shard_map/pallas_call | solution.py:303
  3.3 3.1 %collective-permute-start = (bf16[128,1664]{1,0:T(8,128)(2,1)}, bf16[128,1664]{1,0:T(8,128)(2,1)S(1)}, u32[]{:S(2)}, u32[]{:S(2)}) collective-permute-start(bf16[128,1664]{1,0:T(8,128)(2,1)} %get-tuple-element.33), channel_id=1, source_target_pairs={{4,0},{0,4},{12,8},{8,12},{5,1},{1,5},{13,9},{9,13},{6,2},{2,6},{1... | collective-permute-start | bytes 1277960 | tf_op jit(solution)/shard_map/nearest_over_tm/ppermute | solution.py:676
  6.3 2.6 %collective-permute-start.1 = (bf16[128,640]{1,0:T(8,128)(2,1)}, bf16[128,640]{1,0:T(8,128)(2,1)S(1)}, u32[]{:S(2)}, u32[]{:S(2)}) collective-permute-start(bf16[128,640]{1,0:T(8,128)(2,1)} %get-tuple-element.34), channel_id=1, source_target_pairs={{8,0},{12,4},{0,8},{4,12},{9,1},{13,5},{1,9},{5,13},{10,2},{14,6},... | collective-permute-start | bytes 491528 | tf_op jit(solution)/shard_map/lead_over_tm/ppermute | solution.py:676
  8.9 3.8 %collective-permute-start.6 = (bf16[128,512]{1,0:T(8,128)(2,1)}, bf16[128,512]{1,0:T(8,128)(2,1)S(1)}, u32[]{:S(2)}, u32[]{:S(2)}) collective-permute-start(bf16[128,512]{1,0:T(8,128)(2,1)} %get-tuple-element.44), channel_id=1, source_target_pairs={{12,4},{0,8},{13,5},{1,9},{14,6},{2,10},{15,7},{3,11},{28,20},{16,... | collective-permute-start | bytes 393224 | tf_op jit(solution)/shard_map/rest_over_tm/ppermute | solution.py:676
  12.8 0.7 collective-permute-start.7
  13.5 0.9 %shard_map.120 = (bf16[128,512]{1,0:T(8,128)(2,1)S(1)}, bf16[128,512]{1,0:T(8,128)(2,1)S(1)}, bf16[128,512]{1,0:T(8,128)(2,1)S(1)}, bf16[128,256]{1,0:T(8,128)(2...) custom-call(bf16[128,1280]{1,0:T(8,128)(2,1)S(1)} %copy-done.2, ...), custom_call_target="tpu_custom_call" | custom-call | tf_op jit(solution)/shard_map/pallas_call | solution.py:303
  14.4 6.0 %collective-permute-done.1.refs_1_.refs_3_ = bf16[128,640]{1,0:T(8,128)(2,1)S(1)} collective-permute-done((bf16[128,640]{1,0:T(8,128)(2,1)}, bf16[128,640]{1,0:T(8,128)(2,1)S(1)}, u32[]{:S(2)}, u32[]{:S(2)}) %collective-permute-start.1) | collective-permute-done | bytes 163872 | tf_op jit(solution)/shard_map/lead_over_tm/ppermute | solution.py:676
  20.4 6.4 %collective-permute-done.2.refs_2_.refs_4_ = bf16[128,640]{1,0:T(8,128)(2,1)S(1)} collective-permute-done((bf16[128,640]{1,0:T(8,128)(2,1)}, bf16[128,640]{1,0:T(8,128)(2,1)S(1)}, u32[]{:S(2)}, u32[]{:S(2)}) %collective-permute-start.2) | collective-permute-done | bytes 163872 | tf_op jit(solution)/shard_map/lead_over_tm/ppermute | solution.py:676
  26.9 0.1 collective-permute-start.3
  27.0 0.5 collective-permute-start.8
  27.6 3.5 %collective-permute-start.4 = (bf16[128,512]{1,0:T(8,128)(2,1)S(1)}, bf16[128,512]{1,0:T(8,128)(2,1)S(1)}, u32[]{:S(2)}, u32[]{:S(2)}) collective-permute-start(bf16[128,512]{1,0:T(8,128)(2,1)S(1)} %get-tuple-element.39), channel_id=1, source_target_pairs={{8,0},{12,4},{0,8},{4,12},{9,1},{13,5},{1,9},{5,13},{10,2},{14,6},... | collective-permute-start | bytes 393224 | tf_op jit(solution)/shard_map/late_over_tm/ppermute | solution.py:676
  31.0 1.4 %collective-permute-start.5 = (bf16[128,512]{1,0:T(8,128)(2,1)S(1)}, bf16[128,512]{1,0:T(8,128)(2,1)S(1)}, u32[]{:S(2)}, u32[]{:S(2)}) collective-permute-start(bf16[128,512]{1,0:T(8,128)(2,1)S(1)} %get-tuple-element.40), channel_id=1, source_target_pairs={{12,0},{8,4},{4,8},{0,12},{13,1},{9,5},{5,9},{1,13},{14,2},{10,6},... | collective-permute-start | bytes 393224 | tf_op jit(solution)/shard_map/late_over_tm/ppermute | solution.py:676
  32.4 0.6 copy-done.8
  33.1 3.4 %shard_map.124 = (f32[384,128]{1,0:T(8,128)S(1)}, bf16[384,128]{1,0:T(8,128)(2,1)S(1)}, f32[512,128]{1,0:T(8,128)S(1)}, f32[512,128]{1,0:T(8,128)S(1)}) custom-call(s32[4,4]{1,0:T(4,128)S(1)} %copy-done.8, bf16[128,128]{1,0:T(8,128)(2,1)S(1)} %get-tuple-element.32.refs_1_, bf16[128,1664]{1,0:T(8,128)(2,1)S(1)} %collective-permute-done.refs_0_.refs_2_, ...), custom_call_target="tpu_custom_call" | custom-call | tf_op jit(solution)/shard_map/pallas_call | solution.py:523
  36.5 0.1 collective-permute-start.9
  36.5 4.5 %collective-permute-done.4.refs_1_.refs_8_ = bf16[128,512]{1,0:T(8,128)(2,1)S(1)} collective-permute-done((bf16[128,512]{1,0:T(8,128)(2,1)S(1)}, bf16[128,512]{1,0:T(8,128)(2,1)S(1)}, u32[]{:S(2)}, u32[]{:S(2)}) %collective-permute-start.4) | collective-permute-done | bytes 131104 | tf_op jit(solution)/shard_map/late_over_tm/ppermute | solution.py:676
  41.2 1.4 %collective-permute-start.14 = (bf16[384,128]{1,0:T(8,128)(2,1)S(1)}, bf16[384,128]{1,0:T(8,128)(2,1)S(1)}, u32[]{:S(2)}, u32[]{:S(2)}) collective-permute-start(bf16[384,128]{1,0:T(8,128)(2,1)S(1)} %add_convert_fusion.refs_17_.piece), channel_id=1, source_target_pairs={{12,0},{8,4},{4,8},{0,12},{13,1},{9,5},{5,9},{1,13},{14,2},{10,6},... | collective-permute-start | bytes 294920 | tf_op jit(solution)/shard_map/early_facing_over_tm/ppermute | solution.py:676
  42.6 2.2 %collective-permute-start.13 = (bf16[384,128]{1,0:T(8,128)(2,1)S(1)}, bf16[384,128]{1,0:T(8,128)(2,1)S(1)}, u32[]{:S(2)}, u32[]{:S(2)}) collective-permute-start(bf16[384,128]{1,0:T(8,128)(2,1)S(1)} %add_convert_fusion.refs_17_.piece), channel_id=1, source_target_pairs={{4,0},{0,4},{12,8},{8,12},{5,1},{1,5},{13,9},{9,13},{6,2},{2,6},{1... | collective-permute-start | bytes 294920 | tf_op jit(solution)/shard_map/early_pair_over_tm/ppermute | solution.py:676
  44.8 3.3 %shard_map.126 = (f32[704,128]{1,0:T(8,128)S(1)}, bf16[352,128]{1,0:T(8,128)(2,1)S(1)}, bf16[352,128]{1,0:T(8,128)(2,1)S(1)}) custom-call(s32[4,4]{1,0:T(4,128)S(1)} %copy-done.8, bf16[128,128]{1,0:T(8,128)(2,1)S(1)} %get-tuple-element.32.refs_1_, bf16[128,1664]{1,0:T(8,128)(2,1)S(1)} %collective-permute-done.refs_0_.refs_2_, ...), custom_call_target="tpu_custom_call" | custom-call | tf_op jit(solution)/shard_map/pallas_call | solution.py:523
  48.2 0.5 collective-permute-start.12
  48.7 1.4 %collective-permute-done.13.refs_2_.pair = bf16[384,128]{1,0:T(8,128)(2,1)S(1)} collective-permute-done((bf16[384,128]{1,0:T(8,128)(2,1)S(1)}, bf16[384,128]{1,0:T(8,128)(2,1)S(1)}, u32[]{:S(2)}, u32[]{:S(2)}) %collective-permute-start.13) | collective-permute-done | bytes 98336 | tf_op jit(solution)/shard_map/early_pair_over_tm/ppermute | solution.py:676
  50.1 0.9 %collective-permute-start.15 = (bf16[704,128]{1,0:T(8,128)(2,1)S(1)}, bf16[704,128]{1,0:T(8,128)(2,1)S(1)}, u32[]{:S(2)}, u32[]{:S(2)}) collective-permute-start(bf16[704,128]{1,0:T(8,128)(2,1)S(1)} %get-tuple-element.56), channel_id=1, source_target_pairs={{4,0},{0,4},{12,8},{8,12},{5,1},{1,5},{13,9},{9,13},{6,2},{2,6},{1... | collective-permute-start | bytes 540680 | tf_op jit(solution)/shard_map/late_sums_over_tm/ppermute | solution.py:676
  51.0 1.8 %collective-permute-start.16 = (bf16[320,128]{1,0:T(8,128)(2,1)S(1)}, bf16[320,128]{1,0:T(8,128)(2,1)S(1)}, u32[]{:S(2)}, u32[]{:S(2)}) collective-permute-start(bf16[320,128]{1,0:T(8,128)(2,1)S(1)} %get-tuple-element.57), channel_id=1, source_target_pairs={{8,0},{12,4},{0,8},{4,12},{9,1},{13,5},{1,9},{5,13},{10,2},{14,6},... | collective-permute-start | bytes 245768 | tf_op jit(solution)/shard_map/late_sums_over_tm/ppermute | solution.py:676
  52.8 1.8 %collective-permute-start.17 = (bf16[320,128]{1,0:T(8,128)(2,1)S(1)}, bf16[320,128]{1,0:T(8,128)(2,1)S(1)}, u32[]{:S(2)}, u32[]{:S(2)}) collective-permute-start(bf16[320,128]{1,0:T(8,128)(2,1)S(1)} %get-tuple-element.55.own), channel_id=1, source_target_pairs={{12,0},{8,4},{4,8},{0,12},{13,1},{9,5},{5,9},{1,13},{14,2},{10,6},... | collective-permute-start | bytes 245768 | tf_op jit(solution)/shard_map/late_sums_over_tm/ppermute | solution.py:676
  54.6 1.8 %collective-permute-start.18 = (bf16[192,128]{1,0:T(8,128)(2,1)S(1)}, bf16[192,128]{1,0:T(8,128)(2,1)S(1)}, u32[]{:S(2)}, u32[]{:S(2)}) collective-permute-start(bf16[192,128]{1,0:T(8,128)(2,1)S(1)} %slice.4), channel_id=1, source_target_pairs={{0,8},{12,4},{1,9},{13,5},{2,10},{14,6},{3,11},{15,7},{16,24},{28,... | collective-permute-start | bytes 147464 | tf_op jit(solution)/shard_map/early_lead_over_tm/ppermute | solution.py:731
  56.4 3.2 %collective-permute-done.18.far = bf16[192,128]{1,0:T(8,128)(2,1)S(1)} collective-permute-done((bf16[192,128]{1,0:T(8,128)(2,1)S(1)}, bf16[192,128]{1,0:T(8,128)(2,1)S(1)}, u32[]{:S(2)}, u32[]{:S(2)}) %collective-permute-start.18) | collective-permute-done | bytes 49184 | tf_op jit(solution)/shard_map/early_lead_over_tm/ppermute | solution.py:731
  59.7 1.8 %collective-permute-done.17.last = bf16[320,128]{1,0:T(8,128)(2,1)S(1)} collective-permute-done((bf16[320,128]{1,0:T(8,128)(2,1)S(1)}, bf16[320,128]{1,0:T(8,128)(2,1)S(1)}, u32[]{:S(2)}, u32[]{:S(2)}) %collective-permute-start.17) | collective-permute-done | bytes 81952 | tf_op jit(solution)/shard_map/late_sums_over_tm/ppermute | solution.py:676
  61.6 1.6 %collective-permute-start.21 = (bf16[128,128]{1,0:T(8,128)(2,1)S(1)}, bf16[128,128]{1,0:T(8,128)(2,1)S(1)}, u32[]{:S(2)}, u32[]{:S(2)}) collective-permute-start(bf16[128,128]{1,0:T(8,128)(2,1)S(1)} %get-tuple-element.59), channel_id=1, source_target_pairs={{0,2},{2,0},{1,3},{3,1},{4,6},{6,4},{5,7},{7,5},{8,10},{10,8},{9,1... | collective-permute-start | bytes 98312 | tf_op jit(solution)/shard_map/low_over_head/ppermute | solution.py:50
  63.2 0.3 collective-permute-start.20
  63.5 2.1 %collective-permute-done.21.low_head = bf16[128,128]{1,0:T(8,128)(2,1)S(1)} collective-permute-done((bf16[128,128]{1,0:T(8,128)(2,1)S(1)}, bf16[128,128]{1,0:T(8,128)(2,1)S(1)}, u32[]{:S(2)}, u32[]{:S(2)}) %collective-permute-start.21) | collective-permute-done | bytes 32800 | tf_op jit(solution)/shard_map/low_over_head/ppermute | solution.py:50
  65.6 0.9 %collective-permute-done.20.low_diag = bf16[128,128]{1,0:T(8,128)(2,1)S(1)} collective-permute-done((bf16[128,128]{1,0:T(8,128)(2,1)S(1)}, bf16[128,128]{1,0:T(8,128)(2,1)S(1)}, u32[]{:S(2)}, u32[]{:S(2)}) %collective-permute-start.20) | collective-permute-done | bytes 32800 | tf_op jit(solution)/shard_map/low_over_head/ppermute | solution.py:739
  66.5 1.5 %shard_map.129 = (f32[128,1280]{1,0:T(8,128)}, f32[128,1280]{1,0:T(8,128)}, f32[128,1280]{1,0:T(8,128)}, f32[256,128]{1,0:T(8,128)}) custom-call(bf16[2048,128]{1,0:T(8,128)(2,1)S(1)} %get-tuple-element.58.tail, bf16[2048,128]{1,0:T(8,128)(2,1)S(1)} %collective-permute-done.19.tail2, bf16[128,128]{1,0:T(8,128)(2,1)S(1)} %collective-permute-done.20.low_diag, ...), custom_call_target="tpu_custom_call" | custom-call | tf_op jit(solution)/shard_map/pallas_call | solution.py:639
  (42 shorter events, 0.5 us)
Async XLA Ops:
  0.6 12.8 %copy-start.3 = (bf16[128,1280]{1,0:T(8,128)(2,1)S(1)}, bf16[128,1280]{1,0:T(8,128)(2,1)}, u32[]{:S(2)}) copy-start(bf16[128,1280]{1,0:T(8,128)(2,1)} %do_ref.3) | copy-start | bytes 983044
  0.6 12.8 %copy-start.7 = (bf16[256,128]{1,0:T(8,128)(2,1)S(1)}, bf16[256,128]{1,0:T(8,128)(2,1)}, u32[]{:S(2)}) copy-start(bf16[256,128]{1,0:T(8,128)(2,1)} %t_ref.3) | copy-start | bytes 196612
  0.7 12.8 %copy-start.1 = (bf16[256,1280]{1,0:T(8,128)(2,1)S(1)}, bf16[256,1280]{1,0:T(8,128)(2,1)}, u32[]{:S(2)}) copy-start(bf16[256,1280]{1,0:T(8,128)(2,1)} %fv_ref.3) | copy-start | bytes 1966084
  0.7 12.8 %copy-start = (bf16[256,1280]{1,0:T(8,128)(2,1)S(1)}, bf16[256,1280]{1,0:T(8,128)(2,1)}, u32[]{:S(2)}) copy-start(bf16[256,1280]{1,0:T(8,128)(2,1)} %fk_ref.3) | copy-start | bytes 1966084
  0.7 12.8 %copy-start.2 = (bf16[128,1280]{1,0:T(8,128)(2,1)S(1)}, bf16[128,1280]{1,0:T(8,128)(2,1)}, u32[]{:S(2)}) copy-start(bf16[128,1280]{1,0:T(8,128)(2,1)} %fq_ref.3) | copy-start | bytes 983044
  3.3 23.6 %collective-permute-start = (bf16[128,1664]{1,0:T(8,128)(2,1)}, bf16[128,1664]{1,0:T(8,128)(2,1)S(1)}, u32[]{:S(2)}, u32[]{:S(2)}) collective-permute-start(bf16[128,1664]{1,0:T(8,128)(2,1)} %get-tuple-element.33), channel_id=1, source_target_pairs={{4,0},{0,4},{12,8},{8,12},{5,1},{1,5},{13,9},{9,13},{6,2},{2,6},{1... | collective-permute-start | bytes 1277960 | tf_op jit(solution)/shard_map/nearest_over_tm/ppermute | solution.py:676
  6.3 14.1 %collective-permute-start.1 = (bf16[128,640]{1,0:T(8,128)(2,1)}, bf16[128,640]{1,0:T(8,128)(2,1)S(1)}, u32[]{:S(2)}, u32[]{:S(2)}) collective-permute-start(bf16[128,640]{1,0:T(8,128)(2,1)} %get-tuple-element.34), channel_id=1, source_target_pairs={{8,0},{12,4},{0,8},{4,12},{9,1},{13,5},{1,9},{5,13},{10,2},{14,6},... | collective-permute-start | bytes 491528 | tf_op jit(solution)/shard_map/lead_over_tm/ppermute | solution.py:676
  8.9 17.9 %collective-permute-start.2 = (bf16[128,640]{1,0:T(8,128)(2,1)}, bf16[128,640]{1,0:T(8,128)(2,1)S(1)}, u32[]{:S(2)}, u32[]{:S(2)}) collective-permute-start(bf16[128,640]{1,0:T(8,128)(2,1)} %get-tuple-element.35), channel_id=1, source_target_pairs={{12,0},{8,4},{4,8},{0,12},{13,1},{9,5},{5,9},{1,13},{14,2},{10,6},... | collective-permute-start | bytes 491528 | tf_op jit(solution)/shard_map/lead_over_tm/ppermute | solution.py:676
  8.9 18.0 %collective-permute-start.6 = (bf16[128,512]{1,0:T(8,128)(2,1)}, bf16[128,512]{1,0:T(8,128)(2,1)S(1)}, u32[]{:S(2)}, u32[]{:S(2)}) collective-permute-start(bf16[128,512]{1,0:T(8,128)(2,1)} %get-tuple-element.44), channel_id=1, source_target_pairs={{12,4},{0,8},{13,5},{1,9},{14,6},{2,10},{15,7},{3,11},{28,20},{16,... | collective-permute-start | bytes 393224 | tf_op jit(solution)/shard_map/rest_over_tm/ppermute | solution.py:676
  12.8 14.2 %collective-permute-start.7 = (bf16[128,512]{1,0:T(8,128)(2,1)}, bf16[128,512]{1,0:T(8,128)(2,1)S(1)}, u32[]{:S(2)}, u32[]{:S(2)}) collective-permute-start(bf16[128,512]{1,0:T(8,128)(2,1)} %get-tuple-element.45), channel_id=1, source_target_pairs={{8,4},{4,8},{9,5},{5,9},{10,6},{6,10},{11,7},{7,11},{24,20},{20,24... | collective-permute-start | bytes 393224 | tf_op jit(solution)/shard_map/rest_over_tm/ppermute | solution.py:676
  26.8 5.6 %copy-start.6 = (bf16[128,1280]{1,0:T(8,128)(2,1)S(1)}, bf16[128,1280]{1,0:T(8,128)(2,1)}, u32[]{:S(2)}) copy-start(bf16[128,1280]{1,0:T(8,128)(2,1)} %refs_14_.3) | copy-start | bytes 983044
  26.9 5.6 %copy-start.4 = (bf16[128,1280]{1,0:T(8,128)(2,1)S(1)}, bf16[128,1280]{1,0:T(8,128)(2,1)}, u32[]{:S(2)}) copy-start(bf16[128,1280]{1,0:T(8,128)(2,1)} %refs_12_.1) | copy-start | bytes 983044
  26.9 5.6 %copy-start.5 = (bf16[128,1280]{1,0:T(8,128)(2,1)S(1)}, bf16[128,1280]{1,0:T(8,128)(2,1)}, u32[]{:S(2)}) copy-start(bf16[128,1280]{1,0:T(8,128)(2,1)} %refs_13_.1) | copy-start | bytes 983044
  26.9 5.5 %collective-permute-start.3 = (bf16[128,1152]{1,0:T(8,128)(2,1)S(1)}, bf16[128,1152]{1,0:T(8,128)(2,1)S(1)}, u32[]{:S(2)}, u32[]{:S(2)}) collective-permute-start(bf16[128,1152]{1,0:T(8,128)(2,1)S(1)} %shard_map.122), channel_id=1, source_target_pairs={{0,1},{1,0},{2,3},{3,2},{4,5},{5,4},{6,7},{7,6},{8,9},{9,8},{10,11... | collective-permute-start | bytes 884744 | tf_op jit(solution)/shard_map/lead_in_chip/ppermute | solution.py:50
  27.0 5.4 %collective-permute-start.8 = (bf16[128,768]{1,0:T(8,128)(2,1)S(1)}, bf16[128,768]{1,0:T(8,128)(2,1)S(1)}, u32[]{:S(2)}, u32[]{:S(2)}) collective-permute-start(bf16[128,768]{1,0:T(8,128)(2,1)S(1)} %shard_map.123), channel_id=1, source_target_pairs={{0,1},{1,0},{2,3},{3,2},{4,5},{5,4},{6,7},{7,6},{8,9},{9,8},{10,11... | collective-permute-start | bytes 589832 | tf_op jit(solution)/shard_map/rest_in_chip/ppermute | solution.py:50
  27.6 13.5 %collective-permute-start.4 = (bf16[128,512]{1,0:T(8,128)(2,1)S(1)}, bf16[128,512]{1,0:T(8,128)(2,1)S(1)}, u32[]{:S(2)}, u32[]{:S(2)}) collective-permute-start(bf16[128,512]{1,0:T(8,128)(2,1)S(1)} %get-tuple-element.39), channel_id=1, source_target_pairs={{8,0},{12,4},{0,8},{4,12},{9,1},{13,5},{1,9},{5,13},{10,2},{14,6},... | collective-permute-start | bytes 393224 | tf_op jit(solution)/shard_map/late_over_tm/ppermute | solution.py:676
  31.0 10.0 %collective-permute-start.5 = (bf16[128,512]{1,0:T(8,128)(2,1)S(1)}, bf16[128,512]{1,0:T(8,128)(2,1)S(1)}, u32[]{:S(2)}, u32[]{:S(2)}) collective-permute-start(bf16[128,512]{1,0:T(8,128)(2,1)S(1)} %get-tuple-element.40), channel_id=1, source_target_pairs={{12,0},{8,4},{4,8},{0,12},{13,1},{9,5},{5,9},{1,13},{14,2},{10,6},... | collective-permute-start | bytes 393224 | tf_op jit(solution)/shard_map/late_over_tm/ppermute | solution.py:676
  32.4 0.7 %copy-start.8 = (s32[4,4]{1,0:T(4,128)S(1)}, s32[4,4]{1,0:T(4,128)}, u32[]{:S(2)}) copy-start(s32[4,4]{1,0:T(4,128)} %refs_0_.3) | copy-start | bytes 196
  36.5 4.6 %collective-permute-start.9 = (bf16[384,128]{1,0:T(8,128)(2,1)S(1)}, bf16[384,128]{1,0:T(8,128)(2,1)S(1)}, u32[]{:S(2)}, u32[]{:S(2)}) collective-permute-start(bf16[384,128]{1,0:T(8,128)(2,1)S(1)} %get-tuple-element.47), channel_id=1, source_target_pairs={{0,1},{1,0},{2,3},{3,2},{4,5},{5,4},{6,7},{7,6},{8,9},{9,8},{10,11... | collective-permute-start | bytes 294920 | tf_op jit(solution)/shard_map/early_gradients_in_chip/ppermute | solution.py:50
  41.0 3.7 %collective-permute-start.10 = (bf16[128,768]{1,0:T(8,128)(2,1)S(1)}, bf16[128,768]{1,0:T(8,128)(2,1)S(1)}, u32[]{:S(2)}, u32[]{:S(2)}) collective-permute-start(bf16[128,768]{1,0:T(8,128)(2,1)S(1)} %shard_map.125), channel_id=1, source_target_pairs={{0,1},{1,0},{2,3},{3,2},{4,5},{5,4},{6,7},{7,6},{8,9},{9,8},{10,11... | collective-permute-start | bytes 589832 | tf_op jit(solution)/shard_map/late_in_chip/ppermute | solution.py:50
  41.2 7.6 %collective-permute-start.14 = (bf16[384,128]{1,0:T(8,128)(2,1)S(1)}, bf16[384,128]{1,0:T(8,128)(2,1)S(1)}, u32[]{:S(2)}, u32[]{:S(2)}) collective-permute-start(bf16[384,128]{1,0:T(8,128)(2,1)S(1)} %add_convert_fusion.refs_17_.piece), channel_id=1, source_target_pairs={{12,0},{8,4},{4,8},{0,12},{13,1},{9,5},{5,9},{1,13},{14,2},{10,6},... | collective-permute-start | bytes 294920 | tf_op jit(solution)/shard_map/early_facing_over_tm/ppermute | solution.py:676
  42.6 7.5 %collective-permute-start.13 = (bf16[384,128]{1,0:T(8,128)(2,1)S(1)}, bf16[384,128]{1,0:T(8,128)(2,1)S(1)}, u32[]{:S(2)}, u32[]{:S(2)}) collective-permute-start(bf16[384,128]{1,0:T(8,128)(2,1)S(1)} %add_convert_fusion.refs_17_.piece), channel_id=1, source_target_pairs={{4,0},{0,4},{12,8},{8,12},{5,1},{1,5},{13,9},{9,13},{6,2},{2,6},{1... | collective-permute-start | bytes 294920 | tf_op jit(solution)/shard_map/early_pair_over_tm/ppermute | solution.py:676
  48.1 1.9 %collective-permute-start.11 = (bf16[352,128]{1,0:T(8,128)(2,1)S(1)}, bf16[352,128]{1,0:T(8,128)(2,1)S(1)}, u32[]{:S(2)}, u32[]{:S(2)}) collective-permute-start(bf16[352,128]{1,0:T(8,128)(2,1)S(1)} %get-tuple-element.52), channel_id=1, source_target_pairs={{0,1},{1,0},{2,3},{3,2},{4,5},{5,4},{6,7},{7,6},{8,9},{9,8},{10,11... | collective-permute-start | bytes 270344 | tf_op jit(solution)/shard_map/late_sums_in_chip/ppermute | solution.py:50
  48.2 1.9 %collective-permute-start.12 = (bf16[352,128]{1,0:T(8,128)(2,1)S(1)}, bf16[352,128]{1,0:T(8,128)(2,1)S(1)}, u32[]{:S(2)}, u32[]{:S(2)}) collective-permute-start(bf16[352,128]{1,0:T(8,128)(2,1)S(1)} %get-tuple-element.53), channel_id=1, source_target_pairs={{0,1},{1,0},{2,3},{3,2},{4,5},{5,4},{6,7},{7,6},{8,9},{9,8},{10,11... | collective-permute-start | bytes 270344 | tf_op jit(solution)/shard_map/late_sums_in_chip/ppermute | solution.py:50
  50.1 11.3 %collective-permute-start.15 = (bf16[704,128]{1,0:T(8,128)(2,1)S(1)}, bf16[704,128]{1,0:T(8,128)(2,1)S(1)}, u32[]{:S(2)}, u32[]{:S(2)}) collective-permute-start(bf16[704,128]{1,0:T(8,128)(2,1)S(1)} %get-tuple-element.56), channel_id=1, source_target_pairs={{4,0},{0,4},{12,8},{8,12},{5,1},{1,5},{13,9},{9,13},{6,2},{2,6},{1... | collective-permute-start | bytes 540680 | tf_op jit(solution)/shard_map/late_sums_over_tm/ppermute | solution.py:676
  51.0 8.6 %collective-permute-start.16 = (bf16[320,128]{1,0:T(8,128)(2,1)S(1)}, bf16[320,128]{1,0:T(8,128)(2,1)S(1)}, u32[]{:S(2)}, u32[]{:S(2)}) collective-permute-start(bf16[320,128]{1,0:T(8,128)(2,1)S(1)} %get-tuple-element.57), channel_id=1, source_target_pairs={{8,0},{12,4},{0,8},{4,12},{9,1},{13,5},{1,9},{5,13},{10,2},{14,6},... | collective-permute-start | bytes 245768 | tf_op jit(solution)/shard_map/late_sums_over_tm/ppermute | solution.py:676
  52.8 8.6 %collective-permute-start.17 = (bf16[320,128]{1,0:T(8,128)(2,1)S(1)}, bf16[320,128]{1,0:T(8,128)(2,1)S(1)}, u32[]{:S(2)}, u32[]{:S(2)}) collective-permute-start(bf16[320,128]{1,0:T(8,128)(2,1)S(1)} %get-tuple-element.55.own), channel_id=1, source_target_pairs={{12,0},{8,4},{4,8},{0,12},{13,1},{9,5},{5,9},{1,13},{14,2},{10,6},... | collective-permute-start | bytes 245768 | tf_op jit(solution)/shard_map/late_sums_over_tm/ppermute | solution.py:676
  54.6 5.1 %collective-permute-start.18 = (bf16[192,128]{1,0:T(8,128)(2,1)S(1)}, bf16[192,128]{1,0:T(8,128)(2,1)S(1)}, u32[]{:S(2)}, u32[]{:S(2)}) collective-permute-start(bf16[192,128]{1,0:T(8,128)(2,1)S(1)} %slice.4), channel_id=1, source_target_pairs={{0,8},{12,4},{1,9},{13,5},{2,10},{14,6},{3,11},{15,7},{16,24},{28,... | collective-permute-start | bytes 147464 | tf_op jit(solution)/shard_map/early_lead_over_tm/ppermute | solution.py:731
  61.5 5.0 %collective-permute-start.19 = (bf16[2048,128]{1,0:T(8,128)(2,1)S(1)}, bf16[2048,128]{1,0:T(8,128)(2,1)S(1)}, u32[]{:S(2)}, u32[]{:S(2)}) collective-permute-start(bf16[2048,128]{1,0:T(8,128)(2,1)S(1)} %get-tuple-element.58.tail), channel_id=1, source_target_pairs={{0,1},{1,0},{2,3},{3,2},{4,5},{5,4},{6,7},{7,6},{8,9},{9,8},{10,11... | collective-permute-start | bytes 1572872 | tf_op jit(solution)/shard_map/tail_in_chip/ppermute | solution.py:50
  61.6 4.0 %collective-permute-start.21 = (bf16[128,128]{1,0:T(8,128)(2,1)S(1)}, bf16[128,128]{1,0:T(8,128)(2,1)S(1)}, u32[]{:S(2)}, u32[]{:S(2)}) collective-permute-start(bf16[128,128]{1,0:T(8,128)(2,1)S(1)} %get-tuple-element.59), channel_id=1, source_target_pairs={{0,2},{2,0},{1,3},{3,1},{4,6},{6,4},{5,7},{7,5},{8,10},{10,8},{9,1... | collective-permute-start | bytes 98312 | tf_op jit(solution)/shard_map/low_over_head/ppermute | solution.py:50
  63.2 3.3 %collective-permute-start.20 = (bf16[128,128]{1,0:T(8,128)(2,1)S(1)}, bf16[128,128]{1,0:T(8,128)(2,1)S(1)}, u32[]{:S(2)}, u32[]{:S(2)}) collective-permute-start(bf16[128,128]{1,0:T(8,128)(2,1)S(1)} %get-tuple-element.59), channel_id=1, source_target_pairs={{0,3},{1,2},{2,1},{3,0},{4,7},{5,6},{6,5},{7,4},{8,11},{9,10},{10,... | collective-permute-start | bytes 98312 | tf_op jit(solution)/shard_map/low_over_head/ppermute | solution.py:739

commit v21 on v14

--- a/solution.py
+++ b/solution.py
@@ -15,7 +15,7 @@
 SCALE_2 = SCALE * math.log2(math.e)
 F32 = jnp.float32
 BF16 = jnp.bfloat16
-GIVES = 2
+GIVES = 4
 SMALL = pltpu.CompilerParams(vmem_limit_bytes=16 * 1024 * 1024)
 
 
@@ -731,7 +731,7 @@
         far = lax.ppermute(piece[:cut], "tm", [(0, 2), (3, 1)])
     keep, *gives = head_group([late], band_width, [t_side, late_side], adapters, low, [piece])
     gives = [swap_in_chip("late_sums", g) for g in gives]
-    own_low, sends = hand_out(frames, rows, keep, gives, facing, [pair])
+    own_low, sends = hand_out(frames, rows, keep, gives, facing, [pair, far])
     gots = [meet("late_sums", block, m) for m, block in enumerate(sends, 1)]
     tail, low = collect(rest[1], own_low, sends[2], gots, piece, pair, far, facing)
     diag = [(0, 3), (1, 2), (2, 1), (3, 0)]

time: 68.2 us -> 70.8 us (1.038)
  starting transfers between devices: 28.2 us -> 29.8 us
  waiting for transfers between devices: 26.3 us -> 27.3 us
    ppermute x12, waiting for transfers between devices: 19.8 us -> 23.4 us  [meet(): return lax.ppermute(block, 'tm', [(j ^ m, j) for j in targets])]
    ppermute x1, waiting for transfers between devices: 3.45 us -> 0.01 us  [exchange_plan(): far = lax.ppermute(piece[:cut], 'tm', [(0, 2), (3, 1)])]
    ppermute x1, starting transfers between devices: 1.82 us -> 2.91 us  [exchange_plan(): far = lax.ppermute(piece[:cut], 'tm', [(0, 2), (3, 1)])]
    ppermute x8 -> x10, waiting for transfers between devices: 2.14 us -> 3 us  [swap(): return lax.ppermute(block, axis, [(0, 1), (1, 0)])]
    ppermute x8 -> x10, starting transfers between devices: 2.95 us -> 3.46 us  [swap(): return lax.ppermute(block, axis, [(0, 1), (1, 0)])]
  transfers between devices with their start and end apart: 22 -> 24, of which waited for: 8 -> 11; matrix products, arithmetic and copies ran while one was open for 0% -> 0% of each run, Pallas kernels for 11% -> 11%
where the time goes in v21:
time: 70.8 us; the launch traced here: 70.6 us
  starting transfers between devices  29.8 us (42%)
  waiting for transfers between devices  27.3 us (39%)
  Pallas kernels  11.9 us (17%)
  between operations  0.92 us (1%)
    ppermute x12, waiting for transfers between devices, meet(): return lax.ppermute(block, 'tm', [(j ^ m, j) for j in targets])  23.4 us
    ppermute x12, starting transfers between devices, meet(): return lax.ppermute(block, 'tm', [(j ^ m, j) for j in targets])  23.1 us
    pallas_call x2, Pallas kernels, head_group(): pl.pallas_call(functools.partial(group_kernel, heads, frames, chained, le...  6.73 us
    pallas_call x2, Pallas kernels, pack(): pl.pallas_call(functools.partial(pack_kernel, frames, outputs), in_specs=...  3.51 us
    ppermute x10, starting transfers between devices, swap(): return lax.ppermute(block, axis, [(0, 1), (1, 0)])  3.46 us
    ppermute x10, waiting for transfers between devices, swap(): return lax.ppermute(block, axis, [(0, 1), (1, 0)])  3 us
    ppermute x1, starting transfers between devices, exchange_plan(): far = lax.ppermute(piece[:cut], 'tm', [(0, 2), (3, 1)])  2.91 us
    pallas_call x1, Pallas kernels, place(): pl.pallas_call(functools.partial(place_kernel, frames, lead, late, rest),...  1.5 us
  transfers between devices with their start and end apart: 24, of which 11 were waited for; matrix products, arithmetic and copies ran while one was open for 0% of the time, Pallas kernels for 11%

profile of v21, /device:TPU:0, one launch (start us, length us, event | category | flops | bytes accessed | tf_op | source)
XLA Modules:
  0.0 70.6 jit_solution(3476208575228914773)
XLA Ops:
  0.7 2.6 %shard_map.121 = (bf16[128,1664]{1,0:T(8,128)(2,1)}, bf16[128,640]{1,0:T(8,128)(2,1)}, bf16[128,512]{1,0:T(8,128)(2,1)}, bf16[128,640]{1,0:T(8,128)(2,1)}, bf16[128,512]{1,0:T(8,128)(2,1)}) custom-call(bf16[128,1280]{1,0:T(8,128)(2,1)} %fq_ref.3, bf16[128,1280]{1,0:T(8,128)(2,1)} %do_ref.3, bf16[256,1280]{1,0:T(8,128)(2,1)} %fk_ref.3, ...), custom_call_target="tpu_custom_call" | custom-call | tf_op jit(solution)/shard_map/pallas_call | solution.py:303
  3.3 3.1 %collective-permute-start = (bf16[128,1664]{1,0:T(8,128)(2,1)}, bf16[128,1664]{1,0:T(8,128)(2,1)S(1)}, u32[]{:S(2)}, u32[]{:S(2)}) collective-permute-start(bf16[128,1664]{1,0:T(8,128)(2,1)} %get-tuple-element.35), channel_id=1, source_target_pairs={{4,0},{0,4},{12,8},{8,12},{5,1},{1,5},{13,9},{9,13},{6,2},{2,6},{1... | collective-permute-start | bytes 1277960 | tf_op jit(solution)/shard_map/nearest_over_tm/ppermute | solution.py:676
  6.3 2.6 %collective-permute-start.1 = (bf16[128,640]{1,0:T(8,128)(2,1)}, bf16[128,640]{1,0:T(8,128)(2,1)S(1)}, u32[]{:S(2)}, u32[]{:S(2)}) collective-permute-start(bf16[128,640]{1,0:T(8,128)(2,1)} %get-tuple-element.36), channel_id=1, source_target_pairs={{8,0},{12,4},{0,8},{4,12},{9,1},{13,5},{1,9},{5,13},{10,2},{14,6},... | collective-permute-start | bytes 491528 | tf_op jit(solution)/shard_map/lead_over_tm/ppermute | solution.py:676
  8.9 3.8 %collective-permute-start.6 = (bf16[128,512]{1,0:T(8,128)(2,1)}, bf16[128,512]{1,0:T(8,128)(2,1)S(1)}, u32[]{:S(2)}, u32[]{:S(2)}) collective-permute-start(bf16[128,512]{1,0:T(8,128)(2,1)} %get-tuple-element.46), channel_id=1, source_target_pairs={{12,4},{0,8},{13,5},{1,9},{14,6},{2,10},{15,7},{3,11},{28,20},{16,... | collective-permute-start | bytes 393224 | tf_op jit(solution)/shard_map/rest_over_tm/ppermute | solution.py:676
  12.7 0.7 collective-permute-start.7
  13.5 0.9 %shard_map.120 = (bf16[128,512]{1,0:T(8,128)(2,1)S(1)}, bf16[128,512]{1,0:T(8,128)(2,1)S(1)}, bf16[128,512]{1,0:T(8,128)(2,1)S(1)}, bf16[128,256]{1,0:T(8,128)(2...) custom-call(bf16[128,1280]{1,0:T(8,128)(2,1)S(1)} %copy-done.2, ...), custom_call_target="tpu_custom_call" | custom-call | tf_op jit(solution)/shard_map/pallas_call | solution.py:303
  14.4 6.0 %collective-permute-done.1.refs_1_.refs_3_ = bf16[128,640]{1,0:T(8,128)(2,1)S(1)} collective-permute-done((bf16[128,640]{1,0:T(8,128)(2,1)}, bf16[128,640]{1,0:T(8,128)(2,1)S(1)}, u32[]{:S(2)}, u32[]{:S(2)}) %collective-permute-start.1) | collective-permute-done | bytes 163872 | tf_op jit(solution)/shard_map/lead_over_tm/ppermute | solution.py:676
  20.4 6.4 %collective-permute-done.2.refs_2_.refs_4_ = bf16[128,640]{1,0:T(8,128)(2,1)S(1)} collective-permute-done((bf16[128,640]{1,0:T(8,128)(2,1)}, bf16[128,640]{1,0:T(8,128)(2,1)S(1)}, u32[]{:S(2)}, u32[]{:S(2)}) %collective-permute-start.2) | collective-permute-done | bytes 163872 | tf_op jit(solution)/shard_map/lead_over_tm/ppermute | solution.py:676
  27.0 0.5 collective-permute-start.8
  27.6 3.5 %collective-permute-start.4 = (bf16[128,512]{1,0:T(8,128)(2,1)S(1)}, bf16[128,512]{1,0:T(8,128)(2,1)S(1)}, u32[]{:S(2)}, u32[]{:S(2)}) collective-permute-start(bf16[128,512]{1,0:T(8,128)(2,1)S(1)} %get-tuple-element.41), channel_id=1, source_target_pairs={{8,0},{12,4},{0,8},{4,12},{9,1},{13,5},{1,9},{5,13},{10,2},{14,6},... | collective-permute-start | bytes 393224 | tf_op jit(solution)/shard_map/late_over_tm/ppermute | solution.py:676
  31.0 1.4 %collective-permute-start.5 = (bf16[128,512]{1,0:T(8,128)(2,1)S(1)}, bf16[128,512]{1,0:T(8,128)(2,1)S(1)}, u32[]{:S(2)}, u32[]{:S(2)}) collective-permute-start(bf16[128,512]{1,0:T(8,128)(2,1)S(1)} %get-tuple-element.42), channel_id=1, source_target_pairs={{12,0},{8,4},{4,8},{0,12},{13,1},{9,5},{5,9},{1,13},{14,2},{10,6},... | collective-permute-start | bytes 393224 | tf_op jit(solution)/shard_map/late_over_tm/ppermute | solution.py:676
  32.4 0.6 copy-done.8
  33.1 3.4 %shard_map.124 = (f32[384,128]{1,0:T(8,128)S(1)}, bf16[384,128]{1,0:T(8,128)(2,1)S(1)}, f32[512,128]{1,0:T(8,128)S(1)}, f32[512,128]{1,0:T(8,128)S(1)}) custom-call(s32[4,4]{1,0:T(4,128)S(1)} %copy-done.8, bf16[128,128]{1,0:T(8,128)(2,1)S(1)} %get-tuple-element.34.refs_1_, bf16[128,1664]{1,0:T(8,128)(2,1)S(1)} %collective-permute-done.refs_0_.refs_2_, ...), custom_call_target="tpu_custom_call" | custom-call | tf_op jit(solution)/shard_map/pallas_call | solution.py:523
  36.5 4.5 %collective-permute-done.4.refs_1_.refs_8_ = bf16[128,512]{1,0:T(8,128)(2,1)S(1)} collective-permute-done((bf16[128,512]{1,0:T(8,128)(2,1)S(1)}, bf16[128,512]{1,0:T(8,128)(2,1)S(1)}, u32[]{:S(2)}, u32[]{:S(2)}) %collective-permute-start.4) | collective-permute-done | bytes 131104 | tf_op jit(solution)/shard_map/late_over_tm/ppermute | solution.py:676
  41.2 1.4 %collective-permute-start.15 = (bf16[384,128]{1,0:T(8,128)(2,1)S(1)}, bf16[384,128]{1,0:T(8,128)(2,1)S(1)}, u32[]{:S(2)}, u32[]{:S(2)}) collective-permute-start(bf16[384,128]{1,0:T(8,128)(2,1)S(1)} %add_convert_fusion.refs_17_.piece), channel_id=1, source_target_pairs={{12,0},{8,4},{4,8},{0,12},{13,1},{9,5},{5,9},{1,13},{14,2},{10,6},... | collective-permute-start | bytes 294920 | tf_op jit(solution)/shard_map/early_gradients_over_tm/ppermute | solution.py:676
  42.6 2.2 %collective-permute-start.16 = (bf16[384,128]{1,0:T(8,128)(2,1)S(1)}, bf16[384,128]{1,0:T(8,128)(2,1)S(1)}, u32[]{:S(2)}, u32[]{:S(2)}) collective-permute-start(bf16[384,128]{1,0:T(8,128)(2,1)S(1)} %add_convert_fusion.refs_17_.piece), channel_id=1, source_target_pairs={{4,0},{0,4},{12,8},{8,12},{5,1},{1,5},{13,9},{9,13},{6,2},{2,6},{1... | collective-permute-start | bytes 294920 | tf_op jit(solution)/shard_map/early_gradients_over_tm/ppermute | solution.py:676
  44.8 2.9 %collective-permute-start.17 = (bf16[192,128]{1,0:T(8,128)(2,1)S(1)}, bf16[192,128]{1,0:T(8,128)(2,1)S(1)}, u32[]{:S(2)}, u32[]{:S(2)}) collective-permute-start(bf16[192,128]{1,0:T(8,128)(2,1)S(1)} %slice.4), channel_id=1, source_target_pairs={{0,8},{12,4},{1,9},{13,5},{2,10},{14,6},{3,11},{15,7},{16,24},{28,... | collective-permute-start | bytes 147464 | tf_op jit(solution)/shard_map/early_lead_over_tm/ppermute | solution.py:731
  47.7 3.4 %shard_map.126 = (f32[704,128]{1,0:T(8,128)S(1)}, bf16[176,128]{1,0:T(8,128)(2,1)S(1)}, bf16[176,128]{1,0:T(8,128)(2,1)S(1)}, bf16[176,128]{1,0:T(8,128)(2,1)S(1)}, bf16[176,128]{1,0:T(8,128)(2,1)S(1)}) custom-call(s32[4,4]{1,0:T(4,128)S(1)} %copy-done.8, bf16[128,128]{1,0:T(8,128)(2,1)S(1)} %get-tuple-element.34.refs_1_, ...), custom_call_target="tpu_custom_call" | custom-call | tf_op jit(solution)/shard_map/pallas_call | solution.py:523
  51.2 0.5 collective-permute-start.12
  51.8 0.4 collective-permute-start.14
  52.2 0.2 collective-permute-done.11.refs_0_
  52.6 0.4 collective-permute-done.13.refs_2_
  53.1 0.3 collective-permute-start.18
  53.5 1.7 %collective-permute-start.19 = (bf16[320,128]{1,0:T(8,128)(2,1)S(1)}, bf16[320,128]{1,0:T(8,128)(2,1)S(1)}, u32[]{:S(2)}, u32[]{:S(2)}) collective-permute-start(bf16[320,128]{1,0:T(8,128)(2,1)S(1)} %get-tuple-element.61), channel_id=1, source_target_pairs={{8,0},{12,4},{0,8},{4,12},{9,1},{13,5},{1,9},{5,13},{10,2},{14,6},... | collective-permute-start | bytes 245768 | tf_op jit(solution)/shard_map/late_sums_over_tm/ppermute | solution.py:676
  55.1 2.5 %collective-permute-start.20 = (bf16[320,128]{1,0:T(8,128)(2,1)S(1)}, bf16[320,128]{1,0:T(8,128)(2,1)S(1)}, u32[]{:S(2)}, u32[]{:S(2)}) collective-permute-start(bf16[320,128]{1,0:T(8,128)(2,1)S(1)} %get-tuple-element.59.own), channel_id=1, source_target_pairs={{12,0},{8,4},{4,8},{0,12},{13,1},{9,5},{5,9},{1,13},{14,2},{10,6},... | collective-permute-start | bytes 245768 | tf_op jit(solution)/shard_map/late_sums_over_tm/ppermute | solution.py:676
  57.6 2.6 %collective-permute-done.19.third = bf16[320,128]{1,0:T(8,128)(2,1)S(1)} collective-permute-done((bf16[320,128]{1,0:T(8,128)(2,1)S(1)}, bf16[320,128]{1,0:T(8,128)(2,1)S(1)}, u32[]{:S(2)}, u32[]{:S(2)}) %collective-permute-start.19) | collective-permute-done | bytes 81952 | tf_op jit(solution)/shard_map/late_sums_over_tm/ppermute | solution.py:676
  60.2 3.9 %collective-permute-done.20.last = bf16[320,128]{1,0:T(8,128)(2,1)S(1)} collective-permute-done((bf16[320,128]{1,0:T(8,128)(2,1)S(1)}, bf16[320,128]{1,0:T(8,128)(2,1)S(1)}, u32[]{:S(2)}, u32[]{:S(2)}) %collective-permute-start.20) | collective-permute-done | bytes 81952 | tf_op jit(solution)/shard_map/late_sums_over_tm/ppermute | solution.py:676
  64.2 1.6 %collective-permute-start.22 = (bf16[128,128]{1,0:T(8,128)(2,1)S(1)}, bf16[128,128]{1,0:T(8,128)(2,1)S(1)}, u32[]{:S(2)}, u32[]{:S(2)}) collective-permute-start(bf16[128,128]{1,0:T(8,128)(2,1)S(1)} %get-tuple-element.63), channel_id=1, source_target_pairs={{0,2},{2,0},{1,3},{3,1},{4,6},{6,4},{5,7},{7,5},{8,10},{10,8},{9,1... | collective-permute-start | bytes 98312 | tf_op jit(solution)/shard_map/low_over_head/ppermute | solution.py:50
  65.8 0.3 collective-permute-start.23
  66.1 2.1 %collective-permute-done.22.low_head = bf16[128,128]{1,0:T(8,128)(2,1)S(1)} collective-permute-done((bf16[128,128]{1,0:T(8,128)(2,1)S(1)}, bf16[128,128]{1,0:T(8,128)(2,1)S(1)}, u32[]{:S(2)}, u32[]{:S(2)}) %collective-permute-start.22) | collective-permute-done | bytes 32800 | tf_op jit(solution)/shard_map/low_over_head/ppermute | solution.py:50
  68.2 0.9 %collective-permute-done.23.low_diag = bf16[128,128]{1,0:T(8,128)(2,1)S(1)} collective-permute-done((bf16[128,128]{1,0:T(8,128)(2,1)S(1)}, bf16[128,128]{1,0:T(8,128)(2,1)S(1)}, u32[]{:S(2)}, u32[]{:S(2)}) %collective-permute-start.23) | collective-permute-done | bytes 32800 | tf_op jit(solution)/shard_map/low_over_head/ppermute | solution.py:739
  69.1 1.5 %shard_map.129 = (f32[128,1280]{1,0:T(8,128)}, f32[128,1280]{1,0:T(8,128)}, f32[128,1280]{1,0:T(8,128)}, f32[256,128]{1,0:T(8,128)}) custom-call(bf16[2048,128]{1,0:T(8,128)(2,1)S(1)} %get-tuple-element.62.tail, bf16[2048,128]{1,0:T(8,128)(2,1)S(1)} %collective-permute-done.21.tail2, bf16[128,128]{1,0:T(8,128)(2,1)S(1)} %collective-permute-done.22.low_head, ...), custom_call_target="tpu_custom_call" | custom-call | tf_op jit(solution)/shard_map/pallas_call | solution.py:639
  (46 shorter events, 1.1 us)
Async XLA Ops:
  0.6 12.8 %copy-start.2 = (bf16[128,1280]{1,0:T(8,128)(2,1)S(1)}, bf16[128,1280]{1,0:T(8,128)(2,1)}, u32[]{:S(2)}) copy-start(bf16[128,1280]{1,0:T(8,128)(2,1)} %fq_ref.3) | copy-start | bytes 983044
  0.6 12.8 %copy-start.3 = (bf16[128,1280]{1,0:T(8,128)(2,1)S(1)}, bf16[128,1280]{1,0:T(8,128)(2,1)}, u32[]{:S(2)}) copy-start(bf16[128,1280]{1,0:T(8,128)(2,1)} %do_ref.3) | copy-start | bytes 983044
  0.7 12.8 %copy-start = (bf16[256,1280]{1,0:T(8,128)(2,1)S(1)}, bf16[256,1280]{1,0:T(8,128)(2,1)}, u32[]{:S(2)}) copy-start(bf16[256,1280]{1,0:T(8,128)(2,1)} %fk_ref.3) | copy-start | bytes 1966084
  0.7 12.8 %copy-start.1 = (bf16[256,1280]{1,0:T(8,128)(2,1)S(1)}, bf16[256,1280]{1,0:T(8,128)(2,1)}, u32[]{:S(2)}) copy-start(bf16[256,1280]{1,0:T(8,128)(2,1)} %fv_ref.3) | copy-start | bytes 1966084
  0.7 12.8 %copy-start.7 = (bf16[256,128]{1,0:T(8,128)(2,1)S(1)}, bf16[256,128]{1,0:T(8,128)(2,1)}, u32[]{:S(2)}) copy-start(bf16[256,128]{1,0:T(8,128)(2,1)} %t_ref.3) | copy-start | bytes 196612
  3.3 23.6 %collective-permute-start = (bf16[128,1664]{1,0:T(8,128)(2,1)}, bf16[128,1664]{1,0:T(8,128)(2,1)S(1)}, u32[]{:S(2)}, u32[]{:S(2)}) collective-permute-start(bf16[128,1664]{1,0:T(8,128)(2,1)} %get-tuple-element.35), channel_id=1, source_target_pairs={{4,0},{0,4},{12,8},{8,12},{5,1},{1,5},{13,9},{9,13},{6,2},{2,6},{1... | collective-permute-start | bytes 1277960 | tf_op jit(solution)/shard_map/nearest_over_tm/ppermute | solution.py:676
  6.3 14.1 %collective-permute-start.1 = (bf16[128,640]{1,0:T(8,128)(2,1)}, bf16[128,640]{1,0:T(8,128)(2,1)S(1)}, u32[]{:S(2)}, u32[]{:S(2)}) collective-permute-start(bf16[128,640]{1,0:T(8,128)(2,1)} %get-tuple-element.36), channel_id=1, source_target_pairs={{8,0},{12,4},{0,8},{4,12},{9,1},{13,5},{1,9},{5,13},{10,2},{14,6},... | collective-permute-start | bytes 491528 | tf_op jit(solution)/shard_map/lead_over_tm/ppermute | solution.py:676
  8.9 17.9 %collective-permute-start.2 = (bf16[128,640]{1,0:T(8,128)(2,1)}, bf16[128,640]{1,0:T(8,128)(2,1)S(1)}, u32[]{:S(2)}, u32[]{:S(2)}) collective-permute-start(bf16[128,640]{1,0:T(8,128)(2,1)} %get-tuple-element.37), channel_id=1, source_target_pairs={{12,0},{8,4},{4,8},{0,12},{13,1},{9,5},{5,9},{1,13},{14,2},{10,6},... | collective-permute-start | bytes 491528 | tf_op jit(solution)/shard_map/lead_over_tm/ppermute | solution.py:676
  8.9 18.0 %collective-permute-start.6 = (bf16[128,512]{1,0:T(8,128)(2,1)}, bf16[128,512]{1,0:T(8,128)(2,1)S(1)}, u32[]{:S(2)}, u32[]{:S(2)}) collective-permute-start(bf16[128,512]{1,0:T(8,128)(2,1)} %get-tuple-element.46), channel_id=1, source_target_pairs={{12,4},{0,8},{13,5},{1,9},{14,6},{2,10},{15,7},{3,11},{28,20},{16,... | collective-permute-start | bytes 393224 | tf_op jit(solution)/shard_map/rest_over_tm/ppermute | solution.py:676
  12.7 14.2 %collective-permute-start.7 = (bf16[128,512]{1,0:T(8,128)(2,1)}, bf16[128,512]{1,0:T(8,128)(2,1)S(1)}, u32[]{:S(2)}, u32[]{:S(2)}) collective-permute-start(bf16[128,512]{1,0:T(8,128)(2,1)} %get-tuple-element.47), channel_id=1, source_target_pairs={{8,4},{4,8},{9,5},{5,9},{10,6},{6,10},{11,7},{7,11},{24,20},{20,24... | collective-permute-start | bytes 393224 | tf_op jit(solution)/shard_map/rest_over_tm/ppermute | solution.py:676
  26.8 5.6 %copy-start.6 = (bf16[128,1280]{1,0:T(8,128)(2,1)S(1)}, bf16[128,1280]{1,0:T(8,128)(2,1)}, u32[]{:S(2)}) copy-start(bf16[128,1280]{1,0:T(8,128)(2,1)} %refs_14_.3) | copy-start | bytes 983044
  26.9 5.6 %copy-start.4 = (bf16[128,1280]{1,0:T(8,128)(2,1)S(1)}, bf16[128,1280]{1,0:T(8,128)(2,1)}, u32[]{:S(2)}) copy-start(bf16[128,1280]{1,0:T(8,128)(2,1)} %refs_12_.1) | copy-start | bytes 983044
  26.9 5.6 %copy-start.5 = (bf16[128,1280]{1,0:T(8,128)(2,1)S(1)}, bf16[128,1280]{1,0:T(8,128)(2,1)}, u32[]{:S(2)}) copy-start(bf16[128,1280]{1,0:T(8,128)(2,1)} %refs_13_.1) | copy-start | bytes 983044
  26.9 5.5 %collective-permute-start.3 = (bf16[128,1152]{1,0:T(8,128)(2,1)S(1)}, bf16[128,1152]{1,0:T(8,128)(2,1)S(1)}, u32[]{:S(2)}, u32[]{:S(2)}) collective-permute-start(bf16[128,1152]{1,0:T(8,128)(2,1)S(1)} %shard_map.122), channel_id=1, source_target_pairs={{0,1},{1,0},{2,3},{3,2},{4,5},{5,4},{6,7},{7,6},{8,9},{9,8},{10,11... | collective-permute-start | bytes 884744 | tf_op jit(solution)/shard_map/lead_in_chip/ppermute | solution.py:50
  27.0 5.4 %collective-permute-start.8 = (bf16[128,768]{1,0:T(8,128)(2,1)S(1)}, bf16[128,768]{1,0:T(8,128)(2,1)S(1)}, u32[]{:S(2)}, u32[]{:S(2)}) collective-permute-start(bf16[128,768]{1,0:T(8,128)(2,1)S(1)} %shard_map.123), channel_id=1, source_target_pairs={{0,1},{1,0},{2,3},{3,2},{4,5},{5,4},{6,7},{7,6},{8,9},{9,8},{10,11... | collective-permute-start | bytes 589832 | tf_op jit(solution)/shard_map/rest_in_chip/ppermute | solution.py:50
  27.6 13.5 %collective-permute-start.4 = (bf16[128,512]{1,0:T(8,128)(2,1)S(1)}, bf16[128,512]{1,0:T(8,128)(2,1)S(1)}, u32[]{:S(2)}, u32[]{:S(2)}) collective-permute-start(bf16[128,512]{1,0:T(8,128)(2,1)S(1)} %get-tuple-element.41), channel_id=1, source_target_pairs={{8,0},{12,4},{0,8},{4,12},{9,1},{13,5},{1,9},{5,13},{10,2},{14,6},... | collective-permute-start | bytes 393224 | tf_op jit(solution)/shard_map/late_over_tm/ppermute | solution.py:676
  31.0 10.0 %collective-permute-start.5 = (bf16[128,512]{1,0:T(8,128)(2,1)S(1)}, bf16[128,512]{1,0:T(8,128)(2,1)S(1)}, u32[]{:S(2)}, u32[]{:S(2)}) collective-permute-start(bf16[128,512]{1,0:T(8,128)(2,1)S(1)} %get-tuple-element.42), channel_id=1, source_target_pairs={{12,0},{8,4},{4,8},{0,12},{13,1},{9,5},{5,9},{1,13},{14,2},{10,6},... | collective-permute-start | bytes 393224 | tf_op jit(solution)/shard_map/late_over_tm/ppermute | solution.py:676
  36.5 4.6 %collective-permute-start.9 = (bf16[384,128]{1,0:T(8,128)(2,1)S(1)}, bf16[384,128]{1,0:T(8,128)(2,1)S(1)}, u32[]{:S(2)}, u32[]{:S(2)}) collective-permute-start(bf16[384,128]{1,0:T(8,128)(2,1)S(1)} %get-tuple-element.49), channel_id=1, source_target_pairs={{0,1},{1,0},{2,3},{3,2},{4,5},{5,4},{6,7},{7,6},{8,9},{9,8},{10,11... | collective-permute-start | bytes 294920 | tf_op jit(solution)/shard_map/early_gradients_in_chip/ppermute | solution.py:50
  41.0 6.7 %collective-permute-start.10 = (bf16[128,1536]{1,0:T(8,128)(2,1)S(1)}, bf16[128,1536]{1,0:T(8,128)(2,1)S(1)}, u32[]{:S(2)}, u32[]{:S(2)}) collective-permute-start(bf16[128,1536]{1,0:T(8,128)(2,1)S(1)} %shard_map.125), channel_id=1, source_target_pairs={{0,1},{1,0},{2,3},{3,2},{4,5},{5,4},{6,7},{7,6},{8,9},{9,8},{10,11... | collective-permute-start | bytes 1179656 | tf_op jit(solution)/shard_map/late_in_chip/ppermute | solution.py:50
  41.2 10.6 %collective-permute-start.15 = (bf16[384,128]{1,0:T(8,128)(2,1)S(1)}, bf16[384,128]{1,0:T(8,128)(2,1)S(1)}, u32[]{:S(2)}, u32[]{:S(2)}) collective-permute-start(bf16[384,128]{1,0:T(8,128)(2,1)S(1)} %add_convert_fusion.refs_17_.piece), channel_id=1, source_target_pairs={{12,0},{8,4},{4,8},{0,12},{13,1},{9,5},{5,9},{1,13},{14,2},{10,6},... | collective-permute-start | bytes 294920 | tf_op jit(solution)/shard_map/early_gradients_over_tm/ppermute | solution.py:676
  42.6 9.6 %collective-permute-start.16 = (bf16[384,128]{1,0:T(8,128)(2,1)S(1)}, bf16[384,128]{1,0:T(8,128)(2,1)S(1)}, u32[]{:S(2)}, u32[]{:S(2)}) collective-permute-start(bf16[384,128]{1,0:T(8,128)(2,1)S(1)} %add_convert_fusion.refs_17_.piece), channel_id=1, source_target_pairs={{4,0},{0,4},{12,8},{8,12},{5,1},{1,5},{13,9},{9,13},{6,2},{2,6},{1... | collective-permute-start | bytes 294920 | tf_op jit(solution)/shard_map/early_gradients_over_tm/ppermute | solution.py:676
  44.8 6.9 %collective-permute-start.17 = (bf16[192,128]{1,0:T(8,128)(2,1)S(1)}, bf16[192,128]{1,0:T(8,128)(2,1)S(1)}, u32[]{:S(2)}, u32[]{:S(2)}) collective-permute-start(bf16[192,128]{1,0:T(8,128)(2,1)S(1)} %slice.4), channel_id=1, source_target_pairs={{0,8},{12,4},{1,9},{13,5},{2,10},{14,6},{3,11},{15,7},{16,24},{28,... | collective-permute-start | bytes 147464 | tf_op jit(solution)/shard_map/early_lead_over_tm/ppermute | solution.py:731
  51.1 1.3 %collective-permute-start.11 = (bf16[176,128]{1,0:T(8,128)(2,1)S(1)}, bf16[176,128]{1,0:T(8,128)(2,1)S(1)}, u32[]{:S(2)}, u32[]{:S(2)}) collective-permute-start(bf16[176,128]{1,0:T(8,128)(2,1)S(1)} %get-tuple-element.54), channel_id=1, source_target_pairs={{0,1},{1,0},{2,3},{3,2},{4,5},{5,4},{6,7},{7,6},{8,9},{9,8},{10,11... | collective-permute-start | bytes 135176 | tf_op jit(solution)/shard_map/late_sums_in_chip/ppermute | solution.py:50
  51.2 1.4 %collective-permute-start.12 = (bf16[176,128]{1,0:T(8,128)(2,1)S(1)}, bf16[176,128]{1,0:T(8,128)(2,1)S(1)}, u32[]{:S(2)}, u32[]{:S(2)}) collective-permute-start(bf16[176,128]{1,0:T(8,128)(2,1)S(1)} %get-tuple-element.55), channel_id=1, source_target_pairs={{0,1},{1,0},{2,3},{3,2},{4,5},{5,4},{6,7},{7,6},{8,9},{9,8},{10,11... | collective-permute-start | bytes 135176 | tf_op jit(solution)/shard_map/late_sums_in_chip/ppermute | solution.py:50
  51.7 1.2 %collective-permute-start.13 = (bf16[176,128]{1,0:T(8,128)(2,1)S(1)}, bf16[176,128]{1,0:T(8,128)(2,1)S(1)}, u32[]{:S(2)}, u32[]{:S(2)}) collective-permute-start(bf16[176,128]{1,0:T(8,128)(2,1)S(1)} %get-tuple-element.56), channel_id=1, source_target_pairs={{0,1},{1,0},{2,3},{3,2},{4,5},{5,4},{6,7},{7,6},{8,9},{9,8},{10,11... | collective-permute-start | bytes 135176 | tf_op jit(solution)/shard_map/late_sums_in_chip/ppermute | solution.py:50
  51.8 1.3 %collective-permute-start.14 = (bf16[176,128]{1,0:T(8,128)(2,1)S(1)}, bf16[176,128]{1,0:T(8,128)(2,1)S(1)}, u32[]{:S(2)}, u32[]{:S(2)}) collective-permute-start(bf16[176,128]{1,0:T(8,128)(2,1)S(1)} %get-tuple-element.57), channel_id=1, source_target_pairs={{0,1},{1,0},{2,3},{3,2},{4,5},{5,4},{6,7},{7,6},{8,9},{9,8},{10,11... | collective-permute-start | bytes 135176 | tf_op jit(solution)/shard_map/late_sums_in_chip/ppermute | solution.py:50
  53.1 10.9 %collective-permute-start.18 = (bf16[704,128]{1,0:T(8,128)(2,1)S(1)}, bf16[704,128]{1,0:T(8,128)(2,1)S(1)}, u32[]{:S(2)}, u32[]{:S(2)}) collective-permute-start(bf16[704,128]{1,0:T(8,128)(2,1)S(1)} %get-tuple-element.60), channel_id=1, source_target_pairs={{4,0},{0,4},{12,8},{8,12},{5,1},{1,5},{13,9},{9,13},{6,2},{2,6},{1... | collective-permute-start | bytes 540680 | tf_op jit(solution)/shard_map/late_sums_over_tm/ppermute | solution.py:676
  53.5 6.7 %collective-permute-start.19 = (bf16[320,128]{1,0:T(8,128)(2,1)S(1)}, bf16[320,128]{1,0:T(8,128)(2,1)S(1)}, u32[]{:S(2)}, u32[]{:S(2)}) collective-permute-start(bf16[320,128]{1,0:T(8,128)(2,1)S(1)} %get-tuple-element.61), channel_id=1, source_target_pairs={{8,0},{12,4},{0,8},{4,12},{9,1},{13,5},{1,9},{5,13},{10,2},{14,6},... | collective-permute-start | bytes 245768 | tf_op jit(solution)/shard_map/late_sums_over_tm/ppermute | solution.py:676
  55.1 8.9 %collective-permute-start.20 = (bf16[320,128]{1,0:T(8,128)(2,1)S(1)}, bf16[320,128]{1,0:T(8,128)(2,1)S(1)}, u32[]{:S(2)}, u32[]{:S(2)}) collective-permute-start(bf16[320,128]{1,0:T(8,128)(2,1)S(1)} %get-tuple-element.59.own), channel_id=1, source_target_pairs={{12,0},{8,4},{4,8},{0,12},{13,1},{9,5},{5,9},{1,13},{14,2},{10,6},... | collective-permute-start | bytes 245768 | tf_op jit(solution)/shard_map/late_sums_over_tm/ppermute | solution.py:676
  64.2 5.0 %collective-permute-start.21 = (bf16[2048,128]{1,0:T(8,128)(2,1)S(1)}, bf16[2048,128]{1,0:T(8,128)(2,1)S(1)}, u32[]{:S(2)}, u32[]{:S(2)}) collective-permute-start(bf16[2048,128]{1,0:T(8,128)(2,1)S(1)} %get-tuple-element.62.tail), channel_id=1, source_target_pairs={{0,1},{1,0},{2,3},{3,2},{4,5},{5,4},{6,7},{7,6},{8,9},{9,8},{10,11... | collective-permute-start | bytes 1572872 | tf_op jit(solution)/shard_map/tail_in_chip/ppermute | solution.py:50
  64.2 4.0 %collective-permute-start.22 = (bf16[128,128]{1,0:T(8,128)(2,1)S(1)}, bf16[128,128]{1,0:T(8,128)(2,1)S(1)}, u32[]{:S(2)}, u32[]{:S(2)}) collective-permute-start(bf16[128,128]{1,0:T(8,128)(2,1)S(1)} %get-tuple-element.63), channel_id=1, source_target_pairs={{0,2},{2,0},{1,3},{3,1},{4,6},{6,4},{5,7},{7,5},{8,10},{10,8},{9,1... | collective-permute-start | bytes 98312 | tf_op jit(solution)/shard_map/low_over_head/ppermute | solution.py:50
  65.8 3.3 %collective-permute-start.23 = (bf16[128,128]{1,0:T(8,128)(2,1)S(1)}, bf16[128,128]{1,0:T(8,128)(2,1)S(1)}, u32[]{:S(2)}, u32[]{:S(2)}) collective-permute-start(bf16[128,128]{1,0:T(8,128)(2,1)S(1)} %get-tuple-element.63), channel_id=1, source_target_pairs={{0,3},{1,2},{2,1},{3,0},{4,7},{5,6},{6,5},{7,4},{8,11},{9,10},{10,... | collective-permute-start | bytes 98312 | tf_op jit(solution)/shard_map/low_over_head/ppermute | solution.py:739
  (1 other events, 0.7 us)
